TPU v7x, 32 devices: a whole 2x2x4 slice. The times are simulated.
32 devices in a mesh: groups: 2 (over x), samples: 8 (over z, y), cols: 2 (over core).
Axes of the slice: x: 2, y: 2, z: 4, core: 2. Of those that a mesh axis runs over, the one named last changes fastest.
Arguments:
- kinship: float32 [64, 4, 128, 128], P(('groups', 'samples')), parts along dimension 0, may hold values from 0 to 0.5, as said below
- relatives: int32 [64, 3], P('groups'), parts along dimension 0, may hold values from -1 to 31, as said below
- variance: float32 [8192], P(('groups', 'samples')), parts along dimension 0, may hold values from 0.5 to 2
- phenotypes: float32 [8192, 512], P(('groups', 'samples'), 'cols'), parts along dimension 0, may hold values from -120 to 120
- dosage: float32 [8192, 1024], P(('groups', 'samples'), 'cols'), parts along dimension 0, may hold values from -5 to 5
Outputs:
- solved: float32 [8192, 512], P(('groups', 'samples'), 'cols'), parts along dimension 0
- scores: float32 [2048, 512], P(('groups', 'cols', 'samples')), parts along dimension 0
There are 2 independent parts, one for each index of `groups`. A program takes and returns all parts, laid end to end along the dimension named above; each array names one. Nothing has to cross between parts.
Inputs may be any that keep to these rules, and one draw needn't show every extreme that they name: `relatives`: each entry names a column block held by another device along samples, or is -1. The row blocks of one device name at most 2 blocks held by any single other device, counted with repetition, and some pair of devices reaches 2. The list is mirrored: row block r names column block c exactly as often as c names r. kinship[r, 1 + k] is zero where relatives[r, k] is -1. Where row block r names column block c with tile W, c names r with tile W transposed, pairing every such entry once. Each kinship[r, 0] is symmetric.
All inputs are finite; a program needn't handle non-finite values.
Results may differ from a plain program's by a relative error of at most 0.0001.
Values sent between devices are 32-bit elements; how exact they have to be, the bound alone decides.
No kernel may reach another device: no remote copies, remote signals or barrier semaphores. Data moves between devices by JAX's collectives and lax.ppermute only.
A program may use at most 128 MiB of HBM per device.

v0:
```python
import math

import jax
import jax.numpy as jnp
from jax import lax
from jax.sharding import PartitionSpec as P

ITERS = 2


HIGHEST = lax.Precision.HIGHEST


def slot_table(member, order_rank, values, capacity):
    wanted = member[:, None, :] & (order_rank[:, None, :] == jnp.arange(capacity)[None, :, None])
    chosen = jnp.sum(jnp.where(wanted, values[:, None, :], 0), axis=2)
    return (chosen, jnp.any(wanted, axis=2))


def routing(relatives, block_count, devices, own_index):
    listed = relatives.reshape(devices, -1)
    entry_count = listed.shape[1]
    source = jnp.where(listed >= 0, listed // block_count, -1)
    before = jnp.arange(entry_count)[None, :] < jnp.arange(entry_count)[:, None]
    matches = (source[:, :, None] == source[:, None, :]) & before[None]
    order_rank = jnp.sum(matches.astype(jnp.int32), axis=2)
    capacity = -(-entry_count // (devices - 1))
    incoming_index, incoming_live = slot_table(
        source == own_index, order_rank, listed - own_index * block_count, capacity
    )
    my_source = lax.dynamic_index_in_dim(source, own_index, 0, keepdims=False)
    my_rank = lax.dynamic_index_in_dim(order_rank, own_index, 0, keepdims=False)
    targets = jnp.arange(devices)[:, None] == my_source[None, :]
    entry_ids = jnp.broadcast_to(jnp.arange(entry_count)[None, :], (devices, entry_count))
    rank_rows = jnp.broadcast_to(my_rank[None, :], (devices, entry_count))
    outgoing_index, outgoing_live = slot_table(targets, rank_rows, entry_ids, capacity)
    arrival = jnp.maximum(my_source, 0) * capacity + my_rank
    arrival_live = (my_source >= 0).astype(jnp.float32)
    target_onehot = (
        (incoming_index[:, :, None] == jnp.arange(block_count)[None, None, :])
        & incoming_live[:, :, None]
    ).astype(jnp.float32)
    return (
        incoming_index,
        incoming_live.astype(jnp.float32),
        outgoing_index,
        outgoing_live.astype(jnp.float32),
        arrival,
        arrival_live,
        target_onehot,
    )


def apply_operator(values, own_tiles, far_tiles, diagonal, tables):
    (
        incoming_index,
        incoming_live,
        outgoing_index,
        outgoing_live,
        arrival,
        arrival_live,
        target_onehot,
    ) = tables
    block_count = own_tiles.shape[0]
    tile_rows = own_tiles.shape[1]
    columns = values.shape[1]
    pieces = values.reshape(block_count, tile_rows, columns)
    near_term = jnp.einsum("bij,bjp->bip", own_tiles, pieces, precision=HIGHEST)
    outgoing = jnp.take(pieces, incoming_index, axis=0) * incoming_live[:, :, None, None]
    received = lax.all_to_all(outgoing, "samples", split_axis=0, concat_axis=0, tiled=True)
    flat_recv = received.reshape(-1, tile_rows, columns)
    gathered = jnp.take(flat_recv, arrival, axis=0) * arrival_live[:, None, None]
    gathered = gathered.reshape(block_count, -1, tile_rows, columns)
    far_term = jnp.einsum("bkij,bkjp->bip", far_tiles, gathered, precision=HIGHEST)
    return diagonal[:, None] * values + (near_term + far_term).reshape(values.shape)


def residual_norm(residual, scaled):
    return lax.psum(jnp.sum(residual * scaled, axis=0), "samples")


def curvature(direction, mapped):
    return lax.psum(jnp.sum(direction * mapped, axis=0), "samples")


def per_device(kinship, relatives, variance, phenotypes, dosage):
    devices = lax.axis_size("samples")
    own_index = lax.axis_index("samples")
    block_count = kinship.shape[0]
    tile_rows = kinship.shape[2]
    people_here = phenotypes.shape[0]
    diagonal_mask = jnp.arange(tile_rows)[:, None] == jnp.arange(tile_rows)[None, :]
    own_tiles = jnp.where(diagonal_mask[None], 0.0, kinship[:, 0])
    listed = relatives.reshape(devices, -1)
    my_list = lax.dynamic_index_in_dim(listed, own_index, 0, keepdims=False).reshape(
        block_count, -1
    )
    far_tiles = jnp.where((my_list >= 0)[:, :, None, None], kinship[:, 1:], 0.0)
    row_totals = jnp.sum(own_tiles, axis=2) + jnp.sum(far_tiles, axis=(1, 3))
    diagonal = variance + row_totals.reshape(-1)
    tables = routing(relatives, block_count, devices, own_index)
    solved = jnp.zeros_like(phenotypes)
    residual = phenotypes
    scaled = residual / diagonal[:, None]
    direction = scaled
    norm_now = residual_norm(residual, scaled)
    for iteration in range(ITERS):
        mapped = apply_operator(direction, own_tiles, far_tiles, diagonal, tables)
        step_size = norm_now / curvature(direction, mapped)
        solved = solved + step_size * direction
        if iteration + 1 < ITERS:
            residual = residual - step_size * mapped
            scaled = residual / diagonal[:, None]
            norm_next = residual_norm(residual, scaled)
            direction = scaled + norm_next / norm_now * direction
            norm_now = norm_next
    all_phenos = lax.all_gather(solved, "cols", axis=1, tiled=True)
    norm_scale = 1.0 / math.sqrt(people_here * devices)
    scores = (
        lax.psum_scatter(
            jnp.einsum("pv,pf->vf", dosage, all_phenos, precision=HIGHEST),
            "samples",
            scatter_dimension=0,
            tiled=True,
        )
        * norm_scale
    )
    return (solved, scores)


def solution(mesh):
    return jax.shard_map(
        per_device,
        mesh=mesh,
        in_specs=(
            P(("groups", "samples"), None, None, None),
            P("groups", None),
            P(("groups", "samples")),
            P(("groups", "samples"), "cols"),
            P(("groups", "samples"), "cols"),
        ),
        out_specs=(P(("groups", "samples"), "cols"), P(("groups", "cols", "samples"), None)),
        check_vma=False,
    )
```

profile of v0, /device:TPU:0, one launch (start us, length us, event | category | flops | bytes accessed | tf_op | source)
XLA Modules:
  0.0 281.6 jit_solution(8150922546679243609)
XLA Ops:
  9.2 1.1 fusion.7
  10.3 1.4 fusion
  12.8 2.0 gather_fusion
  14.9 3.2 %select_multiply_fusion.1 = f32[8,2,128,256]{3,2,1,0:T(8,128)} fusion(f32[8,2,128,256]{3,2,1,0:T(8,128)} %bitcast.59, f32[8,2]{1,0:T(8,128)S(1)} %copy.51, pred[8,2]{1,0:T(8,128)(4,1)S(1)} %copy.49), kind=kLoop, calls=%fused_computation.5 | loop fusion | flops 1048576 | bytes 4194384 | tf_op jit(solution)/shard_map/mul | solution.py:69
  18.0 7.3 %all-to-all-start = ((f32[8,2,128,256]{3,2,1,0:T(8,128)}), f32[8,2,128,256]{3,2,1,0:T(8,128)}, u32[]{:S(2)}, u32[]{:S(2)}) async-start(f32[8,2,128,256]{3,2,1,0:T(8,128)} %select_multiply_fusion.1), calls=%async_computation | async-start | bytes 4194304 | tf_op jit(solution)/shard_map/all_to_all | solution.py:70
  25.4 48.2 %all-to-all-done = f32[8,2,128,256]{3,2,1,0:T(8,128)} async-done(((f32[8,2,128,256]{3,2,1,0:T(8,128)}), f32[8,2,128,256]{3,2,1,0:T(8,128)}, u32[]{:S(2)}, u32[]{:S(2)}) %all-to-all-start) | async-done | bytes 2097184 | tf_op jit(solution)/shard_map/all_to_all | solution.py:70
  73.7 3.4 %gather_fusion.1 = f32[12,128,256]{2,1,0:T(8,128)} fusion(f32[16,128,256]{2,1,0:T(8,128)} %bitcast.5, s32[1024]{0:T(1024)S(1)} %pad_clamp_fusion), kind=kCustom, calls=%fused_computation.1.clone | custom fusion | bytes 3145776 | tf_op jit(solution)/shard_map/jit(_take)/gather | solution.py:72
  77.1 1.7 select_multiply_fusion.3
  78.8 1.2 convolution_bitcast_fusion.2
  81.7 19.5 %all-reduce = (f32[256]{0:T(256)S(1)}, f32[256]{0:T(256)S(1)}) all-reduce(f32[256]{0:T(256)S(1)} %get-tuple-element.17, f32[256]{0:T(256)S(1)} %get-tuple-element.16), channel_id=1, replica_groups=mesh['groups'=2,'samples'=8,'cols'=2] {'samples'}, use_global_device_ids=true, to_apply=%region_3.4 | all-reduce | flops 512 | bytes 4096 | tf_op jit(solution)/shard_map/psum | solution.py:79
  101.2 1.3 multiply_reduce_fusion
  102.4 17.1 %psum.30 = f32[256]{0:T(256)S(1)} all-reduce(f32[256]{0:T(256)S(1)} %multiply_reduce_fusion), channel_id=1, replica_groups=mesh['groups'=2,'samples'=8,'cols'=2] {'samples'}, use_global_device_ids=true, to_apply=%region_10.13 | all-reduce | flops 256 | bytes 2048 | tf_op jit(solution)/shard_map/psum | solution.py:79
  119.6 1.3 multiply_add_fusion.1
  120.8 2.0 gather_fusion.2
  122.9 1.9 select_multiply_fusion
  124.8 44.7 %all_to_all.10 = f32[8,2,128,256]{3,2,1,0:T(8,128)} all-to-all(f32[8,2,128,256]{3,2,1,0:T(8,128)S(1)} %select_multiply_fusion), channel_id=1, replica_groups=mesh['groups'=2,'samples'=8,'cols'=2] {'samples'}, dimensions={0} | all-to-all | bytes 4194304 | tf_op jit(solution)/shard_map/all_to_all | solution.py:70
  169.4 3.4 %gather_fusion.3 = f32[12,128,256]{2,1,0:T(8,128)} fusion(f32[16,128,256]{2,1,0:T(8,128)} %bitcast.60, s32[1024]{0:T(1024)S(1)} %pad_clamp_fusion), kind=kCustom, calls=%fused_computation.3.clone | custom fusion | bytes 3145776 | tf_op jit(solution)/shard_map/jit(_take)/gather | solution.py:72
  172.8 1.6 select_multiply_fusion.2
  174.4 1.2 convolution_bitcast_fusion.1
  176.4 19.5 %psum.31 = f32[256]{0:T(256)S(1)} all-reduce(f32[256]{0:T(256)S(1)} %fusion.2), channel_id=1, replica_groups=mesh['groups'=2,'samples'=8,'cols'=2] {'samples'}, use_global_device_ids=true, to_apply=%region_12.15 | all-reduce | flops 256 | bytes 2048 | tf_op jit(solution)/shard_map/psum | solution.py:83
  197.0 6.3 %all-gather.2.cloned.1.call-done = f32[512,512]{1,0:T(8,128)} async-done(((f32[512,256]{1,0:T(8,128)}), f32[512,512]{1,0:T(8,128)}) %all-gather.2.cloned.1.call-update) | async-done | bytes 1048592 | tf_op jit(solution)/shard_map/all_gather | solution.py:117
  203.3 3.1 %convolution_bitcast_fusion = f32[512,512]{0,1:T(8,128)S(1)} fusion(f32[512,512]{1,0:T(8,128)} %all-gather.2.cloned.1.call-done, f32[512,512]{1,0:T(8,128)S(1)} %copy-done), kind=kOutput, calls=%fused_computation.8 | convolution fusion | flops 1610612736 | bytes 3145728 | tf_op jit(solution)/shard_map/pv,pf->vf/dot_general | solution.py:121
  206.4 1.3 copy.57
  207.7 65.2 %reduce-scatter.4.cloned.1.call-done = f32[64,512]{1,0:T(8,128)} async-done(((f32[512,512]{1,0:T(8,128)}), f32[64,512]{1,0:T(8,128)}) %reduce-scatter.4.cloned.1.call-update) | async-done | bytes 131088
  (49 shorter events, 8.5 us)
Async XLA Ops:
  7.2 196.1 %copy-start = (f32[512,512]{1,0:T(8,128)S(1)}, f32[512,512]{1,0:T(8,128)}, u32[]{:S(2)}) copy-start(f32[512,512]{1,0:T(8,128)} %param.13) | copy-start | bytes 3145732
  7.2 5.5 %copy-start.1 = (f32[512,256]{1,0:T(8,128)S(1)}, f32[512,256]{1,0:T(8,128)}, u32[]{:S(2)}) copy-start(f32[512,256]{1,0:T(8,128)} %param.12) | copy-start | bytes 1572868
  18.0 55.6 %all-to-all-start = ((f32[8,2,128,256]{3,2,1,0:T(8,128)}), f32[8,2,128,256]{3,2,1,0:T(8,128)}, u32[]{:S(2)}, u32[]{:S(2)}) async-start(f32[8,2,128,256]{3,2,1,0:T(8,128)} %select_multiply_fusion.1), calls=%async_computation | async-start | bytes 4194304 | tf_op jit(solution)/shard_map/all_to_all | solution.py:70
  25.3 178.0 %all-gather.2.cloned.1.call-start = ((), (), s32[]{:S(2)}) async-start(), calls=%async_computation.3 | async-start | bytes 1572864 | tf_op jit(solution)/shard_map/all_gather | solution.py:117
  77.1 1.7 copy-start.2
  80.6 0.8 copy-start.3
  196.9 76.0 %reduce-scatter.4.cloned.1.call-start = ((), (), s32[]{:S(2)}) async-start(), calls=%async_computation.4 | async-start | bytes 1179648
Sparse Core Ops, SparseCore 0:
  197.1 6.1 all-gather.1
  207.9 65.0 reduce-scatter.3
where the time goes:
time: 282 us
  waiting for transfers between devices  120 us (43%)
  blocking collectives  101 us (36%)
  other arithmetic  16.4 us (6%)
  local copies, waits for them, and re-layouts  16.3 us (6%)
  between operations  14.3 us (5%)
  starting transfers between devices  7.36 us (3%)
  matrix products  6.73 us (2%)
    unnamed x3, waiting for transfers between devices  65.2 us
    all_to_all x1, waiting for transfers between devices, apply_operator(): lax.all_to_all(outgoing, 'samples', split_axis=0, concat_axis=0, tiled=True)  48.2 us
    all_to_all x1, blocking collectives, apply_operator(): lax.all_to_all(outgoing, 'samples', split_axis=0, concat_axis=0, tiled=True)  44.7 us
    psum x2, blocking collectives, residual_norm(): return lax.psum(jnp.sum(residual * scaled, axis=0), 'samples')  36.6 us
    psum x1, blocking collectives, curvature(): return lax.psum(jnp.sum(direction * mapped, axis=0), 'samples')  19.5 us
    all_to_all x1, starting transfers between devices, apply_operator(): lax.all_to_all(outgoing, 'samples', split_axis=0, concat_axis=0, tiled=True)  7.28 us
    gather x2, local copies, waits for them, and re-layouts, apply_operator(): jnp.take(flat_recv, arrival, axis=0) * arrival_live[:, None, None]  6.77 us
    all_gather x1, waiting for transfers between devices, per_device(): all_phenos = lax.all_gather(solved, 'cols', axis=1, tiled=True)  6.31 us
  transfers between devices with their start and end apart: 3, of which 3 were waited for; matrix products, arithmetic and copies ran while one was open for 0% of the time, Pallas kernels for 0%

commit v1 on v0

v1 whole, which is shorter than its diff:
```python
import functools
import math

import jax
import jax.numpy as jnp
from jax import lax
from jax.experimental import pallas as pl
from jax.experimental.pallas import tpu as pltpu
from jax.sharding import PartitionSpec as P

VMEM_LIMIT = 40 * 1024 * 1024


def split(values):
    high = values.astype(jnp.bfloat16)
    low = (values - high.astype(jnp.float32)).astype(jnp.bfloat16)
    return high, low


def product(left, right):
    left_high, left_low = split(left)
    right_high, right_low = split(right)
    dot = functools.partial(jnp.dot, preferred_element_type=jnp.float32)
    return dot(left_high, right_high) + (dot(left_high, right_low) + dot(left_low, right_high))


def on_diagonal(size):
    rows = lax.broadcasted_iota(jnp.int32, (size, size), 0)
    return rows == lax.broadcasted_iota(jnp.int32, (size, size), 1)


def prepare_kernel(devices, capacity, me_ref, list_ref, kinship_ref, variance_ref, phenotypes_ref,
                   direction_ref, diagonal_ref, outgoing_ref, table_ref, first_ref, last_ref):
    block_count, positions, tile = kinship_ref.shape[:3]
    me = me_ref[0]
    for j in range(devices):
        first_ref[j] = jnp.int32(block_count * block_count)
        last_ref[j] = jnp.int32(-1)

    def entry_key(row, position):
        listed = list_ref[me * block_count + row, position]
        safe = jnp.maximum(listed, 0)
        other = safe // block_count
        far_block = safe - other * block_count
        key = jnp.where(me < other, row * block_count + far_block, far_block * block_count + row)
        return listed >= 0, other, key

    def collect(entry, carry):
        row = entry // (positions - 1)
        live, other, key = entry_key(row, entry - row * (positions - 1))

        @pl.when(live)
        def _():
            first_ref[other] = jnp.minimum(first_ref[other], key)
            last_ref[other] = jnp.maximum(last_ref[other], key)

        return carry

    lax.fori_loop(0, block_count * (positions - 1), collect, 0)

    def tabulate(entry, carry):
        row = entry // (positions - 1)
        live, other, key = entry_key(row, entry - row * (positions - 1))
        spare = jnp.where(me == 0, 1, 0)
        is_first = key == first_ref[other]
        handled = jnp.where(me < other, first_ref[other], last_ref[other])
        weight = jnp.where(first_ref[other] == last_ref[other], 1, 2)
        table_ref[0, entry] = jnp.where(live, other, spare)
        table_ref[1, entry] = jnp.where(live & jnp.logical_not(is_first), capacity - 1, 0)
        table_ref[2, entry] = jnp.where(live & (key == handled), weight, 0)
        return carry

    lax.fori_loop(0, block_count * (positions - 1), tabulate, 0)

    def mine(key, other):
        block = jnp.where(me < other, key // block_count, key % block_count)
        return jnp.where((key >= 0) & (key < block_count * block_count), block, 0)

    def send(other, carry):
        first = mine(first_ref[other], other)
        last = mine(last_ref[other], other)
        table_ref[3, other] = jnp.where(me < other, last, first)
        outgoing_ref[other, 0] = direction_ref[pl.ds(pl.multiple_of(first * tile, tile), tile), :]
        if capacity > 1:
            outgoing_ref[other, capacity - 1] = direction_ref[pl.ds(pl.multiple_of(last * tile, tile), tile), :]
        return carry

    diagonal_mask = on_diagonal(tile)
    for row in range(block_count):
        block = slice(row * tile, (row + 1) * tile)
        total = jnp.where(diagonal_mask, variance_ref[row:row + 1, :], kinship_ref[row, 0])
        for position in range(1, positions):
            total = total + kinship_ref[row, position]
        diagonal = jnp.sum(total, axis=1, keepdims=True)
        diagonal_ref[block, :] = diagonal
        direction_ref[block, :] = phenotypes_ref[block, :] / diagonal
    lax.fori_loop(0, devices, send, 0)


def apply_kernel(devices, table_ref, kinship_ref, direction_ref, diagonal_ref, received_ref, phenotypes_ref,
                 scaled_ref, outgoing_ref, sums_ref):
    block_count, positions, tile = kinship_ref.shape[:3]
    diagonal_mask = on_diagonal(tile)
    norm = jnp.zeros((8, direction_ref.shape[1]), jnp.float32)
    cross = jnp.zeros((8, direction_ref.shape[1]), jnp.float32)
    for row in range(block_count):
        block = slice(row * tile, (row + 1) * tile)
        here = direction_ref[block, :]
        mapped = product(jnp.where(diagonal_mask, 0.0, kinship_ref[row, 0]), here)
        for position in range(1, positions):
            entry = row * (positions - 1) + position - 1
            there = received_ref[table_ref[0, entry], table_ref[1, entry]]
            mapped = mapped + product(kinship_ref[row, position], there)
        scaled_ref[block, :] = mapped / diagonal_ref[block, :]
        norm = norm + jnp.sum((here * phenotypes_ref[block, :]).reshape(tile // 8, 8, -1), axis=0)
        cross = cross + jnp.sum((here * mapped).reshape(tile // 8, 8, -1), axis=0)
    sums_ref[0:1, :] = jnp.sum(norm, axis=0, keepdims=True)
    sums_ref[1:2, :] = jnp.sum(cross, axis=0, keepdims=True)

    def send(other, carry):
        block = table_ref[3, other]
        outgoing_ref[other] = scaled_ref[pl.ds(pl.multiple_of(block * tile, tile), tile), :]
        return carry

    lax.fori_loop(0, devices, send, 0)


def curvature_kernel(devices, table_ref, kinship_ref, direction_ref, diagonal_ref, scaled_ref, received_ref,
                     later_ref, all_sums_ref, sums_ref):
    block_count, positions, tile = kinship_ref.shape[:3]
    diagonal_mask = on_diagonal(tile)
    first_sums = jnp.sum(all_sums_ref[...], axis=0)
    rho = first_sums[1:2, :] / first_sums[0:1, :]
    norm = jnp.zeros((8, direction_ref.shape[1]), jnp.float32)
    bend = jnp.zeros((8, direction_ref.shape[1]), jnp.float32)
    for row in range(block_count):
        block = slice(row * tile, (row + 1) * tile)
        here = scaled_ref[block, :] - rho * direction_ref[block, :]
        mapped = product(jnp.where(diagonal_mask, 0.0, kinship_ref[row, 0]), here)
        for position in range(1, positions):
            entry = row * (positions - 1) + position - 1
            other = table_ref[0, entry]
            weight = table_ref[2, entry].astype(jnp.float32)
            there = weight * (later_ref[other] - rho * received_ref[other, table_ref[1, entry]])
            mapped = mapped + product(kinship_ref[row, position], there)
        norm = norm + jnp.sum((here * here * diagonal_ref[block, :]).reshape(tile // 8, 8, -1), axis=0)
        bend = bend + jnp.sum((here * mapped).reshape(tile // 8, 8, -1), axis=0)
    sums_ref[0:1, :] = jnp.sum(norm, axis=0, keepdims=True)
    sums_ref[1:2, :] = jnp.sum(bend, axis=0, keepdims=True)


def call(kernel, out_shape, in_specs, out_specs, scratch_shapes=()):
    return pl.pallas_call(
        kernel,
        out_shape=out_shape,
        in_specs=in_specs,
        out_specs=out_specs,
        scratch_shapes=list(scratch_shapes),
        compiler_params=pltpu.CompilerParams(vmem_limit_bytes=VMEM_LIMIT),
    )


def share(values, axis, devices):
    me = lax.axis_index(axis)
    rows = values.shape[0] // devices
    values = values.reshape(devices, rows, -1)
    step = 1
    while step < devices:
        pairs = [(i, i ^ step) for i in range(devices)]
        bit = (me // step) % 2
        halves = values.reshape(-1, 2, rows, values.shape[-1])
        kept = lax.dynamic_index_in_dim(halves, bit, 1, keepdims=False)
        given = lax.dynamic_index_in_dim(halves, 1 - bit, 1, keepdims=False)
        values = kept + lax.ppermute(given, axis, pairs)
        step *= 2
    return values.reshape(rows, -1)


def per_device(kinship, relatives, variance, phenotypes, dosage):
    devices = lax.axis_size("samples")
    me = lax.axis_index("samples").astype(jnp.int32).reshape(1)
    block_count, positions, tile = kinship.shape[:3]
    people, columns = phenotypes.shape
    entries = block_count * (positions - 1)
    capacity = -(-entries // (devices - 1))
    assert capacity <= 2
    vmem = pl.BlockSpec(memory_space=pltpu.VMEM)
    smem = pl.BlockSpec(memory_space=pltpu.SMEM)
    full = jax.ShapeDtypeStruct((people, columns), jnp.float32)
    sums = jax.ShapeDtypeStruct((2, columns), jnp.float32)
    direction, diagonal, outgoing, table = call(
        functools.partial(prepare_kernel, devices, capacity),
        (
            full,
            jax.ShapeDtypeStruct((people, 1), jnp.float32),
            jax.ShapeDtypeStruct((devices, capacity, tile, columns), jnp.float32),
            jax.ShapeDtypeStruct((4, max(entries, devices)), jnp.int32),
        ),
        [smem, smem, vmem, vmem, vmem],
        (vmem, vmem, vmem, smem),
        [pltpu.SMEM((devices,), jnp.int32), pltpu.SMEM((devices,), jnp.int32)],
    )(me, relatives, kinship, variance.reshape(block_count, tile), phenotypes)

    def variant_sums(values):
        both = lax.all_gather(values, "cols", axis=1, tiled=True)
        partial = lax.dot_general(
            dosage, both, (((0,), (0,)), ((), ())), precision=lax.Precision.HIGH,
            preferred_element_type=jnp.float32,
        )
        return share(partial, "samples", devices)

    received = lax.all_to_all(outgoing, "samples", split_axis=0, concat_axis=0, tiled=True)
    direction_scores = variant_sums(direction)
    scaled, outgoing, first_sums = call(
        functools.partial(apply_kernel, devices),
        (full, jax.ShapeDtypeStruct((devices, tile, columns), jnp.float32), sums),
        [smem, vmem, vmem, vmem, vmem, vmem],
        (vmem, vmem, vmem),
    )(table, kinship, direction, diagonal, received, phenotypes)
    all_first = lax.all_gather(first_sums, ("cols", "samples"), axis=0)
    later = lax.all_to_all(outgoing, "samples", split_axis=0, concat_axis=0, tiled=True)
    scaled_scores = variant_sums(scaled)
    own_col = lax.axis_index("cols")
    own_first = lax.dynamic_slice_in_dim(all_first, own_col * devices, devices, 0)
    second_sums = call(
        functools.partial(curvature_kernel, devices),
        sums,
        [smem] + [vmem] * 7,
        vmem,
    )(table, kinship, direction, diagonal, scaled, received, later, own_first)
    all_second = lax.all_gather(second_sums, ("cols", "samples"), axis=0)

    def coefficients(first, second):
        norm, cross = first[..., 0, :], first[..., 1, :]
        later_norm, bend = second[..., 0, :], second[..., 1, :]
        curve = norm + cross
        ratio = later_norm / curve
        step = jnp.where(later_norm > 0, later_norm / (later_norm + bend - later_norm * ratio), 0.0)
        start = norm / curve
        return start * (1.0 + step * (ratio + cross / norm)), -start * step

    first_both = jnp.sum(all_first.reshape(-1, devices, 2, columns), axis=1)
    second_both = jnp.sum(all_second.reshape(-1, devices, 2, columns), axis=1)
    along, across = coefficients(first_both, second_both)
    own_along = lax.dynamic_index_in_dim(along, own_col, 0, keepdims=True)
    own_across = lax.dynamic_index_in_dim(across, own_col, 0, keepdims=True)
    solved = own_along * direction + own_across * scaled
    norm_scale = 1.0 / math.sqrt(people * devices)
    scores = (along.reshape(1, -1) * direction_scores + across.reshape(1, -1) * scaled_scores) * norm_scale
    return (solved, scores)


def solution(mesh):
    return jax.shard_map(
        per_device,
        mesh=mesh,
        in_specs=(
            P(("groups", "samples"), None, None, None),
            P("groups", None),
            P(("groups", "samples")),
            P(("groups", "samples"), "cols"),
            P(("groups", "samples"), "cols"),
        ),
        out_specs=(P(("groups", "samples"), "cols"), P(("groups", "cols", "samples"), None)),
        check_vma=False,
    )
```

time: 282 us -> 209 us (0.74)
  waiting for transfers between devices: 120 us -> 66 us
  blocking collectives: 101 us -> 72.7 us
  starting transfers between devices: 7.36 us -> 18.2 us
  other arithmetic: 16.4 us -> 6 us
  Pallas kernels: 0 us -> 6.56 us
  local copies, waits for them, and re-layouts: 16.3 us -> 20 us
    all_gather x0 -> x2, blocking collectives: none -> 72.7 us  [the longest x1 43.8 us: per_device(): all_first = lax.all_gather(first_sums, ('cols', 'samples'), axis=0)]
    unnamed x3 -> x2, waiting for transfers between devices: 65.2 us -> 0.7 us
    psum x3 -> x0, blocking collectives: 56.1 us -> none  [the longest x2 36.6 us: residual_norm(): return lax.psum(jnp.sum(residual * scaled, axis=0), 'samples')]
    all_to_all x1 -> x0, blocking collectives: 44.7 us -> none  [apply_operator(): lax.all_to_all(outgoing, 'samples', split_axis=0, concat_axis=0, tiled=True)]
    ppermute x0 -> x6, waiting for transfers between devices: none -> 23.7 us  [share(): values = kept + lax.ppermute(given, axis, pairs)]
    all_to_all x1 -> x2, waiting for transfers between devices: 48.2 us -> 29 us  [per_device(): lax.all_to_all(outgoing, 'samples', split_axis=0, concat_axis=0, tiled=True)]
    unnamed x12 -> x41, local copies, waits for them, and re-layouts: 4.82 us -> 16.9 us
    gather x4 -> x0, local copies, waits for them, and re-layouts: 10.8 us -> none  [the longest x2 6.77 us: apply_operator(): jnp.take(flat_recv, arrival, axis=0) * arrival_live[:, None, None]]
  transfers between devices with their start and end apart: 3 -> 10, of which waited for: 3 -> 5; matrix products, arithmetic and copies ran while one was open for 0% -> 6% of each run, Pallas kernels for 0% -> 2%
where the time goes in v1:
time: 209 us; the launch traced here: 208 us
  blocking collectives  72.7 us (35%)
  waiting for transfers between devices  66 us (32%)
  local copies, waits for them, and re-layouts  20 us (10%)
  starting transfers between devices  18.2 us (9%)
  between operations  14.3 us (7%)
  Pallas kernels  6.56 us (3%)
  other arithmetic  6 us (3%)
  matrix products  4.5 us (2%)
    all_gather x1, blocking collectives, per_device(): all_first = lax.all_gather(first_sums, ('cols', 'samples'), axis=0)  43.8 us
    all_to_all x2, waiting for transfers between devices, per_device(): lax.all_to_all(outgoing, 'samples', split_axis=0, concat_axis=0, tiled=True)  29 us
    all_gather x1, blocking collectives, per_device(): all_second = lax.all_gather(second_sums, ('cols', 'samples'), axis=0)  29 us
    ppermute x6, waiting for transfers between devices, share(): values = kept + lax.ppermute(given, axis, pairs)  23.7 us
    unnamed x41, local copies, waits for them, and re-layouts  16.9 us
    all_gather x2, waiting for transfers between devices, variant_sums(): both = lax.all_gather(values, 'cols', axis=1, tiled=True)  12.7 us
    all_to_all x2, starting transfers between devices, per_device(): lax.all_to_all(outgoing, 'samples', split_axis=0, concat_axis=0, tiled=True)  11.5 us
    ppermute x6, starting transfers between devices, share(): values = kept + lax.ppermute(given, axis, pairs)  6.62 us
  transfers between devices with their start and end apart: 10, of which 5 were waited for; matrix products, arithmetic and copies ran while one was open for 6% of the time, Pallas kernels for 2%

profile of v1, /device:TPU:0, one launch (start us, length us, event | category | flops | bytes accessed | tf_op | source)
XLA Modules:
  0.0 208.4 jit_solution(2013829193486646819)
XLA Ops:
  8.0 1.2 copy-done.1
  9.3 1.0 copy-done.10
  11.0 2.5 %shard_map.68 = (f32[512,256]{1,0:T(8,128)S(1)}, f32[512,1]{1,0:T(8,128)S(1)}, f32[8,2,128,256]{3,2,1,0:T(8,128)S(1)}, s32[4,12]{1,0:T(4,128)S(1)}) custom-call(s32[1]{0:T(128)} %bitcast.me_ref, s32[32,3]{1,0:T(8,128)S(1)} %copy.13.list_ref, f32[4,4,128,128]{3,2,1,0:T(8,128)S(1)} %copy-done.1, f32[4,128]{1,0:T(4,128)S(1)} %bitcast.84, f32[512,256]{1,0:T(8,128)S(1)} %copy-done.10), custom_call_target="tpu_custom_call" | custom-call | tf_op jit(solution)/shard_map/pallas_call | solution.py:191
  14.3 1.4 copy-done.9
  15.7 7.3 %all-to-all-start = ((f32[8,2,128,256]{3,2,1,0:T(8,128)}), f32[8,2,128,256]{3,2,1,0:T(8,128)S(1)}, u32[]{:S(2)}, u32[]{:S(2)}) async-start(f32[8,2,128,256]{3,2,1,0:T(8,128)} %copy-done.9), calls=%async_computation | async-start | bytes 4194304 | tf_op jit(solution)/shard_map/all_to_all | solution.py:212
  23.8 12.6 %all-gather.7.cloned.1.call-done = f32[512,512]{1,0:T(8,128)} async-done(((f32[512,256]{1,0:T(8,128)}), f32[512,512]{1,0:T(8,128)}) %all-gather.7.cloned.1.call-update) | async-done | bytes 1048592 | tf_op jit(solution)/shard_map/all_gather | solution.py:205
  36.4 2.2 %fusion.13 = f32[512,512]{0,1:T(8,128)S(1)} fusion(f32[512,512]{1,0:T(8,128)} %all-gather.7.cloned.1.call-done, f32[512,512]{1,0:T(8,128)S(1)} %copy-done), kind=kOutput, calls=%fused_computation.46 | convolution fusion | flops 805306368 | bytes 3145728 | tf_op jit(solution)/shard_map/dot_general | solution.py:206
  40.5 1.7 collective-permute-start
  42.2 29.0 %all-to-all-done.received_ref = f32[8,2,128,256]{3,2,1,0:T(8,128)S(1)} async-done(((f32[8,2,128,256]{3,2,1,0:T(8,128)}), f32[8,2,128,256]{3,2,1,0:T(8,128)S(1)}, u32[]{:S(2)}, u32[]{:S(2)}) %all-to-all-start) | async-done | bytes 2097184 | tf_op jit(solution)/shard_map/all_to_all | solution.py:212
  71.2 1.2 copy-done.2
  74.5 1.7 shard_map.69
  78.0 1.3 bitcast_add_fusion.1
  80.9 4.3 %all-to-all-start.1 = ((f32[8,128,256]{2,1,0:T(8,128)}), f32[8,128,256]{2,1,0:T(8,128)}, u32[]{:S(2)}, u32[]{:S(2)}) async-start(f32[8,128,256]{2,1,0:T(8,128)} %copy-done.12), calls=%async_computation.1 | async-start | bytes 2097152 | tf_op jit(solution)/shard_map/all_to_all | solution.py:221
  85.2 3.5 %collective-permute-done.1 = f32[2,64,512]{2,1,0:T(8,128)} collective-permute-done((f32[2,64,512]{2,1,0:T(8,128)}, f32[2,64,512]{2,1,0:T(8,128)}, u32[]{:S(2)}, u32[]{:S(2)}) %collective-permute-start.1) | collective-permute-done | bytes 262176 | tf_op jit(solution)/shard_map/ppermute | solution.py:174
  88.6 1.1 bitcast_add_fusion.3
  90.4 4.7 %collective-permute-start.2 = (f32[1,64,512]{2,1,0:T(8,128)}, f32[1,64,512]{2,1,0:T(8,128)}, u32[]{:S(2)}, u32[]{:S(2)}) collective-permute-start(f32[1,64,512]{2,1,0:T(8,128)} %constant_dynamic-slice_fusion.3), channel_id=1, source_target_pairs={{0,8},{2,10},{4,12},{6,14},{8,0},{10,2},{12,4},{14,6},{1,9},{3,11}... | collective-permute-start | bytes 393224 | tf_op jit(solution)/shard_map/ppermute | solution.py:174
  95.2 43.8 %all-gather.2 = f32[16,2,256]{2,1,0:T(2,128)S(1)} all-gather(f32[1,2,256]{2,1,0:T(2,128)S(1)} %bitcast.85), channel_id=2, replica_groups=mesh['groups'=2,'samples'=8,'cols'=2] {'cols','samples'}, dimensions={0}, use_global_device_ids=true | all-gather | bytes 34816 | tf_op jit(solution)/shard_map/all_gather | solution.py:220
  139.0 2.3 %fusion.14 = f32[512,512]{0,1:T(8,128)S(1)} fusion(f32[512,512]{1,0:T(8,128)} %all-gather.9.cloned.1.call-done, f32[512,512]{1,0:T(8,128)S(1)} %copy-done), kind=kOutput, calls=%fused_computation.47 | convolution fusion | flops 805306368 | bytes 3145728 | tf_op jit(solution)/shard_map/dot_general | solution.py:206
  141.4 13.9 %collective-permute-done.3 = f32[4,64,512]{2,1,0:T(8,128)S(1)} collective-permute-done((f32[4,64,512]{2,1,0:T(8,128)S(1)}, f32[4,64,512]{2,1,0:T(8,128)S(1)}, u32[]{:S(2)}, u32[]{:S(2)}) %collective-permute-start.3) | collective-permute-done | bytes 524320 | tf_op jit(solution)/shard_map/ppermute | solution.py:174
  156.9 1.2 copy-done.3
  160.2 2.3 %shard_map.70 = f32[2,256]{1,0:T(2,128)S(1)} custom-call(s32[4,12]{1,0:T(4,128)S(1)} %get-tuple-element.9.table_ref, f32[4,4,128,128]{3,2,1,0:T(8,128)S(1)} %copy-done.3, f32[512,256]{1,0:T(8,128)S(1)} %copy-done.6, f32[512,1]{1,0:T(8,128)S(1)} %get-tuple-element.11.diagonal_ref, f32[512,256]{1,0:T(8,128)S(1)} %copy-done.8, ...), custom_call_target="tpu_custom_call" | custom-call | tf_op jit(solution)/shard_map/pallas_call | solution.py:225
  162.6 29.0 %all-gather.3 = f32[16,2,256]{2,1,0:T(2,128)S(1)} all-gather(f32[1,2,256]{2,1,0:T(2,128)S(1)} %bitcast.83), channel_id=3, replica_groups=mesh['groups'=2,'samples'=8,'cols'=2] {'cols','samples'}, dimensions={0}, use_global_device_ids=true | all-gather | bytes 34816 | tf_op jit(solution)/shard_map/all_gather | solution.py:231
  193.6 6.3 %collective-permute-done.5 = f32[1,64,512]{2,1,0:T(8,128)S(1)} collective-permute-done((f32[1,64,512]{2,1,0:T(8,128)S(1)}, f32[1,64,512]{2,1,0:T(8,128)S(1)}, u32[]{:S(2)}, u32[]{:S(2)}) %collective-permute-start.5) | collective-permute-done | bytes 131104 | tf_op jit(solution)/shard_map/ppermute | solution.py:174
  200.0 1.6 fusion.1
  (67 shorter events, 16.9 us)
Async XLA Ops:
  7.2 29.2 %copy-start = (f32[512,512]{1,0:T(8,128)S(1)}, f32[512,512]{1,0:T(8,128)}, u32[]{:S(2)}) copy-start(f32[512,512]{1,0:T(8,128)} %param.9) | copy-start | bytes 3145732
  8.0 1.2 copy-start.1
  9.3 1.0 copy-start.10
  14.3 1.4 copy-start.9
  15.7 55.5 %all-to-all-start = ((f32[8,2,128,256]{3,2,1,0:T(8,128)}), f32[8,2,128,256]{3,2,1,0:T(8,128)S(1)}, u32[]{:S(2)}, u32[]{:S(2)}) async-start(f32[8,2,128,256]{3,2,1,0:T(8,128)} %copy-done.9), calls=%async_computation | async-start | bytes 4194304 | tf_op jit(solution)/shard_map/all_to_all | solution.py:212
  23.0 13.4 %all-gather.7.cloned.1.call-start = ((), (), s32[]{:S(2)}) async-start(), calls=%async_computation.2 | async-start | bytes 1572864 | tf_op jit(solution)/shard_map/all_gather | solution.py:205
  23.7 115.3 %all-gather.9.cloned.1.call-start = ((), (), s32[]{:S(2)}) async-start(), calls=%async_computation.3 | async-start | bytes 1572864 | tf_op jit(solution)/shard_map/all_gather | solution.py:205
  38.7 1.0 copy-start.14
  40.5 37.5 %collective-permute-start = (f32[4,64,512]{2,1,0:T(8,128)}, f32[4,64,512]{2,1,0:T(8,128)}, u32[]{:S(2)}, u32[]{:S(2)}) collective-permute-start(f32[4,64,512]{2,1,0:T(8,128)} %dynamic-slice_bitcast_fusion.1), channel_id=1, source_target_pairs={{0,2},{2,0},{4,6},{6,4},{8,10},{10,8},{12,14},{14,12},{1,3},{3,1},... | collective-permute-start | bytes 1572872 | tf_op jit(solution)/shard_map/ppermute | solution.py:174
  71.2 1.2 copy-start.2
  72.4 1.0 copy-start.5
  73.5 1.0 copy-start.11
  80.9 7.8 %collective-permute-start.1 = (f32[2,64,512]{2,1,0:T(8,128)}, f32[2,64,512]{2,1,0:T(8,128)}, u32[]{:S(2)}, u32[]{:S(2)}) collective-permute-start(f32[2,64,512]{2,1,0:T(8,128)} %dynamic-slice_bitcast_fusion.3), channel_id=1, source_target_pairs={{0,4},{2,6},{4,0},{6,2},{8,12},{10,14},{12,8},{14,10},{1,5},{3,7},... | collective-permute-start | bytes 786440 | tf_op jit(solution)/shard_map/ppermute | solution.py:174
  80.9 76.0 %all-to-all-start.1 = ((f32[8,128,256]{2,1,0:T(8,128)}), f32[8,128,256]{2,1,0:T(8,128)}, u32[]{:S(2)}, u32[]{:S(2)}) async-start(f32[8,128,256]{2,1,0:T(8,128)} %copy-done.12), calls=%async_computation.1 | async-start | bytes 2097152 | tf_op jit(solution)/shard_map/all_to_all | solution.py:221
  89.7 49.2 %copy-start.18 = (f32[2,64,512]{2,1,0:T(8,128)}, f32[2,64,512]{2,1,0:T(8,128)S(1)}, u32[]{:S(2)}) copy-start(f32[2,64,512]{2,1,0:T(8,128)S(1)} %bitcast_add_fusion.3) | copy-start | bytes 786436
  90.4 103.2 %collective-permute-start.2 = (f32[1,64,512]{2,1,0:T(8,128)}, f32[1,64,512]{2,1,0:T(8,128)}, u32[]{:S(2)}, u32[]{:S(2)}) collective-permute-start(f32[1,64,512]{2,1,0:T(8,128)} %constant_dynamic-slice_fusion.3), channel_id=1, source_target_pairs={{0,8},{2,10},{4,12},{6,14},{8,0},{10,2},{12,4},{14,6},{1,9},{3,11}... | collective-permute-start | bytes 393224 | tf_op jit(solution)/shard_map/ppermute | solution.py:174
  141.3 14.0 %collective-permute-start.3 = (f32[4,64,512]{2,1,0:T(8,128)S(1)}, f32[4,64,512]{2,1,0:T(8,128)S(1)}, u32[]{:S(2)}, u32[]{:S(2)}) collective-permute-start(f32[4,64,512]{2,1,0:T(8,128)S(1)} %dynamic-slice_bitcast_fusion), channel_id=1, source_target_pairs={{0,2},{2,0},{4,6},{6,4},{8,10},{10,8},{12,14},{14,12},{1,3},{3,1},... | collective-permute-start | bytes 1572872 | tf_op jit(solution)/shard_map/ppermute | solution.py:174
  156.9 34.6 %collective-permute-start.4 = (f32[2,64,512]{2,1,0:T(8,128)}, f32[2,64,512]{2,1,0:T(8,128)}, u32[]{:S(2)}, u32[]{:S(2)}) collective-permute-start(f32[2,64,512]{2,1,0:T(8,128)} %dynamic-slice_bitcast_fusion.2), channel_id=1, source_target_pairs={{0,4},{2,6},{4,0},{6,2},{8,12},{10,14},{12,8},{14,10},{1,5},{3,7},... | collective-permute-start | bytes 786440 | tf_op jit(solution)/shard_map/ppermute | solution.py:174
  156.9 1.2 copy-start.3
  158.2 1.0 copy-start.6
  159.2 1.0 copy-start.8
  160.2 31.3 %copy-start.17 = (f32[4,64,512]{2,1,0:T(8,128)S(1)}, f32[4,64,512]{2,1,0:T(8,128)}, u32[]{:S(2)}) copy-start(f32[4,64,512]{2,1,0:T(8,128)} %copy-done.16) | copy-start | bytes 1572868
  162.6 37.4 %copy-start.19 = (f32[2,64,512]{2,1,0:T(8,128)S(1)}, f32[2,64,512]{2,1,0:T(8,128)}, u32[]{:S(2)}) copy-start(f32[2,64,512]{2,1,0:T(8,128)} %copy-done.18) | copy-start | bytes 786436
  192.6 7.3 %collective-permute-start.5 = (f32[1,64,512]{2,1,0:T(8,128)S(1)}, f32[1,64,512]{2,1,0:T(8,128)S(1)}, u32[]{:S(2)}, u32[]{:S(2)}) collective-permute-start(f32[1,64,512]{2,1,0:T(8,128)S(1)} %constant_dynamic-slice_fusion.2), channel_id=1, source_target_pairs={{0,8},{2,10},{4,12},{6,14},{8,0},{10,2},{12,4},{14,6},{1,9},{3,11}... | collective-permute-start | bytes 393224 | tf_op jit(solution)/shard_map/ppermute | solution.py:174
  (6 other events, 4.8 us)
Sparse Core Ops, SparseCore 0:
  25.9 10.4 all-gather.6
  78.2 8.1 all-gather.8

commit v2 on v1

v2 whole, which is shorter than its diff:
```python
import functools
import math

import jax
import jax.numpy as jnp
from jax import lax
from jax.experimental import pallas as pl
from jax.experimental.pallas import tpu as pltpu
from jax.sharding import PartitionSpec as P

VMEM_LIMIT = 40 * 1024 * 1024
SUBLANES = 8


def split(values):
    high = values.astype(jnp.bfloat16)
    low = (values - high.astype(jnp.float32)).astype(jnp.bfloat16)
    return high, low


def product(left, right):
    left_high, left_low = split(left)
    right_high, right_low = split(right)
    dot = functools.partial(jnp.dot, preferred_element_type=jnp.float32)
    return dot(left_high, right_high) + (dot(left_high, right_low) + dot(left_low, right_high))


def on_diagonal(size):
    rows = lax.broadcasted_iota(jnp.int32, (size, size), 0)
    return rows == lax.broadcasted_iota(jnp.int32, (size, size), 1)


def column_sums(values):
    rows, columns = values.shape
    return jnp.sum(values.reshape(rows // SUBLANES, SUBLANES, columns), axis=0)


class Copies:
    def __init__(self, semaphores):
        self.semaphores = semaphores
        self.count = 0

    def start(self, source, target):
        copy = pltpu.make_async_copy(source, target, self.semaphores.at[self.count])
        self.count += 1
        copy.start()
        return copy


def wait_all(copies):
    for copy in copies:
        copy.wait()


def prepare_kernel(devices, capacity, place_ref, list_ref, kinship_hbm, variance_ref, phenotypes_hbm, *refs):
    direction_hbm, diagonal_ref, table_ref = refs[:3]
    outgoing_hbm = refs[3:3 + devices - 1]
    kinship_ref, phenotypes_ref, direction_ref, first_ref, last_ref, semaphores = refs[3 + devices - 1:]
    block_count, positions, tile = kinship_ref.shape[:3]
    copies = Copies(semaphores)
    loads = []
    for row in range(block_count):
        block = pl.ds(row * tile, tile)
        loads.append((
            copies.start(kinship_hbm.at[row], kinship_ref.at[row]),
            copies.start(phenotypes_hbm.at[block], phenotypes_ref.at[block]),
        ))
    me = place_ref[0]
    for j in range(devices):
        first_ref[j] = jnp.int32(block_count * block_count)
        last_ref[j] = jnp.int32(-1)

    def entry_key(row, position):
        listed = list_ref[me * block_count + row, position]
        safe = jnp.maximum(listed, 0)
        other = safe // block_count
        far_block = safe - other * block_count
        key = jnp.where(me < other, row * block_count + far_block, far_block * block_count + row)
        return listed >= 0, other, key

    def collect(entry, carry):
        row = entry // (positions - 1)
        live, other, key = entry_key(row, entry - row * (positions - 1))

        @pl.when(live)
        def _():
            first_ref[other] = jnp.minimum(first_ref[other], key)
            last_ref[other] = jnp.maximum(last_ref[other], key)

        return carry

    lax.fori_loop(0, block_count * (positions - 1), collect, 0)

    def tabulate(entry, carry):
        row = entry // (positions - 1)
        live, other, key = entry_key(row, entry - row * (positions - 1))
        spare = jnp.where(me == 0, 1, 0)
        is_first = key == first_ref[other]
        handled = jnp.where(me < other, first_ref[other], last_ref[other])
        weight = jnp.where(first_ref[other] == last_ref[other], 1, 2)
        table_ref[0, entry] = jnp.where(live, other, spare)
        table_ref[1, entry] = jnp.where(live & jnp.logical_not(is_first), capacity - 1, 0)
        table_ref[2, entry] = jnp.where(live & (key == handled), weight, 0)
        return carry

    lax.fori_loop(0, block_count * (positions - 1), tabulate, 0)

    def mine(key, other):
        block = jnp.where(me < other, key // block_count, key % block_count)
        return jnp.where((key >= 0) & (key < block_count * block_count), block, 0)

    stores = []
    diagonal_mask = on_diagonal(tile)
    for row in range(block_count):
        wait_all(loads[row])
        block = pl.ds(row * tile, tile)
        total = jnp.where(diagonal_mask, variance_ref[row:row + 1, :], kinship_ref[row, 0])
        for position in range(1, positions):
            total = total + kinship_ref[row, position]
        diagonal = jnp.sum(total, axis=1, keepdims=True)
        diagonal_ref[block, :] = diagonal
        direction_ref[block, :] = phenotypes_ref[block, :] / diagonal
    for k in range(1, devices):
        other = me ^ k
        keys = (first_ref[other], last_ref[other])
        blocks = [mine(key, other) for key in keys]
        table_ref[3, k] = jnp.where(me < other, blocks[1], blocks[0])
        for slot in range(capacity):
            start = pl.multiple_of(blocks[slot] * tile, tile)
            stores.append(copies.start(direction_ref.at[pl.ds(start, tile)], outgoing_hbm[k - 1].at[slot]))
    stores.append(copies.start(direction_ref, direction_hbm))
    wait_all(stores)


def apply_kernel(devices, capacity, place_ref, table_ref, kinship_hbm, direction_hbm, diagonal_ref, phenotypes_hbm,
                 *refs):
    received_hbm, refs = refs[:devices - 1], refs[devices - 1:]
    scaled_hbm, sums_ref = refs[:2]
    outgoing_hbm, refs = refs[2:2 + devices - 1], refs[2 + devices - 1:]
    kinship_ref, direction_ref, phenotypes_ref, received_ref, scaled_ref, mapped_ref, semaphores = refs
    block_count, positions, tile = kinship_ref.shape[:3]
    columns = direction_ref.shape[1]
    me = place_ref[0]
    copies = Copies(semaphores)
    loads = [
        copies.start(kinship_hbm, kinship_ref),
        copies.start(direction_hbm, direction_ref),
        copies.start(phenotypes_hbm, phenotypes_ref),
    ]
    arrivals = [copies.start(received_hbm[k - 1], received_ref.at[me ^ k]) for k in range(1, devices)]
    wait_all(loads)
    diagonal_mask = on_diagonal(tile)
    norm = jnp.zeros((SUBLANES, columns), jnp.float32)
    cross = jnp.zeros((SUBLANES, columns), jnp.float32)
    for row in range(block_count):
        block = pl.ds(row * tile, tile)
        here = direction_ref[block, :]
        norm = norm + column_sums(here * phenotypes_ref[block, :])
        mapped_ref[block, :] = product(jnp.where(diagonal_mask, 0.0, kinship_ref[row, 0]), here)
    wait_all(arrivals)
    for row in range(block_count):
        block = pl.ds(row * tile, tile)
        mapped = mapped_ref[block, :]
        for position in range(1, positions):
            entry = row * (positions - 1) + position - 1
            there = received_ref[table_ref[0, entry], table_ref[1, entry]]
            mapped = mapped + product(kinship_ref[row, position], there)
        scaled_ref[block, :] = mapped / diagonal_ref[block, :]
        cross = cross + column_sums(direction_ref[block, :] * mapped)
    sums_ref[...] = jnp.zeros_like(sums_ref)
    sums_ref[0:1, :] = jnp.sum(norm, axis=0, keepdims=True)
    sums_ref[1:2, :] = jnp.sum(cross, axis=0, keepdims=True)
    stores = []
    for k in range(1, devices):
        start = pl.multiple_of(table_ref[3, k] * tile, tile)
        stores.append(copies.start(scaled_ref.at[pl.ds(start, tile)], outgoing_hbm[k - 1].at[pl.ds(0, tile)]))
        stores.append(copies.start(sums_ref, outgoing_hbm[k - 1].at[pl.ds(tile, SUBLANES)]))
    stores.append(copies.start(scaled_ref, scaled_hbm))
    wait_all(stores)


def curvature_kernel(devices, capacity, place_ref, table_ref, kinship_hbm, direction_hbm, diagonal_ref, scaled_hbm,
                     first_sums_ref, *refs):
    received_hbm, refs = refs[:devices - 1], refs[devices - 1:]
    later_hbm, refs = refs[:devices - 1], refs[devices - 1:]
    sums_ref, kinship_ref, direction_ref, scaled_ref, received_ref, later_ref, semaphores = refs
    block_count, positions, tile = kinship_ref.shape[:3]
    columns = direction_ref.shape[1]
    me = place_ref[0]
    copies = Copies(semaphores)
    loads = [copies.start(later_hbm[k - 1], later_ref.at[me ^ k]) for k in range(1, devices)]
    loads += [
        copies.start(kinship_hbm, kinship_ref),
        copies.start(direction_hbm, direction_ref),
        copies.start(scaled_hbm, scaled_ref),
    ]
    arrivals = [copies.start(received_hbm[k - 1], received_ref.at[me ^ k]) for k in range(1, devices)]
    wait_all(loads)
    first_sums = first_sums_ref[...]
    for k in range(1, devices):
        first_sums = first_sums + later_ref[me ^ k, pl.ds(tile, SUBLANES), :]
    rho = first_sums[1:2, :] / first_sums[0:1, :]
    diagonal_mask = on_diagonal(tile)
    norm = jnp.zeros((SUBLANES, columns), jnp.float32)
    bend = jnp.zeros((SUBLANES, columns), jnp.float32)
    for row in range(block_count):
        block = pl.ds(row * tile, tile)
        here = scaled_ref[block, :] - rho * direction_ref[block, :]
        scaled_ref[block, :] = here
        norm = norm + column_sums(here * here * diagonal_ref[block, :])
        bend = bend + column_sums(here * product(jnp.where(diagonal_mask, 0.0, kinship_ref[row, 0]), here))
    wait_all(arrivals)
    for row in range(block_count):
        mapped = jnp.zeros((tile, columns), jnp.float32)
        for position in range(1, positions):
            entry = row * (positions - 1) + position - 1
            other = table_ref[0, entry]
            weight = table_ref[2, entry].astype(jnp.float32)
            there = weight * (
                later_ref[other, pl.ds(0, tile), :] - rho * received_ref[other, table_ref[1, entry]]
            )
            mapped = mapped + product(kinship_ref[row, position], there)
        bend = bend + column_sums(scaled_ref[pl.ds(row * tile, tile), :] * mapped)
    sums_ref[...] = first_sums
    sums_ref[2:3, :] = jnp.sum(norm, axis=0, keepdims=True)
    sums_ref[3:4, :] = jnp.sum(bend, axis=0, keepdims=True)


def coefficients(own, shares):
    norm, cross = own[0:1, :], own[1:2, :]
    total = shares[0]
    for other in shares[1:]:
        total = total + other
    later_norm, bend = total[2:3, :], total[3:4, :]
    curve = norm + cross
    ratio = later_norm / curve
    step = jnp.where(later_norm > 0, later_norm / (later_norm + bend - later_norm * ratio), 0.0)
    start = norm / curve
    return start * (1.0 + step * (ratio + cross / norm)), -start * step


def finish_kernel(devices, norm_scale, place_ref, direction_hbm, scaled_hbm, direction_scores_hbm, scaled_scores_hbm,
                  sums_hbm, *refs):
    others = 2 * devices - 1
    others_hbm, refs = refs[:others], refs[others:]
    (solved_hbm, scores_ref, direction_ref, scaled_ref, direction_scores_ref, scaled_scores_ref, sums_ref,
     semaphores) = refs
    people, columns = direction_ref.shape
    copies = Copies(semaphores)
    arrivals = [copies.start(sums_hbm, sums_ref.at[0])]
    arrivals += [copies.start(others_hbm[i], sums_ref.at[i + 1]) for i in range(others)]
    loads = [
        copies.start(direction_hbm, direction_ref),
        copies.start(scaled_hbm, scaled_ref),
        copies.start(direction_scores_hbm, direction_scores_ref),
        copies.start(scaled_scores_hbm, scaled_scores_ref),
    ]
    wait_all(arrivals)
    own = [sums_ref[i] for i in range(devices)]
    other = [sums_ref[devices + i] for i in range(devices)]
    along, across = coefficients(own[0], own)
    other_along, other_across = coefficients(other[0], other)
    wait_all(loads)
    stores = []
    rows = people // 4
    for part in range(4):
        block = pl.ds(part * rows, rows)
        direction_ref[block, :] = along * direction_ref[block, :] + across * scaled_ref[block, :]
        stores.append(copies.start(direction_ref.at[block], solved_hbm.at[block]))
    column = place_ref[1]
    for start, first, second, offset in (
        (0, along, across, column * columns),
        (columns, other_along, other_across, (1 - column) * columns),
    ):
        here = pl.ds(start, columns)
        scores_ref[:, pl.ds(pl.multiple_of(offset, columns), columns)] = norm_scale * (
            first * direction_scores_ref[:, here] + second * scaled_scores_ref[:, here]
        )
    wait_all(stores)


def call(kernel, out_shape, in_specs, out_specs, scratch_shapes):
    return pl.pallas_call(
        kernel,
        out_shape=out_shape,
        in_specs=in_specs,
        out_specs=out_specs,
        scratch_shapes=list(scratch_shapes),
        compiler_params=pltpu.CompilerParams(vmem_limit_bytes=VMEM_LIMIT),
    )


def swap(values, axis, devices, step):
    return lax.ppermute(values, axis, [(i, i ^ step) for i in range(devices)])


def share(values, devices):
    me = lax.axis_index("samples")
    rows = values.shape[0] // devices
    values = values.reshape(devices, rows, -1)
    step = 1
    while step < devices:
        bit = (me // step) % 2
        halves = values.reshape(-1, 2, rows, values.shape[-1])
        kept = lax.dynamic_index_in_dim(halves, bit, 1, keepdims=False)
        given = lax.dynamic_index_in_dim(halves, 1 - bit, 1, keepdims=False)
        values = kept + swap(given, "samples", devices, step)
        step *= 2
    return values.reshape(rows, -1)


def per_device(kinship, relatives, variance, phenotypes, dosage):
    devices = lax.axis_size("samples")
    place = jnp.stack([lax.axis_index("samples"), lax.axis_index("cols")]).astype(jnp.int32)
    block_count, positions, tile = kinship.shape[:3]
    people, columns = phenotypes.shape
    variants = dosage.shape[1]
    entries = block_count * (positions - 1)
    capacity = -(-entries // (devices - 1))
    assert capacity <= 2
    anywhere = pl.BlockSpec(memory_space=pl.ANY)
    vmem = pl.BlockSpec(memory_space=pltpu.VMEM)
    smem = pl.BlockSpec(memory_space=pltpu.SMEM)
    float_of = lambda *shape: jax.ShapeDtypeStruct(shape, jnp.float32)
    room = lambda *shape: pltpu.VMEM(shape, jnp.float32)
    full = float_of(people, columns)
    full_room = room(people, columns)
    peers = devices - 1
    direction, diagonal, table, *outgoing = call(
        functools.partial(prepare_kernel, devices, capacity),
        [
            full,
            float_of(people, 1),
            jax.ShapeDtypeStruct((4, max(entries, devices)), jnp.int32),
        ] + [float_of(capacity, tile, columns)] * peers,
        [smem, smem, anywhere, vmem, anywhere],
        [anywhere, vmem, smem] + [anywhere] * peers,
        [
            room(*kinship.shape), full_room, full_room,
            pltpu.SMEM((devices,), jnp.int32), pltpu.SMEM((devices,), jnp.int32),
            pltpu.SemaphoreType.DMA((2 * block_count + capacity * peers + 1,)),
        ],
    )(place, relatives, kinship, variance.reshape(block_count, tile), phenotypes)

    def exchange(blocks):
        return [swap(blocks[k - 1], "samples", devices, k) for k in range(1, devices)]

    def variant_sums(values):
        both = jnp.concatenate([values, swap(values, "cols", 2, 1)], axis=1)
        partial = lax.dot_general(
            dosage, both, (((0,), (0,)), ((), ())), precision=lax.Precision.HIGH,
            preferred_element_type=jnp.float32,
        )
        return share(partial, devices)

    received = exchange(outgoing)
    direction_scores = variant_sums(direction)
    scaled, first_sums, *outgoing = call(
        functools.partial(apply_kernel, devices, capacity),
        [full, float_of(SUBLANES, columns)] + [float_of(tile + SUBLANES, columns)] * peers,
        [smem, smem, anywhere, anywhere, vmem, anywhere] + [anywhere] * peers,
        [anywhere, vmem] + [anywhere] * peers,
        [
            room(*kinship.shape), full_room, full_room, room(devices, capacity, tile, columns), full_room, full_room,
            pltpu.SemaphoreType.DMA((3 * peers + 4,)),
        ],
    )(place, table, kinship, direction, diagonal, phenotypes, *received)
    later = exchange(outgoing)
    scaled_scores = variant_sums(scaled)
    sums = call(
        functools.partial(curvature_kernel, devices, capacity),
        float_of(SUBLANES, columns),
        [smem, smem, anywhere, anywhere, vmem, anywhere, vmem] + [anywhere] * (2 * peers),
        vmem,
        [
            room(*kinship.shape), full_room, full_room, room(devices, capacity, tile, columns),
            room(devices, tile + SUBLANES, columns),
            pltpu.SemaphoreType.DMA((2 * peers + 3,)),
        ],
    )(place, table, kinship, direction, diagonal, scaled, first_sums, *received, *later)
    others = [swap(sums, ("samples", "cols"), 2 * devices, 2 * k) for k in range(1, devices)]
    others += [swap(sums, ("samples", "cols"), 2 * devices, 2 * k + 1) for k in range(devices)]
    solved, scores = call(
        functools.partial(finish_kernel, devices, 1.0 / math.sqrt(people * devices)),
        [full, float_of(variants // devices, 2 * columns)],
        [smem] + [anywhere] * (5 + len(others)),
        [anywhere, vmem],
        [
            full_room, full_room, room(variants // devices, 2 * columns), room(variants // devices, 2 * columns),
            room(2 * devices, SUBLANES, columns),
            pltpu.SemaphoreType.DMA((2 * devices + 8,)),
        ],
    )(place, direction, scaled, direction_scores, scaled_scores, sums, *others)
    return (solved, scores)


def solution(mesh):
    return jax.shard_map(
        per_device,
        mesh=mesh,
        in_specs=(
            P(("groups", "samples"), None, None, None),
            P("groups", None),
            P(("groups", "samples")),
            P(("groups", "samples"), "cols"),
            P(("groups", "samples"), "cols"),
        ),
        out_specs=(P(("groups", "samples"), "cols"), P(("groups", "cols", "samples"), None)),
        check_vma=False,
    )
```

time: 209 us -> 169 us (0.81)
  blocking collectives: 72.7 us -> 0 us
  starting transfers between devices: 18.2 us -> 70.1 us
  waiting for transfers between devices: 66 us -> 52.6 us
  between operations: 14.3 us -> 0.96 us
  Pallas kernels: 6.56 us -> 16.5 us
  other arithmetic: 6 us -> 2.45 us
    all_gather x2 -> x0, blocking collectives: 72.7 us -> none  [the longest x1 43.8 us: per_device(): all_first = lax.all_gather(first_sums, ('cols', 'samples'), axis=0)]
    ppermute x6 -> x37, starting transfers between devices: 6.62 us -> 70.1 us  [swap(): return lax.ppermute(values, axis, [(i, i ^ step) for i in range(devices)])]
    all_to_all x2 -> x0, waiting for transfers between devices: 29 us -> none  [per_device(): lax.all_to_all(outgoing, 'samples', split_axis=0, concat_axis=0, tiled=True)]
    ppermute x6 -> x37, waiting for transfers between devices: 23.7 us -> 52.6 us  [swap(): return lax.ppermute(values, axis, [(i, i ^ step) for i in range(devices)])]
    all_gather x2 -> x0, waiting for transfers between devices: 12.7 us -> none  [variant_sums(): both = lax.all_gather(values, 'cols', axis=1, tiled=True)]
    all_to_all x2 -> x0, starting transfers between devices: 11.5 us -> none  [per_device(): lax.all_to_all(outgoing, 'samples', split_axis=0, concat_axis=0, tiled=True)]
    pallas_call x3 -> x4, Pallas kernels: 6.56 us -> 16.5 us  [the longest x1 6.07 us: per_device(): call(functools.partial(prepare_kernel, devices, capacity), [full, float_o...]
    unnamed x41 -> x73, local copies, waits for them, and re-layouts: 16.9 us -> 19.3 us
  transfers between devices with their start and end apart: 10 -> 37, of which waited for: 5 -> 12; matrix products, arithmetic and copies ran while one was open for 6% -> 5% of each run, Pallas kernels for 2% -> 4%
where the time goes in v2:
time: 169 us; the launch traced here: 168 us
  starting transfers between devices  70.1 us (41%)
  waiting for transfers between devices  52.6 us (31%)
  local copies, waits for them, and re-layouts  21.2 us (13%)
  Pallas kernels  16.5 us (10%)
  matrix products  4.13 us (2%)
  other arithmetic  2.45 us (1%)
    ppermute x37, starting transfers between devices, swap(): return lax.ppermute(values, axis, [(i, i ^ step) for i in range(devices)])  70.1 us
    ppermute x37, waiting for transfers between devices, swap(): return lax.ppermute(values, axis, [(i, i ^ step) for i in range(devices)])  52.6 us
    unnamed x73, local copies, waits for them, and re-layouts  19.3 us
    pallas_call x1, Pallas kernels, per_device(): call(functools.partial(prepare_kernel, devices, capacity), [full, float_o...  6.07 us
    dot_general x2, matrix products, variant_sums(): lax.dot_general(dosage, both, (((0,), (0,)), ((), ())), precision=lax.Pre...  4.13 us
    pallas_call x1, Pallas kernels, per_device(): call(functools.partial(curvature_kernel, devices, capacity), float_of(SUB...  3.77 us
    pallas_call x1, Pallas kernels, per_device(): call(functools.partial(apply_kernel, devices, capacity), [full, float_of(...  3.69 us
  transfers between devices with their start and end apart: 37, of which 12 were waited for; matrix products, arithmetic and copies ran while one was open for 5% of the time, Pallas kernels for 4%

profile of v2, /device:TPU:0, one launch (start us, length us, event | category | flops | bytes accessed | tf_op | source)
XLA Modules:
  0.0 167.9 jit_solution(6331185549552868101)
XLA Ops:
  4.5 6.1 %shard_map.68 = (f32[512,256]{1,0:T(8,128)S(1)}, f32[512,1]{1,0:T(8,128)S(1)}, s32[4,12]{1,0:T(4,128)S(1)}, f32[2,128,256]{2,1,0:T(8,128)S(1)}, f32[2,128,256]{2...) custom-call(s32[2]{0:T(128)S(1)} %pad_add_fusion.place_ref, ...), custom_call_target="tpu_custom_call" | custom-call | tf_op jit(solution)/shard_map/pallas_call | solution.py:329
  10.5 3.0 %collective-permute-start = (f32[2,128,256]{2,1,0:T(8,128)S(1)}, f32[2,128,256]{2,1,0:T(8,128)S(1)}, u32[]{:S(2)}, u32[]{:S(2)}) collective-permute-start(f32[2,128,256]{2,1,0:T(8,128)S(1)} %get-tuple-element.24), channel_id=1, source_target_pairs={{0,2},{2,0},{4,6},{6,4},{8,10},{10,8},{12,14},{14,12},{1,3},{3,1},... | collective-permute-start | bytes 786440 | tf_op jit(solution)/shard_map/ppermute | solution.py:294
  15.2 3.0 %collective-permute-start.3 = (f32[2,128,256]{2,1,0:T(8,128)S(1)}, f32[2,128,256]{2,1,0:T(8,128)S(1)}, u32[]{:S(2)}, u32[]{:S(2)}) collective-permute-start(f32[2,128,256]{2,1,0:T(8,128)S(1)} %get-tuple-element.27), channel_id=1, source_target_pairs={{0,8},{2,10},{4,12},{6,14},{8,0},{10,2},{12,4},{14,6},{1,9},{3,11}... | collective-permute-start | bytes 786440 | tf_op jit(solution)/shard_map/ppermute | solution.py:294
  19.9 4.0 %collective-permute-start.4 = (f32[2,128,256]{2,1,0:T(8,128)S(1)}, f32[2,128,256]{2,1,0:T(8,128)S(1)}, u32[]{:S(2)}, u32[]{:S(2)}) collective-permute-start(f32[2,128,256]{2,1,0:T(8,128)S(1)} %get-tuple-element.28), channel_id=1, source_target_pairs={{0,10},{2,8},{4,14},{6,12},{8,2},{10,0},{12,6},{14,4},{1,11},{3,9}... | collective-permute-start | bytes 786440 | tf_op jit(solution)/shard_map/ppermute | solution.py:294
  23.9 8.4 %collective-permute-done.1.refs_1_ = f32[2,128,256]{2,1,0:T(8,128)S(1)} collective-permute-done((f32[2,128,256]{2,1,0:T(8,128)S(1)}, f32[2,128,256]{2,1,0:T(8,128)S(1)}, u32[]{:S(2)}, u32[]{:S(2)}) %collective-permute-start.1) | collective-permute-done | bytes 262176 | tf_op jit(solution)/shard_map/ppermute | solution.py:294
  35.2 3.5 %collective-permute-start.6 = (f32[2,128,256]{2,1,0:T(8,128)S(1)}, f32[2,128,256]{2,1,0:T(8,128)S(1)}, u32[]{:S(2)}, u32[]{:S(2)}) collective-permute-start(f32[2,128,256]{2,1,0:T(8,128)S(1)} %get-tuple-element.30), channel_id=1, source_target_pairs={{0,14},{2,12},{4,10},{6,8},{8,6},{10,4},{12,2},{14,0},{1,15},{3,13... | collective-permute-start | bytes 786440 | tf_op jit(solution)/shard_map/ppermute | solution.py:294
  38.7 15.9 %collective-permute-done.4.refs_4_ = f32[2,128,256]{2,1,0:T(8,128)S(1)} collective-permute-done((f32[2,128,256]{2,1,0:T(8,128)S(1)}, f32[2,128,256]{2,1,0:T(8,128)S(1)}, u32[]{:S(2)}, u32[]{:S(2)}) %collective-permute-start.4) | collective-permute-done | bytes 262176 | tf_op jit(solution)/shard_map/ppermute | solution.py:294
  54.7 3.7 %shard_map.69 = (f32[512,256]{1,0:T(8,128)S(1)}, f32[8,256]{1,0:T(8,128)S(1)}, f32[136,256]{1,0:T(8,128)S(1)}, f32[136,256]{1,0:T(8,128)S(1)}, f32[136,256]{1,0:...) custom-call(s32[2]{0:T(128)S(1)} %pad_add_fusion.place_ref, ...), custom_call_target="tpu_custom_call" | custom-call | tf_op jit(solution)/shard_map/pallas_call | solution.py:358
  62.2 11.7 %collective-permute-start.16 = (f32[136,256]{1,0:T(8,128)}, f32[136,256]{1,0:T(8,128)S(1)}, u32[]{:S(2)}, u32[]{:S(2)}) collective-permute-start(f32[136,256]{1,0:T(8,128)} %copy-done.29), channel_id=1, source_target_pairs={{0,4},{2,6},{4,0},{6,2},{8,12},{10,14},{12,8},{14,10},{1,5},{3,7},... | collective-permute-start | bytes 417800 | tf_op jit(solution)/shard_map/ppermute | solution.py:294
  74.5 4.2 %collective-permute-start.18 = (f32[136,256]{1,0:T(8,128)}, f32[136,256]{1,0:T(8,128)S(1)}, u32[]{:S(2)}, u32[]{:S(2)}) collective-permute-start(f32[136,256]{1,0:T(8,128)} %copy-done.27), channel_id=1, source_target_pairs={{0,8},{2,10},{4,12},{6,14},{8,0},{10,2},{12,4},{14,6},{1,9},{3,11}... | collective-permute-start | bytes 417800 | tf_op jit(solution)/shard_map/ppermute | solution.py:294
  78.7 2.1 %fusion = f32[512,512]{0,1:T(8,128)S(1)} fusion(f32[512,512]{1,0:T(8,128)S(1)} %copy-done, f32[512,256]{1,0:T(8,128)} %collective-permute-done.7, f32[512,256]{1,0:T(8,128)S(1)} %get-tuple-element.21.direction_hbm), kind=kOutput, calls=%fused_computation | convolution fusion | flops 805568512 | bytes 3145728 | tf_op jit(solution)/shard_map/dot_general | solution.py:350
  82.5 2.1 %fusion.4 = f32[512,512]{0,1:T(8,128)S(1)} fusion(f32[512,512]{1,0:T(8,128)S(1)} %copy-done, f32[512,256]{1,0:T(8,128)} %collective-permute-done.11, f32[512,256]{1,0:T(8,128)S(1)} %get-tuple-element.31.scaled_hbm), kind=kOutput, calls=%fused_computation.4 | convolution fusion | flops 805568512 | bytes 3145728 | tf_op jit(solution)/shard_map/dot_general | solution.py:350
  88.3 2.4 %collective-permute-start.20 = (f32[136,256]{1,0:T(8,128)}, f32[136,256]{1,0:T(8,128)}, u32[]{:S(2)}, u32[]{:S(2)}) collective-permute-start(f32[136,256]{1,0:T(8,128)} %get-tuple-element.38), channel_id=1, source_target_pairs={{0,12},{2,14},{4,8},{6,10},{8,4},{10,6},{12,0},{14,2},{1,13},{3,15... | collective-permute-start | bytes 417800 | tf_op jit(solution)/shard_map/ppermute | solution.py:294
  91.4 2.4 %collective-permute-start.21 = (f32[136,256]{1,0:T(8,128)}, f32[136,256]{1,0:T(8,128)}, u32[]{:S(2)}, u32[]{:S(2)}) collective-permute-start(f32[136,256]{1,0:T(8,128)} %get-tuple-element.39), channel_id=1, source_target_pairs={{0,14},{2,12},{4,10},{6,8},{8,6},{10,4},{12,2},{14,0},{1,15},{3,13... | collective-permute-start | bytes 417800 | tf_op jit(solution)/shard_map/ppermute | solution.py:294
  93.7 9.0 %collective-permute-done.19.refs_11_ = f32[136,256]{1,0:T(8,128)} collective-permute-done((f32[136,256]{1,0:T(8,128)}, f32[136,256]{1,0:T(8,128)}, u32[]{:S(2)}, u32[]{:S(2)}) %collective-permute-start.19) | collective-permute-done | bytes 139296 | tf_op jit(solution)/shard_map/ppermute | solution.py:294
  112.8 3.8 %shard_map.70.sums_hbm = f32[8,256]{1,0:T(8,128)S(1)} custom-call(s32[2]{0:T(128)S(1)} %pad_add_fusion.place_ref, s32[4,12]{1,0:T(4,128)S(1)} %get-tuple-element.22.table_ref, f32[4,4,128,128]{3,2,1,0:T(8,128)S(1)} %copy-done.2, f32[512,256]{1,0:T(8,128)S(1)} %get-tuple-element.21.direction_hbm, f32[512,1]{1,0:T(8,128)S(1)} %get-tuple-element.23.diagonal_ref, ...), custom_call_target="tpu_custom_call" | custom-call | tf_op jit(solution)/shard_map/pallas_call | solution.py:370
  117.1 6.3 %collective-permute-start.23 = (f32[8,256]{1,0:T(8,128)S(1)}, f32[8,256]{1,0:T(8,128)S(1)}, u32[]{:S(2)}, u32[]{:S(2)}) collective-permute-start(f32[8,256]{1,0:T(8,128)S(1)} %shard_map.70.sums_hbm), channel_id=1, source_target_pairs={{0,4},{1,5},{2,6},{3,7},{4,0},{5,1},{6,2},{7,3},{8,12},{9,13},{10,... | collective-permute-start | bytes 24584 | tf_op jit(solution)/shard_map/ppermute | solution.py:294
  128.8 4.3 %collective-permute-done.9 = f32[2,64,512]{2,1,0:T(8,128)S(1)} collective-permute-done((f32[2,64,512]{2,1,0:T(8,128)S(1)}, f32[2,64,512]{2,1,0:T(8,128)S(1)}, u32[]{:S(2)}, u32[]{:S(2)}) %collective-permute-start.9) | collective-permute-done | bytes 262176 | tf_op jit(solution)/shard_map/ppermute | solution.py:294
  134.7 4.7 %collective-permute-done.13 = f32[2,64,512]{2,1,0:T(8,128)S(1)} collective-permute-done((f32[2,64,512]{2,1,0:T(8,128)S(1)}, f32[2,64,512]{2,1,0:T(8,128)S(1)}, u32[]{:S(2)}, u32[]{:S(2)}) %collective-permute-start.13) | collective-permute-done | bytes 262176 | tf_op jit(solution)/shard_map/ppermute | solution.py:294
  139.4 3.2 %collective-permute-start.10 = (f32[1,64,512]{2,1,0:T(8,128)S(1)}, f32[1,64,512]{2,1,0:T(8,128)S(1)}, u32[]{:S(2)}, u32[]{:S(2)}) collective-permute-start(f32[1,64,512]{2,1,0:T(8,128)S(1)} %constant_dynamic-slice_fusion.1), channel_id=1, source_target_pairs={{0,8},{2,10},{4,12},{6,14},{8,0},{10,2},{12,4},{14,6},{1,9},{3,11}... | collective-permute-start | bytes 393224 | tf_op jit(solution)/shard_map/ppermute | solution.py:294
  142.9 3.3 %collective-permute-start.27 = (f32[8,256]{1,0:T(8,128)S(1)}, f32[8,256]{1,0:T(8,128)S(1)}, u32[]{:S(2)}, u32[]{:S(2)}) collective-permute-start(f32[8,256]{1,0:T(8,128)S(1)} %shard_map.70.sums_hbm), channel_id=1, source_target_pairs={{0,12},{1,13},{2,14},{3,15},{4,8},{5,9},{6,10},{7,11},{8,4},{9,5},... | collective-permute-start | bytes 24584 | tf_op jit(solution)/shard_map/ppermute | solution.py:294
  149.6 2.8 %collective-permute-start.14 = (f32[1,64,512]{2,1,0:T(8,128)S(1)}, f32[1,64,512]{2,1,0:T(8,128)S(1)}, u32[]{:S(2)}, u32[]{:S(2)}) collective-permute-start(f32[1,64,512]{2,1,0:T(8,128)S(1)} %constant_dynamic-slice_fusion), channel_id=1, source_target_pairs={{0,8},{2,10},{4,12},{6,14},{8,0},{10,2},{12,4},{14,6},{1,9},{3,11}... | collective-permute-start | bytes 393224 | tf_op jit(solution)/shard_map/ppermute | solution.py:294
  161.0 4.0 %collective-permute-done.36.refs_14_ = f32[8,256]{1,0:T(8,128)S(1)} collective-permute-done((f32[8,256]{1,0:T(8,128)S(1)}, f32[8,256]{1,0:T(8,128)S(1)}, u32[]{:S(2)}, u32[]{:S(2)}) %collective-permute-start.36) | collective-permute-done | bytes 8224 | tf_op jit(solution)/shard_map/ppermute | solution.py:294
  165.0 2.9 %shard_map.71 = (f32[512,256]{1,0:T(8,128)}, f32[64,512]{1,0:T(8,128)}) custom-call(s32[2]{0:T(128)S(1)} %pad_add_fusion.place_ref, f32[512,256]{1,0:T(8,128)S(1)} %get-tuple-element.21.direction_hbm, f32[512,256]{1,0:T(8,128)S(1)} %get-tuple-element.31.scaled_hbm, f32[64,512]{1,0:T(8,128)S(1)} %add_bitcast_fusion.1.direction_scores_hbm, ...), custom_call_target="tpu_custom_call" | custom-call | tf_op jit(solution)/shard_map/pallas_call | solution.py:383
  (142 shorter events, 50.4 us)
Async XLA Ops:
  10.5 9.3 %collective-permute-start = (f32[2,128,256]{2,1,0:T(8,128)S(1)}, f32[2,128,256]{2,1,0:T(8,128)S(1)}, u32[]{:S(2)}, u32[]{:S(2)}) collective-permute-start(f32[2,128,256]{2,1,0:T(8,128)S(1)} %get-tuple-element.24), channel_id=1, source_target_pairs={{0,2},{2,0},{4,6},{6,4},{8,10},{10,8},{12,14},{14,12},{1,3},{3,1},... | collective-permute-start | bytes 786440 | tf_op jit(solution)/shard_map/ppermute | solution.py:294
  13.6 18.8 %collective-permute-start.1 = (f32[2,128,256]{2,1,0:T(8,128)S(1)}, f32[2,128,256]{2,1,0:T(8,128)S(1)}, u32[]{:S(2)}, u32[]{:S(2)}) collective-permute-start(f32[2,128,256]{2,1,0:T(8,128)S(1)} %get-tuple-element.25), channel_id=1, source_target_pairs={{0,4},{2,6},{4,0},{6,2},{8,12},{10,14},{12,8},{14,10},{1,5},{3,7},... | collective-permute-start | bytes 786440 | tf_op jit(solution)/shard_map/ppermute | solution.py:294
  15.1 20.1 %collective-permute-start.2 = (f32[2,128,256]{2,1,0:T(8,128)S(1)}, f32[2,128,256]{2,1,0:T(8,128)S(1)}, u32[]{:S(2)}, u32[]{:S(2)}) collective-permute-start(f32[2,128,256]{2,1,0:T(8,128)S(1)} %get-tuple-element.26), channel_id=1, source_target_pairs={{0,6},{2,4},{4,2},{6,0},{8,14},{10,12},{12,10},{14,8},{1,7},{3,5},... | collective-permute-start | bytes 786440 | tf_op jit(solution)/shard_map/ppermute | solution.py:294
  15.2 59.4 %collective-permute-start.7 = (f32[512,256]{1,0:T(8,128)S(1)}, f32[512,256]{1,0:T(8,128)}, u32[]{:S(2)}, u32[]{:S(2)}) collective-permute-start(f32[512,256]{1,0:T(8,128)S(1)} %get-tuple-element.21.direction_hbm), channel_id=1, source_target_pairs={{0,1},{1,0},{2,3},{3,2},{4,5},{5,4},{6,7},{7,6},{8,9},{9,8},{10,11... | collective-permute-start | bytes 1572872 | tf_op jit(solution)/shard_map/ppermute | solution.py:294
  15.2 23.5 %collective-permute-start.3 = (f32[2,128,256]{2,1,0:T(8,128)S(1)}, f32[2,128,256]{2,1,0:T(8,128)S(1)}, u32[]{:S(2)}, u32[]{:S(2)}) collective-permute-start(f32[2,128,256]{2,1,0:T(8,128)S(1)} %get-tuple-element.27), channel_id=1, source_target_pairs={{0,8},{2,10},{4,12},{6,14},{8,0},{10,2},{12,4},{14,6},{1,9},{3,11}... | collective-permute-start | bytes 786440 | tf_op jit(solution)/shard_map/ppermute | solution.py:294
  19.9 34.8 %collective-permute-start.4 = (f32[2,128,256]{2,1,0:T(8,128)S(1)}, f32[2,128,256]{2,1,0:T(8,128)S(1)}, u32[]{:S(2)}, u32[]{:S(2)}) collective-permute-start(f32[2,128,256]{2,1,0:T(8,128)S(1)} %get-tuple-element.28), channel_id=1, source_target_pairs={{0,10},{2,8},{4,14},{6,12},{8,2},{10,0},{12,6},{14,4},{1,11},{3,9}... | collective-permute-start | bytes 786440 | tf_op jit(solution)/shard_map/ppermute | solution.py:294
  32.4 22.3 %collective-permute-start.5 = (f32[2,128,256]{2,1,0:T(8,128)S(1)}, f32[2,128,256]{2,1,0:T(8,128)S(1)}, u32[]{:S(2)}, u32[]{:S(2)}) collective-permute-start(f32[2,128,256]{2,1,0:T(8,128)S(1)} %get-tuple-element.29), channel_id=1, source_target_pairs={{0,12},{2,14},{4,8},{6,10},{8,4},{10,6},{12,0},{14,2},{1,13},{3,15... | collective-permute-start | bytes 786440 | tf_op jit(solution)/shard_map/ppermute | solution.py:294
  35.2 19.4 %collective-permute-start.6 = (f32[2,128,256]{2,1,0:T(8,128)S(1)}, f32[2,128,256]{2,1,0:T(8,128)S(1)}, u32[]{:S(2)}, u32[]{:S(2)}) collective-permute-start(f32[2,128,256]{2,1,0:T(8,128)S(1)} %get-tuple-element.30), channel_id=1, source_target_pairs={{0,14},{2,12},{4,10},{6,8},{8,6},{10,4},{12,2},{14,0},{1,15},{3,13... | collective-permute-start | bytes 786440 | tf_op jit(solution)/shard_map/ppermute | solution.py:294
  61.1 20.6 %collective-permute-start.11 = (f32[512,256]{1,0:T(8,128)S(1)}, f32[512,256]{1,0:T(8,128)}, u32[]{:S(2)}, u32[]{:S(2)}) collective-permute-start(f32[512,256]{1,0:T(8,128)S(1)} %get-tuple-element.31.scaled_hbm), channel_id=1, source_target_pairs={{0,1},{1,0},{2,3},{3,2},{4,5},{5,4},{6,7},{7,6},{8,9},{9,8},{10,11... | collective-permute-start | bytes 1572872 | tf_op jit(solution)/shard_map/ppermute | solution.py:294
  61.7 23.8 %collective-permute-start.15 = (f32[136,256]{1,0:T(8,128)}, f32[136,256]{1,0:T(8,128)S(1)}, u32[]{:S(2)}, u32[]{:S(2)}) collective-permute-start(f32[136,256]{1,0:T(8,128)} %copy-done.30), channel_id=1, source_target_pairs={{0,2},{2,0},{4,6},{6,4},{8,10},{10,8},{12,14},{14,12},{1,3},{3,1},... | collective-permute-start | bytes 417800 | tf_op jit(solution)/shard_map/ppermute | solution.py:294
  62.2 24.9 %collective-permute-start.16 = (f32[136,256]{1,0:T(8,128)}, f32[136,256]{1,0:T(8,128)S(1)}, u32[]{:S(2)}, u32[]{:S(2)}) collective-permute-start(f32[136,256]{1,0:T(8,128)} %copy-done.29), channel_id=1, source_target_pairs={{0,4},{2,6},{4,0},{6,2},{8,12},{10,14},{12,8},{14,10},{1,5},{3,7},... | collective-permute-start | bytes 417800 | tf_op jit(solution)/shard_map/ppermute | solution.py:294
  73.8 13.8 %collective-permute-start.17 = (f32[136,256]{1,0:T(8,128)}, f32[136,256]{1,0:T(8,128)S(1)}, u32[]{:S(2)}, u32[]{:S(2)}) collective-permute-start(f32[136,256]{1,0:T(8,128)} %copy-done.28), channel_id=1, source_target_pairs={{0,6},{2,4},{4,2},{6,0},{8,14},{10,12},{12,10},{14,8},{1,7},{3,5},... | collective-permute-start | bytes 417800 | tf_op jit(solution)/shard_map/ppermute | solution.py:294
  74.5 16.2 %collective-permute-start.18 = (f32[136,256]{1,0:T(8,128)}, f32[136,256]{1,0:T(8,128)S(1)}, u32[]{:S(2)}, u32[]{:S(2)}) collective-permute-start(f32[136,256]{1,0:T(8,128)} %copy-done.27), channel_id=1, source_target_pairs={{0,8},{2,10},{4,12},{6,14},{8,0},{10,2},{12,4},{14,6},{1,9},{3,11}... | collective-permute-start | bytes 417800 | tf_op jit(solution)/shard_map/ppermute | solution.py:294
  82.0 42.3 %collective-permute-start.8 = (f32[4,64,512]{2,1,0:T(8,128)}, f32[4,64,512]{2,1,0:T(8,128)}, u32[]{:S(2)}, u32[]{:S(2)}) collective-permute-start(f32[4,64,512]{2,1,0:T(8,128)} %dynamic-slice_bitcast_fusion.1), channel_id=1, source_target_pairs={{0,2},{2,0},{4,6},{6,4},{8,10},{10,8},{12,14},{14,12},{1,3},{3,1},... | collective-permute-start | bytes 1572872 | tf_op jit(solution)/shard_map/ppermute | solution.py:294
  85.5 41.1 %collective-permute-start.12 = (f32[4,64,512]{2,1,0:T(8,128)}, f32[4,64,512]{2,1,0:T(8,128)}, u32[]{:S(2)}, u32[]{:S(2)}) collective-permute-start(f32[4,64,512]{2,1,0:T(8,128)} %dynamic-slice_bitcast_fusion), channel_id=1, source_target_pairs={{0,2},{2,0},{4,6},{6,4},{8,10},{10,8},{12,14},{14,12},{1,3},{3,1},... | collective-permute-start | bytes 1572872 | tf_op jit(solution)/shard_map/ppermute | solution.py:294
  87.7 15.0 %collective-permute-start.19 = (f32[136,256]{1,0:T(8,128)}, f32[136,256]{1,0:T(8,128)}, u32[]{:S(2)}, u32[]{:S(2)}) collective-permute-start(f32[136,256]{1,0:T(8,128)} %get-tuple-element.37), channel_id=1, source_target_pairs={{0,10},{2,8},{4,14},{6,12},{8,2},{10,0},{12,6},{14,4},{1,11},{3,9}... | collective-permute-start | bytes 417800 | tf_op jit(solution)/shard_map/ppermute | solution.py:294
  88.3 14.4 %collective-permute-start.20 = (f32[136,256]{1,0:T(8,128)}, f32[136,256]{1,0:T(8,128)}, u32[]{:S(2)}, u32[]{:S(2)}) collective-permute-start(f32[136,256]{1,0:T(8,128)} %get-tuple-element.38), channel_id=1, source_target_pairs={{0,12},{2,14},{4,8},{6,10},{8,4},{10,6},{12,0},{14,2},{1,13},{3,15... | collective-permute-start | bytes 417800 | tf_op jit(solution)/shard_map/ppermute | solution.py:294
  91.4 11.3 %collective-permute-start.21 = (f32[136,256]{1,0:T(8,128)}, f32[136,256]{1,0:T(8,128)}, u32[]{:S(2)}, u32[]{:S(2)}) collective-permute-start(f32[136,256]{1,0:T(8,128)} %get-tuple-element.39), channel_id=1, source_target_pairs={{0,14},{2,12},{4,10},{6,8},{8,6},{10,4},{12,2},{14,0},{1,15},{3,13... | collective-permute-start | bytes 417800 | tf_op jit(solution)/shard_map/ppermute | solution.py:294
  116.6 26.1 %collective-permute-start.22 = (f32[8,256]{1,0:T(8,128)S(1)}, f32[8,256]{1,0:T(8,128)S(1)}, u32[]{:S(2)}, u32[]{:S(2)}) collective-permute-start(f32[8,256]{1,0:T(8,128)S(1)} %shard_map.70.sums_hbm), channel_id=1, source_target_pairs={{0,2},{1,3},{2,0},{3,1},{4,6},{5,7},{6,4},{7,5},{8,10},{9,11},{10,... | collective-permute-start | bytes 24584 | tf_op jit(solution)/shard_map/ppermute | solution.py:294
  117.1 25.8 %collective-permute-start.23 = (f32[8,256]{1,0:T(8,128)S(1)}, f32[8,256]{1,0:T(8,128)S(1)}, u32[]{:S(2)}, u32[]{:S(2)}) collective-permute-start(f32[8,256]{1,0:T(8,128)S(1)} %shard_map.70.sums_hbm), channel_id=1, source_target_pairs={{0,4},{1,5},{2,6},{3,7},{4,0},{5,1},{6,2},{7,3},{8,12},{9,13},{10,... | collective-permute-start | bytes 24584 | tf_op jit(solution)/shard_map/ppermute | solution.py:294
  123.4 22.8 %collective-permute-start.24 = (f32[8,256]{1,0:T(8,128)S(1)}, f32[8,256]{1,0:T(8,128)S(1)}, u32[]{:S(2)}, u32[]{:S(2)}) collective-permute-start(f32[8,256]{1,0:T(8,128)S(1)} %shard_map.70.sums_hbm), channel_id=1, source_target_pairs={{0,6},{1,7},{2,4},{3,5},{4,2},{5,3},{6,0},{7,1},{8,14},{9,15},{10,... | collective-permute-start | bytes 24584 | tf_op jit(solution)/shard_map/ppermute | solution.py:294
  124.3 23.2 %collective-permute-start.25 = (f32[8,256]{1,0:T(8,128)S(1)}, f32[8,256]{1,0:T(8,128)S(1)}, u32[]{:S(2)}, u32[]{:S(2)}) collective-permute-start(f32[8,256]{1,0:T(8,128)S(1)} %shard_map.70.sums_hbm), channel_id=1, source_target_pairs={{0,8},{1,9},{2,10},{3,11},{4,12},{5,13},{6,14},{7,15},{8,0},{9,1},... | collective-permute-start | bytes 24584 | tf_op jit(solution)/shard_map/ppermute | solution.py:294
  139.4 10.1 %collective-permute-start.10 = (f32[1,64,512]{2,1,0:T(8,128)S(1)}, f32[1,64,512]{2,1,0:T(8,128)S(1)}, u32[]{:S(2)}, u32[]{:S(2)}) collective-permute-start(f32[1,64,512]{2,1,0:T(8,128)S(1)} %constant_dynamic-slice_fusion.1), channel_id=1, source_target_pairs={{0,8},{2,10},{4,12},{6,14},{8,0},{10,2},{12,4},{14,6},{1,9},{3,11}... | collective-permute-start | bytes 393224 | tf_op jit(solution)/shard_map/ppermute | solution.py:294
  149.6 9.6 %collective-permute-start.14 = (f32[1,64,512]{2,1,0:T(8,128)S(1)}, f32[1,64,512]{2,1,0:T(8,128)S(1)}, u32[]{:S(2)}, u32[]{:S(2)}) collective-permute-start(f32[1,64,512]{2,1,0:T(8,128)S(1)} %constant_dynamic-slice_fusion), channel_id=1, source_target_pairs={{0,8},{2,10},{4,12},{6,14},{8,0},{10,2},{12,4},{14,6},{1,9},{3,11}... | collective-permute-start | bytes 393224 | tf_op jit(solution)/shard_map/ppermute | solution.py:294
  (49 other events, 379.7 us)

commit v3 on v2

--- a/solution.py
+++ b/solution.py
@@ -52,67 +52,64 @@
         copy.wait()
 
 
-def prepare_kernel(devices, capacity, place_ref, list_ref, kinship_hbm, variance_ref, phenotypes_hbm, *refs):
+def quotient(value, divisor):
+    if divisor & (divisor - 1) == 0:
+        return lax.shift_right_logical(value, jnp.int32(divisor.bit_length() - 1))
+    return lax.div(value, jnp.int32(divisor))
+
+
+def prepare_kernel(devices, capacity, list_ref, kinship_hbm, variance_hbm, phenotypes_hbm, *refs):
     direction_hbm, diagonal_ref, table_ref = refs[:3]
     outgoing_hbm = refs[3:3 + devices - 1]
-    kinship_ref, phenotypes_ref, direction_ref, first_ref, last_ref, semaphores = refs[3 + devices - 1:]
+    kinship_ref, variance_ref, phenotypes_ref, direction_ref, first_ref, last_ref, semaphores = refs[3 + devices - 1:]
     block_count, positions, tile = kinship_ref.shape[:3]
     copies = Copies(semaphores)
-    loads = []
+    loads = [copies.start(variance_hbm, variance_ref)]
     for row in range(block_count):
         block = pl.ds(row * tile, tile)
-        loads.append((
-            copies.start(kinship_hbm.at[row], kinship_ref.at[row]),
-            copies.start(phenotypes_hbm.at[block], phenotypes_ref.at[block]),
-        ))
-    me = place_ref[0]
+        loads.append(copies.start(kinship_hbm.at[row], kinship_ref.at[row]))
+        loads.append(copies.start(phenotypes_hbm.at[block], phenotypes_ref.at[block]))
+    me = lax.axis_index("samples")
+    spare = jnp.where(me == 0, 1, 0)
+    top = block_count * block_count
     for j in range(devices):
-        first_ref[j] = jnp.int32(block_count * block_count)
+        first_ref[j] = jnp.int32(top)
         last_ref[j] = jnp.int32(-1)
-
-    def entry_key(row, position):
-        listed = list_ref[me * block_count + row, position]
-        safe = jnp.maximum(listed, 0)
-        other = safe // block_count
-        far_block = safe - other * block_count
-        key = jnp.where(me < other, row * block_count + far_block, far_block * block_count + row)
-        return listed >= 0, other, key
-
-    def collect(entry, carry):
-        row = entry // (positions - 1)
-        live, other, key = entry_key(row, entry - row * (positions - 1))
-
-        @pl.when(live)
-        def _():
-            first_ref[other] = jnp.minimum(first_ref[other], key)
-            last_ref[other] = jnp.maximum(last_ref[other], key)
-
-        return carry
-
-    lax.fori_loop(0, block_count * (positions - 1), collect, 0)
-
-    def tabulate(entry, carry):
-        row = entry // (positions - 1)
-        live, other, key = entry_key(row, entry - row * (positions - 1))
-        spare = jnp.where(me == 0, 1, 0)
-        is_first = key == first_ref[other]
-        handled = jnp.where(me < other, first_ref[other], last_ref[other])
-        weight = jnp.where(first_ref[other] == last_ref[other], 1, 2)
+    entries = []
+    for row in range(block_count):
+        for position in range(positions - 1):
+            listed = list_ref[position, me * block_count + row]
+            live = listed >= 0
+            safe = jnp.maximum(listed, 0)
+            other = quotient(safe, block_count)
+            far_block = safe - other * block_count
+            key = jnp.where(me < other, row * block_count + far_block, far_block * block_count + row)
+            first_ref[other] = jnp.minimum(first_ref[other], jnp.where(live, key, top))
+            last_ref[other] = jnp.maximum(last_ref[other], jnp.where(live, key, -1))
+            entries.append((live, other, key))
+    for entry, (live, other, key) in enumerate(entries):
+        first, last = first_ref[other], last_ref[other]
+        handled = jnp.where(me < other, first, last)
+        weight = jnp.where(first == last, 1, 2)
         table_ref[0, entry] = jnp.where(live, other, spare)
-        table_ref[1, entry] = jnp.where(live & jnp.logical_not(is_first), capacity - 1, 0)
+        table_ref[1, entry] = jnp.where(live & (key != first), capacity - 1, 0)
         table_ref[2, entry] = jnp.where(live & (key == handled), weight, 0)
-        return carry
-
-    lax.fori_loop(0, block_count * (positions - 1), tabulate, 0)
 
     def mine(key, other):
-        block = jnp.where(me < other, key // block_count, key % block_count)
-        return jnp.where((key >= 0) & (key < block_count * block_count), block, 0)
-
+        lower = quotient(jnp.clip(key, 0, top - 1), block_count)
+        higher = jnp.clip(key, 0, top - 1) - lower * block_count
+        return jnp.where((key >= 0) & (key < top), jnp.where(me < other, lower, higher), 0)
+
+    blocks = []
+    for k in range(1, devices):
+        other = me ^ k
+        blocks.append((mine(first_ref[other], other), mine(last_ref[other], other)))
+        table_ref[3, k] = jnp.where(me < other, blocks[-1][1], blocks[-1][0])
     stores = []
     diagonal_mask = on_diagonal(tile)
-    for row in range(block_count):
-        wait_all(loads[row])
+    loads[0].wait()
+    for row in range(block_count):
+        wait_all(loads[1 + 2 * row:3 + 2 * row])
         block = pl.ds(row * tile, tile)
         total = jnp.where(diagonal_mask, variance_ref[row:row + 1, :], kinship_ref[row, 0])
         for position in range(1, positions):
@@ -121,18 +118,14 @@
         diagonal_ref[block, :] = diagonal
         direction_ref[block, :] = phenotypes_ref[block, :] / diagonal
     for k in range(1, devices):
-        other = me ^ k
-        keys = (first_ref[other], last_ref[other])
-        blocks = [mine(key, other) for key in keys]
-        table_ref[3, k] = jnp.where(me < other, blocks[1], blocks[0])
         for slot in range(capacity):
-            start = pl.multiple_of(blocks[slot] * tile, tile)
+            start = pl.multiple_of(blocks[k - 1][slot] * tile, tile)
             stores.append(copies.start(direction_ref.at[pl.ds(start, tile)], outgoing_hbm[k - 1].at[slot]))
     stores.append(copies.start(direction_ref, direction_hbm))
     wait_all(stores)
 
 
-def apply_kernel(devices, capacity, place_ref, table_ref, kinship_hbm, direction_hbm, diagonal_ref, phenotypes_hbm,
+def apply_kernel(devices, capacity, table_ref, kinship_hbm, direction_hbm, diagonal_ref, phenotypes_hbm,
                  *refs):
     received_hbm, refs = refs[:devices - 1], refs[devices - 1:]
     scaled_hbm, sums_ref = refs[:2]
@@ -140,7 +133,7 @@
     kinship_ref, direction_ref, phenotypes_ref, received_ref, scaled_ref, mapped_ref, semaphores = refs
     block_count, positions, tile = kinship_ref.shape[:3]
     columns = direction_ref.shape[1]
-    me = place_ref[0]
+    me = lax.axis_index("samples")
     copies = Copies(semaphores)
     loads = [
         copies.start(kinship_hbm, kinship_ref),
@@ -179,14 +172,14 @@
     wait_all(stores)
 
 
-def curvature_kernel(devices, capacity, place_ref, table_ref, kinship_hbm, direction_hbm, diagonal_ref, scaled_hbm,
+def curvature_kernel(devices, capacity, table_ref, kinship_hbm, direction_hbm, diagonal_ref, scaled_hbm,
                      first_sums_ref, *refs):
     received_hbm, refs = refs[:devices - 1], refs[devices - 1:]
     later_hbm, refs = refs[:devices - 1], refs[devices - 1:]
-    sums_ref, kinship_ref, direction_ref, scaled_ref, received_ref, later_ref, semaphores = refs
+    sums_hbm, kinship_ref, direction_ref, scaled_ref, received_ref, later_ref, all_sums_ref, semaphores = refs
     block_count, positions, tile = kinship_ref.shape[:3]
     columns = direction_ref.shape[1]
-    me = place_ref[0]
+    me = lax.axis_index("samples")
     copies = Copies(semaphores)
     loads = [copies.start(later_hbm[k - 1], later_ref.at[me ^ k]) for k in range(1, devices)]
     loads += [
@@ -221,9 +214,13 @@
             )
             mapped = mapped + product(kinship_ref[row, position], there)
         bend = bend + column_sums(scaled_ref[pl.ds(row * tile, tile), :] * mapped)
-    sums_ref[...] = first_sums
-    sums_ref[2:3, :] = jnp.sum(norm, axis=0, keepdims=True)
-    sums_ref[3:4, :] = jnp.sum(bend, axis=0, keepdims=True)
+    row_ids = lax.broadcasted_iota(jnp.int32, first_sums.shape, 0)
+    sums = jnp.where(row_ids == 2, jnp.sum(norm, axis=0, keepdims=True), first_sums)
+    sums = jnp.where(row_ids == 3, jnp.sum(bend, axis=0, keepdims=True), sums)
+    for i in range(2 * devices):
+        all_sums_ref[i] = sums
+    store = copies.start(all_sums_ref, sums_hbm)
+    store.wait()
 
 
 def coefficients(own, shares):
@@ -239,25 +236,23 @@
     return start * (1.0 + step * (ratio + cross / norm)), -start * step
 
 
-def finish_kernel(devices, norm_scale, place_ref, direction_hbm, scaled_hbm, direction_scores_hbm, scaled_scores_hbm,
-                  sums_hbm, *refs):
-    others = 2 * devices - 1
-    others_hbm, refs = refs[:others], refs[others:]
+def finish_kernel(devices, norm_scale, direction_hbm, scaled_hbm, direction_scores_hbm, scaled_scores_hbm, sums_hbm,
+                  *refs):
     (solved_hbm, scores_ref, direction_ref, scaled_ref, direction_scores_ref, scaled_scores_ref, sums_ref,
      semaphores) = refs
     people, columns = direction_ref.shape
+    column = lax.axis_index("cols")
     copies = Copies(semaphores)
-    arrivals = [copies.start(sums_hbm, sums_ref.at[0])]
-    arrivals += [copies.start(others_hbm[i], sums_ref.at[i + 1]) for i in range(others)]
+    arrival = copies.start(sums_hbm, sums_ref)
     loads = [
         copies.start(direction_hbm, direction_ref),
         copies.start(scaled_hbm, scaled_ref),
         copies.start(direction_scores_hbm, direction_scores_ref),
         copies.start(scaled_scores_hbm, scaled_scores_ref),
     ]
-    wait_all(arrivals)
-    own = [sums_ref[i] for i in range(devices)]
-    other = [sums_ref[devices + i] for i in range(devices)]
+    arrival.wait()
+    own = [sums_ref[2 * i + column] for i in range(devices)]
+    other = [sums_ref[2 * i + 1 - column] for i in range(devices)]
     along, across = coefficients(own[0], own)
     other_along, other_across = coefficients(other[0], other)
     wait_all(loads)
@@ -267,7 +262,6 @@
         block = pl.ds(part * rows, rows)
         direction_ref[block, :] = along * direction_ref[block, :] + across * scaled_ref[block, :]
         stores.append(copies.start(direction_ref.at[block], solved_hbm.at[block]))
-    column = place_ref[1]
     for start, first, second, offset in (
         (0, along, across, column * columns),
         (columns, other_along, other_across, (1 - column) * columns),
@@ -311,14 +305,14 @@
 
 def per_device(kinship, relatives, variance, phenotypes, dosage):
     devices = lax.axis_size("samples")
-    place = jnp.stack([lax.axis_index("samples"), lax.axis_index("cols")]).astype(jnp.int32)
     block_count, positions, tile = kinship.shape[:3]
     people, columns = phenotypes.shape
     variants = dosage.shape[1]
+    share_rows = variants // devices
     entries = block_count * (positions - 1)
     capacity = -(-entries // (devices - 1))
     assert capacity <= 2
-    anywhere = pl.BlockSpec(memory_space=pl.ANY)
+    hbm = pl.BlockSpec(memory_space=pltpu.HBM)
     vmem = pl.BlockSpec(memory_space=pltpu.VMEM)
     smem = pl.BlockSpec(memory_space=pltpu.SMEM)
     float_of = lambda *shape: jax.ShapeDtypeStruct(shape, jnp.float32)
@@ -333,64 +327,68 @@
             float_of(people, 1),
             jax.ShapeDtypeStruct((4, max(entries, devices)), jnp.int32),
         ] + [float_of(capacity, tile, columns)] * peers,
-        [smem, smem, anywhere, vmem, anywhere],
-        [anywhere, vmem, smem] + [anywhere] * peers,
+        [smem, hbm, hbm, hbm],
+        [hbm, vmem, smem] + [hbm] * peers,
         [
-            room(*kinship.shape), full_room, full_room,
+            room(*kinship.shape), room(block_count, tile), full_room, full_room,
             pltpu.SMEM((devices,), jnp.int32), pltpu.SMEM((devices,), jnp.int32),
-            pltpu.SemaphoreType.DMA((2 * block_count + capacity * peers + 1,)),
+            pltpu.SemaphoreType.DMA((2 * block_count + capacity * peers + 2,)),
         ],
-    )(place, relatives, kinship, variance.reshape(block_count, tile), phenotypes)
+    )(relatives.T, kinship, variance.reshape(block_count, tile), phenotypes)
 
     def exchange(blocks):
         return [swap(blocks[k - 1], "samples", devices, k) for k in range(1, devices)]
 
+    both_dosages = jnp.concatenate(
+        [values.reshape(people, devices, share_rows) for values in (dosage, swap(dosage, "cols", 2, 1))], axis=2
+    ).reshape(people, 2 * variants)
+
     def variant_sums(values):
-        both = jnp.concatenate([values, swap(values, "cols", 2, 1)], axis=1)
         partial = lax.dot_general(
-            dosage, both, (((0,), (0,)), ((), ())), precision=lax.Precision.HIGH,
+            both_dosages, values, (((0,), (0,)), ((), ())), precision=lax.Precision.HIGH,
             preferred_element_type=jnp.float32,
         )
-        return share(partial, devices)
+        total = share(partial, devices)
+        return jnp.concatenate([total[:share_rows], swap(total[share_rows:], "cols", 2, 1)], axis=1)
 
     received = exchange(outgoing)
     direction_scores = variant_sums(direction)
+    received, direction_scores = lax.optimization_barrier((received, direction_scores))
     scaled, first_sums, *outgoing = call(
         functools.partial(apply_kernel, devices, capacity),
         [full, float_of(SUBLANES, columns)] + [float_of(tile + SUBLANES, columns)] * peers,
-        [smem, smem, anywhere, anywhere, vmem, anywhere] + [anywhere] * peers,
-        [anywhere, vmem] + [anywhere] * peers,
+        [smem, hbm, hbm, vmem, hbm] + [hbm] * peers,
+        [hbm, vmem] + [hbm] * peers,
         [
             room(*kinship.shape), full_room, full_room, room(devices, capacity, tile, columns), full_room, full_room,
             pltpu.SemaphoreType.DMA((3 * peers + 4,)),
         ],
-    )(place, table, kinship, direction, diagonal, phenotypes, *received)
+    )(table, kinship, direction, diagonal, phenotypes, *received)
     later = exchange(outgoing)
     scaled_scores = variant_sums(scaled)
     sums = call(
         functools.partial(curvature_kernel, devices, capacity),
-        float_of(SUBLANES, columns),
-        [smem, smem, anywhere, anywhere, vmem, anywhere, vmem] + [anywhere] * (2 * peers),
-        vmem,
+        float_of(2 * devices, SUBLANES, columns),
+        [smem, hbm, hbm, vmem, hbm, vmem] + [hbm] * (2 * peers),
+        hbm,
         [
             room(*kinship.shape), full_room, full_room, room(devices, capacity, tile, columns),
-            room(devices, tile + SUBLANES, columns),
-            pltpu.SemaphoreType.DMA((2 * peers + 3,)),
+            room(devices, tile + SUBLANES, columns), room(2 * devices, SUBLANES, columns),
+            pltpu.SemaphoreType.DMA((2 * peers + 4,)),
         ],
-    )(place, table, kinship, direction, diagonal, scaled, first_sums, *received, *later)
-    others = [swap(sums, ("samples", "cols"), 2 * devices, 2 * k) for k in range(1, devices)]
-    others += [swap(sums, ("samples", "cols"), 2 * devices, 2 * k + 1) for k in range(devices)]
+    )(table, kinship, direction, diagonal, scaled, first_sums, *received, *later)
+    all_sums = lax.all_to_all(sums, ("samples", "cols"), split_axis=0, concat_axis=0, tiled=True)
     solved, scores = call(
         functools.partial(finish_kernel, devices, 1.0 / math.sqrt(people * devices)),
-        [full, float_of(variants // devices, 2 * columns)],
-        [smem] + [anywhere] * (5 + len(others)),
-        [anywhere, vmem],
+        [full, float_of(share_rows, 2 * columns)],
+        [hbm] * 5,
+        [hbm, vmem],
         [
-            full_room, full_room, room(variants // devices, 2 * columns), room(variants // devices, 2 * columns),
+            full_room, full_room, room(share_rows, 2 * columns), room(share_rows, 2 * columns),
             room(2 * devices, SUBLANES, columns),
-            pltpu.SemaphoreType.DMA((2 * devices + 8,)),
+            pltpu.SemaphoreType.DMA((9,)),
         ],
-    )(place, direction, scaled, direction_scores, scaled_scores, sums, *others)
+    )(direction, scaled, direction_scores, scaled_scores, all_sums)
     return (solved, scores)
 
 

time: 169 us -> 174 us (1.030)
  waiting for transfers between devices: 52.6 us -> 92.1 us
  starting transfers between devices: 70.1 us -> 50.9 us
  local copies, waits for them, and re-layouts: 21.2 us -> 7.56 us
  other arithmetic: 2.45 us -> 4.8 us
  matrix products: 4.13 us -> 1.99 us
    ppermute x37 -> x23, waiting for transfers between devices: 52.6 us -> 85.6 us  [swap(): return lax.ppermute(values, axis, [(i, i ^ step) for i in range(devices)])]
    ppermute x37 -> x23, starting transfers between devices: 70.1 us -> 44.4 us  [swap(): return lax.ppermute(values, axis, [(i, i ^ step) for i in range(devices)])]
    unnamed x73 -> x37, local copies, waits for them, and re-layouts: 19.3 us -> 5.9 us
    all_to_all x0 -> x1, starting transfers between devices: none -> 6.51 us  [per_device(): lax.all_to_all(sums, ('samples', 'cols'), split_axis=0, concat_axis=0, ti...]
    all_to_all x0 -> x1, waiting for transfers between devices: none -> 6.48 us  [per_device(): lax.all_to_all(sums, ('samples', 'cols'), split_axis=0, concat_axis=0, ti...]
    dot_general x2, matrix products: 4.13 us -> 1.99 us  [variant_sums(): lax.dot_general(both_dosages, values, (((0,), (0,)), ((), ())), precision...]
  transfers between devices with their start and end apart: 37 -> 24, of which waited for: 12 -> 12; matrix products, arithmetic and copies ran while one was open for 5% -> 1% of each run, Pallas kernels for 4% -> 6%
where the time goes in v3:
time: 174 us
  waiting for transfers between devices  92.1 us (53%)
  starting transfers between devices  50.9 us (29%)
  Pallas kernels  15.6 us (9%)
  local copies, waits for them, and re-layouts  7.56 us (4%)
  other arithmetic  4.8 us (3%)
  matrix products  1.99 us (1%)
    ppermute x23, waiting for transfers between devices, swap(): return lax.ppermute(values, axis, [(i, i ^ step) for i in range(devices)])  85.6 us
    ppermute x23, starting transfers between devices, swap(): return lax.ppermute(values, axis, [(i, i ^ step) for i in range(devices)])  44.4 us
    all_to_all x1, starting transfers between devices, per_device(): lax.all_to_all(sums, ('samples', 'cols'), split_axis=0, concat_axis=0, ti...  6.51 us
    all_to_all x1, waiting for transfers between devices, per_device(): lax.all_to_all(sums, ('samples', 'cols'), split_axis=0, concat_axis=0, ti...  6.48 us
    unnamed x37, local copies, waits for them, and re-layouts  5.9 us
    pallas_call x1, Pallas kernels, per_device(): call(functools.partial(prepare_kernel, devices, capacity), [full, float_o...  5.74 us
    pallas_call x1, Pallas kernels, per_device(): call(functools.partial(curvature_kernel, devices, capacity), float_of(2 *...  4.23 us
    pallas_call x1, Pallas kernels, per_device(): call(functools.partial(apply_kernel, devices, capacity), [full, float_of(...  3.51 us
  transfers between devices with their start and end apart: 24, of which 12 were waited for; matrix products, arithmetic and copies ran while one was open for 1% of the time, Pallas kernels for 6%

profile of v3, /device:TPU:0, one launch (start us, length us, event | category | flops | bytes accessed | tf_op | source)
XLA Modules:
  0.0 173.9 jit_solution(17457168445846583472)
XLA Ops:
  0.7 2.7 %copy.8 = f32[512,512]{0,1:T(8,128)} copy(f32[512,512]{1,0:T(8,128)} %param.9) | data formatting | bytes 2097152 | tf_op args[4]
  3.8 5.7 %shard_map.68 = (f32[512,256]{1,0:T(8,128)S(1)}, f32[512,1]{1,0:T(8,128)S(1)}, s32[4,12]{1,0:T(4,128)S(1)}, f32[2,128,256]{2,1,0:T(8,128)S(1)}, f32[2,128,256]{2...) custom-call(s32[3,32]{1,0:T(4,128)S(1)} %bitcast.47, ...), custom_call_target="tpu_custom_call" | custom-call | tf_op jit(solution)/shard_map/pallas_call | solution.py:323
  15.2 2.5 %collective-permute-start.8 = (f32[4,128,256]{2,1,0:T(8,128)}, f32[4,128,256]{2,1,0:T(8,128)}, u32[]{:S(2)}, u32[]{:S(2)}) collective-permute-start(f32[4,128,256]{2,1,0:T(8,128)} %dynamic-slice_bitcast_fusion.1), channel_id=1, source_target_pairs={{0,2},{2,0},{4,6},{6,4},{8,10},{10,8},{12,14},{14,12},{1,3},{3,1},... | collective-permute-start | bytes 1572872 | tf_op jit(solution)/shard_map/ppermute | solution.py:288
  17.8 12.9 %collective-permute-done.8 = f32[4,128,256]{2,1,0:T(8,128)} collective-permute-done((f32[4,128,256]{2,1,0:T(8,128)}, f32[4,128,256]{2,1,0:T(8,128)}, u32[]{:S(2)}, u32[]{:S(2)}) %collective-permute-start.8) | collective-permute-done | bytes 524320 | tf_op jit(solution)/shard_map/ppermute | solution.py:288
  35.3 6.6 %collective-permute-done.9 = f32[2,128,256]{2,1,0:T(8,128)} collective-permute-done((f32[2,128,256]{2,1,0:T(8,128)}, f32[2,128,256]{2,1,0:T(8,128)}, u32[]{:S(2)}, u32[]{:S(2)}) %collective-permute-start.9) | collective-permute-done | bytes 262176 | tf_op jit(solution)/shard_map/ppermute | solution.py:288
  43.0 2.7 %collective-permute-start.10 = (f32[1,128,256]{2,1,0:T(8,128)S(1)}, f32[1,128,256]{2,1,0:T(8,128)S(1)}, u32[]{:S(2)}, u32[]{:S(2)}) collective-permute-start(f32[1,128,256]{2,1,0:T(8,128)S(1)} %constant_dynamic-slice_fusion.1), channel_id=1, source_target_pairs={{0,8},{2,10},{4,12},{6,14},{8,0},{10,2},{12,4},{14,6},{1,9},{3,11}... | collective-permute-start | bytes 393224 | tf_op jit(solution)/shard_map/ppermute | solution.py:288
  48.8 2.4 %collective-permute-done.10 = f32[1,128,256]{2,1,0:T(8,128)S(1)} collective-permute-done((f32[1,128,256]{2,1,0:T(8,128)S(1)}, f32[1,128,256]{2,1,0:T(8,128)S(1)}, u32[]{:S(2)}, u32[]{:S(2)}) %collective-permute-start.10) | collective-permute-done | bytes 131104 | tf_op jit(solution)/shard_map/ppermute | solution.py:288
  54.0 3.1 %collective-permute-start.3 = (f32[2,128,256]{2,1,0:T(8,128)}, f32[2,128,256]{2,1,0:T(8,128)S(1)}, u32[]{:S(2)}, u32[]{:S(2)}) collective-permute-start(f32[2,128,256]{2,1,0:T(8,128)} %copy-done.6), channel_id=1, source_target_pairs={{0,8},{2,10},{4,12},{6,14},{8,0},{10,2},{12,4},{14,6},{1,9},{3,11}... | collective-permute-start | bytes 786440 | tf_op jit(solution)/shard_map/ppermute | solution.py:288
  57.2 2.4 %collective-permute-start.5 = (f32[2,128,256]{2,1,0:T(8,128)}, f32[2,128,256]{2,1,0:T(8,128)S(1)}, u32[]{:S(2)}, u32[]{:S(2)}) collective-permute-start(f32[2,128,256]{2,1,0:T(8,128)} %copy-done.4), channel_id=1, source_target_pairs={{0,12},{2,14},{4,8},{6,10},{8,4},{10,6},{12,0},{14,2},{1,13},{3,15... | collective-permute-start | bytes 786440 | tf_op jit(solution)/shard_map/ppermute | solution.py:288
  59.6 2.3 %collective-permute-start.6 = (f32[2,128,256]{2,1,0:T(8,128)S(1)}, f32[2,128,256]{2,1,0:T(8,128)S(1)}, u32[]{:S(2)}, u32[]{:S(2)}) collective-permute-start(f32[2,128,256]{2,1,0:T(8,128)S(1)} %get-tuple-element.38), channel_id=1, source_target_pairs={{0,14},{2,12},{4,10},{6,8},{8,6},{10,4},{12,2},{14,0},{1,15},{3,13... | collective-permute-start | bytes 786440 | tf_op jit(solution)/shard_map/ppermute | solution.py:288
  61.9 5.5 %collective-permute-done.2.refs_2_ = f32[2,128,256]{2,1,0:T(8,128)S(1)} collective-permute-done((f32[2,128,256]{2,1,0:T(8,128)}, f32[2,128,256]{2,1,0:T(8,128)S(1)}, u32[]{:S(2)}, u32[]{:S(2)}) %collective-permute-start.2) | collective-permute-done | bytes 262176 | tf_op jit(solution)/shard_map/ppermute | solution.py:288
  67.4 19.6 %collective-permute-done.3.refs_3_ = f32[2,128,256]{2,1,0:T(8,128)S(1)} collective-permute-done((f32[2,128,256]{2,1,0:T(8,128)}, f32[2,128,256]{2,1,0:T(8,128)S(1)}, u32[]{:S(2)}, u32[]{:S(2)}) %collective-permute-start.3) | collective-permute-done | bytes 262176 | tf_op jit(solution)/shard_map/ppermute | solution.py:288
  87.0 5.6 %collective-permute-done.4.refs_4_ = f32[2,128,256]{2,1,0:T(8,128)S(1)} collective-permute-done((f32[2,128,256]{2,1,0:T(8,128)}, f32[2,128,256]{2,1,0:T(8,128)S(1)}, u32[]{:S(2)}, u32[]{:S(2)}) %collective-permute-start.4) | collective-permute-done | bytes 262176 | tf_op jit(solution)/shard_map/ppermute | solution.py:288
  92.6 3.5 %shard_map.69 = (f32[512,256]{1,0:T(8,128)S(1)}, f32[8,256]{1,0:T(8,128)S(1)}, f32[136,256]{1,0:T(8,128)S(1)}, f32[136,256]{1,0:T(8,128)S(1)}, f32[136,256]{1,0:...) custom-call(s32[4,12]{1,0:T(4,128)S(1)} %get-tuple-element.30.table_, ...), custom_call_target="tpu_custom_call" | custom-call | tf_op jit(solution)/shard_map/pallas_call | solution.py:357
  98.7 11.6 %collective-permute-done.12 = f32[4,128,256]{2,1,0:T(8,128)S(1)} collective-permute-done((f32[4,128,256]{2,1,0:T(8,128)S(1)}, f32[4,128,256]{2,1,0:T(8,128)S(1)}, u32[]{:S(2)}, u32[]{:S(2)}) %collective-permute-start.12) | collective-permute-done | bytes 524320 | tf_op jit(solution)/shard_map/ppermute | solution.py:288
  110.4 11.9 %collective-permute-start.13 = (f32[2,128,256]{2,1,0:T(8,128)S(1)}, f32[2,128,256]{2,1,0:T(8,128)S(1)}, u32[]{:S(2)}, u32[]{:S(2)}) collective-permute-start(f32[2,128,256]{2,1,0:T(8,128)S(1)} %dynamic-slice_bitcast_fusion.2), channel_id=1, source_target_pairs={{0,4},{2,6},{4,0},{6,2},{8,12},{10,14},{12,8},{14,10},{1,5},{3,7},... | collective-permute-start | bytes 786440 | tf_op jit(solution)/shard_map/ppermute | solution.py:288
  126.6 7.4 %collective-permute-done.13 = f32[2,128,256]{2,1,0:T(8,128)S(1)} collective-permute-done((f32[2,128,256]{2,1,0:T(8,128)S(1)}, f32[2,128,256]{2,1,0:T(8,128)S(1)}, u32[]{:S(2)}, u32[]{:S(2)}) %collective-permute-start.13) | collective-permute-done | bytes 262176 | tf_op jit(solution)/shard_map/ppermute | solution.py:288
  134.4 2.0 %collective-permute-start.21 = (f32[136,256]{1,0:T(8,128)S(1)}, f32[136,256]{1,0:T(8,128)S(1)}, u32[]{:S(2)}, u32[]{:S(2)}) collective-permute-start(f32[136,256]{1,0:T(8,128)S(1)} %get-tuple-element.54), channel_id=1, source_target_pairs={{0,12},{2,14},{4,8},{6,10},{8,4},{10,6},{12,0},{14,2},{1,13},{3,15... | collective-permute-start | bytes 417800 | tf_op jit(solution)/shard_map/ppermute | solution.py:288
  136.5 2.5 %collective-permute-start.22 = (f32[136,256]{1,0:T(8,128)S(1)}, f32[136,256]{1,0:T(8,128)S(1)}, u32[]{:S(2)}, u32[]{:S(2)}) collective-permute-start(f32[136,256]{1,0:T(8,128)S(1)} %get-tuple-element.55), channel_id=1, source_target_pairs={{0,14},{2,12},{4,10},{6,8},{8,6},{10,4},{12,2},{14,0},{1,15},{3,13... | collective-permute-start | bytes 417800 | tf_op jit(solution)/shard_map/ppermute | solution.py:288
  140.0 13.1 %collective-permute-done.20.refs_11_ = f32[136,256]{1,0:T(8,128)S(1)} collective-permute-done((f32[136,256]{1,0:T(8,128)S(1)}, f32[136,256]{1,0:T(8,128)S(1)}, u32[]{:S(2)}, u32[]{:S(2)}) %collective-permute-start.20) | collective-permute-done | bytes 139296 | tf_op jit(solution)/shard_map/ppermute | solution.py:288
  153.1 4.2 %shard_map.70 = f32[16,8,256]{2,1,0:T(8,128)} custom-call(s32[4,12]{1,0:T(4,128)S(1)} %get-tuple-element.30.table_ref, f32[4,4,128,128]{3,2,1,0:T(8,128)S(1)} %copy-done, f32[512,256]{1,0:T(8,128)S(1)} %get-tuple-element.29.direction_hbm, f32[512,1]{1,0:T(8,128)S(1)} %get-tuple-element.31.diagonal_ref, f32[512,256]{1,0:T(8,128)S(1)} %get-tuple-element.46.scaled_hbm, ...), custom_call_target="tpu_custom_call" | custom-call | tf_op jit(solution)/shard_map/pallas_call | solution.py:369
  157.4 6.5 %all-to-all-start = ((f32[16,8,256]{2,1,0:T(8,128)}), f32[16,8,256]{2,1,0:T(8,128)S(1)}, u32[]{:S(2)}, u32[]{:S(2)}) async-start(f32[16,8,256]{2,1,0:T(8,128)} %shard_map.70), calls=%async_computation | async-start | bytes 262144 | tf_op jit(solution)/shard_map/all_to_all | solution.py:380
  165.3 6.5 %all-to-all-done.sums_hbm = f32[16,8,256]{2,1,0:T(8,128)S(1)} async-done(((f32[16,8,256]{2,1,0:T(8,128)}), f32[16,8,256]{2,1,0:T(8,128)S(1)}, u32[]{:S(2)}, u32[]{:S(2)}) %all-to-all-start) | async-done | bytes 131104 | tf_op jit(solution)/shard_map/all_to_all | solution.py:380
  171.8 2.1 %shard_map.71 = (f32[512,256]{1,0:T(8,128)}, f32[64,512]{1,0:T(8,128)}) custom-call(f32[512,256]{1,0:T(8,128)S(1)} %get-tuple-element.29.direction_hbm, f32[512,256]{1,0:T(8,128)S(1)} %get-tuple-element.46.scaled_hbm, f32[64,512]{1,0:T(8,128)S(1)} %pad_maximum_fusion.1.direction_scores_hbm, f32[64,512]{1,0:T(8,128)S(1)} %pad_maximum_fusion.2.scaled_scores_hbm, ...), custom_call_target="tpu_custom_call" | custom-call | tf_op jit(solution)/shard_map/pallas_call | solution.py:381
  (84 shorter events, 27.7 us)
Async XLA Ops:
  3.4 7.0 %collective-permute-start.7 = (f32[512,512]{0,1:T(8,128)}, f32[512,512]{0,1:T(8,128)}, u32[]{:S(2)}, u32[]{:S(2)}) collective-permute-start(f32[512,512]{0,1:T(8,128)} %copy.8), channel_id=1, source_target_pairs={{0,1},{1,0},{2,3},{3,2},{4,5},{5,4},{6,7},{7,6},{8,9},{9,8},{10,11... | collective-permute-start | bytes 3145736 | tf_op jit(solution)/shard_map/ppermute | solution.py:288
  15.2 15.4 %collective-permute-start.8 = (f32[4,128,256]{2,1,0:T(8,128)}, f32[4,128,256]{2,1,0:T(8,128)}, u32[]{:S(2)}, u32[]{:S(2)}) collective-permute-start(f32[4,128,256]{2,1,0:T(8,128)} %dynamic-slice_bitcast_fusion.1), channel_id=1, source_target_pairs={{0,2},{2,0},{4,6},{6,4},{8,10},{10,8},{12,14},{14,12},{1,3},{3,1},... | collective-permute-start | bytes 1572872 | tf_op jit(solution)/shard_map/ppermute | solution.py:288
  33.5 8.4 %collective-permute-start.9 = (f32[2,128,256]{2,1,0:T(8,128)}, f32[2,128,256]{2,1,0:T(8,128)}, u32[]{:S(2)}, u32[]{:S(2)}) collective-permute-start(f32[2,128,256]{2,1,0:T(8,128)} %dynamic-slice_bitcast_fusion.3), channel_id=1, source_target_pairs={{0,4},{2,6},{4,0},{6,2},{8,12},{10,14},{12,8},{14,10},{1,5},{3,7},... | collective-permute-start | bytes 786440 | tf_op jit(solution)/shard_map/ppermute | solution.py:288
  43.0 8.1 %collective-permute-start.10 = (f32[1,128,256]{2,1,0:T(8,128)S(1)}, f32[1,128,256]{2,1,0:T(8,128)S(1)}, u32[]{:S(2)}, u32[]{:S(2)}) collective-permute-start(f32[1,128,256]{2,1,0:T(8,128)S(1)} %constant_dynamic-slice_fusion.1), channel_id=1, source_target_pairs={{0,8},{2,10},{4,12},{6,14},{8,0},{10,2},{12,4},{14,6},{1,9},{3,11}... | collective-permute-start | bytes 393224 | tf_op jit(solution)/shard_map/ppermute | solution.py:288
  45.7 11.5 %collective-permute-start = (f32[2,128,256]{2,1,0:T(8,128)}, f32[2,128,256]{2,1,0:T(8,128)S(1)}, u32[]{:S(2)}, u32[]{:S(2)}) collective-permute-start(f32[2,128,256]{2,1,0:T(8,128)} %copy-done.9), channel_id=1, source_target_pairs={{0,2},{2,0},{4,6},{6,4},{8,10},{10,8},{12,14},{14,12},{1,3},{3,1},... | collective-permute-start | bytes 786440 | tf_op jit(solution)/shard_map/ppermute | solution.py:288
  47.2 10.0 %collective-permute-start.1 = (f32[2,128,256]{2,1,0:T(8,128)}, f32[2,128,256]{2,1,0:T(8,128)S(1)}, u32[]{:S(2)}, u32[]{:S(2)}) collective-permute-start(f32[2,128,256]{2,1,0:T(8,128)} %copy-done.8), channel_id=1, source_target_pairs={{0,4},{2,6},{4,0},{6,2},{8,12},{10,14},{12,8},{14,10},{1,5},{3,7},... | collective-permute-start | bytes 786440 | tf_op jit(solution)/shard_map/ppermute | solution.py:288
  52.1 7.5 %collective-permute-start.11 = (f32[64,256]{1,0:T(8,128)S(1)}, f32[64,256]{1,0:T(8,128)S(1)}, u32[]{:S(2)}, u32[]{:S(2)}) collective-permute-start(f32[64,256]{1,0:T(8,128)S(1)} %get-tuple-element.59), channel_id=1, source_target_pairs={{0,1},{1,0},{2,3},{3,2},{4,5},{5,4},{6,7},{7,6},{8,9},{9,8},{10,11... | collective-permute-start | bytes 196616 | tf_op jit(solution)/shard_map/ppermute | solution.py:288
  52.2 15.2 %collective-permute-start.2 = (f32[2,128,256]{2,1,0:T(8,128)}, f32[2,128,256]{2,1,0:T(8,128)S(1)}, u32[]{:S(2)}, u32[]{:S(2)}) collective-permute-start(f32[2,128,256]{2,1,0:T(8,128)} %copy-done.7), channel_id=1, source_target_pairs={{0,6},{2,4},{4,2},{6,0},{8,14},{10,12},{12,10},{14,8},{1,7},{3,5},... | collective-permute-start | bytes 786440 | tf_op jit(solution)/shard_map/ppermute | solution.py:288
  54.0 32.9 %collective-permute-start.3 = (f32[2,128,256]{2,1,0:T(8,128)}, f32[2,128,256]{2,1,0:T(8,128)S(1)}, u32[]{:S(2)}, u32[]{:S(2)}) collective-permute-start(f32[2,128,256]{2,1,0:T(8,128)} %copy-done.6), channel_id=1, source_target_pairs={{0,8},{2,10},{4,12},{6,14},{8,0},{10,2},{12,4},{14,6},{1,9},{3,11}... | collective-permute-start | bytes 786440 | tf_op jit(solution)/shard_map/ppermute | solution.py:288
  57.2 35.4 %collective-permute-start.4 = (f32[2,128,256]{2,1,0:T(8,128)}, f32[2,128,256]{2,1,0:T(8,128)S(1)}, u32[]{:S(2)}, u32[]{:S(2)}) collective-permute-start(f32[2,128,256]{2,1,0:T(8,128)} %copy-done.5), channel_id=1, source_target_pairs={{0,10},{2,8},{4,14},{6,12},{8,2},{10,0},{12,6},{14,4},{1,11},{3,9}... | collective-permute-start | bytes 786440 | tf_op jit(solution)/shard_map/ppermute | solution.py:288
  57.2 35.4 %collective-permute-start.5 = (f32[2,128,256]{2,1,0:T(8,128)}, f32[2,128,256]{2,1,0:T(8,128)S(1)}, u32[]{:S(2)}, u32[]{:S(2)}) collective-permute-start(f32[2,128,256]{2,1,0:T(8,128)} %copy-done.4), channel_id=1, source_target_pairs={{0,12},{2,14},{4,8},{6,10},{8,4},{10,6},{12,0},{14,2},{1,13},{3,15... | collective-permute-start | bytes 786440 | tf_op jit(solution)/shard_map/ppermute | solution.py:288
  59.6 33.0 %collective-permute-start.6 = (f32[2,128,256]{2,1,0:T(8,128)S(1)}, f32[2,128,256]{2,1,0:T(8,128)S(1)}, u32[]{:S(2)}, u32[]{:S(2)}) collective-permute-start(f32[2,128,256]{2,1,0:T(8,128)S(1)} %get-tuple-element.38), channel_id=1, source_target_pairs={{0,14},{2,12},{4,10},{6,8},{8,6},{10,4},{12,2},{14,0},{1,15},{3,13... | collective-permute-start | bytes 786440 | tf_op jit(solution)/shard_map/ppermute | solution.py:288
  97.2 13.1 %collective-permute-start.12 = (f32[4,128,256]{2,1,0:T(8,128)S(1)}, f32[4,128,256]{2,1,0:T(8,128)S(1)}, u32[]{:S(2)}, u32[]{:S(2)}) collective-permute-start(f32[4,128,256]{2,1,0:T(8,128)S(1)} %dynamic-slice_bitcast_fusion), channel_id=1, source_target_pairs={{0,2},{2,0},{4,6},{6,4},{8,10},{10,8},{12,14},{14,12},{1,3},{3,1},... | collective-permute-start | bytes 1572872 | tf_op jit(solution)/shard_map/ppermute | solution.py:288
  110.4 23.6 %collective-permute-start.13 = (f32[2,128,256]{2,1,0:T(8,128)S(1)}, f32[2,128,256]{2,1,0:T(8,128)S(1)}, u32[]{:S(2)}, u32[]{:S(2)}) collective-permute-start(f32[2,128,256]{2,1,0:T(8,128)S(1)} %dynamic-slice_bitcast_fusion.2), channel_id=1, source_target_pairs={{0,4},{2,6},{4,0},{6,2},{8,12},{10,14},{12,8},{14,10},{1,5},{3,7},... | collective-permute-start | bytes 786440 | tf_op jit(solution)/shard_map/ppermute | solution.py:288
  122.3 12.1 %collective-permute-start.16 = (f32[136,256]{1,0:T(8,128)S(1)}, f32[136,256]{1,0:T(8,128)S(1)}, u32[]{:S(2)}, u32[]{:S(2)}) collective-permute-start(f32[136,256]{1,0:T(8,128)S(1)} %get-tuple-element.49), channel_id=1, source_target_pairs={{0,2},{2,0},{4,6},{6,4},{8,10},{10,8},{12,14},{14,12},{1,3},{3,1},... | collective-permute-start | bytes 417800 | tf_op jit(solution)/shard_map/ppermute | solution.py:288
  123.7 12.7 %collective-permute-start.17 = (f32[136,256]{1,0:T(8,128)S(1)}, f32[136,256]{1,0:T(8,128)S(1)}, u32[]{:S(2)}, u32[]{:S(2)}) collective-permute-start(f32[136,256]{1,0:T(8,128)S(1)} %get-tuple-element.50), channel_id=1, source_target_pairs={{0,4},{2,6},{4,0},{6,2},{8,12},{10,14},{12,8},{14,10},{1,5},{3,7},... | collective-permute-start | bytes 417800 | tf_op jit(solution)/shard_map/ppermute | solution.py:288
  123.8 15.2 %collective-permute-start.18 = (f32[136,256]{1,0:T(8,128)S(1)}, f32[136,256]{1,0:T(8,128)S(1)}, u32[]{:S(2)}, u32[]{:S(2)}) collective-permute-start(f32[136,256]{1,0:T(8,128)S(1)} %get-tuple-element.51), channel_id=1, source_target_pairs={{0,6},{2,4},{4,2},{6,0},{8,14},{10,12},{12,10},{14,8},{1,7},{3,5},... | collective-permute-start | bytes 417800 | tf_op jit(solution)/shard_map/ppermute | solution.py:288
  125.7 14.3 %collective-permute-start.19 = (f32[136,256]{1,0:T(8,128)S(1)}, f32[136,256]{1,0:T(8,128)S(1)}, u32[]{:S(2)}, u32[]{:S(2)}) collective-permute-start(f32[136,256]{1,0:T(8,128)S(1)} %get-tuple-element.52), channel_id=1, source_target_pairs={{0,8},{2,10},{4,12},{6,14},{8,0},{10,2},{12,4},{14,6},{1,9},{3,11}... | collective-permute-start | bytes 417800 | tf_op jit(solution)/shard_map/ppermute | solution.py:288
  134.0 19.1 %collective-permute-start.20 = (f32[136,256]{1,0:T(8,128)S(1)}, f32[136,256]{1,0:T(8,128)S(1)}, u32[]{:S(2)}, u32[]{:S(2)}) collective-permute-start(f32[136,256]{1,0:T(8,128)S(1)} %get-tuple-element.53), channel_id=1, source_target_pairs={{0,10},{2,8},{4,14},{6,12},{8,2},{10,0},{12,6},{14,4},{1,11},{3,9}... | collective-permute-start | bytes 417800 | tf_op jit(solution)/shard_map/ppermute | solution.py:288
  134.4 18.7 %collective-permute-start.21 = (f32[136,256]{1,0:T(8,128)S(1)}, f32[136,256]{1,0:T(8,128)S(1)}, u32[]{:S(2)}, u32[]{:S(2)}) collective-permute-start(f32[136,256]{1,0:T(8,128)S(1)} %get-tuple-element.54), channel_id=1, source_target_pairs={{0,12},{2,14},{4,8},{6,10},{8,4},{10,6},{12,0},{14,2},{1,13},{3,15... | collective-permute-start | bytes 417800 | tf_op jit(solution)/shard_map/ppermute | solution.py:288
  136.5 16.7 %collective-permute-start.22 = (f32[136,256]{1,0:T(8,128)S(1)}, f32[136,256]{1,0:T(8,128)S(1)}, u32[]{:S(2)}, u32[]{:S(2)}) collective-permute-start(f32[136,256]{1,0:T(8,128)S(1)} %get-tuple-element.55), channel_id=1, source_target_pairs={{0,14},{2,12},{4,10},{6,8},{8,6},{10,4},{12,2},{14,0},{1,15},{3,13... | collective-permute-start | bytes 417800 | tf_op jit(solution)/shard_map/ppermute | solution.py:288
  139.0 24.9 %collective-permute-start.14 = (f32[1,128,256]{2,1,0:T(8,128)S(1)}, f32[1,128,256]{2,1,0:T(8,128)S(1)}, u32[]{:S(2)}, u32[]{:S(2)}) collective-permute-start(f32[1,128,256]{2,1,0:T(8,128)S(1)} %constant_dynamic-slice_fusion), channel_id=1, source_target_pairs={{0,8},{2,10},{4,12},{6,14},{8,0},{10,2},{12,4},{14,6},{1,9},{3,11}... | collective-permute-start | bytes 393224 | tf_op jit(solution)/shard_map/ppermute | solution.py:288
  157.4 14.5 %all-to-all-start = ((f32[16,8,256]{2,1,0:T(8,128)}), f32[16,8,256]{2,1,0:T(8,128)S(1)}, u32[]{:S(2)}, u32[]{:S(2)}) async-start(f32[16,8,256]{2,1,0:T(8,128)} %shard_map.70), calls=%async_computation | async-start | bytes 262144 | tf_op jit(solution)/shard_map/all_to_all | solution.py:380
  164.0 1.4 collective-permute-start.15
  (18 other events, 139.8 us)

commit v4 on v3

--- a/solution.py
+++ b/solution.py
@@ -8,7 +8,7 @@
 from jax.experimental.pallas import tpu as pltpu
 from jax.sharding import PartitionSpec as P
 
-VMEM_LIMIT = 40 * 1024 * 1024
+VMEM_LIMIT = 60 * 1024 * 1024
 SUBLANES = 8
 
 
@@ -59,9 +59,8 @@
 
 
 def prepare_kernel(devices, capacity, list_ref, kinship_hbm, variance_hbm, phenotypes_hbm, *refs):
-    direction_hbm, diagonal_ref, table_ref = refs[:3]
-    outgoing_hbm = refs[3:3 + devices - 1]
-    kinship_ref, variance_ref, phenotypes_ref, direction_ref, first_ref, last_ref, semaphores = refs[3 + devices - 1:]
+    (direction_hbm, diagonal_ref, table_ref, outgoing_hbm, kinship_ref, variance_ref, phenotypes_ref, direction_ref,
+     first_ref, last_ref, semaphores) = refs
     block_count, positions, tile = kinship_ref.shape[:3]
     copies = Copies(semaphores)
     loads = [copies.start(variance_hbm, variance_ref)]
@@ -101,10 +100,9 @@
         return jnp.where((key >= 0) & (key < top), jnp.where(me < other, lower, higher), 0)
 
     blocks = []
-    for k in range(1, devices):
-        other = me ^ k
+    for other in range(devices):
         blocks.append((mine(first_ref[other], other), mine(last_ref[other], other)))
-        table_ref[3, k] = jnp.where(me < other, blocks[-1][1], blocks[-1][0])
+        table_ref[3, other] = jnp.where(me < other, blocks[-1][1], blocks[-1][0])
     stores = []
     diagonal_mask = on_diagonal(tile)
     loads[0].wait()
@@ -117,30 +115,26 @@
         diagonal = jnp.sum(total, axis=1, keepdims=True)
         diagonal_ref[block, :] = diagonal
         direction_ref[block, :] = phenotypes_ref[block, :] / diagonal
-    for k in range(1, devices):
+    for other in range(devices):
         for slot in range(capacity):
-            start = pl.multiple_of(blocks[k - 1][slot] * tile, tile)
-            stores.append(copies.start(direction_ref.at[pl.ds(start, tile)], outgoing_hbm[k - 1].at[slot]))
+            start = pl.multiple_of(blocks[other][slot] * tile, tile)
+            stores.append(copies.start(direction_ref.at[pl.ds(start, tile)], outgoing_hbm.at[other, slot]))
     stores.append(copies.start(direction_ref, direction_hbm))
     wait_all(stores)
 
 
-def apply_kernel(devices, capacity, table_ref, kinship_hbm, direction_hbm, diagonal_ref, phenotypes_hbm,
-                 *refs):
-    received_hbm, refs = refs[:devices - 1], refs[devices - 1:]
-    scaled_hbm, sums_ref = refs[:2]
-    outgoing_hbm, refs = refs[2:2 + devices - 1], refs[2 + devices - 1:]
-    kinship_ref, direction_ref, phenotypes_ref, received_ref, scaled_ref, mapped_ref, semaphores = refs
+def apply_kernel(devices, table_ref, kinship_hbm, direction_hbm, diagonal_ref, phenotypes_hbm, received_hbm,
+                 scaled_hbm, outgoing_hbm, sums_ref, kinship_ref, direction_ref, phenotypes_ref, received_ref,
+                 scaled_ref, mapped_ref, semaphores):
     block_count, positions, tile = kinship_ref.shape[:3]
     columns = direction_ref.shape[1]
-    me = lax.axis_index("samples")
     copies = Copies(semaphores)
     loads = [
         copies.start(kinship_hbm, kinship_ref),
         copies.start(direction_hbm, direction_ref),
         copies.start(phenotypes_hbm, phenotypes_ref),
     ]
-    arrivals = [copies.start(received_hbm[k - 1], received_ref.at[me ^ k]) for k in range(1, devices)]
+    arrivals = [copies.start(received_hbm, received_ref)]
     wait_all(loads)
     diagonal_mask = on_diagonal(tile)
     norm = jnp.zeros((SUBLANES, columns), jnp.float32)
@@ -164,34 +158,30 @@
     sums_ref[0:1, :] = jnp.sum(norm, axis=0, keepdims=True)
     sums_ref[1:2, :] = jnp.sum(cross, axis=0, keepdims=True)
     stores = []
-    for k in range(1, devices):
-        start = pl.multiple_of(table_ref[3, k] * tile, tile)
-        stores.append(copies.start(scaled_ref.at[pl.ds(start, tile)], outgoing_hbm[k - 1].at[pl.ds(0, tile)]))
-        stores.append(copies.start(sums_ref, outgoing_hbm[k - 1].at[pl.ds(tile, SUBLANES)]))
+    for other in range(devices):
+        start = pl.multiple_of(table_ref[3, other] * tile, tile)
+        stores.append(copies.start(scaled_ref.at[pl.ds(start, tile)], outgoing_hbm.at[other, pl.ds(0, tile)]))
+        stores.append(copies.start(sums_ref, outgoing_hbm.at[other, pl.ds(tile, SUBLANES)]))
     stores.append(copies.start(scaled_ref, scaled_hbm))
     wait_all(stores)
 
 
-def curvature_kernel(devices, capacity, table_ref, kinship_hbm, direction_hbm, diagonal_ref, scaled_hbm,
-                     first_sums_ref, *refs):
-    received_hbm, refs = refs[:devices - 1], refs[devices - 1:]
-    later_hbm, refs = refs[:devices - 1], refs[devices - 1:]
-    sums_hbm, kinship_ref, direction_ref, scaled_ref, received_ref, later_ref, all_sums_ref, semaphores = refs
+def curvature_kernel(devices, table_ref, kinship_hbm, direction_hbm, diagonal_ref, scaled_hbm, received_hbm,
+                     later_hbm, sums_ref, kinship_ref, direction_ref, scaled_ref, received_ref, later_ref, semaphores):
     block_count, positions, tile = kinship_ref.shape[:3]
     columns = direction_ref.shape[1]
-    me = lax.axis_index("samples")
     copies = Copies(semaphores)
-    loads = [copies.start(later_hbm[k - 1], later_ref.at[me ^ k]) for k in range(1, devices)]
-    loads += [
+    loads = [
+        copies.start(later_hbm, later_ref),
         copies.start(kinship_hbm, kinship_ref),
         copies.start(direction_hbm, direction_ref),
         copies.start(scaled_hbm, scaled_ref),
     ]
-    arrivals = [copies.start(received_hbm[k - 1], received_ref.at[me ^ k]) for k in range(1, devices)]
+    arrivals = [copies.start(received_hbm, received_ref)]
     wait_all(loads)
-    first_sums = first_sums_ref[...]
-    for k in range(1, devices):
-        first_sums = first_sums + later_ref[me ^ k, pl.ds(tile, SUBLANES), :]
+    first_sums = later_ref[0, pl.ds(tile, SUBLANES), :]
+    for other in range(1, devices):
+        first_sums = first_sums + later_ref[other, pl.ds(tile, SUBLANES), :]
     rho = first_sums[1:2, :] / first_sums[0:1, :]
     diagonal_mask = on_diagonal(tile)
     norm = jnp.zeros((SUBLANES, columns), jnp.float32)
@@ -216,19 +206,11 @@
         bend = bend + column_sums(scaled_ref[pl.ds(row * tile, tile), :] * mapped)
     row_ids = lax.broadcasted_iota(jnp.int32, first_sums.shape, 0)
     sums = jnp.where(row_ids == 2, jnp.sum(norm, axis=0, keepdims=True), first_sums)
-    sums = jnp.where(row_ids == 3, jnp.sum(bend, axis=0, keepdims=True), sums)
-    for i in range(2 * devices):
-        all_sums_ref[i] = sums
-    store = copies.start(all_sums_ref, sums_hbm)
-    store.wait()
-
-
-def coefficients(own, shares):
-    norm, cross = own[0:1, :], own[1:2, :]
-    total = shares[0]
-    for other in shares[1:]:
-        total = total + other
-    later_norm, bend = total[2:3, :], total[3:4, :]
+    sums_ref[...] = jnp.where(row_ids == 3, jnp.sum(bend, axis=0, keepdims=True), sums)
+
+
+def coefficients(sums):
+    norm, cross, later_norm, bend = (sums[i:i + 1, :] for i in range(4))
     curve = norm + cross
     ratio = later_norm / curve
     step = jnp.where(later_norm > 0, later_norm / (later_norm + bend - later_norm * ratio), 0.0)
@@ -236,7 +218,7 @@
     return start * (1.0 + step * (ratio + cross / norm)), -start * step
 
 
-def finish_kernel(devices, norm_scale, direction_hbm, scaled_hbm, direction_scores_hbm, scaled_scores_hbm, sums_hbm,
+def finish_kernel(norm_scale, direction_hbm, scaled_hbm, direction_scores_hbm, scaled_scores_hbm, sums_hbm,
                   *refs):
     (solved_hbm, scores_ref, direction_ref, scaled_ref, direction_scores_ref, scaled_scores_ref, sums_ref,
      semaphores) = refs
@@ -251,10 +233,8 @@
         copies.start(scaled_scores_hbm, scaled_scores_ref),
     ]
     arrival.wait()
-    own = [sums_ref[2 * i + column] for i in range(devices)]
-    other = [sums_ref[2 * i + 1 - column] for i in range(devices)]
-    along, across = coefficients(own[0], own)
-    other_along, other_across = coefficients(other[0], other)
+    along, across = coefficients(sums_ref[0])
+    other_along, other_across = coefficients(sums_ref[1])
     wait_all(loads)
     stores = []
     rows = people // 4
@@ -303,6 +283,16 @@
     return values.reshape(rows, -1)
 
 
+def total_sums(sums, devices):
+    both = jnp.stack([sums, swap(sums, "cols", 2, 1)])
+    is_share = (jnp.arange(SUBLANES) // 2 == 1)[None, :, None]
+    step = 1
+    while step < devices:
+        both = both + jnp.where(is_share, swap(both, "samples", devices, step), 0.0)
+        step *= 2
+    return both
+
+
 def per_device(kinship, relatives, variance, phenotypes, dosage):
     devices = lax.axis_size("samples")
     block_count, positions, tile = kinship.shape[:3]
@@ -319,25 +309,25 @@
     room = lambda *shape: pltpu.VMEM(shape, jnp.float32)
     full = float_of(people, columns)
     full_room = room(people, columns)
-    peers = devices - 1
-    direction, diagonal, table, *outgoing = call(
+    direction, diagonal, table, outgoing = call(
         functools.partial(prepare_kernel, devices, capacity),
         [
             full,
             float_of(people, 1),
             jax.ShapeDtypeStruct((4, max(entries, devices)), jnp.int32),
-        ] + [float_of(capacity, tile, columns)] * peers,
+            float_of(devices, capacity, tile, columns),
+        ],
         [smem, hbm, hbm, hbm],
-        [hbm, vmem, smem] + [hbm] * peers,
+        [hbm, vmem, smem, hbm],
         [
             room(*kinship.shape), room(block_count, tile), full_room, full_room,
             pltpu.SMEM((devices,), jnp.int32), pltpu.SMEM((devices,), jnp.int32),
-            pltpu.SemaphoreType.DMA((2 * block_count + capacity * peers + 2,)),
+            pltpu.SemaphoreType.DMA((2 * block_count + capacity * devices + 2,)),
         ],
     )(relatives.T, kinship, variance.reshape(block_count, tile), phenotypes)
 
     def exchange(blocks):
-        return [swap(blocks[k - 1], "samples", devices, k) for k in range(1, devices)]
+        return lax.all_to_all(blocks, "samples", split_axis=0, concat_axis=0, tiled=True)
 
     both_dosages = jnp.concatenate(
         [values.reshape(people, devices, share_rows) for values in (dosage, swap(dosage, "cols", 2, 1))], axis=2
@@ -354,41 +344,41 @@
     received = exchange(outgoing)
     direction_scores = variant_sums(direction)
     received, direction_scores = lax.optimization_barrier((received, direction_scores))
-    scaled, first_sums, *outgoing = call(
-        functools.partial(apply_kernel, devices, capacity),
-        [full, float_of(SUBLANES, columns)] + [float_of(tile + SUBLANES, columns)] * peers,
-        [smem, hbm, hbm, vmem, hbm] + [hbm] * peers,
-        [hbm, vmem] + [hbm] * peers,
-        [
+    scaled, outgoing = call(
+        functools.partial(apply_kernel, devices),
+        [full, float_of(devices, tile + SUBLANES, columns)],
+        [smem, hbm, hbm, vmem, hbm, hbm],
+        [hbm, hbm],
+        [
+            room(SUBLANES, columns),
             room(*kinship.shape), full_room, full_room, room(devices, capacity, tile, columns), full_room, full_room,
-            pltpu.SemaphoreType.DMA((3 * peers + 4,)),
-        ],
-    )(table, kinship, direction, diagonal, phenotypes, *received)
+            pltpu.SemaphoreType.DMA((2 * devices + 5,)),
+        ],
+    )(table, kinship, direction, diagonal, phenotypes, received)
     later = exchange(outgoing)
     scaled_scores = variant_sums(scaled)
     sums = call(
-        functools.partial(curvature_kernel, devices, capacity),
-        float_of(2 * devices, SUBLANES, columns),
-        [smem, hbm, hbm, vmem, hbm, vmem] + [hbm] * (2 * peers),
-        hbm,
+        functools.partial(curvature_kernel, devices),
+        float_of(SUBLANES, columns),
+        [smem, hbm, hbm, vmem, hbm, hbm, hbm],
+        vmem,
         [
             room(*kinship.shape), full_room, full_room, room(devices, capacity, tile, columns),
-            room(devices, tile + SUBLANES, columns), room(2 * devices, SUBLANES, columns),
-            pltpu.SemaphoreType.DMA((2 * peers + 4,)),
-        ],
-    )(table, kinship, direction, diagonal, scaled, first_sums, *received, *later)
-    all_sums = lax.all_to_all(sums, ("samples", "cols"), split_axis=0, concat_axis=0, tiled=True)
+            room(devices, tile + SUBLANES, columns),
+            pltpu.SemaphoreType.DMA((5,)),
+        ],
+    )(table, kinship, direction, diagonal, scaled, received, later)
     solved, scores = call(
-        functools.partial(finish_kernel, devices, 1.0 / math.sqrt(people * devices)),
+        functools.partial(finish_kernel, 1.0 / math.sqrt(people * devices)),
         [full, float_of(share_rows, 2 * columns)],
         [hbm] * 5,
         [hbm, vmem],
         [
             full_room, full_room, room(share_rows, 2 * columns), room(share_rows, 2 * columns),
-            room(2 * devices, SUBLANES, columns),
+            room(2, SUBLANES, columns),
             pltpu.SemaphoreType.DMA((9,)),
         ],
-    )(direction, scaled, direction_scores, scaled_scores, all_sums)
+    )(direction, scaled, direction_scores, scaled_scores, total_sums(sums, devices))
     return (solved, scores)
 
 

time: 174 us -> 152 us (0.87)
  starting transfers between devices: 50.9 us -> 22.3 us
  waiting for transfers between devices: 92.1 us -> 96.2 us
  local copies, waits for them, and re-layouts: 7.56 us -> 4.33 us
  other arithmetic: 4.8 us -> 8.02 us
  Pallas kernels: 15.6 us -> 17.8 us
    ppermute x23 -> x13, starting transfers between devices: 44.4 us -> 11.1 us  [swap(): return lax.ppermute(values, axis, [(i, i ^ step) for i in range(devices)])]
    ppermute x23 -> x13, waiting for transfers between devices: 85.6 us -> 96.2 us  [swap(): return lax.ppermute(values, axis, [(i, i ^ step) for i in range(devices)])]
    all_to_all x1 -> x2, waiting for transfers between devices: 6.48 us -> 0.01 us  [exchange(): lax.all_to_all(blocks, 'samples', split_axis=0, concat_axis=0, tiled=True)]
    all_to_all x1 -> x2, starting transfers between devices: 6.51 us -> 11.3 us  [exchange(): lax.all_to_all(blocks, 'samples', split_axis=0, concat_axis=0, tiled=True)]
    pallas_call x3, Pallas kernels: 9.86 us -> 13.2 us  [the longest x1 5.38 us: per_device(): call(functools.partial(apply_kernel, devices), [full, float_of(devices, t...]
    unnamed x37 -> x9, local copies, waits for them, and re-layouts: 5.9 us -> 3.36 us
    add x0 -> x3, other arithmetic: none -> 2.21 us  [total_sums(): both = both + jnp.where(is_share, swap(both, 'samples', devices, step), 0.0)]
  transfers between devices with their start and end apart: 24 -> 15, of which waited for: 12 -> 10; matrix products, arithmetic and copies ran while one was open for 1% -> 6% of each run, Pallas kernels for 6% -> 6%
where the time goes in v4:
time: 152 us
  waiting for transfers between devices  96.2 us (63%)
  starting transfers between devices  22.3 us (15%)
  Pallas kernels  17.8 us (12%)
  other arithmetic  8.02 us (5%)
  local copies, waits for them, and re-layouts  4.33 us (3%)
  matrix products  1.99 us (1%)
    ppermute x13, waiting for transfers between devices, swap(): return lax.ppermute(values, axis, [(i, i ^ step) for i in range(devices)])  96.2 us
    all_to_all x2, starting transfers between devices, exchange(): lax.all_to_all(blocks, 'samples', split_axis=0, concat_axis=0, tiled=True)  11.3 us
    ppermute x13, starting transfers between devices, swap(): return lax.ppermute(values, axis, [(i, i ^ step) for i in range(devices)])  11.1 us
    pallas_call x1, Pallas kernels, per_device(): call(functools.partial(apply_kernel, devices), [full, float_of(devices, t...  5.38 us
    pallas_call x1, Pallas kernels, per_device(): call(functools.partial(curvature_kernel, devices), float_of(SUBLANES, col...  5 us
    pallas_call x1, Pallas kernels, per_device(): call(functools.partial(prepare_kernel, devices, capacity), [full, float_o...  4.59 us
    unnamed x9, local copies, waits for them, and re-layouts  3.36 us
  transfers between devices with their start and end apart: 15, of which 10 were waited for; matrix products, arithmetic and copies ran while one was open for 6% of the time, Pallas kernels for 6%

profile of v4, /device:TPU:0, one launch (start us, length us, event | category | flops | bytes accessed | tf_op | source)
XLA Modules:
  0.0 151.5 jit_solution(3072228566713931574)
XLA Ops:
  0.6 1.6 %copy.8 = f32[512,512]{0,1:T(8,128)S(1)} copy(f32[512,512]{1,0:T(8,128)} %param.9) | data formatting | bytes 2097152 | tf_op args[4]
  2.7 4.6 %shard_map.68 = (f32[512,256]{1,0:T(8,128)}, f32[512,1]{1,0:T(8,128)}, s32[4,12]{1,0:T(4,128)}, f32[8,2,128,256]{3,2,1,0:T(8,128)}) custom-call(s32[3,32]{1,0:T(4,128)} %bitcast.63, f32[4,4,128,128]{3,2,1,0:T(8,128)} %kinship_hbm.5, f32[4,128]{1,0:T(4,128)} %bitcast.64, f32[512,256]{1,0:T(8,128)} %phenotypes_hbm.3), custom_call_target="tpu_custom_call" | custom-call | tf_op jit(solution)/shard_map/pallas_call | solution.py:312
  7.3 6.9 %all-to-all-start = ((f32[8,2,128,256]{3,2,1,0:T(8,128)}), f32[8,2,128,256]{3,2,1,0:T(8,128)}, u32[]{:S(2)}, u32[]{:S(2)}) async-start(f32[8,2,128,256]{3,2,1,0:T(8,128)} %get-tuple-element.13), calls=%async_computation | async-start | bytes 4194304 | tf_op jit(solution)/shard_map/all_to_all | solution.py:330
  14.2 1.0 copy-done.3
  15.2 1.5 %pad_maximum_fusion = f32[512,8,128]{0,2,1:T(8,128)S(1)} fusion(f32[512,8,64]{0,2,1:T(8,128)} %bitcast.56, f32[512,8,64]{0,2,1:T(8,128)S(1)} %bitcast.51), kind=kLoop, calls=%fused_computation | loop fusion | flops 524288 | bytes 4194304 | tf_op jit(solution)/shard_map/concatenate | solution.py:332
  18.6 2.0 %collective-permute-start.1 = (f32[4,128,256]{2,1,0:T(8,128)}, f32[4,128,256]{2,1,0:T(8,128)}, u32[]{:S(2)}, u32[]{:S(2)}) collective-permute-start(f32[4,128,256]{2,1,0:T(8,128)} %dynamic-slice_bitcast_fusion.1), channel_id=1, source_target_pairs={{0,2},{2,0},{4,6},{6,4},{8,10},{10,8},{12,14},{14,12},{1,3},{3,1},... | collective-permute-start | bytes 1572872 | tf_op jit(solution)/shard_map/ppermute | solution.py:268
  20.6 30.4 %collective-permute-done.1 = f32[4,128,256]{2,1,0:T(8,128)} collective-permute-done((f32[4,128,256]{2,1,0:T(8,128)}, f32[4,128,256]{2,1,0:T(8,128)}, u32[]{:S(2)}, u32[]{:S(2)}) %collective-permute-start.1) | collective-permute-done | bytes 524320 | tf_op jit(solution)/shard_map/ppermute | solution.py:268
  51.0 1.1 bitcast_add_fusion.1
  53.0 15.6 %collective-permute-done.2 = f32[2,128,256]{2,1,0:T(8,128)S(1)} collective-permute-done((f32[2,128,256]{2,1,0:T(8,128)S(1)}, f32[2,128,256]{2,1,0:T(8,128)S(1)}, u32[]{:S(2)}, u32[]{:S(2)}) %collective-permute-start.2) | collective-permute-done | bytes 262176 | tf_op jit(solution)/shard_map/ppermute | solution.py:268
  70.1 8.4 %collective-permute-done.3 = f32[1,128,256]{2,1,0:T(8,128)S(1)} collective-permute-done((f32[1,128,256]{2,1,0:T(8,128)S(1)}, f32[1,128,256]{2,1,0:T(8,128)S(1)}, u32[]{:S(2)}, u32[]{:S(2)}) %collective-permute-start.3) | collective-permute-done | bytes 131104 | tf_op jit(solution)/shard_map/ppermute | solution.py:268
  78.6 1.2 collective-permute-done.4
  80.5 5.4 %shard_map.69 = (f32[512,256]{1,0:T(8,128)}, f32[8,136,256]{2,1,0:T(8,128)}) custom-call(s32[4,12]{1,0:T(4,128)} %get-tuple-element.11.table_ref, f32[4,4,128,128]{3,2,1,0:T(8,128)} %kinship_hbm.5, f32[512,256]{1,0:T(8,128)} %get-tuple-element.10.direction_hbm, f32[512,1]{1,0:T(8,128)} %get-tuple-element.12.diagonal_ref, f32[512,256]{1,0:T(8,128)} %phenotypes_hbm.3, ...), custom_call_target="tpu_custom_call" | custom-call | tf_op jit(solution)/shard_map/pallas_call | solution.py:347
  85.9 4.4 %all-to-all-start.1 = ((f32[8,136,256]{2,1,0:T(8,128)}), f32[8,136,256]{2,1,0:T(8,128)}, u32[]{:S(2)}, u32[]{:S(2)}) async-start(f32[8,136,256]{2,1,0:T(8,128)} %get-tuple-element.17), calls=%async_computation.1 | async-start | bytes 2228224 | tf_op jit(solution)/shard_map/all_to_all | solution.py:330
  91.4 2.0 %collective-permute-start.5 = (f32[4,128,256]{2,1,0:T(8,128)S(1)}, f32[4,128,256]{2,1,0:T(8,128)S(1)}, u32[]{:S(2)}, u32[]{:S(2)}) collective-permute-start(f32[4,128,256]{2,1,0:T(8,128)S(1)} %dynamic-slice_bitcast_fusion), channel_id=1, source_target_pairs={{0,2},{2,0},{4,6},{6,4},{8,10},{10,8},{12,14},{14,12},{1,3},{3,1},... | collective-permute-start | bytes 1572872 | tf_op jit(solution)/shard_map/ppermute | solution.py:268
  93.4 23.0 %collective-permute-done.5 = f32[4,128,256]{2,1,0:T(8,128)S(1)} collective-permute-done((f32[4,128,256]{2,1,0:T(8,128)S(1)}, f32[4,128,256]{2,1,0:T(8,128)S(1)}, u32[]{:S(2)}, u32[]{:S(2)}) %collective-permute-start.5) | collective-permute-done | bytes 524320 | tf_op jit(solution)/shard_map/ppermute | solution.py:268
  116.5 1.5 %collective-permute-start.6 = (f32[2,128,256]{2,1,0:T(8,128)S(1)}, f32[2,128,256]{2,1,0:T(8,128)S(1)}, u32[]{:S(2)}, u32[]{:S(2)}) collective-permute-start(f32[2,128,256]{2,1,0:T(8,128)S(1)} %dynamic-slice_bitcast_fusion.2), channel_id=1, source_target_pairs={{0,4},{2,6},{4,0},{6,2},{8,12},{10,14},{12,8},{14,10},{1,5},{3,7},... | collective-permute-start | bytes 786440 | tf_op jit(solution)/shard_map/ppermute | solution.py:268
  118.0 6.1 %collective-permute-done.6 = f32[2,128,256]{2,1,0:T(8,128)S(1)} collective-permute-done((f32[2,128,256]{2,1,0:T(8,128)S(1)}, f32[2,128,256]{2,1,0:T(8,128)S(1)}, u32[]{:S(2)}, u32[]{:S(2)}) %collective-permute-start.6) | collective-permute-done | bytes 262176 | tf_op jit(solution)/shard_map/ppermute | solution.py:268
  124.1 3.1 %collective-permute-start.7 = (f32[1,128,256]{2,1,0:T(8,128)S(1)}, f32[1,128,256]{2,1,0:T(8,128)S(1)}, u32[]{:S(2)}, u32[]{:S(2)}) collective-permute-start(f32[1,128,256]{2,1,0:T(8,128)S(1)} %constant_dynamic-slice_fusion), channel_id=1, source_target_pairs={{0,8},{2,10},{4,12},{6,14},{8,0},{10,2},{12,4},{14,6},{1,9},{3,11}... | collective-permute-start | bytes 393224 | tf_op jit(solution)/shard_map/ppermute | solution.py:268
  127.3 5.0 %shard_map.70 = f32[8,256]{1,0:T(8,128)} custom-call(s32[4,12]{1,0:T(4,128)} %get-tuple-element.11.table_ref, f32[4,4,128,128]{3,2,1,0:T(8,128)} %kinship_hbm.5, f32[512,256]{1,0:T(8,128)} %get-tuple-element.10.direction_hbm, f32[512,1]{1,0:T(8,128)} %get-tuple-element.12.diagonal_ref, f32[512,256]{1,0:T(8,128)} %get-tuple-element.15.scaled_hbm, ...), custom_call_target="tpu_custom_call" | custom-call | tf_op jit(solution)/shard_map/pallas_call | solution.py:360
  132.3 1.4 collective-permute-done.9
  134.6 3.5 %collective-permute-done.10 = f32[2,8,256]{2,1,0:T(8,128)S(1)} collective-permute-done((f32[2,8,256]{2,1,0:T(8,128)S(1)}, f32[2,8,256]{2,1,0:T(8,128)S(1)}, u32[]{:S(2)}, u32[]{:S(2)}) %collective-permute-start.10) | collective-permute-done | bytes 16416 | tf_op jit(solution)/shard_map/ppermute | solution.py:268
  140.0 2.7 %collective-permute-done.11 = f32[2,8,256]{2,1,0:T(8,128)S(1)} collective-permute-done((f32[2,8,256]{2,1,0:T(8,128)S(1)}, f32[2,8,256]{2,1,0:T(8,128)S(1)}, u32[]{:S(2)}, u32[]{:S(2)}) %collective-permute-start.11) | collective-permute-done | bytes 16416 | tf_op jit(solution)/shard_map/ppermute | solution.py:268
  144.1 3.9 %collective-permute-done.12 = f32[2,8,256]{2,1,0:T(8,128)S(1)} collective-permute-done((f32[2,8,256]{2,1,0:T(8,128)S(1)}, f32[2,8,256]{2,1,0:T(8,128)S(1)}, u32[]{:S(2)}, u32[]{:S(2)}) %collective-permute-start.12) | collective-permute-done | bytes 16416 | tf_op jit(solution)/shard_map/ppermute | solution.py:268
  148.7 2.8 %shard_map.71 = (f32[512,256]{1,0:T(8,128)}, f32[64,512]{1,0:T(8,128)}) custom-call(f32[512,256]{1,0:T(8,128)} %get-tuple-element.10.direction_hbm, f32[512,256]{1,0:T(8,128)} %get-tuple-element.15.scaled_hbm, f32[64,512]{1,0:T(8,128)} %pad_maximum_fusion.1.direction_scores_hbm, f32[64,512]{1,0:T(8,128)} %pad_maximum_fusion.2.scaled_scores_hbm, ...), custom_call_target="tpu_custom_call" | custom-call | tf_op jit(solution)/shard_map/pallas_call | solution.py:371
  (43 shorter events, 11.6 us)
Async XLA Ops:
  2.2 12.0 %collective-permute-start = (f32[512,512]{0,1:T(8,128)S(1)}, f32[512,512]{0,1:T(8,128)S(1)}, u32[]{:S(2)}, u32[]{:S(2)}) collective-permute-start(f32[512,512]{0,1:T(8,128)S(1)} %copy.8), channel_id=1, source_target_pairs={{0,1},{1,0},{2,3},{3,2},{4,5},{5,4},{6,7},{7,6},{8,9},{9,8},{10,11... | collective-permute-start | bytes 3145736 | tf_op jit(solution)/shard_map/ppermute | solution.py:268
  7.3 73.2 %all-to-all-start = ((f32[8,2,128,256]{3,2,1,0:T(8,128)}), f32[8,2,128,256]{3,2,1,0:T(8,128)}, u32[]{:S(2)}, u32[]{:S(2)}) async-start(f32[8,2,128,256]{3,2,1,0:T(8,128)} %get-tuple-element.13), calls=%async_computation | async-start | bytes 4194304 | tf_op jit(solution)/shard_map/all_to_all | solution.py:330
  14.2 1.0 copy-start.3
  15.2 1.6 %copy-start = (f32[512,256]{1,0:T(8,128)S(1)}, f32[512,256]{1,0:T(8,128)}, u32[]{:S(2)}) copy-start(f32[512,256]{1,0:T(8,128)} %get-tuple-element.10.direction_hbm) | copy-start | bytes 1572868
  18.6 32.4 %collective-permute-start.1 = (f32[4,128,256]{2,1,0:T(8,128)}, f32[4,128,256]{2,1,0:T(8,128)}, u32[]{:S(2)}, u32[]{:S(2)}) collective-permute-start(f32[4,128,256]{2,1,0:T(8,128)} %dynamic-slice_bitcast_fusion.1), channel_id=1, source_target_pairs={{0,2},{2,0},{4,6},{6,4},{8,10},{10,8},{12,14},{14,12},{1,3},{3,1},... | collective-permute-start | bytes 1572872 | tf_op jit(solution)/shard_map/ppermute | solution.py:268
  52.1 0.8 copy-start.2
  52.9 15.8 %collective-permute-start.2 = (f32[2,128,256]{2,1,0:T(8,128)S(1)}, f32[2,128,256]{2,1,0:T(8,128)S(1)}, u32[]{:S(2)}, u32[]{:S(2)}) collective-permute-start(f32[2,128,256]{2,1,0:T(8,128)S(1)} %dynamic-slice_bitcast_fusion.3), channel_id=1, source_target_pairs={{0,4},{2,6},{4,0},{6,2},{8,12},{10,14},{12,8},{14,10},{1,5},{3,7},... | collective-permute-start | bytes 786440 | tf_op jit(solution)/shard_map/ppermute | solution.py:268
  69.7 8.8 %collective-permute-start.3 = (f32[1,128,256]{2,1,0:T(8,128)S(1)}, f32[1,128,256]{2,1,0:T(8,128)S(1)}, u32[]{:S(2)}, u32[]{:S(2)}) collective-permute-start(f32[1,128,256]{2,1,0:T(8,128)S(1)} %constant_dynamic-slice_fusion.1), channel_id=1, source_target_pairs={{0,8},{2,10},{4,12},{6,14},{8,0},{10,2},{12,4},{14,6},{1,9},{3,11}... | collective-permute-start | bytes 393224 | tf_op jit(solution)/shard_map/ppermute | solution.py:268
  78.6 1.3 collective-permute-start.4
  85.9 4.4 %copy-start.1 = (f32[512,256]{1,0:T(8,128)S(1)}, f32[512,256]{1,0:T(8,128)}, u32[]{:S(2)}) copy-start(f32[512,256]{1,0:T(8,128)} %get-tuple-element.15.scaled_hbm) | copy-start | bytes 1572868
  85.9 41.3 %all-to-all-start.1 = ((f32[8,136,256]{2,1,0:T(8,128)}), f32[8,136,256]{2,1,0:T(8,128)}, u32[]{:S(2)}, u32[]{:S(2)}) async-start(f32[8,136,256]{2,1,0:T(8,128)} %get-tuple-element.17), calls=%async_computation.1 | async-start | bytes 2228224 | tf_op jit(solution)/shard_map/all_to_all | solution.py:330
  91.4 24.9 %collective-permute-start.5 = (f32[4,128,256]{2,1,0:T(8,128)S(1)}, f32[4,128,256]{2,1,0:T(8,128)S(1)}, u32[]{:S(2)}, u32[]{:S(2)}) collective-permute-start(f32[4,128,256]{2,1,0:T(8,128)S(1)} %dynamic-slice_bitcast_fusion), channel_id=1, source_target_pairs={{0,2},{2,0},{4,6},{6,4},{8,10},{10,8},{12,14},{14,12},{1,3},{3,1},... | collective-permute-start | bytes 1572872 | tf_op jit(solution)/shard_map/ppermute | solution.py:268
  116.5 7.6 %collective-permute-start.6 = (f32[2,128,256]{2,1,0:T(8,128)S(1)}, f32[2,128,256]{2,1,0:T(8,128)S(1)}, u32[]{:S(2)}, u32[]{:S(2)}) collective-permute-start(f32[2,128,256]{2,1,0:T(8,128)S(1)} %dynamic-slice_bitcast_fusion.2), channel_id=1, source_target_pairs={{0,4},{2,6},{4,0},{6,2},{8,12},{10,14},{12,8},{14,10},{1,5},{3,7},... | collective-permute-start | bytes 786440 | tf_op jit(solution)/shard_map/ppermute | solution.py:268
  124.1 10.5 %collective-permute-start.7 = (f32[1,128,256]{2,1,0:T(8,128)S(1)}, f32[1,128,256]{2,1,0:T(8,128)S(1)}, u32[]{:S(2)}, u32[]{:S(2)}) collective-permute-start(f32[1,128,256]{2,1,0:T(8,128)S(1)} %constant_dynamic-slice_fusion), channel_id=1, source_target_pairs={{0,8},{2,10},{4,12},{6,14},{8,0},{10,2},{12,4},{14,6},{1,9},{3,11}... | collective-permute-start | bytes 393224 | tf_op jit(solution)/shard_map/ppermute | solution.py:268
  132.3 1.4 collective-permute-start.9
  134.4 3.7 %collective-permute-start.10 = (f32[2,8,256]{2,1,0:T(8,128)S(1)}, f32[2,8,256]{2,1,0:T(8,128)S(1)}, u32[]{:S(2)}, u32[]{:S(2)}) collective-permute-start(f32[2,8,256]{2,1,0:T(8,128)S(1)} %pad_maximum_fusion.3), channel_id=1, source_target_pairs={{0,2},{2,0},{4,6},{6,4},{8,10},{10,8},{12,14},{14,12},{1,3},{3,1},... | collective-permute-start | bytes 49160 | tf_op jit(solution)/shard_map/ppermute | solution.py:268
  138.9 3.7 %collective-permute-start.11 = (f32[2,8,256]{2,1,0:T(8,128)S(1)}, f32[2,8,256]{2,1,0:T(8,128)S(1)}, u32[]{:S(2)}, u32[]{:S(2)}) collective-permute-start(f32[2,8,256]{2,1,0:T(8,128)S(1)} %select_add_fusion.2), channel_id=1, source_target_pairs={{0,4},{2,6},{4,0},{6,2},{8,12},{10,14},{12,8},{14,10},{1,5},{3,7},... | collective-permute-start | bytes 49160 | tf_op jit(solution)/shard_map/ppermute | solution.py:268
  139.9 3.5 %collective-permute-start.8 = (f32[64,256]{1,0:T(8,128)S(1)}, f32[64,256]{1,0:T(8,128)S(1)}, u32[]{:S(2)}, u32[]{:S(2)}) collective-permute-start(f32[64,256]{1,0:T(8,128)S(1)} %get-tuple-element.19), channel_id=1, source_target_pairs={{0,1},{1,0},{2,3},{3,2},{4,5},{5,4},{6,7},{7,6},{8,9},{9,8},{10,11... | collective-permute-start | bytes 196616 | tf_op jit(solution)/shard_map/ppermute | solution.py:268
  143.4 4.6 %collective-permute-start.12 = (f32[2,8,256]{2,1,0:T(8,128)S(1)}, f32[2,8,256]{2,1,0:T(8,128)S(1)}, u32[]{:S(2)}, u32[]{:S(2)}) collective-permute-start(f32[2,8,256]{2,1,0:T(8,128)S(1)} %select_add_fusion.1), channel_id=1, source_target_pairs={{0,8},{2,10},{4,12},{6,14},{8,0},{10,2},{12,4},{14,6},{1,9},{3,11}... | collective-permute-start | bytes 49160 | tf_op jit(solution)/shard_map/ppermute | solution.py:268

commit v5 on v4

--- a/solution.py
+++ b/solution.py
@@ -18,16 +18,33 @@
     return high, low
 
 
-def product(left, right):
-    left_high, left_low = split(left)
-    right_high, right_low = split(right)
-    dot = functools.partial(jnp.dot, preferred_element_type=jnp.float32)
-    return dot(left_high, right_high) + (dot(left_high, right_low) + dot(left_low, right_high))
+def dot(left, right):
+    return jnp.dot(left, right, preferred_element_type=jnp.float32)
 
 
 def on_diagonal(size):
     rows = lax.broadcasted_iota(jnp.int32, (size, size), 0)
     return rows == lax.broadcasted_iota(jnp.int32, (size, size), 1)
+
+
+def split_tiles(kinship_ref, high_ref, low_ref):
+    block_count, positions, tile = kinship_ref.shape[:3]
+    diagonal_mask = on_diagonal(tile)
+    for row in range(block_count):
+        for position in range(positions):
+            values = kinship_ref[row, position]
+            if position == 0:
+                values = jnp.where(diagonal_mask, 0.0, values)
+            high, low = split(values)
+            high_ref[row, :, pl.ds(position * tile, tile)] = high
+            low_ref[row, :, pl.ds(position * tile, tile)] = low
+
+
+def product(high, low, blocks):
+    parts = [split(block) for block in blocks]
+    blocks_high = jnp.concatenate([part[0] for part in parts], axis=0)
+    blocks_low = jnp.concatenate([part[1] for part in parts], axis=0)
+    return dot(high, blocks_high) + (dot(low, blocks_high) + dot(high, blocks_low))
 
 
 def column_sums(values):
@@ -114,7 +131,7 @@
             total = total + kinship_ref[row, position]
         diagonal = jnp.sum(total, axis=1, keepdims=True)
         diagonal_ref[block, :] = diagonal
-        direction_ref[block, :] = phenotypes_ref[block, :] / diagonal
+        direction_ref[block, :] = phenotypes_ref[block, :] * (1.0 / diagonal)
     for other in range(devices):
         for slot in range(capacity):
             start = pl.multiple_of(blocks[other][slot] * tile, tile)
@@ -125,35 +142,30 @@
 
 def apply_kernel(devices, table_ref, kinship_hbm, direction_hbm, diagonal_ref, phenotypes_hbm, received_hbm,
                  scaled_hbm, outgoing_hbm, sums_ref, kinship_ref, direction_ref, phenotypes_ref, received_ref,
-                 scaled_ref, mapped_ref, semaphores):
+                 scaled_ref, high_ref, low_ref, semaphores):
     block_count, positions, tile = kinship_ref.shape[:3]
     columns = direction_ref.shape[1]
     copies = Copies(semaphores)
-    loads = [
-        copies.start(kinship_hbm, kinship_ref),
-        copies.start(direction_hbm, direction_ref),
-        copies.start(phenotypes_hbm, phenotypes_ref),
-    ]
-    arrivals = [copies.start(received_hbm, received_ref)]
-    wait_all(loads)
-    diagonal_mask = on_diagonal(tile)
+    tiles = copies.start(kinship_hbm, kinship_ref)
+    arrival = copies.start(received_hbm, received_ref)
+    loads = [copies.start(direction_hbm, direction_ref), copies.start(phenotypes_hbm, phenotypes_ref)]
     norm = jnp.zeros((SUBLANES, columns), jnp.float32)
     cross = jnp.zeros((SUBLANES, columns), jnp.float32)
+    tiles.wait()
+    split_tiles(kinship_ref, high_ref, low_ref)
+    wait_all(loads)
+    arrival.wait()
     for row in range(block_count):
         block = pl.ds(row * tile, tile)
         here = direction_ref[block, :]
+        blocks = [here]
+        for position in range(positions - 1):
+            entry = row * (positions - 1) + position
+            blocks.append(received_ref[table_ref[0, entry], table_ref[1, entry]])
+        mapped = product(high_ref[row], low_ref[row], blocks)
+        scaled_ref[block, :] = mapped * (1.0 / diagonal_ref[block, :])
         norm = norm + column_sums(here * phenotypes_ref[block, :])
-        mapped_ref[block, :] = product(jnp.where(diagonal_mask, 0.0, kinship_ref[row, 0]), here)
-    wait_all(arrivals)
-    for row in range(block_count):
-        block = pl.ds(row * tile, tile)
-        mapped = mapped_ref[block, :]
-        for position in range(1, positions):
-            entry = row * (positions - 1) + position - 1
-            there = received_ref[table_ref[0, entry], table_ref[1, entry]]
-            mapped = mapped + product(kinship_ref[row, position], there)
-        scaled_ref[block, :] = mapped / diagonal_ref[block, :]
-        cross = cross + column_sums(direction_ref[block, :] * mapped)
+        cross = cross + column_sums(here * mapped)
     sums_ref[...] = jnp.zeros_like(sums_ref)
     sums_ref[0:1, :] = jnp.sum(norm, axis=0, keepdims=True)
     sums_ref[1:2, :] = jnp.sum(cross, axis=0, keepdims=True)
@@ -167,50 +179,53 @@
 
 
 def curvature_kernel(devices, table_ref, kinship_hbm, direction_hbm, diagonal_ref, scaled_hbm, received_hbm,
-                     later_hbm, sums_ref, kinship_ref, direction_ref, scaled_ref, received_ref, later_ref, semaphores):
+                     later_hbm, sums_hbm, kinship_ref, direction_ref, scaled_ref, received_ref, later_ref, high_ref,
+                     low_ref, sums_ref, semaphores):
     block_count, positions, tile = kinship_ref.shape[:3]
     columns = direction_ref.shape[1]
     copies = Copies(semaphores)
+    tiles = copies.start(kinship_hbm, kinship_ref)
     loads = [
         copies.start(later_hbm, later_ref),
-        copies.start(kinship_hbm, kinship_ref),
         copies.start(direction_hbm, direction_ref),
         copies.start(scaled_hbm, scaled_ref),
+        copies.start(received_hbm, received_ref),
     ]
-    arrivals = [copies.start(received_hbm, received_ref)]
+    tiles.wait()
+    split_tiles(kinship_ref, high_ref, low_ref)
     wait_all(loads)
     first_sums = later_ref[0, pl.ds(tile, SUBLANES), :]
     for other in range(1, devices):
         first_sums = first_sums + later_ref[other, pl.ds(tile, SUBLANES), :]
     rho = first_sums[1:2, :] / first_sums[0:1, :]
-    diagonal_mask = on_diagonal(tile)
     norm = jnp.zeros((SUBLANES, columns), jnp.float32)
     bend = jnp.zeros((SUBLANES, columns), jnp.float32)
     for row in range(block_count):
         block = pl.ds(row * tile, tile)
         here = scaled_ref[block, :] - rho * direction_ref[block, :]
-        scaled_ref[block, :] = here
-        norm = norm + column_sums(here * here * diagonal_ref[block, :])
-        bend = bend + column_sums(here * product(jnp.where(diagonal_mask, 0.0, kinship_ref[row, 0]), here))
-    wait_all(arrivals)
-    for row in range(block_count):
-        mapped = jnp.zeros((tile, columns), jnp.float32)
-        for position in range(1, positions):
-            entry = row * (positions - 1) + position - 1
+        blocks = [here]
+        for position in range(positions - 1):
+            entry = row * (positions - 1) + position
             other = table_ref[0, entry]
             weight = table_ref[2, entry].astype(jnp.float32)
-            there = weight * (
+            blocks.append(weight * (
                 later_ref[other, pl.ds(0, tile), :] - rho * received_ref[other, table_ref[1, entry]]
-            )
-            mapped = mapped + product(kinship_ref[row, position], there)
-        bend = bend + column_sums(scaled_ref[pl.ds(row * tile, tile), :] * mapped)
+            ))
+        mapped = product(high_ref[row], low_ref[row], blocks)
+        norm = norm + column_sums(here * here * diagonal_ref[block, :])
+        bend = bend + column_sums(here * mapped)
     row_ids = lax.broadcasted_iota(jnp.int32, first_sums.shape, 0)
     sums = jnp.where(row_ids == 2, jnp.sum(norm, axis=0, keepdims=True), first_sums)
-    sums_ref[...] = jnp.where(row_ids == 3, jnp.sum(bend, axis=0, keepdims=True), sums)
-
-
-def coefficients(sums):
-    norm, cross, later_norm, bend = (sums[i:i + 1, :] for i in range(4))
+    sums = jnp.where(row_ids == 3, jnp.sum(bend, axis=0, keepdims=True), sums)
+    for i in range(2 * devices):
+        sums_ref[i] = sums
+    store = copies.start(sums_ref, sums_hbm)
+    store.wait()
+
+
+def coefficients(sums, shared):
+    norm, cross = sums[0:1, :], sums[1:2, :]
+    later_norm, bend = shared[2:3, :], shared[3:4, :]
     curve = norm + cross
     ratio = later_norm / curve
     step = jnp.where(later_norm > 0, later_norm / (later_norm + bend - later_norm * ratio), 0.0)
@@ -218,38 +233,47 @@
     return start * (1.0 + step * (ratio + cross / norm)), -start * step
 
 
-def finish_kernel(norm_scale, direction_hbm, scaled_hbm, direction_scores_hbm, scaled_scores_hbm, sums_hbm,
-                  *refs):
-    (solved_hbm, scores_ref, direction_ref, scaled_ref, direction_scores_ref, scaled_scores_ref, sums_ref,
-     semaphores) = refs
+def finish_kernel(devices, norm_scale, direction_hbm, scaled_hbm, direction_scores_hbm, scaled_scores_hbm,
+                  swapped_hbm, sums_hbm, solved_hbm, scores_ref, direction_ref, scaled_ref, direction_scores_ref,
+                  scaled_scores_ref, swapped_ref, sums_ref, semaphores):
     people, columns = direction_ref.shape
+    rows = scores_ref.shape[0]
     column = lax.axis_index("cols")
     copies = Copies(semaphores)
     arrival = copies.start(sums_hbm, sums_ref)
-    loads = [
-        copies.start(direction_hbm, direction_ref),
-        copies.start(scaled_hbm, scaled_ref),
-        copies.start(direction_scores_hbm, direction_scores_ref),
-        copies.start(scaled_scores_hbm, scaled_scores_ref),
+    vectors = [copies.start(direction_hbm, direction_ref), copies.start(scaled_hbm, scaled_ref)]
+    shares = [
+        copies.start(direction_scores_hbm.at[pl.ds(0, rows)], direction_scores_ref),
+        copies.start(scaled_scores_hbm.at[pl.ds(0, rows)], scaled_scores_ref),
+        copies.start(swapped_hbm, swapped_ref),
     ]
+
+    def total(which):
+        sums = sums_ref[which]
+        shared = sums
+        for i in range(1, devices):
+            shared = shared + sums_ref[2 * i + which]
+        return sums, shared
+
     arrival.wait()
-    along, across = coefficients(sums_ref[0])
-    other_along, other_across = coefficients(sums_ref[1])
-    wait_all(loads)
+    along, across = coefficients(*total(column))
+    other_along, other_across = coefficients(*total(1 - column))
+    wait_all(vectors)
     stores = []
-    rows = people // 4
+    part_rows = people // 4
     for part in range(4):
-        block = pl.ds(part * rows, rows)
+        block = pl.ds(part * part_rows, part_rows)
         direction_ref[block, :] = along * direction_ref[block, :] + across * scaled_ref[block, :]
         stores.append(copies.start(direction_ref.at[block], solved_hbm.at[block]))
-    for start, first, second, offset in (
-        (0, along, across, column * columns),
-        (columns, other_along, other_across, (1 - column) * columns),
-    ):
-        here = pl.ds(start, columns)
-        scores_ref[:, pl.ds(pl.multiple_of(offset, columns), columns)] = norm_scale * (
-            first * direction_scores_ref[:, here] + second * scaled_scores_ref[:, here]
-        )
+    wait_all(shares)
+    own = pl.multiple_of(column * columns, columns)
+    other = pl.multiple_of((1 - column) * columns, columns)
+    scores_ref[:, pl.ds(own, columns)] = norm_scale * (
+        along * direction_scores_ref[...] + across * scaled_scores_ref[...]
+    )
+    scores_ref[:, pl.ds(other, columns)] = norm_scale * (
+        other_along * swapped_ref[pl.ds(0, rows), :] + other_across * swapped_ref[pl.ds(rows, rows), :]
+    )
     wait_all(stores)
 
 
@@ -268,29 +292,18 @@
     return lax.ppermute(values, axis, [(i, i ^ step) for i in range(devices)])
 
 
-def share(values, devices):
-    me = lax.axis_index("samples")
-    rows = values.shape[0] // devices
-    values = values.reshape(devices, rows, -1)
-    step = 1
-    while step < devices:
-        bit = (me // step) % 2
-        halves = values.reshape(-1, 2, rows, values.shape[-1])
-        kept = lax.dynamic_index_in_dim(halves, bit, 1, keepdims=False)
-        given = lax.dynamic_index_in_dim(halves, 1 - bit, 1, keepdims=False)
-        values = kept + swap(given, "samples", devices, step)
-        step *= 2
-    return values.reshape(rows, -1)
-
-
-def total_sums(sums, devices):
-    both = jnp.stack([sums, swap(sums, "cols", 2, 1)])
-    is_share = (jnp.arange(SUBLANES) // 2 == 1)[None, :, None]
-    step = 1
-    while step < devices:
-        both = both + jnp.where(is_share, swap(both, "samples", devices, step), 0.0)
-        step *= 2
-    return both
+def halve(values, devices, step):
+    bit = (lax.axis_index("samples") // step) % 2
+    halves = values.reshape(-1, 2, *values.shape[1:])
+    kept = lax.dynamic_index_in_dim(halves, bit, 1, keepdims=False)
+    given = lax.dynamic_index_in_dim(halves, 1 - bit, 1, keepdims=False)
+    return kept, swap(given, "samples", devices, step)
+
+
+def halve_all(values, devices, steps):
+    for step in steps:
+        values = sum(halve(values, devices, step))
+    return values
 
 
 def per_device(kinship, relatives, variance, phenotypes, dosage):
@@ -309,6 +322,7 @@
     room = lambda *shape: pltpu.VMEM(shape, jnp.float32)
     full = float_of(people, columns)
     full_room = room(people, columns)
+    tiles_room = pltpu.VMEM((block_count, tile, positions * tile), jnp.bfloat16)
     direction, diagonal, table, outgoing = call(
         functools.partial(prepare_kernel, devices, capacity),
         [
@@ -333,16 +347,16 @@
         [values.reshape(people, devices, share_rows) for values in (dosage, swap(dosage, "cols", 2, 1))], axis=2
     ).reshape(people, 2 * variants)
 
-    def variant_sums(values):
+    def variant_products(values):
         partial = lax.dot_general(
             both_dosages, values, (((0,), (0,)), ((), ())), precision=lax.Precision.HIGH,
             preferred_element_type=jnp.float32,
         )
-        total = share(partial, devices)
-        return jnp.concatenate([total[:share_rows], swap(total[share_rows:], "cols", 2, 1)], axis=1)
-
+        return partial.reshape(devices, 2 * share_rows, columns)
+
+    steps = [2 ** i for i in range(devices.bit_length() - 1)]
     received = exchange(outgoing)
-    direction_scores = variant_sums(direction)
+    direction_scores = halve_all(variant_products(direction), devices, steps[:1])
     received, direction_scores = lax.optimization_barrier((received, direction_scores))
     scaled, outgoing = call(
         functools.partial(apply_kernel, devices),
@@ -351,34 +365,46 @@
         [hbm, hbm],
         [
             room(SUBLANES, columns),
-            room(*kinship.shape), full_room, full_room, room(devices, capacity, tile, columns), full_room, full_room,
+            room(*kinship.shape), full_room, full_room, room(devices, capacity, tile, columns), full_room,
+            tiles_room, tiles_room,
             pltpu.SemaphoreType.DMA((2 * devices + 5,)),
         ],
     )(table, kinship, direction, diagonal, phenotypes, received)
     later = exchange(outgoing)
-    scaled_scores = variant_sums(scaled)
+    scaled, direction_scores = lax.optimization_barrier((scaled, direction_scores))
+    scaled_scores = halve_all(variant_products(scaled), devices, steps[:1])
+    direction_scores = halve_all(direction_scores, devices, steps[1:2])
+    later, scaled_scores, direction_scores = lax.optimization_barrier((later, scaled_scores, direction_scores))
+    direction_kept, direction_given = halve(direction_scores, devices, steps[2])
+    scaled_kept, scaled_given = halve(scaled_scores, devices, steps[1])
     sums = call(
         functools.partial(curvature_kernel, devices),
-        float_of(SUBLANES, columns),
+        float_of(2 * devices, SUBLANES, columns),
         [smem, hbm, hbm, vmem, hbm, hbm, hbm],
-        vmem,
+        hbm,
         [
             room(*kinship.shape), full_room, full_room, room(devices, capacity, tile, columns),
-            room(devices, tile + SUBLANES, columns),
-            pltpu.SemaphoreType.DMA((5,)),
+            room(devices, tile + SUBLANES, columns), tiles_room, tiles_room,
+            room(2 * devices, SUBLANES, columns),
+            pltpu.SemaphoreType.DMA((6,)),
         ],
     )(table, kinship, direction, diagonal, scaled, received, later)
+    sums, direction_kept, scaled_kept = lax.optimization_barrier((sums, direction_kept, scaled_kept))
+    all_sums = lax.all_to_all(sums, ("samples", "cols"), split_axis=0, concat_axis=0, tiled=True)
+    direction_scores = halve_all(direction_kept + direction_given, devices, steps[3:])[0]
+    scaled_scores = halve_all(scaled_kept + scaled_given, devices, steps[2:])[0]
+    swapped = swap(jnp.concatenate([direction_scores[share_rows:], scaled_scores[share_rows:]]), "cols", 2, 1)
     solved, scores = call(
-        functools.partial(finish_kernel, 1.0 / math.sqrt(people * devices)),
+        functools.partial(finish_kernel, devices, 1.0 / math.sqrt(people * devices)),
         [full, float_of(share_rows, 2 * columns)],
-        [hbm] * 5,
+        [hbm] * 6,
         [hbm, vmem],
         [
-            full_room, full_room, room(share_rows, 2 * columns), room(share_rows, 2 * columns),
-            room(2, SUBLANES, columns),
-            pltpu.SemaphoreType.DMA((9,)),
+            full_room, full_room, room(share_rows, columns), room(share_rows, columns),
+            room(2 * share_rows, columns), room(2 * devices, SUBLANES, columns),
+            pltpu.SemaphoreType.DMA((10,)),
         ],
-    )(direction, scaled, direction_scores, scaled_scores, total_sums(sums, devices))
+    )(direction, scaled, direction_scores, scaled_scores, swapped, all_sums)
     return (solved, scores)
 
 

time: 152 us -> 127 us (0.84)
  waiting for transfers between devices: 96.2 us -> 70.6 us
  starting transfers between devices: 22.3 us -> 27 us
  other arithmetic: 8.02 us -> 4.66 us
    ppermute x13 -> x8, waiting for transfers between devices: 96.2 us -> 60.2 us  [swap(): return lax.ppermute(values, axis, [(i, i ^ step) for i in range(devices)])]
    all_to_all x2, waiting for transfers between devices: 0.01 us -> 10.4 us  [exchange(): lax.all_to_all(blocks, 'samples', split_axis=0, concat_axis=0, tiled=True)]
    all_to_all x0 -> x1, starting transfers between devices: none -> 3.52 us  [per_device(): lax.all_to_all(sums, ('samples', 'cols'), split_axis=0, concat_axis=0, ti...]
    add x9 -> x6, other arithmetic: 4.44 us -> 3.11 us  [the longest x4 3.06 us: halve_all(): values = sum(halve(values, devices, step))]
    ppermute x13 -> x8, starting transfers between devices: 11.1 us -> 11.7 us  [swap(): return lax.ppermute(values, axis, [(i, i ^ step) for i in range(devices)])]
    unnamed x9 -> x21, local copies, waits for them, and re-layouts: 3.36 us -> 3.02 us
  transfers between devices with their start and end apart: 15 -> 11, of which waited for: 10 -> 8; matrix products, arithmetic and copies ran while one was open for 6% -> 6% of each run, Pallas kernels for 6% -> 4%
where the time goes in v5:
time: 127 us
  waiting for transfers between devices  70.6 us (56%)
  starting transfers between devices  27 us (21%)
  Pallas kernels  17.7 us (14%)
  other arithmetic  4.66 us (4%)
  local copies, waits for them, and re-layouts  3.99 us (3%)
  matrix products  1.99 us (2%)
    ppermute x8, waiting for transfers between devices, swap(): return lax.ppermute(values, axis, [(i, i ^ step) for i in range(devices)])  60.2 us
    all_to_all x2, starting transfers between devices, exchange(): lax.all_to_all(blocks, 'samples', split_axis=0, concat_axis=0, tiled=True)  11.8 us
    ppermute x8, starting transfers between devices, swap(): return lax.ppermute(values, axis, [(i, i ^ step) for i in range(devices)])  11.7 us
    all_to_all x2, waiting for transfers between devices, exchange(): lax.all_to_all(blocks, 'samples', split_axis=0, concat_axis=0, tiled=True)  10.4 us
    pallas_call x1, Pallas kernels, per_device(): call(functools.partial(curvature_kernel, devices), float_of(2 * devices,...  5.16 us
    pallas_call x1, Pallas kernels, per_device(): call(functools.partial(apply_kernel, devices), [full, float_of(devices, t...  5.15 us
    pallas_call x1, Pallas kernels, per_device(): call(functools.partial(prepare_kernel, devices, capacity), [full, float_o...  4.59 us
    all_to_all x1, starting transfers between devices, per_device(): lax.all_to_all(sums, ('samples', 'cols'), split_axis=0, concat_axis=0, ti...  3.52 us
  transfers between devices with their start and end apart: 11, of which 8 were waited for; matrix products, arithmetic and copies ran while one was open for 6% of the time, Pallas kernels for 4%

profile of v5, /device:TPU:0, one launch (start us, length us, event | category | flops | bytes accessed | tf_op | source)
XLA Modules:
  0.0 126.9 jit_solution(17117634795614260402)
XLA Ops:
  0.6 4.6 %shard_map.68 = (f32[512,256]{1,0:T(8,128)}, f32[512,1]{1,0:T(8,128)}, s32[4,12]{1,0:T(4,128)}, f32[8,2,128,256]{3,2,1,0:T(8,128)}) custom-call(s32[3,32]{1,0:T(4,128)} %bitcast.54, f32[4,4,128,128]{3,2,1,0:T(8,128)} %kinship_hbm.5, f32[4,128]{1,0:T(4,128)} %bitcast.55, f32[512,256]{1,0:T(8,128)} %phenotypes_hbm.3), custom_call_target="tpu_custom_call" | custom-call | tf_op jit(solution)/shard_map/pallas_call | solution.py:326
  5.2 7.4 %all-to-all-start = ((f32[8,2,128,256]{3,2,1,0:T(8,128)}), f32[8,2,128,256]{3,2,1,0:T(8,128)}, u32[]{:S(2)}, u32[]{:S(2)}) async-start(f32[8,2,128,256]{3,2,1,0:T(8,128)} %get-tuple-element.21), calls=%async_computation | async-start | bytes 4194304 | tf_op jit(solution)/shard_map/all_to_all | solution.py:344
  13.1 2.6 %collective-permute-done = f32[512,512]{0,1:T(8,128)S(1)} collective-permute-done((f32[512,512]{0,1:T(8,128)S(1)}, f32[512,512]{0,1:T(8,128)S(1)}, u32[]{:S(2)}, u32[]{:S(2)}) %collective-permute-start) | collective-permute-done | bytes 1048608 | tf_op jit(solution)/shard_map/ppermute | solution.py:292
  15.7 1.0 copy-done.5
  16.7 1.5 %pad_maximum_fusion = f32[512,8,128]{0,2,1:T(8,128)S(1)} fusion(f32[512,8,64]{0,2,1:T(8,128)} %bitcast.51, f32[512,8,64]{0,2,1:T(8,128)S(1)} %bitcast.47), kind=kLoop, calls=%fused_computation | loop fusion | flops 524288 | bytes 4194304 | tf_op jit(solution)/shard_map/concatenate | solution.py:346
  20.1 2.0 %collective-permute-start.1 = (f32[4,128,256]{2,1,0:T(8,128)}, f32[4,128,256]{2,1,0:T(8,128)}, u32[]{:S(2)}, u32[]{:S(2)}) collective-permute-start(f32[4,128,256]{2,1,0:T(8,128)} %dynamic-slice_bitcast_fusion.1), channel_id=1, source_target_pairs={{0,2},{2,0},{4,6},{6,4},{8,10},{10,8},{12,14},{14,12},{1,3},{3,1},... | collective-permute-start | bytes 1572872 | tf_op jit(solution)/shard_map/ppermute | solution.py:292
  22.2 27.1 %collective-permute-done.1 = f32[4,128,256]{2,1,0:T(8,128)} collective-permute-done((f32[4,128,256]{2,1,0:T(8,128)}, f32[4,128,256]{2,1,0:T(8,128)}, u32[]{:S(2)}, u32[]{:S(2)}) %collective-permute-start.1) | collective-permute-done | bytes 524320 | tf_op jit(solution)/shard_map/ppermute | solution.py:292
  49.3 1.9 %bitcast_add_fusion.1 = f32[4,128,256]{2,1,0:T(8,128)} fusion(f32[4,128,256]{2,1,0:T(8,128)} %collective-permute-done.1, f32[4,2,128,256]{3,2,1,0:T(8,128)S(1)} %fusion.2, s32[]{:T(128)S(6)} %select_n.60), kind=kLoop, calls=%fused_computation.6 | loop fusion | flops 131072 | bytes 1572868 | tf_op jit(solution)/shard_map/add | solution.py:305
  51.2 9.8 %all-to-all-done.received_hbm = f32[8,2,128,256]{3,2,1,0:T(8,128)} async-done(((f32[8,2,128,256]{3,2,1,0:T(8,128)}), f32[8,2,128,256]{3,2,1,0:T(8,128)}, u32[]{:S(2)}, u32[]{:S(2)}) %all-to-all-start) | async-done | bytes 2097184 | tf_op jit(solution)/shard_map/all_to_all | solution.py:344
  61.0 5.1 %shard_map.69 = (f32[512,256]{1,0:T(8,128)}, f32[8,136,256]{2,1,0:T(8,128)}) custom-call(s32[4,12]{1,0:T(4,128)} %get-tuple-element.19.table_ref, f32[4,4,128,128]{3,2,1,0:T(8,128)} %kinship_hbm.5, f32[512,256]{1,0:T(8,128)} %get-tuple-element.18.direction_hbm, f32[512,1]{1,0:T(8,128)} %get-tuple-element.20.diagonal_ref, f32[512,256]{1,0:T(8,128)} %phenotypes_hbm.3, ...), custom_call_target="tpu_custom_call" | custom-call | tf_op jit(solution)/shard_map/pallas_call | solution.py:361
  66.2 4.4 %all-to-all-start.1 = ((f32[8,136,256]{2,1,0:T(8,128)}), f32[8,136,256]{2,1,0:T(8,128)}, u32[]{:S(2)}, u32[]{:S(2)}) async-start(f32[8,136,256]{2,1,0:T(8,128)} %get-tuple-element.26), calls=%async_computation.1 | async-start | bytes 2228224 | tf_op jit(solution)/shard_map/all_to_all | solution.py:344
  71.6 1.0 copy-done.2
  72.7 1.9 %collective-permute-start.2 = (f32[4,128,256]{2,1,0:T(8,128)S(1)}, f32[4,128,256]{2,1,0:T(8,128)S(1)}, u32[]{:S(2)}, u32[]{:S(2)}) collective-permute-start(f32[4,128,256]{2,1,0:T(8,128)S(1)} %dynamic-slice_bitcast_fusion), channel_id=1, source_target_pairs={{0,2},{2,0},{4,6},{6,4},{8,10},{10,8},{12,14},{14,12},{1,3},{3,1},... | collective-permute-start | bytes 1572872 | tf_op jit(solution)/shard_map/ppermute | solution.py:292
  74.6 1.5 %collective-permute-start.3 = (f32[2,128,256]{2,1,0:T(8,128)S(1)}, f32[2,128,256]{2,1,0:T(8,128)S(1)}, u32[]{:S(2)}, u32[]{:S(2)}) collective-permute-start(f32[2,128,256]{2,1,0:T(8,128)S(1)} %dynamic-slice_bitcast_fusion.4), channel_id=1, source_target_pairs={{0,4},{2,6},{4,0},{6,2},{8,12},{10,14},{12,8},{14,10},{1,5},{3,7},... | collective-permute-start | bytes 786440 | tf_op jit(solution)/shard_map/ppermute | solution.py:292
  76.2 17.7 %collective-permute-done.3 = f32[2,128,256]{2,1,0:T(8,128)S(1)} collective-permute-done((f32[2,128,256]{2,1,0:T(8,128)S(1)}, f32[2,128,256]{2,1,0:T(8,128)S(1)}, u32[]{:S(2)}, u32[]{:S(2)}) %collective-permute-start.3) | collective-permute-done | bytes 262176 | tf_op jit(solution)/shard_map/ppermute | solution.py:292
  93.9 2.0 %collective-permute-done.2 = f32[4,128,256]{2,1,0:T(8,128)S(1)} collective-permute-done((f32[4,128,256]{2,1,0:T(8,128)S(1)}, f32[4,128,256]{2,1,0:T(8,128)S(1)}, u32[]{:S(2)}, u32[]{:S(2)}) %collective-permute-start.2) | collective-permute-done | bytes 524320 | tf_op jit(solution)/shard_map/ppermute | solution.py:292
  95.9 1.1 bitcast_add_fusion
  98.6 2.3 %collective-permute-start.4 = (f32[1,128,256]{2,1,0:T(8,128)S(1)}, f32[1,128,256]{2,1,0:T(8,128)S(1)}, u32[]{:S(2)}, u32[]{:S(2)}) collective-permute-start(f32[1,128,256]{2,1,0:T(8,128)S(1)} %get-tuple-element.36), channel_id=1, source_target_pairs={{0,8},{2,10},{4,12},{6,14},{8,0},{10,2},{12,4},{14,6},{1,9},{3,11}... | collective-permute-start | bytes 393224 | tf_op jit(solution)/shard_map/ppermute | solution.py:292
  100.9 5.2 %shard_map.70 = f32[16,8,256]{2,1,0:T(8,128)} custom-call(s32[4,12]{1,0:T(4,128)} %get-tuple-element.19.table_ref, f32[4,4,128,128]{3,2,1,0:T(8,128)} %kinship_hbm.5, f32[512,256]{1,0:T(8,128)} %get-tuple-element.18.direction_hbm, f32[512,1]{1,0:T(8,128)} %get-tuple-element.20.diagonal_ref, f32[512,256]{1,0:T(8,128)} %get-tuple-element.25.scaled_hbm, ...), custom_call_target="tpu_custom_call" | custom-call | tf_op jit(solution)/shard_map/pallas_call | solution.py:380
  106.0 3.5 %all-to-all-start.2 = ((f32[16,8,256]{2,1,0:T(8,128)}), f32[16,8,256]{2,1,0:T(8,128)S(1)}, u32[]{:S(2)}, u32[]{:S(2)}) async-start(f32[16,8,256]{2,1,0:T(8,128)} %shard_map.70), calls=%async_computation.2 | async-start | bytes 262144 | tf_op jit(solution)/shard_map/all_to_all | solution.py:393
  109.7 2.8 %collective-permute-start.6 = (f32[1,128,256]{2,1,0:T(8,128)S(1)}, f32[1,128,256]{2,1,0:T(8,128)S(1)}, u32[]{:S(2)}, u32[]{:S(2)}) collective-permute-start(f32[1,128,256]{2,1,0:T(8,128)S(1)} %constant_dynamic-slice_fusion), channel_id=1, source_target_pairs={{0,8},{2,10},{4,12},{6,14},{8,0},{10,2},{12,4},{14,6},{1,9},{3,11}... | collective-permute-start | bytes 393224 | tf_op jit(solution)/shard_map/ppermute | solution.py:292
  112.5 9.4 %collective-permute-done.6 = f32[1,128,256]{2,1,0:T(8,128)S(1)} collective-permute-done((f32[1,128,256]{2,1,0:T(8,128)S(1)}, f32[1,128,256]{2,1,0:T(8,128)S(1)}, u32[]{:S(2)}, u32[]{:S(2)}) %collective-permute-start.6) | collective-permute-done | bytes 131104 | tf_op jit(solution)/shard_map/ppermute | solution.py:292
  122.1 1.3 %collective-permute-done.7.swapped_hbm = f32[128,256]{1,0:T(8,128)S(1)} collective-permute-done((f32[128,256]{1,0:T(8,128)S(1)}, f32[128,256]{1,0:T(8,128)S(1)}, u32[]{:S(2)}, u32[]{:S(2)}) %collective-permute-start.7) | collective-permute-done | bytes 131104 | tf_op jit(solution)/shard_map/ppermute | solution.py:292
  124.1 2.8 %shard_map.71 = (f32[512,256]{1,0:T(8,128)}, f32[64,512]{1,0:T(8,128)}) custom-call(f32[512,256]{1,0:T(8,128)} %get-tuple-element.18.direction_hbm, f32[512,256]{1,0:T(8,128)} %get-tuple-element.25.scaled_hbm, f32[128,256]{1,0:T(8,128)} %bitcast.52, f32[128,256]{1,0:T(8,128)} %bitcast.53, f32[128,256]{1,0:T(8,128)} %copy-done.9, f32[16,8,256]{2,1,0:T(8,128)} %copy-done.8), custom_call_target="tpu_custom_call" | custom-call | tf_op jit(solution)/shard_map/pallas_call | solution.py:397
  (41 shorter events, 5.8 us)
Async XLA Ops:
  5.2 7.4 %copy-start.4 = (f32[512,512]{1,0:T(8,128)S(1)}, f32[512,512]{1,0:T(8,128)}, u32[]{:S(2)}) copy-start(f32[512,512]{1,0:T(8,128)} %param.9) | copy-start | bytes 3145732
  5.2 55.8 %all-to-all-start = ((f32[8,2,128,256]{3,2,1,0:T(8,128)}), f32[8,2,128,256]{3,2,1,0:T(8,128)}, u32[]{:S(2)}, u32[]{:S(2)}) async-start(f32[8,2,128,256]{3,2,1,0:T(8,128)} %get-tuple-element.21), calls=%async_computation | async-start | bytes 4194304 | tf_op jit(solution)/shard_map/all_to_all | solution.py:344
  13.0 2.7 %collective-permute-start = (f32[512,512]{0,1:T(8,128)S(1)}, f32[512,512]{0,1:T(8,128)S(1)}, u32[]{:S(2)}, u32[]{:S(2)}) collective-permute-start(f32[512,512]{0,1:T(8,128)S(1)} %copy.8), channel_id=1, source_target_pairs={{0,1},{1,0},{2,3},{3,2},{4,5},{5,4},{6,7},{7,6},{8,9},{9,8},{10,11... | collective-permute-start | bytes 3145736 | tf_op jit(solution)/shard_map/ppermute | solution.py:292
  15.7 1.0 copy-start.5
  16.7 1.5 %copy-start = (f32[512,256]{1,0:T(8,128)S(1)}, f32[512,256]{1,0:T(8,128)}, u32[]{:S(2)}) copy-start(f32[512,256]{1,0:T(8,128)} %get-tuple-element.18.direction_hbm) | copy-start | bytes 1572868
  20.1 29.2 %collective-permute-start.1 = (f32[4,128,256]{2,1,0:T(8,128)}, f32[4,128,256]{2,1,0:T(8,128)}, u32[]{:S(2)}, u32[]{:S(2)}) collective-permute-start(f32[4,128,256]{2,1,0:T(8,128)} %dynamic-slice_bitcast_fusion.1), channel_id=1, source_target_pairs={{0,2},{2,0},{4,6},{6,4},{8,10},{10,8},{12,14},{14,12},{1,3},{3,1},... | collective-permute-start | bytes 1572872 | tf_op jit(solution)/shard_map/ppermute | solution.py:292
  66.2 4.4 %copy-start.1 = (f32[512,256]{1,0:T(8,128)S(1)}, f32[512,256]{1,0:T(8,128)}, u32[]{:S(2)}) copy-start(f32[512,256]{1,0:T(8,128)} %get-tuple-element.25.scaled_hbm) | copy-start | bytes 1572868
  66.2 31.4 %all-to-all-start.1 = ((f32[8,136,256]{2,1,0:T(8,128)}), f32[8,136,256]{2,1,0:T(8,128)}, u32[]{:S(2)}, u32[]{:S(2)}) async-start(f32[8,136,256]{2,1,0:T(8,128)} %get-tuple-element.26), calls=%async_computation.1 | async-start | bytes 2228224 | tf_op jit(solution)/shard_map/all_to_all | solution.py:344
  70.6 4.0 %copy-start.3 = (f32[4,128,256]{2,1,0:T(8,128)S(1)}, f32[4,128,256]{2,1,0:T(8,128)}, u32[]{:S(2)}) copy-start(f32[4,128,256]{2,1,0:T(8,128)} %bitcast_add_fusion.1) | copy-start | bytes 1572868
  71.6 1.0 copy-start.2
  72.7 23.2 %collective-permute-start.2 = (f32[4,128,256]{2,1,0:T(8,128)S(1)}, f32[4,128,256]{2,1,0:T(8,128)S(1)}, u32[]{:S(2)}, u32[]{:S(2)}) collective-permute-start(f32[4,128,256]{2,1,0:T(8,128)S(1)} %dynamic-slice_bitcast_fusion), channel_id=1, source_target_pairs={{0,2},{2,0},{4,6},{6,4},{8,10},{10,8},{12,14},{14,12},{1,3},{3,1},... | collective-permute-start | bytes 1572872 | tf_op jit(solution)/shard_map/ppermute | solution.py:292
  74.6 19.2 %collective-permute-start.3 = (f32[2,128,256]{2,1,0:T(8,128)S(1)}, f32[2,128,256]{2,1,0:T(8,128)S(1)}, u32[]{:S(2)}, u32[]{:S(2)}) collective-permute-start(f32[2,128,256]{2,1,0:T(8,128)S(1)} %dynamic-slice_bitcast_fusion.4), channel_id=1, source_target_pairs={{0,4},{2,6},{4,0},{6,2},{8,12},{10,14},{12,8},{14,10},{1,5},{3,7},... | collective-permute-start | bytes 786440 | tf_op jit(solution)/shard_map/ppermute | solution.py:292
  97.6 12.0 %collective-permute-start.5 = (f32[2,128,256]{2,1,0:T(8,128)S(1)}, f32[2,128,256]{2,1,0:T(8,128)S(1)}, u32[]{:S(2)}, u32[]{:S(2)}) collective-permute-start(f32[2,128,256]{2,1,0:T(8,128)S(1)} %get-tuple-element.34), channel_id=1, source_target_pairs={{0,4},{2,6},{4,0},{6,2},{8,12},{10,14},{12,8},{14,10},{1,5},{3,7},... | collective-permute-start | bytes 786440 | tf_op jit(solution)/shard_map/ppermute | solution.py:292
  98.6 11.0 %collective-permute-start.4 = (f32[1,128,256]{2,1,0:T(8,128)S(1)}, f32[1,128,256]{2,1,0:T(8,128)S(1)}, u32[]{:S(2)}, u32[]{:S(2)}) collective-permute-start(f32[1,128,256]{2,1,0:T(8,128)S(1)} %get-tuple-element.36), channel_id=1, source_target_pairs={{0,8},{2,10},{4,12},{6,14},{8,0},{10,2},{12,4},{14,6},{1,9},{3,11}... | collective-permute-start | bytes 393224 | tf_op jit(solution)/shard_map/ppermute | solution.py:292
  106.0 16.1 %all-to-all-start.2 = ((f32[16,8,256]{2,1,0:T(8,128)}), f32[16,8,256]{2,1,0:T(8,128)S(1)}, u32[]{:S(2)}, u32[]{:S(2)}) async-start(f32[16,8,256]{2,1,0:T(8,128)} %shard_map.70), calls=%async_computation.2 | async-start | bytes 262144 | tf_op jit(solution)/shard_map/all_to_all | solution.py:393
  109.6 13.8 %copy-start.6 = (f32[1,128,256]{2,1,0:T(8,128)}, f32[1,128,256]{2,1,0:T(8,128)S(1)}, u32[]{:S(2)}) copy-start(f32[1,128,256]{2,1,0:T(8,128)S(1)} %add.76) | copy-start | bytes 393220
  109.7 12.3 %collective-permute-start.6 = (f32[1,128,256]{2,1,0:T(8,128)S(1)}, f32[1,128,256]{2,1,0:T(8,128)S(1)}, u32[]{:S(2)}, u32[]{:S(2)}) collective-permute-start(f32[1,128,256]{2,1,0:T(8,128)S(1)} %constant_dynamic-slice_fusion), channel_id=1, source_target_pairs={{0,8},{2,10},{4,12},{6,14},{8,0},{10,2},{12,4},{14,6},{1,9},{3,11}... | collective-permute-start | bytes 393224 | tf_op jit(solution)/shard_map/ppermute | solution.py:292
  122.0 1.5 %copy-start.7 = (f32[1,128,256]{2,1,0:T(8,128)}, f32[1,128,256]{2,1,0:T(8,128)S(1)}, u32[]{:S(2)}) copy-start(f32[1,128,256]{2,1,0:T(8,128)S(1)} %dynamic-slice_add_fusion) | copy-start | bytes 393220
  122.0 1.4 %collective-permute-start.7 = (f32[128,256]{1,0:T(8,128)S(1)}, f32[128,256]{1,0:T(8,128)S(1)}, u32[]{:S(2)}, u32[]{:S(2)}) collective-permute-start(f32[128,256]{1,0:T(8,128)S(1)} %pad_maximum_fusion.1), channel_id=1, source_target_pairs={{0,1},{1,0},{2,3},{3,2},{4,5},{5,4},{6,7},{7,6},{8,9},{9,8},{10,11... | collective-permute-start | bytes 393224 | tf_op jit(solution)/shard_map/ppermute | solution.py:292
  122.1 1.3 %copy-start.8 = (f32[16,8,256]{2,1,0:T(8,128)}, f32[16,8,256]{2,1,0:T(8,128)S(1)}, u32[]{:S(2)}) copy-start(f32[16,8,256]{2,1,0:T(8,128)S(1)} %all-to-all-done.2.sums_hbm) | copy-start | bytes 393220
  123.4 0.6 copy-start.9

commit v6 on v5

--- a/solution.py
+++ b/solution.py
@@ -75,10 +75,12 @@
     return lax.div(value, jnp.int32(divisor))
 
 
-def prepare_kernel(devices, capacity, list_ref, kinship_hbm, variance_hbm, phenotypes_hbm, *refs):
-    (direction_hbm, diagonal_ref, table_ref, outgoing_hbm, kinship_ref, variance_ref, phenotypes_ref, direction_ref,
-     first_ref, last_ref, semaphores) = refs
+def prepare_kernel(devices, capacity, list_ref, kinship_hbm, variance_hbm, phenotypes_hbm, direction_hbm, left_hbm,
+                   right_hbm, diagonal_ref, table_ref, forward_ref, outgoing_hbm, kinship_ref, variance_ref,
+                   phenotypes_ref, direction_ref, first_ref, last_ref, semaphores):
     block_count, positions, tile = kinship_ref.shape[:3]
+    columns = direction_ref.shape[1]
+    half = devices // 2
     copies = Copies(semaphores)
     loads = [copies.start(variance_hbm, variance_ref)]
     for row in range(block_count):
@@ -86,40 +88,56 @@
         loads.append(copies.start(kinship_hbm.at[row], kinship_ref.at[row]))
         loads.append(copies.start(phenotypes_hbm.at[block], phenotypes_ref.at[block]))
     me = lax.axis_index("samples")
-    spare = jnp.where(me == 0, 1, 0)
+    partner = me ^ half
+    base = me & half
+    spare = me ^ 1
     top = block_count * block_count
-    for j in range(devices):
-        first_ref[j] = jnp.int32(top)
-        last_ref[j] = jnp.int32(-1)
-    entries = []
-    for row in range(block_count):
-        for position in range(positions - 1):
-            listed = list_ref[position, me * block_count + row]
-            live = listed >= 0
-            safe = jnp.maximum(listed, 0)
-            other = quotient(safe, block_count)
-            far_block = safe - other * block_count
-            key = jnp.where(me < other, row * block_count + far_block, far_block * block_count + row)
-            first_ref[other] = jnp.minimum(first_ref[other], jnp.where(live, key, top))
-            last_ref[other] = jnp.maximum(last_ref[other], jnp.where(live, key, -1))
-            entries.append((live, other, key))
-    for entry, (live, other, key) in enumerate(entries):
+
+    def collect(device):
+        for j in range(devices):
+            first_ref[j] = jnp.int32(top)
+            last_ref[j] = jnp.int32(-1)
+        found = []
+        for row in range(block_count):
+            for position in range(positions - 1):
+                listed = list_ref[position, device * block_count + row]
+                live = listed >= 0
+                safe = jnp.maximum(listed, 0)
+                other = quotient(safe, block_count)
+                far_block = safe - other * block_count
+                key = jnp.where(device < other, row * block_count + far_block, far_block * block_count + row)
+                first_ref[other] = jnp.minimum(first_ref[other], jnp.where(live, key, top))
+                last_ref[other] = jnp.maximum(last_ref[other], jnp.where(live, key, -1))
+                found.append((live, other, far_block, key))
+        return found
+
+    def blocks_for(device, other):
+        blocks = []
+        for key in (first_ref[other], last_ref[other]):
+            safe = jnp.clip(key, 0, top - 1)
+            lower = quotient(safe, block_count)
+            higher = safe - lower * block_count
+            blocks.append(jnp.where(key == safe, jnp.where(device < other, lower, higher), 0))
+        return blocks
+
+    collect(partner)
+    for i in range(half):
+        blocks = blocks_for(partner, base + i)
+        for slot in range(capacity):
+            forward_ref[slot, i] = blocks[slot]
+    for entry, (live, other, far_block, key) in enumerate(collect(me)):
         first, last = first_ref[other], last_ref[other]
         handled = jnp.where(me < other, first, last)
         weight = jnp.where(first == last, 1, 2)
-        table_ref[0, entry] = jnp.where(live, other, spare)
-        table_ref[1, entry] = jnp.where(live & (key != first), capacity - 1, 0)
+        slot = jnp.where(key == first, 0, capacity - 1)
+        place = jnp.where(other == partner, devices * capacity + far_block, other * capacity + slot)
+        table_ref[0, entry] = jnp.where(live, place, spare * capacity)
+        table_ref[1, entry] = jnp.where(live, other, spare)
         table_ref[2, entry] = jnp.where(live & (key == handled), weight, 0)
-
-    def mine(key, other):
-        lower = quotient(jnp.clip(key, 0, top - 1), block_count)
-        higher = jnp.clip(key, 0, top - 1) - lower * block_count
-        return jnp.where((key >= 0) & (key < top), jnp.where(me < other, lower, higher), 0)
-
-    blocks = []
     for other in range(devices):
-        blocks.append((mine(first_ref[other], other), mine(last_ref[other], other)))
-        table_ref[3, other] = jnp.where(me < other, blocks[-1][1], blocks[-1][0])
+        blocks = blocks_for(me, other)
+        table_ref[3, other] = jnp.where(me < other, blocks[1], blocks[0])
+    near = [blocks_for(me, base + i) for i in range(half)]
     stores = []
     diagonal_mask = on_diagonal(tile)
     loads[0].wait()
@@ -132,36 +150,68 @@
         diagonal = jnp.sum(total, axis=1, keepdims=True)
         diagonal_ref[block, :] = diagonal
         direction_ref[block, :] = phenotypes_ref[block, :] * (1.0 / diagonal)
-    for other in range(devices):
+        stores.append(copies.start(direction_ref.at[block, pl.ds(0, columns // 2)], left_hbm.at[row]))
+        stores.append(copies.start(direction_ref.at[block, pl.ds(columns // 2, columns // 2)], right_hbm.at[row]))
+        stores.append(copies.start(direction_ref.at[block], direction_hbm.at[block]))
+    for i in range(half):
         for slot in range(capacity):
-            start = pl.multiple_of(blocks[other][slot] * tile, tile)
-            stores.append(copies.start(direction_ref.at[pl.ds(start, tile)], outgoing_hbm.at[other, slot]))
-    stores.append(copies.start(direction_ref, direction_hbm))
+            start = pl.multiple_of(near[i][slot] * tile, tile)
+            stores.append(copies.start(direction_ref.at[pl.ds(start, tile)], outgoing_hbm.at[i * capacity + slot]))
     wait_all(stores)
 
 
-def apply_kernel(devices, table_ref, kinship_hbm, direction_hbm, diagonal_ref, phenotypes_hbm, received_hbm,
-                 scaled_hbm, outgoing_hbm, sums_ref, kinship_ref, direction_ref, phenotypes_ref, received_ref,
+def forward_kernel(forward_ref, partner_hbm, outgoing_hbm, semaphores):
+    capacity, half = forward_ref.shape
+    copies = Copies(semaphores)
+    stores = []
+    for i in range(half):
+        for slot in range(capacity):
+            stores.append(copies.start(partner_hbm.at[forward_ref[slot, i]], outgoing_hbm.at[i * capacity + slot]))
+    wait_all(stores)
+
+
+def load_received(copies, devices, capacity, near_hbm, far_hbm, partner_hbm, received_ref):
+    half = devices // 2
+    base = lax.axis_index("samples") & half
+    width = received_ref.shape[2] // 2
+    count = half * capacity
+    loads = [copies.start(near_hbm, received_ref.at[pl.ds(base * capacity, count)])]
+    for side in range(2):
+        lanes = pl.ds(side * width, width)
+        loads.append(copies.start(
+            far_hbm[side], received_ref.at[pl.ds((half - base) * capacity, count), :, lanes]
+        ))
+        loads.append(copies.start(
+            partner_hbm[side], received_ref.at[pl.ds(devices * capacity, partner_hbm[side].shape[0]), :, lanes]
+        ))
+    return loads
+
+
+def apply_kernel(devices, capacity, table_ref, kinship_hbm, direction_hbm, diagonal_ref, phenotypes_hbm, near_hbm,
+                 far_left_hbm, far_right_hbm, partner_left_hbm, partner_right_hbm, scaled_hbm, outgoing_hbm, sums_ref, kinship_ref, direction_ref, phenotypes_ref, received_ref,
                  scaled_ref, high_ref, low_ref, semaphores):
     block_count, positions, tile = kinship_ref.shape[:3]
     columns = direction_ref.shape[1]
     copies = Copies(semaphores)
     tiles = copies.start(kinship_hbm, kinship_ref)
-    arrival = copies.start(received_hbm, received_ref)
+    arrivals = load_received(
+        copies, devices, capacity, near_hbm, (far_left_hbm, far_right_hbm), (partner_left_hbm, partner_right_hbm),
+        received_ref,
+    )
     loads = [copies.start(direction_hbm, direction_ref), copies.start(phenotypes_hbm, phenotypes_ref)]
     norm = jnp.zeros((SUBLANES, columns), jnp.float32)
     cross = jnp.zeros((SUBLANES, columns), jnp.float32)
     tiles.wait()
     split_tiles(kinship_ref, high_ref, low_ref)
     wait_all(loads)
-    arrival.wait()
+    wait_all(arrivals)
     for row in range(block_count):
         block = pl.ds(row * tile, tile)
         here = direction_ref[block, :]
         blocks = [here]
         for position in range(positions - 1):
             entry = row * (positions - 1) + position
-            blocks.append(received_ref[table_ref[0, entry], table_ref[1, entry]])
+            blocks.append(received_ref[table_ref[0, entry]])
         mapped = product(high_ref[row], low_ref[row], blocks)
         scaled_ref[block, :] = mapped * (1.0 / diagonal_ref[block, :])
         norm = norm + column_sums(here * phenotypes_ref[block, :])
@@ -178,8 +228,8 @@
     wait_all(stores)
 
 
-def curvature_kernel(devices, table_ref, kinship_hbm, direction_hbm, diagonal_ref, scaled_hbm, received_hbm,
-                     later_hbm, sums_hbm, kinship_ref, direction_ref, scaled_ref, received_ref, later_ref, high_ref,
+def curvature_kernel(devices, capacity, table_ref, kinship_hbm, direction_hbm, diagonal_ref, scaled_hbm, near_hbm,
+                     far_left_hbm, far_right_hbm, partner_left_hbm, partner_right_hbm, later_hbm, sums_hbm, kinship_ref, direction_ref, scaled_ref, received_ref, later_ref, high_ref,
                      low_ref, sums_ref, semaphores):
     block_count, positions, tile = kinship_ref.shape[:3]
     columns = direction_ref.shape[1]
@@ -189,8 +239,11 @@
         copies.start(later_hbm, later_ref),
         copies.start(direction_hbm, direction_ref),
         copies.start(scaled_hbm, scaled_ref),
-        copies.start(received_hbm, received_ref),
     ]
+    loads += load_received(
+        copies, devices, capacity, near_hbm, (far_left_hbm, far_right_hbm), (partner_left_hbm, partner_right_hbm),
+        received_ref,
+    )
     tiles.wait()
     split_tiles(kinship_ref, high_ref, low_ref)
     wait_all(loads)
@@ -206,11 +259,9 @@
         blocks = [here]
         for position in range(positions - 1):
             entry = row * (positions - 1) + position
-            other = table_ref[0, entry]
             weight = table_ref[2, entry].astype(jnp.float32)
-            blocks.append(weight * (
-                later_ref[other, pl.ds(0, tile), :] - rho * received_ref[other, table_ref[1, entry]]
-            ))
+            there = later_ref[table_ref[1, entry], pl.ds(0, tile), :]
+            blocks.append(weight * (there - rho * received_ref[table_ref[0, entry]]))
         mapped = product(high_ref[row], low_ref[row], blocks)
         norm = norm + column_sums(here * here * diagonal_ref[block, :])
         bend = bend + column_sums(here * mapped)
@@ -323,25 +374,41 @@
     full = float_of(people, columns)
     full_room = room(people, columns)
     tiles_room = pltpu.VMEM((block_count, tile, positions * tile), jnp.bfloat16)
-    direction, diagonal, table, outgoing = call(
+    half = devices // 2
+    side = float_of(block_count, tile, columns // 2)
+    direction, left, right, diagonal, table, forward, outgoing = call(
         functools.partial(prepare_kernel, devices, capacity),
         [
-            full,
+            full, side, side,
             float_of(people, 1),
             jax.ShapeDtypeStruct((4, max(entries, devices)), jnp.int32),
-            float_of(devices, capacity, tile, columns),
+            jax.ShapeDtypeStruct((capacity, half), jnp.int32),
+            float_of(half * capacity, tile, columns),
         ],
         [smem, hbm, hbm, hbm],
-        [hbm, vmem, smem, hbm],
+        [hbm, hbm, hbm, vmem, smem, smem, hbm],
         [
             room(*kinship.shape), room(block_count, tile), full_room, full_room,
             pltpu.SMEM((devices,), jnp.int32), pltpu.SMEM((devices,), jnp.int32),
-            pltpu.SemaphoreType.DMA((2 * block_count + capacity * devices + 2,)),
+            pltpu.SemaphoreType.DMA((5 * block_count + capacity * half + 1,)),
         ],
     )(relatives.T, kinship, variance.reshape(block_count, tile), phenotypes)
 
-    def exchange(blocks):
-        return lax.all_to_all(blocks, "samples", split_axis=0, concat_axis=0, tiled=True)
+    def exchange(blocks, groups=None):
+        return lax.all_to_all(
+            blocks, "samples", split_axis=0, concat_axis=0, axis_index_groups=groups, tiled=True
+        )
+
+    halves = [list(range(half)), list(range(half, devices))]
+
+    def hand_on(partner_blocks):
+        return exchange(call(
+            forward_kernel,
+            float_of(half * capacity, tile, columns // 2),
+            [smem, hbm],
+            hbm,
+            [pltpu.SemaphoreType.DMA((half * capacity,))],
+        )(forward, partner_blocks), halves)
 
     both_dosages = jnp.concatenate(
         [values.reshape(people, devices, share_rows) for values in (dosage, swap(dosage, "cols", 2, 1))], axis=2
@@ -355,21 +422,23 @@
         return partial.reshape(devices, 2 * share_rows, columns)
 
     steps = [2 ** i for i in range(devices.bit_length() - 1)]
-    received = exchange(outgoing)
+    partners = [swap(blocks, "samples", devices, half) for blocks in (left, right)]
+    near = exchange(outgoing, halves)
+    received = [near] + [hand_on(blocks) for blocks in partners] + partners
     direction_scores = halve_all(variant_products(direction), devices, steps[:1])
     received, direction_scores = lax.optimization_barrier((received, direction_scores))
     scaled, outgoing = call(
-        functools.partial(apply_kernel, devices),
+        functools.partial(apply_kernel, devices, capacity),
         [full, float_of(devices, tile + SUBLANES, columns)],
-        [smem, hbm, hbm, vmem, hbm, hbm],
+        [smem, hbm, hbm, vmem] + [hbm] * 6,
         [hbm, hbm],
         [
             room(SUBLANES, columns),
-            room(*kinship.shape), full_room, full_room, room(devices, capacity, tile, columns), full_room,
+            room(*kinship.shape), full_room, full_room, room(devices * capacity + block_count, tile, columns), full_room,
             tiles_room, tiles_room,
-            pltpu.SemaphoreType.DMA((2 * devices + 5,)),
+            pltpu.SemaphoreType.DMA((2 * devices + 9,)),
         ],
-    )(table, kinship, direction, diagonal, phenotypes, received)
+    )(table, kinship, direction, diagonal, phenotypes, *received)
     later = exchange(outgoing)
     scaled, direction_scores = lax.optimization_barrier((scaled, direction_scores))
     scaled_scores = halve_all(variant_products(scaled), devices, steps[:1])
@@ -378,17 +447,17 @@
     direction_kept, direction_given = halve(direction_scores, devices, steps[2])
     scaled_kept, scaled_given = halve(scaled_scores, devices, steps[1])
     sums = call(
-        functools.partial(curvature_kernel, devices),
+        functools.partial(curvature_kernel, devices, capacity),
         float_of(2 * devices, SUBLANES, columns),
-        [smem, hbm, hbm, vmem, hbm, hbm, hbm],
+        [smem, hbm, hbm, vmem] + [hbm] * 7,
         hbm,
         [
-            room(*kinship.shape), full_room, full_room, room(devices, capacity, tile, columns),
+            room(*kinship.shape), full_room, full_room, room(devices * capacity + block_count, tile, columns),
             room(devices, tile + SUBLANES, columns), tiles_room, tiles_room,
             room(2 * devices, SUBLANES, columns),
-            pltpu.SemaphoreType.DMA((6,)),
+            pltpu.SemaphoreType.DMA((10,)),
         ],
-    )(table, kinship, direction, diagonal, scaled, received, later)
+    )(table, kinship, direction, diagonal, scaled, *received, later)
     sums, direction_kept, scaled_kept = lax.optimization_barrier((sums, direction_kept, scaled_kept))
     all_sums = lax.all_to_all(sums, ("samples", "cols"), split_axis=0, concat_axis=0, tiled=True)
     direction_scores = halve_all(direction_kept + direction_given, devices, steps[3:])[0]

time: 127 us -> 186 us (1.46)
  Pallas kernels: 17.7 us -> 53.2 us
  blocking collectives: 0 us -> 15.8 us
  starting transfers between devices: 27 us -> 34.1 us
  waiting for transfers between devices: 70.6 us -> 67.4 us
  local copies, waits for them, and re-layouts: 3.99 us -> 6.27 us
    pallas_call x3 -> x5, Pallas kernels: 14.9 us -> 50.4 us  [the longest x2 35.5 us: hand_on(): call(forward_kernel, float_of(half * capacity, tile, columns // 2), [smem...]
    all_to_all x0 -> x1, blocking collectives: none -> 15.8 us  [exchange(): lax.all_to_all(blocks, 'samples', split_axis=0, concat_axis=0, axis_index...]
    all_to_all x2 -> x3, waiting for transfers between devices: 10.4 us -> 0.5 us  [exchange(): lax.all_to_all(blocks, 'samples', split_axis=0, concat_axis=0, axis_index...]
    ppermute x8 -> x10, starting transfers between devices: 11.7 us -> 18.8 us  [swap(): return lax.ppermute(values, axis, [(i, i ^ step) for i in range(devices)])]
    ppermute x8 -> x10, waiting for transfers between devices: 60.2 us -> 66.9 us  [swap(): return lax.ppermute(values, axis, [(i, i ^ step) for i in range(devices)])]
    unnamed x21 -> x31, local copies, waits for them, and re-layouts: 3.02 us -> 5.31 us
    all_to_all x2 -> x3, starting transfers between devices: 11.8 us -> 11.8 us  [exchange(): lax.all_to_all(blocks, 'samples', split_axis=0, concat_axis=0, axis_index...]
  transfers between devices with their start and end apart: 11 -> 14, of which waited for: 8 -> 8; matrix products, arithmetic and copies ran while one was open for 6% -> 5% of each run, Pallas kernels for 4% -> 12%
where the time goes in v6:
time: 186 us; the launch traced here: 185 us
  waiting for transfers between devices  67.4 us (36%)
  Pallas kernels  53.2 us (29%)
  starting transfers between devices  34.1 us (18%)
  blocking collectives  15.8 us (8%)
  local copies, waits for them, and re-layouts  6.27 us (3%)
  other arithmetic  5.16 us (3%)
  matrix products  1.99 us (1%)
    ppermute x10, waiting for transfers between devices, swap(): return lax.ppermute(values, axis, [(i, i ^ step) for i in range(devices)])  66.9 us
    pallas_call x2, Pallas kernels, hand_on(): call(forward_kernel, float_of(half * capacity, tile, columns // 2), [smem...  35.5 us
    ppermute x10, starting transfers between devices, swap(): return lax.ppermute(values, axis, [(i, i ^ step) for i in range(devices)])  18.8 us
    all_to_all x1, blocking collectives, exchange(): lax.all_to_all(blocks, 'samples', split_axis=0, concat_axis=0, axis_index...  15.8 us
    all_to_all x3, starting transfers between devices, exchange(): lax.all_to_all(blocks, 'samples', split_axis=0, concat_axis=0, axis_index...  11.8 us
    pallas_call x1, Pallas kernels, per_device(): call(functools.partial(apply_kernel, devices, capacity), [full, float_of(...  5.35 us
    unnamed x31, local copies, waits for them, and re-layouts  5.31 us
    pallas_call x1, Pallas kernels, per_device(): call(functools.partial(curvature_kernel, devices, capacity), float_of(2 *...  5.23 us
  transfers between devices with their start and end apart: 14, of which 8 were waited for; matrix products, arithmetic and copies ran while one was open for 5% of the time, Pallas kernels for 12%

profile of v6, /device:TPU:0, one launch (start us, length us, event | category | flops | bytes accessed | tf_op | source)
XLA Modules:
  0.0 184.8 jit_solution(5453117234414566119)
XLA Ops:
  0.6 4.3 %shard_map.68 = (f32[512,256]{1,0:T(8,128)}, f32[4,128,128]{2,1,0:T(8,128)}, f32[4,128,128]{2,1,0:T(8,128)}, f32[512,1]{1,0:T(8,128)}, s32[4,12]{1,0:T(4,128)}, /*index=5*/s32[2,4]{1,0:T(2,128)}, f32[8,128,256]{2,1,0:T(8,128)}) custom-call(s32[3,32]{1,0:T(4,128)} %bitcast.53, f32[4,4,128,128]{3,2,1,0:T(8,128)} %kinship_hbm.5, f32[4,128]{1,0:T(4,128)} %bitcast.54, ...), custom_call_target="tpu_custom_call" | custom-call | tf_op jit(solution)/shard_map/pallas_call | solution.py:379
  5.0 4.1 %collective-permute-start.1 = (f32[4,128,128]{2,1,0:T(8,128)}, f32[4,128,128]{2,1,0:T(8,128)S(1)}, u32[]{:S(2)}, u32[]{:S(2)}) collective-permute-start(f32[4,128,128]{2,1,0:T(8,128)} %get-tuple-element.31), channel_id=1, source_target_pairs={{0,8},{2,10},{4,12},{6,14},{8,0},{10,2},{12,4},{14,6},{1,9},{3,11}... | collective-permute-start | bytes 786440 | tf_op jit(solution)/shard_map/ppermute | solution.py:343
  9.1 12.1 %collective-permute-done.1.partner_hbm.partner_right_hbm = f32[4,128,128]{2,1,0:T(8,128)S(1)} collective-permute-done((f32[4,128,128]{2,1,0:T(8,128)}, f32[4,128,128]{2,1,0:T(8,128)S(1)}, u32[]{:S(2)}, u32[]{:S(2)}) %collective-permute-start.1) | collective-permute-done | bytes 262176 | tf_op jit(solution)/shard_map/ppermute | solution.py:343
  21.9 17.7 %shard_map.70 = f32[8,128,128]{2,1,0:T(8,128)} custom-call(s32[2,4]{1,0:T(2,128)} %get-tuple-element.29.forward_ref, f32[4,128,128]{2,1,0:T(8,128)} %copy-done.7), custom_call_target="tpu_custom_call" | custom-call | tf_op jit(solution)/shard_map/pallas_call | solution.py:405
  39.7 3.5 %all-to-all-start.2 = ((f32[8,128,128]{2,1,0:T(8,128)}), f32[8,128,128]{2,1,0:T(8,128)S(1)}, u32[]{:S(2)}, u32[]{:S(2)}) async-start(f32[8,128,128]{2,1,0:T(8,128)} %shard_map.70), calls=%async_computation.2 | async-start | bytes 1048576 | tf_op jit(solution)/shard_map/all_to_all | solution.py:398
  43.1 2.9 %collective-permute-start = (f32[4,128,128]{2,1,0:T(8,128)}, f32[4,128,128]{2,1,0:T(8,128)S(1)}, u32[]{:S(2)}, u32[]{:S(2)}) collective-permute-start(f32[4,128,128]{2,1,0:T(8,128)} %get-tuple-element.30), channel_id=1, source_target_pairs={{0,8},{2,10},{4,12},{6,14},{8,0},{10,2},{12,4},{14,6},{1,9},{3,11}... | collective-permute-start | bytes 786440 | tf_op jit(solution)/shard_map/ppermute | solution.py:343
  46.4 8.0 %collective-permute-done.partner_hbm.partner_left_hbm = f32[4,128,128]{2,1,0:T(8,128)S(1)} collective-permute-done((f32[4,128,128]{2,1,0:T(8,128)}, f32[4,128,128]{2,1,0:T(8,128)S(1)}, u32[]{:S(2)}, u32[]{:S(2)}) %collective-permute-start) | collective-permute-done | bytes 262176 | tf_op jit(solution)/shard_map/ppermute | solution.py:343
  55.1 17.7 %shard_map.69 = f32[8,128,128]{2,1,0:T(8,128)} custom-call(s32[2,4]{1,0:T(2,128)} %get-tuple-element.29.forward_ref, f32[4,128,128]{2,1,0:T(8,128)} %copy-done.8), custom_call_target="tpu_custom_call" | custom-call | tf_op jit(solution)/shard_map/pallas_call | solution.py:405
  72.9 15.8 %all_to_all.25.far_left_hbm = f32[8,128,128]{2,1,0:T(8,128)} all-to-all(f32[8,128,128]{2,1,0:T(8,128)} %shard_map.69), channel_id=1, replica_groups={{0,2,4,6},{8,10,12,14},{1,3,5,7},{9,11,13,15},{16,18,20,22},{24,26,28,3..., dimensions={0} | all-to-all | bytes 1048576 | tf_op jit(solution)/shard_map/all_to_all | solution.py:398
  88.6 3.5 %all-to-all-start = ((f32[8,128,256]{2,1,0:T(8,128)}), f32[8,128,256]{2,1,0:T(8,128)S(1)}, u32[]{:S(2)}, u32[]{:S(2)}) async-start(f32[8,128,256]{2,1,0:T(8,128)} %get-tuple-element.28), calls=%async_computation | async-start | bytes 2097152 | tf_op jit(solution)/shard_map/all_to_all | solution.py:398
  96.9 1.9 %collective-permute-start.3 = (f32[4,128,256]{2,1,0:T(8,128)}, f32[4,128,256]{2,1,0:T(8,128)}, u32[]{:S(2)}, u32[]{:S(2)}) collective-permute-start(f32[4,128,256]{2,1,0:T(8,128)} %dynamic-slice_bitcast_fusion.1), channel_id=1, source_target_pairs={{0,2},{2,0},{4,6},{6,4},{8,10},{10,8},{12,14},{14,12},{1,3},{3,1},... | collective-permute-start | bytes 1572872 | tf_op jit(solution)/shard_map/ppermute | solution.py:343
  98.8 16.3 %collective-permute-done.3 = f32[4,128,256]{2,1,0:T(8,128)} collective-permute-done((f32[4,128,256]{2,1,0:T(8,128)}, f32[4,128,256]{2,1,0:T(8,128)}, u32[]{:S(2)}, u32[]{:S(2)}) %collective-permute-start.3) | collective-permute-done | bytes 524320 | tf_op jit(solution)/shard_map/ppermute | solution.py:343
  115.1 2.1 %bitcast_add_fusion.1 = f32[4,128,256]{2,1,0:T(8,128)} fusion(f32[4,128,256]{2,1,0:T(8,128)} %collective-permute-done.3, f32[4,2,128,256]{3,2,1,0:T(8,128)} %copy-done.5, s32[]{:T(128)S(6)} %select_n.60), kind=kLoop, calls=%fused_computation.6 | loop fusion | flops 131072 | bytes 1572868 | tf_op jit(solution)/shard_map/add | solution.py:356
  118.2 5.4 %shard_map.71 = (f32[512,256]{1,0:T(8,128)}, f32[8,136,256]{2,1,0:T(8,128)}) custom-call(s32[4,12]{1,0:T(4,128)} %get-tuple-element.26.table_ref, f32[4,4,128,128]{3,2,1,0:T(8,128)} %kinship_hbm.5, f32[512,256]{1,0:T(8,128)} %get-tuple-element.25.direction_hbm, f32[512,1]{1,0:T(8,128)} %get-tuple-element.27.diagonal_ref, f32[512,256]{1,0:T(8,128)} %phenotypes_hbm.3, ...), custom_call_target="tpu_custom_call" | custom-call | tf_op jit(solution)/shard_map/pallas_call | solution.py:430
  123.5 4.8 %all-to-all-start.3 = ((f32[8,136,256]{2,1,0:T(8,128)}), f32[8,136,256]{2,1,0:T(8,128)}, u32[]{:S(2)}, u32[]{:S(2)}) async-start(f32[8,136,256]{2,1,0:T(8,128)} %get-tuple-element.40), calls=%async_computation.3 | async-start | bytes 2228224 | tf_op jit(solution)/shard_map/all_to_all | solution.py:398
  130.4 2.1 %collective-permute-start.4 = (f32[4,128,256]{2,1,0:T(8,128)S(1)}, f32[4,128,256]{2,1,0:T(8,128)S(1)}, u32[]{:S(2)}, u32[]{:S(2)}) collective-permute-start(f32[4,128,256]{2,1,0:T(8,128)S(1)} %dynamic-slice_bitcast_fusion), channel_id=1, source_target_pairs={{0,2},{2,0},{4,6},{6,4},{8,10},{10,8},{12,14},{14,12},{1,3},{3,1},... | collective-permute-start | bytes 1572872 | tf_op jit(solution)/shard_map/ppermute | solution.py:343
  134.0 17.6 %collective-permute-done.5 = f32[2,128,256]{2,1,0:T(8,128)S(1)} collective-permute-done((f32[2,128,256]{2,1,0:T(8,128)S(1)}, f32[2,128,256]{2,1,0:T(8,128)S(1)}, u32[]{:S(2)}, u32[]{:S(2)}) %collective-permute-start.5) | collective-permute-done | bytes 262176 | tf_op jit(solution)/shard_map/ppermute | solution.py:343
  151.6 2.1 %collective-permute-done.4 = f32[4,128,256]{2,1,0:T(8,128)S(1)} collective-permute-done((f32[4,128,256]{2,1,0:T(8,128)S(1)}, f32[4,128,256]{2,1,0:T(8,128)S(1)}, u32[]{:S(2)}, u32[]{:S(2)}) %collective-permute-start.4) | collective-permute-done | bytes 524320 | tf_op jit(solution)/shard_map/ppermute | solution.py:343
  156.5 2.2 %collective-permute-start.6 = (f32[1,128,256]{2,1,0:T(8,128)S(1)}, f32[1,128,256]{2,1,0:T(8,128)S(1)}, u32[]{:S(2)}, u32[]{:S(2)}) collective-permute-start(f32[1,128,256]{2,1,0:T(8,128)S(1)} %get-tuple-element.50), channel_id=1, source_target_pairs={{0,8},{2,10},{4,12},{6,14},{8,0},{10,2},{12,4},{14,6},{1,9},{3,11}... | collective-permute-start | bytes 393224 | tf_op jit(solution)/shard_map/ppermute | solution.py:343
  158.7 5.2 %shard_map.72 = f32[16,8,256]{2,1,0:T(8,128)} custom-call(s32[4,12]{1,0:T(4,128)} %get-tuple-element.26.table_ref, f32[4,4,128,128]{3,2,1,0:T(8,128)} %kinship_hbm.5, f32[512,256]{1,0:T(8,128)} %get-tuple-element.25.direction_hbm, f32[512,1]{1,0:T(8,128)} %get-tuple-element.27.diagonal_ref, f32[512,256]{1,0:T(8,128)} %get-tuple-element.39.scaled_hbm, ...), custom_call_target="tpu_custom_call" | custom-call | tf_op jit(solution)/shard_map/pallas_call | solution.py:449
  164.0 3.5 %all-to-all-start.4 = ((f32[16,8,256]{2,1,0:T(8,128)}), f32[16,8,256]{2,1,0:T(8,128)S(1)}, u32[]{:S(2)}, u32[]{:S(2)}) async-start(f32[16,8,256]{2,1,0:T(8,128)} %shard_map.72), calls=%async_computation.4 | async-start | bytes 262144 | tf_op jit(solution)/shard_map/all_to_all | solution.py:462
  167.6 2.8 %collective-permute-start.8 = (f32[1,128,256]{2,1,0:T(8,128)S(1)}, f32[1,128,256]{2,1,0:T(8,128)S(1)}, u32[]{:S(2)}, u32[]{:S(2)}) collective-permute-start(f32[1,128,256]{2,1,0:T(8,128)S(1)} %constant_dynamic-slice_fusion), channel_id=1, source_target_pairs={{0,8},{2,10},{4,12},{6,14},{8,0},{10,2},{12,4},{14,6},{1,9},{3,11}... | collective-permute-start | bytes 393224 | tf_op jit(solution)/shard_map/ppermute | solution.py:343
  170.4 9.4 %collective-permute-done.8 = f32[1,128,256]{2,1,0:T(8,128)S(1)} collective-permute-done((f32[1,128,256]{2,1,0:T(8,128)S(1)}, f32[1,128,256]{2,1,0:T(8,128)S(1)}, u32[]{:S(2)}, u32[]{:S(2)}) %collective-permute-start.8) | collective-permute-done | bytes 131104 | tf_op jit(solution)/shard_map/ppermute | solution.py:343
  182.0 2.8 %shard_map.73 = (f32[512,256]{1,0:T(8,128)}, f32[64,512]{1,0:T(8,128)}) custom-call(f32[512,256]{1,0:T(8,128)} %get-tuple-element.25.direction_hbm, f32[512,256]{1,0:T(8,128)} %get-tuple-element.39.scaled_hbm, f32[128,256]{1,0:T(8,128)} %bitcast.51, f32[128,256]{1,0:T(8,128)} %bitcast.52, f32[128,256]{1,0:T(8,128)} %copy-done.14, f32[16,8,256]{2,1,0:T(8,128)} %copy-done.13), custom_call_target="tpu_custom_call" | custom-call | tf_op jit(solution)/shard_map/pallas_call | solution.py:466
  (60 shorter events, 15.9 us)
Async XLA Ops:
  0.6 45.4 %copy-start.10 = (f32[512,512]{1,0:T(8,128)S(1)}, f32[512,512]{1,0:T(8,128)}, u32[]{:S(2)}) copy-start(f32[512,512]{1,0:T(8,128)} %param.9) | copy-start | bytes 3145732
  5.0 16.2 %collective-permute-start.1 = (f32[4,128,128]{2,1,0:T(8,128)}, f32[4,128,128]{2,1,0:T(8,128)S(1)}, u32[]{:S(2)}, u32[]{:S(2)}) collective-permute-start(f32[4,128,128]{2,1,0:T(8,128)} %get-tuple-element.31), channel_id=1, source_target_pairs={{0,8},{2,10},{4,12},{6,14},{8,0},{10,2},{12,4},{14,6},{1,9},{3,11}... | collective-permute-start | bytes 786440 | tf_op jit(solution)/shard_map/ppermute | solution.py:343
  39.7 33.2 %all-to-all-start.2 = ((f32[8,128,128]{2,1,0:T(8,128)}), f32[8,128,128]{2,1,0:T(8,128)S(1)}, u32[]{:S(2)}, u32[]{:S(2)}) async-start(f32[8,128,128]{2,1,0:T(8,128)} %shard_map.70), calls=%async_computation.2 | async-start | bytes 1048576 | tf_op jit(solution)/shard_map/all_to_all | solution.py:398
  43.1 11.3 %collective-permute-start = (f32[4,128,128]{2,1,0:T(8,128)}, f32[4,128,128]{2,1,0:T(8,128)S(1)}, u32[]{:S(2)}, u32[]{:S(2)}) collective-permute-start(f32[4,128,128]{2,1,0:T(8,128)} %get-tuple-element.30), channel_id=1, source_target_pairs={{0,8},{2,10},{4,12},{6,14},{8,0},{10,2},{12,4},{14,6},{1,9},{3,11}... | collective-permute-start | bytes 786440 | tf_op jit(solution)/shard_map/ppermute | solution.py:343
  46.3 45.8 %copy-start.6 = (f32[512,512]{0,1:T(8,128)}, f32[512,512]{0,1:T(8,128)S(1)}, u32[]{:S(2)}) copy-start(f32[512,512]{0,1:T(8,128)S(1)} %copy.8) | copy-start | bytes 3145732
  46.3 45.8 %collective-permute-start.2 = (f32[512,512]{0,1:T(8,128)S(1)}, f32[512,512]{0,1:T(8,128)}, u32[]{:S(2)}, u32[]{:S(2)}) collective-permute-start(f32[512,512]{0,1:T(8,128)S(1)} %copy.8), channel_id=1, source_target_pairs={{0,1},{1,0},{2,3},{3,2},{4,5},{5,4},{6,7},{7,6},{8,9},{9,8},{10,11... | collective-permute-start | bytes 3145736 | tf_op jit(solution)/shard_map/ppermute | solution.py:343
  72.8 19.3 %copy-start.3 = (f32[8,128,128]{2,1,0:T(8,128)}, f32[8,128,128]{2,1,0:T(8,128)S(1)}, u32[]{:S(2)}) copy-start(f32[8,128,128]{2,1,0:T(8,128)S(1)} %all-to-all-done.2.far_right_hbm) | copy-start | bytes 1572868
  88.6 28.6 %all-to-all-start = ((f32[8,128,256]{2,1,0:T(8,128)}), f32[8,128,256]{2,1,0:T(8,128)S(1)}, u32[]{:S(2)}, u32[]{:S(2)}) async-start(f32[8,128,256]{2,1,0:T(8,128)} %get-tuple-element.28), calls=%async_computation | async-start | bytes 2097152 | tf_op jit(solution)/shard_map/all_to_all | solution.py:398
  92.2 1.9 %copy-start.1 = (f32[512,256]{1,0:T(8,128)S(1)}, f32[512,256]{1,0:T(8,128)}, u32[]{:S(2)}) copy-start(f32[512,256]{1,0:T(8,128)} %get-tuple-element.25.direction_hbm) | copy-start | bytes 1572868
  96.9 18.2 %collective-permute-start.3 = (f32[4,128,256]{2,1,0:T(8,128)}, f32[4,128,256]{2,1,0:T(8,128)}, u32[]{:S(2)}, u32[]{:S(2)}) collective-permute-start(f32[4,128,256]{2,1,0:T(8,128)} %dynamic-slice_bitcast_fusion.1), channel_id=1, source_target_pairs={{0,2},{2,0},{4,6},{6,4},{8,10},{10,8},{12,14},{14,12},{1,3},{3,1},... | collective-permute-start | bytes 1572872 | tf_op jit(solution)/shard_map/ppermute | solution.py:343
  117.2 1.0 copy-start
  123.5 4.8 %copy-start.2 = (f32[512,256]{1,0:T(8,128)S(1)}, f32[512,256]{1,0:T(8,128)}, u32[]{:S(2)}) copy-start(f32[512,256]{1,0:T(8,128)} %get-tuple-element.39.scaled_hbm) | copy-start | bytes 1572868
  123.5 31.8 %all-to-all-start.3 = ((f32[8,136,256]{2,1,0:T(8,128)}), f32[8,136,256]{2,1,0:T(8,128)}, u32[]{:S(2)}, u32[]{:S(2)}) async-start(f32[8,136,256]{2,1,0:T(8,128)} %get-tuple-element.40), calls=%async_computation.3 | async-start | bytes 2228224 | tf_op jit(solution)/shard_map/all_to_all | solution.py:398
  128.3 4.1 %copy-start.9 = (f32[4,128,256]{2,1,0:T(8,128)S(1)}, f32[4,128,256]{2,1,0:T(8,128)}, u32[]{:S(2)}) copy-start(f32[4,128,256]{2,1,0:T(8,128)} %bitcast_add_fusion.1) | copy-start | bytes 1572868
  130.4 23.4 %collective-permute-start.4 = (f32[4,128,256]{2,1,0:T(8,128)S(1)}, f32[4,128,256]{2,1,0:T(8,128)S(1)}, u32[]{:S(2)}, u32[]{:S(2)}) collective-permute-start(f32[4,128,256]{2,1,0:T(8,128)S(1)} %dynamic-slice_bitcast_fusion), channel_id=1, source_target_pairs={{0,2},{2,0},{4,6},{6,4},{8,10},{10,8},{12,14},{14,12},{1,3},{3,1},... | collective-permute-start | bytes 1572872 | tf_op jit(solution)/shard_map/ppermute | solution.py:343
  132.5 19.1 %collective-permute-start.5 = (f32[2,128,256]{2,1,0:T(8,128)S(1)}, f32[2,128,256]{2,1,0:T(8,128)S(1)}, u32[]{:S(2)}, u32[]{:S(2)}) collective-permute-start(f32[2,128,256]{2,1,0:T(8,128)S(1)} %dynamic-slice_bitcast_fusion.4), channel_id=1, source_target_pairs={{0,4},{2,6},{4,0},{6,2},{8,12},{10,14},{12,8},{14,10},{1,5},{3,7},... | collective-permute-start | bytes 786440 | tf_op jit(solution)/shard_map/ppermute | solution.py:343
  155.4 12.1 %collective-permute-start.7 = (f32[2,128,256]{2,1,0:T(8,128)S(1)}, f32[2,128,256]{2,1,0:T(8,128)S(1)}, u32[]{:S(2)}, u32[]{:S(2)}) collective-permute-start(f32[2,128,256]{2,1,0:T(8,128)S(1)} %get-tuple-element.48), channel_id=1, source_target_pairs={{0,4},{2,6},{4,0},{6,2},{8,12},{10,14},{12,8},{14,10},{1,5},{3,7},... | collective-permute-start | bytes 786440 | tf_op jit(solution)/shard_map/ppermute | solution.py:343
  156.5 11.0 %collective-permute-start.6 = (f32[1,128,256]{2,1,0:T(8,128)S(1)}, f32[1,128,256]{2,1,0:T(8,128)S(1)}, u32[]{:S(2)}, u32[]{:S(2)}) collective-permute-start(f32[1,128,256]{2,1,0:T(8,128)S(1)} %get-tuple-element.50), channel_id=1, source_target_pairs={{0,8},{2,10},{4,12},{6,14},{8,0},{10,2},{12,4},{14,6},{1,9},{3,11}... | collective-permute-start | bytes 393224 | tf_op jit(solution)/shard_map/ppermute | solution.py:343
  164.0 16.1 %all-to-all-start.4 = ((f32[16,8,256]{2,1,0:T(8,128)}), f32[16,8,256]{2,1,0:T(8,128)S(1)}, u32[]{:S(2)}, u32[]{:S(2)}) async-start(f32[16,8,256]{2,1,0:T(8,128)} %shard_map.72), calls=%async_computation.4 | async-start | bytes 262144 | tf_op jit(solution)/shard_map/all_to_all | solution.py:462
  167.5 13.8 %copy-start.11 = (f32[1,128,256]{2,1,0:T(8,128)}, f32[1,128,256]{2,1,0:T(8,128)S(1)}, u32[]{:S(2)}) copy-start(f32[1,128,256]{2,1,0:T(8,128)S(1)} %add.76) | copy-start | bytes 393220
  167.6 12.3 %collective-permute-start.8 = (f32[1,128,256]{2,1,0:T(8,128)S(1)}, f32[1,128,256]{2,1,0:T(8,128)S(1)}, u32[]{:S(2)}, u32[]{:S(2)}) collective-permute-start(f32[1,128,256]{2,1,0:T(8,128)S(1)} %constant_dynamic-slice_fusion), channel_id=1, source_target_pairs={{0,8},{2,10},{4,12},{6,14},{8,0},{10,2},{12,4},{14,6},{1,9},{3,11}... | collective-permute-start | bytes 393224 | tf_op jit(solution)/shard_map/ppermute | solution.py:343
  179.9 1.5 copy-start.12
  179.9 1.4 collective-permute-start.9
  180.0 1.3 copy-start.13
  (5 other events, 4.0 us)

commit v7 on v6

--- a/solution.py
+++ b/solution.py
@@ -75,11 +75,10 @@
     return lax.div(value, jnp.int32(divisor))
 
 
-def prepare_kernel(devices, capacity, list_ref, kinship_hbm, variance_hbm, phenotypes_hbm, direction_hbm, left_hbm,
-                   right_hbm, diagonal_ref, table_ref, forward_ref, outgoing_hbm, kinship_ref, variance_ref,
-                   phenotypes_ref, direction_ref, first_ref, last_ref, semaphores):
+def prepare_kernel(devices, capacity, list_ref, kinship_hbm, variance_hbm, phenotypes_hbm, direction_hbm, diagonal_ref,
+                   table_ref, forward_ref, outgoing_hbm, kinship_ref, variance_ref, phenotypes_ref, direction_ref,
+                   first_ref, last_ref, semaphores):
     block_count, positions, tile = kinship_ref.shape[:3]
-    columns = direction_ref.shape[1]
     half = devices // 2
     copies = Copies(semaphores)
     loads = [copies.start(variance_hbm, variance_ref)]
@@ -150,8 +149,6 @@
         diagonal = jnp.sum(total, axis=1, keepdims=True)
         diagonal_ref[block, :] = diagonal
         direction_ref[block, :] = phenotypes_ref[block, :] * (1.0 / diagonal)
-        stores.append(copies.start(direction_ref.at[block, pl.ds(0, columns // 2)], left_hbm.at[row]))
-        stores.append(copies.start(direction_ref.at[block, pl.ds(columns // 2, columns // 2)], right_hbm.at[row]))
         stores.append(copies.start(direction_ref.at[block], direction_hbm.at[block]))
     for i in range(half):
         for slot in range(capacity):
@@ -160,44 +157,38 @@
     wait_all(stores)
 
 
-def forward_kernel(forward_ref, partner_hbm, outgoing_hbm, semaphores):
+def forward_kernel(forward_ref, partner_hbm, outgoing_hbm, partner_ref, semaphores):
     capacity, half = forward_ref.shape
+    tile = outgoing_hbm.shape[1]
     copies = Copies(semaphores)
+    copies.start(partner_hbm, partner_ref).wait()
     stores = []
     for i in range(half):
         for slot in range(capacity):
-            stores.append(copies.start(partner_hbm.at[forward_ref[slot, i]], outgoing_hbm.at[i * capacity + slot]))
+            start = pl.multiple_of(forward_ref[slot, i] * tile, tile)
+            stores.append(copies.start(partner_ref.at[pl.ds(start, tile)], outgoing_hbm.at[i * capacity + slot]))
     wait_all(stores)
 
 
 def load_received(copies, devices, capacity, near_hbm, far_hbm, partner_hbm, received_ref):
     half = devices // 2
     base = lax.axis_index("samples") & half
-    width = received_ref.shape[2] // 2
     count = half * capacity
-    loads = [copies.start(near_hbm, received_ref.at[pl.ds(base * capacity, count)])]
-    for side in range(2):
-        lanes = pl.ds(side * width, width)
-        loads.append(copies.start(
-            far_hbm[side], received_ref.at[pl.ds((half - base) * capacity, count), :, lanes]
-        ))
-        loads.append(copies.start(
-            partner_hbm[side], received_ref.at[pl.ds(devices * capacity, partner_hbm[side].shape[0]), :, lanes]
-        ))
-    return loads
+    return [
+        copies.start(near_hbm, received_ref.at[pl.ds(base * capacity, count)]),
+        copies.start(far_hbm, received_ref.at[pl.ds((half - base) * capacity, count)]),
+        copies.start(partner_hbm, received_ref.at[pl.ds(devices * capacity, partner_hbm.shape[0])]),
+    ]
 
 
 def apply_kernel(devices, capacity, table_ref, kinship_hbm, direction_hbm, diagonal_ref, phenotypes_hbm, near_hbm,
-                 far_left_hbm, far_right_hbm, partner_left_hbm, partner_right_hbm, scaled_hbm, outgoing_hbm, sums_ref, kinship_ref, direction_ref, phenotypes_ref, received_ref,
+                 far_hbm, partner_hbm, scaled_hbm, outgoing_hbm, sums_ref, kinship_ref, direction_ref, phenotypes_ref, received_ref,
                  scaled_ref, high_ref, low_ref, semaphores):
     block_count, positions, tile = kinship_ref.shape[:3]
     columns = direction_ref.shape[1]
     copies = Copies(semaphores)
     tiles = copies.start(kinship_hbm, kinship_ref)
-    arrivals = load_received(
-        copies, devices, capacity, near_hbm, (far_left_hbm, far_right_hbm), (partner_left_hbm, partner_right_hbm),
-        received_ref,
-    )
+    arrivals = load_received(copies, devices, capacity, near_hbm, far_hbm, partner_hbm, received_ref)
     loads = [copies.start(direction_hbm, direction_ref), copies.start(phenotypes_hbm, phenotypes_ref)]
     norm = jnp.zeros((SUBLANES, columns), jnp.float32)
     cross = jnp.zeros((SUBLANES, columns), jnp.float32)
@@ -229,7 +220,7 @@
 
 
 def curvature_kernel(devices, capacity, table_ref, kinship_hbm, direction_hbm, diagonal_ref, scaled_hbm, near_hbm,
-                     far_left_hbm, far_right_hbm, partner_left_hbm, partner_right_hbm, later_hbm, sums_hbm, kinship_ref, direction_ref, scaled_ref, received_ref, later_ref, high_ref,
+                     far_hbm, partner_hbm, later_hbm, sums_hbm, kinship_ref, direction_ref, scaled_ref, received_ref, later_ref, high_ref,
                      low_ref, sums_ref, semaphores):
     block_count, positions, tile = kinship_ref.shape[:3]
     columns = direction_ref.shape[1]
@@ -240,10 +231,7 @@
         copies.start(direction_hbm, direction_ref),
         copies.start(scaled_hbm, scaled_ref),
     ]
-    loads += load_received(
-        copies, devices, capacity, near_hbm, (far_left_hbm, far_right_hbm), (partner_left_hbm, partner_right_hbm),
-        received_ref,
-    )
+    loads += load_received(copies, devices, capacity, near_hbm, far_hbm, partner_hbm, received_ref)
     tiles.wait()
     split_tiles(kinship_ref, high_ref, low_ref)
     wait_all(loads)
@@ -375,22 +363,21 @@
     full_room = room(people, columns)
     tiles_room = pltpu.VMEM((block_count, tile, positions * tile), jnp.bfloat16)
     half = devices // 2
-    side = float_of(block_count, tile, columns // 2)
-    direction, left, right, diagonal, table, forward, outgoing = call(
+    direction, diagonal, table, forward, outgoing = call(
         functools.partial(prepare_kernel, devices, capacity),
         [
-            full, side, side,
+            full,
             float_of(people, 1),
             jax.ShapeDtypeStruct((4, max(entries, devices)), jnp.int32),
             jax.ShapeDtypeStruct((capacity, half), jnp.int32),
             float_of(half * capacity, tile, columns),
         ],
         [smem, hbm, hbm, hbm],
-        [hbm, hbm, hbm, vmem, smem, smem, hbm],
+        [hbm, vmem, smem, smem, hbm],
         [
             room(*kinship.shape), room(block_count, tile), full_room, full_room,
             pltpu.SMEM((devices,), jnp.int32), pltpu.SMEM((devices,), jnp.int32),
-            pltpu.SemaphoreType.DMA((5 * block_count + capacity * half + 1,)),
+            pltpu.SemaphoreType.DMA((3 * block_count + capacity * half + 1,)),
         ],
     )(relatives.T, kinship, variance.reshape(block_count, tile), phenotypes)
 
@@ -400,15 +387,6 @@
         )
 
     halves = [list(range(half)), list(range(half, devices))]
-
-    def hand_on(partner_blocks):
-        return exchange(call(
-            forward_kernel,
-            float_of(half * capacity, tile, columns // 2),
-            [smem, hbm],
-            hbm,
-            [pltpu.SemaphoreType.DMA((half * capacity,))],
-        )(forward, partner_blocks), halves)
 
     both_dosages = jnp.concatenate(
         [values.reshape(people, devices, share_rows) for values in (dosage, swap(dosage, "cols", 2, 1))], axis=2
@@ -422,15 +400,23 @@
         return partial.reshape(devices, 2 * share_rows, columns)
 
     steps = [2 ** i for i in range(devices.bit_length() - 1)]
-    partners = [swap(blocks, "samples", devices, half) for blocks in (left, right)]
+    partner = swap(direction, "samples", devices, half)
     near = exchange(outgoing, halves)
-    received = [near] + [hand_on(blocks) for blocks in partners] + partners
+    partner, near = lax.optimization_barrier((partner, near))
+    far = exchange(call(
+        forward_kernel,
+        float_of(half * capacity, tile, columns),
+        [smem, hbm],
+        hbm,
+        [full_room, pltpu.SemaphoreType.DMA((half * capacity + 1,))],
+    )(forward, partner), halves)
+    received = [near, far, partner.reshape(block_count, tile, columns)]
     direction_scores = halve_all(variant_products(direction), devices, steps[:1])
     received, direction_scores = lax.optimization_barrier((received, direction_scores))
     scaled, outgoing = call(
         functools.partial(apply_kernel, devices, capacity),
         [full, float_of(devices, tile + SUBLANES, columns)],
-        [smem, hbm, hbm, vmem] + [hbm] * 6,
+        [smem, hbm, hbm, vmem] + [hbm] * 4,
         [hbm, hbm],
         [
             room(SUBLANES, columns),
@@ -449,7 +435,7 @@
     sums = call(
         functools.partial(curvature_kernel, devices, capacity),
         float_of(2 * devices, SUBLANES, columns),
-        [smem, hbm, hbm, vmem] + [hbm] * 7,
+        [smem, hbm, hbm, vmem] + [hbm] * 5,
         hbm,
         [
             room(*kinship.shape), full_room, full_room, room(devices * capacity + block_count, tile, columns),
@@ -459,9 +445,11 @@
         ],
     )(table, kinship, direction, diagonal, scaled, *received, later)
     sums, direction_kept, scaled_kept = lax.optimization_barrier((sums, direction_kept, scaled_kept))
+    direction_scores = halve_all(direction_kept + direction_given, devices, steps[3:])[0]
+    scaled_kept, scaled_given = halve(scaled_kept + scaled_given, devices, steps[2])
+    sums, scaled_kept, direction_scores = lax.optimization_barrier((sums, scaled_kept, direction_scores))
     all_sums = lax.all_to_all(sums, ("samples", "cols"), split_axis=0, concat_axis=0, tiled=True)
-    direction_scores = halve_all(direction_kept + direction_given, devices, steps[3:])[0]
-    scaled_scores = halve_all(scaled_kept + scaled_given, devices, steps[2:])[0]
+    scaled_scores = halve_all(scaled_kept + scaled_given, devices, steps[3:])[0]
     swapped = swap(jnp.concatenate([direction_scores[share_rows:], scaled_scores[share_rows:]]), "cols", 2, 1)
     solved, scores = call(
         functools.partial(finish_kernel, devices, 1.0 / math.sqrt(people * devices)),

time: 186 us -> 138 us (0.74)
  Pallas kernels: 53.2 us -> 20.3 us
  blocking collectives: 15.8 us -> 0 us
  waiting for transfers between devices: 67.4 us -> 73.1 us
  starting transfers between devices: 34.1 us -> 31.3 us
    pallas_call x3 -> x2, Pallas kernels: 39.8 us -> 6.87 us  [the longest x1 4.09 us: per_device(): call(functools.partial(prepare_kernel, devices, capacity), [full, float_o...]
    all_to_all x1 -> x0, blocking collectives: 15.8 us -> none  [exchange(): lax.all_to_all(blocks, 'samples', split_axis=0, concat_axis=0, axis_index...]
    all_to_all x1, waiting for transfers between devices: 0.01 us -> 5.64 us  [per_device(): lax.all_to_all(sums, ('samples', 'cols'), split_axis=0, concat_axis=0, ti...]
    ppermute x10 -> x9, starting transfers between devices: 18.8 us -> 13.1 us  [swap(): return lax.ppermute(values, axis, [(i, i ^ step) for i in range(devices)])]
    all_to_all x3, starting transfers between devices: 11.8 us -> 14 us  [exchange(): lax.all_to_all(blocks, 'samples', split_axis=0, concat_axis=0, axis_index...]
    unnamed x31 -> x25, local copies, waits for them, and re-layouts: 5.31 us -> 4.06 us
    ppermute x10 -> x9, waiting for transfers between devices: 66.9 us -> 66.8 us  [swap(): return lax.ppermute(values, axis, [(i, i ^ step) for i in range(devices)])]
  transfers between devices with their start and end apart: 14 -> 13, of which waited for: 8 -> 8; matrix products, arithmetic and copies ran while one was open for 5% -> 7% of each run, Pallas kernels for 12% -> 6%
where the time goes in v7:
time: 138 us
  waiting for transfers between devices  73.1 us (53%)
  starting transfers between devices  31.3 us (23%)
  Pallas kernels  20.3 us (15%)
  local copies, waits for them, and re-layouts  5.05 us (4%)
  other arithmetic  5.01 us (4%)
  matrix products  1.99 us (1%)
    ppermute x9, waiting for transfers between devices, swap(): return lax.ppermute(values, axis, [(i, i ^ step) for i in range(devices)])  66.8 us
    all_to_all x3, starting transfers between devices, exchange(): lax.all_to_all(blocks, 'samples', split_axis=0, concat_axis=0, axis_index...  14 us
    ppermute x9, starting transfers between devices, swap(): return lax.ppermute(values, axis, [(i, i ^ step) for i in range(devices)])  13.1 us
    all_to_all x1, waiting for transfers between devices, per_device(): lax.all_to_all(sums, ('samples', 'cols'), split_axis=0, concat_axis=0, ti...  5.64 us
    pallas_call x1, Pallas kernels, per_device(): call(functools.partial(apply_kernel, devices, capacity), [full, float_of(...  5.34 us
    pallas_call x1, Pallas kernels, per_device(): call(functools.partial(curvature_kernel, devices, capacity), float_of(2 *...  5.25 us
    all_to_all x1, starting transfers between devices, per_device(): lax.all_to_all(sums, ('samples', 'cols'), split_axis=0, concat_axis=0, ti...  4.11 us
    pallas_call x1, Pallas kernels, per_device(): call(functools.partial(prepare_kernel, devices, capacity), [full, float_o...  4.09 us
  transfers between devices with their start and end apart: 13, of which 8 were waited for; matrix products, arithmetic and copies ran while one was open for 7% of the time, Pallas kernels for 6%

profile of v7, /device:TPU:0, one launch (start us, length us, event | category | flops | bytes accessed | tf_op | source)
XLA Modules:
  0.0 137.7 jit_solution(3781385793997022178)
XLA Ops:
  0.6 4.1 %shard_map.68 = (f32[512,256]{1,0:T(8,128)}, f32[512,1]{1,0:T(8,128)}, s32[4,12]{1,0:T(4,128)}, s32[2,4]{1,0:T(2,128)}, f32[8,128,256]{2,1,0:T(8,128)}) custom-call(s32[3,32]{1,0:T(4,128)} %bitcast.54, f32[4,4,128,128]{3,2,1,0:T(8,128)} %kinship_hbm.5, f32[4,128]{1,0:T(4,128)} %bitcast.55, f32[512,256]{1,0:T(8,128)} %phenotypes_hbm.3), custom_call_target="tpu_custom_call" | custom-call | tf_op jit(solution)/shard_map/pallas_call | solution.py:366
  4.7 5.4 %all-to-all-start = ((f32[8,128,256]{2,1,0:T(8,128)}), f32[8,128,256]{2,1,0:T(8,128)S(1)}, u32[]{:S(2)}, u32[]{:S(2)}) async-start(f32[8,128,256]{2,1,0:T(8,128)} %get-tuple-element.29), calls=%async_computation | async-start | bytes 2097152 | tf_op jit(solution)/shard_map/all_to_all | solution.py:385
  10.1 1.6 %copy.8 = f32[512,512]{0,1:T(8,128)S(1)} copy(f32[512,512]{1,0:T(8,128)} %param.9) | data formatting | bytes 2097152 | tf_op args[4]
  11.8 2.7 %collective-permute-start = (f32[512,256]{1,0:T(8,128)S(1)}, f32[512,256]{1,0:T(8,128)S(1)}, u32[]{:S(2)}, u32[]{:S(2)}) collective-permute-start(f32[512,256]{1,0:T(8,128)S(1)} %copy-done.1), channel_id=1, source_target_pairs={{0,8},{2,10},{4,12},{6,14},{8,0},{10,2},{12,4},{14,6},{1,9},{3,11}... | collective-permute-start | bytes 1572872 | tf_op jit(solution)/shard_map/ppermute | solution.py:331
  14.4 23.9 %collective-permute-done.partner_hbm = f32[512,256]{1,0:T(8,128)S(1)} collective-permute-done((f32[512,256]{1,0:T(8,128)S(1)}, f32[512,256]{1,0:T(8,128)S(1)}, u32[]{:S(2)}, u32[]{:S(2)}) %collective-permute-start) | collective-permute-done | bytes 524320 | tf_op jit(solution)/shard_map/ppermute | solution.py:331
  39.1 2.8 %shard_map.69 = f32[8,128,256]{2,1,0:T(8,128)} custom-call(s32[2,4]{1,0:T(2,128)} %get-tuple-element.31.forward_ref, f32[512,256]{1,0:T(8,128)} %copy-done.4), custom_call_target="tpu_custom_call" | custom-call | tf_op jit(solution)/shard_map/pallas_call | solution.py:406
  41.9 4.3 %all-to-all-start.1 = ((f32[8,128,256]{2,1,0:T(8,128)}), f32[8,128,256]{2,1,0:T(8,128)}, u32[]{:S(2)}, u32[]{:S(2)}) async-start(f32[8,128,256]{2,1,0:T(8,128)} %shard_map.69), calls=%async_computation.1 | async-start | bytes 2097152 | tf_op jit(solution)/shard_map/all_to_all | solution.py:385
  46.2 1.9 %pad_maximum_fusion = f32[512,8,128]{0,2,1:T(8,128)S(1)} fusion(f32[512,8,64]{0,2,1:T(8,128)} %bitcast.4, f32[512,8,64]{0,2,1:T(8,128)} %bitcast.49), kind=kLoop, calls=%fused_computation | loop fusion | flops 524288 | bytes 4194304 | tf_op jit(solution)/shard_map/concatenate | solution.py:391
  49.9 2.0 %collective-permute-start.2 = (f32[4,128,256]{2,1,0:T(8,128)}, f32[4,128,256]{2,1,0:T(8,128)}, u32[]{:S(2)}, u32[]{:S(2)}) collective-permute-start(f32[4,128,256]{2,1,0:T(8,128)} %dynamic-slice_bitcast_fusion.1), channel_id=1, source_target_pairs={{0,2},{2,0},{4,6},{6,4},{8,10},{10,8},{12,14},{14,12},{1,3},{3,1},... | collective-permute-start | bytes 1572872 | tf_op jit(solution)/shard_map/ppermute | solution.py:331
  51.9 19.5 %collective-permute-done.2 = f32[4,128,256]{2,1,0:T(8,128)} collective-permute-done((f32[4,128,256]{2,1,0:T(8,128)}, f32[4,128,256]{2,1,0:T(8,128)}, u32[]{:S(2)}, u32[]{:S(2)}) %collective-permute-start.2) | collective-permute-done | bytes 524320 | tf_op jit(solution)/shard_map/ppermute | solution.py:331
  71.4 1.9 %bitcast_add_fusion.1 = f32[4,128,256]{2,1,0:T(8,128)} fusion(f32[4,128,256]{2,1,0:T(8,128)} %collective-permute-done.2, f32[4,2,128,256]{3,2,1,0:T(8,128)S(1)} %fusion.2, s32[]{:T(128)S(6)} %select_n.60), kind=kLoop, calls=%fused_computation.6 | loop fusion | flops 131072 | bytes 1572868 | tf_op jit(solution)/shard_map/add | solution.py:344
  73.3 5.3 %shard_map.70 = (f32[512,256]{1,0:T(8,128)}, f32[8,136,256]{2,1,0:T(8,128)}) custom-call(s32[4,12]{1,0:T(4,128)} %get-tuple-element.27.table_ref, f32[4,4,128,128]{3,2,1,0:T(8,128)} %kinship_hbm.5, f32[512,256]{1,0:T(8,128)} %get-tuple-element.26.direction_hbm, f32[512,1]{1,0:T(8,128)} %get-tuple-element.28.diagonal_ref, f32[512,256]{1,0:T(8,128)} %phenotypes_hbm.3, ...), custom_call_target="tpu_custom_call" | custom-call | tf_op jit(solution)/shard_map/pallas_call | solution.py:416
  78.7 4.4 %all-to-all-start.2 = ((f32[8,136,256]{2,1,0:T(8,128)}), f32[8,136,256]{2,1,0:T(8,128)}, u32[]{:S(2)}, u32[]{:S(2)}) async-start(f32[8,136,256]{2,1,0:T(8,128)} %get-tuple-element.39), calls=%async_computation.2 | async-start | bytes 2228224 | tf_op jit(solution)/shard_map/all_to_all | solution.py:385
  85.2 2.0 %collective-permute-start.3 = (f32[4,128,256]{2,1,0:T(8,128)S(1)}, f32[4,128,256]{2,1,0:T(8,128)S(1)}, u32[]{:S(2)}, u32[]{:S(2)}) collective-permute-start(f32[4,128,256]{2,1,0:T(8,128)S(1)} %dynamic-slice_bitcast_fusion), channel_id=1, source_target_pairs={{0,2},{2,0},{4,6},{6,4},{8,10},{10,8},{12,14},{14,12},{1,3},{3,1},... | collective-permute-start | bytes 1572872 | tf_op jit(solution)/shard_map/ppermute | solution.py:331
  87.2 1.5 %collective-permute-start.4 = (f32[2,128,256]{2,1,0:T(8,128)S(1)}, f32[2,128,256]{2,1,0:T(8,128)S(1)}, u32[]{:S(2)}, u32[]{:S(2)}) collective-permute-start(f32[2,128,256]{2,1,0:T(8,128)S(1)} %dynamic-slice_bitcast_fusion.4), channel_id=1, source_target_pairs={{0,4},{2,6},{4,0},{6,2},{8,12},{10,14},{12,8},{14,10},{1,5},{3,7},... | collective-permute-start | bytes 786440 | tf_op jit(solution)/shard_map/ppermute | solution.py:331
  88.7 18.8 %collective-permute-done.4 = f32[2,128,256]{2,1,0:T(8,128)S(1)} collective-permute-done((f32[2,128,256]{2,1,0:T(8,128)S(1)}, f32[2,128,256]{2,1,0:T(8,128)S(1)}, u32[]{:S(2)}, u32[]{:S(2)}) %collective-permute-start.4) | collective-permute-done | bytes 262176 | tf_op jit(solution)/shard_map/ppermute | solution.py:331
  111.4 2.4 %collective-permute-start.6 = (f32[1,128,256]{2,1,0:T(8,128)S(1)}, f32[1,128,256]{2,1,0:T(8,128)S(1)}, u32[]{:S(2)}, u32[]{:S(2)}) collective-permute-start(f32[1,128,256]{2,1,0:T(8,128)S(1)} %get-tuple-element.54), channel_id=1, source_target_pairs={{0,8},{2,10},{4,12},{6,14},{8,0},{10,2},{12,4},{14,6},{1,9},{3,11}... | collective-permute-start | bytes 393224 | tf_op jit(solution)/shard_map/ppermute | solution.py:331
  113.9 5.2 %shard_map.71 = f32[16,8,256]{2,1,0:T(8,128)} custom-call(s32[4,12]{1,0:T(4,128)} %get-tuple-element.27.table_ref, f32[4,4,128,128]{3,2,1,0:T(8,128)} %kinship_hbm.5, f32[512,256]{1,0:T(8,128)} %get-tuple-element.26.direction_hbm, f32[512,1]{1,0:T(8,128)} %get-tuple-element.28.diagonal_ref, f32[512,256]{1,0:T(8,128)} %get-tuple-element.38.scaled_hbm, ...), custom_call_target="tpu_custom_call" | custom-call | tf_op jit(solution)/shard_map/pallas_call | solution.py:435
  119.1 1.4 collective-permute-done.5
  120.6 1.5 %collective-permute-start.7 = (f32[1,128,256]{2,1,0:T(8,128)S(1)}, f32[1,128,256]{2,1,0:T(8,128)S(1)}, u32[]{:S(2)}, u32[]{:S(2)}) collective-permute-start(f32[1,128,256]{2,1,0:T(8,128)S(1)} %get-tuple-element.52), channel_id=1, source_target_pairs={{0,8},{2,10},{4,12},{6,14},{8,0},{10,2},{12,4},{14,6},{1,9},{3,11}... | collective-permute-start | bytes 393224 | tf_op jit(solution)/shard_map/ppermute | solution.py:331
  122.1 4.1 %all-to-all-start.3 = ((f32[16,8,256]{2,1,0:T(8,128)}), f32[16,8,256]{2,1,0:T(8,128)S(1)}, u32[]{:S(2)}, u32[]{:S(2)}) async-start(f32[16,8,256]{2,1,0:T(8,128)} %shard_map.71), calls=%async_computation.3 | async-start | bytes 262144 | tf_op jit(solution)/shard_map/all_to_all | solution.py:451
  126.2 2.2 %collective-permute-done.7 = f32[1,128,256]{2,1,0:T(8,128)S(1)} collective-permute-done((f32[1,128,256]{2,1,0:T(8,128)S(1)}, f32[1,128,256]{2,1,0:T(8,128)S(1)}, u32[]{:S(2)}, u32[]{:S(2)}) %collective-permute-start.7) | collective-permute-done | bytes 131104 | tf_op jit(solution)/shard_map/ppermute | solution.py:331
  128.5 5.6 %all-to-all-done.3.sums_hbm = f32[16,8,256]{2,1,0:T(8,128)S(1)} async-done(((f32[16,8,256]{2,1,0:T(8,128)}), f32[16,8,256]{2,1,0:T(8,128)S(1)}, u32[]{:S(2)}, u32[]{:S(2)}) %all-to-all-start.3) | async-done | bytes 131104 | tf_op jit(solution)/shard_map/all_to_all | solution.py:451
  134.9 2.8 %shard_map.72 = (f32[512,256]{1,0:T(8,128)}, f32[64,512]{1,0:T(8,128)}) custom-call(f32[512,256]{1,0:T(8,128)} %get-tuple-element.26.direction_hbm, f32[512,256]{1,0:T(8,128)} %get-tuple-element.38.scaled_hbm, f32[128,256]{1,0:T(8,128)} %copy-done.8, f32[128,256]{1,0:T(8,128)} %bitcast.53, f32[128,256]{1,0:T(8,128)} %copy-done.11, f32[16,8,256]{2,1,0:T(8,128)} %copy-done.10), custom_call_target="tpu_custom_call" | custom-call | tf_op jit(solution)/shard_map/pallas_call | solution.py:454
  (50 shorter events, 9.6 us)
Async XLA Ops:
  4.7 7.1 %copy-start.1 = (f32[512,256]{1,0:T(8,128)S(1)}, f32[512,256]{1,0:T(8,128)}, u32[]{:S(2)}) copy-start(f32[512,256]{1,0:T(8,128)} %get-tuple-element.26.direction_hbm) | copy-start | bytes 1572868
  4.7 33.6 %all-to-all-start = ((f32[8,128,256]{2,1,0:T(8,128)}), f32[8,128,256]{2,1,0:T(8,128)S(1)}, u32[]{:S(2)}, u32[]{:S(2)}) async-start(f32[8,128,256]{2,1,0:T(8,128)} %get-tuple-element.29), calls=%async_computation | async-start | bytes 2097152 | tf_op jit(solution)/shard_map/all_to_all | solution.py:385
  11.7 34.5 %copy-start.6 = (f32[512,512]{0,1:T(8,128)}, f32[512,512]{0,1:T(8,128)S(1)}, u32[]{:S(2)}) copy-start(f32[512,512]{0,1:T(8,128)S(1)} %copy.8) | copy-start | bytes 3145732
  11.7 34.5 %collective-permute-start.1 = (f32[512,512]{0,1:T(8,128)S(1)}, f32[512,512]{0,1:T(8,128)}, u32[]{:S(2)}, u32[]{:S(2)}) collective-permute-start(f32[512,512]{0,1:T(8,128)S(1)} %copy.8), channel_id=1, source_target_pairs={{0,1},{1,0},{2,3},{3,2},{4,5},{5,4},{6,7},{7,6},{8,9},{9,8},{10,11... | collective-permute-start | bytes 3145736 | tf_op jit(solution)/shard_map/ppermute | solution.py:331
  11.8 26.5 %collective-permute-start = (f32[512,256]{1,0:T(8,128)S(1)}, f32[512,256]{1,0:T(8,128)S(1)}, u32[]{:S(2)}, u32[]{:S(2)}) collective-permute-start(f32[512,256]{1,0:T(8,128)S(1)} %copy-done.1), channel_id=1, source_target_pairs={{0,8},{2,10},{4,12},{6,14},{8,0},{10,2},{12,4},{14,6},{1,9},{3,11}... | collective-permute-start | bytes 1572872 | tf_op jit(solution)/shard_map/ppermute | solution.py:331
  38.3 0.8 copy-start.4
  38.3 9.8 %copy-start = (f32[8,128,256]{2,1,0:T(8,128)}, f32[8,128,256]{2,1,0:T(8,128)S(1)}, u32[]{:S(2)}) copy-start(f32[8,128,256]{2,1,0:T(8,128)S(1)} %all-to-all-done.near_hbm) | copy-start | bytes 3145732
  41.9 31.4 %all-to-all-start.1 = ((f32[8,128,256]{2,1,0:T(8,128)}), f32[8,128,256]{2,1,0:T(8,128)}, u32[]{:S(2)}, u32[]{:S(2)}) async-start(f32[8,128,256]{2,1,0:T(8,128)} %shard_map.69), calls=%async_computation.1 | async-start | bytes 2097152 | tf_op jit(solution)/shard_map/all_to_all | solution.py:385
  46.2 1.9 %copy-start.2 = (f32[512,256]{1,0:T(8,128)S(1)}, f32[512,256]{1,0:T(8,128)}, u32[]{:S(2)}) copy-start(f32[512,256]{1,0:T(8,128)} %get-tuple-element.26.direction_hbm) | copy-start | bytes 1572868
  49.9 21.5 %collective-permute-start.2 = (f32[4,128,256]{2,1,0:T(8,128)}, f32[4,128,256]{2,1,0:T(8,128)}, u32[]{:S(2)}, u32[]{:S(2)}) collective-permute-start(f32[4,128,256]{2,1,0:T(8,128)} %dynamic-slice_bitcast_fusion.1), channel_id=1, source_target_pairs={{0,2},{2,0},{4,6},{6,4},{8,10},{10,8},{12,14},{14,12},{1,3},{3,1},... | collective-permute-start | bytes 1572872 | tf_op jit(solution)/shard_map/ppermute | solution.py:331
  78.7 4.4 %copy-start.3 = (f32[512,256]{1,0:T(8,128)S(1)}, f32[512,256]{1,0:T(8,128)}, u32[]{:S(2)}) copy-start(f32[512,256]{1,0:T(8,128)} %get-tuple-element.38.scaled_hbm) | copy-start | bytes 1572868
  78.7 31.8 %all-to-all-start.2 = ((f32[8,136,256]{2,1,0:T(8,128)}), f32[8,136,256]{2,1,0:T(8,128)}, u32[]{:S(2)}, u32[]{:S(2)}) async-start(f32[8,136,256]{2,1,0:T(8,128)} %get-tuple-element.39), calls=%async_computation.2 | async-start | bytes 2228224 | tf_op jit(solution)/shard_map/all_to_all | solution.py:385
  83.1 4.0 %copy-start.7 = (f32[4,128,256]{2,1,0:T(8,128)S(1)}, f32[4,128,256]{2,1,0:T(8,128)}, u32[]{:S(2)}) copy-start(f32[4,128,256]{2,1,0:T(8,128)} %bitcast_add_fusion.1) | copy-start | bytes 1572868
  84.1 1.0 copy-start.5
  85.2 23.5 %collective-permute-start.3 = (f32[4,128,256]{2,1,0:T(8,128)S(1)}, f32[4,128,256]{2,1,0:T(8,128)S(1)}, u32[]{:S(2)}, u32[]{:S(2)}) collective-permute-start(f32[4,128,256]{2,1,0:T(8,128)S(1)} %dynamic-slice_bitcast_fusion), channel_id=1, source_target_pairs={{0,2},{2,0},{4,6},{6,4},{8,10},{10,8},{12,14},{14,12},{1,3},{3,1},... | collective-permute-start | bytes 1572872 | tf_op jit(solution)/shard_map/ppermute | solution.py:331
  87.2 20.3 %collective-permute-start.4 = (f32[2,128,256]{2,1,0:T(8,128)S(1)}, f32[2,128,256]{2,1,0:T(8,128)S(1)}, u32[]{:S(2)}, u32[]{:S(2)}) collective-permute-start(f32[2,128,256]{2,1,0:T(8,128)S(1)} %dynamic-slice_bitcast_fusion.4), channel_id=1, source_target_pairs={{0,4},{2,6},{4,0},{6,2},{8,12},{10,14},{12,8},{14,10},{1,5},{3,7},... | collective-permute-start | bytes 786440 | tf_op jit(solution)/shard_map/ppermute | solution.py:331
  110.5 10.0 %collective-permute-start.5 = (f32[2,128,256]{2,1,0:T(8,128)S(1)}, f32[2,128,256]{2,1,0:T(8,128)S(1)}, u32[]{:S(2)}, u32[]{:S(2)}) collective-permute-start(f32[2,128,256]{2,1,0:T(8,128)S(1)} %get-tuple-element.50), channel_id=1, source_target_pairs={{0,4},{2,6},{4,0},{6,2},{8,12},{10,14},{12,8},{14,10},{1,5},{3,7},... | collective-permute-start | bytes 786440 | tf_op jit(solution)/shard_map/ppermute | solution.py:331
  111.4 10.6 %collective-permute-start.6 = (f32[1,128,256]{2,1,0:T(8,128)S(1)}, f32[1,128,256]{2,1,0:T(8,128)S(1)}, u32[]{:S(2)}, u32[]{:S(2)}) collective-permute-start(f32[1,128,256]{2,1,0:T(8,128)S(1)} %get-tuple-element.54), channel_id=1, source_target_pairs={{0,8},{2,10},{4,12},{6,14},{8,0},{10,2},{12,4},{14,6},{1,9},{3,11}... | collective-permute-start | bytes 393224 | tf_op jit(solution)/shard_map/ppermute | solution.py:331
  120.6 7.8 %collective-permute-start.7 = (f32[1,128,256]{2,1,0:T(8,128)S(1)}, f32[1,128,256]{2,1,0:T(8,128)S(1)}, u32[]{:S(2)}, u32[]{:S(2)}) collective-permute-start(f32[1,128,256]{2,1,0:T(8,128)S(1)} %get-tuple-element.52), channel_id=1, source_target_pairs={{0,8},{2,10},{4,12},{6,14},{8,0},{10,2},{12,4},{14,6},{1,9},{3,11}... | collective-permute-start | bytes 393224 | tf_op jit(solution)/shard_map/ppermute | solution.py:331
  122.1 12.1 %copy-start.8 = (f32[128,256]{1,0:T(8,128)}, f32[128,256]{1,0:T(8,128)S(1)}, u32[]{:S(2)}) copy-start(f32[128,256]{1,0:T(8,128)S(1)} %add_bitcast_fusion.direction_scores_hbm) | copy-start | bytes 393220
  122.1 12.1 %all-to-all-start.3 = ((f32[16,8,256]{2,1,0:T(8,128)}), f32[16,8,256]{2,1,0:T(8,128)S(1)}, u32[]{:S(2)}, u32[]{:S(2)}) async-start(f32[16,8,256]{2,1,0:T(8,128)} %shard_map.71), calls=%async_computation.3 | async-start | bytes 262144 | tf_op jit(solution)/shard_map/all_to_all | solution.py:451
  128.4 5.8 %copy-start.9 = (f32[1,128,256]{2,1,0:T(8,128)}, f32[1,128,256]{2,1,0:T(8,128)S(1)}, u32[]{:S(2)}) copy-start(f32[1,128,256]{2,1,0:T(8,128)S(1)} %add.78) | copy-start | bytes 393220
  128.5 5.7 %collective-permute-start.8 = (f32[128,256]{1,0:T(8,128)S(1)}, f32[128,256]{1,0:T(8,128)S(1)}, u32[]{:S(2)}, u32[]{:S(2)}) collective-permute-start(f32[128,256]{1,0:T(8,128)S(1)} %pad_maximum_fusion.1), channel_id=1, source_target_pairs={{0,1},{1,0},{2,3},{3,2},{4,5},{5,4},{6,7},{7,6},{8,9},{9,8},{10,11... | collective-permute-start | bytes 393224 | tf_op jit(solution)/shard_map/ppermute | solution.py:331
  134.2 0.7 copy-start.11
  (1 other events, 0.7 us)

commit v8 on v7

--- a/solution.py
+++ b/solution.py
@@ -76,10 +76,11 @@
 
 
 def prepare_kernel(devices, capacity, list_ref, kinship_hbm, variance_hbm, phenotypes_hbm, direction_hbm, diagonal_ref,
-                   table_ref, forward_ref, outgoing_hbm, kinship_ref, variance_ref, phenotypes_ref, direction_ref,
-                   first_ref, last_ref, semaphores):
+                   table_ref, forward_ref, *refs):
+    half = devices // 2
+    outgoing_hbm, refs = refs[:half - 1], refs[half - 1:]
+    kinship_ref, variance_ref, phenotypes_ref, direction_ref, first_ref, last_ref, semaphores = refs
     block_count, positions, tile = kinship_ref.shape[:3]
-    half = devices // 2
     copies = Copies(semaphores)
     loads = [copies.start(variance_hbm, variance_ref)]
     for row in range(block_count):
@@ -88,7 +89,6 @@
         loads.append(copies.start(phenotypes_hbm.at[block], phenotypes_ref.at[block]))
     me = lax.axis_index("samples")
     partner = me ^ half
-    base = me & half
     spare = me ^ 1
     top = block_count * block_count
 
@@ -120,10 +120,10 @@
         return blocks
 
     collect(partner)
-    for i in range(half):
-        blocks = blocks_for(partner, base + i)
+    for k in range(1, half):
+        blocks = blocks_for(partner, me ^ k)
         for slot in range(capacity):
-            forward_ref[slot, i] = blocks[slot]
+            forward_ref[slot, k] = blocks[slot]
     for entry, (live, other, far_block, key) in enumerate(collect(me)):
         first, last = first_ref[other], last_ref[other]
         handled = jnp.where(me < other, first, last)
@@ -136,7 +136,7 @@
     for other in range(devices):
         blocks = blocks_for(me, other)
         table_ref[3, other] = jnp.where(me < other, blocks[1], blocks[0])
-    near = [blocks_for(me, base + i) for i in range(half)]
+    near = [blocks_for(me, me ^ k) for k in range(1, half)]
     stores = []
     diagonal_mask = on_diagonal(tile)
     loads[0].wait()
@@ -150,45 +150,49 @@
         diagonal_ref[block, :] = diagonal
         direction_ref[block, :] = phenotypes_ref[block, :] * (1.0 / diagonal)
         stores.append(copies.start(direction_ref.at[block], direction_hbm.at[block]))
-    for i in range(half):
+    for k in range(1, half):
         for slot in range(capacity):
-            start = pl.multiple_of(near[i][slot] * tile, tile)
-            stores.append(copies.start(direction_ref.at[pl.ds(start, tile)], outgoing_hbm.at[i * capacity + slot]))
+            start = pl.multiple_of(near[k - 1][slot] * tile, tile)
+            stores.append(copies.start(direction_ref.at[pl.ds(start, tile)], outgoing_hbm[k - 1].at[slot]))
     wait_all(stores)
 
 
-def forward_kernel(forward_ref, partner_hbm, outgoing_hbm, partner_ref, semaphores):
+def forward_kernel(forward_ref, *refs):
     capacity, half = forward_ref.shape
-    tile = outgoing_hbm.shape[1]
+    partner_hbm = refs[half - 1]
+    outgoing_hbm, (partner_ref, semaphores) = refs[-1 - half:-2], refs[-2:]
+    tile = outgoing_hbm[0].shape[1]
     copies = Copies(semaphores)
     copies.start(partner_hbm, partner_ref).wait()
     stores = []
-    for i in range(half):
+    for k in range(1, half):
         for slot in range(capacity):
-            start = pl.multiple_of(forward_ref[slot, i] * tile, tile)
-            stores.append(copies.start(partner_ref.at[pl.ds(start, tile)], outgoing_hbm.at[i * capacity + slot]))
+            start = pl.multiple_of(forward_ref[slot, k] * tile, tile)
+            stores.append(copies.start(partner_ref.at[pl.ds(start, tile)], outgoing_hbm[k - 1].at[slot]))
     wait_all(stores)
 
 
-def load_received(copies, devices, capacity, near_hbm, far_hbm, partner_hbm, received_ref):
+def load_received(copies, devices, capacity, received_hbm, received_ref):
     half = devices // 2
-    base = lax.axis_index("samples") & half
-    count = half * capacity
-    return [
-        copies.start(near_hbm, received_ref.at[pl.ds(base * capacity, count)]),
-        copies.start(far_hbm, received_ref.at[pl.ds((half - base) * capacity, count)]),
-        copies.start(partner_hbm, received_ref.at[pl.ds(devices * capacity, partner_hbm.shape[0])]),
-    ]
-
-
-def apply_kernel(devices, capacity, table_ref, kinship_hbm, direction_hbm, diagonal_ref, phenotypes_hbm, near_hbm,
-                 far_hbm, partner_hbm, scaled_hbm, outgoing_hbm, sums_ref, kinship_ref, direction_ref, phenotypes_ref, received_ref,
-                 scaled_ref, high_ref, low_ref, semaphores):
+    me = lax.axis_index("samples")
+    near_hbm, far_hbm, partner_hbm = received_hbm[:half - 1], received_hbm[half - 1:-1], received_hbm[-1]
+    loads = [copies.start(partner_hbm, received_ref.at[pl.ds(devices * capacity, partner_hbm.shape[0])])]
+    for k in range(1, half):
+        mate = me ^ k
+        loads.append(copies.start(near_hbm[k - 1], received_ref.at[pl.ds(mate * capacity, capacity)]))
+        loads.append(copies.start(far_hbm[k - 1], received_ref.at[pl.ds((mate ^ half) * capacity, capacity)]))
+    return loads
+
+
+def apply_kernel(devices, capacity, table_ref, kinship_hbm, direction_hbm, diagonal_ref, phenotypes_hbm, *refs):
+    received_hbm, refs = refs[:devices - 1], refs[devices - 1:]
+    (scaled_hbm, outgoing_hbm, sums_ref, kinship_ref, direction_ref, phenotypes_ref, received_ref, scaled_ref, high_ref,
+     low_ref, semaphores) = refs
     block_count, positions, tile = kinship_ref.shape[:3]
     columns = direction_ref.shape[1]
     copies = Copies(semaphores)
     tiles = copies.start(kinship_hbm, kinship_ref)
-    arrivals = load_received(copies, devices, capacity, near_hbm, far_hbm, partner_hbm, received_ref)
+    arrivals = load_received(copies, devices, capacity, received_hbm, received_ref)
     loads = [copies.start(direction_hbm, direction_ref), copies.start(phenotypes_hbm, phenotypes_ref)]
     norm = jnp.zeros((SUBLANES, columns), jnp.float32)
     cross = jnp.zeros((SUBLANES, columns), jnp.float32)
@@ -219,9 +223,11 @@
     wait_all(stores)
 
 
-def curvature_kernel(devices, capacity, table_ref, kinship_hbm, direction_hbm, diagonal_ref, scaled_hbm, near_hbm,
-                     far_hbm, partner_hbm, later_hbm, sums_hbm, kinship_ref, direction_ref, scaled_ref, received_ref, later_ref, high_ref,
-                     low_ref, sums_ref, semaphores):
+def curvature_kernel(devices, capacity, table_ref, kinship_hbm, direction_hbm, diagonal_ref, scaled_hbm, later_hbm,
+                     *refs):
+    received_hbm = refs[:devices - 1]
+    (sums_hbm, kinship_ref, direction_ref, scaled_ref, received_ref, later_ref, high_ref, low_ref, sums_ref,
+     semaphores) = refs[-10:]
     block_count, positions, tile = kinship_ref.shape[:3]
     columns = direction_ref.shape[1]
     copies = Copies(semaphores)
@@ -231,7 +237,7 @@
         copies.start(direction_hbm, direction_ref),
         copies.start(scaled_hbm, scaled_ref),
     ]
-    loads += load_received(copies, devices, capacity, near_hbm, far_hbm, partner_hbm, received_ref)
+    loads += load_received(copies, devices, capacity, received_hbm, received_ref)
     tiles.wait()
     split_tiles(kinship_ref, high_ref, low_ref)
     wait_all(loads)
@@ -331,18 +337,8 @@
     return lax.ppermute(values, axis, [(i, i ^ step) for i in range(devices)])
 
 
-def halve(values, devices, step):
-    bit = (lax.axis_index("samples") // step) % 2
-    halves = values.reshape(-1, 2, *values.shape[1:])
-    kept = lax.dynamic_index_in_dim(halves, bit, 1, keepdims=False)
-    given = lax.dynamic_index_in_dim(halves, 1 - bit, 1, keepdims=False)
-    return kept, swap(given, "samples", devices, step)
-
-
-def halve_all(values, devices, steps):
-    for step in steps:
-        values = sum(halve(values, devices, step))
-    return values
+def after(value, *others):
+    return lax.optimization_barrier((value, *others))[0]
 
 
 def per_device(kinship, relatives, variance, phenotypes, dosage):
@@ -355,6 +351,7 @@
     capacity = -(-entries // (devices - 1))
     assert capacity <= 2
     hbm = pl.BlockSpec(memory_space=pltpu.HBM)
+    anywhere = pl.BlockSpec(memory_space=pl.ANY)
     vmem = pl.BlockSpec(memory_space=pltpu.VMEM)
     smem = pl.BlockSpec(memory_space=pltpu.SMEM)
     float_of = lambda *shape: jax.ShapeDtypeStruct(shape, jnp.float32)
@@ -363,98 +360,113 @@
     full_room = room(people, columns)
     tiles_room = pltpu.VMEM((block_count, tile, positions * tile), jnp.bfloat16)
     half = devices // 2
-    direction, diagonal, table, forward, outgoing = call(
+    near_by = list(range(1, half))
+    direction, diagonal, table, forward, *outgoing = call(
         functools.partial(prepare_kernel, devices, capacity),
         [
             full,
             float_of(people, 1),
             jax.ShapeDtypeStruct((4, max(entries, devices)), jnp.int32),
             jax.ShapeDtypeStruct((capacity, half), jnp.int32),
-            float_of(half * capacity, tile, columns),
-        ],
+        ] + [float_of(capacity, tile, columns)] * (half - 1),
         [smem, hbm, hbm, hbm],
-        [hbm, vmem, smem, smem, hbm],
+        [hbm, vmem, smem, smem] + [hbm] * (half - 1),
         [
             room(*kinship.shape), room(block_count, tile), full_room, full_room,
             pltpu.SMEM((devices,), jnp.int32), pltpu.SMEM((devices,), jnp.int32),
-            pltpu.SemaphoreType.DMA((3 * block_count + capacity * half + 1,)),
+            pltpu.SemaphoreType.DMA((3 * block_count + capacity * (half - 1) + 1,)),
         ],
     )(relatives.T, kinship, variance.reshape(block_count, tile), phenotypes)
 
-    def exchange(blocks, groups=None):
-        return lax.all_to_all(
-            blocks, "samples", split_axis=0, concat_axis=0, axis_index_groups=groups, tiled=True
-        )
-
-    halves = [list(range(half)), list(range(half, devices))]
-
-    both_dosages = jnp.concatenate(
-        [values.reshape(people, devices, share_rows) for values in (dosage, swap(dosage, "cols", 2, 1))], axis=2
-    ).reshape(people, 2 * variants)
+    def to_mates(blocks):
+        return [swap(block, "samples", devices, k) for k, block in zip(near_by, blocks)]
+
+    me = lax.axis_index("samples")
+    dosage = after(dosage, direction)
+    other_dosage = swap(dosage, "cols", 2, 1)
+    dosages = [values.reshape(people, devices, share_rows) for values in (dosage, other_dosage)]
+    fourth = devices // 4
+    grouped = [
+        jnp.concatenate([
+            lax.dynamic_index_in_dim(values, me ^ (4 * j + k), 1, keepdims=False)
+            for j in range(fourth) for values in dosages
+        ], axis=1)
+        for k in range(4)
+    ]
 
     def variant_products(values):
-        partial = lax.dot_general(
-            both_dosages, values, (((0,), (0,)), ((), ())), precision=lax.Precision.HIGH,
-            preferred_element_type=jnp.float32,
-        )
-        return partial.reshape(devices, 2 * share_rows, columns)
-
-    steps = [2 ** i for i in range(devices.bit_length() - 1)]
+        return [
+            lax.dot_general(
+                group, values, (((0,), (0,)), ((), ())), precision=lax.Precision.HIGH,
+                preferred_element_type=jnp.float32,
+            ).reshape(fourth, 2 * share_rows, columns)
+            for group in grouped
+        ]
+
+    def neighbour_shares(products):
+        return [swap(products[k], "samples", devices, k) for k in range(1, 4)]
+
+    def over_the_middle(values):
+        return values[:fourth // 2], swap(values[fourth // 2:], "samples", devices, half)
+
+    def remaining(values):
+        step = half // 2
+        while values.shape[0] > 1:
+            count = values.shape[0] // 2
+            values = values[:count] + swap(values[count:], "samples", devices, step)
+            step //= 2
+        return values[0]
+
+    near = to_mates(after(outgoing, other_dosage))
     partner = swap(direction, "samples", devices, half)
-    near = exchange(outgoing, halves)
-    partner, near = lax.optimization_barrier((partner, near))
-    far = exchange(call(
+    direction_products = variant_products(direction)
+    direction_shares = neighbour_shares(direction_products)
+    far = to_mates(call(
         forward_kernel,
-        float_of(half * capacity, tile, columns),
-        [smem, hbm],
-        hbm,
-        [full_room, pltpu.SemaphoreType.DMA((half * capacity + 1,))],
-    )(forward, partner), halves)
-    received = [near, far, partner.reshape(block_count, tile, columns)]
-    direction_scores = halve_all(variant_products(direction), devices, steps[:1])
-    received, direction_scores = lax.optimization_barrier((received, direction_scores))
+        [float_of(capacity, tile, columns)] * (half - 1),
+        [smem] + [anywhere] * (half + 4),
+        [hbm] * (half - 1),
+        [full_room, pltpu.SemaphoreType.DMA((capacity * (half - 1) + 1,))],
+    )(forward, *near, partner, *direction_products))
+    received = near + far + [partner.reshape(block_count, tile, columns)]
     scaled, outgoing = call(
         functools.partial(apply_kernel, devices, capacity),
         [full, float_of(devices, tile + SUBLANES, columns)],
-        [smem, hbm, hbm, vmem] + [hbm] * 4,
+        [smem, hbm, hbm, vmem, hbm] + [anywhere] * (devices - 1),
         [hbm, hbm],
         [
             room(SUBLANES, columns),
-            room(*kinship.shape), full_room, full_room, room(devices * capacity + block_count, tile, columns), full_room,
-            tiles_room, tiles_room,
-            pltpu.SemaphoreType.DMA((2 * devices + 9,)),
+            room(*kinship.shape), full_room, full_room, room(devices * capacity + block_count, tile, columns),
+            full_room, tiles_room, tiles_room,
+            pltpu.SemaphoreType.DMA((3 * devices + 5,)),
         ],
     )(table, kinship, direction, diagonal, phenotypes, *received)
-    later = exchange(outgoing)
-    scaled, direction_scores = lax.optimization_barrier((scaled, direction_scores))
-    scaled_scores = halve_all(variant_products(scaled), devices, steps[:1])
-    direction_scores = halve_all(direction_scores, devices, steps[1:2])
-    later, scaled_scores, direction_scores = lax.optimization_barrier((later, scaled_scores, direction_scores))
-    direction_kept, direction_given = halve(direction_scores, devices, steps[2])
-    scaled_kept, scaled_given = halve(scaled_scores, devices, steps[1])
+    later = lax.all_to_all(outgoing, "samples", split_axis=0, concat_axis=0, tiled=True)
+    scaled_products = variant_products(scaled)
+    scaled_sum = scaled_products[0] + sum(neighbour_shares(scaled_products))
+    direction_sum = after(direction_products[0], scaled) + sum(direction_shares)
+    scaled_kept, scaled_taken = over_the_middle(scaled_sum)
+    direction_kept, direction_taken = over_the_middle(direction_sum)
     sums = call(
         functools.partial(curvature_kernel, devices, capacity),
         float_of(2 * devices, SUBLANES, columns),
-        [smem, hbm, hbm, vmem] + [hbm] * 5,
+        [smem, hbm, hbm, vmem, hbm, hbm] + [anywhere] * devices,
         hbm,
         [
             room(*kinship.shape), full_room, full_room, room(devices * capacity + block_count, tile, columns),
             room(devices, tile + SUBLANES, columns), tiles_room, tiles_room,
             room(2 * devices, SUBLANES, columns),
-            pltpu.SemaphoreType.DMA((10,)),
+            pltpu.SemaphoreType.DMA((2 * devices + 5,)),
         ],
-    )(table, kinship, direction, diagonal, scaled, *received, later)
-    sums, direction_kept, scaled_kept = lax.optimization_barrier((sums, direction_kept, scaled_kept))
-    direction_scores = halve_all(direction_kept + direction_given, devices, steps[3:])[0]
-    scaled_kept, scaled_given = halve(scaled_kept + scaled_given, devices, steps[2])
-    sums, scaled_kept, direction_scores = lax.optimization_barrier((sums, scaled_kept, direction_scores))
+    )(table, kinship, direction, diagonal, scaled, later, *received, scaled_sum)
     all_sums = lax.all_to_all(sums, ("samples", "cols"), split_axis=0, concat_axis=0, tiled=True)
-    scaled_scores = halve_all(scaled_kept + scaled_given, devices, steps[3:])[0]
+    direction_scores = remaining(after(direction_kept, sums) + direction_taken)
+    scaled_scores = remaining(after(scaled_kept, sums) + scaled_taken)
     swapped = swap(jnp.concatenate([direction_scores[share_rows:], scaled_scores[share_rows:]]), "cols", 2, 1)
     solved, scores = call(
         functools.partial(finish_kernel, devices, 1.0 / math.sqrt(people * devices)),
         [full, float_of(share_rows, 2 * columns)],
-        [hbm] * 6,
+        [hbm, hbm] + [anywhere] * 4,
         [hbm, vmem],
         [
             full_room, full_room, room(share_rows, columns), room(share_rows, columns),

time: 138 us -> 123 us (0.89)
  waiting for transfers between devices: 73.1 us -> 56 us
  matrix products: 1.99 us -> 5.9 us
  other arithmetic: 5.01 us -> 1.3 us
  local copies, waits for them, and re-layouts: 5.05 us -> 7.42 us
    ppermute x9 -> x17, waiting for transfers between devices: 66.8 us -> 49.6 us  [swap(): return lax.ppermute(values, axis, [(i, i ^ step) for i in range(devices)])]
    ppermute x9 -> x17, starting transfers between devices: 13.1 us -> 20.4 us  [swap(): return lax.ppermute(values, axis, [(i, i ^ step) for i in range(devices)])]
    all_to_all x3 -> x1, starting transfers between devices: 14 us -> 6.94 us  [per_device(): lax.all_to_all(outgoing, 'samples', split_axis=0, concat_axis=0, tiled=True)]
    dot_general x2 -> x8, matrix products: 1.99 us -> 5.9 us  [variant_products(): lax.dot_general(group, values, (((0,), (0,)), ((), ())), precision=lax.Pr...]
    concatenate x1 -> x0, other arithmetic: 1.88 us -> none  [per_device(): jnp.concatenate([values.reshape(people, devices, share_rows) for values i...]
    add x5 -> x4, other arithmetic: 3.1 us -> 1.28 us  [the longest x1 1.18 us: per_device(): direction_sum = after(direction_products[0], scaled) + sum(direction_shares)]
    optimization_barrier x0 -> x1, local copies, waits for them, and re-layouts: none -> 1.61 us  [after(): return lax.optimization_barrier((value, *others))[0]]
    unnamed x25 -> x58, local copies, waits for them, and re-layouts: 4.06 us -> 4.3 us
  transfers between devices with their start and end apart: 13 -> 19, of which waited for: 8 -> 8; matrix products, arithmetic and copies ran while one was open for 7% -> 7% of each run, Pallas kernels for 6% -> 8%
where the time goes in v8:
time: 123 us
  waiting for transfers between devices  56 us (46%)
  starting transfers between devices  31.1 us (25%)
  Pallas kernels  19.9 us (16%)
  local copies, waits for them, and re-layouts  7.42 us (6%)
  matrix products  5.9 us (5%)
  other arithmetic  1.3 us (1%)
    ppermute x17, waiting for transfers between devices, swap(): return lax.ppermute(values, axis, [(i, i ^ step) for i in range(devices)])  49.6 us
    ppermute x17, starting transfers between devices, swap(): return lax.ppermute(values, axis, [(i, i ^ step) for i in range(devices)])  20.4 us
    all_to_all x1, starting transfers between devices, per_device(): lax.all_to_all(outgoing, 'samples', split_axis=0, concat_axis=0, tiled=True)  6.94 us
    all_to_all x1, waiting for transfers between devices, per_device(): lax.all_to_all(sums, ('samples', 'cols'), split_axis=0, concat_axis=0, ti...  6.34 us
    dot_general x8, matrix products, variant_products(): lax.dot_general(group, values, (((0,), (0,)), ((), ())), precision=lax.Pr...  5.9 us
    pallas_call x1, Pallas kernels, per_device(): call(functools.partial(apply_kernel, devices, capacity), [full, float_of(...  5.26 us
    pallas_call x1, Pallas kernels, per_device(): call(functools.partial(curvature_kernel, devices, capacity), float_of(2 *...  5.16 us
    unnamed x58, local copies, waits for them, and re-layouts  4.3 us
  transfers between devices with their start and end apart: 19, of which 8 were waited for; matrix products, arithmetic and copies ran while one was open for 7% of the time, Pallas kernels for 8%

profile of v8, /device:TPU:0, one launch (start us, length us, event | category | flops | bytes accessed | tf_op | source)
XLA Modules:
  0.0 122.7 jit_solution(6005418406252309658)
XLA Ops:
  0.6 4.0 %shard_map.68 = (f32[512,256]{1,0:T(8,128)}, f32[512,1]{1,0:T(8,128)}, s32[4,12]{1,0:T(4,128)}, s32[2,4]{1,0:T(2,128)}, f32[2,128,256]{2,1,0:T(8,128)}, /*index=5*/f32[2,128,256]{2,1,0:T(8,128)}, f32[2,128,256]{2,1,0:T(8,128)}) custom-call(s32[3,32]{1,0:T(4,128)} %bitcast.70, f32[4,4,128,128]{3,2,1,0:T(8,128)} %kinship_hbm.5, f32[4,128]{1,0:T(4,128)} %bitcast.71, ...), custom_call_target="tpu_custom_call" | custom-call | tf_op jit(solution)/shard_map/pallas_call | solution.py:364
  4.6 1.6 %copy.7 = f32[512,512]{0,1:T(8,128)S(1)} copy(f32[512,512]{1,0:T(8,128)} %param.9) | data formatting | bytes 2097152 | tf_op jit(solution)/shard_map/optimization_barrier | solution.py:341
  6.8 3.7 %collective-permute-start.4 = (f32[512,256]{1,0:T(8,128)S(1)}, f32[512,256]{1,0:T(8,128)S(1)}, u32[]{:S(2)}, u32[]{:S(2)}) collective-permute-start(f32[512,256]{1,0:T(8,128)S(1)} %copy-done), channel_id=1, source_target_pairs={{0,8},{2,10},{4,12},{6,14},{8,0},{10,2},{12,4},{14,6},{1,9},{3,11}... | collective-permute-start | bytes 1572872 | tf_op jit(solution)/shard_map/ppermute | solution.py:337
  10.6 1.6 %collective-permute-start.1 = (f32[2,128,256]{2,1,0:T(8,128)}, f32[2,128,256]{2,1,0:T(8,128)S(1)}, u32[]{:S(2)}, u32[]{:S(2)}) collective-permute-start(f32[2,128,256]{2,1,0:T(8,128)} %get-tuple-element.28), channel_id=1, source_target_pairs={{0,2},{2,0},{4,6},{6,4},{8,10},{10,8},{12,14},{14,12},{1,3},{3,1},... | collective-permute-start | bytes 786440 | tf_op jit(solution)/shard_map/ppermute | solution.py:337
  12.2 1.6 %collective-permute-start.2 = (f32[2,128,256]{2,1,0:T(8,128)}, f32[2,128,256]{2,1,0:T(8,128)S(1)}, u32[]{:S(2)}, u32[]{:S(2)}) collective-permute-start(f32[2,128,256]{2,1,0:T(8,128)} %get-tuple-element.29), channel_id=1, source_target_pairs={{0,4},{2,6},{4,0},{6,2},{8,12},{10,14},{12,8},{14,10},{1,5},{3,7},... | collective-permute-start | bytes 786440 | tf_op jit(solution)/shard_map/ppermute | solution.py:337
  14.2 1.4 %dynamic-slice_bitcast_fusion.2 = (f32[512,64]{0,1:T(8,128)S(1)}, f32[512,64]{0,1:T(8,128)S(1)}, f32[512,64]{0,1:T(8,128)S(1)}, f32[512,64]{0,1:T(8,128)S(1)}, f...) fusion(f32[512,8,64]{0,2,1:T(8,128)} %bitcast.4, ...), kind=kLoop, calls=%fused_computation.17 | loop fusion | bytes 2097184 | tf_op jit(solution)/shard_map/jit(dynamic_index_in_dim)/squeeze | solution.py:391
  19.9 14.4 %collective-permute-done.4.refs_3_ = f32[512,256]{1,0:T(8,128)S(1)} collective-permute-done((f32[512,256]{1,0:T(8,128)S(1)}, f32[512,256]{1,0:T(8,128)S(1)}, u32[]{:S(2)}, u32[]{:S(2)}) %collective-permute-start.4) | collective-permute-done | bytes 524320 | tf_op jit(solution)/shard_map/ppermute | solution.py:337
  34.3 1.8 %collective-permute-done.3.refs_2_ = f32[2,128,256]{2,1,0:T(8,128)S(1)} collective-permute-done((f32[2,128,256]{2,1,0:T(8,128)S(1)}, f32[2,128,256]{2,1,0:T(8,128)S(1)}, u32[]{:S(2)}, u32[]{:S(2)}) %collective-permute-start.3) | collective-permute-done | bytes 262176 | tf_op jit(solution)/shard_map/ppermute | solution.py:337
  36.9 2.7 %shard_map.69 = (f32[2,128,256]{2,1,0:T(8,128)}, f32[2,128,256]{2,1,0:T(8,128)}, f32[2,128,256]{2,1,0:T(8,128)}) custom-call(s32[2,4]{1,0:T(2,128)} %get-tuple-element.31.forward_ref, f32[2,128,256]{2,1,0:T(8,128)} %copy-done.4, f32[2,128,256]{2,1,0:T(8,128)} %copy-done.5, f32[2,128,256]{2,1,0:T(8,128)} %copy-done.6, f32[512,256]{1,0:T(8,128)} %copy-done.2, ...), custom_call_target="tpu_custom_call" | custom-call | tf_op jit(solution)/shard_map/pallas_call | solution.py:424
  39.6 1.5 %collective-permute-start.5 = (f32[2,128,256]{2,1,0:T(8,128)}, f32[2,128,256]{2,1,0:T(8,128)S(1)}, u32[]{:S(2)}, u32[]{:S(2)}) collective-permute-start(f32[2,128,256]{2,1,0:T(8,128)} %get-tuple-element.32), channel_id=1, source_target_pairs={{0,2},{2,0},{4,6},{6,4},{8,10},{10,8},{12,14},{14,12},{1,3},{3,1},... | collective-permute-start | bytes 786440 | tf_op jit(solution)/shard_map/ppermute | solution.py:337
  41.1 2.0 %collective-permute-start.7 = (f32[2,128,256]{2,1,0:T(8,128)}, f32[2,128,256]{2,1,0:T(8,128)S(1)}, u32[]{:S(2)}, u32[]{:S(2)}) collective-permute-start(f32[2,128,256]{2,1,0:T(8,128)} %get-tuple-element.34), channel_id=1, source_target_pairs={{0,6},{2,4},{4,2},{6,0},{8,14},{10,12},{12,10},{14,8},{1,7},{3,5},... | collective-permute-start | bytes 786440 | tf_op jit(solution)/shard_map/ppermute | solution.py:337
  43.2 1.5 %collective-permute-start.8 = (f32[2,128,256]{2,1,0:T(8,128)}, f32[2,128,256]{2,1,0:T(8,128)}, u32[]{:S(2)}, u32[]{:S(2)}) collective-permute-start(f32[2,128,256]{2,1,0:T(8,128)} %bitcast.13.refs_5_), channel_id=1, source_target_pairs={{0,2},{2,0},{4,6},{6,4},{8,10},{10,8},{12,14},{14,12},{1,3},{3,1},... | collective-permute-start | bytes 786440 | tf_op jit(solution)/shard_map/ppermute | solution.py:337
  44.6 8.7 %collective-permute-done.5.refs_3_ = f32[2,128,256]{2,1,0:T(8,128)S(1)} collective-permute-done((f32[2,128,256]{2,1,0:T(8,128)}, f32[2,128,256]{2,1,0:T(8,128)S(1)}, u32[]{:S(2)}, u32[]{:S(2)}) %collective-permute-start.5) | collective-permute-done | bytes 262176 | tf_op jit(solution)/shard_map/ppermute | solution.py:337
  53.8 2.4 %collective-permute-done.7.refs_5_ = f32[2,128,256]{2,1,0:T(8,128)S(1)} collective-permute-done((f32[2,128,256]{2,1,0:T(8,128)}, f32[2,128,256]{2,1,0:T(8,128)S(1)}, u32[]{:S(2)}, u32[]{:S(2)}) %collective-permute-start.7) | collective-permute-done | bytes 262176 | tf_op jit(solution)/shard_map/ppermute | solution.py:337
  56.9 5.3 %shard_map.70 = (f32[512,256]{1,0:T(8,128)}, f32[8,136,256]{2,1,0:T(8,128)}) custom-call(s32[4,12]{1,0:T(4,128)} %get-tuple-element.22.table_ref, f32[4,4,128,128]{3,2,1,0:T(8,128)} %kinship_hbm.5, f32[512,256]{1,0:T(8,128)} %get-tuple-element.21.direction_hbm, f32[512,1]{1,0:T(8,128)} %get-tuple-element.23.diagonal_ref, f32[512,256]{1,0:T(8,128)} %phenotypes_hbm.3, ...), custom_call_target="tpu_custom_call" | custom-call | tf_op jit(solution)/shard_map/pallas_call | solution.py:432
  62.2 6.9 %all-to-all-start = ((f32[8,136,256]{2,1,0:T(8,128)}), f32[8,136,256]{2,1,0:T(8,128)S(1)}, u32[]{:S(2)}, u32[]{:S(2)}) async-start(f32[8,136,256]{2,1,0:T(8,128)} %get-tuple-element.37), calls=%async_computation | async-start | bytes 2228224 | tf_op jit(solution)/shard_map/all_to_all | solution.py:444
  70.5 3.0 %collective-permute-start.13 = (f32[2,128,256]{2,1,0:T(8,128)S(1)}, f32[2,128,256]{2,1,0:T(8,128)S(1)}, u32[]{:S(2)}, u32[]{:S(2)}) collective-permute-start(f32[2,128,256]{2,1,0:T(8,128)S(1)} %bitcast.67), channel_id=1, source_target_pairs={{0,6},{2,4},{4,2},{6,0},{8,14},{10,12},{12,10},{14,8},{1,7},{3,5},... | collective-permute-start | bytes 786440 | tf_op jit(solution)/shard_map/ppermute | solution.py:337
  75.8 2.9 %collective-permute-start.14 = (f32[1,128,256]{2,1,0:T(8,128)S(1)}, f32[1,128,256]{2,1,0:T(8,128)S(1)}, u32[]{:S(2)}, u32[]{:S(2)}) collective-permute-start(f32[1,128,256]{2,1,0:T(8,128)S(1)} %get-tuple-element.58), channel_id=1, source_target_pairs={{0,8},{2,10},{4,12},{6,14},{8,0},{10,2},{12,4},{14,6},{1,9},{3,11}... | collective-permute-start | bytes 393224 | tf_op jit(solution)/shard_map/ppermute | solution.py:337
  79.2 18.0 %collective-permute-done.13 = f32[2,128,256]{2,1,0:T(8,128)S(1)} collective-permute-done((f32[2,128,256]{2,1,0:T(8,128)S(1)}, f32[2,128,256]{2,1,0:T(8,128)S(1)}, u32[]{:S(2)}, u32[]{:S(2)}) %collective-permute-start.13) | collective-permute-done | bytes 262176 | tf_op jit(solution)/shard_map/ppermute | solution.py:337
  97.2 3.3 %collective-permute-done.12 = f32[2,128,256]{2,1,0:T(8,128)S(1)} collective-permute-done((f32[2,128,256]{2,1,0:T(8,128)S(1)}, f32[2,128,256]{2,1,0:T(8,128)S(1)}, u32[]{:S(2)}, u32[]{:S(2)}) %collective-permute-start.12) | collective-permute-done | bytes 262176 | tf_op jit(solution)/shard_map/ppermute | solution.py:337
  102.3 5.2 %shard_map.71 = f32[16,8,256]{2,1,0:T(8,128)} custom-call(s32[4,12]{1,0:T(4,128)} %get-tuple-element.22.table_ref, f32[4,4,128,128]{3,2,1,0:T(8,128)} %kinship_hbm.5, f32[512,256]{1,0:T(8,128)} %get-tuple-element.21.direction_hbm, f32[512,1]{1,0:T(8,128)} %get-tuple-element.23.diagonal_ref, f32[512,256]{1,0:T(8,128)} %get-tuple-element.35.scaled_hbm, ...), custom_call_target="tpu_custom_call" | custom-call | tf_op jit(solution)/shard_map/pallas_call | solution.py:450
  107.5 3.7 %all-to-all-start.1 = ((f32[16,8,256]{2,1,0:T(8,128)}), f32[16,8,256]{2,1,0:T(8,128)S(1)}, u32[]{:S(2)}, u32[]{:S(2)}) async-start(f32[16,8,256]{2,1,0:T(8,128)} %shard_map.71), calls=%async_computation.1 | async-start | bytes 262144 | tf_op jit(solution)/shard_map/all_to_all | solution.py:462
  112.8 6.3 %all-to-all-done.1.sums_hbm = f32[16,8,256]{2,1,0:T(8,128)S(1)} async-done(((f32[16,8,256]{2,1,0:T(8,128)}), f32[16,8,256]{2,1,0:T(8,128)S(1)}, u32[]{:S(2)}, u32[]{:S(2)}) %all-to-all-start.1) | async-done | bytes 131104 | tf_op jit(solution)/shard_map/all_to_all | solution.py:462
  119.8 2.8 %shard_map.72 = (f32[512,256]{1,0:T(8,128)}, f32[64,512]{1,0:T(8,128)}) custom-call(f32[512,256]{1,0:T(8,128)} %get-tuple-element.21.direction_hbm, f32[512,256]{1,0:T(8,128)} %get-tuple-element.35.scaled_hbm, f32[128,256]{1,0:T(8,128)} %bitcast.65, f32[128,256]{1,0:T(8,128)} %bitcast.66, f32[128,256]{1,0:T(8,128)} %copy-done.27, f32[16,8,256]{2,1,0:T(8,128)} %copy-done.26), custom_call_target="tpu_custom_call" | custom-call | tf_op jit(solution)/shard_map/pallas_call | solution.py:466
  (97 shorter events, 15.3 us)
Async XLA Ops:
  6.3 7.5 %copy-start.28 = (f32[2,128,256]{2,1,0:T(8,128)S(1)}, f32[2,128,256]{2,1,0:T(8,128)}, u32[]{:S(2)}) copy-start(f32[2,128,256]{2,1,0:T(8,128)} %get-tuple-element.30) | copy-start | bytes 786436
  6.3 4.3 %collective-permute-start = (f32[512,512]{0,1:T(8,128)S(1)}, f32[512,512]{0,1:T(8,128)}, u32[]{:S(2)}, u32[]{:S(2)}) collective-permute-start(f32[512,512]{0,1:T(8,128)S(1)} %copy.7), channel_id=1, source_target_pairs={{0,1},{1,0},{2,3},{3,2},{4,5},{5,4},{6,7},{7,6},{8,9},{9,8},{10,11... | collective-permute-start | bytes 3145736 | tf_op jit(solution)/shard_map/ppermute | solution.py:337
  6.8 27.5 %collective-permute-start.4 = (f32[512,256]{1,0:T(8,128)S(1)}, f32[512,256]{1,0:T(8,128)S(1)}, u32[]{:S(2)}, u32[]{:S(2)}) collective-permute-start(f32[512,256]{1,0:T(8,128)S(1)} %copy-done), channel_id=1, source_target_pairs={{0,8},{2,10},{4,12},{6,14},{8,0},{10,2},{12,4},{14,6},{1,9},{3,11}... | collective-permute-start | bytes 1572872 | tf_op jit(solution)/shard_map/ppermute | solution.py:337
  10.6 23.7 %collective-permute-start.1 = (f32[2,128,256]{2,1,0:T(8,128)}, f32[2,128,256]{2,1,0:T(8,128)S(1)}, u32[]{:S(2)}, u32[]{:S(2)}) collective-permute-start(f32[2,128,256]{2,1,0:T(8,128)} %get-tuple-element.28), channel_id=1, source_target_pairs={{0,2},{2,0},{4,6},{6,4},{8,10},{10,8},{12,14},{14,12},{1,3},{3,1},... | collective-permute-start | bytes 786440 | tf_op jit(solution)/shard_map/ppermute | solution.py:337
  12.2 22.1 %collective-permute-start.2 = (f32[2,128,256]{2,1,0:T(8,128)}, f32[2,128,256]{2,1,0:T(8,128)S(1)}, u32[]{:S(2)}, u32[]{:S(2)}) collective-permute-start(f32[2,128,256]{2,1,0:T(8,128)} %get-tuple-element.29), channel_id=1, source_target_pairs={{0,4},{2,6},{4,0},{6,2},{8,12},{10,14},{12,8},{14,10},{1,5},{3,7},... | collective-permute-start | bytes 786440 | tf_op jit(solution)/shard_map/ppermute | solution.py:337
  13.8 22.4 %collective-permute-start.3 = (f32[2,128,256]{2,1,0:T(8,128)S(1)}, f32[2,128,256]{2,1,0:T(8,128)S(1)}, u32[]{:S(2)}, u32[]{:S(2)}) collective-permute-start(f32[2,128,256]{2,1,0:T(8,128)S(1)} %copy-done.28), channel_id=1, source_target_pairs={{0,6},{2,4},{4,2},{6,0},{8,14},{10,12},{12,10},{14,8},{1,7},{3,5},... | collective-permute-start | bytes 786440 | tf_op jit(solution)/shard_map/ppermute | solution.py:337
  39.6 13.7 %collective-permute-start.5 = (f32[2,128,256]{2,1,0:T(8,128)}, f32[2,128,256]{2,1,0:T(8,128)S(1)}, u32[]{:S(2)}, u32[]{:S(2)}) collective-permute-start(f32[2,128,256]{2,1,0:T(8,128)} %get-tuple-element.32), channel_id=1, source_target_pairs={{0,2},{2,0},{4,6},{6,4},{8,10},{10,8},{12,14},{14,12},{1,3},{3,1},... | collective-permute-start | bytes 786440 | tf_op jit(solution)/shard_map/ppermute | solution.py:337
  41.1 12.7 %collective-permute-start.6 = (f32[2,128,256]{2,1,0:T(8,128)}, f32[2,128,256]{2,1,0:T(8,128)S(1)}, u32[]{:S(2)}, u32[]{:S(2)}) collective-permute-start(f32[2,128,256]{2,1,0:T(8,128)} %get-tuple-element.33), channel_id=1, source_target_pairs={{0,4},{2,6},{4,0},{6,2},{8,12},{10,14},{12,8},{14,10},{1,5},{3,7},... | collective-permute-start | bytes 786440 | tf_op jit(solution)/shard_map/ppermute | solution.py:337
  41.1 15.1 %collective-permute-start.7 = (f32[2,128,256]{2,1,0:T(8,128)}, f32[2,128,256]{2,1,0:T(8,128)S(1)}, u32[]{:S(2)}, u32[]{:S(2)}) collective-permute-start(f32[2,128,256]{2,1,0:T(8,128)} %get-tuple-element.34), channel_id=1, source_target_pairs={{0,6},{2,4},{4,2},{6,0},{8,14},{10,12},{12,10},{14,8},{1,7},{3,5},... | collective-permute-start | bytes 786440 | tf_op jit(solution)/shard_map/ppermute | solution.py:337
  43.2 31.3 %collective-permute-start.8 = (f32[2,128,256]{2,1,0:T(8,128)}, f32[2,128,256]{2,1,0:T(8,128)}, u32[]{:S(2)}, u32[]{:S(2)}) collective-permute-start(f32[2,128,256]{2,1,0:T(8,128)} %bitcast.13.refs_5_), channel_id=1, source_target_pairs={{0,2},{2,0},{4,6},{6,4},{8,10},{10,8},{12,14},{14,12},{1,3},{3,1},... | collective-permute-start | bytes 786440 | tf_op jit(solution)/shard_map/ppermute | solution.py:337
  44.6 30.0 %collective-permute-start.9 = (f32[2,128,256]{2,1,0:T(8,128)}, f32[2,128,256]{2,1,0:T(8,128)}, u32[]{:S(2)}, u32[]{:S(2)}) collective-permute-start(f32[2,128,256]{2,1,0:T(8,128)} %bitcast.18.refs_6_), channel_id=1, source_target_pairs={{0,4},{2,6},{4,0},{6,2},{8,12},{10,14},{12,8},{14,10},{1,5},{3,7},... | collective-permute-start | bytes 786440 | tf_op jit(solution)/shard_map/ppermute | solution.py:337
  53.3 21.4 %collective-permute-start.10 = (f32[2,128,256]{2,1,0:T(8,128)}, f32[2,128,256]{2,1,0:T(8,128)}, u32[]{:S(2)}, u32[]{:S(2)}) collective-permute-start(f32[2,128,256]{2,1,0:T(8,128)} %bitcast.23.refs_7_), channel_id=1, source_target_pairs={{0,6},{2,4},{4,2},{6,0},{8,14},{10,12},{12,10},{14,8},{1,7},{3,5},... | collective-permute-start | bytes 786440 | tf_op jit(solution)/shard_map/ppermute | solution.py:337
  62.2 7.0 %copy-start.1 = (f32[512,256]{1,0:T(8,128)S(1)}, f32[512,256]{1,0:T(8,128)}, u32[]{:S(2)}) copy-start(f32[512,256]{1,0:T(8,128)} %get-tuple-element.35.scaled_hbm) | copy-start | bytes 1572868
  62.2 7.0 %copy-start.10 = (f32[512,64]{0,1:T(8,128)S(1)}, f32[512,64]{0,1:T(8,128)}, u32[]{:S(2)}) copy-start(f32[512,64]{0,1:T(8,128)} %copy-done.9) | copy-start | bytes 393220
  62.2 38.5 %all-to-all-start = ((f32[8,136,256]{2,1,0:T(8,128)}), f32[8,136,256]{2,1,0:T(8,128)S(1)}, u32[]{:S(2)}, u32[]{:S(2)}) async-start(f32[8,136,256]{2,1,0:T(8,128)} %get-tuple-element.37), calls=%async_computation | async-start | bytes 2228224 | tf_op jit(solution)/shard_map/all_to_all | solution.py:444
  70.5 26.7 %collective-permute-start.13 = (f32[2,128,256]{2,1,0:T(8,128)S(1)}, f32[2,128,256]{2,1,0:T(8,128)S(1)}, u32[]{:S(2)}, u32[]{:S(2)}) collective-permute-start(f32[2,128,256]{2,1,0:T(8,128)S(1)} %bitcast.67), channel_id=1, source_target_pairs={{0,6},{2,4},{4,2},{6,0},{8,14},{10,12},{12,10},{14,8},{1,7},{3,5},... | collective-permute-start | bytes 786440 | tf_op jit(solution)/shard_map/ppermute | solution.py:337
  73.5 27.0 %collective-permute-start.12 = (f32[2,128,256]{2,1,0:T(8,128)S(1)}, f32[2,128,256]{2,1,0:T(8,128)S(1)}, u32[]{:S(2)}, u32[]{:S(2)}) collective-permute-start(f32[2,128,256]{2,1,0:T(8,128)S(1)} %bitcast.68), channel_id=1, source_target_pairs={{0,4},{2,6},{4,0},{6,2},{8,12},{10,14},{12,8},{14,10},{1,5},{3,7},... | collective-permute-start | bytes 786440 | tf_op jit(solution)/shard_map/ppermute | solution.py:337
  74.5 26.0 %collective-permute-start.11 = (f32[2,128,256]{2,1,0:T(8,128)S(1)}, f32[2,128,256]{2,1,0:T(8,128)S(1)}, u32[]{:S(2)}, u32[]{:S(2)}) collective-permute-start(f32[2,128,256]{2,1,0:T(8,128)S(1)} %bitcast.69), channel_id=1, source_target_pairs={{0,2},{2,0},{4,6},{6,4},{8,10},{10,8},{12,14},{14,12},{1,3},{3,1},... | collective-permute-start | bytes 786440 | tf_op jit(solution)/shard_map/ppermute | solution.py:337
  75.8 35.4 %collective-permute-start.14 = (f32[1,128,256]{2,1,0:T(8,128)S(1)}, f32[1,128,256]{2,1,0:T(8,128)S(1)}, u32[]{:S(2)}, u32[]{:S(2)}) collective-permute-start(f32[1,128,256]{2,1,0:T(8,128)S(1)} %get-tuple-element.58), channel_id=1, source_target_pairs={{0,8},{2,10},{4,12},{6,14},{8,0},{10,2},{12,4},{14,6},{1,9},{3,11}... | collective-permute-start | bytes 393224 | tf_op jit(solution)/shard_map/ppermute | solution.py:337
  100.6 10.7 %collective-permute-start.15 = (f32[1,128,256]{2,1,0:T(8,128)S(1)}, f32[1,128,256]{2,1,0:T(8,128)S(1)}, u32[]{:S(2)}, u32[]{:S(2)}) collective-permute-start(f32[1,128,256]{2,1,0:T(8,128)S(1)} %get-tuple-element.56), channel_id=1, source_target_pairs={{0,8},{2,10},{4,12},{6,14},{8,0},{10,2},{12,4},{14,6},{1,9},{3,11}... | collective-permute-start | bytes 393224 | tf_op jit(solution)/shard_map/ppermute | solution.py:337
  107.5 11.7 %all-to-all-start.1 = ((f32[16,8,256]{2,1,0:T(8,128)}), f32[16,8,256]{2,1,0:T(8,128)S(1)}, u32[]{:S(2)}, u32[]{:S(2)}) async-start(f32[16,8,256]{2,1,0:T(8,128)} %shard_map.71), calls=%async_computation.1 | async-start | bytes 262144 | tf_op jit(solution)/shard_map/all_to_all | solution.py:462
  111.3 7.9 %copy-start.24 = (f32[1,128,256]{2,1,0:T(8,128)}, f32[1,128,256]{2,1,0:T(8,128)S(1)}, u32[]{:S(2)}) copy-start(f32[1,128,256]{2,1,0:T(8,128)S(1)} %add.71) | copy-start | bytes 393220
  111.3 7.8 %copy-start.25 = (f32[1,128,256]{2,1,0:T(8,128)}, f32[1,128,256]{2,1,0:T(8,128)S(1)}, u32[]{:S(2)}) copy-start(f32[1,128,256]{2,1,0:T(8,128)S(1)} %add.72) | copy-start | bytes 393220
  111.4 1.5 %collective-permute-start.16 = (f32[128,256]{1,0:T(8,128)S(1)}, f32[128,256]{1,0:T(8,128)S(1)}, u32[]{:S(2)}, u32[]{:S(2)}) collective-permute-start(f32[128,256]{1,0:T(8,128)S(1)} %pad_maximum_fusion.12), channel_id=1, source_target_pairs={{0,1},{1,0},{2,3},{3,2},{4,5},{5,4},{6,7},{7,6},{8,9},{9,8},{10,11... | collective-permute-start | bytes 393224 | tf_op jit(solution)/shard_map/ppermute | solution.py:337
  (24 other events, 67.4 us)

commit v9 on v8

v9 whole, which is shorter than its diff:
```python
import functools
import math

import jax
import jax.numpy as jnp
from jax import lax
from jax.experimental import pallas as pl
from jax.experimental.layout import Layout, with_layout_constraint
from jax.experimental.pallas import tpu as pltpu
from jax.sharding import PartitionSpec as P

VMEM_LIMIT = 24 * 1024 * 1024
SUBLANES = 8


def split(values):
    high = values.astype(jnp.bfloat16)
    low = (values - high.astype(jnp.float32)).astype(jnp.bfloat16)
    return high, low


def dot(left, right):
    return jnp.dot(left, right, preferred_element_type=jnp.float32)


def on_diagonal(size):
    rows = lax.broadcasted_iota(jnp.int32, (size, size), 0)
    return rows == lax.broadcasted_iota(jnp.int32, (size, size), 1)


def split_tiles(kinship_ref, high_ref, low_ref):
    block_count, positions, tile = kinship_ref.shape[:3]
    diagonal_mask = on_diagonal(tile)
    for row in range(block_count):
        for position in range(positions):
            values = kinship_ref[row, position]
            if position == 0:
                values = jnp.where(diagonal_mask, 0.0, values)
            high, low = split(values)
            high_ref[row, :, pl.ds(position * tile, tile)] = high
            low_ref[row, :, pl.ds(position * tile, tile)] = low


def product(high, low, blocks):
    parts = [split(block) for block in blocks]
    blocks_high = jnp.concatenate([part[0] for part in parts], axis=0)
    blocks_low = jnp.concatenate([part[1] for part in parts], axis=0)
    return dot(high, blocks_high) + (dot(low, blocks_high) + dot(high, blocks_low))


def column_sums(values):
    rows, columns = values.shape
    return jnp.sum(values.reshape(rows // SUBLANES, SUBLANES, columns), axis=0)


class Copies:
    def __init__(self, semaphores):
        self.semaphores = semaphores
        self.count = 0

    def start(self, source, target):
        copy = pltpu.make_async_copy(source, target, self.semaphores.at[self.count])
        self.count += 1
        copy.start()
        return copy


def wait_all(copies):
    for copy in copies:
        copy.wait()


def quotient(value, divisor):
    if divisor & (divisor - 1) == 0:
        return lax.shift_right_logical(value, jnp.int32(divisor.bit_length() - 1))
    return lax.div(value, jnp.int32(divisor))


def direction_kernel(kinship_ref, variance_ref, phenotypes_ref, direction_ref, diagonal_ref, sums_ref):
    block_count, positions, tile = kinship_ref.shape[:3]
    norm = jnp.zeros((SUBLANES, direction_ref.shape[1]), jnp.float32)
    diagonal_mask = on_diagonal(tile)
    for row in range(block_count):
        block = pl.ds(row * tile, tile)
        total = jnp.where(diagonal_mask, variance_ref[row:row + 1, :], kinship_ref[row, 0])
        for position in range(1, positions):
            total = total + kinship_ref[row, position]
        diagonal = jnp.sum(total, axis=1, keepdims=True)
        diagonal_ref[block, :] = diagonal
        here = phenotypes_ref[block, :] * (1.0 / diagonal)
        direction_ref[block, :] = here
        norm = norm + column_sums(here * phenotypes_ref[block, :])
    row_ids = lax.broadcasted_iota(jnp.int32, norm.shape, 0)
    sums_ref[...] = jnp.where(row_ids == 0, jnp.sum(norm, axis=0, keepdims=True), 0.0)


def route_kernel(devices, capacity, list_ref, kinship_ref, direction_ref, table_ref, forward_ref, high_ref, low_ref,
                 *refs):
    half = devices // 2
    outgoing_refs, (first_ref, last_ref) = refs[:half - 1], refs[half - 1:]
    block_count, positions, tile = kinship_ref.shape[:3]
    split_tiles(kinship_ref, high_ref, low_ref)
    me = lax.axis_index("samples")
    partner = me ^ half
    spare = me ^ 1
    top = block_count * block_count

    def collect(device):
        for j in range(devices):
            first_ref[j] = jnp.int32(top)
            last_ref[j] = jnp.int32(-1)
        found = []
        for row in range(block_count):
            for position in range(positions - 1):
                listed = list_ref[position, device * block_count + row]
                live = listed >= 0
                safe = jnp.maximum(listed, 0)
                other = quotient(safe, block_count)
                far_block = safe - other * block_count
                key = jnp.where(device < other, row * block_count + far_block, far_block * block_count + row)
                first_ref[other] = jnp.minimum(first_ref[other], jnp.where(live, key, top))
                last_ref[other] = jnp.maximum(last_ref[other], jnp.where(live, key, -1))
                found.append((live, other, far_block, key))
        return found

    def blocks_for(device, other):
        blocks = []
        for key in (first_ref[other], last_ref[other]):
            safe = jnp.clip(key, 0, top - 1)
            lower = quotient(safe, block_count)
            higher = safe - lower * block_count
            blocks.append(jnp.where(key == safe, jnp.where(device < other, lower, higher), 0))
        return blocks

    collect(partner)
    for k in range(1, half):
        blocks = blocks_for(partner, me ^ k)
        for slot in range(capacity):
            forward_ref[slot, k] = blocks[slot]
    for entry, (live, other, far_block, key) in enumerate(collect(me)):
        first, last = first_ref[other], last_ref[other]
        handled = jnp.where(me < other, first, last)
        weight = jnp.where(first == last, 1, 2)
        slot = jnp.where(key == first, 0, capacity - 1)
        place = jnp.where(other == partner, devices * capacity + far_block, other * capacity + slot)
        table_ref[0, entry] = jnp.where(live, place, spare * capacity)
        table_ref[1, entry] = jnp.where(live, other, spare)
        table_ref[2, entry] = jnp.where(live & (key == handled), weight, 0)
    for other in range(devices):
        blocks = blocks_for(me, other)
        table_ref[3, other] = jnp.where(me < other, blocks[1], blocks[0])
    near = [blocks_for(me, me ^ k) for k in range(1, half)]
    for k in range(1, half):
        for slot in range(capacity):
            start = pl.multiple_of(near[k - 1][slot] * tile, tile)
            outgoing_refs[k - 1][slot] = direction_ref[pl.ds(start, tile), :]


def forward_kernel(forward_ref, partner_ref, *refs):
    capacity, half = forward_ref.shape
    outgoing_refs = refs[1 - half:]
    tile = outgoing_refs[0].shape[1]
    for k in range(1, half):
        for slot in range(capacity):
            start = pl.multiple_of(forward_ref[slot, k] * tile, tile)
            outgoing_refs[k - 1][slot] = partner_ref[pl.ds(start, tile), :]


def gather_received(devices, capacity, received_refs, gathered_ref):
    half = devices // 2
    me = lax.axis_index("samples")
    near_refs, far_refs, partner_ref = received_refs[:half - 1], received_refs[half - 1:-1], received_refs[-1]
    gathered_ref[pl.ds(devices * capacity, partner_ref.shape[0])] = partner_ref[...]
    for k in range(1, half):
        mate = me ^ k
        gathered_ref[pl.ds(mate * capacity, capacity)] = near_refs[k - 1][...]
        gathered_ref[pl.ds((mate ^ half) * capacity, capacity)] = far_refs[k - 1][...]


def apply_kernel(devices, capacity, table_ref, high_ref, low_ref, direction_ref, diagonal_ref, norm_ref, *refs):
    received_refs = refs[:devices - 1]
    scaled_ref, sums_ref, gathered_ref, *outgoing_refs = refs[-2 - devices:]
    gather_received(devices, capacity, received_refs, gathered_ref)
    block_count, tile, depth = high_ref.shape
    others = depth // tile - 1
    cross = jnp.zeros(sums_ref.shape, jnp.float32)
    for row in range(block_count):
        block = pl.ds(row * tile, tile)
        here = direction_ref[block, :]
        blocks = [here] + [gathered_ref[table_ref[0, row * others + i]] for i in range(others)]
        mapped = product(high_ref[row], low_ref[row], blocks)
        scaled_ref[block, :] = mapped * (1.0 / diagonal_ref[block, :])
        cross = cross + column_sums(here * mapped)
    row_ids = lax.broadcasted_iota(jnp.int32, cross.shape, 0)
    sums = jnp.where(row_ids == 1, jnp.sum(cross, axis=0, keepdims=True), norm_ref[...])
    sums_ref[...] = sums
    me = lax.axis_index("samples")
    for k in range(1, devices):
        start = pl.multiple_of(table_ref[3, me ^ k] * tile, tile)
        outgoing_refs[k - 1][pl.ds(0, tile), :] = scaled_ref[pl.ds(start, tile), :]
        outgoing_refs[k - 1][pl.ds(tile, SUBLANES), :] = sums


def curvature_kernel(devices, table_ref, high_ref, low_ref, direction_ref, diagonal_ref, scaled_ref, own_sums_ref,
                     gathered_ref, *refs):
    later_refs = refs[:devices - 1]
    sums_hbm, later_ref, sums_ref, semaphores = refs[-4:]
    block_count, tile, depth = high_ref.shape
    others = depth // tile - 1
    me = lax.axis_index("samples")
    first_sums = own_sums_ref[...]
    for k in range(1, devices):
        later_ref[me ^ k] = later_refs[k - 1][pl.ds(0, tile), :]
        first_sums = first_sums + later_refs[k - 1][pl.ds(tile, SUBLANES), :]
    rho = first_sums[1:2, :] / first_sums[0:1, :]
    norm = jnp.zeros(first_sums.shape, jnp.float32)
    bend = jnp.zeros(first_sums.shape, jnp.float32)
    for row in range(block_count):
        block = pl.ds(row * tile, tile)
        here = scaled_ref[block, :] - rho * direction_ref[block, :]
        blocks = [here]
        for i in range(others):
            entry = row * others + i
            weight = table_ref[2, entry].astype(jnp.float32)
            blocks.append(weight * (later_ref[table_ref[1, entry]] - rho * gathered_ref[table_ref[0, entry]]))
        mapped = product(high_ref[row], low_ref[row], blocks)
        norm = norm + column_sums(here * here * diagonal_ref[block, :])
        bend = bend + column_sums(here * mapped)
    row_ids = lax.broadcasted_iota(jnp.int32, first_sums.shape, 0)
    sums = jnp.where(row_ids == 2, jnp.sum(norm, axis=0, keepdims=True), first_sums)
    sums = jnp.where(row_ids == 3, jnp.sum(bend, axis=0, keepdims=True), sums)
    for i in range(2 * devices):
        sums_ref[i] = sums
    Copies(semaphores).start(sums_ref, sums_hbm).wait()


def coefficients(sums, shared):
    norm, cross = sums[0:1, :], sums[1:2, :]
    later_norm, bend = shared[2:3, :], shared[3:4, :]
    curve = norm + cross
    ratio = later_norm / curve
    step = jnp.where(later_norm > 0, later_norm / (later_norm + bend - later_norm * ratio), 0.0)
    start = norm / curve
    return start * (1.0 + step * (ratio + cross / norm)), -start * step


def finish_kernel(devices, norm_scale, direction_ref, scaled_ref, direction_scores_ref, scaled_scores_ref, swapped_ref,
                  sums_ref, solved_hbm, scores_ref, solved_ref, semaphores):
    people, columns = direction_ref.shape
    rows = scores_ref.shape[0]
    column = lax.axis_index("cols")
    copies = Copies(semaphores)

    def total(which):
        sums = sums_ref[which]
        shared = sums
        for i in range(1, devices):
            shared = shared + sums_ref[2 * i + which]
        return sums, shared

    along, across = coefficients(*total(column))
    other_along, other_across = coefficients(*total(1 - column))
    stores = []
    part_rows = people // 4
    for part in range(4):
        block = pl.ds(part * part_rows, part_rows)
        solved_ref[block, :] = along * direction_ref[block, :] + across * scaled_ref[block, :]
        stores.append(copies.start(solved_ref.at[block], solved_hbm.at[block]))
    own = pl.multiple_of(column * columns, columns)
    other = pl.multiple_of((1 - column) * columns, columns)
    here = pl.ds(0, rows)
    scores_ref[:, pl.ds(own, columns)] = norm_scale * (
        along * direction_scores_ref[here, :] + across * scaled_scores_ref[here, :]
    )
    scores_ref[:, pl.ds(other, columns)] = norm_scale * (
        other_along * swapped_ref[here, :] + other_across * swapped_ref[pl.ds(rows, rows), :]
    )
    wait_all(stores)


def call(kernel, out_shape, in_specs, out_specs, scratch_shapes=()):
    return pl.pallas_call(
        kernel,
        out_shape=out_shape,
        in_specs=in_specs,
        out_specs=out_specs,
        scratch_shapes=list(scratch_shapes),
        compiler_params=pltpu.CompilerParams(vmem_limit_bytes=VMEM_LIMIT),
    )


def swap(values, axis, devices, step):
    return lax.ppermute(values, axis, [(i, i ^ step) for i in range(devices)])


def after(value, *others):
    return lax.optimization_barrier((value, *others))[0]


def per_device(kinship, relatives, variance, phenotypes, dosage):
    devices = lax.axis_size("samples")
    block_count, positions, tile = kinship.shape[:3]
    people, columns = phenotypes.shape
    variants = dosage.shape[1]
    share_rows = variants // devices
    entries = block_count * (positions - 1)
    capacity = -(-entries // (devices - 1))
    assert capacity <= 2
    hbm = pl.BlockSpec(memory_space=pltpu.HBM)
    anywhere = pl.BlockSpec(memory_space=pl.ANY)
    vmem = pl.BlockSpec(memory_space=pltpu.VMEM)
    smem = pl.BlockSpec(memory_space=pltpu.SMEM)
    float_of = lambda *shape: jax.ShapeDtypeStruct(shape, jnp.float32)
    room = lambda *shape: pltpu.VMEM(shape, jnp.float32)
    full = float_of(people, columns)
    full_room = room(people, columns)
    half = devices // 2
    near_by = list(range(1, half))
    direction, diagonal, norm = call(
        direction_kernel,
        [full, float_of(people, 1), float_of(SUBLANES, columns)],
        [vmem] * 3,
        [vmem] * 3,
    )(kinship, variance.reshape(block_count, tile), phenotypes)
    tiles = jax.ShapeDtypeStruct((block_count, tile, positions * tile), jnp.bfloat16)
    table, forward, high, low, *outgoing = call(
        functools.partial(route_kernel, devices, capacity),
        [
            jax.ShapeDtypeStruct((4, max(entries, devices)), jnp.int32),
            jax.ShapeDtypeStruct((capacity, half), jnp.int32),
            tiles, tiles,
        ] + [float_of(capacity, tile, columns)] * (half - 1),
        [smem, vmem, vmem],
        [smem, smem] + [vmem] * (half + 1),
        [pltpu.SMEM((devices,), jnp.int32), pltpu.SMEM((devices,), jnp.int32)],
    )(relatives.T, kinship, direction)

    def to_mates(blocks):
        return [swap(block, "samples", devices, k) for k, block in zip(near_by, blocks)]

    me = lax.axis_index("samples")
    dosage = after(dosage, table)
    other_dosage = with_layout_constraint(swap(dosage, "cols", 2, 1), Layout((0, 1)))
    dosages = [values.reshape(people, devices, share_rows) for values in (dosage, other_dosage)]
    bits = half.bit_length() - 1
    even = [sum(((i >> b) & 1) << (bits - b) for b in range(bits)) for i in range(half)]
    steps = [2 << i for i in range(bits)]
    grouped = [
        jnp.concatenate([
            lax.dynamic_index_in_dim(values, me ^ k ^ odd, 1, keepdims=False)
            for k in even for values in dosages
        ], axis=1)
        for odd in range(2)
    ]

    def variant_products(values):
        return [
            lax.dot_general(
                group, values, (((0,), (0,)), ((), ())), precision=lax.Precision.HIGH,
                preferred_element_type=jnp.float32,
            ).reshape(half, 2 * share_rows, columns)
            for group in grouped
        ]

    def halved(values, step):
        count = values.shape[0] // 2
        return values[:count], swap(values[count:], "samples", devices, step)

    partner = swap(direction, "samples", devices, half)
    near = to_mates(outgoing)
    direction_even, direction_odd = variant_products(direction)
    direction_share = swap(direction_odd, "samples", devices, 1)
    far = to_mates(call(
        forward_kernel,
        [float_of(capacity, tile, columns)] * (half - 1),
        [smem, vmem] + [anywhere] * (half + 1),
        [vmem] * (half - 1),
    )(forward, partner, *near, direction_even, direction_odd))
    received = near + far + [partner.reshape(block_count, tile, columns)]
    scaled, own_sums, gathered, *outgoing = call(
        functools.partial(apply_kernel, devices, capacity),
        [full, float_of(SUBLANES, columns), float_of(devices * capacity + block_count, tile, columns)]
        + [float_of(tile + SUBLANES, columns)] * (devices - 1),
        [smem] + [vmem] * (devices + 4) + [anywhere],
        [vmem] * (devices + 2),
    )(table, high, low, direction, diagonal, norm, *received, direction_share)
    order = [k for k in range(half, devices)] + near_by
    sent = {k: swap(outgoing[k - 1], "samples", devices, k) for k in order}
    later = [sent[k] for k in range(1, devices)]
    scaled_even, scaled_odd = variant_products(scaled)
    scaled_sum = scaled_even + swap(scaled_odd, "samples", devices, 1)
    direction_sum = after(direction_even, scaled) + direction_share
    for step in steps[:-1]:
        direction_kept, direction_taken = halved(direction_sum, step)
        direction_sum = direction_kept + direction_taken
    direction_kept, direction_taken = halved(direction_sum, steps[-1])
    scaled_kept, scaled_taken = halved(scaled_sum, steps[0])
    sums = call(
        functools.partial(curvature_kernel, devices),
        float_of(2 * devices, SUBLANES, columns),
        [smem] + [vmem] * (devices + 6) + [anywhere],
        hbm,
        [room(devices, tile, columns), room(2 * devices, SUBLANES, columns), pltpu.SemaphoreType.DMA((1,))],
    )(table, high, low, direction, diagonal, scaled, own_sums, gathered, *later, scaled_sum)
    scaled_sum = after(scaled_kept, sums) + scaled_taken
    for step in steps[1:-1]:
        scaled_kept, scaled_taken = halved(scaled_sum, step)
        scaled_sum = scaled_kept + scaled_taken
    scaled_kept, scaled_taken = halved(scaled_sum, steps[-1])
    all_sums = lax.all_to_all(
        after(sums, scaled_kept), ("samples", "cols"), split_axis=0, concat_axis=0, tiled=True
    )
    direction_scores = (after(direction_kept, sums) + direction_taken)[0]
    scaled_scores = (scaled_kept + scaled_taken)[0]
    swapped = swap(jnp.concatenate([direction_scores[share_rows:], scaled_scores[share_rows:]]), "cols", 2, 1)
    solved, scores = call(
        functools.partial(finish_kernel, devices, 1.0 / math.sqrt(people * devices)),
        [full, float_of(share_rows, 2 * columns)],
        [vmem] * 6,
        [hbm, vmem],
        [full_room, pltpu.SemaphoreType.DMA((4,))],
    )(direction, scaled, direction_scores, scaled_scores, swapped, all_sums)
    return (solved, scores)


def solution(mesh):
    return jax.shard_map(
        per_device,
        mesh=mesh,
        in_specs=(
            P(("groups", "samples"), None, None, None),
            P("groups", None),
            P(("groups", "samples")),
            P(("groups", "samples"), "cols"),
            P(("groups", "samples"), "cols"),
        ),
        out_specs=(P(("groups", "samples"), "cols"), P(("groups", "cols", "samples"), None)),
        check_vma=False,
    )
```

time: 123 us -> 127 us (1.033)
  local copies, waits for them, and re-layouts: 7.42 us -> 22.3 us
  Pallas kernels: 19.9 us -> 8.23 us
  starting transfers between devices: 31.1 us -> 42 us
  waiting for transfers between devices: 56 us -> 48 us
  matrix products: 5.9 us -> 3.69 us
    unnamed x58 -> x19, local copies, waits for them, and re-layouts: 4.3 us -> 15.4 us
    ppermute x17 -> x22, starting transfers between devices: 20.4 us -> 31.2 us  [swap(): return lax.ppermute(values, axis, [(i, i ^ step) for i in range(devices)])]
    all_to_all x2 -> x1, waiting for transfers between devices: 6.34 us -> 0.01 us  [per_device(): lax.all_to_all(after(sums, scaled_kept), ('samples', 'cols'), split_axis=...]
    pallas_call x2 -> x3, Pallas kernels: 9.16 us -> 4.23 us  [the longest x1 2.21 us: per_device(): call(functools.partial(curvature_kernel, devices), float_of(2 * devices,...]
    pallas_call x1, Pallas kernels: 5.26 us -> 1.88 us  [per_device(): call(functools.partial(apply_kernel, devices, capacity), [full, float_of(...]
    another operation x0 -> x1, local copies, waits for them, and re-layouts: none -> 2.55 us  [per_device(): with_layout_constraint(swap(dosage, 'cols', 2, 1), Layout((0, 1)))]
    dot_general x8 -> x4, matrix products: 5.9 us -> 3.69 us  [variant_products(): lax.dot_general(group, values, (((0,), (0,)), ((), ())), precision=lax.Pr...]
    pallas_call x1, Pallas kernels: 2.71 us -> 0.61 us  [per_device(): call(forward_kernel, [float_of(capacity, tile, columns)] * (half - 1), [s...]
  transfers between devices with their start and end apart: 19 -> 23, of which waited for: 8 -> 7; matrix products, arithmetic and copies ran while one was open for 7% -> 18% of each run, Pallas kernels for 8% -> 2%
where the time goes in v9:
time: 127 us; the launch traced here: 126 us
  waiting for transfers between devices  48 us (38%)
  starting transfers between devices  42 us (33%)
  local copies, waits for them, and re-layouts  22.3 us (18%)
  Pallas kernels  8.23 us (6%)
  matrix products  3.69 us (3%)
    ppermute x22, waiting for transfers between devices, swap(): return lax.ppermute(values, axis, [(i, i ^ step) for i in range(devices)])  48 us
    ppermute x22, starting transfers between devices, swap(): return lax.ppermute(values, axis, [(i, i ^ step) for i in range(devices)])  31.2 us
    unnamed x19, local copies, waits for them, and re-layouts  15.4 us
    all_to_all x1, starting transfers between devices, per_device(): lax.all_to_all(after(sums, scaled_kept), ('samples', 'cols'), split_axis=...  10.8 us
    dot_general x4, matrix products, variant_products(): lax.dot_general(group, values, (((0,), (0,)), ((), ())), precision=lax.Pr...  3.69 us
    another operation x1, local copies, waits for them, and re-layouts, per_device(): with_layout_constraint(swap(dosage, 'cols', 2, 1), Layout((0, 1)))  2.55 us
  transfers between devices with their start and end apart: 23, of which 7 were waited for; matrix products, arithmetic and copies ran while one was open for 18% of the time, Pallas kernels for 2%

profile of v9, /device:TPU:0, one launch (start us, length us, event | category | flops | bytes accessed | tf_op | source)
XLA Modules:
  0.0 126.3 jit_solution(12165871541902240996)
XLA Ops:
  4.4 1.9 %shard_map.69 = (s32[4,12]{1,0:T(4,128)S(1)}, s32[2,4]{1,0:T(2,128)S(1)}, bf16[4,128,512]{2,1,0:T(8,128)(2,1)S(1)}, bf16[4,128,512]{2,1,0:T(8,128)(2,1)S(1)}, f3...) custom-call(s32[3,32]{1,0:T(4,128)S(1)} %bitcast.63, f32[4,4,128,128]{3,2,1,0:T(8,128)S(1)} %copy-done, ...), custom_call_target="tpu_custom_call" | custom-call | tf_op jit(solution)/shard_map/pallas_call | solution.py:326
  6.8 3.7 %collective-permute-start.3 = (f32[512,256]{1,0:T(8,128)S(1)}, f32[512,256]{1,0:T(8,128)S(1)}, u32[]{:S(2)}, u32[]{:S(2)}) collective-permute-start(f32[512,256]{1,0:T(8,128)S(1)} %get-tuple-element.30.direction_ref), channel_id=1, source_target_pairs={{0,8},{2,10},{4,12},{6,14},{8,0},{10,2},{12,4},{14,6},{1,9},{3,11}... | collective-permute-start | bytes 1572872 | tf_op jit(solution)/shard_map/ppermute | solution.py:293
  14.0 2.5 %copy.7 = f32[512,512]{0,1:T(8,128)} copy(f32[512,512]{1,0:T(8,128)} %param.9) | data formatting | bytes 2097152 | tf_op jit(solution)/shard_map/optimization_barrier | solution.py:297
  16.5 1.7 %bitcast_dynamic-update-slice_fusion.7 = (f32[512,512]{0,1:T(8,128)}, f32[512,512]{0,1:T(8,128)}) fusion(f32[512,8,64]{0,2,1:T(8,128)} %bitcast.64, s32[]{:T(128)S(6)} %select_n.37, s32[]{:T(128)S(6)} %select_n.33), kind=kLoop, calls=%fused_computation.9 | loop fusion | bytes 524296
  18.2 2.6 %copy.8 = f32[512,512]{0,1:T(8,128)} copy(f32[512,512]{1,0:T(8,128)} %collective-permute-done.4) | data formatting | bytes 2097152 | tf_op jit(solution)/shard_map/layout_constraint | solution.py:343
  20.7 1.7 %bitcast_dynamic-update-slice_fusion.6 = (f32[512,512]{0,1:T(8,128)}, f32[512,512]{0,1:T(8,128)}) fusion(f32[512,512]{0,1:T(8,128)} %get-tuple-element.72, f32[512,8,64]{0,2,1:T(8,128)} %bitcast.68, s32[]{:T(128)S(6)} %select_n.37, f32[512,512]{0,1:T(8,128)} %get-tuple-element.73, s32[]{:T(128)S(6)} %select_n.33), kind=kLoop, calls=%fused_computation.8 | loop fusion | bytes 524296
  22.4 1.7 %bitcast_dynamic-update-slice_fusion.5 = (f32[512,512]{0,1:T(8,128)}, f32[512,512]{0,1:T(8,128)}) fusion(f32[512,512]{0,1:T(8,128)} %get-tuple-element.70, f32[512,8,64]{0,2,1:T(8,128)} %bitcast.65, s32[]{:T(128)S(6)} %select_n.38, f32[512,512]{0,1:T(8,128)} %get-tuple-element.71, s32[]{:T(128)S(6)} %select_n.34), kind=kLoop, calls=%fused_computation.7 | loop fusion | bytes 524296
  24.1 1.7 %bitcast_dynamic-update-slice_fusion.4 = (f32[512,512]{0,1:T(8,128)}, f32[512,512]{0,1:T(8,128)}) fusion(f32[512,512]{0,1:T(8,128)} %get-tuple-element.68, f32[512,8,64]{0,2,1:T(8,128)} %bitcast.69, s32[]{:T(128)S(6)} %select_n.38, f32[512,512]{0,1:T(8,128)} %get-tuple-element.69, s32[]{:T(128)S(6)} %select_n.34), kind=kLoop, calls=%fused_computation.6 | loop fusion | bytes 524296
  25.8 1.7 %bitcast_dynamic-update-slice_fusion.3 = (f32[512,512]{0,1:T(8,128)}, f32[512,512]{0,1:T(8,128)}) fusion(f32[512,512]{0,1:T(8,128)} %get-tuple-element.66, f32[512,8,64]{0,2,1:T(8,128)} %bitcast.66, s32[]{:T(128)S(6)} %select_n.39, f32[512,512]{0,1:T(8,128)} %get-tuple-element.67, s32[]{:T(128)S(6)} %select_n.35), kind=kLoop, calls=%fused_computation.5 | loop fusion | bytes 524296
  27.5 1.7 %bitcast_dynamic-update-slice_fusion.2 = (f32[512,512]{0,1:T(8,128)}, f32[512,512]{0,1:T(8,128)}) fusion(f32[512,512]{0,1:T(8,128)} %get-tuple-element.64, f32[512,8,64]{0,2,1:T(8,128)} %bitcast.70, s32[]{:T(128)S(6)} %select_n.39, f32[512,512]{0,1:T(8,128)} %get-tuple-element.65, s32[]{:T(128)S(6)} %select_n.35), kind=kLoop, calls=%fused_computation.4 | loop fusion | bytes 524296
  29.2 1.7 %bitcast_dynamic-update-slice_fusion.1 = (f32[512,512]{0,1:T(8,128)}, f32[512,512]{0,1:T(8,128)}) fusion(f32[512,512]{0,1:T(8,128)} %get-tuple-element.62, f32[512,8,64]{0,2,1:T(8,128)} %bitcast.67, s32[]{:T(128)S(6)} %select_n.40, f32[512,512]{0,1:T(8,128)} %get-tuple-element.63, s32[]{:T(128)S(6)} %select_n.36), kind=kLoop, calls=%fused_computation.3 | loop fusion | bytes 524296
  30.9 1.7 %bitcast_dynamic-update-slice_fusion = (f32[512,512]{0,1:T(8,128)}, f32[512,512]{0,1:T(8,128)}) fusion(f32[512,512]{0,1:T(8,128)} %get-tuple-element.60, f32[512,8,64]{0,2,1:T(8,128)} %bitcast.71, s32[]{:T(128)S(6)} %select_n.40, f32[512,512]{0,1:T(8,128)} %get-tuple-element.61, s32[]{:T(128)S(6)} %select_n.36), kind=kLoop, calls=%fused_computation.2 | loop fusion | bytes 524296 | tf_op jit(solution)/shard_map/concatenate | solution.py:349
  32.6 1.9 %fusion.3 = f32[512,256]{1,0:T(8,128)S(1)} fusion(f32[512,512]{0,1:T(8,128)} %get-tuple-element.58, f32[512,256]{1,0:T(8,128)S(1)} %get-tuple-element.30.direction_ref), kind=kOutput, calls=%fused_computation.24 | convolution fusion | flops 402653184 | bytes 2097152 | tf_op jit(solution)/shard_map/dot_general | solution.py:358
  40.9 18.0 %collective-permute-done.5.refs_3_ = f32[2,128,256]{2,1,0:T(8,128)S(1)} collective-permute-done((f32[2,128,256]{2,1,0:T(8,128)S(1)}, f32[2,128,256]{2,1,0:T(8,128)S(1)}, u32[]{:S(2)}, u32[]{:S(2)}) %collective-permute-start.5) | collective-permute-done | bytes 262176 | tf_op jit(solution)/shard_map/ppermute | solution.py:293
  59.0 1.9 %shard_map.71 = (f32[512,256]{1,0:T(8,128)S(1)}, f32[8,256]{1,0:T(8,128)S(1)}, f32[20,128,256]{2,1,0:T(8,128)S(1)}, f32[136,256]{1,0:T(8,128)S(1)}, f32[136,256]...) custom-call(s32[4,12]{1,0:T(4,128)S(1)} %get-tuple-element.31.table_, ...), custom_call_target="tpu_custom_call" | custom-call | tf_op jit(solution)/shard_map/pallas_call | solution.py:380
  66.6 1.6 %collective-permute-start.9 = (f32[2,128,256]{2,1,0:T(8,128)S(1)}, f32[2,128,256]{2,1,0:T(8,128)S(1)}, u32[]{:S(2)}, u32[]{:S(2)}) collective-permute-start(f32[2,128,256]{2,1,0:T(8,128)S(1)} %slice.49), channel_id=1, source_target_pairs={{0,4},{2,6},{4,0},{6,2},{8,12},{10,14},{12,8},{14,10},{1,5},{3,7},... | collective-permute-start | bytes 786440 | tf_op jit(solution)/shard_map/ppermute | solution.py:293
  68.9 7.5 %collective-permute-done.9 = f32[2,128,256]{2,1,0:T(8,128)S(1)} collective-permute-done((f32[2,128,256]{2,1,0:T(8,128)S(1)}, f32[2,128,256]{2,1,0:T(8,128)S(1)}, u32[]{:S(2)}, u32[]{:S(2)}) %collective-permute-start.9) | collective-permute-done | bytes 262176 | tf_op jit(solution)/shard_map/ppermute | solution.py:293
  79.7 3.6 %collective-permute-start.15 = (f32[136,256]{1,0:T(8,128)S(1)}, f32[136,256]{1,0:T(8,128)S(1)}, u32[]{:S(2)}, u32[]{:S(2)}) collective-permute-start(f32[136,256]{1,0:T(8,128)S(1)} %get-tuple-element.53), channel_id=1, source_target_pairs={{0,12},{2,14},{4,8},{6,10},{8,4},{10,6},{12,0},{14,2},{1,13},{3,15... | collective-permute-start | bytes 417800 | tf_op jit(solution)/shard_map/ppermute | solution.py:293
  85.8 7.7 %collective-permute-done.13.refs_3_ = f32[136,256]{1,0:T(8,128)S(1)} collective-permute-done((f32[136,256]{1,0:T(8,128)S(1)}, f32[136,256]{1,0:T(8,128)S(1)}, u32[]{:S(2)}, u32[]{:S(2)}) %collective-permute-start.13) | collective-permute-done | bytes 139296 | tf_op jit(solution)/shard_map/ppermute | solution.py:293
  93.5 4.3 %collective-permute-done.14.refs_4_ = f32[136,256]{1,0:T(8,128)S(1)} collective-permute-done((f32[136,256]{1,0:T(8,128)S(1)}, f32[136,256]{1,0:T(8,128)S(1)}, u32[]{:S(2)}, u32[]{:S(2)}) %collective-permute-start.14) | collective-permute-done | bytes 139296 | tf_op jit(solution)/shard_map/ppermute | solution.py:293
  97.9 2.2 %shard_map.72 = f32[16,8,256]{2,1,0:T(8,128)} custom-call(s32[4,12]{1,0:T(4,128)S(1)} %get-tuple-element.31.table_ref, bf16[4,128,512]{2,1,0:T(8,128)(2,1)S(1)} %get-tuple-element.32.high_ref, bf16[4,128,512]{2,1,0:T(8,128)(2,1)S(1)} %get-tuple-element.33.low_ref, f32[512,256]{1,0:T(8,128)S(1)} %get-tuple-element.30.direction_ref, ...), custom_call_target="tpu_custom_call" | custom-call | tf_op jit(solution)/shard_map/pallas_call | solution.py:398
  100.1 10.8 %all-to-all-start = ((f32[16,8,256]{2,1,0:T(8,128)}), f32[16,8,256]{2,1,0:T(8,128)S(1)}, u32[]{:S(2)}, u32[]{:S(2)}) async-start(f32[16,8,256]{2,1,0:T(8,128)} %shard_map.72), calls=%async_computation | async-start | bytes 262144 | tf_op jit(solution)/shard_map/all_to_all | solution.py:410
  111.9 2.9 %collective-permute-start.20 = (f32[1,128,256]{2,1,0:T(8,128)S(1)}, f32[1,128,256]{2,1,0:T(8,128)S(1)}, u32[]{:S(2)}, u32[]{:S(2)}) collective-permute-start(f32[1,128,256]{2,1,0:T(8,128)S(1)} %slice.55), channel_id=1, source_target_pairs={{0,8},{2,10},{4,12},{6,14},{8,0},{10,2},{12,4},{14,6},{1,9},{3,11}... | collective-permute-start | bytes 393224 | tf_op jit(solution)/shard_map/ppermute | solution.py:293
  114.8 8.5 %collective-permute-done.20 = f32[1,128,256]{2,1,0:T(8,128)S(1)} collective-permute-done((f32[1,128,256]{2,1,0:T(8,128)S(1)}, f32[1,128,256]{2,1,0:T(8,128)S(1)}, u32[]{:S(2)}, u32[]{:S(2)}) %collective-permute-start.20) | collective-permute-done | bytes 131104 | tf_op jit(solution)/shard_map/ppermute | solution.py:293
  (67 shorter events, 30.4 us)
Async XLA Ops:
  6.3 11.9 %collective-permute-start.4 = (f32[512,512]{1,0:T(8,128)}, f32[512,512]{1,0:T(8,128)}, u32[]{:S(2)}, u32[]{:S(2)}) collective-permute-start(f32[512,512]{1,0:T(8,128)} %param.9), channel_id=1, source_target_pairs={{0,1},{1,0},{2,3},{3,2},{4,5},{5,4},{6,7},{7,6},{8,9},{9,8},{10,11... | collective-permute-start | bytes 3145736 | tf_op jit(solution)/shard_map/ppermute | solution.py:293
  6.8 29.9 %collective-permute-start.3 = (f32[512,256]{1,0:T(8,128)S(1)}, f32[512,256]{1,0:T(8,128)S(1)}, u32[]{:S(2)}, u32[]{:S(2)}) collective-permute-start(f32[512,256]{1,0:T(8,128)S(1)} %get-tuple-element.30.direction_ref), channel_id=1, source_target_pairs={{0,8},{2,10},{4,12},{6,14},{8,0},{10,2},{12,4},{14,6},{1,9},{3,11}... | collective-permute-start | bytes 1572872 | tf_op jit(solution)/shard_map/ppermute | solution.py:293
  10.5 26.2 %collective-permute-start = (f32[2,128,256]{2,1,0:T(8,128)}, f32[2,128,256]{2,1,0:T(8,128)S(1)}, u32[]{:S(2)}, u32[]{:S(2)}) collective-permute-start(f32[2,128,256]{2,1,0:T(8,128)} %get-tuple-element.36), channel_id=1, source_target_pairs={{0,2},{2,0},{4,6},{6,4},{8,10},{10,8},{12,14},{14,12},{1,3},{3,1},... | collective-permute-start | bytes 786440 | tf_op jit(solution)/shard_map/ppermute | solution.py:293
  12.0 24.7 %collective-permute-start.1 = (f32[2,128,256]{2,1,0:T(8,128)}, f32[2,128,256]{2,1,0:T(8,128)S(1)}, u32[]{:S(2)}, u32[]{:S(2)}) collective-permute-start(f32[2,128,256]{2,1,0:T(8,128)} %get-tuple-element.37), channel_id=1, source_target_pairs={{0,4},{2,6},{4,0},{6,2},{8,12},{10,14},{12,8},{14,10},{1,5},{3,7},... | collective-permute-start | bytes 786440 | tf_op jit(solution)/shard_map/ppermute | solution.py:293
  13.6 23.1 %collective-permute-start.2 = (f32[2,128,256]{2,1,0:T(8,128)}, f32[2,128,256]{2,1,0:T(8,128)}, u32[]{:S(2)}, u32[]{:S(2)}) collective-permute-start(f32[2,128,256]{2,1,0:T(8,128)} %get-tuple-element.38), channel_id=1, source_target_pairs={{0,6},{2,4},{4,2},{6,0},{8,14},{10,12},{12,10},{14,8},{1,7},{3,5},... | collective-permute-start | bytes 786440 | tf_op jit(solution)/shard_map/ppermute | solution.py:293
  34.5 24.5 %collective-permute-start.8 = (f32[4,128,256]{2,1,0:T(8,128)S(1)}, f32[4,128,256]{2,1,0:T(8,128)S(1)}, u32[]{:S(2)}, u32[]{:S(2)}) collective-permute-start(f32[4,128,256]{2,1,0:T(8,128)S(1)} %bitcast.57), channel_id=1, source_target_pairs={{0,2},{2,0},{4,6},{6,4},{8,10},{10,8},{12,14},{14,12},{1,3},{3,1},... | collective-permute-start | bytes 1572872 | tf_op jit(solution)/shard_map/ppermute | solution.py:293
  37.3 23.5 %copy-start.4 = (f32[512,512]{0,1:T(8,128)S(1)}, f32[512,512]{0,1:T(8,128)}, u32[]{:S(2)}) copy-start(f32[512,512]{0,1:T(8,128)} %get-tuple-element.58) | copy-start | bytes 3145732
  37.4 21.6 %collective-permute-start.5 = (f32[2,128,256]{2,1,0:T(8,128)S(1)}, f32[2,128,256]{2,1,0:T(8,128)S(1)}, u32[]{:S(2)}, u32[]{:S(2)}) collective-permute-start(f32[2,128,256]{2,1,0:T(8,128)S(1)} %get-tuple-element.41), channel_id=1, source_target_pairs={{0,2},{2,0},{4,6},{6,4},{8,10},{10,8},{12,14},{14,12},{1,3},{3,1},... | collective-permute-start | bytes 786440 | tf_op jit(solution)/shard_map/ppermute | solution.py:293
  38.2 20.7 %collective-permute-start.6 = (f32[2,128,256]{2,1,0:T(8,128)S(1)}, f32[2,128,256]{2,1,0:T(8,128)S(1)}, u32[]{:S(2)}, u32[]{:S(2)}) collective-permute-start(f32[2,128,256]{2,1,0:T(8,128)S(1)} %get-tuple-element.42), channel_id=1, source_target_pairs={{0,4},{2,6},{4,0},{6,2},{8,12},{10,14},{12,8},{14,10},{1,5},{3,7},... | collective-permute-start | bytes 786440 | tf_op jit(solution)/shard_map/ppermute | solution.py:293
  39.5 19.5 %collective-permute-start.7 = (f32[2,128,256]{2,1,0:T(8,128)S(1)}, f32[2,128,256]{2,1,0:T(8,128)S(1)}, u32[]{:S(2)}, u32[]{:S(2)}) collective-permute-start(f32[2,128,256]{2,1,0:T(8,128)S(1)} %get-tuple-element.43), channel_id=1, source_target_pairs={{0,6},{2,4},{4,2},{6,0},{8,14},{10,12},{12,10},{14,8},{1,7},{3,5},... | collective-permute-start | bytes 786440 | tf_op jit(solution)/shard_map/ppermute | solution.py:293
  61.5 16.8 %collective-permute-start.17 = (f32[4,128,256]{2,1,0:T(8,128)S(1)}, f32[4,128,256]{2,1,0:T(8,128)S(1)}, u32[]{:S(2)}, u32[]{:S(2)}) collective-permute-start(f32[4,128,256]{2,1,0:T(8,128)S(1)} %bitcast.73), channel_id=1, source_target_pairs={{0,2},{2,0},{4,6},{6,4},{8,10},{10,8},{12,14},{14,12},{1,3},{3,1},... | collective-permute-start | bytes 1572872 | tf_op jit(solution)/shard_map/ppermute | solution.py:293
  63.0 16.7 %collective-permute-start.10 = (f32[136,256]{1,0:T(8,128)S(1)}, f32[136,256]{1,0:T(8,128)S(1)}, u32[]{:S(2)}, u32[]{:S(2)}) collective-permute-start(f32[136,256]{1,0:T(8,128)S(1)} %get-tuple-element.48), channel_id=1, source_target_pairs={{0,2},{2,0},{4,6},{6,4},{8,10},{10,8},{12,14},{14,12},{1,3},{3,1},... | collective-permute-start | bytes 417800 | tf_op jit(solution)/shard_map/ppermute | solution.py:293
  63.5 19.8 %collective-permute-start.11 = (f32[136,256]{1,0:T(8,128)S(1)}, f32[136,256]{1,0:T(8,128)S(1)}, u32[]{:S(2)}, u32[]{:S(2)}) collective-permute-start(f32[136,256]{1,0:T(8,128)S(1)} %get-tuple-element.49), channel_id=1, source_target_pairs={{0,4},{2,6},{4,0},{6,2},{8,12},{10,14},{12,8},{14,10},{1,5},{3,7},... | collective-permute-start | bytes 417800 | tf_op jit(solution)/shard_map/ppermute | solution.py:293
  65.1 19.4 %collective-permute-start.12 = (f32[136,256]{1,0:T(8,128)S(1)}, f32[136,256]{1,0:T(8,128)S(1)}, u32[]{:S(2)}, u32[]{:S(2)}) collective-permute-start(f32[136,256]{1,0:T(8,128)S(1)} %get-tuple-element.50), channel_id=1, source_target_pairs={{0,6},{2,4},{4,2},{6,0},{8,14},{10,12},{12,10},{14,8},{1,7},{3,5},... | collective-permute-start | bytes 417800 | tf_op jit(solution)/shard_map/ppermute | solution.py:293
  66.6 9.7 %collective-permute-start.9 = (f32[2,128,256]{2,1,0:T(8,128)S(1)}, f32[2,128,256]{2,1,0:T(8,128)S(1)}, u32[]{:S(2)}, u32[]{:S(2)}) collective-permute-start(f32[2,128,256]{2,1,0:T(8,128)S(1)} %slice.49), channel_id=1, source_target_pairs={{0,4},{2,6},{4,0},{6,2},{8,12},{10,14},{12,8},{14,10},{1,5},{3,7},... | collective-permute-start | bytes 786440 | tf_op jit(solution)/shard_map/ppermute | solution.py:293
  76.3 17.2 %collective-permute-start.13 = (f32[136,256]{1,0:T(8,128)S(1)}, f32[136,256]{1,0:T(8,128)S(1)}, u32[]{:S(2)}, u32[]{:S(2)}) collective-permute-start(f32[136,256]{1,0:T(8,128)S(1)} %get-tuple-element.51), channel_id=1, source_target_pairs={{0,8},{2,10},{4,12},{6,14},{8,0},{10,2},{12,4},{14,6},{1,9},{3,11}... | collective-permute-start | bytes 417800 | tf_op jit(solution)/shard_map/ppermute | solution.py:293
  78.2 19.6 %collective-permute-start.14 = (f32[136,256]{1,0:T(8,128)S(1)}, f32[136,256]{1,0:T(8,128)S(1)}, u32[]{:S(2)}, u32[]{:S(2)}) collective-permute-start(f32[136,256]{1,0:T(8,128)S(1)} %get-tuple-element.52), channel_id=1, source_target_pairs={{0,10},{2,8},{4,14},{6,12},{8,2},{10,0},{12,6},{14,4},{1,11},{3,9}... | collective-permute-start | bytes 417800 | tf_op jit(solution)/shard_map/ppermute | solution.py:293
  79.7 18.1 %collective-permute-start.15 = (f32[136,256]{1,0:T(8,128)S(1)}, f32[136,256]{1,0:T(8,128)S(1)}, u32[]{:S(2)}, u32[]{:S(2)}) collective-permute-start(f32[136,256]{1,0:T(8,128)S(1)} %get-tuple-element.53), channel_id=1, source_target_pairs={{0,12},{2,14},{4,8},{6,10},{8,4},{10,6},{12,0},{14,2},{1,13},{3,15... | collective-permute-start | bytes 417800 | tf_op jit(solution)/shard_map/ppermute | solution.py:293
  83.3 14.5 %collective-permute-start.16 = (f32[136,256]{1,0:T(8,128)S(1)}, f32[136,256]{1,0:T(8,128)S(1)}, u32[]{:S(2)}, u32[]{:S(2)}) collective-permute-start(f32[136,256]{1,0:T(8,128)S(1)} %get-tuple-element.54), channel_id=1, source_target_pairs={{0,14},{2,12},{4,10},{6,8},{8,6},{10,4},{12,2},{14,0},{1,15},{3,13... | collective-permute-start | bytes 417800 | tf_op jit(solution)/shard_map/ppermute | solution.py:293
  84.5 26.4 %collective-permute-start.19 = (f32[2,128,256]{2,1,0:T(8,128)S(1)}, f32[2,128,256]{2,1,0:T(8,128)}, u32[]{:S(2)}, u32[]{:S(2)}) collective-permute-start(f32[2,128,256]{2,1,0:T(8,128)S(1)} %get-tuple-element.74), channel_id=1, source_target_pairs={{0,4},{2,6},{4,0},{6,2},{8,12},{10,14},{12,8},{14,10},{1,5},{3,7},... | collective-permute-start | bytes 786440 | tf_op jit(solution)/shard_map/ppermute | solution.py:293
  93.5 17.4 %collective-permute-start.18 = (f32[1,128,256]{2,1,0:T(8,128)S(1)}, f32[1,128,256]{2,1,0:T(8,128)S(1)}, u32[]{:S(2)}, u32[]{:S(2)}) collective-permute-start(f32[1,128,256]{2,1,0:T(8,128)S(1)} %get-tuple-element.76), channel_id=1, source_target_pairs={{0,8},{2,10},{4,12},{6,14},{8,0},{10,2},{12,4},{14,6},{1,9},{3,11}... | collective-permute-start | bytes 393224 | tf_op jit(solution)/shard_map/ppermute | solution.py:293
  100.1 23.4 %all-to-all-start = ((f32[16,8,256]{2,1,0:T(8,128)}), f32[16,8,256]{2,1,0:T(8,128)S(1)}, u32[]{:S(2)}, u32[]{:S(2)}) async-start(f32[16,8,256]{2,1,0:T(8,128)} %shard_map.72), calls=%async_computation | async-start | bytes 262144 | tf_op jit(solution)/shard_map/all_to_all | solution.py:410
  111.9 11.4 %collective-permute-start.20 = (f32[1,128,256]{2,1,0:T(8,128)S(1)}, f32[1,128,256]{2,1,0:T(8,128)S(1)}, u32[]{:S(2)}, u32[]{:S(2)}) collective-permute-start(f32[1,128,256]{2,1,0:T(8,128)S(1)} %slice.55), channel_id=1, source_target_pairs={{0,8},{2,10},{4,12},{6,14},{8,0},{10,2},{12,4},{14,6},{1,9},{3,11}... | collective-permute-start | bytes 393224 | tf_op jit(solution)/shard_map/ppermute | solution.py:293
  123.4 1.4 %collective-permute-start.21 = (f32[128,256]{1,0:T(8,128)S(1)}, f32[128,256]{1,0:T(8,128)S(1)}, u32[]{:S(2)}, u32[]{:S(2)}) collective-permute-start(f32[128,256]{1,0:T(8,128)S(1)} %pad_maximum_fusion), channel_id=1, source_target_pairs={{0,1},{1,0},{2,3},{3,2},{4,5},{5,4},{6,7},{7,6},{8,9},{9,8},{10,11... | collective-permute-start | bytes 393224 | tf_op jit(solution)/shard_map/ppermute | solution.py:293
  (5 other events, 7.1 us)

commit v10 on v9

--- a/solution.py
+++ b/solution.py
@@ -10,6 +10,7 @@
 from jax.sharding import PartitionSpec as P
 
 VMEM_LIMIT = 24 * 1024 * 1024
+LARGE_VMEM = 56 * 1024 * 1024
 SUBLANES = 8
 
 
@@ -94,8 +95,8 @@
     sums_ref[...] = jnp.where(row_ids == 0, jnp.sum(norm, axis=0, keepdims=True), 0.0)
 
 
-def route_kernel(devices, capacity, list_ref, kinship_ref, direction_ref, table_ref, forward_ref, high_ref, low_ref,
-                 *refs):
+def route_kernel(devices, capacity, list_ref, kinship_ref, direction_ref, gate_ref, table_ref, forward_ref, high_ref,
+                 low_ref, *refs):
     half = devices // 2
     outgoing_refs, (first_ref, last_ref) = refs[:half - 1], refs[half - 1:]
     block_count, positions, tile = kinship_ref.shape[:3]
@@ -179,7 +180,7 @@
 
 def apply_kernel(devices, capacity, table_ref, high_ref, low_ref, direction_ref, diagonal_ref, norm_ref, *refs):
     received_refs = refs[:devices - 1]
-    scaled_ref, sums_ref, gathered_ref, *outgoing_refs = refs[-2 - devices:]
+    scaled_ref, sums_ref, gathered_ref, outgoing_ref = refs[-4:]
     gather_received(devices, capacity, received_refs, gathered_ref)
     block_count, tile, depth = high_ref.shape
     others = depth // tile - 1
@@ -194,24 +195,20 @@
     row_ids = lax.broadcasted_iota(jnp.int32, cross.shape, 0)
     sums = jnp.where(row_ids == 1, jnp.sum(cross, axis=0, keepdims=True), norm_ref[...])
     sums_ref[...] = sums
-    me = lax.axis_index("samples")
-    for k in range(1, devices):
-        start = pl.multiple_of(table_ref[3, me ^ k] * tile, tile)
-        outgoing_refs[k - 1][pl.ds(0, tile), :] = scaled_ref[pl.ds(start, tile), :]
-        outgoing_refs[k - 1][pl.ds(tile, SUBLANES), :] = sums
-
-
-def curvature_kernel(devices, table_ref, high_ref, low_ref, direction_ref, diagonal_ref, scaled_ref, own_sums_ref,
-                     gathered_ref, *refs):
-    later_refs = refs[:devices - 1]
-    sums_hbm, later_ref, sums_ref, semaphores = refs[-4:]
+    for other in range(devices):
+        start = pl.multiple_of(table_ref[3, other] * tile, tile)
+        outgoing_ref[other, pl.ds(0, tile), :] = scaled_ref[pl.ds(start, tile), :]
+        outgoing_ref[other, pl.ds(tile, SUBLANES), :] = sums
+
+
+def curvature_kernel(devices, table_ref, high_ref, low_ref, direction_ref, diagonal_ref, scaled_ref, gathered_ref,
+                     later_ref, *refs):
+    sums_ref = refs[-1]
     block_count, tile, depth = high_ref.shape
     others = depth // tile - 1
-    me = lax.axis_index("samples")
-    first_sums = own_sums_ref[...]
-    for k in range(1, devices):
-        later_ref[me ^ k] = later_refs[k - 1][pl.ds(0, tile), :]
-        first_sums = first_sums + later_refs[k - 1][pl.ds(tile, SUBLANES), :]
+    first_sums = later_ref[0, pl.ds(tile, SUBLANES), :]
+    for other in range(1, devices):
+        first_sums = first_sums + later_ref[other, pl.ds(tile, SUBLANES), :]
     rho = first_sums[1:2, :] / first_sums[0:1, :]
     norm = jnp.zeros(first_sums.shape, jnp.float32)
     bend = jnp.zeros(first_sums.shape, jnp.float32)
@@ -222,16 +219,44 @@
         for i in range(others):
             entry = row * others + i
             weight = table_ref[2, entry].astype(jnp.float32)
-            blocks.append(weight * (later_ref[table_ref[1, entry]] - rho * gathered_ref[table_ref[0, entry]]))
+            there = later_ref[table_ref[1, entry], pl.ds(0, tile), :]
+            blocks.append(weight * (there - rho * gathered_ref[table_ref[0, entry]]))
         mapped = product(high_ref[row], low_ref[row], blocks)
         norm = norm + column_sums(here * here * diagonal_ref[block, :])
         bend = bend + column_sums(here * mapped)
     row_ids = lax.broadcasted_iota(jnp.int32, first_sums.shape, 0)
     sums = jnp.where(row_ids == 2, jnp.sum(norm, axis=0, keepdims=True), first_sums)
-    sums = jnp.where(row_ids == 3, jnp.sum(bend, axis=0, keepdims=True), sums)
-    for i in range(2 * devices):
-        sums_ref[i] = sums
-    Copies(semaphores).start(sums_ref, sums_hbm).wait()
+    sums_ref[...] = jnp.where(row_ids == 3, jnp.sum(bend, axis=0, keepdims=True), sums)
+
+
+def add_kernel(sums_ref, kept_ref, taken_ref, all_sums_ref, near_ref, far_ref):
+    count = near_ref.shape[0]
+    near_ref[...] = kept_ref[pl.ds(0, count)] + taken_ref[pl.ds(0, count)]
+    far_ref[...] = kept_ref[pl.ds(count, count)] + taken_ref[pl.ds(count, count)]
+    for i in range(all_sums_ref.shape[0]):
+        all_sums_ref[i] = sums_ref[...]
+
+
+def group_kernel(order, own_ref, other_ref, high_ref, low_ref):
+    rows = own_ref.shape[0] // (2 * len(order))
+    me = lax.axis_index("samples")
+    for odd in range(2):
+        for i, distance in enumerate(order):
+            start = pl.multiple_of((me ^ distance ^ odd) * rows, rows)
+            for j, dosage_ref in enumerate((own_ref, other_ref)):
+                high, low = split(dosage_ref[pl.ds(start, rows), :])
+                here = pl.ds((2 * i + j) * rows, rows)
+                high_ref[odd, here, :] = high
+                low_ref[odd, here, :] = low
+
+
+def score_kernel(high_ref, low_ref, values_ref, even_ref, odd_ref):
+    count, rows = even_ref.shape[:2]
+    for odd, out_ref in enumerate((even_ref, odd_ref)):
+        for i in range(0, count, 4):
+            here = pl.ds(i * rows, 4 * rows)
+            total = product(high_ref[odd, here, :], low_ref[odd, here, :], [values_ref[...]])
+            out_ref[pl.ds(i, 4)] = total.reshape(4, rows, -1)
 
 
 def coefficients(sums, shared):
@@ -278,14 +303,14 @@
     wait_all(stores)
 
 
-def call(kernel, out_shape, in_specs, out_specs, scratch_shapes=()):
+def call(kernel, out_shape, in_specs, out_specs, scratch_shapes=(), limit=VMEM_LIMIT):
     return pl.pallas_call(
         kernel,
         out_shape=out_shape,
         in_specs=in_specs,
         out_specs=out_specs,
         scratch_shapes=list(scratch_shapes),
-        compiler_params=pltpu.CompilerParams(vmem_limit_bytes=VMEM_LIMIT),
+        compiler_params=pltpu.CompilerParams(vmem_limit_bytes=limit),
     )
 
 
@@ -322,6 +347,13 @@
         [vmem] * 3,
         [vmem] * 3,
     )(kinship, variance.reshape(block_count, tile), phenotypes)
+    def to_mates(blocks):
+        return [swap(block, "samples", devices, k) for k, block in zip(near_by, blocks)]
+
+    bits = half.bit_length() - 1
+    even = [sum(((i >> b) & 1) << (bits - b) for b in range(bits)) for i in range(half)]
+    steps = [2 << i for i in range(bits)]
+    other_dosage = with_layout_constraint(swap(after(dosage, direction), "cols", 2, 1), Layout((0, 1)))
     tiles = jax.ShapeDtypeStruct((block_count, tile, positions * tile), jnp.bfloat16)
     table, forward, high, low, *outgoing = call(
         functools.partial(route_kernel, devices, capacity),
@@ -330,37 +362,22 @@
             jax.ShapeDtypeStruct((capacity, half), jnp.int32),
             tiles, tiles,
         ] + [float_of(capacity, tile, columns)] * (half - 1),
-        [smem, vmem, vmem],
+        [smem, vmem, vmem, anywhere],
         [smem, smem] + [vmem] * (half + 1),
         [pltpu.SMEM((devices,), jnp.int32), pltpu.SMEM((devices,), jnp.int32)],
-    )(relatives.T, kinship, direction)
-
-    def to_mates(blocks):
-        return [swap(block, "samples", devices, k) for k, block in zip(near_by, blocks)]
-
-    me = lax.axis_index("samples")
-    dosage = after(dosage, table)
-    other_dosage = with_layout_constraint(swap(dosage, "cols", 2, 1), Layout((0, 1)))
-    dosages = [values.reshape(people, devices, share_rows) for values in (dosage, other_dosage)]
-    bits = half.bit_length() - 1
-    even = [sum(((i >> b) & 1) << (bits - b) for b in range(bits)) for i in range(half)]
-    steps = [2 << i for i in range(bits)]
-    grouped = [
-        jnp.concatenate([
-            lax.dynamic_index_in_dim(values, me ^ k ^ odd, 1, keepdims=False)
-            for k in even for values in dosages
-        ], axis=1)
-        for odd in range(2)
-    ]
+    )(relatives.T, kinship, direction, other_dosage)
+
+
+    parts = jax.ShapeDtypeStruct((2, variants, people), jnp.bfloat16)
+    large = VMEM_LIMIT if variants <= people else LARGE_VMEM
+    grouped = call(
+        functools.partial(group_kernel, even), [parts] * 2, [vmem] * 2, [vmem] * 2, limit=large
+    )(after(dosage, table).T, other_dosage.T)
 
     def variant_products(values):
-        return [
-            lax.dot_general(
-                group, values, (((0,), (0,)), ((), ())), precision=lax.Precision.HIGH,
-                preferred_element_type=jnp.float32,
-            ).reshape(half, 2 * share_rows, columns)
-            for group in grouped
-        ]
+        return call(
+            score_kernel, [float_of(half, 2 * share_rows, columns)] * 2, [vmem] * 3, [vmem] * 2, limit=large
+        )(*grouped, values)
 
     def halved(values, step):
         count = values.shape[0] // 2
@@ -377,16 +394,16 @@
         [vmem] * (half - 1),
     )(forward, partner, *near, direction_even, direction_odd))
     received = near + far + [partner.reshape(block_count, tile, columns)]
-    scaled, own_sums, gathered, *outgoing = call(
+    scaled, sums, gathered, outgoing = call(
         functools.partial(apply_kernel, devices, capacity),
-        [full, float_of(SUBLANES, columns), float_of(devices * capacity + block_count, tile, columns)]
-        + [float_of(tile + SUBLANES, columns)] * (devices - 1),
+        [
+            full, float_of(SUBLANES, columns), float_of(devices * capacity + block_count, tile, columns),
+            float_of(devices, tile + SUBLANES, columns),
+        ],
         [smem] + [vmem] * (devices + 4) + [anywhere],
-        [vmem] * (devices + 2),
+        [vmem] * 4,
     )(table, high, low, direction, diagonal, norm, *received, direction_share)
-    order = [k for k in range(half, devices)] + near_by
-    sent = {k: swap(outgoing[k - 1], "samples", devices, k) for k in order}
-    later = [sent[k] for k in range(1, devices)]
+    later = lax.all_to_all(outgoing, "samples", split_axis=0, concat_axis=0, tiled=True)
     scaled_even, scaled_odd = variant_products(scaled)
     scaled_sum = scaled_even + swap(scaled_odd, "samples", devices, 1)
     direction_sum = after(direction_even, scaled) + direction_share
@@ -397,21 +414,21 @@
     scaled_kept, scaled_taken = halved(scaled_sum, steps[0])
     sums = call(
         functools.partial(curvature_kernel, devices),
-        float_of(2 * devices, SUBLANES, columns),
-        [smem] + [vmem] * (devices + 6) + [anywhere],
-        hbm,
-        [room(devices, tile, columns), room(2 * devices, SUBLANES, columns), pltpu.SemaphoreType.DMA((1,))],
-    )(table, high, low, direction, diagonal, scaled, own_sums, gathered, *later, scaled_sum)
-    scaled_sum = after(scaled_kept, sums) + scaled_taken
-    for step in steps[1:-1]:
+        float_of(SUBLANES, columns),
+        [smem] + [vmem] * 7 + [anywhere] * 2,
+        vmem,
+    )(table, high, low, direction, diagonal, scaled, gathered, later, scaled_sum, direction_sum)
+    half_sum = float_of(scaled_kept.shape[0] // 2, 2 * share_rows, columns)
+    all_sums, scaled_kept, scaled_given = call(
+        add_kernel, [float_of(2 * devices, SUBLANES, columns), half_sum, half_sum], [vmem] * 3, [vmem] * 3
+    )(sums, scaled_kept, scaled_taken)
+    all_sums = lax.all_to_all(all_sums, ("samples", "cols"), split_axis=0, concat_axis=0, tiled=True)
+    scaled_sum = scaled_kept + swap(scaled_given, "samples", devices, steps[1])
+    for step in steps[2:]:
         scaled_kept, scaled_taken = halved(scaled_sum, step)
         scaled_sum = scaled_kept + scaled_taken
-    scaled_kept, scaled_taken = halved(scaled_sum, steps[-1])
-    all_sums = lax.all_to_all(
-        after(sums, scaled_kept), ("samples", "cols"), split_axis=0, concat_axis=0, tiled=True
-    )
     direction_scores = (after(direction_kept, sums) + direction_taken)[0]
-    scaled_scores = (scaled_kept + scaled_taken)[0]
+    scaled_scores = scaled_sum[0]
     swapped = swap(jnp.concatenate([direction_scores[share_rows:], scaled_scores[share_rows:]]), "cols", 2, 1)
     solved, scores = call(
         functools.partial(finish_kernel, devices, 1.0 / math.sqrt(people * devices)),

time: 127 us -> 123 us (0.969)
  starting transfers between devices: 42 us -> 35.2 us
  Pallas kernels: 8.23 us -> 12.8 us
  waiting for transfers between devices: 48 us -> 52.5 us
  matrix products: 3.69 us -> 0 us
  local copies, waits for them, and re-layouts: 22.3 us -> 19.6 us
    ppermute x22 -> x15, starting transfers between devices: 31.2 us -> 23.7 us  [swap(): return lax.ppermute(values, axis, [(i, i ^ step) for i in range(devices)])]
    ppermute x22 -> x15, waiting for transfers between devices: 48 us -> 52.5 us  [swap(): return lax.ppermute(values, axis, [(i, i ^ step) for i in range(devices)])]
    dot_general x4 -> x0, matrix products: 3.69 us -> none  [variant_products(): lax.dot_general(group, values, (((0,), (0,)), ((), ())), precision=lax.Pr...]
    pallas_call x1 -> x5, Pallas kernels: 2.21 us -> 5.32 us  [the longest x2 1.96 us: variant_products(): call(score_kernel, [float_of(half, 2 * share_rows, columns)] * 2, [vmem]...]
    concatenate x1 -> x0, local copies, waits for them, and re-layouts: 1.69 us -> none  [per_device(): jnp.concatenate([lax.dynamic_index_in_dim(values, me ^ k ^ odd, 1, keepdi...]
    slice x4 -> x3, local copies, waits for them, and re-layouts: 0.08 us -> 1.56 us  [halved(): return (values[:count], swap(values[count:], 'samples', devices, step))]
    all_to_all x1 -> x2, starting transfers between devices: 10.8 us -> 11.6 us  [the longest x1 6.72 us: per_device(): lax.all_to_all(outgoing, 'samples', split_axis=0, concat_axis=0, tiled=True)]
    unnamed x19 -> x42, local copies, waits for them, and re-layouts: 15.4 us -> 15.1 us
  transfers between devices with their start and end apart: 23 -> 17, of which waited for: 7 -> 9; matrix products, arithmetic and copies ran while one was open for 18% -> 5% of each run, Pallas kernels for 2% -> 7%
where the time goes in v10:
time: 123 us; the launch traced here: 122 us
  waiting for transfers between devices  52.5 us (43%)
  starting transfers between devices  35.2 us (29%)
  local copies, waits for them, and re-layouts  19.6 us (16%)
  Pallas kernels  12.8 us (10%)
    ppermute x15, waiting for transfers between devices, swap(): return lax.ppermute(values, axis, [(i, i ^ step) for i in range(devices)])  52.5 us
    ppermute x15, starting transfers between devices, swap(): return lax.ppermute(values, axis, [(i, i ^ step) for i in range(devices)])  23.7 us
    unnamed x42, local copies, waits for them, and re-layouts  15.1 us
    all_to_all x1, starting transfers between devices, per_device(): lax.all_to_all(outgoing, 'samples', split_axis=0, concat_axis=0, tiled=True)  6.72 us
    all_to_all x1, starting transfers between devices, per_device(): lax.all_to_all(all_sums, ('samples', 'cols'), split_axis=0, concat_axis=0...  4.83 us
    pallas_call x1, Pallas kernels, per_device(): call(functools.partial(apply_kernel, devices, capacity), [full, float_of(...  2.76 us
  transfers between devices with their start and end apart: 17, of which 9 were waited for; matrix products, arithmetic and copies ran while one was open for 5% of the time, Pallas kernels for 7%

profile of v10, /device:TPU:0, one launch (start us, length us, event | category | flops | bytes accessed | tf_op | source)
XLA Modules:
  0.0 122.2 jit_solution(10351280139143846584)
XLA Ops:
  5.4 3.6 %collective-permute-start.4 = (f32[512,256]{1,0:T(8,128)S(1)}, f32[512,256]{1,0:T(8,128)}, u32[]{:S(2)}, u32[]{:S(2)}) collective-permute-start(f32[512,256]{1,0:T(8,128)S(1)} %get-tuple-element.31.direction_ref.values_ref), channel_id=1, source_target_pairs={{0,8},{2,10},{4,12},{6,14},{8,0},{10,2},{12,4},{14,6},{1,9},{3,11}... | collective-permute-start | bytes 1572872 | tf_op jit(solution)/shard_map/ppermute | solution.py:318
  8.9 1.9 %shard_map.69 = (s32[4,12]{1,0:T(4,128)S(1)}, s32[2,4]{1,0:T(2,128)S(1)}, bf16[4,128,512]{2,1,0:T(8,128)(2,1)S(1)}, bf16[4,128,512]{2,1,0:T(8,128)(2,1)S(1)}, f3...) custom-call(s32[3,32]{1,0:T(4,128)S(1)} %bitcast.16, f32[4,4,128,128]{3,2,1,0:T(8,128)S(1)} %copy-done, ...), custom_call_target="tpu_custom_call" | custom-call | tf_op jit(solution)/shard_map/pallas_call | solution.py:358
  11.6 1.6 %collective-permute-start.1 = (f32[2,128,256]{2,1,0:T(8,128)}, f32[2,128,256]{2,1,0:T(8,128)}, u32[]{:S(2)}, u32[]{:S(2)}) collective-permute-start(f32[2,128,256]{2,1,0:T(8,128)} %get-tuple-element.38), channel_id=1, source_target_pairs={{0,2},{2,0},{4,6},{6,4},{8,10},{10,8},{12,14},{14,12},{1,3},{3,1},... | collective-permute-start | bytes 786440 | tf_op jit(solution)/shard_map/ppermute | solution.py:318
  13.2 1.6 %collective-permute-start.2 = (f32[2,128,256]{2,1,0:T(8,128)}, f32[2,128,256]{2,1,0:T(8,128)}, u32[]{:S(2)}, u32[]{:S(2)}) collective-permute-start(f32[2,128,256]{2,1,0:T(8,128)} %get-tuple-element.39), channel_id=1, source_target_pairs={{0,4},{2,6},{4,0},{6,2},{8,12},{10,14},{12,8},{14,10},{1,5},{3,7},... | collective-permute-start | bytes 786440 | tf_op jit(solution)/shard_map/ppermute | solution.py:318
  15.1 1.6 %copy.7 = f32[512,512]{0,1:T(8,128)S(1)} copy(f32[512,512]{1,0:T(8,128)} %param.9) | data formatting | bytes 2097152 | tf_op jit(solution)/shard_map/optimization_barrier | solution.py:322
  20.9 1.6 %collective-permute-start.8 = (f32[4,128,256]{2,1,0:T(8,128)S(1)}, f32[4,128,256]{2,1,0:T(8,128)S(1)}, u32[]{:S(2)}, u32[]{:S(2)}) collective-permute-start(f32[4,128,256]{2,1,0:T(8,128)S(1)} %get-tuple-element.46.refs_4_), channel_id=1, source_target_pairs={{0,2},{2,0},{4,6},{6,4},{8,10},{10,8},{12,14},{14,12},{1,3},{3,1},... | collective-permute-start | bytes 1572872 | tf_op jit(solution)/shard_map/ppermute | solution.py:318
  22.4 10.5 %collective-permute-done.4.partner_ref = f32[512,256]{1,0:T(8,128)} collective-permute-done((f32[512,256]{1,0:T(8,128)S(1)}, f32[512,256]{1,0:T(8,128)}, u32[]{:S(2)}, u32[]{:S(2)}) %collective-permute-start.4) | collective-permute-done | bytes 524320 | tf_op jit(solution)/shard_map/ppermute | solution.py:318
  33.0 4.4 %collective-permute-done.3.refs_2_ = f32[2,128,256]{2,1,0:T(8,128)} collective-permute-done((f32[2,128,256]{2,1,0:T(8,128)}, f32[2,128,256]{2,1,0:T(8,128)}, u32[]{:S(2)}, u32[]{:S(2)}) %collective-permute-start.3) | collective-permute-done | bytes 262176 | tf_op jit(solution)/shard_map/ppermute | solution.py:318
  38.6 1.5 %collective-permute-start.5 = (f32[2,128,256]{2,1,0:T(8,128)S(1)}, f32[2,128,256]{2,1,0:T(8,128)S(1)}, u32[]{:S(2)}, u32[]{:S(2)}) collective-permute-start(f32[2,128,256]{2,1,0:T(8,128)S(1)} %get-tuple-element.47), channel_id=1, source_target_pairs={{0,2},{2,0},{4,6},{6,4},{8,10},{10,8},{12,14},{14,12},{1,3},{3,1},... | collective-permute-start | bytes 786440 | tf_op jit(solution)/shard_map/ppermute | solution.py:318
  40.1 2.0 %collective-permute-start.7 = (f32[2,128,256]{2,1,0:T(8,128)S(1)}, f32[2,128,256]{2,1,0:T(8,128)S(1)}, u32[]{:S(2)}, u32[]{:S(2)}) collective-permute-start(f32[2,128,256]{2,1,0:T(8,128)S(1)} %get-tuple-element.49), channel_id=1, source_target_pairs={{0,6},{2,4},{4,2},{6,0},{8,14},{10,12},{12,10},{14,8},{1,7},{3,5},... | collective-permute-start | bytes 786440 | tf_op jit(solution)/shard_map/ppermute | solution.py:318
  42.2 4.8 %collective-permute-done.5.refs_3_ = f32[2,128,256]{2,1,0:T(8,128)S(1)} collective-permute-done((f32[2,128,256]{2,1,0:T(8,128)S(1)}, f32[2,128,256]{2,1,0:T(8,128)S(1)}, u32[]{:S(2)}, u32[]{:S(2)}) %collective-permute-start.5) | collective-permute-done | bytes 262176 | tf_op jit(solution)/shard_map/ppermute | solution.py:318
  47.0 2.4 %collective-permute-done.6.refs_4_ = f32[2,128,256]{2,1,0:T(8,128)S(1)} collective-permute-done((f32[2,128,256]{2,1,0:T(8,128)S(1)}, f32[2,128,256]{2,1,0:T(8,128)S(1)}, u32[]{:S(2)}, u32[]{:S(2)}) %collective-permute-start.6) | collective-permute-done | bytes 262176 | tf_op jit(solution)/shard_map/ppermute | solution.py:318
  49.4 3.3 %collective-permute-done.7.refs_5_ = f32[2,128,256]{2,1,0:T(8,128)S(1)} collective-permute-done((f32[2,128,256]{2,1,0:T(8,128)S(1)}, f32[2,128,256]{2,1,0:T(8,128)S(1)}, u32[]{:S(2)}, u32[]{:S(2)}) %collective-permute-start.7) | collective-permute-done | bytes 262176 | tf_op jit(solution)/shard_map/ppermute | solution.py:318
  52.7 2.8 %shard_map.73 = (f32[512,256]{1,0:T(8,128)S(1)}, f32[8,256]{1,0:T(8,128)}, f32[20,128,256]{2,1,0:T(8,128)S(1)}, f32[8,136,256]{2,1,0:T(8,128)S(1)}) custom-call(s32[4,12]{1,0:T(4,128)S(1)} %get-tuple-element.33.table_ref, bf16[4,128,512]{2,1,0:T(8,128)(2,1)S(1)} %get-tuple-element.34.high_ref, bf16[4,128,512]{2,1,0:T(8,128)(2,1)S(1)} %copy-done.9, ...), custom_call_target="tpu_custom_call" | custom-call | tf_op jit(solution)/shard_map/pallas_call | solution.py:397
  58.0 6.7 %all-to-all-start = ((f32[8,136,256]{2,1,0:T(8,128)}), f32[8,136,256]{2,1,0:T(8,128)S(1)}, u32[]{:S(2)}, u32[]{:S(2)}) async-start(f32[8,136,256]{2,1,0:T(8,128)} %copy-done.13), calls=%async_computation | async-start | bytes 2228224 | tf_op jit(solution)/shard_map/all_to_all | solution.py:406
  68.1 2.1 %collective-permute-start.10 = (f32[4,128,256]{2,1,0:T(8,128)S(1)}, f32[4,128,256]{2,1,0:T(8,128)S(1)}, u32[]{:S(2)}, u32[]{:S(2)}) collective-permute-start(f32[4,128,256]{2,1,0:T(8,128)S(1)} %get-tuple-element.55), channel_id=1, source_target_pairs={{0,2},{2,0},{4,6},{6,4},{8,10},{10,8},{12,14},{14,12},{1,3},{3,1},... | collective-permute-start | bytes 1572872 | tf_op jit(solution)/shard_map/ppermute | solution.py:318
  71.8 15.0 %collective-permute-done.9 = f32[2,128,256]{2,1,0:T(8,128)S(1)} collective-permute-done((f32[2,128,256]{2,1,0:T(8,128)S(1)}, f32[2,128,256]{2,1,0:T(8,128)S(1)}, u32[]{:S(2)}, u32[]{:S(2)}) %collective-permute-start.9) | collective-permute-done | bytes 262176 | tf_op jit(solution)/shard_map/ppermute | solution.py:318
  86.9 2.0 %collective-permute-done.10 = f32[4,128,256]{2,1,0:T(8,128)S(1)} collective-permute-done((f32[4,128,256]{2,1,0:T(8,128)S(1)}, f32[4,128,256]{2,1,0:T(8,128)S(1)}, u32[]{:S(2)}, u32[]{:S(2)}) %collective-permute-start.10) | collective-permute-done | bytes 524320 | tf_op jit(solution)/shard_map/ppermute | solution.py:318
  91.7 3.3 %collective-permute-start.11 = (f32[1,128,256]{2,1,0:T(8,128)}, f32[1,128,256]{2,1,0:T(8,128)}, u32[]{:S(2)}, u32[]{:S(2)}) collective-permute-start(f32[1,128,256]{2,1,0:T(8,128)} %get-tuple-element.62), channel_id=1, source_target_pairs={{0,8},{2,10},{4,12},{6,14},{8,0},{10,2},{12,4},{14,6},{1,9},{3,11}... | collective-permute-start | bytes 393224 | tf_op jit(solution)/shard_map/ppermute | solution.py:318
  95.1 1.7 %copy-done.7 = f32[20,128,256]{2,1,0:T(8,128)S(1)} copy-done((f32[20,128,256]{2,1,0:T(8,128)S(1)}, f32[20,128,256]{2,1,0:T(8,128)}, u32[]{:S(2)}) %copy-start.7) | copy-done | bytes 2621464
  100.3 1.6 %shard_map.76 = (f32[16,8,256]{2,1,0:T(8,128)}, f32[1,128,256]{2,1,0:T(8,128)S(1)}, f32[1,128,256]{2,1,0:T(8,128)S(1)}) custom-call(f32[8,256]{1,0:T(8,128)S(1)} %shard_map.75.sums_ref, f32[2,128,256]{2,1,0:T(8,128)S(1)} %copy-done.16, f32[2,128,256]{2,1,0:T(8,128)} %collective-permute-done.12.taken_ref), custom_call_target="tpu_custom_call" | custom-call | tf_op jit(solution)/shard_map/pallas_call | solution.py:422
  101.9 4.8 %all-to-all-start.1 = ((f32[16,8,256]{2,1,0:T(8,128)}), f32[16,8,256]{2,1,0:T(8,128)S(1)}, u32[]{:S(2)}, u32[]{:S(2)}) async-start(f32[16,8,256]{2,1,0:T(8,128)} %get-tuple-element.59), calls=%async_computation.1 | async-start | bytes 262144 | tf_op jit(solution)/shard_map/all_to_all | solution.py:425
  106.8 2.8 %collective-permute-start.13 = (f32[1,128,256]{2,1,0:T(8,128)S(1)}, f32[1,128,256]{2,1,0:T(8,128)S(1)}, u32[]{:S(2)}, u32[]{:S(2)}) collective-permute-start(f32[1,128,256]{2,1,0:T(8,128)S(1)} %get-tuple-element.58), channel_id=1, source_target_pairs={{0,8},{2,10},{4,12},{6,14},{8,0},{10,2},{12,4},{14,6},{1,9},{3,11}... | collective-permute-start | bytes 393224 | tf_op jit(solution)/shard_map/ppermute | solution.py:318
  110.6 8.6 %collective-permute-done.13 = f32[1,128,256]{2,1,0:T(8,128)S(1)} collective-permute-done((f32[1,128,256]{2,1,0:T(8,128)S(1)}, f32[1,128,256]{2,1,0:T(8,128)S(1)}, u32[]{:S(2)}, u32[]{:S(2)}) %collective-permute-start.13) | collective-permute-done | bytes 131104 | tf_op jit(solution)/shard_map/ppermute | solution.py:318
  (75 shorter events, 28.9 us)
Async XLA Ops:
  3.6 5.4 %copy-start.19 = (s32[32,3]{0,1:T(4,128)S(1)}, s32[32,3]{0,1:T(4,128)}, u32[]{:S(2)}) copy-start(s32[32,3]{0,1:T(4,128)} %param.6) | copy-start | bytes 1156
  3.8 48.9 %copy-start.14 = (f32[512,1]{1,0:T(8,128)}, f32[512,1]{1,0:T(8,128)S(1)}, u32[]{:S(2)}) copy-start(f32[512,1]{1,0:T(8,128)S(1)} %get-tuple-element.36.diagonal_ref) | copy-start | bytes 6148
  4.9 4.0 %collective-permute-start = (f32[512,512]{1,0:T(8,128)S(1)}, f32[512,512]{1,0:T(8,128)S(1)}, u32[]{:S(2)}, u32[]{:S(2)}) collective-permute-start(f32[512,512]{1,0:T(8,128)S(1)} %copy-done.20), channel_id=1, source_target_pairs={{0,1},{1,0},{2,3},{3,2},{4,5},{5,4},{6,7},{7,6},{8,9},{9,8},{10,11... | collective-permute-start | bytes 3145736 | tf_op jit(solution)/shard_map/ppermute | solution.py:318
  5.4 27.6 %collective-permute-start.4 = (f32[512,256]{1,0:T(8,128)S(1)}, f32[512,256]{1,0:T(8,128)}, u32[]{:S(2)}, u32[]{:S(2)}) collective-permute-start(f32[512,256]{1,0:T(8,128)S(1)} %get-tuple-element.31.direction_ref.values_ref), channel_id=1, source_target_pairs={{0,8},{2,10},{4,12},{6,14},{8,0},{10,2},{12,4},{14,6},{1,9},{3,11}... | collective-permute-start | bytes 1572872 | tf_op jit(solution)/shard_map/ppermute | solution.py:318
  11.6 21.3 %collective-permute-start.1 = (f32[2,128,256]{2,1,0:T(8,128)}, f32[2,128,256]{2,1,0:T(8,128)}, u32[]{:S(2)}, u32[]{:S(2)}) collective-permute-start(f32[2,128,256]{2,1,0:T(8,128)} %get-tuple-element.38), channel_id=1, source_target_pairs={{0,2},{2,0},{4,6},{6,4},{8,10},{10,8},{12,14},{14,12},{1,3},{3,1},... | collective-permute-start | bytes 786440 | tf_op jit(solution)/shard_map/ppermute | solution.py:318
  13.2 19.8 %collective-permute-start.2 = (f32[2,128,256]{2,1,0:T(8,128)}, f32[2,128,256]{2,1,0:T(8,128)}, u32[]{:S(2)}, u32[]{:S(2)}) collective-permute-start(f32[2,128,256]{2,1,0:T(8,128)} %get-tuple-element.39), channel_id=1, source_target_pairs={{0,4},{2,6},{4,0},{6,2},{8,12},{10,14},{12,8},{14,10},{1,5},{3,7},... | collective-permute-start | bytes 786440 | tf_op jit(solution)/shard_map/ppermute | solution.py:318
  14.8 22.6 %collective-permute-start.3 = (f32[2,128,256]{2,1,0:T(8,128)}, f32[2,128,256]{2,1,0:T(8,128)}, u32[]{:S(2)}, u32[]{:S(2)}) collective-permute-start(f32[2,128,256]{2,1,0:T(8,128)} %get-tuple-element.40), channel_id=1, source_target_pairs={{0,6},{2,4},{4,2},{6,0},{8,14},{10,12},{12,10},{14,8},{1,7},{3,5},... | collective-permute-start | bytes 786440 | tf_op jit(solution)/shard_map/ppermute | solution.py:318
  20.9 21.3 %collective-permute-start.8 = (f32[4,128,256]{2,1,0:T(8,128)S(1)}, f32[4,128,256]{2,1,0:T(8,128)S(1)}, u32[]{:S(2)}, u32[]{:S(2)}) collective-permute-start(f32[4,128,256]{2,1,0:T(8,128)S(1)} %get-tuple-element.46.refs_4_), channel_id=1, source_target_pairs={{0,2},{2,0},{4,6},{6,4},{8,10},{10,8},{12,14},{14,12},{1,3},{3,1},... | collective-permute-start | bytes 1572872 | tf_op jit(solution)/shard_map/ppermute | solution.py:318
  37.4 15.3 %copy-start.9 = (bf16[4,128,512]{2,1,0:T(8,128)(2,1)S(1)}, bf16[4,128,512]{2,1,0:T(8,128)(2,1)}, u32[]{:S(2)}) copy-start(bf16[4,128,512]{2,1,0:T(8,128)(2,1)} %copy-done.8) | copy-start | bytes 1572868
  38.6 8.4 %collective-permute-start.5 = (f32[2,128,256]{2,1,0:T(8,128)S(1)}, f32[2,128,256]{2,1,0:T(8,128)S(1)}, u32[]{:S(2)}, u32[]{:S(2)}) collective-permute-start(f32[2,128,256]{2,1,0:T(8,128)S(1)} %get-tuple-element.47), channel_id=1, source_target_pairs={{0,2},{2,0},{4,6},{6,4},{8,10},{10,8},{12,14},{14,12},{1,3},{3,1},... | collective-permute-start | bytes 786440 | tf_op jit(solution)/shard_map/ppermute | solution.py:318
  40.1 9.2 %collective-permute-start.6 = (f32[2,128,256]{2,1,0:T(8,128)S(1)}, f32[2,128,256]{2,1,0:T(8,128)S(1)}, u32[]{:S(2)}, u32[]{:S(2)}) collective-permute-start(f32[2,128,256]{2,1,0:T(8,128)S(1)} %get-tuple-element.48), channel_id=1, source_target_pairs={{0,4},{2,6},{4,0},{6,2},{8,12},{10,14},{12,8},{14,10},{1,5},{3,7},... | collective-permute-start | bytes 786440 | tf_op jit(solution)/shard_map/ppermute | solution.py:318
  40.1 12.6 %collective-permute-start.7 = (f32[2,128,256]{2,1,0:T(8,128)S(1)}, f32[2,128,256]{2,1,0:T(8,128)S(1)}, u32[]{:S(2)}, u32[]{:S(2)}) collective-permute-start(f32[2,128,256]{2,1,0:T(8,128)S(1)} %get-tuple-element.49), channel_id=1, source_target_pairs={{0,6},{2,4},{4,2},{6,0},{8,14},{10,12},{12,10},{14,8},{1,7},{3,5},... | collective-permute-start | bytes 786440 | tf_op jit(solution)/shard_map/ppermute | solution.py:318
  42.2 13.3 %copy-start.11 = (f32[4,128,256]{2,1,0:T(8,128)}, f32[4,128,256]{2,1,0:T(8,128)S(1)}, u32[]{:S(2)}) copy-start(f32[4,128,256]{2,1,0:T(8,128)S(1)} %collective-permute-done.8.refs_7_) | copy-start | bytes 1572868
  55.5 1.5 %copy-start.6 = (f32[20,128,256]{2,1,0:T(8,128)}, f32[20,128,256]{2,1,0:T(8,128)S(1)}, u32[]{:S(2)}) copy-start(f32[20,128,256]{2,1,0:T(8,128)S(1)} %get-tuple-element.52.gathered_ref) | copy-start | bytes 7864324
  58.0 37.1 %all-to-all-start = ((f32[8,136,256]{2,1,0:T(8,128)}), f32[8,136,256]{2,1,0:T(8,128)S(1)}, u32[]{:S(2)}, u32[]{:S(2)}) async-start(f32[8,136,256]{2,1,0:T(8,128)} %copy-done.13), calls=%async_computation | async-start | bytes 2228224 | tf_op jit(solution)/shard_map/all_to_all | solution.py:406
  67.1 3.1 %copy-start.12 = (f32[4,128,256]{2,1,0:T(8,128)S(1)}, f32[4,128,256]{2,1,0:T(8,128)}, u32[]{:S(2)}) copy-start(f32[4,128,256]{2,1,0:T(8,128)} %copy-done.11) | copy-start | bytes 1572868
  68.1 20.8 %collective-permute-start.10 = (f32[4,128,256]{2,1,0:T(8,128)S(1)}, f32[4,128,256]{2,1,0:T(8,128)S(1)}, u32[]{:S(2)}, u32[]{:S(2)}) collective-permute-start(f32[4,128,256]{2,1,0:T(8,128)S(1)} %get-tuple-element.55), channel_id=1, source_target_pairs={{0,2},{2,0},{4,6},{6,4},{8,10},{10,8},{12,14},{14,12},{1,3},{3,1},... | collective-permute-start | bytes 1572872 | tf_op jit(solution)/shard_map/ppermute | solution.py:318
  70.3 16.5 %collective-permute-start.9 = (f32[2,128,256]{2,1,0:T(8,128)S(1)}, f32[2,128,256]{2,1,0:T(8,128)S(1)}, u32[]{:S(2)}, u32[]{:S(2)}) collective-permute-start(f32[2,128,256]{2,1,0:T(8,128)S(1)} %slice.41), channel_id=1, source_target_pairs={{0,4},{2,6},{4,0},{6,2},{8,12},{10,14},{12,8},{14,10},{1,5},{3,7},... | collective-permute-start | bytes 786440 | tf_op jit(solution)/shard_map/ppermute | solution.py:318
  89.8 10.4 %collective-permute-start.12 = (f32[2,128,256]{2,1,0:T(8,128)}, f32[2,128,256]{2,1,0:T(8,128)}, u32[]{:S(2)}, u32[]{:S(2)}) collective-permute-start(f32[2,128,256]{2,1,0:T(8,128)} %get-tuple-element.60), channel_id=1, source_target_pairs={{0,4},{2,6},{4,0},{6,2},{8,12},{10,14},{12,8},{14,10},{1,5},{3,7},... | collective-permute-start | bytes 786440 | tf_op jit(solution)/shard_map/ppermute | solution.py:318
  91.7 17.9 %collective-permute-start.11 = (f32[1,128,256]{2,1,0:T(8,128)}, f32[1,128,256]{2,1,0:T(8,128)}, u32[]{:S(2)}, u32[]{:S(2)}) collective-permute-start(f32[1,128,256]{2,1,0:T(8,128)} %get-tuple-element.62), channel_id=1, source_target_pairs={{0,8},{2,10},{4,12},{6,14},{8,0},{10,2},{12,4},{14,6},{1,9},{3,11}... | collective-permute-start | bytes 393224 | tf_op jit(solution)/shard_map/ppermute | solution.py:318
  95.1 1.7 %copy-start.7 = (f32[20,128,256]{2,1,0:T(8,128)S(1)}, f32[20,128,256]{2,1,0:T(8,128)}, u32[]{:S(2)}) copy-start(f32[20,128,256]{2,1,0:T(8,128)} %copy-done.6) | copy-start | bytes 7864324
  101.9 17.4 %all-to-all-start.1 = ((f32[16,8,256]{2,1,0:T(8,128)}), f32[16,8,256]{2,1,0:T(8,128)S(1)}, u32[]{:S(2)}, u32[]{:S(2)}) async-start(f32[16,8,256]{2,1,0:T(8,128)} %get-tuple-element.59), calls=%async_computation.1 | async-start | bytes 262144 | tf_op jit(solution)/shard_map/all_to_all | solution.py:425
  106.8 12.5 %collective-permute-start.13 = (f32[1,128,256]{2,1,0:T(8,128)S(1)}, f32[1,128,256]{2,1,0:T(8,128)S(1)}, u32[]{:S(2)}, u32[]{:S(2)}) collective-permute-start(f32[1,128,256]{2,1,0:T(8,128)S(1)} %get-tuple-element.58), channel_id=1, source_target_pairs={{0,8},{2,10},{4,12},{6,14},{8,0},{10,2},{12,4},{14,6},{1,9},{3,11}... | collective-permute-start | bytes 393224 | tf_op jit(solution)/shard_map/ppermute | solution.py:318
  119.3 1.4 %collective-permute-start.14 = (f32[128,256]{1,0:T(8,128)S(1)}, f32[128,256]{1,0:T(8,128)S(1)}, u32[]{:S(2)}, u32[]{:S(2)}) collective-permute-start(f32[128,256]{1,0:T(8,128)S(1)} %pad_maximum_fusion), channel_id=1, source_target_pairs={{0,1},{1,0},{2,3},{3,2},{4,5},{5,4},{6,7},{7,6},{8,9},{9,8},{10,11... | collective-permute-start | bytes 393224 | tf_op jit(solution)/shard_map/ppermute | solution.py:318
  (14 other events, 15.6 us)

commit v11 on v10

--- a/solution.py
+++ b/solution.py
@@ -178,9 +178,30 @@
         gathered_ref[pl.ds((mate ^ half) * capacity, capacity)] = far_refs[k - 1][...]
 
 
-def apply_kernel(devices, capacity, table_ref, high_ref, low_ref, direction_ref, diagonal_ref, norm_ref, *refs):
+def score_products(high_ref, low_ref, values, even_ref, odd_ref):
+    count, rows = even_ref.shape[:2]
+    for odd, out_ref in enumerate((even_ref, odd_ref)):
+        for i in range(0, count, 4):
+            here = pl.ds(i * rows, 4 * rows)
+            total = product(high_ref[odd, here, :], low_ref[odd, here, :], [values])
+            out_ref[pl.ds(i, 4)] = total.reshape(4, rows, -1)
+
+
+def score_kernel(order, high_ref, low_ref, values_ref, out_ref):
+    rows = out_ref.shape[1]
+    me = lax.axis_index("samples")
+    for odd in range(2):
+        for i in range(0, len(order), 4):
+            here = pl.ds(i * rows, 4 * rows)
+            total = product(high_ref[odd, here, :], low_ref[odd, here, :], [values_ref[...]])
+            for j in range(4):
+                out_ref[me ^ order[i + j] ^ odd] = total[j * rows:(j + 1) * rows]
+
+
+def apply_kernel(devices, capacity, table_ref, high_ref, low_ref, direction_ref, diagonal_ref, norm_ref,
+                 dosage_high_ref, dosage_low_ref, *refs):
     received_refs = refs[:devices - 1]
-    scaled_ref, sums_ref, gathered_ref, outgoing_ref = refs[-4:]
+    scaled_ref, sums_ref, gathered_ref, even_ref, odd_ref, *outgoing_refs = refs[-4 - devices:]
     gather_received(devices, capacity, received_refs, gathered_ref)
     block_count, tile, depth = high_ref.shape
     others = depth // tile - 1
@@ -195,20 +216,24 @@
     row_ids = lax.broadcasted_iota(jnp.int32, cross.shape, 0)
     sums = jnp.where(row_ids == 1, jnp.sum(cross, axis=0, keepdims=True), norm_ref[...])
     sums_ref[...] = sums
-    for other in range(devices):
-        start = pl.multiple_of(table_ref[3, other] * tile, tile)
-        outgoing_ref[other, pl.ds(0, tile), :] = scaled_ref[pl.ds(start, tile), :]
-        outgoing_ref[other, pl.ds(tile, SUBLANES), :] = sums
-
-
-def curvature_kernel(devices, table_ref, high_ref, low_ref, direction_ref, diagonal_ref, scaled_ref, gathered_ref,
-                     later_ref, *refs):
-    sums_ref = refs[-1]
+    me = lax.axis_index("samples")
+    for k in range(1, devices):
+        start = pl.multiple_of(table_ref[3, me ^ k] * tile, tile)
+        outgoing_refs[k - 1][pl.ds(0, tile), :] = scaled_ref[pl.ds(start, tile), :]
+        outgoing_refs[k - 1][pl.ds(tile, SUBLANES), :] = sums
+    score_products(dosage_high_ref, dosage_low_ref, scaled_ref[...], even_ref, odd_ref)
+
+
+def curvature_kernel(order, table_ref, high_ref, low_ref, direction_ref, diagonal_ref, scaled_ref, own_sums_ref,
+                     gathered_ref, *refs):
+    later_refs, (first_sums_ref, sums_ref, later_ref) = refs[:len(order)], refs[-3:]
     block_count, tile, depth = high_ref.shape
     others = depth // tile - 1
-    first_sums = later_ref[0, pl.ds(tile, SUBLANES), :]
-    for other in range(1, devices):
-        first_sums = first_sums + later_ref[other, pl.ds(tile, SUBLANES), :]
+    me = lax.axis_index("samples")
+    first_sums = own_sums_ref[...]
+    for distance, arrived_ref in zip(order, later_refs):
+        later_ref[me ^ distance] = arrived_ref[pl.ds(0, tile), :]
+        first_sums = first_sums + arrived_ref[pl.ds(tile, SUBLANES), :]
     rho = first_sums[1:2, :] / first_sums[0:1, :]
     norm = jnp.zeros(first_sums.shape, jnp.float32)
     bend = jnp.zeros(first_sums.shape, jnp.float32)
@@ -219,22 +244,27 @@
         for i in range(others):
             entry = row * others + i
             weight = table_ref[2, entry].astype(jnp.float32)
-            there = later_ref[table_ref[1, entry], pl.ds(0, tile), :]
-            blocks.append(weight * (there - rho * gathered_ref[table_ref[0, entry]]))
+            blocks.append(weight * (later_ref[table_ref[1, entry]] - rho * gathered_ref[table_ref[0, entry]]))
         mapped = product(high_ref[row], low_ref[row], blocks)
         norm = norm + column_sums(here * here * diagonal_ref[block, :])
         bend = bend + column_sums(here * mapped)
     row_ids = lax.broadcasted_iota(jnp.int32, first_sums.shape, 0)
-    sums = jnp.where(row_ids == 2, jnp.sum(norm, axis=0, keepdims=True), first_sums)
+    sums = jnp.where(row_ids == 2, jnp.sum(norm, axis=0, keepdims=True), 0.0)
     sums_ref[...] = jnp.where(row_ids == 3, jnp.sum(bend, axis=0, keepdims=True), sums)
-
-
-def add_kernel(sums_ref, kept_ref, taken_ref, all_sums_ref, near_ref, far_ref):
+    first_sums_ref[...] = first_sums
+
+
+def add_kernel(kept_ref, taken_ref, *refs):
+    near_ref, far_ref = refs[-2:]
     count = near_ref.shape[0]
     near_ref[...] = kept_ref[pl.ds(0, count)] + taken_ref[pl.ds(0, count)]
     far_ref[...] = kept_ref[pl.ds(count, count)] + taken_ref[pl.ds(count, count)]
-    for i in range(all_sums_ref.shape[0]):
-        all_sums_ref[i] = sums_ref[...]
+
+
+def last_add_kernel(kept_ref, taken_ref, own_ref, other_ref):
+    rows = own_ref.shape[0]
+    own_ref[...] = kept_ref[0, pl.ds(0, rows), :] + taken_ref[0, pl.ds(0, rows), :]
+    other_ref[...] = kept_ref[0, pl.ds(rows, rows), :] + taken_ref[0, pl.ds(rows, rows), :]
 
 
 def group_kernel(order, own_ref, other_ref, high_ref, low_ref):
@@ -250,18 +280,8 @@
                 low_ref[odd, here, :] = low
 
 
-def score_kernel(high_ref, low_ref, values_ref, even_ref, odd_ref):
-    count, rows = even_ref.shape[:2]
-    for odd, out_ref in enumerate((even_ref, odd_ref)):
-        for i in range(0, count, 4):
-            here = pl.ds(i * rows, 4 * rows)
-            total = product(high_ref[odd, here, :], low_ref[odd, here, :], [values_ref[...]])
-            out_ref[pl.ds(i, 4)] = total.reshape(4, rows, -1)
-
-
-def coefficients(sums, shared):
-    norm, cross = sums[0:1, :], sums[1:2, :]
-    later_norm, bend = shared[2:3, :], shared[3:4, :]
+def coefficients(sums):
+    norm, cross, later_norm, bend = (sums[i:i + 1, :] for i in range(4))
     curve = norm + cross
     ratio = later_norm / curve
     step = jnp.where(later_norm > 0, later_norm / (later_norm + bend - later_norm * ratio), 0.0)
@@ -269,22 +289,14 @@
     return start * (1.0 + step * (ratio + cross / norm)), -start * step
 
 
-def finish_kernel(devices, norm_scale, direction_ref, scaled_ref, direction_scores_ref, scaled_scores_ref, swapped_ref,
-                  sums_ref, solved_hbm, scores_ref, solved_ref, semaphores):
+def finish_kernel(norm_scale, direction_ref, scaled_ref, direction_scores_ref, own_scores_ref, swapped_ref,
+                  other_scores_ref, sums_ref, other_sums_ref, solved_hbm, scores_ref, solved_ref, semaphores):
     people, columns = direction_ref.shape
     rows = scores_ref.shape[0]
     column = lax.axis_index("cols")
     copies = Copies(semaphores)
-
-    def total(which):
-        sums = sums_ref[which]
-        shared = sums
-        for i in range(1, devices):
-            shared = shared + sums_ref[2 * i + which]
-        return sums, shared
-
-    along, across = coefficients(*total(column))
-    other_along, other_across = coefficients(*total(1 - column))
+    along, across = coefficients(sums_ref[...])
+    other_along, other_across = coefficients(other_sums_ref[...])
     stores = []
     part_rows = people // 4
     for part in range(4):
@@ -293,12 +305,11 @@
         stores.append(copies.start(solved_ref.at[block], solved_hbm.at[block]))
     own = pl.multiple_of(column * columns, columns)
     other = pl.multiple_of((1 - column) * columns, columns)
-    here = pl.ds(0, rows)
     scores_ref[:, pl.ds(own, columns)] = norm_scale * (
-        along * direction_scores_ref[here, :] + across * scaled_scores_ref[here, :]
+        along * direction_scores_ref[pl.ds(0, rows), :] + across * own_scores_ref[...]
     )
     scores_ref[:, pl.ds(other, columns)] = norm_scale * (
-        other_along * swapped_ref[here, :] + other_across * swapped_ref[pl.ds(rows, rows), :]
+        other_along * swapped_ref[...] + other_across * other_scores_ref[...]
     )
     wait_all(stores)
 
@@ -374,69 +385,68 @@
         functools.partial(group_kernel, even), [parts] * 2, [vmem] * 2, [vmem] * 2, limit=large
     )(after(dosage, table).T, other_dosage.T)
 
-    def variant_products(values):
-        return call(
-            score_kernel, [float_of(half, 2 * share_rows, columns)] * 2, [vmem] * 3, [vmem] * 2, limit=large
-        )(*grouped, values)
-
-    def halved(values, step):
-        count = values.shape[0] // 2
-        return values[:count], swap(values[count:], "samples", devices, step)
+    products = float_of(half, 2 * share_rows, columns)
 
     partner = swap(direction, "samples", devices, half)
     near = to_mates(outgoing)
-    direction_even, direction_odd = variant_products(direction)
-    direction_share = swap(direction_odd, "samples", devices, 1)
+    direction_products = call(
+        functools.partial(score_kernel, even), float_of(devices, 2 * share_rows, columns), [vmem] * 3, vmem, limit=large
+    )(*grouped, direction)
+    direction_scores = lax.psum_scatter(
+        direction_products.reshape(2 * variants, columns), "samples", scatter_dimension=0, tiled=True
+    )
     far = to_mates(call(
         forward_kernel,
         [float_of(capacity, tile, columns)] * (half - 1),
-        [smem, vmem] + [anywhere] * (half + 1),
+        [smem, vmem] + [anywhere] * half,
         [vmem] * (half - 1),
-    )(forward, partner, *near, direction_even, direction_odd))
+    )(forward, partner, *near, direction_products))
     received = near + far + [partner.reshape(block_count, tile, columns)]
-    scaled, sums, gathered, outgoing = call(
+    scaled, own_sums, gathered, scaled_even, scaled_odd, *outgoing = call(
         functools.partial(apply_kernel, devices, capacity),
         [
             full, float_of(SUBLANES, columns), float_of(devices * capacity + block_count, tile, columns),
-            float_of(devices, tile + SUBLANES, columns),
-        ],
-        [smem] + [vmem] * (devices + 4) + [anywhere],
-        [vmem] * 4,
-    )(table, high, low, direction, diagonal, norm, *received, direction_share)
-    later = lax.all_to_all(outgoing, "samples", split_axis=0, concat_axis=0, tiled=True)
-    scaled_even, scaled_odd = variant_products(scaled)
-    scaled_sum = scaled_even + swap(scaled_odd, "samples", devices, 1)
-    direction_sum = after(direction_even, scaled) + direction_share
-    for step in steps[:-1]:
-        direction_kept, direction_taken = halved(direction_sum, step)
-        direction_sum = direction_kept + direction_taken
-    direction_kept, direction_taken = halved(direction_sum, steps[-1])
-    scaled_kept, scaled_taken = halved(scaled_sum, steps[0])
-    sums = call(
-        functools.partial(curvature_kernel, devices),
-        float_of(SUBLANES, columns),
-        [smem] + [vmem] * 7 + [anywhere] * 2,
-        vmem,
-    )(table, high, low, direction, diagonal, scaled, gathered, later, scaled_sum, direction_sum)
-    half_sum = float_of(scaled_kept.shape[0] // 2, 2 * share_rows, columns)
-    all_sums, scaled_kept, scaled_given = call(
-        add_kernel, [float_of(2 * devices, SUBLANES, columns), half_sum, half_sum], [vmem] * 3, [vmem] * 3
-    )(sums, scaled_kept, scaled_taken)
-    all_sums = lax.all_to_all(all_sums, ("samples", "cols"), split_axis=0, concat_axis=0, tiled=True)
-    scaled_sum = scaled_kept + swap(scaled_given, "samples", devices, steps[1])
-    for step in steps[2:]:
-        scaled_kept, scaled_taken = halved(scaled_sum, step)
-        scaled_sum = scaled_kept + scaled_taken
-    direction_scores = (after(direction_kept, sums) + direction_taken)[0]
-    scaled_scores = scaled_sum[0]
-    swapped = swap(jnp.concatenate([direction_scores[share_rows:], scaled_scores[share_rows:]]), "cols", 2, 1)
+            products, products,
+        ] + [float_of(tile + SUBLANES, columns)] * (devices - 1),
+        [smem] + [vmem] * (devices + 6),
+        [vmem] * (devices + 4),
+        limit=large,
+    )(table, high, low, direction, diagonal, norm, *grouped, *received)
+    scaled_share = swap(scaled_odd, "samples", devices, 1)
+    order = [k for k in range(half, devices)] + near_by
+    later = [swap(outgoing[k - 1], "samples", devices, k) for k in order]
+    rows = float_of(half // 2, 2 * share_rows, columns)
+    kept, given = call(add_kernel, [rows] * 2, [vmem] * 2, [vmem] * 2)(scaled_even, scaled_share)
+    taken = swap(given, "samples", devices, steps[0])
+    first_sums, sums = call(
+        functools.partial(curvature_kernel, order),
+        [float_of(SUBLANES, columns)] * 2,
+        [smem] + [vmem] * (devices + 6) + [anywhere],
+        [vmem] * 2,
+        [room(devices, tile, columns)],
+    )(table, high, low, direction, diagonal, scaled, own_sums, gathered, *later, given)
+    for step in steps[1:]:
+        rows = float_of(kept.shape[0] // 2, 2 * share_rows, columns)
+        kept, given = call(
+            add_kernel, [rows] * 2, [vmem] * 2 + [anywhere], [vmem] * 2
+        )(kept, taken, sums)
+        taken = swap(given, "samples", devices, step)
+    for step in [1] + steps:
+        sums = sums + swap(sums, "samples", devices, step)
+    sums = sums + first_sums
+    rows = float_of(share_rows, columns)
+    own_scores, other_scores = call(last_add_kernel, [rows] * 2, [vmem] * 2, [vmem] * 2)(kept, taken)
     solved, scores = call(
-        functools.partial(finish_kernel, devices, 1.0 / math.sqrt(people * devices)),
+        functools.partial(finish_kernel, 1.0 / math.sqrt(people * devices)),
         [full, float_of(share_rows, 2 * columns)],
-        [vmem] * 6,
+        [vmem] * 8,
         [hbm, vmem],
         [full_room, pltpu.SemaphoreType.DMA((4,))],
-    )(direction, scaled, direction_scores, scaled_scores, swapped, all_sums)
+    )(
+        direction, scaled, direction_scores, own_scores,
+        *(swap(rows, "cols", 2, 1) for rows in (direction_scores[share_rows:], other_scores)),
+        sums, swap(sums, "cols", 2, 1),
+    )
     return (solved, scores)
 
 

time: 123 us -> 146 us (1.19)
  between operations: 0.85 us -> 14.2 us
  starting transfers between devices: 35.2 us -> 44.2 us
  waiting for transfers between devices: 52.5 us -> 61.3 us
  local copies, waits for them, and re-layouts: 19.6 us -> 16.3 us
  Pallas kernels: 12.8 us -> 10 us
    ppermute x15 -> x24, starting transfers between devices: 23.7 us -> 44.2 us  [swap(): return lax.ppermute(values, axis, [(i, i ^ step) for i in range(devices)])]
    all_to_all x2 -> x0, starting transfers between devices: 11.6 us -> none  [the longest x1 6.72 us: per_device(): lax.all_to_all(outgoing, 'samples', split_axis=0, concat_axis=0, tiled=True)]
    ppermute x15 -> x24, waiting for transfers between devices: 52.5 us -> 61.2 us  [swap(): return lax.ppermute(values, axis, [(i, i ^ step) for i in range(devices)])]
    unnamed x42 -> x38, local copies, waits for them, and re-layouts: 15.1 us -> 12.8 us
    slice x4 -> x0, local copies, waits for them, and re-layouts: 1.57 us -> none  [the longest x3 1.56 us: halved(): return (values[:count], swap(values[count:], 'samples', devices, step))]
    pallas_call x5 -> x6, Pallas kernels: 6.59 us -> 5.13 us  [the longest x1 2.02 us: per_device(): call(functools.partial(score_kernel, even), float_of(devices, 2 * share_r...]
  transfers between devices with their start and end apart: 17 -> 25, of which waited for: 9 -> 14; matrix products, arithmetic and copies ran while one was open for 5% -> 1% of each run, Pallas kernels for 7% -> 3%
where the time goes in v11:
time: 146 us
  waiting for transfers between devices  61.3 us (42%)
  starting transfers between devices  44.2 us (30%)
  local copies, waits for them, and re-layouts  16.3 us (11%)
  between operations  14.2 us (10%)
  Pallas kernels  10 us (7%)
    ppermute x24, waiting for transfers between devices, swap(): return lax.ppermute(values, axis, [(i, i ^ step) for i in range(devices)])  61.2 us
    ppermute x24, starting transfers between devices, swap(): return lax.ppermute(values, axis, [(i, i ^ step) for i in range(devices)])  44.2 us
    unnamed x38, local copies, waits for them, and re-layouts  12.8 us
  transfers between devices with their start and end apart: 25, of which 14 were waited for; matrix products, arithmetic and copies ran while one was open for 1% of the time, Pallas kernels for 3%

profile of v11, /device:TPU:0, one launch (start us, length us, event | category | flops | bytes accessed | tf_op | source)
XLA Modules:
  0.0 146.0 jit_solution(14088739490129790651)
XLA Ops:
  10.9 2.5 %collective-permute-done.gate_ref = f32[512,512]{1,0:T(8,128)S(1)} collective-permute-done((f32[512,512]{1,0:T(8,128)}, f32[512,512]{1,0:T(8,128)S(1)}, u32[]{:S(2)}, u32[]{:S(2)}) %collective-permute-start) | collective-permute-done | bytes 1048608 | tf_op jit(solution)/shard_map/ppermute | solution.py:329
  14.0 1.6 %shard_map.69 = (s32[4,12]{1,0:T(4,128)S(1)}, s32[2,4]{1,0:T(2,128)S(1)}, bf16[4,128,512]{2,1,0:T(8,128)(2,1)S(1)}, bf16[4,128,512]{2,1,0:T(8,128)(2,1)S(1)}, f3...) custom-call(s32[3,32]{1,0:T(4,128)S(1)} %bitcast.10, ...), custom_call_target="tpu_custom_call" | custom-call | tf_op jit(solution)/shard_map/pallas_call | solution.py:369
  24.8 2.0 %shard_map.71.refs_3_ = f32[8,128,256]{2,1,0:T(8,128)} custom-call(bf16[2,512,512]{2,1,0:T(8,128)(2,1)S(1)} %get-tuple-element.47.high_ref.dosage_high_ref, bf16[2,512,512]{2,1,0:T(8,128)(2,1)S(1)} %get-tuple-element.48.low_ref.dosage_low_ref, f32[512,256]{1,0:T(8,128)S(1)} %get-tuple-element.39.direction_ref.values_ref), custom_call_target="tpu_custom_call" | custom-call | tf_op jit(solution)/shard_map/pallas_call | solution.py:392
  26.8 4.0 %collective-permute-start.4 = (f32[512,256]{1,0:T(8,128)S(1)}, f32[512,256]{1,0:T(8,128)S(1)}, u32[]{:S(2)}, u32[]{:S(2)}) collective-permute-start(f32[512,256]{1,0:T(8,128)S(1)} %get-tuple-element.39.direction_ref.values_ref), channel_id=1, source_target_pairs={{0,8},{2,10},{4,12},{6,14},{8,0},{10,2},{12,4},{14,6},{1,9},{3,11}... | collective-permute-start | bytes 1572872 | tf_op jit(solution)/shard_map/ppermute | solution.py:329
  34.3 25.8 %collective-permute-done.4.partner_ref = f32[512,256]{1,0:T(8,128)S(1)} collective-permute-done((f32[512,256]{1,0:T(8,128)S(1)}, f32[512,256]{1,0:T(8,128)S(1)}, u32[]{:S(2)}, u32[]{:S(2)}) %collective-permute-start.4) | collective-permute-done | bytes 524320 | tf_op jit(solution)/shard_map/ppermute | solution.py:329
  60.2 1.9 %collective-permute-done.3.refs_2_ = f32[2,128,256]{2,1,0:T(8,128)S(1)} collective-permute-done((f32[2,128,256]{2,1,0:T(8,128)S(1)}, f32[2,128,256]{2,1,0:T(8,128)S(1)}, u32[]{:S(2)}, u32[]{:S(2)}) %collective-permute-start.3) | collective-permute-done | bytes 262176 | tf_op jit(solution)/shard_map/ppermute | solution.py:329
  62.7 2.2 %collective-permute-start.5 = (f32[2,128,256]{2,1,0:T(8,128)S(1)}, f32[2,128,256]{2,1,0:T(8,128)S(1)}, u32[]{:S(2)}, u32[]{:S(2)}) collective-permute-start(f32[2,128,256]{2,1,0:T(8,128)S(1)} %get-tuple-element.53), channel_id=1, source_target_pairs={{0,2},{2,0},{4,6},{6,4},{8,10},{10,8},{12,14},{14,12},{1,3},{3,1},... | collective-permute-start | bytes 786440 | tf_op jit(solution)/shard_map/ppermute | solution.py:329
  66.4 5.4 %collective-permute-done.5.refs_3_ = f32[2,128,256]{2,1,0:T(8,128)S(1)} collective-permute-done((f32[2,128,256]{2,1,0:T(8,128)S(1)}, f32[2,128,256]{2,1,0:T(8,128)S(1)}, u32[]{:S(2)}, u32[]{:S(2)}) %collective-permute-start.5) | collective-permute-done | bytes 262176 | tf_op jit(solution)/shard_map/ppermute | solution.py:329
  71.8 2.4 %collective-permute-done.6.refs_4_ = f32[2,128,256]{2,1,0:T(8,128)S(1)} collective-permute-done((f32[2,128,256]{2,1,0:T(8,128)S(1)}, f32[2,128,256]{2,1,0:T(8,128)S(1)}, u32[]{:S(2)}, u32[]{:S(2)}) %collective-permute-start.6) | collective-permute-done | bytes 262176 | tf_op jit(solution)/shard_map/ppermute | solution.py:329
  74.2 2.9 %collective-permute-done.7.refs_5_ = f32[2,128,256]{2,1,0:T(8,128)S(1)} collective-permute-done((f32[2,128,256]{2,1,0:T(8,128)S(1)}, f32[2,128,256]{2,1,0:T(8,128)S(1)}, u32[]{:S(2)}, u32[]{:S(2)}) %collective-permute-start.7) | collective-permute-done | bytes 262176 | tf_op jit(solution)/shard_map/ppermute | solution.py:329
  79.3 2.3 %shard_map.73 = (f32[512,256]{1,0:T(8,128)S(1)}, f32[8,256]{1,0:T(8,128)S(1)}, f32[20,128,256]{2,1,0:T(8,128)S(1)}, f32[4,128,256]{2,1,0:T(8,128)S(1)}, f32[4,12...) custom-call(s32[4,12]{1,0:T(4,128)S(1)} %get-tuple-element.41.table_, ...), custom_call_target="tpu_custom_call" | custom-call | tf_op jit(solution)/shard_map/pallas_call | solution.py:405
  83.0 3.4 %collective-permute-start.10 = (f32[136,256]{1,0:T(8,128)S(1)}, f32[136,256]{1,0:T(8,128)S(1)}, u32[]{:S(2)}, u32[]{:S(2)}) collective-permute-start(f32[136,256]{1,0:T(8,128)S(1)} %get-tuple-element.63), channel_id=1, source_target_pairs={{0,8},{2,10},{4,12},{6,14},{8,0},{10,2},{12,4},{14,6},{1,9},{3,11}... | collective-permute-start | bytes 417800 | tf_op jit(solution)/shard_map/ppermute | solution.py:329
  86.4 3.1 %collective-permute-start.12 = (f32[136,256]{1,0:T(8,128)S(1)}, f32[136,256]{1,0:T(8,128)S(1)}, u32[]{:S(2)}, u32[]{:S(2)}) collective-permute-start(f32[136,256]{1,0:T(8,128)S(1)} %get-tuple-element.65), channel_id=1, source_target_pairs={{0,12},{2,14},{4,8},{6,10},{8,4},{10,6},{12,0},{14,2},{1,13},{3,15... | collective-permute-start | bytes 417800 | tf_op jit(solution)/shard_map/ppermute | solution.py:329
  89.5 3.8 %collective-permute-done.8.taken_ref = f32[4,128,256]{2,1,0:T(8,128)S(1)} collective-permute-done((f32[4,128,256]{2,1,0:T(8,128)S(1)}, f32[4,128,256]{2,1,0:T(8,128)S(1)}, u32[]{:S(2)}, u32[]{:S(2)}) %collective-permute-start.8) | collective-permute-done | bytes 524320 | tf_op jit(solution)/shard_map/ppermute | solution.py:329
  93.3 7.4 %collective-permute-start.9 = (f32[2,128,256]{2,1,0:T(8,128)S(1)}, f32[2,128,256]{2,1,0:T(8,128)S(1)}, u32[]{:S(2)}, u32[]{:S(2)}) collective-permute-start(f32[2,128,256]{2,1,0:T(8,128)S(1)} %get-tuple-element.60.refs_7_), channel_id=1, source_target_pairs={{0,4},{2,6},{4,0},{6,2},{8,12},{10,14},{12,8},{14,10},{1,5},{3,7},... | collective-permute-start | bytes 786440 | tf_op jit(solution)/shard_map/ppermute | solution.py:329
  100.7 4.7 %collective-permute-start.13 = (f32[136,256]{1,0:T(8,128)S(1)}, f32[136,256]{1,0:T(8,128)S(1)}, u32[]{:S(2)}, u32[]{:S(2)}) collective-permute-start(f32[136,256]{1,0:T(8,128)S(1)} %get-tuple-element.66), channel_id=1, source_target_pairs={{0,14},{2,12},{4,10},{6,8},{8,6},{10,4},{12,2},{14,0},{1,15},{3,13... | collective-permute-start | bytes 417800 | tf_op jit(solution)/shard_map/ppermute | solution.py:329
  106.8 5.3 %collective-permute-start.16 = (f32[136,256]{1,0:T(8,128)S(1)}, f32[136,256]{1,0:T(8,128)S(1)}, u32[]{:S(2)}, u32[]{:S(2)}) collective-permute-start(f32[136,256]{1,0:T(8,128)S(1)} %get-tuple-element.69), channel_id=1, source_target_pairs={{0,6},{2,4},{4,2},{6,0},{8,14},{10,12},{12,10},{14,8},{1,7},{3,5},... | collective-permute-start | bytes 417800 | tf_op jit(solution)/shard_map/ppermute | solution.py:329
  112.2 3.5 %collective-permute-done.13.refs_3_ = f32[136,256]{1,0:T(8,128)S(1)} collective-permute-done((f32[136,256]{1,0:T(8,128)S(1)}, f32[136,256]{1,0:T(8,128)S(1)}, u32[]{:S(2)}, u32[]{:S(2)}) %collective-permute-start.13) | collective-permute-done | bytes 139296 | tf_op jit(solution)/shard_map/ppermute | solution.py:329
  115.7 1.7 %collective-permute-done.15.refs_5_ = f32[136,256]{1,0:T(8,128)S(1)} collective-permute-done((f32[136,256]{1,0:T(8,128)S(1)}, f32[136,256]{1,0:T(8,128)S(1)}, u32[]{:S(2)}, u32[]{:S(2)}) %collective-permute-start.15) | collective-permute-done | bytes 139296 | tf_op jit(solution)/shard_map/ppermute | solution.py:329
  117.3 2.8 %collective-permute-done.16.refs_6_ = f32[136,256]{1,0:T(8,128)S(1)} collective-permute-done((f32[136,256]{1,0:T(8,128)S(1)}, f32[136,256]{1,0:T(8,128)S(1)}, u32[]{:S(2)}, u32[]{:S(2)}) %collective-permute-start.16) | collective-permute-done | bytes 139296 | tf_op jit(solution)/shard_map/ppermute | solution.py:329
  123.6 2.9 %collective-permute-done.20 = f32[8,256]{1,0:T(8,128)S(1)} collective-permute-done((f32[8,256]{1,0:T(8,128)S(1)}, f32[8,256]{1,0:T(8,128)S(1)}, u32[]{:S(2)}, u32[]{:S(2)}) %collective-permute-start.20) | collective-permute-done | bytes 8224 | tf_op jit(solution)/shard_map/ppermute | solution.py:329
  126.5 2.1 %collective-permute-start.21 = (f32[8,256]{1,0:T(8,128)S(1)}, f32[8,256]{1,0:T(8,128)S(1)}, u32[]{:S(2)}, u32[]{:S(2)}) collective-permute-start(f32[8,256]{1,0:T(8,128)S(1)} %add.14), channel_id=1, source_target_pairs={{0,4},{2,6},{4,0},{6,2},{8,12},{10,14},{12,8},{14,10},{1,5},{3,7},... | collective-permute-start | bytes 24584 | tf_op jit(solution)/shard_map/ppermute | solution.py:329
  128.6 2.4 %collective-permute-done.21 = f32[8,256]{1,0:T(8,128)S(1)} collective-permute-done((f32[8,256]{1,0:T(8,128)S(1)}, f32[8,256]{1,0:T(8,128)S(1)}, u32[]{:S(2)}, u32[]{:S(2)}) %collective-permute-start.21) | collective-permute-done | bytes 8224 | tf_op jit(solution)/shard_map/ppermute | solution.py:329
  133.5 2.1 %collective-permute-done.22 = f32[8,256]{1,0:T(8,128)S(1)} collective-permute-done((f32[8,256]{1,0:T(8,128)S(1)}, f32[8,256]{1,0:T(8,128)S(1)}, u32[]{:S(2)}, u32[]{:S(2)}) %collective-permute-start.22) | collective-permute-done | bytes 8224 | tf_op jit(solution)/shard_map/ppermute | solution.py:329
  (82 shorter events, 33.5 us)
Async XLA Ops:
  7.2 125.0 %reduce-scatter.2.cloned.1.call-start = ((), (), s32[]{:S(2)}) async-start(), calls=%async_computation.1 | async-start | bytes 1179648 | tf_op jit(solution)/shard_map/reduce_scatter | solution.py:395
  10.3 3.0 %collective-permute-start = (f32[512,512]{1,0:T(8,128)}, f32[512,512]{1,0:T(8,128)S(1)}, u32[]{:S(2)}, u32[]{:S(2)}) collective-permute-start(f32[512,512]{1,0:T(8,128)} %param.9), channel_id=1, source_target_pairs={{0,1},{1,0},{2,3},{3,2},{4,5},{5,4},{6,7},{7,6},{8,9},{9,8},{10,11... | collective-permute-start | bytes 3145736 | tf_op jit(solution)/shard_map/ppermute | solution.py:329
  26.8 33.4 %collective-permute-start.4 = (f32[512,256]{1,0:T(8,128)S(1)}, f32[512,256]{1,0:T(8,128)S(1)}, u32[]{:S(2)}, u32[]{:S(2)}) collective-permute-start(f32[512,256]{1,0:T(8,128)S(1)} %get-tuple-element.39.direction_ref.values_ref), channel_id=1, source_target_pairs={{0,8},{2,10},{4,12},{6,14},{8,0},{10,2},{12,4},{14,6},{1,9},{3,11}... | collective-permute-start | bytes 1572872 | tf_op jit(solution)/shard_map/ppermute | solution.py:329
  30.8 29.3 %collective-permute-start.1 = (f32[2,128,256]{2,1,0:T(8,128)}, f32[2,128,256]{2,1,0:T(8,128)S(1)}, u32[]{:S(2)}, u32[]{:S(2)}) collective-permute-start(f32[2,128,256]{2,1,0:T(8,128)} %copy-done.17), channel_id=1, source_target_pairs={{0,2},{2,0},{4,6},{6,4},{8,10},{10,8},{12,14},{14,12},{1,3},{3,1},... | collective-permute-start | bytes 786440 | tf_op jit(solution)/shard_map/ppermute | solution.py:329
  32.4 27.8 %collective-permute-start.2 = (f32[2,128,256]{2,1,0:T(8,128)S(1)}, f32[2,128,256]{2,1,0:T(8,128)S(1)}, u32[]{:S(2)}, u32[]{:S(2)}) collective-permute-start(f32[2,128,256]{2,1,0:T(8,128)S(1)} %copy-done.16), channel_id=1, source_target_pairs={{0,4},{2,6},{4,0},{6,2},{8,12},{10,14},{12,8},{14,10},{1,5},{3,7},... | collective-permute-start | bytes 786440 | tf_op jit(solution)/shard_map/ppermute | solution.py:329
  33.9 28.1 %collective-permute-start.3 = (f32[2,128,256]{2,1,0:T(8,128)S(1)}, f32[2,128,256]{2,1,0:T(8,128)S(1)}, u32[]{:S(2)}, u32[]{:S(2)}) collective-permute-start(f32[2,128,256]{2,1,0:T(8,128)S(1)} %copy-done.14), channel_id=1, source_target_pairs={{0,6},{2,4},{4,2},{6,0},{8,14},{10,12},{12,10},{14,8},{1,7},{3,5},... | collective-permute-start | bytes 786440 | tf_op jit(solution)/shard_map/ppermute | solution.py:329
  62.7 9.1 %collective-permute-start.5 = (f32[2,128,256]{2,1,0:T(8,128)S(1)}, f32[2,128,256]{2,1,0:T(8,128)S(1)}, u32[]{:S(2)}, u32[]{:S(2)}) collective-permute-start(f32[2,128,256]{2,1,0:T(8,128)S(1)} %get-tuple-element.53), channel_id=1, source_target_pairs={{0,2},{2,0},{4,6},{6,4},{8,10},{10,8},{12,14},{14,12},{1,3},{3,1},... | collective-permute-start | bytes 786440 | tf_op jit(solution)/shard_map/ppermute | solution.py:329
  64.9 9.3 %collective-permute-start.6 = (f32[2,128,256]{2,1,0:T(8,128)S(1)}, f32[2,128,256]{2,1,0:T(8,128)S(1)}, u32[]{:S(2)}, u32[]{:S(2)}) collective-permute-start(f32[2,128,256]{2,1,0:T(8,128)S(1)} %get-tuple-element.54), channel_id=1, source_target_pairs={{0,4},{2,6},{4,0},{6,2},{8,12},{10,14},{12,8},{14,10},{1,5},{3,7},... | collective-permute-start | bytes 786440 | tf_op jit(solution)/shard_map/ppermute | solution.py:329
  64.9 12.3 %collective-permute-start.7 = (f32[2,128,256]{2,1,0:T(8,128)S(1)}, f32[2,128,256]{2,1,0:T(8,128)S(1)}, u32[]{:S(2)}, u32[]{:S(2)}) collective-permute-start(f32[2,128,256]{2,1,0:T(8,128)S(1)} %get-tuple-element.55), channel_id=1, source_target_pairs={{0,6},{2,4},{4,2},{6,0},{8,14},{10,12},{12,10},{14,8},{1,7},{3,5},... | collective-permute-start | bytes 786440 | tf_op jit(solution)/shard_map/ppermute | solution.py:329
  81.5 11.7 %collective-permute-start.8 = (f32[4,128,256]{2,1,0:T(8,128)S(1)}, f32[4,128,256]{2,1,0:T(8,128)S(1)}, u32[]{:S(2)}, u32[]{:S(2)}) collective-permute-start(f32[4,128,256]{2,1,0:T(8,128)S(1)} %get-tuple-element.58), channel_id=1, source_target_pairs={{0,2},{2,0},{4,6},{6,4},{8,10},{10,8},{12,14},{14,12},{1,3},{3,1},... | collective-permute-start | bytes 1572872 | tf_op jit(solution)/shard_map/ppermute | solution.py:329
  83.0 22.4 %collective-permute-start.10 = (f32[136,256]{1,0:T(8,128)S(1)}, f32[136,256]{1,0:T(8,128)S(1)}, u32[]{:S(2)}, u32[]{:S(2)}) collective-permute-start(f32[136,256]{1,0:T(8,128)S(1)} %get-tuple-element.63), channel_id=1, source_target_pairs={{0,8},{2,10},{4,12},{6,14},{8,0},{10,2},{12,4},{14,6},{1,9},{3,11}... | collective-permute-start | bytes 417800 | tf_op jit(solution)/shard_map/ppermute | solution.py:329
  86.4 19.3 %collective-permute-start.11 = (f32[136,256]{1,0:T(8,128)S(1)}, f32[136,256]{1,0:T(8,128)S(1)}, u32[]{:S(2)}, u32[]{:S(2)}) collective-permute-start(f32[136,256]{1,0:T(8,128)S(1)} %get-tuple-element.64), channel_id=1, source_target_pairs={{0,10},{2,8},{4,14},{6,12},{8,2},{10,0},{12,6},{14,4},{1,11},{3,9}... | collective-permute-start | bytes 417800 | tf_op jit(solution)/shard_map/ppermute | solution.py:329
  86.4 20.4 %collective-permute-start.12 = (f32[136,256]{1,0:T(8,128)S(1)}, f32[136,256]{1,0:T(8,128)S(1)}, u32[]{:S(2)}, u32[]{:S(2)}) collective-permute-start(f32[136,256]{1,0:T(8,128)S(1)} %get-tuple-element.65), channel_id=1, source_target_pairs={{0,12},{2,14},{4,8},{6,10},{8,4},{10,6},{12,0},{14,2},{1,13},{3,15... | collective-permute-start | bytes 417800 | tf_op jit(solution)/shard_map/ppermute | solution.py:329
  93.3 28.4 %collective-permute-start.9 = (f32[2,128,256]{2,1,0:T(8,128)S(1)}, f32[2,128,256]{2,1,0:T(8,128)S(1)}, u32[]{:S(2)}, u32[]{:S(2)}) collective-permute-start(f32[2,128,256]{2,1,0:T(8,128)S(1)} %get-tuple-element.60.refs_7_), channel_id=1, source_target_pairs={{0,4},{2,6},{4,0},{6,2},{8,12},{10,14},{12,8},{14,10},{1,5},{3,7},... | collective-permute-start | bytes 786440 | tf_op jit(solution)/shard_map/ppermute | solution.py:329
  100.7 14.9 %collective-permute-start.13 = (f32[136,256]{1,0:T(8,128)S(1)}, f32[136,256]{1,0:T(8,128)S(1)}, u32[]{:S(2)}, u32[]{:S(2)}) collective-permute-start(f32[136,256]{1,0:T(8,128)S(1)} %get-tuple-element.66), channel_id=1, source_target_pairs={{0,14},{2,12},{4,10},{6,8},{8,6},{10,4},{12,2},{14,0},{1,15},{3,13... | collective-permute-start | bytes 417800 | tf_op jit(solution)/shard_map/ppermute | solution.py:329
  105.5 10.2 %collective-permute-start.14 = (f32[136,256]{1,0:T(8,128)S(1)}, f32[136,256]{1,0:T(8,128)S(1)}, u32[]{:S(2)}, u32[]{:S(2)}) collective-permute-start(f32[136,256]{1,0:T(8,128)S(1)} %get-tuple-element.67), channel_id=1, source_target_pairs={{0,2},{2,0},{4,6},{6,4},{8,10},{10,8},{12,14},{14,12},{1,3},{3,1},... | collective-permute-start | bytes 417800 | tf_op jit(solution)/shard_map/ppermute | solution.py:329
  105.7 11.6 %collective-permute-start.15 = (f32[136,256]{1,0:T(8,128)S(1)}, f32[136,256]{1,0:T(8,128)S(1)}, u32[]{:S(2)}, u32[]{:S(2)}) collective-permute-start(f32[136,256]{1,0:T(8,128)S(1)} %get-tuple-element.68), channel_id=1, source_target_pairs={{0,4},{2,6},{4,0},{6,2},{8,12},{10,14},{12,8},{14,10},{1,5},{3,7},... | collective-permute-start | bytes 417800 | tf_op jit(solution)/shard_map/ppermute | solution.py:329
  106.8 13.3 %collective-permute-start.16 = (f32[136,256]{1,0:T(8,128)S(1)}, f32[136,256]{1,0:T(8,128)S(1)}, u32[]{:S(2)}, u32[]{:S(2)}) collective-permute-start(f32[136,256]{1,0:T(8,128)S(1)} %get-tuple-element.69), channel_id=1, source_target_pairs={{0,6},{2,4},{4,2},{6,0},{8,14},{10,12},{12,10},{14,8},{1,7},{3,5},... | collective-permute-start | bytes 417800 | tf_op jit(solution)/shard_map/ppermute | solution.py:329
  121.7 10.3 %collective-permute-start.17 = (f32[1,128,256]{2,1,0:T(8,128)S(1)}, f32[1,128,256]{2,1,0:T(8,128)S(1)}, u32[]{:S(2)}, u32[]{:S(2)}) collective-permute-start(f32[1,128,256]{2,1,0:T(8,128)S(1)} %get-tuple-element.72), channel_id=1, source_target_pairs={{0,8},{2,10},{4,12},{6,14},{8,0},{10,2},{12,4},{14,6},{1,9},{3,11}... | collective-permute-start | bytes 393224 | tf_op jit(solution)/shard_map/ppermute | solution.py:329
  122.8 3.7 %collective-permute-start.20 = (f32[8,256]{1,0:T(8,128)S(1)}, f32[8,256]{1,0:T(8,128)S(1)}, u32[]{:S(2)}, u32[]{:S(2)}) collective-permute-start(f32[8,256]{1,0:T(8,128)S(1)} %get-tuple-element.70.refs_0_), channel_id=1, source_target_pairs={{0,2},{2,0},{4,6},{6,4},{8,10},{10,8},{12,14},{14,12},{1,3},{3,1},... | collective-permute-start | bytes 24584 | tf_op jit(solution)/shard_map/ppermute | solution.py:329
  126.5 4.5 %collective-permute-start.21 = (f32[8,256]{1,0:T(8,128)S(1)}, f32[8,256]{1,0:T(8,128)S(1)}, u32[]{:S(2)}, u32[]{:S(2)}) collective-permute-start(f32[8,256]{1,0:T(8,128)S(1)} %add.14), channel_id=1, source_target_pairs={{0,4},{2,6},{4,0},{6,2},{8,12},{10,14},{12,8},{14,10},{1,5},{3,7},... | collective-permute-start | bytes 24584 | tf_op jit(solution)/shard_map/ppermute | solution.py:329
  131.0 4.5 %collective-permute-start.22 = (f32[8,256]{1,0:T(8,128)S(1)}, f32[8,256]{1,0:T(8,128)S(1)}, u32[]{:S(2)}, u32[]{:S(2)}) collective-permute-start(f32[8,256]{1,0:T(8,128)S(1)} %add.15), channel_id=1, source_target_pairs={{0,8},{2,10},{4,12},{6,14},{8,0},{10,2},{12,4},{14,6},{1,9},{3,11}... | collective-permute-start | bytes 24584 | tf_op jit(solution)/shard_map/ppermute | solution.py:329
  132.0 4.7 %collective-permute-start.19 = (f32[64,256]{1,0:T(8,128)S(1)}, f32[64,256]{1,0:T(8,128)S(1)}, u32[]{:S(2)}, u32[]{:S(2)}) collective-permute-start(f32[64,256]{1,0:T(8,128)S(1)} %get-tuple-element.74), channel_id=1, source_target_pairs={{0,1},{1,0},{2,3},{3,2},{4,5},{5,4},{6,7},{7,6},{8,9},{9,8},{10,11... | collective-permute-start | bytes 196616 | tf_op jit(solution)/shard_map/ppermute | solution.py:329
  133.0 3.7 %collective-permute-start.18 = (f32[64,256]{1,0:T(8,128)S(1)}, f32[64,256]{1,0:T(8,128)S(1)}, u32[]{:S(2)}, u32[]{:S(2)}) collective-permute-start(f32[64,256]{1,0:T(8,128)S(1)} %slice.4), channel_id=1, source_target_pairs={{0,1},{1,0},{2,3},{3,2},{4,5},{5,4},{6,7},{7,6},{8,9},{9,8},{10,11... | collective-permute-start | bytes 196616 | tf_op jit(solution)/shard_map/ppermute | solution.py:329
  (20 other events, 121.7 us)
Sparse Core Ops, SparseCore 0:
  26.9 80.8 reduce-scatter.1

commit v12 on v10

--- a/solution.py
+++ b/solution.py
@@ -178,30 +178,49 @@
         gathered_ref[pl.ds((mate ^ half) * capacity, capacity)] = far_refs[k - 1][...]
 
 
-def apply_kernel(devices, capacity, table_ref, high_ref, low_ref, direction_ref, diagonal_ref, norm_ref, *refs):
+def score_products(high_ref, low_ref, values, even_ref, odd_ref):
+    count, rows = even_ref.shape[:2]
+    for odd, out_ref in enumerate((even_ref, odd_ref)):
+        for i in range(0, count, 4):
+            here = pl.ds(i * rows, 4 * rows)
+            total = product(high_ref[odd, here, :], low_ref[odd, here, :], [values])
+            out_ref[pl.ds(i, 4)] = total.reshape(4, rows, -1)
+
+
+def score_kernel(high_ref, low_ref, values_ref, even_ref, odd_ref):
+    score_products(high_ref, low_ref, values_ref[...], even_ref, odd_ref)
+
+
+def apply_kernel(devices, capacity, table_ref, high_ref, low_ref, direction_ref, diagonal_ref, norm_ref,
+                 dosage_high_ref, dosage_low_ref, *refs):
     received_refs = refs[:devices - 1]
-    scaled_ref, sums_ref, gathered_ref, outgoing_ref = refs[-4:]
+    scaled_ref, handled_ref, outgoing_ref, even_ref, odd_ref, gathered_ref = refs[-6:]
     gather_received(devices, capacity, received_refs, gathered_ref)
     block_count, tile, depth = high_ref.shape
     others = depth // tile - 1
-    cross = jnp.zeros(sums_ref.shape, jnp.float32)
+    cross = jnp.zeros(norm_ref.shape, jnp.float32)
     for row in range(block_count):
         block = pl.ds(row * tile, tile)
         here = direction_ref[block, :]
-        blocks = [here] + [gathered_ref[table_ref[0, row * others + i]] for i in range(others)]
-        mapped = product(high_ref[row], low_ref[row], blocks)
+        blocks = [gathered_ref[table_ref[0, row * others + i]] for i in range(others)]
+        weights = [table_ref[2, row * others + i].astype(jnp.float32) for i in range(others)]
+        mapped = product(high_ref[row], low_ref[row], [here] + blocks)
+        far = pl.ds(tile, depth - tile)
+        handled_ref[block, :] = product(
+            high_ref[row, :, far], low_ref[row, :, far], [weight * there for weight, there in zip(weights, blocks)]
+        )
         scaled_ref[block, :] = mapped * (1.0 / diagonal_ref[block, :])
         cross = cross + column_sums(here * mapped)
     row_ids = lax.broadcasted_iota(jnp.int32, cross.shape, 0)
     sums = jnp.where(row_ids == 1, jnp.sum(cross, axis=0, keepdims=True), norm_ref[...])
-    sums_ref[...] = sums
     for other in range(devices):
         start = pl.multiple_of(table_ref[3, other] * tile, tile)
         outgoing_ref[other, pl.ds(0, tile), :] = scaled_ref[pl.ds(start, tile), :]
         outgoing_ref[other, pl.ds(tile, SUBLANES), :] = sums
-
-
-def curvature_kernel(devices, table_ref, high_ref, low_ref, direction_ref, diagonal_ref, scaled_ref, gathered_ref,
+    score_products(dosage_high_ref, dosage_low_ref, scaled_ref[...], even_ref, odd_ref)
+
+
+def curvature_kernel(devices, table_ref, high_ref, low_ref, direction_ref, diagonal_ref, scaled_ref, handled_ref,
                      later_ref, *refs):
     sums_ref = refs[-1]
     block_count, tile, depth = high_ref.shape
@@ -219,22 +238,30 @@
         for i in range(others):
             entry = row * others + i
             weight = table_ref[2, entry].astype(jnp.float32)
-            there = later_ref[table_ref[1, entry], pl.ds(0, tile), :]
-            blocks.append(weight * (there - rho * gathered_ref[table_ref[0, entry]]))
-        mapped = product(high_ref[row], low_ref[row], blocks)
+            blocks.append(weight * later_ref[table_ref[1, entry], pl.ds(0, tile), :])
+        mapped = product(high_ref[row], low_ref[row], blocks) - rho * handled_ref[block, :]
         norm = norm + column_sums(here * here * diagonal_ref[block, :])
         bend = bend + column_sums(here * mapped)
     row_ids = lax.broadcasted_iota(jnp.int32, first_sums.shape, 0)
     sums = jnp.where(row_ids == 2, jnp.sum(norm, axis=0, keepdims=True), first_sums)
-    sums_ref[...] = jnp.where(row_ids == 3, jnp.sum(bend, axis=0, keepdims=True), sums)
-
-
-def add_kernel(sums_ref, kept_ref, taken_ref, all_sums_ref, near_ref, far_ref):
+    sums = jnp.where(row_ids == 3, jnp.sum(bend, axis=0, keepdims=True), sums)
+    for i in range(2 * devices):
+        sums_ref[i] = sums
+
+
+def add_kernel(kept_ref, taken_ref, near_ref, far_ref):
     count = near_ref.shape[0]
     near_ref[...] = kept_ref[pl.ds(0, count)] + taken_ref[pl.ds(0, count)]
     far_ref[...] = kept_ref[pl.ds(count, count)] + taken_ref[pl.ds(count, count)]
-    for i in range(all_sums_ref.shape[0]):
-        all_sums_ref[i] = sums_ref[...]
+
+
+def last_add_kernel(first_kept_ref, first_taken_ref, second_kept_ref, second_taken_ref, gate_ref, own_ref, other_ref):
+    rows = own_ref.shape[1]
+    for i, (kept_ref, taken_ref) in enumerate(
+        ((first_kept_ref, first_taken_ref), (second_kept_ref, second_taken_ref))
+    ):
+        own_ref[i] = kept_ref[0, pl.ds(0, rows), :] + taken_ref[0, pl.ds(0, rows), :]
+        other_ref[i] = kept_ref[0, pl.ds(rows, rows), :] + taken_ref[0, pl.ds(rows, rows), :]
 
 
 def group_kernel(order, own_ref, other_ref, high_ref, low_ref):
@@ -250,15 +277,6 @@
                 low_ref[odd, here, :] = low
 
 
-def score_kernel(high_ref, low_ref, values_ref, even_ref, odd_ref):
-    count, rows = even_ref.shape[:2]
-    for odd, out_ref in enumerate((even_ref, odd_ref)):
-        for i in range(0, count, 4):
-            here = pl.ds(i * rows, 4 * rows)
-            total = product(high_ref[odd, here, :], low_ref[odd, here, :], [values_ref[...]])
-            out_ref[pl.ds(i, 4)] = total.reshape(4, rows, -1)
-
-
 def coefficients(sums, shared):
     norm, cross = sums[0:1, :], sums[1:2, :]
     later_norm, bend = shared[2:3, :], shared[3:4, :]
@@ -269,10 +287,9 @@
     return start * (1.0 + step * (ratio + cross / norm)), -start * step
 
 
-def finish_kernel(devices, norm_scale, direction_ref, scaled_ref, direction_scores_ref, scaled_scores_ref, swapped_ref,
-                  sums_ref, solved_hbm, scores_ref, solved_ref, semaphores):
+def finish_kernel(devices, norm_scale, direction_ref, scaled_ref, own_scores_ref, other_scores_ref, sums_ref, solved_hbm,
+                  scores_ref, solved_ref, semaphores):
     people, columns = direction_ref.shape
-    rows = scores_ref.shape[0]
     column = lax.axis_index("cols")
     copies = Copies(semaphores)
 
@@ -293,12 +310,11 @@
         stores.append(copies.start(solved_ref.at[block], solved_hbm.at[block]))
     own = pl.multiple_of(column * columns, columns)
     other = pl.multiple_of((1 - column) * columns, columns)
-    here = pl.ds(0, rows)
     scores_ref[:, pl.ds(own, columns)] = norm_scale * (
-        along * direction_scores_ref[here, :] + across * scaled_scores_ref[here, :]
+        along * own_scores_ref[0] + across * own_scores_ref[1]
     )
     scores_ref[:, pl.ds(other, columns)] = norm_scale * (
-        other_along * swapped_ref[here, :] + other_across * swapped_ref[pl.ds(rows, rows), :]
+        other_along * other_scores_ref[0] + other_across * other_scores_ref[1]
     )
     wait_all(stores)
 
@@ -374,18 +390,17 @@
         functools.partial(group_kernel, even), [parts] * 2, [vmem] * 2, [vmem] * 2, limit=large
     )(after(dosage, table).T, other_dosage.T)
 
-    def variant_products(values):
-        return call(
-            score_kernel, [float_of(half, 2 * share_rows, columns)] * 2, [vmem] * 3, [vmem] * 2, limit=large
-        )(*grouped, values)
-
-    def halved(values, step):
-        count = values.shape[0] // 2
-        return values[:count], swap(values[count:], "samples", devices, step)
+    products = float_of(half, 2 * share_rows, columns)
+
+    def add_step(kept, taken):
+        rows = float_of(kept.shape[0] // 2, 2 * share_rows, columns)
+        return call(add_kernel, [rows] * 2, [vmem] * 2, [vmem] * 2)(kept, taken)
 
     partner = swap(direction, "samples", devices, half)
     near = to_mates(outgoing)
-    direction_even, direction_odd = variant_products(direction)
+    direction_even, direction_odd = call(
+        score_kernel, [products] * 2, [vmem] * 3, [vmem] * 2, limit=large
+    )(*grouped, direction)
     direction_share = swap(direction_odd, "samples", devices, 1)
     far = to_mates(call(
         forward_kernel,
@@ -394,49 +409,43 @@
         [vmem] * (half - 1),
     )(forward, partner, *near, direction_even, direction_odd))
     received = near + far + [partner.reshape(block_count, tile, columns)]
-    scaled, sums, gathered, outgoing = call(
+    scaled, handled, outgoing, scaled_even, scaled_odd = call(
         functools.partial(apply_kernel, devices, capacity),
-        [
-            full, float_of(SUBLANES, columns), float_of(devices * capacity + block_count, tile, columns),
-            float_of(devices, tile + SUBLANES, columns),
-        ],
-        [smem] + [vmem] * (devices + 4) + [anywhere],
-        [vmem] * 4,
-    )(table, high, low, direction, diagonal, norm, *received, direction_share)
+        [full, full, float_of(devices, tile + SUBLANES, columns), products, products],
+        [smem] + [vmem] * (devices + 6) + [anywhere],
+        [vmem] * 5,
+        [room(devices * capacity + block_count, tile, columns)],
+        limit=large,
+    )(table, high, low, direction, diagonal, norm, *grouped, *received, direction_share)
     later = lax.all_to_all(outgoing, "samples", split_axis=0, concat_axis=0, tiled=True)
-    scaled_even, scaled_odd = variant_products(scaled)
-    scaled_sum = scaled_even + swap(scaled_odd, "samples", devices, 1)
-    direction_sum = after(direction_even, scaled) + direction_share
+    scaled_share = swap(scaled_odd, "samples", devices, 1)
+    direction_kept, direction_given = add_step(direction_even, direction_share)
+    scaled_kept, scaled_given = add_step(scaled_even, scaled_share)
     for step in steps[:-1]:
-        direction_kept, direction_taken = halved(direction_sum, step)
-        direction_sum = direction_kept + direction_taken
-    direction_kept, direction_taken = halved(direction_sum, steps[-1])
-    scaled_kept, scaled_taken = halved(scaled_sum, steps[0])
+        direction_taken = swap(after(direction_given, scaled), "samples", devices, step)
+        direction_kept, direction_given = add_step(direction_kept, direction_taken)
+        scaled_taken = swap(scaled_given, "samples", devices, step)
+        scaled_kept, scaled_given = add_step(scaled_kept, scaled_taken)
+    direction_taken = swap(direction_given, "samples", devices, steps[-1])
+    scaled_taken = swap(scaled_given, "samples", devices, steps[-1])
     sums = call(
         functools.partial(curvature_kernel, devices),
-        float_of(SUBLANES, columns),
+        float_of(2 * devices, SUBLANES, columns),
         [smem] + [vmem] * 7 + [anywhere] * 2,
         vmem,
-    )(table, high, low, direction, diagonal, scaled, gathered, later, scaled_sum, direction_sum)
-    half_sum = float_of(scaled_kept.shape[0] // 2, 2 * share_rows, columns)
-    all_sums, scaled_kept, scaled_given = call(
-        add_kernel, [float_of(2 * devices, SUBLANES, columns), half_sum, half_sum], [vmem] * 3, [vmem] * 3
-    )(sums, scaled_kept, scaled_taken)
-    all_sums = lax.all_to_all(all_sums, ("samples", "cols"), split_axis=0, concat_axis=0, tiled=True)
-    scaled_sum = scaled_kept + swap(scaled_given, "samples", devices, steps[1])
-    for step in steps[2:]:
-        scaled_kept, scaled_taken = halved(scaled_sum, step)
-        scaled_sum = scaled_kept + scaled_taken
-    direction_scores = (after(direction_kept, sums) + direction_taken)[0]
-    scaled_scores = scaled_sum[0]
-    swapped = swap(jnp.concatenate([direction_scores[share_rows:], scaled_scores[share_rows:]]), "cols", 2, 1)
+    )(table, high, low, direction, diagonal, scaled, handled, later, direction_given, scaled_given)
+    all_sums = lax.all_to_all(sums, ("samples", "cols"), split_axis=0, concat_axis=0, tiled=True)
+    rows = float_of(2, share_rows, columns)
+    own_scores, other_scores = call(
+        last_add_kernel, [rows] * 2, [vmem] * 4 + [anywhere], [vmem] * 2
+    )(direction_kept, direction_taken, scaled_kept, scaled_taken, sums)
     solved, scores = call(
         functools.partial(finish_kernel, devices, 1.0 / math.sqrt(people * devices)),
         [full, float_of(share_rows, 2 * columns)],
-        [vmem] * 6,
+        [vmem] * 5,
         [hbm, vmem],
         [full_room, pltpu.SemaphoreType.DMA((4,))],
-    )(direction, scaled, direction_scores, scaled_scores, swapped, all_sums)
+    )(direction, scaled, own_scores, swap(other_scores, "cols", 2, 1), all_sums)
     return (solved, scores)
 
 

time: 123 us -> 120 us (0.976)
  waiting for transfers between devices: 52.5 us -> 55.9 us
  starting transfers between devices: 35.2 us -> 32.4 us
  local copies, waits for them, and re-layouts: 19.6 us -> 16.8 us
    all_to_all x1, waiting for transfers between devices: 0.01 us -> 3.65 us  [per_device(): lax.all_to_all(sums, ('samples', 'cols'), split_axis=0, concat_axis=0, ti...]
    ppermute x15, starting transfers between devices: 23.7 us -> 20.6 us  [swap(): return lax.ppermute(values, axis, [(i, i ^ step) for i in range(devices)])]
    slice x5 -> x0, local copies, waits for them, and re-layouts: 1.58 us -> none  [the longest x3 1.56 us: halved(): return (values[:count], swap(values[count:], 'samples', devices, step))]
    pallas_call x5 -> x8, Pallas kernels: 7.83 us -> 9.35 us  [the longest x1 3.88 us: per_device(): call(functools.partial(apply_kernel, devices, capacity), [full, full, flo...]
    unnamed x42 -> x56, local copies, waits for them, and re-layouts: 15.1 us -> 13.9 us
  transfers between devices with their start and end apart: 17 -> 17, of which waited for: 9 -> 10; matrix products, arithmetic and copies ran while one was open for 5% -> 2% of each run, Pallas kernels for 7% -> 7%
where the time goes in v12:
time: 120 us
  waiting for transfers between devices  55.9 us (47%)
  starting transfers between devices  32.4 us (27%)
  local copies, waits for them, and re-layouts  16.8 us (14%)
  Pallas kernels  13.8 us (12%)
    ppermute x15, waiting for transfers between devices, swap(): return lax.ppermute(values, axis, [(i, i ^ step) for i in range(devices)])  52.2 us
    ppermute x15, starting transfers between devices, swap(): return lax.ppermute(values, axis, [(i, i ^ step) for i in range(devices)])  20.6 us
    unnamed x56, local copies, waits for them, and re-layouts  13.9 us
    all_to_all x1, starting transfers between devices, per_device(): lax.all_to_all(outgoing, 'samples', split_axis=0, concat_axis=0, tiled=True)  6.86 us
    all_to_all x1, starting transfers between devices, per_device(): lax.all_to_all(sums, ('samples', 'cols'), split_axis=0, concat_axis=0, ti...  4.91 us
    pallas_call x1, Pallas kernels, per_device(): call(functools.partial(apply_kernel, devices, capacity), [full, full, flo...  3.88 us
    all_to_all x1, waiting for transfers between devices, per_device(): lax.all_to_all(sums, ('samples', 'cols'), split_axis=0, concat_axis=0, ti...  3.65 us
  transfers between devices with their start and end apart: 17, of which 10 were waited for; matrix products, arithmetic and copies ran while one was open for 2% of the time, Pallas kernels for 7%

profile of v12, /device:TPU:0, one launch (start us, length us, event | category | flops | bytes accessed | tf_op | source)
XLA Modules:
  0.0 119.7 jit_solution(602351587440181036)
XLA Ops:
  5.4 3.6 %collective-permute-start.4 = (f32[512,256]{1,0:T(8,128)S(1)}, f32[512,256]{1,0:T(8,128)S(1)}, u32[]{:S(2)}, u32[]{:S(2)}) collective-permute-start(f32[512,256]{1,0:T(8,128)S(1)} %get-tuple-element.37.direction_ref.values_ref), channel_id=1, source_target_pairs={{0,8},{2,10},{4,12},{6,14},{8,0},{10,2},{12,4},{14,6},{1,9},{3,11}... | collective-permute-start | bytes 1572872 | tf_op jit(solution)/shard_map/ppermute | solution.py:334
  8.9 1.9 %shard_map.69 = (s32[4,12]{1,0:T(4,128)S(1)}, s32[2,4]{1,0:T(2,128)S(1)}, bf16[4,128,512]{2,1,0:T(8,128)(2,1)S(1)}, bf16[4,128,512]{2,1,0:T(8,128)(2,1)S(1)}, f3...) custom-call(s32[3,32]{1,0:T(4,128)S(1)} %bitcast.9, f32[4,4,128,128]{3,2,1,0:T(8,128)S(1)} %copy-done, ...), custom_call_target="tpu_custom_call" | custom-call | tf_op jit(solution)/shard_map/pallas_call | solution.py:374
  12.4 1.6 %collective-permute-start.1 = (f32[2,128,256]{2,1,0:T(8,128)}, f32[2,128,256]{2,1,0:T(8,128)S(1)}, u32[]{:S(2)}, u32[]{:S(2)}) collective-permute-start(f32[2,128,256]{2,1,0:T(8,128)} %get-tuple-element.47), channel_id=1, source_target_pairs={{0,2},{2,0},{4,6},{6,4},{8,10},{10,8},{12,14},{14,12},{1,3},{3,1},... | collective-permute-start | bytes 786440 | tf_op jit(solution)/shard_map/ppermute | solution.py:334
  14.0 1.6 %collective-permute-start.2 = (f32[2,128,256]{2,1,0:T(8,128)}, f32[2,128,256]{2,1,0:T(8,128)}, u32[]{:S(2)}, u32[]{:S(2)}) collective-permute-start(f32[2,128,256]{2,1,0:T(8,128)} %get-tuple-element.48), channel_id=1, source_target_pairs={{0,4},{2,6},{4,0},{6,2},{8,12},{10,14},{12,8},{14,10},{1,5},{3,7},... | collective-permute-start | bytes 786440 | tf_op jit(solution)/shard_map/ppermute | solution.py:334
  15.9 1.6 %copy.7 = f32[512,512]{0,1:T(8,128)S(1)} copy(f32[512,512]{1,0:T(8,128)} %param.9) | data formatting | bytes 2097152 | tf_op jit(solution)/shard_map/optimization_barrier | solution.py:338
  21.3 1.7 %collective-permute-start.8 = (f32[4,128,256]{2,1,0:T(8,128)S(1)}, f32[4,128,256]{2,1,0:T(8,128)S(1)}, u32[]{:S(2)}, u32[]{:S(2)}) collective-permute-start(f32[4,128,256]{2,1,0:T(8,128)S(1)} %get-tuple-element.52.refs_4_), channel_id=1, source_target_pairs={{0,2},{2,0},{4,6},{6,4},{8,10},{10,8},{12,14},{14,12},{1,3},{3,1},... | collective-permute-start | bytes 1572872 | tf_op jit(solution)/shard_map/ppermute | solution.py:334
  22.9 9.9 %collective-permute-done.4.partner_ref = f32[512,256]{1,0:T(8,128)S(1)} collective-permute-done((f32[512,256]{1,0:T(8,128)S(1)}, f32[512,256]{1,0:T(8,128)S(1)}, u32[]{:S(2)}, u32[]{:S(2)}) %collective-permute-start.4) | collective-permute-done | bytes 524320 | tf_op jit(solution)/shard_map/ppermute | solution.py:334
  33.6 4.6 %collective-permute-done.3.refs_2_ = f32[2,128,256]{2,1,0:T(8,128)} collective-permute-done((f32[2,128,256]{2,1,0:T(8,128)}, f32[2,128,256]{2,1,0:T(8,128)}, u32[]{:S(2)}, u32[]{:S(2)}) %collective-permute-start.3) | collective-permute-done | bytes 262176 | tf_op jit(solution)/shard_map/ppermute | solution.py:334
  38.8 1.5 %collective-permute-start.5 = (f32[2,128,256]{2,1,0:T(8,128)S(1)}, f32[2,128,256]{2,1,0:T(8,128)S(1)}, u32[]{:S(2)}, u32[]{:S(2)}) collective-permute-start(f32[2,128,256]{2,1,0:T(8,128)S(1)} %get-tuple-element.53), channel_id=1, source_target_pairs={{0,2},{2,0},{4,6},{6,4},{8,10},{10,8},{12,14},{14,12},{1,3},{3,1},... | collective-permute-start | bytes 786440 | tf_op jit(solution)/shard_map/ppermute | solution.py:334
  40.4 2.0 %collective-permute-start.7 = (f32[2,128,256]{2,1,0:T(8,128)S(1)}, f32[2,128,256]{2,1,0:T(8,128)S(1)}, u32[]{:S(2)}, u32[]{:S(2)}) collective-permute-start(f32[2,128,256]{2,1,0:T(8,128)S(1)} %get-tuple-element.55), channel_id=1, source_target_pairs={{0,6},{2,4},{4,2},{6,0},{8,14},{10,12},{12,10},{14,8},{1,7},{3,5},... | collective-permute-start | bytes 786440 | tf_op jit(solution)/shard_map/ppermute | solution.py:334
  42.4 4.8 %collective-permute-done.5.refs_3_ = f32[2,128,256]{2,1,0:T(8,128)S(1)} collective-permute-done((f32[2,128,256]{2,1,0:T(8,128)S(1)}, f32[2,128,256]{2,1,0:T(8,128)S(1)}, u32[]{:S(2)}, u32[]{:S(2)}) %collective-permute-start.5) | collective-permute-done | bytes 262176 | tf_op jit(solution)/shard_map/ppermute | solution.py:334
  47.2 2.4 %collective-permute-done.6.refs_4_ = f32[2,128,256]{2,1,0:T(8,128)S(1)} collective-permute-done((f32[2,128,256]{2,1,0:T(8,128)S(1)}, f32[2,128,256]{2,1,0:T(8,128)S(1)}, u32[]{:S(2)}, u32[]{:S(2)}) %collective-permute-start.6) | collective-permute-done | bytes 262176 | tf_op jit(solution)/shard_map/ppermute | solution.py:334
  49.6 3.3 %collective-permute-done.7.refs_5_ = f32[2,128,256]{2,1,0:T(8,128)S(1)} collective-permute-done((f32[2,128,256]{2,1,0:T(8,128)S(1)}, f32[2,128,256]{2,1,0:T(8,128)S(1)}, u32[]{:S(2)}, u32[]{:S(2)}) %collective-permute-start.7) | collective-permute-done | bytes 262176 | tf_op jit(solution)/shard_map/ppermute | solution.py:334
  52.9 3.9 %shard_map.73 = (f32[512,256]{1,0:T(8,128)S(1)}, f32[512,256]{1,0:T(8,128)S(1)}, f32[8,136,256]{2,1,0:T(8,128)S(1)}, f32[4,128,256]{2,1,0:T(8,128)S(1)}, f32[4,128,256]{2,1,0:T(8,128)}) custom-call(s32[4,12]{1,0:T(4,128)S(1)} %get-tuple-element.39.table_ref, bf16[4,128,512]{2,1,0:T(8,128)(2,1)S(1)} %copy-done.5, bf16[4,128,512]{2,1,0:T(8,128)(2,1)S(1)} %copy-done.8, ...), custom_call_target="tpu_custom_call" | custom-call | tf_op jit(solution)/shard_map/pallas_call | solution.py:412
  60.3 6.9 %all-to-all-start = ((f32[8,136,256]{2,1,0:T(8,128)}), f32[8,136,256]{2,1,0:T(8,128)S(1)}, u32[]{:S(2)}, u32[]{:S(2)}) async-start(f32[8,136,256]{2,1,0:T(8,128)} %copy-done.12), calls=%async_computation | async-start | bytes 2228224 | tf_op jit(solution)/shard_map/all_to_all | solution.py:420
  67.2 2.0 %collective-permute-start.11 = (f32[4,128,256]{2,1,0:T(8,128)}, f32[4,128,256]{2,1,0:T(8,128)S(1)}, u32[]{:S(2)}, u32[]{:S(2)}) collective-permute-start(f32[4,128,256]{2,1,0:T(8,128)} %get-tuple-element.63), channel_id=1, source_target_pairs={{0,2},{2,0},{4,6},{6,4},{8,10},{10,8},{12,14},{14,12},{1,3},{3,1},... | collective-permute-start | bytes 1572872 | tf_op jit(solution)/shard_map/ppermute | solution.py:334
  69.3 1.5 %collective-permute-start.9 = (f32[2,128,256]{2,1,0:T(8,128)S(1)}, f32[2,128,256]{2,1,0:T(8,128)S(1)}, u32[]{:S(2)}, u32[]{:S(2)}) collective-permute-start(f32[2,128,256]{2,1,0:T(8,128)S(1)} %get-tuple-element.59), channel_id=1, source_target_pairs={{0,4},{2,6},{4,0},{6,2},{8,12},{10,14},{12,8},{14,10},{1,5},{3,7},... | collective-permute-start | bytes 786440 | tf_op jit(solution)/shard_map/ppermute | solution.py:334
  70.8 19.8 %collective-permute-done.11.taken_ref = f32[4,128,256]{2,1,0:T(8,128)S(1)} collective-permute-done((f32[4,128,256]{2,1,0:T(8,128)}, f32[4,128,256]{2,1,0:T(8,128)S(1)}, u32[]{:S(2)}, u32[]{:S(2)}) %collective-permute-start.11) | collective-permute-done | bytes 524320 | tf_op jit(solution)/shard_map/ppermute | solution.py:334
  92.3 2.9 %collective-permute-start.10 = (f32[1,128,256]{2,1,0:T(8,128)}, f32[1,128,256]{2,1,0:T(8,128)}, u32[]{:S(2)}, u32[]{:S(2)}) collective-permute-start(f32[1,128,256]{2,1,0:T(8,128)} %get-tuple-element.61.refs_0_), channel_id=1, source_target_pairs={{0,8},{2,10},{4,12},{6,14},{8,0},{10,2},{12,4},{14,6},{1,9},{3,11}... | collective-permute-start | bytes 393224 | tf_op jit(solution)/shard_map/ppermute | solution.py:334
  95.2 5.7 %collective-permute-done.12.taken_ref = f32[2,128,256]{2,1,0:T(8,128)S(1)} collective-permute-done((f32[2,128,256]{2,1,0:T(8,128)S(1)}, f32[2,128,256]{2,1,0:T(8,128)S(1)}, u32[]{:S(2)}, u32[]{:S(2)}) %collective-permute-start.12) | collective-permute-done | bytes 262176 | tf_op jit(solution)/shard_map/ppermute | solution.py:334
  103.3 2.0 %shard_map.78.gate_ref = f32[16,8,256]{2,1,0:T(8,128)} custom-call(s32[4,12]{1,0:T(4,128)S(1)} %get-tuple-element.39.table_ref, bf16[4,128,512]{2,1,0:T(8,128)(2,1)S(1)} %copy-done.6, bf16[4,128,512]{2,1,0:T(8,128)(2,1)S(1)} %copy-done.9, f32[512,256]{1,0:T(8,128)S(1)} %get-tuple-element.37.direction_ref.values_ref, f32[512,1]{1,0:T(8,128)S(1)} %copy-done.15, ...), custom_call_target="tpu_custom_call" | custom-call | tf_op jit(solution)/shard_map/pallas_call | solution.py:431
  105.3 4.9 %all-to-all-start.1 = ((f32[16,8,256]{2,1,0:T(8,128)}), f32[16,8,256]{2,1,0:T(8,128)S(1)}, u32[]{:S(2)}, u32[]{:S(2)}) async-start(f32[16,8,256]{2,1,0:T(8,128)} %shard_map.78.gate_ref), calls=%async_computation.1 | async-start | bytes 262144 | tf_op jit(solution)/shard_map/all_to_all | solution.py:437
  114.5 3.6 %all-to-all-done.1.sums_ref = f32[16,8,256]{2,1,0:T(8,128)S(1)} async-done(((f32[16,8,256]{2,1,0:T(8,128)}), f32[16,8,256]{2,1,0:T(8,128)S(1)}, u32[]{:S(2)}, u32[]{:S(2)}) %all-to-all-start.1) | async-done | bytes 131104 | tf_op jit(solution)/shard_map/all_to_all | solution.py:437
  118.2 1.5 %shard_map.80 = (f32[512,256]{1,0:T(8,128)}, f32[64,512]{1,0:T(8,128)}) custom-call(f32[512,256]{1,0:T(8,128)S(1)} %get-tuple-element.37.direction_ref.values_ref, f32[512,256]{1,0:T(8,128)S(1)} %copy-done.11, f32[2,64,256]{2,1,0:T(8,128)S(1)} %get-tuple-element.70.own_scores_ref, f32[2,64,256]{2,1,0:T(8,128)S(1)} %collective-permute-done.14.other_scores_ref, ...), custom_call_target="tpu_custom_call" | custom-call | tf_op jit(solution)/shard_map/pallas_call | solution.py:442
  (81 shorter events, 23.7 us)
Async XLA Ops:
  4.9 4.0 %collective-permute-start = (f32[512,512]{1,0:T(8,128)S(1)}, f32[512,512]{1,0:T(8,128)S(1)}, u32[]{:S(2)}, u32[]{:S(2)}) collective-permute-start(f32[512,512]{1,0:T(8,128)S(1)} %copy-done.27), channel_id=1, source_target_pairs={{0,1},{1,0},{2,3},{3,2},{4,5},{5,4},{6,7},{7,6},{8,9},{9,8},{10,11... | collective-permute-start | bytes 3145736 | tf_op jit(solution)/shard_map/ppermute | solution.py:334
  5.4 27.5 %collective-permute-start.4 = (f32[512,256]{1,0:T(8,128)S(1)}, f32[512,256]{1,0:T(8,128)S(1)}, u32[]{:S(2)}, u32[]{:S(2)}) collective-permute-start(f32[512,256]{1,0:T(8,128)S(1)} %get-tuple-element.37.direction_ref.values_ref), channel_id=1, source_target_pairs={{0,8},{2,10},{4,12},{6,14},{8,0},{10,2},{12,4},{14,6},{1,9},{3,11}... | collective-permute-start | bytes 1572872 | tf_op jit(solution)/shard_map/ppermute | solution.py:334
  12.4 20.5 %collective-permute-start.1 = (f32[2,128,256]{2,1,0:T(8,128)}, f32[2,128,256]{2,1,0:T(8,128)S(1)}, u32[]{:S(2)}, u32[]{:S(2)}) collective-permute-start(f32[2,128,256]{2,1,0:T(8,128)} %get-tuple-element.47), channel_id=1, source_target_pairs={{0,2},{2,0},{4,6},{6,4},{8,10},{10,8},{12,14},{14,12},{1,3},{3,1},... | collective-permute-start | bytes 786440 | tf_op jit(solution)/shard_map/ppermute | solution.py:334
  14.0 19.6 %collective-permute-start.2 = (f32[2,128,256]{2,1,0:T(8,128)}, f32[2,128,256]{2,1,0:T(8,128)}, u32[]{:S(2)}, u32[]{:S(2)}) collective-permute-start(f32[2,128,256]{2,1,0:T(8,128)} %get-tuple-element.48), channel_id=1, source_target_pairs={{0,4},{2,6},{4,0},{6,2},{8,12},{10,14},{12,8},{14,10},{1,5},{3,7},... | collective-permute-start | bytes 786440 | tf_op jit(solution)/shard_map/ppermute | solution.py:334
  15.6 22.6 %collective-permute-start.3 = (f32[2,128,256]{2,1,0:T(8,128)}, f32[2,128,256]{2,1,0:T(8,128)}, u32[]{:S(2)}, u32[]{:S(2)}) collective-permute-start(f32[2,128,256]{2,1,0:T(8,128)} %get-tuple-element.49), channel_id=1, source_target_pairs={{0,6},{2,4},{4,2},{6,0},{8,14},{10,12},{12,10},{14,8},{1,7},{3,5},... | collective-permute-start | bytes 786440 | tf_op jit(solution)/shard_map/ppermute | solution.py:334
  21.3 17.5 %copy-start.2 = (f32[4,128,256]{2,1,0:T(8,128)}, f32[4,128,256]{2,1,0:T(8,128)S(1)}, u32[]{:S(2)}) copy-start(f32[4,128,256]{2,1,0:T(8,128)S(1)} %get-tuple-element.51.refs_3_.kept_ref) | copy-start | bytes 1572868
  21.3 21.1 %collective-permute-start.8 = (f32[4,128,256]{2,1,0:T(8,128)S(1)}, f32[4,128,256]{2,1,0:T(8,128)S(1)}, u32[]{:S(2)}, u32[]{:S(2)}) collective-permute-start(f32[4,128,256]{2,1,0:T(8,128)S(1)} %get-tuple-element.52.refs_4_), channel_id=1, source_target_pairs={{0,2},{2,0},{4,6},{6,4},{8,10},{10,8},{12,14},{14,12},{1,3},{3,1},... | collective-permute-start | bytes 1572872 | tf_op jit(solution)/shard_map/ppermute | solution.py:334
  38.2 14.7 %copy-start.14 = (f32[512,1]{1,0:T(8,128)S(1)}, f32[512,1]{1,0:T(8,128)}, u32[]{:S(2)}) copy-start(f32[512,1]{1,0:T(8,128)} %copy-done.13) | copy-start | bytes 6148
  38.8 8.4 %collective-permute-start.5 = (f32[2,128,256]{2,1,0:T(8,128)S(1)}, f32[2,128,256]{2,1,0:T(8,128)S(1)}, u32[]{:S(2)}, u32[]{:S(2)}) collective-permute-start(f32[2,128,256]{2,1,0:T(8,128)S(1)} %get-tuple-element.53), channel_id=1, source_target_pairs={{0,2},{2,0},{4,6},{6,4},{8,10},{10,8},{12,14},{14,12},{1,3},{3,1},... | collective-permute-start | bytes 786440 | tf_op jit(solution)/shard_map/ppermute | solution.py:334
  40.4 9.2 %collective-permute-start.6 = (f32[2,128,256]{2,1,0:T(8,128)S(1)}, f32[2,128,256]{2,1,0:T(8,128)S(1)}, u32[]{:S(2)}, u32[]{:S(2)}) collective-permute-start(f32[2,128,256]{2,1,0:T(8,128)S(1)} %get-tuple-element.54), channel_id=1, source_target_pairs={{0,4},{2,6},{4,0},{6,2},{8,12},{10,14},{12,8},{14,10},{1,5},{3,7},... | collective-permute-start | bytes 786440 | tf_op jit(solution)/shard_map/ppermute | solution.py:334
  40.4 12.6 %collective-permute-start.7 = (f32[2,128,256]{2,1,0:T(8,128)S(1)}, f32[2,128,256]{2,1,0:T(8,128)S(1)}, u32[]{:S(2)}, u32[]{:S(2)}) collective-permute-start(f32[2,128,256]{2,1,0:T(8,128)S(1)} %get-tuple-element.55), channel_id=1, source_target_pairs={{0,6},{2,4},{4,2},{6,0},{8,14},{10,12},{12,10},{14,8},{1,7},{3,5},... | collective-permute-start | bytes 786440 | tf_op jit(solution)/shard_map/ppermute | solution.py:334
  60.3 41.9 %all-to-all-start = ((f32[8,136,256]{2,1,0:T(8,128)}), f32[8,136,256]{2,1,0:T(8,128)S(1)}, u32[]{:S(2)}, u32[]{:S(2)}) async-start(f32[8,136,256]{2,1,0:T(8,128)} %copy-done.12), calls=%async_computation | async-start | bytes 2228224 | tf_op jit(solution)/shard_map/all_to_all | solution.py:420
  67.1 23.4 %copy-start.18 = (f32[4,128,256]{2,1,0:T(8,128)S(1)}, f32[4,128,256]{2,1,0:T(8,128)}, u32[]{:S(2)}) copy-start(f32[4,128,256]{2,1,0:T(8,128)} %copy-done.17) | copy-start | bytes 1572868
  67.2 23.4 %collective-permute-start.11 = (f32[4,128,256]{2,1,0:T(8,128)}, f32[4,128,256]{2,1,0:T(8,128)S(1)}, u32[]{:S(2)}, u32[]{:S(2)}) collective-permute-start(f32[4,128,256]{2,1,0:T(8,128)} %get-tuple-element.63), channel_id=1, source_target_pairs={{0,2},{2,0},{4,6},{6,4},{8,10},{10,8},{12,14},{14,12},{1,3},{3,1},... | collective-permute-start | bytes 1572872 | tf_op jit(solution)/shard_map/ppermute | solution.py:334
  69.2 33.0 %copy-start.6 = (bf16[4,128,512]{2,1,0:T(8,128)(2,1)S(1)}, bf16[4,128,512]{2,1,0:T(8,128)(2,1)}, u32[]{:S(2)}) copy-start(bf16[4,128,512]{2,1,0:T(8,128)(2,1)} %copy-done.4) | copy-start | bytes 1572868
  69.2 33.0 %copy-start.9 = (bf16[4,128,512]{2,1,0:T(8,128)(2,1)S(1)}, bf16[4,128,512]{2,1,0:T(8,128)(2,1)}, u32[]{:S(2)}) copy-start(bf16[4,128,512]{2,1,0:T(8,128)(2,1)} %copy-done.7) | copy-start | bytes 1572868
  69.3 33.0 %copy-start.11 = (f32[512,256]{1,0:T(8,128)S(1)}, f32[512,256]{1,0:T(8,128)}, u32[]{:S(2)}) copy-start(f32[512,256]{1,0:T(8,128)} %copy-done.10) | copy-start | bytes 1572868
  69.3 33.0 %copy-start.15 = (f32[512,1]{1,0:T(8,128)S(1)}, f32[512,1]{1,0:T(8,128)}, u32[]{:S(2)}) copy-start(f32[512,1]{1,0:T(8,128)} %copy-done.13) | copy-start | bytes 6148
  69.3 22.3 %collective-permute-start.9 = (f32[2,128,256]{2,1,0:T(8,128)S(1)}, f32[2,128,256]{2,1,0:T(8,128)S(1)}, u32[]{:S(2)}, u32[]{:S(2)}) collective-permute-start(f32[2,128,256]{2,1,0:T(8,128)S(1)} %get-tuple-element.59), channel_id=1, source_target_pairs={{0,4},{2,6},{4,0},{6,2},{8,12},{10,14},{12,8},{14,10},{1,5},{3,7},... | collective-permute-start | bytes 786440 | tf_op jit(solution)/shard_map/ppermute | solution.py:334
  90.6 10.2 %collective-permute-start.12 = (f32[2,128,256]{2,1,0:T(8,128)S(1)}, f32[2,128,256]{2,1,0:T(8,128)S(1)}, u32[]{:S(2)}, u32[]{:S(2)}) collective-permute-start(f32[2,128,256]{2,1,0:T(8,128)S(1)} %get-tuple-element.65), channel_id=1, source_target_pairs={{0,4},{2,6},{4,0},{6,2},{8,12},{10,14},{12,8},{14,10},{1,5},{3,7},... | collective-permute-start | bytes 786440 | tf_op jit(solution)/shard_map/ppermute | solution.py:334
  92.3 17.9 %collective-permute-start.10 = (f32[1,128,256]{2,1,0:T(8,128)}, f32[1,128,256]{2,1,0:T(8,128)}, u32[]{:S(2)}, u32[]{:S(2)}) collective-permute-start(f32[1,128,256]{2,1,0:T(8,128)} %get-tuple-element.61.refs_0_), channel_id=1, source_target_pairs={{0,8},{2,10},{4,12},{6,14},{8,0},{10,2},{12,4},{14,6},{1,9},{3,11}... | collective-permute-start | bytes 393224 | tf_op jit(solution)/shard_map/ppermute | solution.py:334
  102.2 8.0 %collective-permute-start.13 = (f32[1,128,256]{2,1,0:T(8,128)}, f32[1,128,256]{2,1,0:T(8,128)}, u32[]{:S(2)}, u32[]{:S(2)}) collective-permute-start(f32[1,128,256]{2,1,0:T(8,128)} %get-tuple-element.67.refs_1_), channel_id=1, source_target_pairs={{0,8},{2,10},{4,12},{6,14},{8,0},{10,2},{12,4},{14,6},{1,9},{3,11}... | collective-permute-start | bytes 393224 | tf_op jit(solution)/shard_map/ppermute | solution.py:334
  105.3 12.9 %all-to-all-start.1 = ((f32[16,8,256]{2,1,0:T(8,128)}), f32[16,8,256]{2,1,0:T(8,128)S(1)}, u32[]{:S(2)}, u32[]{:S(2)}) async-start(f32[16,8,256]{2,1,0:T(8,128)} %shard_map.78.gate_ref), calls=%async_computation.1 | async-start | bytes 262144 | tf_op jit(solution)/shard_map/all_to_all | solution.py:437
  113.1 1.5 %collective-permute-start.14 = (f32[2,64,256]{2,1,0:T(8,128)S(1)}, f32[2,64,256]{2,1,0:T(8,128)S(1)}, u32[]{:S(2)}, u32[]{:S(2)}) collective-permute-start(f32[2,64,256]{2,1,0:T(8,128)S(1)} %get-tuple-element.71), channel_id=1, source_target_pairs={{0,1},{1,0},{2,3},{3,2},{4,5},{5,4},{6,7},{7,6},{8,9},{9,8},{10,11... | collective-permute-start | bytes 393224 | tf_op jit(solution)/shard_map/ppermute | solution.py:334
  (21 other events, 68.4 us)

commit v13 on v12

--- a/solution.py
+++ b/solution.py
@@ -77,11 +77,21 @@
     return lax.div(value, jnp.int32(divisor))
 
 
-def direction_kernel(kinship_ref, variance_ref, phenotypes_ref, direction_ref, diagonal_ref, sums_ref):
+def direction_kernel(kinship_hbm, variance_hbm, phenotypes_hbm, direction_ref, direction_hbm, diagonal_hbm, sums_ref,
+                     kinship_ref, variance_ref, phenotypes_ref, diagonal_ref, semaphores):
     block_count, positions, tile = kinship_ref.shape[:3]
+    copies = Copies(semaphores)
+    loads = [copies.start(variance_hbm, variance_ref)]
+    for row in range(block_count):
+        block = pl.ds(row * tile, tile)
+        loads.append(copies.start(kinship_hbm.at[row], kinship_ref.at[row]))
+        loads.append(copies.start(phenotypes_hbm.at[block], phenotypes_ref.at[block]))
+    stores = []
     norm = jnp.zeros((SUBLANES, direction_ref.shape[1]), jnp.float32)
     diagonal_mask = on_diagonal(tile)
+    loads[0].wait()
     for row in range(block_count):
+        wait_all(loads[1 + 2 * row:3 + 2 * row])
         block = pl.ds(row * tile, tile)
         total = jnp.where(diagonal_mask, variance_ref[row:row + 1, :], kinship_ref[row, 0])
         for position in range(1, positions):
@@ -91,16 +101,21 @@
         here = phenotypes_ref[block, :] * (1.0 / diagonal)
         direction_ref[block, :] = here
         norm = norm + column_sums(here * phenotypes_ref[block, :])
+        stores.append(copies.start(direction_ref.at[block], direction_hbm.at[block]))
+    stores.append(copies.start(diagonal_ref, diagonal_hbm))
     row_ids = lax.broadcasted_iota(jnp.int32, norm.shape, 0)
     sums_ref[...] = jnp.where(row_ids == 0, jnp.sum(norm, axis=0, keepdims=True), 0.0)
-
-
-def route_kernel(devices, capacity, list_ref, kinship_ref, direction_ref, gate_ref, table_ref, forward_ref, high_ref,
-                 low_ref, *refs):
+    wait_all(stores)
+
+
+def route_kernel(devices, capacity, list_ref, kinship_hbm, direction_ref, gate_ref, table_ref, forward_ref, high_hbm,
+                 low_hbm, *refs):
     half = devices // 2
-    outgoing_refs, (first_ref, last_ref) = refs[:half - 1], refs[half - 1:]
+    outgoing_refs, refs = refs[:half - 1], refs[half - 1:]
+    first_ref, last_ref, kinship_ref, high_ref, low_ref, semaphores = refs
+    copies = Copies(semaphores)
+    load = copies.start(kinship_hbm, kinship_ref)
     block_count, positions, tile = kinship_ref.shape[:3]
-    split_tiles(kinship_ref, high_ref, low_ref)
     me = lax.axis_index("samples")
     partner = me ^ half
     spare = me ^ 1
@@ -151,10 +166,14 @@
         blocks = blocks_for(me, other)
         table_ref[3, other] = jnp.where(me < other, blocks[1], blocks[0])
     near = [blocks_for(me, me ^ k) for k in range(1, half)]
+    load.wait()
+    split_tiles(kinship_ref, high_ref, low_ref)
+    stores = [copies.start(high_ref, high_hbm), copies.start(low_ref, low_hbm)]
     for k in range(1, half):
         for slot in range(capacity):
             start = pl.multiple_of(near[k - 1][slot] * tile, tile)
             outgoing_refs[k - 1][slot] = direction_ref[pl.ds(start, tile), :]
+    wait_all(stores)
 
 
 def forward_kernel(forward_ref, partner_ref, *refs):
@@ -191,39 +210,56 @@
     score_products(high_ref, low_ref, values_ref[...], even_ref, odd_ref)
 
 
-def apply_kernel(devices, capacity, table_ref, high_ref, low_ref, direction_ref, diagonal_ref, norm_ref,
-                 dosage_high_ref, dosage_low_ref, *refs):
+def apply_kernel(devices, capacity, table_ref, high_hbm, low_hbm, diagonal_hbm, direction_ref, norm_ref, dosage_high_ref,
+                 dosage_low_ref, *refs):
     received_refs = refs[:devices - 1]
-    scaled_ref, handled_ref, outgoing_ref, even_ref, odd_ref, gathered_ref = refs[-6:]
+    (scaled_hbm, handled_hbm, outgoing_hbm, even_ref, odd_ref, gathered_ref, high_ref, low_ref, diagonal_ref, scaled_ref,
+     handled_ref, sums_ref, semaphores) = refs[-13:]
+    copies = Copies(semaphores)
+    loads = [
+        copies.start(high_hbm, high_ref), copies.start(low_hbm, low_ref), copies.start(diagonal_hbm, diagonal_ref)
+    ]
     gather_received(devices, capacity, received_refs, gathered_ref)
+    wait_all(loads)
     block_count, tile, depth = high_ref.shape
     others = depth // tile - 1
     cross = jnp.zeros(norm_ref.shape, jnp.float32)
     for row in range(block_count):
         block = pl.ds(row * tile, tile)
         here = direction_ref[block, :]
-        blocks = [gathered_ref[table_ref[0, row * others + i]] for i in range(others)]
-        weights = [table_ref[2, row * others + i].astype(jnp.float32) for i in range(others)]
-        mapped = product(high_ref[row], low_ref[row], [here] + blocks)
-        far = pl.ds(tile, depth - tile)
-        handled_ref[block, :] = product(
-            high_ref[row, :, far], low_ref[row, :, far], [weight * there for weight, there in zip(weights, blocks)]
-        )
+        blocks = [here] + [gathered_ref[table_ref[0, row * others + i]] for i in range(others)]
+        mapped = product(high_ref[row], low_ref[row], blocks)
         scaled_ref[block, :] = mapped * (1.0 / diagonal_ref[block, :])
         cross = cross + column_sums(here * mapped)
     row_ids = lax.broadcasted_iota(jnp.int32, cross.shape, 0)
-    sums = jnp.where(row_ids == 1, jnp.sum(cross, axis=0, keepdims=True), norm_ref[...])
+    sums_ref[...] = jnp.where(row_ids == 1, jnp.sum(cross, axis=0, keepdims=True), norm_ref[...])
+    stores = [copies.start(scaled_ref, scaled_hbm)]
     for other in range(devices):
         start = pl.multiple_of(table_ref[3, other] * tile, tile)
-        outgoing_ref[other, pl.ds(0, tile), :] = scaled_ref[pl.ds(start, tile), :]
-        outgoing_ref[other, pl.ds(tile, SUBLANES), :] = sums
+        stores.append(copies.start(scaled_ref.at[pl.ds(start, tile)], outgoing_hbm.at[other, pl.ds(0, tile)]))
+        stores.append(copies.start(sums_ref, outgoing_hbm.at[other, pl.ds(tile, SUBLANES)]))
     score_products(dosage_high_ref, dosage_low_ref, scaled_ref[...], even_ref, odd_ref)
-
-
-def curvature_kernel(devices, table_ref, high_ref, low_ref, direction_ref, diagonal_ref, scaled_ref, handled_ref,
-                     later_ref, *refs):
-    sums_ref = refs[-1]
+    far = pl.ds(tile, depth - tile)
+    for row in range(block_count):
+        blocks = []
+        for i in range(others):
+            weight = table_ref[2, row * others + i].astype(jnp.float32)
+            blocks.append(weight * gathered_ref[table_ref[0, row * others + i]])
+        handled_ref[pl.ds(row * tile, tile), :] = product(high_ref[row, :, far], low_ref[row, :, far], blocks)
+    stores.append(copies.start(handled_ref, handled_hbm))
+    wait_all(stores)
+
+
+def curvature_kernel(devices, table_ref, high_hbm, low_hbm, direction_hbm, diagonal_hbm, scaled_hbm, handled_hbm,
+                     later_hbm, *refs):
+    (sums_hbm, sums_ref, high_ref, low_ref, direction_ref, diagonal_ref, scaled_ref, handled_ref, later_ref,
+     semaphores) = refs[-10:]
     block_count, tile, depth = high_ref.shape
+    copies = Copies(semaphores)
+    wait_all([copies.start(source, target) for source, target in (
+        (later_hbm, later_ref), (scaled_hbm, scaled_ref), (direction_hbm, direction_ref), (high_hbm, high_ref),
+        (low_hbm, low_ref), (handled_hbm, handled_ref), (diagonal_hbm, diagonal_ref),
+    )])
     others = depth // tile - 1
     first_sums = later_ref[0, pl.ds(tile, SUBLANES), :]
     for other in range(1, devices):
@@ -247,6 +283,7 @@
     sums = jnp.where(row_ids == 3, jnp.sum(bend, axis=0, keepdims=True), sums)
     for i in range(2 * devices):
         sums_ref[i] = sums
+    copies.start(sums_ref, sums_hbm).wait()
 
 
 def add_kernel(kept_ref, taken_ref, near_ref, far_ref):
@@ -255,7 +292,7 @@
     far_ref[...] = kept_ref[pl.ds(count, count)] + taken_ref[pl.ds(count, count)]
 
 
-def last_add_kernel(first_kept_ref, first_taken_ref, second_kept_ref, second_taken_ref, gate_ref, own_ref, other_ref):
+def last_add_kernel(first_kept_ref, first_taken_ref, second_kept_ref, second_taken_ref, own_ref, other_ref):
     rows = own_ref.shape[1]
     for i, (kept_ref, taken_ref) in enumerate(
         ((first_kept_ref, first_taken_ref), (second_kept_ref, second_taken_ref))
@@ -287,11 +324,12 @@
     return start * (1.0 + step * (ratio + cross / norm)), -start * step
 
 
-def finish_kernel(devices, norm_scale, direction_ref, scaled_ref, own_scores_ref, other_scores_ref, sums_ref, solved_hbm,
-                  scores_ref, solved_ref, semaphores):
+def finish_kernel(devices, norm_scale, direction_hbm, scaled_hbm, own_scores_ref, other_scores_ref, sums_ref, solved_hbm,
+                  scores_ref, direction_ref, scaled_ref, semaphores):
     people, columns = direction_ref.shape
     column = lax.axis_index("cols")
     copies = Copies(semaphores)
+    loads = [copies.start(direction_hbm, direction_ref), copies.start(scaled_hbm, scaled_ref)]
 
     def total(which):
         sums = sums_ref[which]
@@ -302,12 +340,13 @@
 
     along, across = coefficients(*total(column))
     other_along, other_across = coefficients(*total(1 - column))
+    wait_all(loads)
     stores = []
     part_rows = people // 4
     for part in range(4):
         block = pl.ds(part * part_rows, part_rows)
-        solved_ref[block, :] = along * direction_ref[block, :] + across * scaled_ref[block, :]
-        stores.append(copies.start(solved_ref.at[block], solved_hbm.at[block]))
+        direction_ref[block, :] = along * direction_ref[block, :] + across * scaled_ref[block, :]
+        stores.append(copies.start(direction_ref.at[block], solved_hbm.at[block]))
     own = pl.multiple_of(column * columns, columns)
     other = pl.multiple_of((1 - column) * columns, columns)
     scores_ref[:, pl.ds(own, columns)] = norm_scale * (
@@ -357,12 +396,24 @@
     full_room = room(people, columns)
     half = devices // 2
     near_by = list(range(1, half))
-    direction, diagonal, norm = call(
+    kinship = pltpu.with_memory_space_constraint(kinship, pltpu.HBM)
+    tiles_room = pltpu.VMEM((block_count, tile, positions * tile), jnp.bfloat16)
+    tiles_out = pltpu.HBM((block_count, tile, positions * tile), jnp.bfloat16)
+    full_out = pltpu.HBM((people, columns), jnp.float32)
+    direction, direction_kept_hbm, diagonal, norm = call(
         direction_kernel,
-        [full, float_of(people, 1), float_of(SUBLANES, columns)],
-        [vmem] * 3,
-        [vmem] * 3,
-    )(kinship, variance.reshape(block_count, tile), phenotypes)
+        [full, full_out, pltpu.HBM((people, 1), jnp.float32), float_of(SUBLANES, columns)],
+        [hbm] * 3,
+        [vmem, hbm, hbm, vmem],
+        [
+            room(*kinship.shape), room(block_count, tile), full_room, room(people, 1),
+            pltpu.SemaphoreType.DMA((3 * block_count + 2,)),
+        ],
+    )(
+        kinship,
+        pltpu.with_memory_space_constraint(variance.reshape(block_count, tile), pltpu.HBM),
+        pltpu.with_memory_space_constraint(phenotypes, pltpu.HBM),
+    )
     def to_mates(blocks):
         return [swap(block, "samples", devices, k) for k, block in zip(near_by, blocks)]
 
@@ -370,17 +421,19 @@
     even = [sum(((i >> b) & 1) << (bits - b) for b in range(bits)) for i in range(half)]
     steps = [2 << i for i in range(bits)]
     other_dosage = with_layout_constraint(swap(after(dosage, direction), "cols", 2, 1), Layout((0, 1)))
-    tiles = jax.ShapeDtypeStruct((block_count, tile, positions * tile), jnp.bfloat16)
     table, forward, high, low, *outgoing = call(
         functools.partial(route_kernel, devices, capacity),
         [
             jax.ShapeDtypeStruct((4, max(entries, devices)), jnp.int32),
             jax.ShapeDtypeStruct((capacity, half), jnp.int32),
-            tiles, tiles,
+            tiles_out, tiles_out,
         ] + [float_of(capacity, tile, columns)] * (half - 1),
-        [smem, vmem, vmem, anywhere],
-        [smem, smem] + [vmem] * (half + 1),
-        [pltpu.SMEM((devices,), jnp.int32), pltpu.SMEM((devices,), jnp.int32)],
+        [smem, hbm, vmem, anywhere],
+        [smem, smem, hbm, hbm] + [vmem] * (half - 1),
+        [
+            pltpu.SMEM((devices,), jnp.int32), pltpu.SMEM((devices,), jnp.int32),
+            room(*kinship.shape), tiles_room, tiles_room, pltpu.SemaphoreType.DMA((3,)),
+        ],
     )(relatives.T, kinship, direction, other_dosage)
 
 
@@ -411,12 +464,17 @@
     received = near + far + [partner.reshape(block_count, tile, columns)]
     scaled, handled, outgoing, scaled_even, scaled_odd = call(
         functools.partial(apply_kernel, devices, capacity),
-        [full, full, float_of(devices, tile + SUBLANES, columns), products, products],
-        [smem] + [vmem] * (devices + 6) + [anywhere],
-        [vmem] * 5,
-        [room(devices * capacity + block_count, tile, columns)],
+        [
+            full_out, full_out, pltpu.HBM((devices, tile + SUBLANES, columns), jnp.float32), products, products,
+        ],
+        [smem, hbm, hbm, hbm] + [vmem] * (devices + 3) + [anywhere],
+        [hbm, hbm, hbm, vmem, vmem],
+        [
+            room(devices * capacity + block_count, tile, columns), tiles_room, tiles_room, room(people, 1), full_room,
+            full_room, room(SUBLANES, columns), pltpu.SemaphoreType.DMA((2 * devices + 5,)),
+        ],
         limit=large,
-    )(table, high, low, direction, diagonal, norm, *grouped, *received, direction_share)
+    )(table, high, low, diagonal, direction, norm, *grouped, *received, direction_share)
     later = lax.all_to_all(outgoing, "samples", split_axis=0, concat_axis=0, tiled=True)
     scaled_share = swap(scaled_odd, "samples", devices, 1)
     direction_kept, direction_given = add_step(direction_even, direction_share)
@@ -428,24 +486,29 @@
         scaled_kept, scaled_given = add_step(scaled_kept, scaled_taken)
     direction_taken = swap(direction_given, "samples", devices, steps[-1])
     scaled_taken = swap(scaled_given, "samples", devices, steps[-1])
+    rows = float_of(2, share_rows, columns)
+    own_scores, other_scores = call(
+        last_add_kernel, [rows] * 2, [vmem] * 4, [vmem] * 2
+    )(direction_kept, direction_taken, scaled_kept, scaled_taken)
+    other_scores = swap(other_scores, "cols", 2, 1)
     sums = call(
         functools.partial(curvature_kernel, devices),
-        float_of(2 * devices, SUBLANES, columns),
-        [smem] + [vmem] * 7 + [anywhere] * 2,
-        vmem,
-    )(table, high, low, direction, diagonal, scaled, handled, later, direction_given, scaled_given)
+        pltpu.HBM((2 * devices, SUBLANES, columns), jnp.float32),
+        [smem] + [hbm] * 6 + [anywhere] * 2,
+        hbm,
+        [
+            room(2 * devices, SUBLANES, columns), tiles_room, tiles_room, full_room, room(people, 1), full_room,
+            full_room, room(devices, tile + SUBLANES, columns), pltpu.SemaphoreType.DMA((8,)),
+        ],
+    )(table, high, low, direction_kept_hbm, diagonal, scaled, handled, later, other_scores)
     all_sums = lax.all_to_all(sums, ("samples", "cols"), split_axis=0, concat_axis=0, tiled=True)
-    rows = float_of(2, share_rows, columns)
-    own_scores, other_scores = call(
-        last_add_kernel, [rows] * 2, [vmem] * 4 + [anywhere], [vmem] * 2
-    )(direction_kept, direction_taken, scaled_kept, scaled_taken, sums)
     solved, scores = call(
         functools.partial(finish_kernel, devices, 1.0 / math.sqrt(people * devices)),
         [full, float_of(share_rows, 2 * columns)],
-        [vmem] * 5,
+        [hbm, hbm, vmem, vmem, vmem],
         [hbm, vmem],
-        [full_room, pltpu.SemaphoreType.DMA((4,))],
-    )(direction, scaled, own_scores, swap(other_scores, "cols", 2, 1), all_sums)
+        [full_room, full_room, pltpu.SemaphoreType.DMA((6,))],
+    )(direction_kept_hbm, scaled, own_scores, other_scores, all_sums)
     return (solved, scores)
 
 

time: 120 us -> 127 us (1.058)
  blocking collectives: 0 us -> 11.4 us
  local copies, waits for them, and re-layouts: 16.8 us -> 9 us
  starting transfers between devices: 32.4 us -> 27.4 us
  waiting for transfers between devices: 55.9 us -> 60.7 us
  Pallas kernels: 13.8 us -> 16.7 us
    all_to_all x0 -> x1, blocking collectives: none -> 11.4 us  [per_device(): lax.all_to_all(sums, ('samples', 'cols'), split_axis=0, concat_axis=0, ti...]
    ppermute x15, waiting for transfers between devices: 52.2 us -> 60.7 us  [swap(): return lax.ppermute(values, axis, [(i, i ^ step) for i in range(devices)])]
    unnamed x56 -> x40, local copies, waits for them, and re-layouts: 13.9 us -> 6.1 us
    all_to_all x1 -> x0, starting transfers between devices: 4.91 us -> none  [per_device(): lax.all_to_all(sums, ('samples', 'cols'), split_axis=0, concat_axis=0, ti...]
    all_to_all x1 -> x0, waiting for transfers between devices: 3.65 us -> none  [per_device(): lax.all_to_all(sums, ('samples', 'cols'), split_axis=0, concat_axis=0, ti...]
    pallas_call x4, Pallas kernels: 7.07 us -> 9.33 us  [the longest x1 4.39 us: per_device(): call(functools.partial(apply_kernel, devices, capacity), [full_out, full_...]
    pallas_call x1, Pallas kernels: 1.87 us -> 3.81 us  [per_device(): call(functools.partial(route_kernel, devices, capacity), [jax.ShapeDtypeS...]
    pallas_call x4, Pallas kernels: 1.47 us -> 0.17 us  [add_step(): return call(add_kernel, [rows] * 2, [vmem] * 2, [vmem] * 2)(kept, taken)]
  transfers between devices with their start and end apart: 17 -> 16, of which waited for: 10 -> 10; matrix products, arithmetic and copies ran while one was open for 2% -> 2% of each run, Pallas kernels for 7% -> 5%
where the time goes in v13:
time: 127 us; the launch traced here: 126 us
  waiting for transfers between devices  60.7 us (48%)
  starting transfers between devices  27.4 us (22%)
  Pallas kernels  16.7 us (13%)
  blocking collectives  11.4 us (9%)
  local copies, waits for them, and re-layouts  9 us (7%)
    ppermute x15, waiting for transfers between devices, swap(): return lax.ppermute(values, axis, [(i, i ^ step) for i in range(devices)])  60.7 us
    ppermute x15, starting transfers between devices, swap(): return lax.ppermute(values, axis, [(i, i ^ step) for i in range(devices)])  20.5 us
    all_to_all x1, blocking collectives, per_device(): lax.all_to_all(sums, ('samples', 'cols'), split_axis=0, concat_axis=0, ti...  11.4 us
    all_to_all x1, starting transfers between devices, per_device(): lax.all_to_all(outgoing, 'samples', split_axis=0, concat_axis=0, tiled=True)  6.91 us
    unnamed x40, local copies, waits for them, and re-layouts  6.1 us
    pallas_call x1, Pallas kernels, per_device(): call(functools.partial(apply_kernel, devices, capacity), [full_out, full_...  4.39 us
    pallas_call x1, Pallas kernels, per_device(): call(functools.partial(route_kernel, devices, capacity), [jax.ShapeDtypeS...  3.81 us
  transfers between devices with their start and end apart: 16, of which 10 were waited for; matrix products, arithmetic and copies ran while one was open for 2% of the time, Pallas kernels for 5%

profile of v13, /device:TPU:0, one launch (start us, length us, event | category | flops | bytes accessed | tf_op | source)
XLA Modules:
  0.0 126.1 jit_solution(12805958237806233718)
XLA Ops:
  0.7 2.4 %shard_map.68 = (f32[512,256]{1,0:T(8,128)S(1)}, f32[512,256]{1,0:T(8,128)}, f32[512,1]{1,0:T(8,128)}, f32[8,256]{1,0:T(8,128)S(1)}) custom-call(f32[4,4,128,128]{3,2,1,0:T(8,128)} %kinship_hbm.3, f32[4,128]{1,0:T(4,128)} %bitcast.9, f32[512,256]{1,0:T(8,128)} %phenotypes_hbm.1), custom_call_target="tpu_custom_call" | custom-call | tf_op jit(solution)/shard_map/pallas_call | solution.py:403
  3.6 3.7 %collective-permute-start.4 = (f32[512,256]{1,0:T(8,128)S(1)}, f32[512,256]{1,0:T(8,128)S(1)}, u32[]{:S(2)}, u32[]{:S(2)}) collective-permute-start(f32[512,256]{1,0:T(8,128)S(1)} %get-tuple-element.39.direction_ref.values_ref), channel_id=1, source_target_pairs={{0,8},{2,10},{4,12},{6,14},{8,0},{10,2},{12,4},{14,6},{1,9},{3,11}... | collective-permute-start | bytes 1572872 | tf_op jit(solution)/shard_map/ppermute | solution.py:373
  7.3 3.8 %shard_map.69 = (s32[4,12]{1,0:T(4,128)S(1)}, s32[2,4]{1,0:T(2,128)S(1)}, bf16[4,128,512]{2,1,0:T(8,128)(2,1)}, bf16[4,128,512]{2,1,0:T(8,128)(2,1)}, f32[2,128,...) custom-call(s32[3,32]{1,0:T(4,128)S(1)} %bitcast.8, f32[4,4,128,128]{3,2,1,0:T(8,128)} %kinship_hbm.3, ...), custom_call_target="tpu_custom_call" | custom-call | tf_op jit(solution)/shard_map/pallas_call | solution.py:424
  11.1 1.6 %collective-permute-start.1 = (f32[2,128,256]{2,1,0:T(8,128)}, f32[2,128,256]{2,1,0:T(8,128)S(1)}, u32[]{:S(2)}, u32[]{:S(2)}) collective-permute-start(f32[2,128,256]{2,1,0:T(8,128)} %get-tuple-element.49), channel_id=1, source_target_pairs={{0,2},{2,0},{4,6},{6,4},{8,10},{10,8},{12,14},{14,12},{1,3},{3,1},... | collective-permute-start | bytes 786440 | tf_op jit(solution)/shard_map/ppermute | solution.py:373
  12.7 1.6 %collective-permute-start.2 = (f32[2,128,256]{2,1,0:T(8,128)}, f32[2,128,256]{2,1,0:T(8,128)}, u32[]{:S(2)}, u32[]{:S(2)}) collective-permute-start(f32[2,128,256]{2,1,0:T(8,128)} %get-tuple-element.50), channel_id=1, source_target_pairs={{0,4},{2,6},{4,0},{6,2},{8,12},{10,14},{12,8},{14,10},{1,5},{3,7},... | collective-permute-start | bytes 786440 | tf_op jit(solution)/shard_map/ppermute | solution.py:373
  14.7 1.6 %copy.7 = f32[512,512]{0,1:T(8,128)S(1)} copy(f32[512,512]{1,0:T(8,128)} %param.9) | data formatting | bytes 2097152 | tf_op jit(solution)/shard_map/optimization_barrier | solution.py:377
  20.0 1.6 %collective-permute-start.8 = (f32[4,128,256]{2,1,0:T(8,128)S(1)}, f32[4,128,256]{2,1,0:T(8,128)S(1)}, u32[]{:S(2)}, u32[]{:S(2)}) collective-permute-start(f32[4,128,256]{2,1,0:T(8,128)S(1)} %get-tuple-element.54.refs_4_), channel_id=1, source_target_pairs={{0,2},{2,0},{4,6},{6,4},{8,10},{10,8},{12,14},{14,12},{1,3},{3,1},... | collective-permute-start | bytes 1572872 | tf_op jit(solution)/shard_map/ppermute | solution.py:373
  21.6 9.5 %collective-permute-done.4.partner_ref = f32[512,256]{1,0:T(8,128)S(1)} collective-permute-done((f32[512,256]{1,0:T(8,128)S(1)}, f32[512,256]{1,0:T(8,128)S(1)}, u32[]{:S(2)}, u32[]{:S(2)}) %collective-permute-start.4) | collective-permute-done | bytes 524320 | tf_op jit(solution)/shard_map/ppermute | solution.py:373
  32.3 4.6 %collective-permute-done.3.refs_2_ = f32[2,128,256]{2,1,0:T(8,128)} collective-permute-done((f32[2,128,256]{2,1,0:T(8,128)}, f32[2,128,256]{2,1,0:T(8,128)}, u32[]{:S(2)}, u32[]{:S(2)}) %collective-permute-start.3) | collective-permute-done | bytes 262176 | tf_op jit(solution)/shard_map/ppermute | solution.py:373
  39.0 2.0 %collective-permute-start.7 = (f32[2,128,256]{2,1,0:T(8,128)S(1)}, f32[2,128,256]{2,1,0:T(8,128)S(1)}, u32[]{:S(2)}, u32[]{:S(2)}) collective-permute-start(f32[2,128,256]{2,1,0:T(8,128)S(1)} %get-tuple-element.57), channel_id=1, source_target_pairs={{0,6},{2,4},{4,2},{6,0},{8,14},{10,12},{12,10},{14,8},{1,7},{3,5},... | collective-permute-start | bytes 786440 | tf_op jit(solution)/shard_map/ppermute | solution.py:373
  41.1 4.8 %collective-permute-done.5.refs_3_ = f32[2,128,256]{2,1,0:T(8,128)S(1)} collective-permute-done((f32[2,128,256]{2,1,0:T(8,128)S(1)}, f32[2,128,256]{2,1,0:T(8,128)S(1)}, u32[]{:S(2)}, u32[]{:S(2)}) %collective-permute-start.5) | collective-permute-done | bytes 262176 | tf_op jit(solution)/shard_map/ppermute | solution.py:373
  45.9 2.4 %collective-permute-done.6.refs_4_ = f32[2,128,256]{2,1,0:T(8,128)S(1)} collective-permute-done((f32[2,128,256]{2,1,0:T(8,128)S(1)}, f32[2,128,256]{2,1,0:T(8,128)S(1)}, u32[]{:S(2)}, u32[]{:S(2)}) %collective-permute-start.6) | collective-permute-done | bytes 262176 | tf_op jit(solution)/shard_map/ppermute | solution.py:373
  48.3 3.3 %collective-permute-done.7.refs_5_ = f32[2,128,256]{2,1,0:T(8,128)S(1)} collective-permute-done((f32[2,128,256]{2,1,0:T(8,128)S(1)}, f32[2,128,256]{2,1,0:T(8,128)S(1)}, u32[]{:S(2)}, u32[]{:S(2)}) %collective-permute-start.7) | collective-permute-done | bytes 262176 | tf_op jit(solution)/shard_map/ppermute | solution.py:373
  51.6 4.4 %shard_map.73 = (f32[512,256]{1,0:T(8,128)}, f32[512,256]{1,0:T(8,128)}, f32[8,136,256]{2,1,0:T(8,128)}, f32[4,128,256]{2,1,0:T(8,128)S(1)}, f32[4,128,256]{2,1,0:T(8,128)S(1)}) custom-call(s32[4,12]{1,0:T(4,128)S(1)} %get-tuple-element.41.table_ref, bf16[4,128,512]{2,1,0:T(8,128)(2,1)S(1)} %copy-done.1, bf16[4,128,512]{2,1,0:T(8,128)(2,1)S(1)} %copy-done.3, ...), custom_call_target="tpu_custom_call" | custom-call | tf_op jit(solution)/shard_map/pallas_call | solution.py:465
  57.6 6.9 %all-to-all-start = ((f32[8,136,256]{2,1,0:T(8,128)}), f32[8,136,256]{2,1,0:T(8,128)S(1)}, u32[]{:S(2)}, u32[]{:S(2)}) async-start(f32[8,136,256]{2,1,0:T(8,128)} %get-tuple-element.73), calls=%async_computation | async-start | bytes 2228224 | tf_op jit(solution)/shard_map/all_to_all | solution.py:478
  64.5 2.1 %collective-permute-start.11 = (f32[4,128,256]{2,1,0:T(8,128)S(1)}, f32[4,128,256]{2,1,0:T(8,128)S(1)}, u32[]{:S(2)}, u32[]{:S(2)}) collective-permute-start(f32[4,128,256]{2,1,0:T(8,128)S(1)} %copy-done.18), channel_id=1, source_target_pairs={{0,2},{2,0},{4,6},{6,4},{8,10},{10,8},{12,14},{14,12},{1,3},{3,1},... | collective-permute-start | bytes 1572872 | tf_op jit(solution)/shard_map/ppermute | solution.py:373
  66.6 1.5 %collective-permute-start.9 = (f32[2,128,256]{2,1,0:T(8,128)S(1)}, f32[2,128,256]{2,1,0:T(8,128)S(1)}, u32[]{:S(2)}, u32[]{:S(2)}) collective-permute-start(f32[2,128,256]{2,1,0:T(8,128)S(1)} %get-tuple-element.61), channel_id=1, source_target_pairs={{0,4},{2,6},{4,0},{6,2},{8,12},{10,14},{12,8},{14,10},{1,5},{3,7},... | collective-permute-start | bytes 786440 | tf_op jit(solution)/shard_map/ppermute | solution.py:373
  68.1 19.7 %collective-permute-done.11.taken_ref = f32[4,128,256]{2,1,0:T(8,128)S(1)} collective-permute-done((f32[4,128,256]{2,1,0:T(8,128)S(1)}, f32[4,128,256]{2,1,0:T(8,128)S(1)}, u32[]{:S(2)}, u32[]{:S(2)}) %collective-permute-start.11) | collective-permute-done | bytes 524320 | tf_op jit(solution)/shard_map/ppermute | solution.py:373
  89.0 3.0 %collective-permute-start.10 = (f32[1,128,256]{2,1,0:T(8,128)S(1)}, f32[1,128,256]{2,1,0:T(8,128)S(1)}, u32[]{:S(2)}, u32[]{:S(2)}) collective-permute-start(f32[1,128,256]{2,1,0:T(8,128)S(1)} %get-tuple-element.63), channel_id=1, source_target_pairs={{0,8},{2,10},{4,12},{6,14},{8,0},{10,2},{12,4},{14,6},{1,9},{3,11}... | collective-permute-start | bytes 393224 | tf_op jit(solution)/shard_map/ppermute | solution.py:373
  92.0 6.2 %collective-permute-done.12.taken_ref = f32[2,128,256]{2,1,0:T(8,128)S(1)} collective-permute-done((f32[2,128,256]{2,1,0:T(8,128)S(1)}, f32[2,128,256]{2,1,0:T(8,128)S(1)}, u32[]{:S(2)}, u32[]{:S(2)}) %collective-permute-start.12) | collective-permute-done | bytes 262176 | tf_op jit(solution)/shard_map/ppermute | solution.py:373
  98.3 7.7 %collective-permute-done.13.second_taken_ref = f32[1,128,256]{2,1,0:T(8,128)S(1)} collective-permute-done((f32[1,128,256]{2,1,0:T(8,128)S(1)}, f32[1,128,256]{2,1,0:T(8,128)S(1)}, u32[]{:S(2)}, u32[]{:S(2)}) %collective-permute-start.13) | collective-permute-done | bytes 131104 | tf_op jit(solution)/shard_map/ppermute | solution.py:373
  110.6 2.5 %shard_map.79 = f32[16,8,256]{2,1,0:T(8,128)} custom-call(s32[4,12]{1,0:T(4,128)S(1)} %get-tuple-element.41.table_ref, bf16[4,128,512]{2,1,0:T(8,128)(2,1)S(1)} %copy-done.2, bf16[4,128,512]{2,1,0:T(8,128)(2,1)S(1)} %copy-done.4, f32[512,256]{1,0:T(8,128)S(1)} %copy-done.5, f32[512,1]{1,0:T(8,128)S(1)} %copy-done.8, f32[512,256]{1,0:T(8,128)S(1)} %copy-done.6, ...), custom_call_target="tpu_custom_call" | custom-call | tf_op jit(solution)/shard_map/pallas_call | solution.py:494
  113.1 11.4 %all_to_all.10.sums_ref = f32[16,8,256]{2,1,0:T(8,128)S(1)} all-to-all(f32[16,8,256]{2,1,0:T(8,128)} %shard_map.79), channel_id=1, replica_groups=mesh['groups'=2,'samples'=8,'cols'=2] {'samples','cols'}, dimensions={0} | all-to-all | bytes 262144 | tf_op jit(solution)/shard_map/all_to_all | solution.py:504
  124.5 1.6 %shard_map.80 = (f32[512,256]{1,0:T(8,128)}, f32[64,512]{1,0:T(8,128)}) custom-call(f32[512,256]{1,0:T(8,128)S(1)} %copy-done.5, f32[512,256]{1,0:T(8,128)S(1)} %copy-done.6, f32[2,64,256]{2,1,0:T(8,128)S(1)} %copy-done.15, f32[2,64,256]{2,1,0:T(8,128)S(1)} %copy-done.13, f32[16,8,256]{2,1,0:T(8,128)S(1)} %all_to_all.10.sums_ref), custom_call_target="tpu_custom_call" | custom-call | tf_op jit(solution)/shard_map/pallas_call | solution.py:505
  (64 shorter events, 15.4 us)
Async XLA Ops:
  3.1 4.2 %collective-permute-start = (f32[512,512]{1,0:T(8,128)S(1)}, f32[512,512]{1,0:T(8,128)S(1)}, u32[]{:S(2)}, u32[]{:S(2)}) collective-permute-start(f32[512,512]{1,0:T(8,128)S(1)} %copy-done.19), channel_id=1, source_target_pairs={{0,1},{1,0},{2,3},{3,2},{4,5},{5,4},{6,7},{7,6},{8,9},{9,8},{10,11... | collective-permute-start | bytes 3145736 | tf_op jit(solution)/shard_map/ppermute | solution.py:373
  3.6 27.5 %collective-permute-start.4 = (f32[512,256]{1,0:T(8,128)S(1)}, f32[512,256]{1,0:T(8,128)S(1)}, u32[]{:S(2)}, u32[]{:S(2)}) collective-permute-start(f32[512,256]{1,0:T(8,128)S(1)} %get-tuple-element.39.direction_ref.values_ref), channel_id=1, source_target_pairs={{0,8},{2,10},{4,12},{6,14},{8,0},{10,2},{12,4},{14,6},{1,9},{3,11}... | collective-permute-start | bytes 1572872 | tf_op jit(solution)/shard_map/ppermute | solution.py:373
  11.1 20.0 %collective-permute-start.1 = (f32[2,128,256]{2,1,0:T(8,128)}, f32[2,128,256]{2,1,0:T(8,128)S(1)}, u32[]{:S(2)}, u32[]{:S(2)}) collective-permute-start(f32[2,128,256]{2,1,0:T(8,128)} %get-tuple-element.49), channel_id=1, source_target_pairs={{0,2},{2,0},{4,6},{6,4},{8,10},{10,8},{12,14},{14,12},{1,3},{3,1},... | collective-permute-start | bytes 786440 | tf_op jit(solution)/shard_map/ppermute | solution.py:373
  12.7 19.6 %collective-permute-start.2 = (f32[2,128,256]{2,1,0:T(8,128)}, f32[2,128,256]{2,1,0:T(8,128)}, u32[]{:S(2)}, u32[]{:S(2)}) collective-permute-start(f32[2,128,256]{2,1,0:T(8,128)} %get-tuple-element.50), channel_id=1, source_target_pairs={{0,4},{2,6},{4,0},{6,2},{8,12},{10,14},{12,8},{14,10},{1,5},{3,7},... | collective-permute-start | bytes 786440 | tf_op jit(solution)/shard_map/ppermute | solution.py:373
  14.3 22.6 %collective-permute-start.3 = (f32[2,128,256]{2,1,0:T(8,128)}, f32[2,128,256]{2,1,0:T(8,128)}, u32[]{:S(2)}, u32[]{:S(2)}) collective-permute-start(f32[2,128,256]{2,1,0:T(8,128)} %get-tuple-element.51), channel_id=1, source_target_pairs={{0,6},{2,4},{4,2},{6,0},{8,14},{10,12},{12,10},{14,8},{1,7},{3,5},... | collective-permute-start | bytes 786440 | tf_op jit(solution)/shard_map/ppermute | solution.py:373
  20.0 21.0 %collective-permute-start.8 = (f32[4,128,256]{2,1,0:T(8,128)S(1)}, f32[4,128,256]{2,1,0:T(8,128)S(1)}, u32[]{:S(2)}, u32[]{:S(2)}) collective-permute-start(f32[4,128,256]{2,1,0:T(8,128)S(1)} %get-tuple-element.54.refs_4_), channel_id=1, source_target_pairs={{0,2},{2,0},{4,6},{6,4},{8,10},{10,8},{12,14},{14,12},{1,3},{3,1},... | collective-permute-start | bytes 1572872 | tf_op jit(solution)/shard_map/ppermute | solution.py:373
  36.9 14.7 %copy-start.3 = (bf16[4,128,512]{2,1,0:T(8,128)(2,1)S(1)}, bf16[4,128,512]{2,1,0:T(8,128)(2,1)}, u32[]{:S(2)}) copy-start(bf16[4,128,512]{2,1,0:T(8,128)(2,1)} %get-tuple-element.43.low_hbm) | copy-start | bytes 1572868
  36.9 14.7 %copy-start.7 = (f32[512,1]{1,0:T(8,128)S(1)}, f32[512,1]{1,0:T(8,128)}, u32[]{:S(2)}) copy-start(f32[512,1]{1,0:T(8,128)} %get-tuple-element.44.diagonal_hbm) | copy-start | bytes 6148
  37.5 8.4 %collective-permute-start.5 = (f32[2,128,256]{2,1,0:T(8,128)S(1)}, f32[2,128,256]{2,1,0:T(8,128)S(1)}, u32[]{:S(2)}, u32[]{:S(2)}) collective-permute-start(f32[2,128,256]{2,1,0:T(8,128)S(1)} %get-tuple-element.55), channel_id=1, source_target_pairs={{0,2},{2,0},{4,6},{6,4},{8,10},{10,8},{12,14},{14,12},{1,3},{3,1},... | collective-permute-start | bytes 786440 | tf_op jit(solution)/shard_map/ppermute | solution.py:373
  39.0 9.2 %collective-permute-start.6 = (f32[2,128,256]{2,1,0:T(8,128)S(1)}, f32[2,128,256]{2,1,0:T(8,128)S(1)}, u32[]{:S(2)}, u32[]{:S(2)}) collective-permute-start(f32[2,128,256]{2,1,0:T(8,128)S(1)} %get-tuple-element.56), channel_id=1, source_target_pairs={{0,4},{2,6},{4,0},{6,2},{8,12},{10,14},{12,8},{14,10},{1,5},{3,7},... | collective-permute-start | bytes 786440 | tf_op jit(solution)/shard_map/ppermute | solution.py:373
  39.0 12.5 %collective-permute-start.7 = (f32[2,128,256]{2,1,0:T(8,128)S(1)}, f32[2,128,256]{2,1,0:T(8,128)S(1)}, u32[]{:S(2)}, u32[]{:S(2)}) collective-permute-start(f32[2,128,256]{2,1,0:T(8,128)S(1)} %get-tuple-element.57), channel_id=1, source_target_pairs={{0,6},{2,4},{4,2},{6,0},{8,14},{10,12},{12,10},{14,8},{1,7},{3,5},... | collective-permute-start | bytes 786440 | tf_op jit(solution)/shard_map/ppermute | solution.py:373
  57.6 51.1 %all-to-all-start = ((f32[8,136,256]{2,1,0:T(8,128)}), f32[8,136,256]{2,1,0:T(8,128)S(1)}, u32[]{:S(2)}, u32[]{:S(2)}) async-start(f32[8,136,256]{2,1,0:T(8,128)} %get-tuple-element.73), calls=%async_computation | async-start | bytes 2228224 | tf_op jit(solution)/shard_map/all_to_all | solution.py:478
  64.5 23.4 %copy-start.10 = (f32[4,128,256]{2,1,0:T(8,128)S(1)}, f32[4,128,256]{2,1,0:T(8,128)}, u32[]{:S(2)}) copy-start(f32[4,128,256]{2,1,0:T(8,128)} %copy-done.9) | copy-start | bytes 1572868
  64.5 23.4 %collective-permute-start.11 = (f32[4,128,256]{2,1,0:T(8,128)S(1)}, f32[4,128,256]{2,1,0:T(8,128)S(1)}, u32[]{:S(2)}, u32[]{:S(2)}) collective-permute-start(f32[4,128,256]{2,1,0:T(8,128)S(1)} %copy-done.18), channel_id=1, source_target_pairs={{0,2},{2,0},{4,6},{6,4},{8,10},{10,8},{12,14},{14,12},{1,3},{3,1},... | collective-permute-start | bytes 1572872 | tf_op jit(solution)/shard_map/ppermute | solution.py:373
  66.6 22.4 %collective-permute-start.9 = (f32[2,128,256]{2,1,0:T(8,128)S(1)}, f32[2,128,256]{2,1,0:T(8,128)S(1)}, u32[]{:S(2)}, u32[]{:S(2)}) collective-permute-start(f32[2,128,256]{2,1,0:T(8,128)S(1)} %get-tuple-element.61), channel_id=1, source_target_pairs={{0,4},{2,6},{4,0},{6,2},{8,12},{10,14},{12,8},{14,10},{1,5},{3,7},... | collective-permute-start | bytes 786440 | tf_op jit(solution)/shard_map/ppermute | solution.py:373
  87.9 20.8 %copy-start.2 = (bf16[4,128,512]{2,1,0:T(8,128)(2,1)S(1)}, bf16[4,128,512]{2,1,0:T(8,128)(2,1)}, u32[]{:S(2)}) copy-start(bf16[4,128,512]{2,1,0:T(8,128)(2,1)} %get-tuple-element.42.high_hbm) | copy-start | bytes 1572868
  87.9 20.8 %copy-start.4 = (bf16[4,128,512]{2,1,0:T(8,128)(2,1)S(1)}, bf16[4,128,512]{2,1,0:T(8,128)(2,1)}, u32[]{:S(2)}) copy-start(bf16[4,128,512]{2,1,0:T(8,128)(2,1)} %get-tuple-element.43.low_hbm) | copy-start | bytes 1572868
  87.9 20.8 %copy-start.5 = (f32[512,256]{1,0:T(8,128)S(1)}, f32[512,256]{1,0:T(8,128)}, u32[]{:S(2)}) copy-start(f32[512,256]{1,0:T(8,128)} %get-tuple-element.38.direction_hbm) | copy-start | bytes 1572868
  87.9 20.8 %copy-start.6 = (f32[512,256]{1,0:T(8,128)S(1)}, f32[512,256]{1,0:T(8,128)}, u32[]{:S(2)}) copy-start(f32[512,256]{1,0:T(8,128)} %get-tuple-element.58.scaled_hbm) | copy-start | bytes 1572868
  87.9 20.8 %copy-start.8 = (f32[512,1]{1,0:T(8,128)S(1)}, f32[512,1]{1,0:T(8,128)}, u32[]{:S(2)}) copy-start(f32[512,1]{1,0:T(8,128)} %get-tuple-element.44.diagonal_hbm) | copy-start | bytes 6148
  88.0 10.2 %collective-permute-start.12 = (f32[2,128,256]{2,1,0:T(8,128)S(1)}, f32[2,128,256]{2,1,0:T(8,128)S(1)}, u32[]{:S(2)}, u32[]{:S(2)}) collective-permute-start(f32[2,128,256]{2,1,0:T(8,128)S(1)} %get-tuple-element.67), channel_id=1, source_target_pairs={{0,4},{2,6},{4,0},{6,2},{8,12},{10,14},{12,8},{14,10},{1,5},{3,7},... | collective-permute-start | bytes 786440 | tf_op jit(solution)/shard_map/ppermute | solution.py:373
  89.0 9.3 %collective-permute-start.10 = (f32[1,128,256]{2,1,0:T(8,128)S(1)}, f32[1,128,256]{2,1,0:T(8,128)S(1)}, u32[]{:S(2)}, u32[]{:S(2)}) collective-permute-start(f32[1,128,256]{2,1,0:T(8,128)S(1)} %get-tuple-element.63), channel_id=1, source_target_pairs={{0,8},{2,10},{4,12},{6,14},{8,0},{10,2},{12,4},{14,6},{1,9},{3,11}... | collective-permute-start | bytes 393224 | tf_op jit(solution)/shard_map/ppermute | solution.py:373
  98.2 7.7 %collective-permute-start.13 = (f32[1,128,256]{2,1,0:T(8,128)S(1)}, f32[1,128,256]{2,1,0:T(8,128)S(1)}, u32[]{:S(2)}, u32[]{:S(2)}) collective-permute-start(f32[1,128,256]{2,1,0:T(8,128)S(1)} %get-tuple-element.69), channel_id=1, source_target_pairs={{0,8},{2,10},{4,12},{6,14},{8,0},{10,2},{12,4},{14,6},{1,9},{3,11}... | collective-permute-start | bytes 393224 | tf_op jit(solution)/shard_map/ppermute | solution.py:373
  106.6 1.3 %collective-permute-start.14 = (f32[2,64,256]{2,1,0:T(8,128)S(1)}, f32[2,64,256]{2,1,0:T(8,128)S(1)}, u32[]{:S(2)}, u32[]{:S(2)}) collective-permute-start(f32[2,64,256]{2,1,0:T(8,128)S(1)} %get-tuple-element.71), channel_id=1, source_target_pairs={{0,1},{1,0},{2,3},{3,2},{4,5},{5,4},{6,7},{7,6},{8,9},{9,8},{10,11... | collective-permute-start | bytes 393224 | tf_op jit(solution)/shard_map/ppermute | solution.py:373
  (12 other events, 50.7 us)

commit v14 on v13

--- a/solution.py
+++ b/solution.py
@@ -213,8 +213,8 @@
 def apply_kernel(devices, capacity, table_ref, high_hbm, low_hbm, diagonal_hbm, direction_ref, norm_ref, dosage_high_ref,
                  dosage_low_ref, *refs):
     received_refs = refs[:devices - 1]
-    (scaled_hbm, handled_hbm, outgoing_hbm, even_ref, odd_ref, gathered_ref, high_ref, low_ref, diagonal_ref, scaled_ref,
-     handled_ref, sums_ref, semaphores) = refs[-13:]
+    (scaled_hbm, handled_hbm, outgoing_hbm, even_hbm, odd_hbm, gathered_ref, high_ref, low_ref, diagonal_ref, scaled_ref,
+     handled_ref, sums_ref, even_ref, odd_ref, semaphores) = refs[-15:]
     copies = Copies(semaphores)
     loads = [
         copies.start(high_hbm, high_ref), copies.start(low_hbm, low_ref), copies.start(diagonal_hbm, diagonal_ref)
@@ -239,6 +239,7 @@
         stores.append(copies.start(scaled_ref.at[pl.ds(start, tile)], outgoing_hbm.at[other, pl.ds(0, tile)]))
         stores.append(copies.start(sums_ref, outgoing_hbm.at[other, pl.ds(tile, SUBLANES)]))
     score_products(dosage_high_ref, dosage_low_ref, scaled_ref[...], even_ref, odd_ref)
+    stores += [copies.start(odd_ref, odd_hbm), copies.start(even_ref, even_hbm)]
     far = pl.ds(tile, depth - tile)
     for row in range(block_count):
         blocks = []
@@ -252,8 +253,8 @@
 
 def curvature_kernel(devices, table_ref, high_hbm, low_hbm, direction_hbm, diagonal_hbm, scaled_hbm, handled_hbm,
                      later_hbm, *refs):
-    (sums_hbm, sums_ref, high_ref, low_ref, direction_ref, diagonal_ref, scaled_ref, handled_ref, later_ref,
-     semaphores) = refs[-10:]
+    (sums_ref, high_ref, low_ref, direction_ref, diagonal_ref, scaled_ref, handled_ref, later_ref,
+     semaphores) = refs[-9:]
     block_count, tile, depth = high_ref.shape
     copies = Copies(semaphores)
     wait_all([copies.start(source, target) for source, target in (
@@ -283,13 +284,18 @@
     sums = jnp.where(row_ids == 3, jnp.sum(bend, axis=0, keepdims=True), sums)
     for i in range(2 * devices):
         sums_ref[i] = sums
-    copies.start(sums_ref, sums_hbm).wait()
 
 
 def add_kernel(kept_ref, taken_ref, near_ref, far_ref):
     count = near_ref.shape[0]
     near_ref[...] = kept_ref[pl.ds(0, count)] + taken_ref[pl.ds(0, count)]
     far_ref[...] = kept_ref[pl.ds(count, count)] + taken_ref[pl.ds(count, count)]
+
+
+def gated_add_kernel(kept_ref, taken_ref, sums_ref, near_ref, far_ref, sums_hbm, semaphores):
+    store = Copies(semaphores).start(sums_ref, sums_hbm)
+    add_kernel(kept_ref, taken_ref, near_ref, far_ref)
+    store.wait()
 
 
 def last_add_kernel(first_kept_ref, first_taken_ref, second_kept_ref, second_taken_ref, own_ref, other_ref):
@@ -465,13 +471,15 @@
     scaled, handled, outgoing, scaled_even, scaled_odd = call(
         functools.partial(apply_kernel, devices, capacity),
         [
-            full_out, full_out, pltpu.HBM((devices, tile + SUBLANES, columns), jnp.float32), products, products,
+            full_out, full_out, pltpu.HBM((devices, tile + SUBLANES, columns), jnp.float32),
+            pltpu.HBM(products.shape, jnp.float32), pltpu.HBM(products.shape, jnp.float32),
         ],
         [smem, hbm, hbm, hbm] + [vmem] * (devices + 3) + [anywhere],
-        [hbm, hbm, hbm, vmem, vmem],
+        [hbm] * 5,
         [
             room(devices * capacity + block_count, tile, columns), tiles_room, tiles_room, room(people, 1), full_room,
-            full_room, room(SUBLANES, columns), pltpu.SemaphoreType.DMA((2 * devices + 5,)),
+            full_room, room(SUBLANES, columns), room(*products.shape), room(*products.shape),
+            pltpu.SemaphoreType.DMA((2 * devices + 7,)),
         ],
         limit=large,
     )(table, high, low, diagonal, direction, norm, *grouped, *received, direction_share)
@@ -482,33 +490,42 @@
     for step in steps[:-1]:
         direction_taken = swap(after(direction_given, scaled), "samples", devices, step)
         direction_kept, direction_given = add_step(direction_kept, direction_taken)
-        scaled_taken = swap(scaled_given, "samples", devices, step)
-        scaled_kept, scaled_given = add_step(scaled_kept, scaled_taken)
     direction_taken = swap(direction_given, "samples", devices, steps[-1])
+    scaled_taken = swap(scaled_given, "samples", devices, steps[0])
+    at_home = lambda *arrays: [pltpu.with_memory_space_constraint(array, pltpu.HBM) for array in arrays]
+    sums = call(
+        functools.partial(curvature_kernel, devices),
+        float_of(2 * devices, SUBLANES, columns),
+        [smem] + [hbm] * 6 + [anywhere] * 3,
+        vmem,
+        [
+            tiles_room, tiles_room, full_room, room(people, 1), full_room, full_room,
+            room(devices, tile + SUBLANES, columns), pltpu.SemaphoreType.DMA((7,)),
+        ],
+    )(
+        table, *at_home(high, low, direction_kept_hbm, diagonal, scaled, handled), later, scaled_given, direction_given
+    )
+    scaled_kept, scaled_given, sums = call(
+        gated_add_kernel, [float_of(scaled_kept.shape[0] // 2, 2 * share_rows, columns)] * 2
+        + [pltpu.HBM(sums.shape, jnp.float32)], [vmem] * 3, [vmem, vmem, hbm], [pltpu.SemaphoreType.DMA((1,))]
+    )(scaled_kept, scaled_taken, sums)
+    sums, scaled_given = lax.optimization_barrier((sums, scaled_given))
+    for step in steps[1:-1]:
+        scaled_kept, scaled_given = add_step(scaled_kept, swap(scaled_given, "samples", devices, step))
     scaled_taken = swap(scaled_given, "samples", devices, steps[-1])
+    all_sums = lax.all_to_all(sums, ("samples", "cols"), split_axis=0, concat_axis=0, tiled=True)
     rows = float_of(2, share_rows, columns)
     own_scores, other_scores = call(
         last_add_kernel, [rows] * 2, [vmem] * 4, [vmem] * 2
     )(direction_kept, direction_taken, scaled_kept, scaled_taken)
     other_scores = swap(other_scores, "cols", 2, 1)
-    sums = call(
-        functools.partial(curvature_kernel, devices),
-        pltpu.HBM((2 * devices, SUBLANES, columns), jnp.float32),
-        [smem] + [hbm] * 6 + [anywhere] * 2,
-        hbm,
-        [
-            room(2 * devices, SUBLANES, columns), tiles_room, tiles_room, full_room, room(people, 1), full_room,
-            full_room, room(devices, tile + SUBLANES, columns), pltpu.SemaphoreType.DMA((8,)),
-        ],
-    )(table, high, low, direction_kept_hbm, diagonal, scaled, handled, later, other_scores)
-    all_sums = lax.all_to_all(sums, ("samples", "cols"), split_axis=0, concat_axis=0, tiled=True)
     solved, scores = call(
         functools.partial(finish_kernel, devices, 1.0 / math.sqrt(people * devices)),
         [full, float_of(share_rows, 2 * columns)],
         [hbm, hbm, vmem, vmem, vmem],
         [hbm, vmem],
         [full_room, full_room, pltpu.SemaphoreType.DMA((6,))],
-    )(direction_kept_hbm, scaled, own_scores, other_scores, all_sums)
+    )(*at_home(direction_kept_hbm, scaled), own_scores, other_scores, all_sums)
     return (solved, scores)
 
 

time: 127 us -> 114 us (0.90)
  blocking collectives: 11.4 us -> 0 us
  starting transfers between devices: 27.4 us -> 32.4 us
  local copies, waits for them, and re-layouts: 9 us -> 4.12 us
  waiting for transfers between devices: 60.7 us -> 56.3 us
  Pallas kernels: 16.7 us -> 19.7 us
    all_to_all x1 -> x0, blocking collectives: 11.4 us -> none  [per_device(): lax.all_to_all(sums, ('samples', 'cols'), split_axis=0, concat_axis=0, ti...]
    ppermute x15, waiting for transfers between devices: 60.7 us -> 51.2 us  [swap(): return lax.ppermute(values, axis, [(i, i ^ step) for i in range(devices)])]
    all_to_all x0 -> x1, waiting for transfers between devices: none -> 5.07 us  [per_device(): lax.all_to_all(sums, ('samples', 'cols'), split_axis=0, concat_axis=0, ti...]
    all_to_all x0 -> x1, starting transfers between devices: none -> 4.93 us  [per_device(): lax.all_to_all(sums, ('samples', 'cols'), split_axis=0, concat_axis=0, ti...]
    unnamed x40 -> x16, local copies, waits for them, and re-layouts: 6.1 us -> 1.25 us
    pallas_call x1 -> x2, Pallas kernels: 2.47 us -> 3.98 us  [the longest x1 3.32 us: per_device(): call(functools.partial(curvature_kernel, devices), float_of(2 * devices,...]
  transfers between devices with their start and end apart: 16 -> 17, of which waited for: 10 -> 10; matrix products, arithmetic and copies ran while one was open for 2% -> 3% of each run, Pallas kernels for 5% -> 9%
where the time goes in v14:
time: 114 us; the launch traced here: 113 us
  waiting for transfers between devices  56.3 us (49%)
  starting transfers between devices  32.4 us (28%)
  Pallas kernels  19.7 us (17%)
  local copies, waits for them, and re-layouts  4.12 us (4%)
    ppermute x15, waiting for transfers between devices, swap(): return lax.ppermute(values, axis, [(i, i ^ step) for i in range(devices)])  51.2 us
    ppermute x15, starting transfers between devices, swap(): return lax.ppermute(values, axis, [(i, i ^ step) for i in range(devices)])  20.5 us
    all_to_all x1, starting transfers between devices, per_device(): lax.all_to_all(outgoing, 'samples', split_axis=0, concat_axis=0, tiled=True)  6.92 us
    all_to_all x1, waiting for transfers between devices, per_device(): lax.all_to_all(sums, ('samples', 'cols'), split_axis=0, concat_axis=0, ti...  5.07 us
    all_to_all x1, starting transfers between devices, per_device(): lax.all_to_all(sums, ('samples', 'cols'), split_axis=0, concat_axis=0, ti...  4.93 us
    pallas_call x1, Pallas kernels, per_device(): call(functools.partial(apply_kernel, devices, capacity), [full_out, full_...  4.71 us
    pallas_call x1, Pallas kernels, per_device(): call(functools.partial(route_kernel, devices, capacity), [jax.ShapeDtypeS...  3.78 us
    pallas_call x1, Pallas kernels, per_device(): call(functools.partial(curvature_kernel, devices), float_of(2 * devices,...  3.32 us
  transfers between devices with their start and end apart: 17, of which 10 were waited for; matrix products, arithmetic and copies ran while one was open for 3% of the time, Pallas kernels for 9%

profile of v14, /device:TPU:0, one launch (start us, length us, event | category | flops | bytes accessed | tf_op | source)
XLA Modules:
  0.0 113.3 jit_solution(623396893233010642)
XLA Ops:
  0.7 2.5 %shard_map.68 = (f32[512,256]{1,0:T(8,128)S(1)}, f32[512,256]{1,0:T(8,128)}, f32[512,1]{1,0:T(8,128)}, f32[8,256]{1,0:T(8,128)S(1)}) custom-call(f32[4,4,128,128]{3,2,1,0:T(8,128)} %kinship_hbm.3, f32[4,128]{1,0:T(4,128)} %bitcast.9, f32[512,256]{1,0:T(8,128)} %phenotypes_hbm.1), custom_call_target="tpu_custom_call" | custom-call | tf_op jit(solution)/shard_map/pallas_call | solution.py:409
  3.6 3.7 %collective-permute-start.4 = (f32[512,256]{1,0:T(8,128)S(1)}, f32[512,256]{1,0:T(8,128)S(1)}, u32[]{:S(2)}, u32[]{:S(2)}) collective-permute-start(f32[512,256]{1,0:T(8,128)S(1)} %get-tuple-element.42.direction_ref.values_ref), channel_id=1, source_target_pairs={{0,8},{2,10},{4,12},{6,14},{8,0},{10,2},{12,4},{14,6},{1,9},{3,11}... | collective-permute-start | bytes 1572872 | tf_op jit(solution)/shard_map/ppermute | solution.py:379
  7.3 3.8 %shard_map.69 = (s32[4,12]{1,0:T(4,128)S(1)}, s32[2,4]{1,0:T(2,128)S(1)}, bf16[4,128,512]{2,1,0:T(8,128)(2,1)}, bf16[4,128,512]{2,1,0:T(8,128)(2,1)}, f32[2,128,...) custom-call(s32[3,32]{1,0:T(4,128)S(1)} %bitcast.8, f32[4,4,128,128]{3,2,1,0:T(8,128)} %kinship_hbm.3, ...), custom_call_target="tpu_custom_call" | custom-call | tf_op jit(solution)/shard_map/pallas_call | solution.py:430
  11.1 1.6 %collective-permute-start.1 = (f32[2,128,256]{2,1,0:T(8,128)}, f32[2,128,256]{2,1,0:T(8,128)S(1)}, u32[]{:S(2)}, u32[]{:S(2)}) collective-permute-start(f32[2,128,256]{2,1,0:T(8,128)} %get-tuple-element.52), channel_id=1, source_target_pairs={{0,2},{2,0},{4,6},{6,4},{8,10},{10,8},{12,14},{14,12},{1,3},{3,1},... | collective-permute-start | bytes 786440 | tf_op jit(solution)/shard_map/ppermute | solution.py:379
  12.7 1.6 %collective-permute-start.2 = (f32[2,128,256]{2,1,0:T(8,128)}, f32[2,128,256]{2,1,0:T(8,128)}, u32[]{:S(2)}, u32[]{:S(2)}) collective-permute-start(f32[2,128,256]{2,1,0:T(8,128)} %get-tuple-element.53), channel_id=1, source_target_pairs={{0,4},{2,6},{4,0},{6,2},{8,12},{10,14},{12,8},{14,10},{1,5},{3,7},... | collective-permute-start | bytes 786440 | tf_op jit(solution)/shard_map/ppermute | solution.py:379
  14.7 1.6 %copy.7 = f32[512,512]{0,1:T(8,128)S(1)} copy(f32[512,512]{1,0:T(8,128)} %param.9) | data formatting | bytes 2097152 | tf_op jit(solution)/shard_map/optimization_barrier | solution.py:383
  20.0 1.6 %collective-permute-start.8 = (f32[4,128,256]{2,1,0:T(8,128)S(1)}, f32[4,128,256]{2,1,0:T(8,128)S(1)}, u32[]{:S(2)}, u32[]{:S(2)}) collective-permute-start(f32[4,128,256]{2,1,0:T(8,128)S(1)} %get-tuple-element.57.refs_4_), channel_id=1, source_target_pairs={{0,2},{2,0},{4,6},{6,4},{8,10},{10,8},{12,14},{14,12},{1,3},{3,1},... | collective-permute-start | bytes 1572872 | tf_op jit(solution)/shard_map/ppermute | solution.py:379
  21.6 9.6 %collective-permute-done.4.partner_ref = f32[512,256]{1,0:T(8,128)S(1)} collective-permute-done((f32[512,256]{1,0:T(8,128)S(1)}, f32[512,256]{1,0:T(8,128)S(1)}, u32[]{:S(2)}, u32[]{:S(2)}) %collective-permute-start.4) | collective-permute-done | bytes 524320 | tf_op jit(solution)/shard_map/ppermute | solution.py:379
  32.2 4.6 %collective-permute-done.3.refs_2_ = f32[2,128,256]{2,1,0:T(8,128)} collective-permute-done((f32[2,128,256]{2,1,0:T(8,128)}, f32[2,128,256]{2,1,0:T(8,128)}, u32[]{:S(2)}, u32[]{:S(2)}) %collective-permute-start.3) | collective-permute-done | bytes 262176 | tf_op jit(solution)/shard_map/ppermute | solution.py:379
  39.0 2.0 %collective-permute-start.7 = (f32[2,128,256]{2,1,0:T(8,128)S(1)}, f32[2,128,256]{2,1,0:T(8,128)S(1)}, u32[]{:S(2)}, u32[]{:S(2)}) collective-permute-start(f32[2,128,256]{2,1,0:T(8,128)S(1)} %get-tuple-element.60), channel_id=1, source_target_pairs={{0,6},{2,4},{4,2},{6,0},{8,14},{10,12},{12,10},{14,8},{1,7},{3,5},... | collective-permute-start | bytes 786440 | tf_op jit(solution)/shard_map/ppermute | solution.py:379
  41.1 4.8 %collective-permute-done.5.refs_3_ = f32[2,128,256]{2,1,0:T(8,128)S(1)} collective-permute-done((f32[2,128,256]{2,1,0:T(8,128)S(1)}, f32[2,128,256]{2,1,0:T(8,128)S(1)}, u32[]{:S(2)}, u32[]{:S(2)}) %collective-permute-start.5) | collective-permute-done | bytes 262176 | tf_op jit(solution)/shard_map/ppermute | solution.py:379
  45.9 2.4 %collective-permute-done.6.refs_4_ = f32[2,128,256]{2,1,0:T(8,128)S(1)} collective-permute-done((f32[2,128,256]{2,1,0:T(8,128)S(1)}, f32[2,128,256]{2,1,0:T(8,128)S(1)}, u32[]{:S(2)}, u32[]{:S(2)}) %collective-permute-start.6) | collective-permute-done | bytes 262176 | tf_op jit(solution)/shard_map/ppermute | solution.py:379
  48.3 3.3 %collective-permute-done.7.refs_5_ = f32[2,128,256]{2,1,0:T(8,128)S(1)} collective-permute-done((f32[2,128,256]{2,1,0:T(8,128)S(1)}, f32[2,128,256]{2,1,0:T(8,128)S(1)}, u32[]{:S(2)}, u32[]{:S(2)}) %collective-permute-start.7) | collective-permute-done | bytes 262176 | tf_op jit(solution)/shard_map/ppermute | solution.py:379
  51.6 4.7 %shard_map.73 = (f32[512,256]{1,0:T(8,128)}, f32[512,256]{1,0:T(8,128)}, f32[8,136,256]{2,1,0:T(8,128)}, f32[4,128,256]{2,1,0:T(8,128)}, f32[4,128,256]{2,1,0:T(8,128)}) custom-call(s32[4,12]{1,0:T(4,128)S(1)} %get-tuple-element.44.table_ref, bf16[4,128,512]{2,1,0:T(8,128)(2,1)S(1)} %copy-done.1, bf16[4,128,512]{2,1,0:T(8,128)(2,1)S(1)} %copy-done.2, ...), custom_call_target="tpu_custom_call" | custom-call | tf_op jit(solution)/shard_map/pallas_call | solution.py:471
  56.3 6.9 %all-to-all-start = ((f32[8,136,256]{2,1,0:T(8,128)}), f32[8,136,256]{2,1,0:T(8,128)S(1)}, u32[]{:S(2)}, u32[]{:S(2)}) async-start(f32[8,136,256]{2,1,0:T(8,128)} %get-tuple-element.72), calls=%async_computation | async-start | bytes 2228224 | tf_op jit(solution)/shard_map/all_to_all | solution.py:486
  63.2 2.0 %collective-permute-start.11 = (f32[4,128,256]{2,1,0:T(8,128)S(1)}, f32[4,128,256]{2,1,0:T(8,128)S(1)}, u32[]{:S(2)}, u32[]{:S(2)}) collective-permute-start(f32[4,128,256]{2,1,0:T(8,128)S(1)} %copy-done.7), channel_id=1, source_target_pairs={{0,2},{2,0},{4,6},{6,4},{8,10},{10,8},{12,14},{14,12},{1,3},{3,1},... | collective-permute-start | bytes 1572872 | tf_op jit(solution)/shard_map/ppermute | solution.py:379
  66.8 19.8 %collective-permute-done.11.taken_ref = f32[4,128,256]{2,1,0:T(8,128)S(1)} collective-permute-done((f32[4,128,256]{2,1,0:T(8,128)S(1)}, f32[4,128,256]{2,1,0:T(8,128)S(1)}, u32[]{:S(2)}, u32[]{:S(2)}) %collective-permute-start.11) | collective-permute-done | bytes 524320 | tf_op jit(solution)/shard_map/ppermute | solution.py:379
  87.7 3.0 %collective-permute-start.10 = (f32[1,128,256]{2,1,0:T(8,128)S(1)}, f32[1,128,256]{2,1,0:T(8,128)S(1)}, u32[]{:S(2)}, u32[]{:S(2)}) collective-permute-start(f32[1,128,256]{2,1,0:T(8,128)S(1)} %get-tuple-element.66.refs_1_), channel_id=1, source_target_pairs={{0,8},{2,10},{4,12},{6,14},{8,0},{10,2},{12,4},{14,6},{1,9},{3,11}... | collective-permute-start | bytes 393224 | tf_op jit(solution)/shard_map/ppermute | solution.py:379
  90.7 3.3 %shard_map.77.sums_ref = f32[16,8,256]{2,1,0:T(8,128)S(1)} custom-call(s32[4,12]{1,0:T(4,128)S(1)} %get-tuple-element.44.table_ref, bf16[4,128,512]{2,1,0:T(8,128)(2,1)} %get-tuple-element.45.high_hbm, bf16[4,128,512]{2,1,0:T(8,128)(2,1)} %get-tuple-element.46.low_hbm, f32[512,256]{1,0:T(8,128)} %get-tuple-element.41.direction_hbm, ...), custom_call_target="tpu_custom_call" | custom-call | tf_op jit(solution)/shard_map/pallas_call | solution.py:496
  94.0 2.9 %collective-permute-done.12.taken_ref = f32[2,128,256]{2,1,0:T(8,128)S(1)} collective-permute-done((f32[2,128,256]{2,1,0:T(8,128)S(1)}, f32[2,128,256]{2,1,0:T(8,128)S(1)}, u32[]{:S(2)}, u32[]{:S(2)}) %collective-permute-start.12) | collective-permute-done | bytes 262176 | tf_op jit(solution)/shard_map/ppermute | solution.py:379
  97.7 4.9 %all-to-all-start.1 = ((f32[16,8,256]{2,1,0:T(8,128)}), f32[16,8,256]{2,1,0:T(8,128)S(1)}, u32[]{:S(2)}, u32[]{:S(2)}) async-start(f32[16,8,256]{2,1,0:T(8,128)} %get-tuple-element.79), calls=%async_computation.1 | async-start | bytes 262144 | tf_op jit(solution)/shard_map/all_to_all | solution.py:516
  102.6 2.7 %collective-permute-done.13.second_taken_ref = f32[1,128,256]{2,1,0:T(8,128)S(1)} collective-permute-done((f32[1,128,256]{2,1,0:T(8,128)S(1)}, f32[1,128,256]{2,1,0:T(8,128)S(1)}, u32[]{:S(2)}, u32[]{:S(2)}) %collective-permute-start.13) | collective-permute-done | bytes 131104 | tf_op jit(solution)/shard_map/ppermute | solution.py:379
  105.5 5.1 %all-to-all-done.1.sums_ref = f32[16,8,256]{2,1,0:T(8,128)S(1)} async-done(((f32[16,8,256]{2,1,0:T(8,128)}), f32[16,8,256]{2,1,0:T(8,128)S(1)}, u32[]{:S(2)}, u32[]{:S(2)}) %all-to-all-start.1) | async-done | bytes 131104 | tf_op jit(solution)/shard_map/all_to_all | solution.py:516
  110.5 2.7 %shard_map.80 = (f32[512,256]{1,0:T(8,128)}, f32[64,512]{1,0:T(8,128)}) custom-call(f32[512,256]{1,0:T(8,128)} %get-tuple-element.41.direction_hbm, f32[512,256]{1,0:T(8,128)} %get-tuple-element.61.scaled_hbm, f32[2,64,256]{2,1,0:T(8,128)S(1)} %get-tuple-element.77.own_scores_ref, f32[2,64,256]{2,1,0:T(8,128)S(1)} %collective-permute-done.14.other_scores_ref, ...), custom_call_target="tpu_custom_call" | custom-call | tf_op jit(solution)/shard_map/pallas_call | solution.py:522
  (41 shorter events, 11.5 us)
Async XLA Ops:
  0.6 2.5 %copy-start.6 = (f32[512,512]{1,0:T(8,128)S(1)}, f32[512,512]{1,0:T(8,128)}, u32[]{:S(2)}) copy-start(f32[512,512]{1,0:T(8,128)} %param.9) | copy-start | bytes 3145732
  0.6 6.7 %copy-start.5 = (s32[32,3]{0,1:T(4,128)S(1)}, s32[32,3]{0,1:T(4,128)}, u32[]{:S(2)}) copy-start(s32[32,3]{0,1:T(4,128)} %param.6) | copy-start | bytes 1156
  3.1 4.2 %collective-permute-start = (f32[512,512]{1,0:T(8,128)S(1)}, f32[512,512]{1,0:T(8,128)S(1)}, u32[]{:S(2)}, u32[]{:S(2)}) collective-permute-start(f32[512,512]{1,0:T(8,128)S(1)} %copy-done.6), channel_id=1, source_target_pairs={{0,1},{1,0},{2,3},{3,2},{4,5},{5,4},{6,7},{7,6},{8,9},{9,8},{10,11... | collective-permute-start | bytes 3145736 | tf_op jit(solution)/shard_map/ppermute | solution.py:379
  3.6 27.5 %collective-permute-start.4 = (f32[512,256]{1,0:T(8,128)S(1)}, f32[512,256]{1,0:T(8,128)S(1)}, u32[]{:S(2)}, u32[]{:S(2)}) collective-permute-start(f32[512,256]{1,0:T(8,128)S(1)} %get-tuple-element.42.direction_ref.values_ref), channel_id=1, source_target_pairs={{0,8},{2,10},{4,12},{6,14},{8,0},{10,2},{12,4},{14,6},{1,9},{3,11}... | collective-permute-start | bytes 1572872 | tf_op jit(solution)/shard_map/ppermute | solution.py:379
  11.1 20.1 %collective-permute-start.1 = (f32[2,128,256]{2,1,0:T(8,128)}, f32[2,128,256]{2,1,0:T(8,128)S(1)}, u32[]{:S(2)}, u32[]{:S(2)}) collective-permute-start(f32[2,128,256]{2,1,0:T(8,128)} %get-tuple-element.52), channel_id=1, source_target_pairs={{0,2},{2,0},{4,6},{6,4},{8,10},{10,8},{12,14},{14,12},{1,3},{3,1},... | collective-permute-start | bytes 786440 | tf_op jit(solution)/shard_map/ppermute | solution.py:379
  12.7 19.6 %collective-permute-start.2 = (f32[2,128,256]{2,1,0:T(8,128)}, f32[2,128,256]{2,1,0:T(8,128)}, u32[]{:S(2)}, u32[]{:S(2)}) collective-permute-start(f32[2,128,256]{2,1,0:T(8,128)} %get-tuple-element.53), channel_id=1, source_target_pairs={{0,4},{2,6},{4,0},{6,2},{8,12},{10,14},{12,8},{14,10},{1,5},{3,7},... | collective-permute-start | bytes 786440 | tf_op jit(solution)/shard_map/ppermute | solution.py:379
  14.3 22.6 %collective-permute-start.3 = (f32[2,128,256]{2,1,0:T(8,128)}, f32[2,128,256]{2,1,0:T(8,128)}, u32[]{:S(2)}, u32[]{:S(2)}) collective-permute-start(f32[2,128,256]{2,1,0:T(8,128)} %get-tuple-element.54), channel_id=1, source_target_pairs={{0,6},{2,4},{4,2},{6,0},{8,14},{10,12},{12,10},{14,8},{1,7},{3,5},... | collective-permute-start | bytes 786440 | tf_op jit(solution)/shard_map/ppermute | solution.py:379
  20.0 21.1 %collective-permute-start.8 = (f32[4,128,256]{2,1,0:T(8,128)S(1)}, f32[4,128,256]{2,1,0:T(8,128)S(1)}, u32[]{:S(2)}, u32[]{:S(2)}) collective-permute-start(f32[4,128,256]{2,1,0:T(8,128)S(1)} %get-tuple-element.57.refs_4_), channel_id=1, source_target_pairs={{0,2},{2,0},{4,6},{6,4},{8,10},{10,8},{12,14},{14,12},{1,3},{3,1},... | collective-permute-start | bytes 1572872 | tf_op jit(solution)/shard_map/ppermute | solution.py:379
  36.9 14.7 %copy-start.1 = (bf16[4,128,512]{2,1,0:T(8,128)(2,1)S(1)}, bf16[4,128,512]{2,1,0:T(8,128)(2,1)}, u32[]{:S(2)}) copy-start(bf16[4,128,512]{2,1,0:T(8,128)(2,1)} %get-tuple-element.45.high_hbm) | copy-start | bytes 1572868
  36.9 14.7 %copy-start.2 = (bf16[4,128,512]{2,1,0:T(8,128)(2,1)S(1)}, bf16[4,128,512]{2,1,0:T(8,128)(2,1)}, u32[]{:S(2)}) copy-start(bf16[4,128,512]{2,1,0:T(8,128)(2,1)} %get-tuple-element.46.low_hbm) | copy-start | bytes 1572868
  36.9 14.7 %copy-start.3 = (f32[512,1]{1,0:T(8,128)S(1)}, f32[512,1]{1,0:T(8,128)}, u32[]{:S(2)}) copy-start(f32[512,1]{1,0:T(8,128)} %get-tuple-element.47.diagonal_hbm) | copy-start | bytes 6148
  37.5 8.4 %collective-permute-start.5 = (f32[2,128,256]{2,1,0:T(8,128)S(1)}, f32[2,128,256]{2,1,0:T(8,128)S(1)}, u32[]{:S(2)}, u32[]{:S(2)}) collective-permute-start(f32[2,128,256]{2,1,0:T(8,128)S(1)} %get-tuple-element.58), channel_id=1, source_target_pairs={{0,2},{2,0},{4,6},{6,4},{8,10},{10,8},{12,14},{14,12},{1,3},{3,1},... | collective-permute-start | bytes 786440 | tf_op jit(solution)/shard_map/ppermute | solution.py:379
  39.0 9.2 %collective-permute-start.6 = (f32[2,128,256]{2,1,0:T(8,128)S(1)}, f32[2,128,256]{2,1,0:T(8,128)S(1)}, u32[]{:S(2)}, u32[]{:S(2)}) collective-permute-start(f32[2,128,256]{2,1,0:T(8,128)S(1)} %get-tuple-element.59), channel_id=1, source_target_pairs={{0,4},{2,6},{4,0},{6,2},{8,12},{10,14},{12,8},{14,10},{1,5},{3,7},... | collective-permute-start | bytes 786440 | tf_op jit(solution)/shard_map/ppermute | solution.py:379
  39.0 12.5 %collective-permute-start.7 = (f32[2,128,256]{2,1,0:T(8,128)S(1)}, f32[2,128,256]{2,1,0:T(8,128)S(1)}, u32[]{:S(2)}, u32[]{:S(2)}) collective-permute-start(f32[2,128,256]{2,1,0:T(8,128)S(1)} %get-tuple-element.60), channel_id=1, source_target_pairs={{0,6},{2,4},{4,2},{6,0},{8,14},{10,12},{12,10},{14,8},{1,7},{3,5},... | collective-permute-start | bytes 786440 | tf_op jit(solution)/shard_map/ppermute | solution.py:379
  56.3 6.9 %copy-start.7 = (f32[4,128,256]{2,1,0:T(8,128)S(1)}, f32[4,128,256]{2,1,0:T(8,128)}, u32[]{:S(2)}) copy-start(f32[4,128,256]{2,1,0:T(8,128)} %get-tuple-element.68) | copy-start | bytes 1572868
  56.3 30.3 %copy-start.4 = (f32[4,128,256]{2,1,0:T(8,128)S(1)}, f32[4,128,256]{2,1,0:T(8,128)}, u32[]{:S(2)}) copy-start(f32[4,128,256]{2,1,0:T(8,128)} %get-tuple-element.67.kept_ref) | copy-start | bytes 1572868
  56.3 34.4 %all-to-all-start = ((f32[8,136,256]{2,1,0:T(8,128)}), f32[8,136,256]{2,1,0:T(8,128)S(1)}, u32[]{:S(2)}, u32[]{:S(2)}) async-start(f32[8,136,256]{2,1,0:T(8,128)} %get-tuple-element.72), calls=%async_computation | async-start | bytes 2228224 | tf_op jit(solution)/shard_map/all_to_all | solution.py:486
  63.2 23.4 %collective-permute-start.11 = (f32[4,128,256]{2,1,0:T(8,128)S(1)}, f32[4,128,256]{2,1,0:T(8,128)S(1)}, u32[]{:S(2)}, u32[]{:S(2)}) collective-permute-start(f32[4,128,256]{2,1,0:T(8,128)S(1)} %copy-done.7), channel_id=1, source_target_pairs={{0,2},{2,0},{4,6},{6,4},{8,10},{10,8},{12,14},{14,12},{1,3},{3,1},... | collective-permute-start | bytes 1572872 | tf_op jit(solution)/shard_map/ppermute | solution.py:379
  65.3 22.4 %collective-permute-start.9 = (f32[2,128,256]{2,1,0:T(8,128)S(1)}, f32[2,128,256]{2,1,0:T(8,128)S(1)}, u32[]{:S(2)}, u32[]{:S(2)}) collective-permute-start(f32[2,128,256]{2,1,0:T(8,128)S(1)} %get-tuple-element.64), channel_id=1, source_target_pairs={{0,4},{2,6},{4,0},{6,2},{8,12},{10,14},{12,8},{14,10},{1,5},{3,7},... | collective-permute-start | bytes 786440 | tf_op jit(solution)/shard_map/ppermute | solution.py:379
  86.7 10.2 %collective-permute-start.12 = (f32[2,128,256]{2,1,0:T(8,128)S(1)}, f32[2,128,256]{2,1,0:T(8,128)S(1)}, u32[]{:S(2)}, u32[]{:S(2)}) collective-permute-start(f32[2,128,256]{2,1,0:T(8,128)S(1)} %get-tuple-element.70.refs_0_), channel_id=1, source_target_pairs={{0,4},{2,6},{4,0},{6,2},{8,12},{10,14},{12,8},{14,10},{1,5},{3,7},... | collective-permute-start | bytes 786440 | tf_op jit(solution)/shard_map/ppermute | solution.py:379
  87.7 14.9 %collective-permute-start.10 = (f32[1,128,256]{2,1,0:T(8,128)S(1)}, f32[1,128,256]{2,1,0:T(8,128)S(1)}, u32[]{:S(2)}, u32[]{:S(2)}) collective-permute-start(f32[1,128,256]{2,1,0:T(8,128)S(1)} %get-tuple-element.66.refs_1_), channel_id=1, source_target_pairs={{0,8},{2,10},{4,12},{6,14},{8,0},{10,2},{12,4},{14,6},{1,9},{3,11}... | collective-permute-start | bytes 393224 | tf_op jit(solution)/shard_map/ppermute | solution.py:379
  97.6 7.8 %collective-permute-start.13 = (f32[1,128,256]{2,1,0:T(8,128)S(1)}, f32[1,128,256]{2,1,0:T(8,128)S(1)}, u32[]{:S(2)}, u32[]{:S(2)}) collective-permute-start(f32[1,128,256]{2,1,0:T(8,128)S(1)} %get-tuple-element.76), channel_id=1, source_target_pairs={{0,8},{2,10},{4,12},{6,14},{8,0},{10,2},{12,4},{14,6},{1,9},{3,11}... | collective-permute-start | bytes 393224 | tf_op jit(solution)/shard_map/ppermute | solution.py:379
  97.7 12.9 %all-to-all-start.1 = ((f32[16,8,256]{2,1,0:T(8,128)}), f32[16,8,256]{2,1,0:T(8,128)S(1)}, u32[]{:S(2)}, u32[]{:S(2)}) async-start(f32[16,8,256]{2,1,0:T(8,128)} %get-tuple-element.79), calls=%async_computation.1 | async-start | bytes 262144 | tf_op jit(solution)/shard_map/all_to_all | solution.py:516
  105.4 5.2 %collective-permute-start.14 = (f32[2,64,256]{2,1,0:T(8,128)S(1)}, f32[2,64,256]{2,1,0:T(8,128)S(1)}, u32[]{:S(2)}, u32[]{:S(2)}) collective-permute-start(f32[2,64,256]{2,1,0:T(8,128)S(1)} %get-tuple-element.78), channel_id=1, source_target_pairs={{0,1},{1,0},{2,3},{3,2},{4,5},{5,4},{6,7},{7,6},{8,9},{9,8},{10,11... | collective-permute-start | bytes 393224 | tf_op jit(solution)/shard_map/ppermute | solution.py:379
  (1 other events, 1.2 us)

commit v15 on v13

--- a/solution.py
+++ b/solution.py
@@ -108,14 +108,18 @@
     wait_all(stores)
 
 
-def route_kernel(devices, capacity, list_ref, kinship_hbm, direction_ref, gate_ref, table_ref, forward_ref, high_hbm,
-                 low_hbm, *refs):
+def tiles_kernel(kinship_hbm, high_hbm, low_hbm, kinship_ref, high_ref, low_ref, semaphores):
+    copies = Copies(semaphores)
+    copies.start(kinship_hbm, kinship_ref).wait()
+    split_tiles(kinship_ref, high_ref, low_ref)
+    wait_all([copies.start(high_ref, high_hbm), copies.start(low_ref, low_hbm)])
+
+
+def route_kernel(devices, capacity, block_count, list_ref, direction_ref, gate_ref, table_ref, forward_ref, *refs):
     half = devices // 2
-    outgoing_refs, refs = refs[:half - 1], refs[half - 1:]
-    first_ref, last_ref, kinship_ref, high_ref, low_ref, semaphores = refs
-    copies = Copies(semaphores)
-    load = copies.start(kinship_hbm, kinship_ref)
-    block_count, positions, tile = kinship_ref.shape[:3]
+    outgoing_refs, (first_ref, last_ref) = refs[:half - 1], refs[half - 1:]
+    positions = list_ref.shape[0] + 1
+    tile = direction_ref.shape[0] // block_count
     me = lax.axis_index("samples")
     partner = me ^ half
     spare = me ^ 1
@@ -166,14 +170,10 @@
         blocks = blocks_for(me, other)
         table_ref[3, other] = jnp.where(me < other, blocks[1], blocks[0])
     near = [blocks_for(me, me ^ k) for k in range(1, half)]
-    load.wait()
-    split_tiles(kinship_ref, high_ref, low_ref)
-    stores = [copies.start(high_ref, high_hbm), copies.start(low_ref, low_hbm)]
     for k in range(1, half):
         for slot in range(capacity):
             start = pl.multiple_of(near[k - 1][slot] * tile, tile)
             outgoing_refs[k - 1][slot] = direction_ref[pl.ds(start, tile), :]
-    wait_all(stores)
 
 
 def forward_kernel(forward_ref, partner_ref, *refs):
@@ -191,10 +191,10 @@
     me = lax.axis_index("samples")
     near_refs, far_refs, partner_ref = received_refs[:half - 1], received_refs[half - 1:-1], received_refs[-1]
     gathered_ref[pl.ds(devices * capacity, partner_ref.shape[0])] = partner_ref[...]
-    for k in range(1, half):
-        mate = me ^ k
-        gathered_ref[pl.ds(mate * capacity, capacity)] = near_refs[k - 1][...]
-        gathered_ref[pl.ds((mate ^ half) * capacity, capacity)] = far_refs[k - 1][...]
+    for i in range(half - 1):
+        mate = me ^ (half - 1 - i)
+        gathered_ref[pl.ds(mate * capacity, capacity)] = near_refs[i][...]
+        gathered_ref[pl.ds((mate ^ half) * capacity, capacity)] = far_refs[i][...]
 
 
 def score_products(high_ref, low_ref, values, even_ref, odd_ref):
@@ -210,11 +210,10 @@
     score_products(high_ref, low_ref, values_ref[...], even_ref, odd_ref)
 
 
-def apply_kernel(devices, capacity, table_ref, high_hbm, low_hbm, diagonal_hbm, direction_ref, norm_ref, dosage_high_ref,
-                 dosage_low_ref, *refs):
+def apply_kernel(devices, capacity, table_ref, high_hbm, low_hbm, diagonal_hbm, direction_ref, norm_ref, *refs):
     received_refs = refs[:devices - 1]
-    (scaled_hbm, handled_hbm, outgoing_hbm, even_ref, odd_ref, gathered_ref, high_ref, low_ref, diagonal_ref, scaled_ref,
-     handled_ref, sums_ref, semaphores) = refs[-13:]
+    (scaled_ref, scaled_hbm, handled_hbm, outgoing_hbm, gathered_ref, high_ref, low_ref, diagonal_ref, handled_ref,
+     sums_ref, semaphores) = refs[-11:]
     copies = Copies(semaphores)
     loads = [
         copies.start(high_hbm, high_ref), copies.start(low_hbm, low_ref), copies.start(diagonal_hbm, diagonal_ref)
@@ -233,12 +232,12 @@
         cross = cross + column_sums(here * mapped)
     row_ids = lax.broadcasted_iota(jnp.int32, cross.shape, 0)
     sums_ref[...] = jnp.where(row_ids == 1, jnp.sum(cross, axis=0, keepdims=True), norm_ref[...])
-    stores = [copies.start(scaled_ref, scaled_hbm)]
+    stores = []
     for other in range(devices):
         start = pl.multiple_of(table_ref[3, other] * tile, tile)
         stores.append(copies.start(scaled_ref.at[pl.ds(start, tile)], outgoing_hbm.at[other, pl.ds(0, tile)]))
         stores.append(copies.start(sums_ref, outgoing_hbm.at[other, pl.ds(tile, SUBLANES)]))
-    score_products(dosage_high_ref, dosage_low_ref, scaled_ref[...], even_ref, odd_ref)
+    stores.append(copies.start(scaled_ref, scaled_hbm))
     far = pl.ds(tile, depth - tile)
     for row in range(block_count):
         blocks = []
@@ -286,7 +285,8 @@
     copies.start(sums_ref, sums_hbm).wait()
 
 
-def add_kernel(kept_ref, taken_ref, near_ref, far_ref):
+def add_kernel(kept_ref, taken_ref, *refs):
+    near_ref, far_ref = refs[-2:]
     count = near_ref.shape[0]
     near_ref[...] = kept_ref[pl.ds(0, count)] + taken_ref[pl.ds(0, count)]
     far_ref[...] = kept_ref[pl.ds(count, count)] + taken_ref[pl.ds(count, count)]
@@ -324,8 +324,8 @@
     return start * (1.0 + step * (ratio + cross / norm)), -start * step
 
 
-def finish_kernel(devices, norm_scale, direction_hbm, scaled_hbm, own_scores_ref, other_scores_ref, sums_ref, solved_hbm,
-                  scores_ref, direction_ref, scaled_ref, semaphores):
+def solved_kernel(devices, direction_hbm, scaled_hbm, sums_ref, solved_hbm, factors_ref, direction_ref, scaled_ref,
+                  semaphores):
     people, columns = direction_ref.shape
     column = lax.axis_index("cols")
     copies = Copies(semaphores)
@@ -339,7 +339,8 @@
         return sums, shared
 
     along, across = coefficients(*total(column))
-    other_along, other_across = coefficients(*total(1 - column))
+    factors = jnp.concatenate([along, across, *coefficients(*total(1 - column))], axis=0)
+    factors_ref[...] = jnp.concatenate([factors, factors], axis=0)
     wait_all(loads)
     stores = []
     part_rows = people // 4
@@ -347,15 +348,16 @@
         block = pl.ds(part * part_rows, part_rows)
         direction_ref[block, :] = along * direction_ref[block, :] + across * scaled_ref[block, :]
         stores.append(copies.start(direction_ref.at[block], solved_hbm.at[block]))
-    own = pl.multiple_of(column * columns, columns)
-    other = pl.multiple_of((1 - column) * columns, columns)
-    scores_ref[:, pl.ds(own, columns)] = norm_scale * (
-        along * own_scores_ref[0] + across * own_scores_ref[1]
-    )
-    scores_ref[:, pl.ds(other, columns)] = norm_scale * (
-        other_along * other_scores_ref[0] + other_across * other_scores_ref[1]
-    )
     wait_all(stores)
+
+
+def scores_kernel(norm_scale, factors_ref, own_ref, other_ref, scores_ref):
+    columns = own_ref.shape[2]
+    column = lax.axis_index("cols")
+    for which, rows_ref, place in ((0, own_ref, column), (2, other_ref, 1 - column)):
+        along, across = factors_ref[which:which + 1, :], factors_ref[which + 1:which + 2, :]
+        here = pl.ds(pl.multiple_of(place * columns, columns), columns)
+        scores_ref[:, here] = norm_scale * (along * rows_ref[0] + across * rows_ref[1])
 
 
 def call(kernel, out_shape, in_specs, out_specs, scratch_shapes=(), limit=VMEM_LIMIT):
@@ -395,8 +397,9 @@
     full = float_of(people, columns)
     full_room = room(people, columns)
     half = devices // 2
-    near_by = list(range(1, half))
-    kinship = pltpu.with_memory_space_constraint(kinship, pltpu.HBM)
+    near_by = list(range(half - 1, 0, -1))
+    at_home = lambda *arrays: [pltpu.with_memory_space_constraint(array, pltpu.HBM) for array in arrays]
+    kinship, = at_home(kinship)
     tiles_room = pltpu.VMEM((block_count, tile, positions * tile), jnp.bfloat16)
     tiles_out = pltpu.HBM((block_count, tile, positions * tile), jnp.bfloat16)
     full_out = pltpu.HBM((people, columns), jnp.float32)
@@ -410,32 +413,29 @@
             pltpu.SemaphoreType.DMA((3 * block_count + 2,)),
         ],
     )(
-        kinship,
-        pltpu.with_memory_space_constraint(variance.reshape(block_count, tile), pltpu.HBM),
-        pltpu.with_memory_space_constraint(phenotypes, pltpu.HBM),
+        kinship, *at_home(variance.reshape(block_count, tile), phenotypes)
     )
     def to_mates(blocks):
-        return [swap(block, "samples", devices, k) for k, block in zip(near_by, blocks)]
+        return [swap(blocks[k - 1], "samples", devices, k) for k in near_by]
 
     bits = half.bit_length() - 1
     even = [sum(((i >> b) & 1) << (bits - b) for b in range(bits)) for i in range(half)]
     steps = [2 << i for i in range(bits)]
     other_dosage = with_layout_constraint(swap(after(dosage, direction), "cols", 2, 1), Layout((0, 1)))
-    table, forward, high, low, *outgoing = call(
-        functools.partial(route_kernel, devices, capacity),
+    table, forward, *outgoing = call(
+        functools.partial(route_kernel, devices, capacity, block_count),
         [
             jax.ShapeDtypeStruct((4, max(entries, devices)), jnp.int32),
             jax.ShapeDtypeStruct((capacity, half), jnp.int32),
-            tiles_out, tiles_out,
         ] + [float_of(capacity, tile, columns)] * (half - 1),
-        [smem, hbm, vmem, anywhere],
-        [smem, smem, hbm, hbm] + [vmem] * (half - 1),
-        [
-            pltpu.SMEM((devices,), jnp.int32), pltpu.SMEM((devices,), jnp.int32),
-            room(*kinship.shape), tiles_room, tiles_room, pltpu.SemaphoreType.DMA((3,)),
-        ],
-    )(relatives.T, kinship, direction, other_dosage)
-
+        [smem, vmem, anywhere],
+        [smem, smem] + [vmem] * (half - 1),
+        [pltpu.SMEM((devices,), jnp.int32), pltpu.SMEM((devices,), jnp.int32)],
+    )(relatives.T, direction, other_dosage)
+    high, low = call(
+        tiles_kernel, [tiles_out] * 2, [hbm], [hbm] * 2,
+        [room(*kinship.shape), tiles_room, tiles_room, pltpu.SemaphoreType.DMA((3,))],
+    )(kinship)
 
     parts = jax.ShapeDtypeStruct((2, variants, people), jnp.bfloat16)
     large = VMEM_LIMIT if variants <= people else LARGE_VMEM
@@ -445,9 +445,11 @@
 
     products = float_of(half, 2 * share_rows, columns)
 
-    def add_step(kept, taken):
+    def add_step(kept, taken, *gates):
         rows = float_of(kept.shape[0] // 2, 2 * share_rows, columns)
-        return call(add_kernel, [rows] * 2, [vmem] * 2, [vmem] * 2)(kept, taken)
+        return call(
+            add_kernel, [rows] * 2, [vmem] * 2 + [hbm] * len(gates), [vmem] * 2
+        )(kept, taken, *at_home(*gates))
 
     partner = swap(direction, "samples", devices, half)
     near = to_mates(outgoing)
@@ -458,23 +460,24 @@
     far = to_mates(call(
         forward_kernel,
         [float_of(capacity, tile, columns)] * (half - 1),
-        [smem, vmem] + [anywhere] * (half + 1),
+        [smem, vmem] + [anywhere] * (half + 1) + [hbm] * 2,
         [vmem] * (half - 1),
-    )(forward, partner, *near, direction_even, direction_odd))
+    )(forward, partner, *near, direction_even, direction_odd, *at_home(high, low)))
     received = near + far + [partner.reshape(block_count, tile, columns)]
-    scaled, handled, outgoing, scaled_even, scaled_odd = call(
+    scaled_here, scaled, handled, outgoing = call(
         functools.partial(apply_kernel, devices, capacity),
+        [full, full_out, full_out, pltpu.HBM((devices, tile + SUBLANES, columns), jnp.float32)],
+        [smem, hbm, hbm, hbm] + [vmem] * (devices + 1) + [anywhere],
+        [vmem] + [hbm] * 3,
         [
-            full_out, full_out, pltpu.HBM((devices, tile + SUBLANES, columns), jnp.float32), products, products,
-        ],
-        [smem, hbm, hbm, hbm] + [vmem] * (devices + 3) + [anywhere],
-        [hbm, hbm, hbm, vmem, vmem],
-        [
-            room(devices * capacity + block_count, tile, columns), tiles_room, tiles_room, room(people, 1), full_room,
+            room(devices * capacity + block_count, tile, columns), tiles_room, tiles_room, room(people, 1),
             full_room, room(SUBLANES, columns), pltpu.SemaphoreType.DMA((2 * devices + 5,)),
         ],
         limit=large,
-    )(table, high, low, diagonal, direction, norm, *grouped, *received, direction_share)
+    )(table, *at_home(high, low, diagonal), direction, norm, *received, direction_share)
+    scaled_even, scaled_odd = call(
+        score_kernel, [products] * 2, [vmem] * 3, [vmem] * 2, limit=large
+    )(*grouped, scaled_here)
     later = lax.all_to_all(outgoing, "samples", split_axis=0, concat_axis=0, tiled=True)
     scaled_share = swap(scaled_odd, "samples", devices, 1)
     direction_kept, direction_given = add_step(direction_even, direction_share)
@@ -482,33 +485,39 @@
     for step in steps[:-1]:
         direction_taken = swap(after(direction_given, scaled), "samples", devices, step)
         direction_kept, direction_given = add_step(direction_kept, direction_taken)
-        scaled_taken = swap(scaled_given, "samples", devices, step)
-        scaled_kept, scaled_given = add_step(scaled_kept, scaled_taken)
     direction_taken = swap(direction_given, "samples", devices, steps[-1])
-    scaled_taken = swap(scaled_given, "samples", devices, steps[-1])
-    rows = float_of(2, share_rows, columns)
-    own_scores, other_scores = call(
-        last_add_kernel, [rows] * 2, [vmem] * 4, [vmem] * 2
-    )(direction_kept, direction_taken, scaled_kept, scaled_taken)
-    other_scores = swap(other_scores, "cols", 2, 1)
+    scaled_taken = swap(scaled_given, "samples", devices, steps[0])
     sums = call(
         functools.partial(curvature_kernel, devices),
         pltpu.HBM((2 * devices, SUBLANES, columns), jnp.float32),
-        [smem] + [hbm] * 6 + [anywhere] * 2,
+        [smem] + [hbm] * 6 + [anywhere] * 3,
         hbm,
         [
             room(2 * devices, SUBLANES, columns), tiles_room, tiles_room, full_room, room(people, 1), full_room,
             full_room, room(devices, tile + SUBLANES, columns), pltpu.SemaphoreType.DMA((8,)),
         ],
-    )(table, high, low, direction_kept_hbm, diagonal, scaled, handled, later, other_scores)
+    )(
+        table, *at_home(high, low, direction_kept_hbm, diagonal, scaled, handled), later, scaled_given, direction_given
+    )
     all_sums = lax.all_to_all(sums, ("samples", "cols"), split_axis=0, concat_axis=0, tiled=True)
-    solved, scores = call(
-        functools.partial(finish_kernel, devices, 1.0 / math.sqrt(people * devices)),
-        [full, float_of(share_rows, 2 * columns)],
-        [hbm, hbm, vmem, vmem, vmem],
+    for step in steps[1:]:
+        scaled_kept, scaled_given = add_step(scaled_kept, scaled_taken, sums)
+        scaled_taken = swap(scaled_given, "samples", devices, step)
+    rows = float_of(2, share_rows, columns)
+    own_scores, other_scores = call(
+        last_add_kernel, [rows] * 2, [vmem] * 4, [vmem] * 2
+    )(direction_kept, direction_taken, scaled_kept, scaled_taken)
+    solved, factors = call(
+        functools.partial(solved_kernel, devices),
+        [full, float_of(SUBLANES, columns)],
+        [hbm, hbm, vmem],
         [hbm, vmem],
         [full_room, full_room, pltpu.SemaphoreType.DMA((6,))],
-    )(direction_kept_hbm, scaled, own_scores, other_scores, all_sums)
+    )(*at_home(direction_kept_hbm, scaled), all_sums)
+    scores = call(
+        functools.partial(scores_kernel, 1.0 / math.sqrt(people * devices)),
+        float_of(share_rows, 2 * columns), [vmem] * 3, vmem,
+    )(factors, own_scores, swap(other_scores, "cols", 2, 1))
     return (solved, scores)
 
 

time: 127 us -> 115 us (0.906)
  blocking collectives: 11.4 us -> 0 us
  waiting for transfers between devices: 60.7 us -> 52.1 us
  starting transfers between devices: 27.4 us -> 32.5 us
  Pallas kernels: 16.7 us -> 21.6 us
  local copies, waits for them, and re-layouts: 9 us -> 6.96 us
    ppermute x15, waiting for transfers between devices: 60.7 us -> 46.6 us  [swap(): return lax.ppermute(values, axis, [(i, i ^ step) for i in range(devices)])]
    all_to_all x1 -> x0, blocking collectives: 11.4 us -> none  [per_device(): lax.all_to_all(sums, ('samples', 'cols'), split_axis=0, concat_axis=0, ti...]
    all_to_all x0 -> x1, waiting for transfers between devices: none -> 5.47 us  [per_device(): lax.all_to_all(sums, ('samples', 'cols'), split_axis=0, concat_axis=0, ti...]
    all_to_all x0 -> x1, starting transfers between devices: none -> 4.43 us  [per_device(): lax.all_to_all(sums, ('samples', 'cols'), split_axis=0, concat_axis=0, ti...]
    pallas_call x7 -> x9, Pallas kernels: 9.98 us -> 11.9 us  [the longest x1 4.86 us: per_device(): call(functools.partial(apply_kernel, devices, capacity), [full, full_out,...]
    unnamed x40 -> x20, local copies, waits for them, and re-layouts: 6.1 us -> 4.32 us
    ppermute x15, starting transfers between devices: 20.5 us -> 22.1 us  [swap(): return lax.ppermute(values, axis, [(i, i ^ step) for i in range(devices)])]
    pallas_call x1, Pallas kernels: 2.47 us -> 3.97 us  [per_device(): call(functools.partial(curvature_kernel, devices), pltpu.HBM((2 * devices...]
  transfers between devices with their start and end apart: 16 -> 17, of which waited for: 10 -> 9; matrix products, arithmetic and copies ran while one was open for 2% -> 2% of each run, Pallas kernels for 5% -> 12%
where the time goes in v15:
time: 115 us; the launch traced here: 114 us
  waiting for transfers between devices  52.1 us (45%)
  starting transfers between devices  32.5 us (28%)
  Pallas kernels  21.6 us (19%)
  local copies, waits for them, and re-layouts  6.96 us (6%)
    ppermute x15, waiting for transfers between devices, swap(): return lax.ppermute(values, axis, [(i, i ^ step) for i in range(devices)])  46.6 us
    ppermute x15, starting transfers between devices, swap(): return lax.ppermute(values, axis, [(i, i ^ step) for i in range(devices)])  22.1 us
    all_to_all x1, starting transfers between devices, per_device(): lax.all_to_all(outgoing, 'samples', split_axis=0, concat_axis=0, tiled=True)  5.94 us
    all_to_all x1, waiting for transfers between devices, per_device(): lax.all_to_all(sums, ('samples', 'cols'), split_axis=0, concat_axis=0, ti...  5.47 us
    pallas_call x1, Pallas kernels, per_device(): call(functools.partial(apply_kernel, devices, capacity), [full, full_out,...  4.86 us
    all_to_all x1, starting transfers between devices, per_device(): lax.all_to_all(sums, ('samples', 'cols'), split_axis=0, concat_axis=0, ti...  4.43 us
    unnamed x20, local copies, waits for them, and re-layouts  4.32 us
    pallas_call x1, Pallas kernels, per_device(): call(functools.partial(curvature_kernel, devices), pltpu.HBM((2 * devices...  3.97 us
  transfers between devices with their start and end apart: 17, of which 9 were waited for; matrix products, arithmetic and copies ran while one was open for 2% of the time, Pallas kernels for 12%

profile of v15, /device:TPU:0, one launch (start us, length us, event | category | flops | bytes accessed | tf_op | source)
XLA Modules:
  0.0 114.0 jit_solution(4988027615435955574)
XLA Ops:
  0.7 2.4 %shard_map.68 = (f32[512,256]{1,0:T(8,128)S(1)}, f32[512,256]{1,0:T(8,128)}, f32[512,1]{1,0:T(8,128)}, f32[8,256]{1,0:T(8,128)S(1)}) custom-call(f32[4,4,128,128]{3,2,1,0:T(8,128)} %kinship_hbm.3, f32[4,128]{1,0:T(4,128)} %bitcast.8, f32[512,256]{1,0:T(8,128)} %phenotypes_hbm.1), custom_call_target="tpu_custom_call" | custom-call | tf_op jit(solution)/shard_map/pallas_call | solution.py:406
  3.6 3.7 %collective-permute-start.4 = (f32[512,256]{1,0:T(8,128)S(1)}, f32[512,256]{1,0:T(8,128)}, u32[]{:S(2)}, u32[]{:S(2)}) collective-permute-start(f32[512,256]{1,0:T(8,128)S(1)} %get-tuple-element.42.direction_ref.values_ref), channel_id=1, source_target_pairs={{0,8},{2,10},{4,12},{6,14},{8,0},{10,2},{12,4},{14,6},{1,9},{3,11}... | collective-permute-start | bytes 1572872 | tf_op jit(solution)/shard_map/ppermute | solution.py:375
  7.3 1.8 %shard_map.69 = (s32[4,12]{1,0:T(4,128)S(1)}, s32[2,4]{1,0:T(2,128)S(1)}, f32[2,128,256]{2,1,0:T(8,128)}, f32[2,128,256]{2,1,0:T(8,128)}, f32[2,128,256]{2,1,0:T(8,128)}) custom-call(s32[3,32]{1,0:T(4,128)S(1)} %bitcast.7, f32[512,256]{1,0:T(8,128)S(1)} %get-tuple-element.42.direction_ref.values_ref, f32[512,512]{1,0:T(8,128)S(1)} %collective-permute-done.gate_ref), custom_call_target="tpu_custom_call" | custom-call | tf_op jit(solution)/shard_map/pallas_call | solution.py:425
  9.1 2.6 %collective-permute-start.1 = (f32[2,128,256]{2,1,0:T(8,128)}, f32[2,128,256]{2,1,0:T(8,128)S(1)}, u32[]{:S(2)}, u32[]{:S(2)}) collective-permute-start(f32[2,128,256]{2,1,0:T(8,128)} %get-tuple-element.49), channel_id=1, source_target_pairs={{0,6},{2,4},{4,2},{6,0},{8,14},{10,12},{12,10},{14,8},{1,7},{3,5},... | collective-permute-start | bytes 786440 | tf_op jit(solution)/shard_map/ppermute | solution.py:375
  19.0 1.6 %collective-permute-start.8 = (f32[4,128,256]{2,1,0:T(8,128)S(1)}, f32[4,128,256]{2,1,0:T(8,128)S(1)}, u32[]{:S(2)}, u32[]{:S(2)}) collective-permute-start(f32[4,128,256]{2,1,0:T(8,128)S(1)} %get-tuple-element.57.refs_4_), channel_id=1, source_target_pairs={{0,2},{2,0},{4,6},{6,4},{8,10},{10,8},{12,14},{14,12},{1,3},{3,1},... | collective-permute-start | bytes 1572872 | tf_op jit(solution)/shard_map/ppermute | solution.py:375
  20.6 2.3 %shard_map.70 = (bf16[4,128,512]{2,1,0:T(8,128)(2,1)}, bf16[4,128,512]{2,1,0:T(8,128)(2,1)}) custom-call(f32[4,4,128,128]{3,2,1,0:T(8,128)} %kinship_hbm.3), custom_call_target="tpu_custom_call" | custom-call | tf_op jit(solution)/shard_map/pallas_call | solution.py:435
  22.9 8.3 %collective-permute-done.4.partner_ref = f32[512,256]{1,0:T(8,128)} collective-permute-done((f32[512,256]{1,0:T(8,128)S(1)}, f32[512,256]{1,0:T(8,128)}, u32[]{:S(2)}, u32[]{:S(2)}) %collective-permute-start.4) | collective-permute-done | bytes 524320 | tf_op jit(solution)/shard_map/ppermute | solution.py:375
  31.3 3.3 %collective-permute-done.2.refs_1_ = f32[2,128,256]{2,1,0:T(8,128)} collective-permute-done((f32[2,128,256]{2,1,0:T(8,128)}, f32[2,128,256]{2,1,0:T(8,128)}, u32[]{:S(2)}, u32[]{:S(2)}) %collective-permute-start.2) | collective-permute-done | bytes 262176 | tf_op jit(solution)/shard_map/ppermute | solution.py:375
  35.8 2.0 %collective-permute-start.6 = (f32[2,128,256]{2,1,0:T(8,128)S(1)}, f32[2,128,256]{2,1,0:T(8,128)S(1)}, u32[]{:S(2)}, u32[]{:S(2)}) collective-permute-start(f32[2,128,256]{2,1,0:T(8,128)S(1)} %get-tuple-element.59), channel_id=1, source_target_pairs={{0,4},{2,6},{4,0},{6,2},{8,12},{10,14},{12,8},{14,10},{1,5},{3,7},... | collective-permute-start | bytes 786440 | tf_op jit(solution)/shard_map/ppermute | solution.py:375
  39.3 6.7 %collective-permute-done.5.refs_3_ = f32[2,128,256]{2,1,0:T(8,128)S(1)} collective-permute-done((f32[2,128,256]{2,1,0:T(8,128)S(1)}, f32[2,128,256]{2,1,0:T(8,128)S(1)}, u32[]{:S(2)}, u32[]{:S(2)}) %collective-permute-start.5) | collective-permute-done | bytes 262176 | tf_op jit(solution)/shard_map/ppermute | solution.py:375
  45.9 3.0 %collective-permute-done.6.refs_4_ = f32[2,128,256]{2,1,0:T(8,128)S(1)} collective-permute-done((f32[2,128,256]{2,1,0:T(8,128)S(1)}, f32[2,128,256]{2,1,0:T(8,128)S(1)}, u32[]{:S(2)}, u32[]{:S(2)}) %collective-permute-start.6) | collective-permute-done | bytes 262176 | tf_op jit(solution)/shard_map/ppermute | solution.py:375
  49.8 4.9 %shard_map.74 = (f32[512,256]{1,0:T(8,128)S(1)}, f32[512,256]{1,0:T(8,128)}, f32[512,256]{1,0:T(8,128)}, f32[8,136,256]{2,1,0:T(8,128)}) custom-call(s32[4,12]{1,0:T(4,128)S(1)} %get-tuple-element.44.table_ref, bf16[4,128,512]{2,1,0:T(8,128)(2,1)} %get-tuple-element.45.refs_5_.high_hbm, bf16[4,128,512]{2,1,0:T(8,128)(2,1)} %get-tuple-element.46.refs_6_.low_hbm, ...), custom_call_target="tpu_custom_call" | custom-call | tf_op jit(solution)/shard_map/pallas_call | solution.py:467
  55.5 5.9 %all-to-all-start = ((f32[8,136,256]{2,1,0:T(8,128)}), f32[8,136,256]{2,1,0:T(8,128)S(1)}, u32[]{:S(2)}, u32[]{:S(2)}) async-start(f32[8,136,256]{2,1,0:T(8,128)} %get-tuple-element.63), calls=%async_computation | async-start | bytes 2228224 | tf_op jit(solution)/shard_map/all_to_all | solution.py:481
  63.5 2.1 %collective-permute-start.9 = (f32[4,128,256]{2,1,0:T(8,128)S(1)}, f32[4,128,256]{2,1,0:T(8,128)S(1)}, u32[]{:S(2)}, u32[]{:S(2)}) collective-permute-start(f32[4,128,256]{2,1,0:T(8,128)S(1)} %get-tuple-element.66), channel_id=1, source_target_pairs={{0,2},{2,0},{4,6},{6,4},{8,10},{10,8},{12,14},{14,12},{1,3},{3,1},... | collective-permute-start | bytes 1572872 | tf_op jit(solution)/shard_map/ppermute | solution.py:375
  65.6 1.5 %collective-permute-start.10 = (f32[2,128,256]{2,1,0:T(8,128)S(1)}, f32[2,128,256]{2,1,0:T(8,128)S(1)}, u32[]{:S(2)}, u32[]{:S(2)}) collective-permute-start(f32[2,128,256]{2,1,0:T(8,128)S(1)} %get-tuple-element.70), channel_id=1, source_target_pairs={{0,4},{2,6},{4,0},{6,2},{8,12},{10,14},{12,8},{14,10},{1,5},{3,7},... | collective-permute-start | bytes 786440 | tf_op jit(solution)/shard_map/ppermute | solution.py:375
  67.2 20.0 %collective-permute-done.9.taken_ref = f32[4,128,256]{2,1,0:T(8,128)S(1)} collective-permute-done((f32[4,128,256]{2,1,0:T(8,128)S(1)}, f32[4,128,256]{2,1,0:T(8,128)S(1)}, u32[]{:S(2)}, u32[]{:S(2)}) %collective-permute-start.9) | collective-permute-done | bytes 524320 | tf_op jit(solution)/shard_map/ppermute | solution.py:375
  88.7 2.4 %collective-permute-start.11 = (f32[1,128,256]{2,1,0:T(8,128)S(1)}, f32[1,128,256]{2,1,0:T(8,128)S(1)}, u32[]{:S(2)}, u32[]{:S(2)}) collective-permute-start(f32[1,128,256]{2,1,0:T(8,128)S(1)} %get-tuple-element.71.refs_1_), channel_id=1, source_target_pairs={{0,8},{2,10},{4,12},{6,14},{8,0},{10,2},{12,4},{14,6},{1,9},{3,11}... | collective-permute-start | bytes 393224 | tf_op jit(solution)/shard_map/ppermute | solution.py:375
  91.2 4.0 %shard_map.79.refs_0_ = f32[16,8,256]{2,1,0:T(8,128)} custom-call(s32[4,12]{1,0:T(4,128)S(1)} %get-tuple-element.44.table_ref, bf16[4,128,512]{2,1,0:T(8,128)(2,1)} %get-tuple-element.45.refs_5_.high_hbm, bf16[4,128,512]{2,1,0:T(8,128)(2,1)} %get-tuple-element.46.refs_6_.low_hbm, f32[512,256]{1,0:T(8,128)} %get-tuple-element.41.direction_hbm, ...), custom_call_target="tpu_custom_call" | custom-call | tf_op jit(solution)/shard_map/pallas_call | solution.py:490
  95.2 2.1 %collective-permute-done.12.taken_ref = f32[2,128,256]{2,1,0:T(8,128)S(1)} collective-permute-done((f32[2,128,256]{2,1,0:T(8,128)S(1)}, f32[2,128,256]{2,1,0:T(8,128)S(1)}, u32[]{:S(2)}, u32[]{:S(2)}) %collective-permute-start.12) | collective-permute-done | bytes 262176 | tf_op jit(solution)/shard_map/ppermute | solution.py:375
  97.3 1.6 %collective-permute-start.13 = (f32[1,128,256]{2,1,0:T(8,128)S(1)}, f32[1,128,256]{2,1,0:T(8,128)S(1)}, u32[]{:S(2)}, u32[]{:S(2)}) collective-permute-start(f32[1,128,256]{2,1,0:T(8,128)S(1)} %get-tuple-element.77), channel_id=1, source_target_pairs={{0,8},{2,10},{4,12},{6,14},{8,0},{10,2},{12,4},{14,6},{1,9},{3,11}... | collective-permute-start | bytes 393224 | tf_op jit(solution)/shard_map/ppermute | solution.py:375
  98.9 4.4 %all-to-all-start.1 = ((f32[16,8,256]{2,1,0:T(8,128)}), f32[16,8,256]{2,1,0:T(8,128)S(1)}, u32[]{:S(2)}, u32[]{:S(2)}) async-start(f32[16,8,256]{2,1,0:T(8,128)} %shard_map.79.refs_0_), calls=%async_computation.1 | async-start | bytes 262144 | tf_op jit(solution)/shard_map/all_to_all | solution.py:502
  103.3 2.3 %collective-permute-done.13.second_taken_ref = f32[1,128,256]{2,1,0:T(8,128)S(1)} collective-permute-done((f32[1,128,256]{2,1,0:T(8,128)S(1)}, f32[1,128,256]{2,1,0:T(8,128)S(1)}, u32[]{:S(2)}, u32[]{:S(2)}) %collective-permute-start.13) | collective-permute-done | bytes 131104 | tf_op jit(solution)/shard_map/ppermute | solution.py:375
  105.8 5.5 %all-to-all-done.1.sums_ref = f32[16,8,256]{2,1,0:T(8,128)S(1)} async-done(((f32[16,8,256]{2,1,0:T(8,128)}), f32[16,8,256]{2,1,0:T(8,128)S(1)}, u32[]{:S(2)}, u32[]{:S(2)}) %all-to-all-start.1) | async-done | bytes 131104 | tf_op jit(solution)/shard_map/all_to_all | solution.py:502
  111.2 2.0 %shard_map.80 = (f32[512,256]{1,0:T(8,128)}, f32[8,256]{1,0:T(8,128)S(1)}) custom-call(f32[512,256]{1,0:T(8,128)} %get-tuple-element.41.direction_hbm, f32[512,256]{1,0:T(8,128)} %get-tuple-element.61.scaled_hbm, f32[16,8,256]{2,1,0:T(8,128)S(1)} %all-to-all-done.1.sums_ref), custom_call_target="tpu_custom_call" | custom-call | tf_op jit(solution)/shard_map/pallas_call | solution.py:510
  (48 shorter events, 16.6 us)
Async XLA Ops:
  0.6 2.5 %copy-start.9 = (f32[512,512]{1,0:T(8,128)S(1)}, f32[512,512]{1,0:T(8,128)}, u32[]{:S(2)}) copy-start(f32[512,512]{1,0:T(8,128)} %param.9) | copy-start | bytes 3145732
  0.6 6.7 %copy-start.8 = (s32[32,3]{0,1:T(4,128)S(1)}, s32[32,3]{0,1:T(4,128)}, u32[]{:S(2)}) copy-start(s32[32,3]{0,1:T(4,128)} %param.6) | copy-start | bytes 1156
  3.1 4.2 %collective-permute-start = (f32[512,512]{1,0:T(8,128)S(1)}, f32[512,512]{1,0:T(8,128)S(1)}, u32[]{:S(2)}, u32[]{:S(2)}) collective-permute-start(f32[512,512]{1,0:T(8,128)S(1)} %copy-done.9), channel_id=1, source_target_pairs={{0,1},{1,0},{2,3},{3,2},{4,5},{5,4},{6,7},{7,6},{8,9},{9,8},{10,11... | collective-permute-start | bytes 3145736 | tf_op jit(solution)/shard_map/ppermute | solution.py:375
  3.6 27.6 %collective-permute-start.4 = (f32[512,256]{1,0:T(8,128)S(1)}, f32[512,256]{1,0:T(8,128)}, u32[]{:S(2)}, u32[]{:S(2)}) collective-permute-start(f32[512,256]{1,0:T(8,128)S(1)} %get-tuple-element.42.direction_ref.values_ref), channel_id=1, source_target_pairs={{0,8},{2,10},{4,12},{6,14},{8,0},{10,2},{12,4},{14,6},{1,9},{3,11}... | collective-permute-start | bytes 1572872 | tf_op jit(solution)/shard_map/ppermute | solution.py:375
  9.1 22.1 %collective-permute-start.1 = (f32[2,128,256]{2,1,0:T(8,128)}, f32[2,128,256]{2,1,0:T(8,128)S(1)}, u32[]{:S(2)}, u32[]{:S(2)}) collective-permute-start(f32[2,128,256]{2,1,0:T(8,128)} %get-tuple-element.49), channel_id=1, source_target_pairs={{0,6},{2,4},{4,2},{6,0},{8,14},{10,12},{12,10},{14,8},{1,7},{3,5},... | collective-permute-start | bytes 786440 | tf_op jit(solution)/shard_map/ppermute | solution.py:375
  11.7 22.8 %collective-permute-start.2 = (f32[2,128,256]{2,1,0:T(8,128)}, f32[2,128,256]{2,1,0:T(8,128)}, u32[]{:S(2)}, u32[]{:S(2)}) collective-permute-start(f32[2,128,256]{2,1,0:T(8,128)} %get-tuple-element.50), channel_id=1, source_target_pairs={{0,4},{2,6},{4,0},{6,2},{8,12},{10,14},{12,8},{14,10},{1,5},{3,7},... | collective-permute-start | bytes 786440 | tf_op jit(solution)/shard_map/ppermute | solution.py:375
  12.2 22.4 %collective-permute-start.3 = (f32[2,128,256]{2,1,0:T(8,128)}, f32[2,128,256]{2,1,0:T(8,128)}, u32[]{:S(2)}, u32[]{:S(2)}) collective-permute-start(f32[2,128,256]{2,1,0:T(8,128)} %get-tuple-element.51), channel_id=1, source_target_pairs={{0,2},{2,0},{4,6},{6,4},{8,10},{10,8},{12,14},{14,12},{1,3},{3,1},... | collective-permute-start | bytes 786440 | tf_op jit(solution)/shard_map/ppermute | solution.py:375
  15.3 1.2 %copy-start = (f32[512,512]{0,1:T(8,128)S(1)}, f32[512,512]{0,1:T(8,128)}, u32[]{:S(2)}) copy-start(f32[512,512]{0,1:T(8,128)} %copy.7) | copy-start | bytes 3145732
  19.0 16.7 %copy-start.2 = (f32[4,128,256]{2,1,0:T(8,128)}, f32[4,128,256]{2,1,0:T(8,128)S(1)}, u32[]{:S(2)}) copy-start(f32[4,128,256]{2,1,0:T(8,128)S(1)} %get-tuple-element.56.refs_3_.kept_ref) | copy-start | bytes 1572868
  19.0 20.2 %collective-permute-start.8 = (f32[4,128,256]{2,1,0:T(8,128)S(1)}, f32[4,128,256]{2,1,0:T(8,128)S(1)}, u32[]{:S(2)}, u32[]{:S(2)}) collective-permute-start(f32[4,128,256]{2,1,0:T(8,128)S(1)} %get-tuple-element.57.refs_4_), channel_id=1, source_target_pairs={{0,2},{2,0},{4,6},{6,4},{8,10},{10,8},{12,14},{14,12},{1,3},{3,1},... | collective-permute-start | bytes 1572872 | tf_op jit(solution)/shard_map/ppermute | solution.py:375
  35.7 10.3 %collective-permute-start.5 = (f32[2,128,256]{2,1,0:T(8,128)S(1)}, f32[2,128,256]{2,1,0:T(8,128)S(1)}, u32[]{:S(2)}, u32[]{:S(2)}) collective-permute-start(f32[2,128,256]{2,1,0:T(8,128)S(1)} %get-tuple-element.58), channel_id=1, source_target_pairs={{0,6},{2,4},{4,2},{6,0},{8,14},{10,12},{12,10},{14,8},{1,7},{3,5},... | collective-permute-start | bytes 786440 | tf_op jit(solution)/shard_map/ppermute | solution.py:375
  35.8 13.2 %collective-permute-start.6 = (f32[2,128,256]{2,1,0:T(8,128)S(1)}, f32[2,128,256]{2,1,0:T(8,128)S(1)}, u32[]{:S(2)}, u32[]{:S(2)}) collective-permute-start(f32[2,128,256]{2,1,0:T(8,128)S(1)} %get-tuple-element.59), channel_id=1, source_target_pairs={{0,4},{2,6},{4,0},{6,2},{8,12},{10,14},{12,8},{14,10},{1,5},{3,7},... | collective-permute-start | bytes 786440 | tf_op jit(solution)/shard_map/ppermute | solution.py:375
  37.8 12.0 %collective-permute-start.7 = (f32[2,128,256]{2,1,0:T(8,128)S(1)}, f32[2,128,256]{2,1,0:T(8,128)S(1)}, u32[]{:S(2)}, u32[]{:S(2)}) collective-permute-start(f32[2,128,256]{2,1,0:T(8,128)S(1)} %get-tuple-element.60), channel_id=1, source_target_pairs={{0,2},{2,0},{4,6},{6,4},{8,10},{10,8},{12,14},{14,12},{1,3},{3,1},... | collective-permute-start | bytes 786440 | tf_op jit(solution)/shard_map/ppermute | solution.py:375
  39.3 15.4 %copy-start.4 = (f32[4,128,256]{2,1,0:T(8,128)}, f32[4,128,256]{2,1,0:T(8,128)S(1)}, u32[]{:S(2)}) copy-start(f32[4,128,256]{2,1,0:T(8,128)S(1)} %collective-permute-done.8.refs_7_.taken_ref) | copy-start | bytes 1572868
  55.5 35.7 %all-to-all-start = ((f32[8,136,256]{2,1,0:T(8,128)}), f32[8,136,256]{2,1,0:T(8,128)S(1)}, u32[]{:S(2)}, u32[]{:S(2)}) async-start(f32[8,136,256]{2,1,0:T(8,128)} %get-tuple-element.63), calls=%async_computation | async-start | bytes 2228224 | tf_op jit(solution)/shard_map/all_to_all | solution.py:481
  62.5 3.1 %copy-start.3 = (f32[4,128,256]{2,1,0:T(8,128)S(1)}, f32[4,128,256]{2,1,0:T(8,128)}, u32[]{:S(2)}) copy-start(f32[4,128,256]{2,1,0:T(8,128)} %copy-done.2) | copy-start | bytes 1572868
  62.5 3.1 %copy-start.5 = (f32[4,128,256]{2,1,0:T(8,128)S(1)}, f32[4,128,256]{2,1,0:T(8,128)}, u32[]{:S(2)}) copy-start(f32[4,128,256]{2,1,0:T(8,128)} %copy-done.4) | copy-start | bytes 1572868
  63.5 23.6 %collective-permute-start.9 = (f32[4,128,256]{2,1,0:T(8,128)S(1)}, f32[4,128,256]{2,1,0:T(8,128)S(1)}, u32[]{:S(2)}, u32[]{:S(2)}) collective-permute-start(f32[4,128,256]{2,1,0:T(8,128)S(1)} %get-tuple-element.66), channel_id=1, source_target_pairs={{0,2},{2,0},{4,6},{6,4},{8,10},{10,8},{12,14},{14,12},{1,3},{3,1},... | collective-permute-start | bytes 1572872 | tf_op jit(solution)/shard_map/ppermute | solution.py:375
  65.6 23.1 %collective-permute-start.10 = (f32[2,128,256]{2,1,0:T(8,128)S(1)}, f32[2,128,256]{2,1,0:T(8,128)S(1)}, u32[]{:S(2)}, u32[]{:S(2)}) collective-permute-start(f32[2,128,256]{2,1,0:T(8,128)S(1)} %get-tuple-element.70), channel_id=1, source_target_pairs={{0,4},{2,6},{4,0},{6,2},{8,12},{10,14},{12,8},{14,10},{1,5},{3,7},... | collective-permute-start | bytes 786440 | tf_op jit(solution)/shard_map/ppermute | solution.py:375
  87.2 10.0 %collective-permute-start.12 = (f32[2,128,256]{2,1,0:T(8,128)S(1)}, f32[2,128,256]{2,1,0:T(8,128)S(1)}, u32[]{:S(2)}, u32[]{:S(2)}) collective-permute-start(f32[2,128,256]{2,1,0:T(8,128)S(1)} %get-tuple-element.67.refs_0_), channel_id=1, source_target_pairs={{0,4},{2,6},{4,0},{6,2},{8,12},{10,14},{12,8},{14,10},{1,5},{3,7},... | collective-permute-start | bytes 786440 | tf_op jit(solution)/shard_map/ppermute | solution.py:375
  88.7 14.6 %collective-permute-start.11 = (f32[1,128,256]{2,1,0:T(8,128)S(1)}, f32[1,128,256]{2,1,0:T(8,128)S(1)}, u32[]{:S(2)}, u32[]{:S(2)}) collective-permute-start(f32[1,128,256]{2,1,0:T(8,128)S(1)} %get-tuple-element.71.refs_1_), channel_id=1, source_target_pairs={{0,8},{2,10},{4,12},{6,14},{8,0},{10,2},{12,4},{14,6},{1,9},{3,11}... | collective-permute-start | bytes 393224 | tf_op jit(solution)/shard_map/ppermute | solution.py:375
  97.3 8.4 %collective-permute-start.13 = (f32[1,128,256]{2,1,0:T(8,128)S(1)}, f32[1,128,256]{2,1,0:T(8,128)S(1)}, u32[]{:S(2)}, u32[]{:S(2)}) collective-permute-start(f32[1,128,256]{2,1,0:T(8,128)S(1)} %get-tuple-element.77), channel_id=1, source_target_pairs={{0,8},{2,10},{4,12},{6,14},{8,0},{10,2},{12,4},{14,6},{1,9},{3,11}... | collective-permute-start | bytes 393224 | tf_op jit(solution)/shard_map/ppermute | solution.py:375
  98.9 12.4 %all-to-all-start.1 = ((f32[16,8,256]{2,1,0:T(8,128)}), f32[16,8,256]{2,1,0:T(8,128)S(1)}, u32[]{:S(2)}, u32[]{:S(2)}) async-start(f32[16,8,256]{2,1,0:T(8,128)} %shard_map.79.refs_0_), calls=%async_computation.1 | async-start | bytes 262144 | tf_op jit(solution)/shard_map/all_to_all | solution.py:502
  105.7 7.6 %collective-permute-start.14 = (f32[2,64,256]{2,1,0:T(8,128)S(1)}, f32[2,64,256]{2,1,0:T(8,128)S(1)}, u32[]{:S(2)}, u32[]{:S(2)}) collective-permute-start(f32[2,64,256]{2,1,0:T(8,128)S(1)} %get-tuple-element.79), channel_id=1, source_target_pairs={{0,1},{1,0},{2,3},{3,2},{4,5},{5,4},{6,7},{7,6},{8,9},{9,8},{10,11... | collective-permute-start | bytes 393224 | tf_op jit(solution)/shard_map/ppermute | solution.py:375
  (3 other events, 3.1 us)

commit v16 on v15

--- a/solution.py
+++ b/solution.py
@@ -29,7 +29,7 @@
     return rows == lax.broadcasted_iota(jnp.int32, (size, size), 1)
 
 
-def split_tiles(kinship_ref, high_ref, low_ref):
+def split_tiles(kinship_ref, stacked_ref):
     block_count, positions, tile = kinship_ref.shape[:3]
     diagonal_mask = on_diagonal(tile)
     for row in range(block_count):
@@ -38,8 +38,18 @@
             if position == 0:
                 values = jnp.where(diagonal_mask, 0.0, values)
             high, low = split(values)
-            high_ref[row, :, pl.ds(position * tile, tile)] = high
-            low_ref[row, :, pl.ds(position * tile, tile)] = low
+            here = pl.ds(position * tile, tile)
+            stacked_ref[row, pl.ds(0, tile), here] = high
+            stacked_ref[row, pl.ds(tile, tile), here] = low
+
+
+def tile_product(stacked, blocks):
+    tile = stacked.shape[0] // 2
+    parts = [split(block) for block in blocks]
+    blocks_high = jnp.concatenate([part[0] for part in parts], axis=0)
+    blocks_low = jnp.concatenate([part[1] for part in parts], axis=0)
+    both = dot(stacked, blocks_high)
+    return both[:tile] + (both[tile:] + dot(stacked[:tile], blocks_low))
 
 
 def product(high, low, blocks):
@@ -108,11 +118,11 @@
     wait_all(stores)
 
 
-def tiles_kernel(kinship_hbm, high_hbm, low_hbm, kinship_ref, high_ref, low_ref, semaphores):
+def tiles_kernel(kinship_hbm, stacked_hbm, kinship_ref, stacked_ref, semaphores):
     copies = Copies(semaphores)
     copies.start(kinship_hbm, kinship_ref).wait()
-    split_tiles(kinship_ref, high_ref, low_ref)
-    wait_all([copies.start(high_ref, high_hbm), copies.start(low_ref, low_hbm)])
+    split_tiles(kinship_ref, stacked_ref)
+    copies.start(stacked_ref, stacked_hbm).wait()
 
 
 def route_kernel(devices, capacity, block_count, list_ref, direction_ref, gate_ref, table_ref, forward_ref, *refs):
@@ -210,24 +220,30 @@
     score_products(high_ref, low_ref, values_ref[...], even_ref, odd_ref)
 
 
-def apply_kernel(devices, capacity, table_ref, high_hbm, low_hbm, diagonal_hbm, direction_ref, norm_ref, *refs):
+def apply_kernel(devices, capacity, table_ref, stacked_hbm, diagonal_hbm, direction_ref, norm_ref, dosage_high_ref,
+                 dosage_low_ref, *refs):
     received_refs = refs[:devices - 1]
-    (scaled_ref, scaled_hbm, handled_hbm, outgoing_hbm, gathered_ref, high_ref, low_ref, diagonal_ref, handled_ref,
-     sums_ref, semaphores) = refs[-11:]
+    (scaled_hbm, handled_hbm, outgoing_hbm, even_hbm, odd_hbm, gathered_ref, stacked_ref, diagonal_ref, scaled_ref,
+     handled_ref, sums_ref, even_ref, odd_ref, semaphores) = refs[-14:]
     copies = Copies(semaphores)
-    loads = [
-        copies.start(high_hbm, high_ref), copies.start(low_hbm, low_ref), copies.start(diagonal_hbm, diagonal_ref)
-    ]
+    loads = [copies.start(stacked_hbm, stacked_ref), copies.start(diagonal_hbm, diagonal_ref)]
     gather_received(devices, capacity, received_refs, gathered_ref)
     wait_all(loads)
-    block_count, tile, depth = high_ref.shape
+    block_count, tile, depth = stacked_ref.shape[0], stacked_ref.shape[1] // 2, stacked_ref.shape[2]
     others = depth // tile - 1
     cross = jnp.zeros(norm_ref.shape, jnp.float32)
     for row in range(block_count):
         block = pl.ds(row * tile, tile)
         here = direction_ref[block, :]
-        blocks = [here] + [gathered_ref[table_ref[0, row * others + i]] for i in range(others)]
-        mapped = product(high_ref[row], low_ref[row], blocks)
+        mapped = tile_product(stacked_ref[row, :, pl.ds(0, tile)], [here])
+        handled = jnp.zeros_like(mapped)
+        for i in range(others):
+            entry = row * others + i
+            there = gathered_ref[table_ref[0, entry]]
+            term = tile_product(stacked_ref[row, :, pl.ds((1 + i) * tile, tile)], [there])
+            mapped = mapped + term
+            handled = handled + table_ref[2, entry].astype(jnp.float32) * term
+        handled_ref[block, :] = handled
         scaled_ref[block, :] = mapped * (1.0 / diagonal_ref[block, :])
         cross = cross + column_sums(here * mapped)
     row_ids = lax.broadcasted_iota(jnp.int32, cross.shape, 0)
@@ -237,29 +253,30 @@
         start = pl.multiple_of(table_ref[3, other] * tile, tile)
         stores.append(copies.start(scaled_ref.at[pl.ds(start, tile)], outgoing_hbm.at[other, pl.ds(0, tile)]))
         stores.append(copies.start(sums_ref, outgoing_hbm.at[other, pl.ds(tile, SUBLANES)]))
-    stores.append(copies.start(scaled_ref, scaled_hbm))
-    far = pl.ds(tile, depth - tile)
+    stores += [copies.start(scaled_ref, scaled_hbm), copies.start(handled_ref, handled_hbm)]
+    score_products(dosage_high_ref, dosage_low_ref, scaled_ref[...], even_ref, odd_ref)
+    stores += [copies.start(odd_ref, odd_hbm), copies.start(even_ref, even_hbm)]
+    wait_all(stores)
+
+
+def curvature_kernel(devices, table_ref, stacked_hbm, direction_hbm, diagonal_hbm, scaled_hbm, handled_hbm, later_hbm,
+                     *refs):
+    (sums_hbm, sums_ref, stacked_ref, direction_ref, diagonal_ref, scaled_ref, handled_ref, later_ref,
+     semaphores) = refs[-9:]
+    block_count, tile, depth = stacked_ref.shape[0], stacked_ref.shape[1] // 2, stacked_ref.shape[2]
+    others = depth // tile - 1
+    copies = Copies(semaphores)
+    arrival = copies.start(later_hbm, later_ref)
+    loads = []
     for row in range(block_count):
-        blocks = []
-        for i in range(others):
-            weight = table_ref[2, row * others + i].astype(jnp.float32)
-            blocks.append(weight * gathered_ref[table_ref[0, row * others + i]])
-        handled_ref[pl.ds(row * tile, tile), :] = product(high_ref[row, :, far], low_ref[row, :, far], blocks)
-    stores.append(copies.start(handled_ref, handled_hbm))
-    wait_all(stores)
-
-
-def curvature_kernel(devices, table_ref, high_hbm, low_hbm, direction_hbm, diagonal_hbm, scaled_hbm, handled_hbm,
-                     later_hbm, *refs):
-    (sums_hbm, sums_ref, high_ref, low_ref, direction_ref, diagonal_ref, scaled_ref, handled_ref, later_ref,
-     semaphores) = refs[-10:]
-    block_count, tile, depth = high_ref.shape
-    copies = Copies(semaphores)
-    wait_all([copies.start(source, target) for source, target in (
-        (later_hbm, later_ref), (scaled_hbm, scaled_ref), (direction_hbm, direction_ref), (high_hbm, high_ref),
-        (low_hbm, low_ref), (handled_hbm, handled_ref), (diagonal_hbm, diagonal_ref),
-    )])
-    others = depth // tile - 1
+        block = pl.ds(row * tile, tile)
+        loads.append([copies.start(stacked_hbm.at[row], stacked_ref.at[row])] + [
+            copies.start(source.at[block], target.at[block]) for source, target in (
+                (scaled_hbm, scaled_ref), (direction_hbm, direction_ref), (handled_hbm, handled_ref),
+                (diagonal_hbm, diagonal_ref),
+            )
+        ])
+    arrival.wait()
     first_sums = later_ref[0, pl.ds(tile, SUBLANES), :]
     for other in range(1, devices):
         first_sums = first_sums + later_ref[other, pl.ds(tile, SUBLANES), :]
@@ -267,6 +284,7 @@
     norm = jnp.zeros(first_sums.shape, jnp.float32)
     bend = jnp.zeros(first_sums.shape, jnp.float32)
     for row in range(block_count):
+        wait_all(loads[row])
         block = pl.ds(row * tile, tile)
         here = scaled_ref[block, :] - rho * direction_ref[block, :]
         blocks = [here]
@@ -274,7 +292,7 @@
             entry = row * others + i
             weight = table_ref[2, entry].astype(jnp.float32)
             blocks.append(weight * later_ref[table_ref[1, entry], pl.ds(0, tile), :])
-        mapped = product(high_ref[row], low_ref[row], blocks) - rho * handled_ref[block, :]
+        mapped = tile_product(stacked_ref[row], blocks) - rho * handled_ref[block, :]
         norm = norm + column_sums(here * here * diagonal_ref[block, :])
         bend = bend + column_sums(here * mapped)
     row_ids = lax.broadcasted_iota(jnp.int32, first_sums.shape, 0)
@@ -400,8 +418,8 @@
     near_by = list(range(half - 1, 0, -1))
     at_home = lambda *arrays: [pltpu.with_memory_space_constraint(array, pltpu.HBM) for array in arrays]
     kinship, = at_home(kinship)
-    tiles_room = pltpu.VMEM((block_count, tile, positions * tile), jnp.bfloat16)
-    tiles_out = pltpu.HBM((block_count, tile, positions * tile), jnp.bfloat16)
+    tiles_room = pltpu.VMEM((block_count, 2 * tile, positions * tile), jnp.bfloat16)
+    tiles_out = pltpu.HBM((block_count, 2 * tile, positions * tile), jnp.bfloat16)
     full_out = pltpu.HBM((people, columns), jnp.float32)
     direction, direction_kept_hbm, diagonal, norm = call(
         direction_kernel,
@@ -432,9 +450,9 @@
         [smem, smem] + [vmem] * (half - 1),
         [pltpu.SMEM((devices,), jnp.int32), pltpu.SMEM((devices,), jnp.int32)],
     )(relatives.T, direction, other_dosage)
-    high, low = call(
-        tiles_kernel, [tiles_out] * 2, [hbm], [hbm] * 2,
-        [room(*kinship.shape), tiles_room, tiles_room, pltpu.SemaphoreType.DMA((3,))],
+    stacked = call(
+        tiles_kernel, tiles_out, [hbm], hbm,
+        [room(*kinship.shape), tiles_room, pltpu.SemaphoreType.DMA((2,))],
     )(kinship)
 
     parts = jax.ShapeDtypeStruct((2, variants, people), jnp.bfloat16)
@@ -449,7 +467,7 @@
         rows = float_of(kept.shape[0] // 2, 2 * share_rows, columns)
         return call(
             add_kernel, [rows] * 2, [vmem] * 2 + [hbm] * len(gates), [vmem] * 2
-        )(kept, taken, *at_home(*gates))
+        )(kept, taken, *gates)
 
     partner = swap(direction, "samples", devices, half)
     near = to_mates(outgoing)
@@ -460,48 +478,47 @@
     far = to_mates(call(
         forward_kernel,
         [float_of(capacity, tile, columns)] * (half - 1),
-        [smem, vmem] + [anywhere] * (half + 1) + [hbm] * 2,
+        [smem, vmem] + [anywhere] * (half + 1) + [hbm],
         [vmem] * (half - 1),
-    )(forward, partner, *near, direction_even, direction_odd, *at_home(high, low)))
+    )(forward, partner, *near, direction_even, direction_odd, *at_home(stacked)))
     received = near + far + [partner.reshape(block_count, tile, columns)]
-    scaled_here, scaled, handled, outgoing = call(
+    products_out = pltpu.HBM(products.shape, jnp.float32)
+    scaled, handled, outgoing, scaled_even, scaled_odd = call(
         functools.partial(apply_kernel, devices, capacity),
-        [full, full_out, full_out, pltpu.HBM((devices, tile + SUBLANES, columns), jnp.float32)],
-        [smem, hbm, hbm, hbm] + [vmem] * (devices + 1) + [anywhere],
-        [vmem] + [hbm] * 3,
         [
-            room(devices * capacity + block_count, tile, columns), tiles_room, tiles_room, room(people, 1),
-            full_room, room(SUBLANES, columns), pltpu.SemaphoreType.DMA((2 * devices + 5,)),
+            full_out, full_out, pltpu.HBM((devices, tile + SUBLANES, columns), jnp.float32), products_out, products_out,
+        ],
+        [smem, hbm, hbm] + [vmem] * (devices + 3) + [anywhere],
+        [hbm] * 5,
+        [
+            room(devices * capacity + block_count, tile, columns), tiles_room, room(people, 1), full_room, full_room,
+            room(SUBLANES, columns), room(*products.shape), room(*products.shape),
+            pltpu.SemaphoreType.DMA((2 * devices + 6,)),
         ],
         limit=large,
-    )(table, *at_home(high, low, diagonal), direction, norm, *received, direction_share)
-    scaled_even, scaled_odd = call(
-        score_kernel, [products] * 2, [vmem] * 3, [vmem] * 2, limit=large
-    )(*grouped, scaled_here)
+    )(table, *at_home(stacked, diagonal), direction, norm, *grouped, *received, direction_share)
     later = lax.all_to_all(outgoing, "samples", split_axis=0, concat_axis=0, tiled=True)
     scaled_share = swap(scaled_odd, "samples", devices, 1)
     direction_kept, direction_given = add_step(direction_even, direction_share)
-    scaled_kept, scaled_given = add_step(scaled_even, scaled_share)
     for step in steps[:-1]:
         direction_taken = swap(after(direction_given, scaled), "samples", devices, step)
         direction_kept, direction_given = add_step(direction_kept, direction_taken)
     direction_taken = swap(direction_given, "samples", devices, steps[-1])
+    scaled_kept, scaled_given = add_step(scaled_even, scaled_share, direction_taken)
     scaled_taken = swap(scaled_given, "samples", devices, steps[0])
     sums = call(
         functools.partial(curvature_kernel, devices),
         pltpu.HBM((2 * devices, SUBLANES, columns), jnp.float32),
-        [smem] + [hbm] * 6 + [anywhere] * 3,
+        [smem] + [hbm] * 5 + [anywhere] * 2,
         hbm,
         [
-            room(2 * devices, SUBLANES, columns), tiles_room, tiles_room, full_room, room(people, 1), full_room,
-            full_room, room(devices, tile + SUBLANES, columns), pltpu.SemaphoreType.DMA((8,)),
+            room(2 * devices, SUBLANES, columns), tiles_room, full_room, room(people, 1), full_room, full_room,
+            room(devices, tile + SUBLANES, columns), pltpu.SemaphoreType.DMA((5 * block_count + 2,)),
         ],
-    )(
-        table, *at_home(high, low, direction_kept_hbm, diagonal, scaled, handled), later, scaled_given, direction_given
-    )
+    )(table, *at_home(stacked, direction_kept_hbm, diagonal, scaled, handled), later, scaled_given)
     all_sums = lax.all_to_all(sums, ("samples", "cols"), split_axis=0, concat_axis=0, tiled=True)
     for step in steps[1:]:
-        scaled_kept, scaled_given = add_step(scaled_kept, scaled_taken, sums)
+        scaled_kept, scaled_given = add_step(scaled_kept, scaled_taken, *at_home(sums))
         scaled_taken = swap(scaled_given, "samples", devices, step)
     rows = float_of(2, share_rows, columns)
     own_scores, other_scores = call(

time: 115 us -> 119 us (1.035)
  waiting for transfers between devices: 52.1 us -> 60.3 us
  local copies, waits for them, and re-layouts: 6.96 us -> 4.12 us
    ppermute x15, waiting for transfers between devices: 46.6 us -> 54.3 us  [swap(): return lax.ppermute(values, axis, [(i, i ^ step) for i in range(devices)])]
    unnamed x20 -> x8, local copies, waits for them, and re-layouts: 4.32 us -> 1.24 us
    ppermute x15, starting transfers between devices: 22.1 us -> 20.8 us  [swap(): return lax.ppermute(values, axis, [(i, i ^ step) for i in range(devices)])]
  transfers between devices with their start and end apart: 17 -> 17, of which waited for: 9 -> 10; matrix products, arithmetic and copies ran while one was open for 2% -> 2% of each run, Pallas kernels for 12% -> 10%
where the time goes in v16:
time: 119 us
  waiting for transfers between devices  60.3 us (51%)
  starting transfers between devices  32.3 us (27%)
  Pallas kernels  21.5 us (18%)
  local copies, waits for them, and re-layouts  4.12 us (3%)
    ppermute x15, waiting for transfers between devices, swap(): return lax.ppermute(values, axis, [(i, i ^ step) for i in range(devices)])  54.3 us
    ppermute x15, starting transfers between devices, swap(): return lax.ppermute(values, axis, [(i, i ^ step) for i in range(devices)])  20.8 us
    all_to_all x1, starting transfers between devices, per_device(): lax.all_to_all(outgoing, 'samples', split_axis=0, concat_axis=0, tiled=True)  5.95 us
    all_to_all x1, waiting for transfers between devices, per_device(): lax.all_to_all(sums, ('samples', 'cols'), split_axis=0, concat_axis=0, ti...  5.94 us
    pallas_call x1, Pallas kernels, per_device(): call(functools.partial(apply_kernel, devices, capacity), [full_out, full_...  5.89 us
    all_to_all x1, starting transfers between devices, per_device(): lax.all_to_all(sums, ('samples', 'cols'), split_axis=0, concat_axis=0, ti...  5.53 us
    pallas_call x1, Pallas kernels, per_device(): call(functools.partial(curvature_kernel, devices), pltpu.HBM((2 * devices...  4.16 us
    pallas_call x1, Pallas kernels, per_device(): call(direction_kernel, [full, full_out, pltpu.HBM((people, 1), jnp.float3...  2.46 us
  transfers between devices with their start and end apart: 17, of which 10 were waited for; matrix products, arithmetic and copies ran while one was open for 2% of the time, Pallas kernels for 10%

profile of v16, /device:TPU:0, one launch (start us, length us, event | category | flops | bytes accessed | tf_op | source)
XLA Modules:
  0.0 119.0 jit_solution(15691596825768725802)
XLA Ops:
  0.7 2.5 %shard_map.68 = (f32[512,256]{1,0:T(8,128)S(1)}, f32[512,256]{1,0:T(8,128)}, f32[512,1]{1,0:T(8,128)}, f32[8,256]{1,0:T(8,128)S(1)}) custom-call(f32[4,4,128,128]{3,2,1,0:T(8,128)} %kinship_hbm.3, f32[4,128]{1,0:T(4,128)} %bitcast.9, f32[512,256]{1,0:T(8,128)} %phenotypes_hbm.1), custom_call_target="tpu_custom_call" | custom-call | tf_op jit(solution)/shard_map/pallas_call | solution.py:424
  3.7 3.7 %collective-permute-start.4 = (f32[512,256]{1,0:T(8,128)S(1)}, f32[512,256]{1,0:T(8,128)S(1)}, u32[]{:S(2)}, u32[]{:S(2)}) collective-permute-start(f32[512,256]{1,0:T(8,128)S(1)} %get-tuple-element.39.direction_ref.values_ref), channel_id=1, source_target_pairs={{0,8},{2,10},{4,12},{6,14},{8,0},{10,2},{12,4},{14,6},{1,9},{3,11}... | collective-permute-start | bytes 1572872 | tf_op jit(solution)/shard_map/ppermute | solution.py:393
  7.3 1.8 %shard_map.69 = (s32[4,12]{1,0:T(4,128)S(1)}, s32[2,4]{1,0:T(2,128)S(1)}, f32[2,128,256]{2,1,0:T(8,128)}, f32[2,128,256]{2,1,0:T(8,128)}, f32[2,128,256]{2,1,0:T(8,128)}) custom-call(s32[3,32]{1,0:T(4,128)S(1)} %bitcast.8, f32[512,256]{1,0:T(8,128)S(1)} %get-tuple-element.39.direction_ref.values_ref, f32[512,512]{1,0:T(8,128)S(1)} %collective-permute-done.gate_ref), custom_call_target="tpu_custom_call" | custom-call | tf_op jit(solution)/shard_map/pallas_call | solution.py:443
  9.1 2.6 %collective-permute-start.1 = (f32[2,128,256]{2,1,0:T(8,128)}, f32[2,128,256]{2,1,0:T(8,128)S(1)}, u32[]{:S(2)}, u32[]{:S(2)}) collective-permute-start(f32[2,128,256]{2,1,0:T(8,128)} %get-tuple-element.47), channel_id=1, source_target_pairs={{0,6},{2,4},{4,2},{6,0},{8,14},{10,12},{12,10},{14,8},{1,7},{3,5},... | collective-permute-start | bytes 786440 | tf_op jit(solution)/shard_map/ppermute | solution.py:393
  12.7 1.6 %copy.7 = f32[512,512]{0,1:T(8,128)S(1)} copy(f32[512,512]{1,0:T(8,128)} %param.9) | data formatting | bytes 2097152 | tf_op jit(solution)/shard_map/optimization_barrier | solution.py:397
  18.0 1.6 %collective-permute-start.8 = (f32[4,128,256]{2,1,0:T(8,128)S(1)}, f32[4,128,256]{2,1,0:T(8,128)S(1)}, u32[]{:S(2)}, u32[]{:S(2)}) collective-permute-start(f32[4,128,256]{2,1,0:T(8,128)S(1)} %get-tuple-element.52.refs_4_), channel_id=1, source_target_pairs={{0,2},{2,0},{4,6},{6,4},{8,10},{10,8},{12,14},{14,12},{1,3},{3,1},... | collective-permute-start | bytes 1572872 | tf_op jit(solution)/shard_map/ppermute | solution.py:393
  19.6 2.4 %shard_map.70.refs_5_.stacked_hbm = bf16[4,256,512]{2,1,0:T(8,128)(2,1)} custom-call(f32[4,4,128,128]{3,2,1,0:T(8,128)} %kinship_hbm.3), custom_call_target="tpu_custom_call" | custom-call | tf_op jit(solution)/shard_map/pallas_call | solution.py:453
  22.0 9.2 %collective-permute-done.4.partner_ref = f32[512,256]{1,0:T(8,128)S(1)} collective-permute-done((f32[512,256]{1,0:T(8,128)S(1)}, f32[512,256]{1,0:T(8,128)S(1)}, u32[]{:S(2)}, u32[]{:S(2)}) %collective-permute-start.4) | collective-permute-done | bytes 524320 | tf_op jit(solution)/shard_map/ppermute | solution.py:393
  31.2 3.4 %collective-permute-done.2.refs_1_ = f32[2,128,256]{2,1,0:T(8,128)} collective-permute-done((f32[2,128,256]{2,1,0:T(8,128)}, f32[2,128,256]{2,1,0:T(8,128)}, u32[]{:S(2)}, u32[]{:S(2)}) %collective-permute-start.2) | collective-permute-done | bytes 262176 | tf_op jit(solution)/shard_map/ppermute | solution.py:393
  35.2 2.0 %collective-permute-start.6 = (f32[2,128,256]{2,1,0:T(8,128)S(1)}, f32[2,128,256]{2,1,0:T(8,128)S(1)}, u32[]{:S(2)}, u32[]{:S(2)}) collective-permute-start(f32[2,128,256]{2,1,0:T(8,128)S(1)} %get-tuple-element.54), channel_id=1, source_target_pairs={{0,4},{2,6},{4,0},{6,2},{8,12},{10,14},{12,8},{14,10},{1,5},{3,7},... | collective-permute-start | bytes 786440 | tf_op jit(solution)/shard_map/ppermute | solution.py:393
  38.7 6.7 %collective-permute-done.5.refs_3_ = f32[2,128,256]{2,1,0:T(8,128)S(1)} collective-permute-done((f32[2,128,256]{2,1,0:T(8,128)S(1)}, f32[2,128,256]{2,1,0:T(8,128)S(1)}, u32[]{:S(2)}, u32[]{:S(2)}) %collective-permute-start.5) | collective-permute-done | bytes 262176 | tf_op jit(solution)/shard_map/ppermute | solution.py:393
  45.4 3.0 %collective-permute-done.6.refs_4_ = f32[2,128,256]{2,1,0:T(8,128)S(1)} collective-permute-done((f32[2,128,256]{2,1,0:T(8,128)S(1)}, f32[2,128,256]{2,1,0:T(8,128)S(1)}, u32[]{:S(2)}, u32[]{:S(2)}) %collective-permute-start.6) | collective-permute-done | bytes 262176 | tf_op jit(solution)/shard_map/ppermute | solution.py:393
  49.3 5.9 %shard_map.74 = (f32[512,256]{1,0:T(8,128)}, f32[512,256]{1,0:T(8,128)}, f32[8,136,256]{2,1,0:T(8,128)}, f32[4,128,256]{2,1,0:T(8,128)}, f32[4,128,256]{2,1,0:T(8,128)}) custom-call(s32[4,12]{1,0:T(4,128)S(1)} %get-tuple-element.41.table_ref, bf16[4,256,512]{2,1,0:T(8,128)(2,1)} %shard_map.70.refs_5_.stacked_hbm, f32[512,1]{1,0:T(8,128)} %get-tuple-element.42.diagonal_hbm, ...), custom_call_target="tpu_custom_call" | custom-call | tf_op jit(solution)/shard_map/pallas_call | solution.py:486
  55.2 6.0 %all-to-all-start = ((f32[8,136,256]{2,1,0:T(8,128)}), f32[8,136,256]{2,1,0:T(8,128)S(1)}, u32[]{:S(2)}, u32[]{:S(2)}) async-start(f32[8,136,256]{2,1,0:T(8,128)} %get-tuple-element.58), calls=%async_computation | async-start | bytes 2228224 | tf_op jit(solution)/shard_map/all_to_all | solution.py:500
  61.1 2.0 %collective-permute-start.9 = (f32[4,128,256]{2,1,0:T(8,128)}, f32[4,128,256]{2,1,0:T(8,128)S(1)}, u32[]{:S(2)}, u32[]{:S(2)}) collective-permute-start(f32[4,128,256]{2,1,0:T(8,128)} %get-tuple-element.60), channel_id=1, source_target_pairs={{0,2},{2,0},{4,6},{6,4},{8,10},{10,8},{12,14},{14,12},{1,3},{3,1},... | collective-permute-start | bytes 1572872 | tf_op jit(solution)/shard_map/ppermute | solution.py:393
  64.8 20.7 %collective-permute-done.10.taken_ref = f32[2,128,256]{2,1,0:T(8,128)S(1)} collective-permute-done((f32[2,128,256]{2,1,0:T(8,128)S(1)}, f32[2,128,256]{2,1,0:T(8,128)S(1)}, u32[]{:S(2)}, u32[]{:S(2)}) %collective-permute-start.10) | collective-permute-done | bytes 262176 | tf_op jit(solution)/shard_map/ppermute | solution.py:393
  85.5 4.2 %collective-permute-start.11 = (f32[1,128,256]{2,1,0:T(8,128)S(1)}, f32[1,128,256]{2,1,0:T(8,128)S(1)}, u32[]{:S(2)}, u32[]{:S(2)}) collective-permute-start(f32[1,128,256]{2,1,0:T(8,128)S(1)} %get-tuple-element.64), channel_id=1, source_target_pairs={{0,8},{2,10},{4,12},{6,14},{8,0},{10,2},{12,4},{14,6},{1,9},{3,11}... | collective-permute-start | bytes 393224 | tf_op jit(solution)/shard_map/ppermute | solution.py:393
  89.7 5.3 %collective-permute-done.11.refs_0_.first_taken_ref = f32[1,128,256]{2,1,0:T(8,128)S(1)} collective-permute-done((f32[1,128,256]{2,1,0:T(8,128)S(1)}, f32[1,128,256]{2,1,0:T(8,128)S(1)}, u32[]{:S(2)}, u32[]{:S(2)}) %collective-permute-start.11) | collective-permute-done | bytes 131104 | tf_op jit(solution)/shard_map/ppermute | solution.py:393
  95.2 4.2 %shard_map.78.refs_0_ = f32[16,8,256]{2,1,0:T(8,128)} custom-call(s32[4,12]{1,0:T(4,128)S(1)} %get-tuple-element.41.table_ref, bf16[4,256,512]{2,1,0:T(8,128)(2,1)} %shard_map.70.refs_5_.stacked_hbm, f32[512,256]{1,0:T(8,128)} %get-tuple-element.38.direction_hbm, f32[512,1]{1,0:T(8,128)} %get-tuple-element.42.diagonal_hbm, ...), custom_call_target="tpu_custom_call" | custom-call | tf_op jit(solution)/shard_map/pallas_call | solution.py:509
  99.4 3.3 %collective-permute-done.12.taken_ref = f32[2,128,256]{2,1,0:T(8,128)S(1)} collective-permute-done((f32[2,128,256]{2,1,0:T(8,128)S(1)}, f32[2,128,256]{2,1,0:T(8,128)S(1)}, u32[]{:S(2)}, u32[]{:S(2)}) %collective-permute-start.12) | collective-permute-done | bytes 262176 | tf_op jit(solution)/shard_map/ppermute | solution.py:393
  102.7 5.5 %all-to-all-start.1 = ((f32[16,8,256]{2,1,0:T(8,128)}), f32[16,8,256]{2,1,0:T(8,128)S(1)}, u32[]{:S(2)}, u32[]{:S(2)}) async-start(f32[16,8,256]{2,1,0:T(8,128)} %shard_map.78.refs_0_), calls=%async_computation.1 | async-start | bytes 262144 | tf_op jit(solution)/shard_map/all_to_all | solution.py:519
  108.3 1.9 %collective-permute-done.13.second_taken_ref = f32[1,128,256]{2,1,0:T(8,128)S(1)} collective-permute-done((f32[1,128,256]{2,1,0:T(8,128)S(1)}, f32[1,128,256]{2,1,0:T(8,128)S(1)}, u32[]{:S(2)}, u32[]{:S(2)}) %collective-permute-start.13) | collective-permute-done | bytes 131104 | tf_op jit(solution)/shard_map/ppermute | solution.py:393
  110.3 5.9 %all-to-all-done.1.sums_ref = f32[16,8,256]{2,1,0:T(8,128)S(1)} async-done(((f32[16,8,256]{2,1,0:T(8,128)}), f32[16,8,256]{2,1,0:T(8,128)S(1)}, u32[]{:S(2)}, u32[]{:S(2)}) %all-to-all-start.1) | async-done | bytes 131104 | tf_op jit(solution)/shard_map/all_to_all | solution.py:519
  116.2 2.0 %shard_map.79 = (f32[512,256]{1,0:T(8,128)}, f32[8,256]{1,0:T(8,128)S(1)}) custom-call(f32[512,256]{1,0:T(8,128)} %get-tuple-element.38.direction_hbm, f32[512,256]{1,0:T(8,128)} %get-tuple-element.56.scaled_hbm, f32[16,8,256]{2,1,0:T(8,128)S(1)} %all-to-all-done.1.sums_ref), custom_call_target="tpu_custom_call" | custom-call | tf_op jit(solution)/shard_map/pallas_call | solution.py:527
  (35 shorter events, 10.9 us)
Async XLA Ops:
  0.6 2.5 %copy-start.3 = (f32[512,512]{1,0:T(8,128)S(1)}, f32[512,512]{1,0:T(8,128)}, u32[]{:S(2)}) copy-start(f32[512,512]{1,0:T(8,128)} %param.9) | copy-start | bytes 3145732
  0.6 6.7 %copy-start.2 = (s32[32,3]{0,1:T(4,128)S(1)}, s32[32,3]{0,1:T(4,128)}, u32[]{:S(2)}) copy-start(s32[32,3]{0,1:T(4,128)} %param.6) | copy-start | bytes 1156
  3.1 4.2 %collective-permute-start = (f32[512,512]{1,0:T(8,128)S(1)}, f32[512,512]{1,0:T(8,128)S(1)}, u32[]{:S(2)}, u32[]{:S(2)}) collective-permute-start(f32[512,512]{1,0:T(8,128)S(1)} %copy-done.3), channel_id=1, source_target_pairs={{0,1},{1,0},{2,3},{3,2},{4,5},{5,4},{6,7},{7,6},{8,9},{9,8},{10,11... | collective-permute-start | bytes 3145736 | tf_op jit(solution)/shard_map/ppermute | solution.py:393
  3.7 27.5 %collective-permute-start.4 = (f32[512,256]{1,0:T(8,128)S(1)}, f32[512,256]{1,0:T(8,128)S(1)}, u32[]{:S(2)}, u32[]{:S(2)}) collective-permute-start(f32[512,256]{1,0:T(8,128)S(1)} %get-tuple-element.39.direction_ref.values_ref), channel_id=1, source_target_pairs={{0,8},{2,10},{4,12},{6,14},{8,0},{10,2},{12,4},{14,6},{1,9},{3,11}... | collective-permute-start | bytes 1572872 | tf_op jit(solution)/shard_map/ppermute | solution.py:393
  9.1 22.1 %collective-permute-start.1 = (f32[2,128,256]{2,1,0:T(8,128)}, f32[2,128,256]{2,1,0:T(8,128)S(1)}, u32[]{:S(2)}, u32[]{:S(2)}) collective-permute-start(f32[2,128,256]{2,1,0:T(8,128)} %get-tuple-element.47), channel_id=1, source_target_pairs={{0,6},{2,4},{4,2},{6,0},{8,14},{10,12},{12,10},{14,8},{1,7},{3,5},... | collective-permute-start | bytes 786440 | tf_op jit(solution)/shard_map/ppermute | solution.py:393
  11.7 22.8 %collective-permute-start.2 = (f32[2,128,256]{2,1,0:T(8,128)}, f32[2,128,256]{2,1,0:T(8,128)}, u32[]{:S(2)}, u32[]{:S(2)}) collective-permute-start(f32[2,128,256]{2,1,0:T(8,128)} %get-tuple-element.48), channel_id=1, source_target_pairs={{0,4},{2,6},{4,0},{6,2},{8,12},{10,14},{12,8},{14,10},{1,5},{3,7},... | collective-permute-start | bytes 786440 | tf_op jit(solution)/shard_map/ppermute | solution.py:393
  12.2 22.4 %collective-permute-start.3 = (f32[2,128,256]{2,1,0:T(8,128)}, f32[2,128,256]{2,1,0:T(8,128)}, u32[]{:S(2)}, u32[]{:S(2)}) collective-permute-start(f32[2,128,256]{2,1,0:T(8,128)} %get-tuple-element.49), channel_id=1, source_target_pairs={{0,2},{2,0},{4,6},{6,4},{8,10},{10,8},{12,14},{14,12},{1,3},{3,1},... | collective-permute-start | bytes 786440 | tf_op jit(solution)/shard_map/ppermute | solution.py:393
  15.6 1.2 %copy-start = (f32[512,512]{0,1:T(8,128)S(1)}, f32[512,512]{0,1:T(8,128)}, u32[]{:S(2)}) copy-start(f32[512,512]{0,1:T(8,128)} %copy.8) | copy-start | bytes 3145732
  18.0 20.7 %collective-permute-start.8 = (f32[4,128,256]{2,1,0:T(8,128)S(1)}, f32[4,128,256]{2,1,0:T(8,128)S(1)}, u32[]{:S(2)}, u32[]{:S(2)}) collective-permute-start(f32[4,128,256]{2,1,0:T(8,128)S(1)} %get-tuple-element.52.refs_4_), channel_id=1, source_target_pairs={{0,2},{2,0},{4,6},{6,4},{8,10},{10,8},{12,14},{14,12},{1,3},{3,1},... | collective-permute-start | bytes 1572872 | tf_op jit(solution)/shard_map/ppermute | solution.py:393
  35.2 10.3 %collective-permute-start.5 = (f32[2,128,256]{2,1,0:T(8,128)S(1)}, f32[2,128,256]{2,1,0:T(8,128)S(1)}, u32[]{:S(2)}, u32[]{:S(2)}) collective-permute-start(f32[2,128,256]{2,1,0:T(8,128)S(1)} %get-tuple-element.53), channel_id=1, source_target_pairs={{0,6},{2,4},{4,2},{6,0},{8,14},{10,12},{12,10},{14,8},{1,7},{3,5},... | collective-permute-start | bytes 786440 | tf_op jit(solution)/shard_map/ppermute | solution.py:393
  35.2 13.2 %collective-permute-start.6 = (f32[2,128,256]{2,1,0:T(8,128)S(1)}, f32[2,128,256]{2,1,0:T(8,128)S(1)}, u32[]{:S(2)}, u32[]{:S(2)}) collective-permute-start(f32[2,128,256]{2,1,0:T(8,128)S(1)} %get-tuple-element.54), channel_id=1, source_target_pairs={{0,4},{2,6},{4,0},{6,2},{8,12},{10,14},{12,8},{14,10},{1,5},{3,7},... | collective-permute-start | bytes 786440 | tf_op jit(solution)/shard_map/ppermute | solution.py:393
  37.3 12.0 %collective-permute-start.7 = (f32[2,128,256]{2,1,0:T(8,128)S(1)}, f32[2,128,256]{2,1,0:T(8,128)S(1)}, u32[]{:S(2)}, u32[]{:S(2)}) collective-permute-start(f32[2,128,256]{2,1,0:T(8,128)S(1)} %get-tuple-element.55), channel_id=1, source_target_pairs={{0,2},{2,0},{4,6},{6,4},{8,10},{10,8},{12,14},{14,12},{1,3},{3,1},... | collective-permute-start | bytes 786440 | tf_op jit(solution)/shard_map/ppermute | solution.py:393
  55.2 40.0 %all-to-all-start = ((f32[8,136,256]{2,1,0:T(8,128)}), f32[8,136,256]{2,1,0:T(8,128)S(1)}, u32[]{:S(2)}, u32[]{:S(2)}) async-start(f32[8,136,256]{2,1,0:T(8,128)} %get-tuple-element.58), calls=%async_computation | async-start | bytes 2228224 | tf_op jit(solution)/shard_map/all_to_all | solution.py:500
  61.1 33.9 %copy-start.1 = (f32[4,128,256]{2,1,0:T(8,128)S(1)}, f32[4,128,256]{2,1,0:T(8,128)}, u32[]{:S(2)}) copy-start(f32[4,128,256]{2,1,0:T(8,128)} %get-tuple-element.59.kept_ref) | copy-start | bytes 1572868
  61.1 33.9 %collective-permute-start.9 = (f32[4,128,256]{2,1,0:T(8,128)}, f32[4,128,256]{2,1,0:T(8,128)S(1)}, u32[]{:S(2)}, u32[]{:S(2)}) collective-permute-start(f32[4,128,256]{2,1,0:T(8,128)} %get-tuple-element.60), channel_id=1, source_target_pairs={{0,2},{2,0},{4,6},{6,4},{8,10},{10,8},{12,14},{14,12},{1,3},{3,1},... | collective-permute-start | bytes 1572872 | tf_op jit(solution)/shard_map/ppermute | solution.py:393
  63.2 22.3 %collective-permute-start.10 = (f32[2,128,256]{2,1,0:T(8,128)S(1)}, f32[2,128,256]{2,1,0:T(8,128)S(1)}, u32[]{:S(2)}, u32[]{:S(2)}) collective-permute-start(f32[2,128,256]{2,1,0:T(8,128)S(1)} %get-tuple-element.63), channel_id=1, source_target_pairs={{0,4},{2,6},{4,0},{6,2},{8,12},{10,14},{12,8},{14,10},{1,5},{3,7},... | collective-permute-start | bytes 786440 | tf_op jit(solution)/shard_map/ppermute | solution.py:393
  85.5 9.5 %collective-permute-start.11 = (f32[1,128,256]{2,1,0:T(8,128)S(1)}, f32[1,128,256]{2,1,0:T(8,128)S(1)}, u32[]{:S(2)}, u32[]{:S(2)}) collective-permute-start(f32[1,128,256]{2,1,0:T(8,128)S(1)} %get-tuple-element.64), channel_id=1, source_target_pairs={{0,8},{2,10},{4,12},{6,14},{8,0},{10,2},{12,4},{14,6},{1,9},{3,11}... | collective-permute-start | bytes 393224 | tf_op jit(solution)/shard_map/ppermute | solution.py:393
  95.1 7.5 %collective-permute-start.12 = (f32[2,128,256]{2,1,0:T(8,128)S(1)}, f32[2,128,256]{2,1,0:T(8,128)S(1)}, u32[]{:S(2)}, u32[]{:S(2)}) collective-permute-start(f32[2,128,256]{2,1,0:T(8,128)S(1)} %get-tuple-element.65.refs_0_), channel_id=1, source_target_pairs={{0,4},{2,6},{4,0},{6,2},{8,12},{10,14},{12,8},{14,10},{1,5},{3,7},... | collective-permute-start | bytes 786440 | tf_op jit(solution)/shard_map/ppermute | solution.py:393
  102.7 7.5 %collective-permute-start.13 = (f32[1,128,256]{2,1,0:T(8,128)S(1)}, f32[1,128,256]{2,1,0:T(8,128)S(1)}, u32[]{:S(2)}, u32[]{:S(2)}) collective-permute-start(f32[1,128,256]{2,1,0:T(8,128)S(1)} %get-tuple-element.71), channel_id=1, source_target_pairs={{0,8},{2,10},{4,12},{6,14},{8,0},{10,2},{12,4},{14,6},{1,9},{3,11}... | collective-permute-start | bytes 393224 | tf_op jit(solution)/shard_map/ppermute | solution.py:393
  102.7 13.5 %all-to-all-start.1 = ((f32[16,8,256]{2,1,0:T(8,128)}), f32[16,8,256]{2,1,0:T(8,128)S(1)}, u32[]{:S(2)}, u32[]{:S(2)}) async-start(f32[16,8,256]{2,1,0:T(8,128)} %shard_map.78.refs_0_), calls=%async_computation.1 | async-start | bytes 262144 | tf_op jit(solution)/shard_map/all_to_all | solution.py:519
  110.2 8.1 %collective-permute-start.14 = (f32[2,64,256]{2,1,0:T(8,128)S(1)}, f32[2,64,256]{2,1,0:T(8,128)S(1)}, u32[]{:S(2)}, u32[]{:S(2)}) collective-permute-start(f32[2,64,256]{2,1,0:T(8,128)S(1)} %get-tuple-element.73), channel_id=1, source_target_pairs={{0,1},{1,0},{2,3},{3,2},{4,5},{5,4},{6,7},{7,6},{8,9},{9,8},{10,11... | collective-permute-start | bytes 393224 | tf_op jit(solution)/shard_map/ppermute | solution.py:393

commit v17 on v15

--- a/solution.py
+++ b/solution.py
@@ -210,10 +210,11 @@
     score_products(high_ref, low_ref, values_ref[...], even_ref, odd_ref)
 
 
-def apply_kernel(devices, capacity, table_ref, high_hbm, low_hbm, diagonal_hbm, direction_ref, norm_ref, *refs):
+def apply_kernel(devices, capacity, table_ref, high_hbm, low_hbm, diagonal_hbm, direction_ref, norm_ref, dosage_high_ref,
+                 dosage_low_ref, *refs):
     received_refs = refs[:devices - 1]
-    (scaled_ref, scaled_hbm, handled_hbm, outgoing_hbm, gathered_ref, high_ref, low_ref, diagonal_ref, handled_ref,
-     sums_ref, semaphores) = refs[-11:]
+    (scaled_hbm, handled_hbm, outgoing_hbm, products_hbm, gathered_ref, high_ref, low_ref, diagonal_ref, scaled_ref,
+     handled_ref, sums_ref, even_ref, odd_ref, semaphores) = refs[-14:]
     copies = Copies(semaphores)
     loads = [
         copies.start(high_hbm, high_ref), copies.start(low_hbm, low_ref), copies.start(diagonal_hbm, diagonal_ref)
@@ -232,12 +233,14 @@
         cross = cross + column_sums(here * mapped)
     row_ids = lax.broadcasted_iota(jnp.int32, cross.shape, 0)
     sums_ref[...] = jnp.where(row_ids == 1, jnp.sum(cross, axis=0, keepdims=True), norm_ref[...])
-    stores = []
+    stores = [copies.start(scaled_ref, scaled_hbm)]
     for other in range(devices):
         start = pl.multiple_of(table_ref[3, other] * tile, tile)
         stores.append(copies.start(scaled_ref.at[pl.ds(start, tile)], outgoing_hbm.at[other, pl.ds(0, tile)]))
         stores.append(copies.start(sums_ref, outgoing_hbm.at[other, pl.ds(tile, SUBLANES)]))
-    stores.append(copies.start(scaled_ref, scaled_hbm))
+    score_products(dosage_high_ref, dosage_low_ref, scaled_ref[...], even_ref, odd_ref)
+    own_bit = lax.axis_index("samples") & 1
+    stores += [copies.start(odd_ref, products_hbm.at[1 - own_bit]), copies.start(even_ref, products_hbm.at[own_bit])]
     far = pl.ds(tile, depth - tile)
     for row in range(block_count):
         blocks = []
@@ -290,6 +293,12 @@
     count = near_ref.shape[0]
     near_ref[...] = kept_ref[pl.ds(0, count)] + taken_ref[pl.ds(0, count)]
     far_ref[...] = kept_ref[pl.ds(count, count)] + taken_ref[pl.ds(count, count)]
+
+
+def pair_kernel(products_ref, near_ref, far_ref):
+    count = near_ref.shape[0]
+    near_ref[...] = products_ref[0, pl.ds(0, count)] + products_ref[1, pl.ds(0, count)]
+    far_ref[...] = products_ref[0, pl.ds(count, count)] + products_ref[1, pl.ds(count, count)]
 
 
 def last_add_kernel(first_kept_ref, first_taken_ref, second_kept_ref, second_taken_ref, own_ref, other_ref):
@@ -464,24 +473,30 @@
         [vmem] * (half - 1),
     )(forward, partner, *near, direction_even, direction_odd, *at_home(high, low)))
     received = near + far + [partner.reshape(block_count, tile, columns)]
-    scaled_here, scaled, handled, outgoing = call(
+    scaled, handled, outgoing, scaled_products = call(
         functools.partial(apply_kernel, devices, capacity),
-        [full, full_out, full_out, pltpu.HBM((devices, tile + SUBLANES, columns), jnp.float32)],
-        [smem, hbm, hbm, hbm] + [vmem] * (devices + 1) + [anywhere],
-        [vmem] + [hbm] * 3,
         [
-            room(devices * capacity + block_count, tile, columns), tiles_room, tiles_room, room(people, 1),
-            full_room, room(SUBLANES, columns), pltpu.SemaphoreType.DMA((2 * devices + 5,)),
+            full_out, full_out, pltpu.HBM((devices, tile + SUBLANES, columns), jnp.float32),
+            pltpu.HBM((2, *products.shape), jnp.float32),
+        ],
+        [smem, hbm, hbm, hbm] + [vmem] * (devices + 3) + [anywhere],
+        [hbm] * 4,
+        [
+            room(devices * capacity + block_count, tile, columns), tiles_room, tiles_room, room(people, 1), full_room,
+            full_room, room(SUBLANES, columns), room(*products.shape), room(*products.shape),
+            pltpu.SemaphoreType.DMA((2 * devices + 7,)),
         ],
         limit=large,
-    )(table, *at_home(high, low, diagonal), direction, norm, *received, direction_share)
-    scaled_even, scaled_odd = call(
-        score_kernel, [products] * 2, [vmem] * 3, [vmem] * 2, limit=large
-    )(*grouped, scaled_here)
+    )(table, *at_home(high, low, diagonal), direction, norm, *grouped, *received, direction_share)
+    scaled_products = lax.all_to_all(
+        scaled_products, "samples", split_axis=0, concat_axis=0, tiled=True,
+        axis_index_groups=[[i, i + 1] for i in range(0, devices, 2)],
+    )
     later = lax.all_to_all(outgoing, "samples", split_axis=0, concat_axis=0, tiled=True)
-    scaled_share = swap(scaled_odd, "samples", devices, 1)
     direction_kept, direction_given = add_step(direction_even, direction_share)
-    scaled_kept, scaled_given = add_step(scaled_even, scaled_share)
+    scaled_kept, scaled_given = call(
+        pair_kernel, [float_of(half // 2, 2 * share_rows, columns)] * 2, [vmem], [vmem] * 2
+    )(scaled_products)
     for step in steps[:-1]:
         direction_taken = swap(after(direction_given, scaled), "samples", devices, step)
         direction_kept, direction_given = add_step(direction_kept, direction_taken)

time: 115 us -> 130 us (1.13)
  blocking collectives: 0 us -> 17.6 us
  waiting for transfers between devices: 52.1 us -> 57.5 us
  starting transfers between devices: 32.5 us -> 28.4 us
  local copies, waits for them, and re-layouts: 6.96 us -> 4.11 us
    all_to_all x0 -> x1, blocking collectives: none -> 17.6 us  [per_device(): lax.all_to_all(scaled_products, 'samples', split_axis=0, concat_axis=0, t...]
    ppermute x15 -> x14, waiting for transfers between devices: 46.6 us -> 51.6 us  [swap(): return lax.ppermute(values, axis, [(i, i ^ step) for i in range(devices)])]
    ppermute x15 -> x14, starting transfers between devices: 22.1 us -> 18.1 us  [swap(): return lax.ppermute(values, axis, [(i, i ^ step) for i in range(devices)])]
    unnamed x20 -> x14, local copies, waits for them, and re-layouts: 4.32 us -> 1.25 us
    pallas_call x1 -> x2, Pallas kernels: 4.86 us -> 5.76 us  [the longest x1 5.7 us: per_device(): call(functools.partial(apply_kernel, devices, capacity), [full_out, full_...]
  transfers between devices with their start and end apart: 17 -> 16, of which waited for: 9 -> 9; matrix products, arithmetic and copies ran while one was open for 2% -> 2% of each run, Pallas kernels for 12% -> 9%
where the time goes in v17:
time: 130 us; the launch traced here: 129 us
  waiting for transfers between devices  57.5 us (44%)
  starting transfers between devices  28.4 us (22%)
  Pallas kernels  21 us (16%)
  blocking collectives  17.6 us (14%)
  local copies, waits for them, and re-layouts  4.11 us (3%)
    ppermute x14, waiting for transfers between devices, swap(): return lax.ppermute(values, axis, [(i, i ^ step) for i in range(devices)])  51.6 us
    ppermute x14, starting transfers between devices, swap(): return lax.ppermute(values, axis, [(i, i ^ step) for i in range(devices)])  18.1 us
    all_to_all x1, blocking collectives, per_device(): lax.all_to_all(scaled_products, 'samples', split_axis=0, concat_axis=0, t...  17.6 us
    all_to_all x1, starting transfers between devices, per_device(): lax.all_to_all(outgoing, 'samples', split_axis=0, concat_axis=0, tiled=True)  6.02 us
    all_to_all x1, waiting for transfers between devices, per_device(): lax.all_to_all(sums, ('samples', 'cols'), split_axis=0, concat_axis=0, ti...  5.95 us
    pallas_call x1, Pallas kernels, per_device(): call(functools.partial(apply_kernel, devices, capacity), [full_out, full_...  5.7 us
    all_to_all x1, starting transfers between devices, per_device(): lax.all_to_all(sums, ('samples', 'cols'), split_axis=0, concat_axis=0, ti...  4.2 us
    pallas_call x1, Pallas kernels, per_device(): call(functools.partial(curvature_kernel, devices), pltpu.HBM((2 * devices...  3.98 us
  transfers between devices with their start and end apart: 16, of which 9 were waited for; matrix products, arithmetic and copies ran while one was open for 2% of the time, Pallas kernels for 9%

profile of v17, /device:TPU:0, one launch (start us, length us, event | category | flops | bytes accessed | tf_op | source)
XLA Modules:
  0.0 129.5 jit_solution(4933775742929337896)
XLA Ops:
  0.7 2.4 %shard_map.68 = (f32[512,256]{1,0:T(8,128)S(1)}, f32[512,256]{1,0:T(8,128)}, f32[512,1]{1,0:T(8,128)}, f32[8,256]{1,0:T(8,128)S(1)}) custom-call(f32[4,4,128,128]{3,2,1,0:T(8,128)} %kinship_hbm.3, f32[4,128]{1,0:T(4,128)} %bitcast.9, f32[512,256]{1,0:T(8,128)} %phenotypes_hbm.1), custom_call_target="tpu_custom_call" | custom-call | tf_op jit(solution)/shard_map/pallas_call | solution.py:415
  3.6 3.7 %collective-permute-start.4 = (f32[512,256]{1,0:T(8,128)S(1)}, f32[512,256]{1,0:T(8,128)S(1)}, u32[]{:S(2)}, u32[]{:S(2)}) collective-permute-start(f32[512,256]{1,0:T(8,128)S(1)} %get-tuple-element.40.direction_ref.values_ref), channel_id=1, source_target_pairs={{0,8},{2,10},{4,12},{6,14},{8,0},{10,2},{12,4},{14,6},{1,9},{3,11}... | collective-permute-start | bytes 1572872 | tf_op jit(solution)/shard_map/ppermute | solution.py:384
  7.3 1.8 %shard_map.69 = (s32[4,12]{1,0:T(4,128)S(1)}, s32[2,4]{1,0:T(2,128)S(1)}, f32[2,128,256]{2,1,0:T(8,128)}, f32[2,128,256]{2,1,0:T(8,128)}, f32[2,128,256]{2,1,0:T(8,128)}) custom-call(s32[3,32]{1,0:T(4,128)S(1)} %bitcast.8, f32[512,256]{1,0:T(8,128)S(1)} %get-tuple-element.40.direction_ref.values_ref, f32[512,512]{1,0:T(8,128)S(1)} %collective-permute-done.gate_ref), custom_call_target="tpu_custom_call" | custom-call | tf_op jit(solution)/shard_map/pallas_call | solution.py:434
  9.1 2.6 %collective-permute-start.1 = (f32[2,128,256]{2,1,0:T(8,128)}, f32[2,128,256]{2,1,0:T(8,128)S(1)}, u32[]{:S(2)}, u32[]{:S(2)}) collective-permute-start(f32[2,128,256]{2,1,0:T(8,128)} %get-tuple-element.50), channel_id=1, source_target_pairs={{0,6},{2,4},{4,2},{6,0},{8,14},{10,12},{12,10},{14,8},{1,7},{3,5},... | collective-permute-start | bytes 786440 | tf_op jit(solution)/shard_map/ppermute | solution.py:384
  12.7 1.6 %copy.7 = f32[512,512]{0,1:T(8,128)S(1)} copy(f32[512,512]{1,0:T(8,128)} %param.9) | data formatting | bytes 2097152 | tf_op jit(solution)/shard_map/optimization_barrier | solution.py:388
  18.0 1.6 %collective-permute-start.8 = (f32[4,128,256]{2,1,0:T(8,128)S(1)}, f32[4,128,256]{2,1,0:T(8,128)S(1)}, u32[]{:S(2)}, u32[]{:S(2)}) collective-permute-start(f32[4,128,256]{2,1,0:T(8,128)S(1)} %get-tuple-element.55.refs_4_), channel_id=1, source_target_pairs={{0,2},{2,0},{4,6},{6,4},{8,10},{10,8},{12,14},{14,12},{1,3},{3,1},... | collective-permute-start | bytes 1572872 | tf_op jit(solution)/shard_map/ppermute | solution.py:384
  19.6 2.3 %shard_map.70 = (bf16[4,128,512]{2,1,0:T(8,128)(2,1)}, bf16[4,128,512]{2,1,0:T(8,128)(2,1)}) custom-call(f32[4,4,128,128]{3,2,1,0:T(8,128)} %kinship_hbm.3), custom_call_target="tpu_custom_call" | custom-call | tf_op jit(solution)/shard_map/pallas_call | solution.py:444
  21.9 9.2 %collective-permute-done.4.partner_ref = f32[512,256]{1,0:T(8,128)S(1)} collective-permute-done((f32[512,256]{1,0:T(8,128)S(1)}, f32[512,256]{1,0:T(8,128)S(1)}, u32[]{:S(2)}, u32[]{:S(2)}) %collective-permute-start.4) | collective-permute-done | bytes 524320 | tf_op jit(solution)/shard_map/ppermute | solution.py:384
  31.2 3.4 %collective-permute-done.2.refs_1_ = f32[2,128,256]{2,1,0:T(8,128)} collective-permute-done((f32[2,128,256]{2,1,0:T(8,128)}, f32[2,128,256]{2,1,0:T(8,128)}, u32[]{:S(2)}, u32[]{:S(2)}) %collective-permute-start.2) | collective-permute-done | bytes 262176 | tf_op jit(solution)/shard_map/ppermute | solution.py:384
  35.3 2.0 %collective-permute-start.6 = (f32[2,128,256]{2,1,0:T(8,128)S(1)}, f32[2,128,256]{2,1,0:T(8,128)S(1)}, u32[]{:S(2)}, u32[]{:S(2)}) collective-permute-start(f32[2,128,256]{2,1,0:T(8,128)S(1)} %get-tuple-element.57), channel_id=1, source_target_pairs={{0,4},{2,6},{4,0},{6,2},{8,12},{10,14},{12,8},{14,10},{1,5},{3,7},... | collective-permute-start | bytes 786440 | tf_op jit(solution)/shard_map/ppermute | solution.py:384
  37.3 1.5 %collective-permute-start.7 = (f32[2,128,256]{2,1,0:T(8,128)S(1)}, f32[2,128,256]{2,1,0:T(8,128)S(1)}, u32[]{:S(2)}, u32[]{:S(2)}) collective-permute-start(f32[2,128,256]{2,1,0:T(8,128)S(1)} %get-tuple-element.58), channel_id=1, source_target_pairs={{0,2},{2,0},{4,6},{6,4},{8,10},{10,8},{12,14},{14,12},{1,3},{3,1},... | collective-permute-start | bytes 786440 | tf_op jit(solution)/shard_map/ppermute | solution.py:384
  38.7 6.7 %collective-permute-done.5.refs_3_ = f32[2,128,256]{2,1,0:T(8,128)S(1)} collective-permute-done((f32[2,128,256]{2,1,0:T(8,128)S(1)}, f32[2,128,256]{2,1,0:T(8,128)S(1)}, u32[]{:S(2)}, u32[]{:S(2)}) %collective-permute-start.5) | collective-permute-done | bytes 262176 | tf_op jit(solution)/shard_map/ppermute | solution.py:384
  45.4 3.0 %collective-permute-done.6.refs_4_ = f32[2,128,256]{2,1,0:T(8,128)S(1)} collective-permute-done((f32[2,128,256]{2,1,0:T(8,128)S(1)}, f32[2,128,256]{2,1,0:T(8,128)S(1)}, u32[]{:S(2)}, u32[]{:S(2)}) %collective-permute-start.6) | collective-permute-done | bytes 262176 | tf_op jit(solution)/shard_map/ppermute | solution.py:384
  49.3 5.7 %shard_map.74 = (f32[512,256]{1,0:T(8,128)}, f32[512,256]{1,0:T(8,128)}, f32[8,136,256]{2,1,0:T(8,128)}, f32[2,4,128,256]{3,2,1,0:T(8,128)}) custom-call(s32[4,12]{1,0:T(4,128)S(1)} %get-tuple-element.42.table_ref, bf16[4,128,512]{2,1,0:T(8,128)(2,1)} %get-tuple-element.43.refs_5_.high_hbm, bf16[4,128,512]{2,1,0:T(8,128)(2,1)} %get-tuple-element.44.refs_6_.low_hbm, ...), custom_call_target="tpu_custom_call" | custom-call | tf_op jit(solution)/shard_map/pallas_call | solution.py:476
  55.0 17.6 %all_to_all.15.products_ref = f32[2,4,128,256]{3,2,1,0:T(8,128)S(1)} all-to-all(f32[2,4,128,256]{3,2,1,0:T(8,128)} %get-tuple-element.62), channel_id=1, replica_groups={{0,2},{4,6},{8,10},{12,14},{1,3},{5,7},{9,11},{13,15},{16,18},{20,22},{..., dimensions={0} | all-to-all | bytes 2097152 | tf_op jit(solution)/shard_map/all_to_all | solution.py:491
  72.7 6.0 %all-to-all-start = ((f32[8,136,256]{2,1,0:T(8,128)}), f32[8,136,256]{2,1,0:T(8,128)S(1)}, u32[]{:S(2)}, u32[]{:S(2)}) async-start(f32[8,136,256]{2,1,0:T(8,128)} %get-tuple-element.61), calls=%async_computation | async-start | bytes 2228224 | tf_op jit(solution)/shard_map/all_to_all | solution.py:495
  78.8 2.1 %collective-permute-start.9 = (f32[2,128,256]{2,1,0:T(8,128)S(1)}, f32[2,128,256]{2,1,0:T(8,128)S(1)}, u32[]{:S(2)}, u32[]{:S(2)}) collective-permute-start(f32[2,128,256]{2,1,0:T(8,128)S(1)} %get-tuple-element.66), channel_id=1, source_target_pairs={{0,4},{2,6},{4,0},{6,2},{8,12},{10,14},{12,8},{14,10},{1,5},{3,7},... | collective-permute-start | bytes 786440 | tf_op jit(solution)/shard_map/ppermute | solution.py:384
  81.0 26.5 %collective-permute-done.9.taken_ref = f32[2,128,256]{2,1,0:T(8,128)S(1)} collective-permute-done((f32[2,128,256]{2,1,0:T(8,128)S(1)}, f32[2,128,256]{2,1,0:T(8,128)S(1)}, u32[]{:S(2)}, u32[]{:S(2)}) %collective-permute-start.9) | collective-permute-done | bytes 262176 | tf_op jit(solution)/shard_map/ppermute | solution.py:384
  108.5 4.0 %shard_map.78.refs_0_ = f32[16,8,256]{2,1,0:T(8,128)} custom-call(s32[4,12]{1,0:T(4,128)S(1)} %get-tuple-element.42.table_ref, bf16[4,128,512]{2,1,0:T(8,128)(2,1)} %get-tuple-element.43.refs_5_.high_hbm, bf16[4,128,512]{2,1,0:T(8,128)(2,1)} %get-tuple-element.44.refs_6_.low_hbm, f32[512,256]{1,0:T(8,128)} %get-tuple-element.39.direction_hbm, ...), custom_call_target="tpu_custom_call" | custom-call | tf_op jit(solution)/shard_map/pallas_call | solution.py:505
  112.5 2.0 %collective-permute-start.12 = (f32[1,128,256]{2,1,0:T(8,128)S(1)}, f32[1,128,256]{2,1,0:T(8,128)S(1)}, u32[]{:S(2)}, u32[]{:S(2)}) collective-permute-start(f32[1,128,256]{2,1,0:T(8,128)S(1)} %get-tuple-element.73), channel_id=1, source_target_pairs={{0,8},{2,10},{4,12},{6,14},{8,0},{10,2},{12,4},{14,6},{1,9},{3,11}... | collective-permute-start | bytes 393224 | tf_op jit(solution)/shard_map/ppermute | solution.py:384
  114.6 4.2 %all-to-all-start.2 = ((f32[16,8,256]{2,1,0:T(8,128)}), f32[16,8,256]{2,1,0:T(8,128)S(1)}, u32[]{:S(2)}, u32[]{:S(2)}) async-start(f32[16,8,256]{2,1,0:T(8,128)} %shard_map.78.refs_0_), calls=%async_computation.2 | async-start | bytes 262144 | tf_op jit(solution)/shard_map/all_to_all | solution.py:517
  118.8 1.8 %collective-permute-done.12.second_taken_ref = f32[1,128,256]{2,1,0:T(8,128)S(1)} collective-permute-done((f32[1,128,256]{2,1,0:T(8,128)S(1)}, f32[1,128,256]{2,1,0:T(8,128)S(1)}, u32[]{:S(2)}, u32[]{:S(2)}) %collective-permute-start.12) | collective-permute-done | bytes 131104 | tf_op jit(solution)/shard_map/ppermute | solution.py:384
  120.8 5.9 %all-to-all-done.2.sums_ref = f32[16,8,256]{2,1,0:T(8,128)S(1)} async-done(((f32[16,8,256]{2,1,0:T(8,128)}), f32[16,8,256]{2,1,0:T(8,128)S(1)}, u32[]{:S(2)}, u32[]{:S(2)}) %all-to-all-start.2) | async-done | bytes 131104 | tf_op jit(solution)/shard_map/all_to_all | solution.py:517
  126.7 2.0 %shard_map.79 = (f32[512,256]{1,0:T(8,128)}, f32[8,256]{1,0:T(8,128)S(1)}) custom-call(f32[512,256]{1,0:T(8,128)} %get-tuple-element.39.direction_hbm, f32[512,256]{1,0:T(8,128)} %get-tuple-element.59.scaled_hbm, f32[16,8,256]{2,1,0:T(8,128)S(1)} %all-to-all-done.2.sums_ref), custom_call_target="tpu_custom_call" | custom-call | tf_op jit(solution)/shard_map/pallas_call | solution.py:525
  (40 shorter events, 8.9 us)
Async XLA Ops:
  0.6 2.5 %copy-start.6 = (f32[512,512]{1,0:T(8,128)S(1)}, f32[512,512]{1,0:T(8,128)}, u32[]{:S(2)}) copy-start(f32[512,512]{1,0:T(8,128)} %param.9) | copy-start | bytes 3145732
  0.6 6.7 %copy-start.5 = (s32[32,3]{0,1:T(4,128)S(1)}, s32[32,3]{0,1:T(4,128)}, u32[]{:S(2)}) copy-start(s32[32,3]{0,1:T(4,128)} %param.6) | copy-start | bytes 1156
  3.1 4.2 %collective-permute-start = (f32[512,512]{1,0:T(8,128)S(1)}, f32[512,512]{1,0:T(8,128)S(1)}, u32[]{:S(2)}, u32[]{:S(2)}) collective-permute-start(f32[512,512]{1,0:T(8,128)S(1)} %copy-done.6), channel_id=1, source_target_pairs={{0,1},{1,0},{2,3},{3,2},{4,5},{5,4},{6,7},{7,6},{8,9},{9,8},{10,11... | collective-permute-start | bytes 3145736 | tf_op jit(solution)/shard_map/ppermute | solution.py:384
  3.6 27.5 %collective-permute-start.4 = (f32[512,256]{1,0:T(8,128)S(1)}, f32[512,256]{1,0:T(8,128)S(1)}, u32[]{:S(2)}, u32[]{:S(2)}) collective-permute-start(f32[512,256]{1,0:T(8,128)S(1)} %get-tuple-element.40.direction_ref.values_ref), channel_id=1, source_target_pairs={{0,8},{2,10},{4,12},{6,14},{8,0},{10,2},{12,4},{14,6},{1,9},{3,11}... | collective-permute-start | bytes 1572872 | tf_op jit(solution)/shard_map/ppermute | solution.py:384
  9.1 22.0 %collective-permute-start.1 = (f32[2,128,256]{2,1,0:T(8,128)}, f32[2,128,256]{2,1,0:T(8,128)S(1)}, u32[]{:S(2)}, u32[]{:S(2)}) collective-permute-start(f32[2,128,256]{2,1,0:T(8,128)} %get-tuple-element.50), channel_id=1, source_target_pairs={{0,6},{2,4},{4,2},{6,0},{8,14},{10,12},{12,10},{14,8},{1,7},{3,5},... | collective-permute-start | bytes 786440 | tf_op jit(solution)/shard_map/ppermute | solution.py:384
  11.7 22.8 %collective-permute-start.2 = (f32[2,128,256]{2,1,0:T(8,128)}, f32[2,128,256]{2,1,0:T(8,128)}, u32[]{:S(2)}, u32[]{:S(2)}) collective-permute-start(f32[2,128,256]{2,1,0:T(8,128)} %get-tuple-element.51), channel_id=1, source_target_pairs={{0,4},{2,6},{4,0},{6,2},{8,12},{10,14},{12,8},{14,10},{1,5},{3,7},... | collective-permute-start | bytes 786440 | tf_op jit(solution)/shard_map/ppermute | solution.py:384
  12.2 22.4 %collective-permute-start.3 = (f32[2,128,256]{2,1,0:T(8,128)}, f32[2,128,256]{2,1,0:T(8,128)}, u32[]{:S(2)}, u32[]{:S(2)}) collective-permute-start(f32[2,128,256]{2,1,0:T(8,128)} %get-tuple-element.52), channel_id=1, source_target_pairs={{0,2},{2,0},{4,6},{6,4},{8,10},{10,8},{12,14},{14,12},{1,3},{3,1},... | collective-permute-start | bytes 786440 | tf_op jit(solution)/shard_map/ppermute | solution.py:384
  15.5 1.2 copy-start
  18.0 17.2 %copy-start.1 = (f32[4,128,256]{2,1,0:T(8,128)}, f32[4,128,256]{2,1,0:T(8,128)S(1)}, u32[]{:S(2)}) copy-start(f32[4,128,256]{2,1,0:T(8,128)S(1)} %get-tuple-element.54.refs_3_.kept_ref) | copy-start | bytes 1572868
  18.0 20.7 %collective-permute-start.8 = (f32[4,128,256]{2,1,0:T(8,128)S(1)}, f32[4,128,256]{2,1,0:T(8,128)S(1)}, u32[]{:S(2)}, u32[]{:S(2)}) collective-permute-start(f32[4,128,256]{2,1,0:T(8,128)S(1)} %get-tuple-element.55.refs_4_), channel_id=1, source_target_pairs={{0,2},{2,0},{4,6},{6,4},{8,10},{10,8},{12,14},{14,12},{1,3},{3,1},... | collective-permute-start | bytes 1572872 | tf_op jit(solution)/shard_map/ppermute | solution.py:384
  35.2 10.3 %collective-permute-start.5 = (f32[2,128,256]{2,1,0:T(8,128)S(1)}, f32[2,128,256]{2,1,0:T(8,128)S(1)}, u32[]{:S(2)}, u32[]{:S(2)}) collective-permute-start(f32[2,128,256]{2,1,0:T(8,128)S(1)} %get-tuple-element.56), channel_id=1, source_target_pairs={{0,6},{2,4},{4,2},{6,0},{8,14},{10,12},{12,10},{14,8},{1,7},{3,5},... | collective-permute-start | bytes 786440 | tf_op jit(solution)/shard_map/ppermute | solution.py:384
  35.3 13.2 %collective-permute-start.6 = (f32[2,128,256]{2,1,0:T(8,128)S(1)}, f32[2,128,256]{2,1,0:T(8,128)S(1)}, u32[]{:S(2)}, u32[]{:S(2)}) collective-permute-start(f32[2,128,256]{2,1,0:T(8,128)S(1)} %get-tuple-element.57), channel_id=1, source_target_pairs={{0,4},{2,6},{4,0},{6,2},{8,12},{10,14},{12,8},{14,10},{1,5},{3,7},... | collective-permute-start | bytes 786440 | tf_op jit(solution)/shard_map/ppermute | solution.py:384
  37.3 12.0 %collective-permute-start.7 = (f32[2,128,256]{2,1,0:T(8,128)S(1)}, f32[2,128,256]{2,1,0:T(8,128)S(1)}, u32[]{:S(2)}, u32[]{:S(2)}) collective-permute-start(f32[2,128,256]{2,1,0:T(8,128)S(1)} %get-tuple-element.58), channel_id=1, source_target_pairs={{0,2},{2,0},{4,6},{6,4},{8,10},{10,8},{12,14},{14,12},{1,3},{3,1},... | collective-permute-start | bytes 786440 | tf_op jit(solution)/shard_map/ppermute | solution.py:384
  38.7 16.3 %copy-start.3 = (f32[4,128,256]{2,1,0:T(8,128)}, f32[4,128,256]{2,1,0:T(8,128)S(1)}, u32[]{:S(2)}) copy-start(f32[4,128,256]{2,1,0:T(8,128)S(1)} %collective-permute-done.8.refs_7_.taken_ref) | copy-start | bytes 1572868
  72.7 6.0 %copy-start.2 = (f32[4,128,256]{2,1,0:T(8,128)S(1)}, f32[4,128,256]{2,1,0:T(8,128)}, u32[]{:S(2)}) copy-start(f32[4,128,256]{2,1,0:T(8,128)} %copy-done.1) | copy-start | bytes 1572868
  72.7 6.0 %copy-start.4 = (f32[4,128,256]{2,1,0:T(8,128)S(1)}, f32[4,128,256]{2,1,0:T(8,128)}, u32[]{:S(2)}) copy-start(f32[4,128,256]{2,1,0:T(8,128)} %copy-done.3) | copy-start | bytes 1572868
  72.7 35.8 %all-to-all-start = ((f32[8,136,256]{2,1,0:T(8,128)}), f32[8,136,256]{2,1,0:T(8,128)S(1)}, u32[]{:S(2)}, u32[]{:S(2)}) async-start(f32[8,136,256]{2,1,0:T(8,128)} %get-tuple-element.61), calls=%async_computation | async-start | bytes 2228224 | tf_op jit(solution)/shard_map/all_to_all | solution.py:495
  78.8 28.7 %collective-permute-start.9 = (f32[2,128,256]{2,1,0:T(8,128)S(1)}, f32[2,128,256]{2,1,0:T(8,128)S(1)}, u32[]{:S(2)}, u32[]{:S(2)}) collective-permute-start(f32[2,128,256]{2,1,0:T(8,128)S(1)} %get-tuple-element.66), channel_id=1, source_target_pairs={{0,4},{2,6},{4,0},{6,2},{8,12},{10,14},{12,8},{14,10},{1,5},{3,7},... | collective-permute-start | bytes 786440 | tf_op jit(solution)/shard_map/ppermute | solution.py:384
  80.9 31.6 %collective-permute-start.11 = (f32[2,128,256]{2,1,0:T(8,128)S(1)}, f32[2,128,256]{2,1,0:T(8,128)S(1)}, u32[]{:S(2)}, u32[]{:S(2)}) collective-permute-start(f32[2,128,256]{2,1,0:T(8,128)S(1)} %get-tuple-element.63.refs_0_), channel_id=1, source_target_pairs={{0,4},{2,6},{4,0},{6,2},{8,12},{10,14},{12,8},{14,10},{1,5},{3,7},... | collective-permute-start | bytes 786440 | tf_op jit(solution)/shard_map/ppermute | solution.py:384
  107.5 11.4 %collective-permute-start.10 = (f32[1,128,256]{2,1,0:T(8,128)S(1)}, f32[1,128,256]{2,1,0:T(8,128)S(1)}, u32[]{:S(2)}, u32[]{:S(2)}) collective-permute-start(f32[1,128,256]{2,1,0:T(8,128)S(1)} %get-tuple-element.67.refs_1_), channel_id=1, source_target_pairs={{0,8},{2,10},{4,12},{6,14},{8,0},{10,2},{12,4},{14,6},{1,9},{3,11}... | collective-permute-start | bytes 393224 | tf_op jit(solution)/shard_map/ppermute | solution.py:384
  112.5 8.1 %collective-permute-start.12 = (f32[1,128,256]{2,1,0:T(8,128)S(1)}, f32[1,128,256]{2,1,0:T(8,128)S(1)}, u32[]{:S(2)}, u32[]{:S(2)}) collective-permute-start(f32[1,128,256]{2,1,0:T(8,128)S(1)} %get-tuple-element.73), channel_id=1, source_target_pairs={{0,8},{2,10},{4,12},{6,14},{8,0},{10,2},{12,4},{14,6},{1,9},{3,11}... | collective-permute-start | bytes 393224 | tf_op jit(solution)/shard_map/ppermute | solution.py:384
  114.6 12.1 %all-to-all-start.2 = ((f32[16,8,256]{2,1,0:T(8,128)}), f32[16,8,256]{2,1,0:T(8,128)S(1)}, u32[]{:S(2)}, u32[]{:S(2)}) async-start(f32[16,8,256]{2,1,0:T(8,128)} %shard_map.78.refs_0_), calls=%async_computation.2 | async-start | bytes 262144 | tf_op jit(solution)/shard_map/all_to_all | solution.py:517
  120.7 8.1 %collective-permute-start.13 = (f32[2,64,256]{2,1,0:T(8,128)S(1)}, f32[2,64,256]{2,1,0:T(8,128)S(1)}, u32[]{:S(2)}, u32[]{:S(2)}) collective-permute-start(f32[2,64,256]{2,1,0:T(8,128)S(1)} %get-tuple-element.75), channel_id=1, source_target_pairs={{0,1},{1,0},{2,3},{3,2},{4,5},{5,4},{6,7},{7,6},{8,9},{9,8},{10,11... | collective-permute-start | bytes 393224 | tf_op jit(solution)/shard_map/ppermute | solution.py:384

commit v18 on v17

--- a/solution.py
+++ b/solution.py
@@ -213,8 +213,8 @@
 def apply_kernel(devices, capacity, table_ref, high_hbm, low_hbm, diagonal_hbm, direction_ref, norm_ref, dosage_high_ref,
                  dosage_low_ref, *refs):
     received_refs = refs[:devices - 1]
-    (scaled_hbm, handled_hbm, outgoing_hbm, products_hbm, gathered_ref, high_ref, low_ref, diagonal_ref, scaled_ref,
-     handled_ref, sums_ref, even_ref, odd_ref, semaphores) = refs[-14:]
+    (scaled_hbm, handled_hbm, outgoing_hbm, even_hbm, odd_hbm, gathered_ref, high_ref, low_ref, diagonal_ref, scaled_ref,
+     handled_ref, sums_ref, even_ref, odd_ref, semaphores) = refs[-15:]
     copies = Copies(semaphores)
     loads = [
         copies.start(high_hbm, high_ref), copies.start(low_hbm, low_ref), copies.start(diagonal_hbm, diagonal_ref)
@@ -239,8 +239,7 @@
         stores.append(copies.start(scaled_ref.at[pl.ds(start, tile)], outgoing_hbm.at[other, pl.ds(0, tile)]))
         stores.append(copies.start(sums_ref, outgoing_hbm.at[other, pl.ds(tile, SUBLANES)]))
     score_products(dosage_high_ref, dosage_low_ref, scaled_ref[...], even_ref, odd_ref)
-    own_bit = lax.axis_index("samples") & 1
-    stores += [copies.start(odd_ref, products_hbm.at[1 - own_bit]), copies.start(even_ref, products_hbm.at[own_bit])]
+    stores += [copies.start(odd_ref, odd_hbm), copies.start(even_ref, even_hbm)]
     far = pl.ds(tile, depth - tile)
     for row in range(block_count):
         blocks = []
@@ -288,26 +287,33 @@
     copies.start(sums_ref, sums_hbm).wait()
 
 
-def add_kernel(kept_ref, taken_ref, *refs):
-    near_ref, far_ref = refs[-2:]
+def add_kernel(kept_ref, taken_ref, near_ref, far_ref):
     count = near_ref.shape[0]
     near_ref[...] = kept_ref[pl.ds(0, count)] + taken_ref[pl.ds(0, count)]
     far_ref[...] = kept_ref[pl.ds(count, count)] + taken_ref[pl.ds(count, count)]
 
 
-def pair_kernel(products_ref, near_ref, far_ref):
-    count = near_ref.shape[0]
-    near_ref[...] = products_ref[0, pl.ds(0, count)] + products_ref[1, pl.ds(0, count)]
-    far_ref[...] = products_ref[0, pl.ds(count, count)] + products_ref[1, pl.ds(count, count)]
-
-
-def last_add_kernel(first_kept_ref, first_taken_ref, second_kept_ref, second_taken_ref, own_ref, other_ref):
+def merge_kernel(first_kept_ref, first_taken_ref, second_kept_ref, second_taken_ref, gate_ref, near_ref, far_ref):
+    count = first_kept_ref.shape[0] // 2
+    for start, out_ref in ((0, near_ref), (count, far_ref)):
+        here = pl.ds(start, count)
+        out_ref[pl.ds(0, count)] = first_kept_ref[here] + first_taken_ref[here]
+        out_ref[pl.ds(count, count)] = second_kept_ref[here] + second_taken_ref[here]
+
+
+def add_both_kernel(kept_ref, taken_ref, near_ref, far_ref):
+    count = kept_ref.shape[0] // 4
+    for start, out_ref in ((0, near_ref), (count, far_ref)):
+        for i in range(2):
+            here = pl.ds(2 * i * count + start, count)
+            out_ref[pl.ds(i * count, count)] = kept_ref[here] + taken_ref[here]
+
+
+def last_add_kernel(kept_ref, taken_ref, own_ref, other_ref):
     rows = own_ref.shape[1]
-    for i, (kept_ref, taken_ref) in enumerate(
-        ((first_kept_ref, first_taken_ref), (second_kept_ref, second_taken_ref))
-    ):
-        own_ref[i] = kept_ref[0, pl.ds(0, rows), :] + taken_ref[0, pl.ds(0, rows), :]
-        other_ref[i] = kept_ref[0, pl.ds(rows, rows), :] + taken_ref[0, pl.ds(rows, rows), :]
+    for start, out_ref in ((0, own_ref), (rows, other_ref)):
+        here = pl.ds(start, rows)
+        out_ref[...] = kept_ref[:, here, :] + taken_ref[:, here, :]
 
 
 def group_kernel(order, own_ref, other_ref, high_ref, low_ref):
@@ -454,11 +460,9 @@
 
     products = float_of(half, 2 * share_rows, columns)
 
-    def add_step(kept, taken, *gates):
+    def add_step(kernel, kept, *taken):
         rows = float_of(kept.shape[0] // 2, 2 * share_rows, columns)
-        return call(
-            add_kernel, [rows] * 2, [vmem] * 2 + [hbm] * len(gates), [vmem] * 2
-        )(kept, taken, *at_home(*gates))
+        return call(kernel, [rows] * 2, [vmem] * (1 + len(taken)), [vmem] * 2)(kept, *taken)
 
     partner = swap(direction, "samples", devices, half)
     near = to_mates(outgoing)
@@ -473,55 +477,47 @@
         [vmem] * (half - 1),
     )(forward, partner, *near, direction_even, direction_odd, *at_home(high, low)))
     received = near + far + [partner.reshape(block_count, tile, columns)]
-    scaled, handled, outgoing, scaled_products = call(
+    products_out = pltpu.HBM(products.shape, jnp.float32)
+    scaled, handled, outgoing, scaled_even, scaled_odd = call(
         functools.partial(apply_kernel, devices, capacity),
         [
-            full_out, full_out, pltpu.HBM((devices, tile + SUBLANES, columns), jnp.float32),
-            pltpu.HBM((2, *products.shape), jnp.float32),
+            full_out, full_out, pltpu.HBM((devices, tile + SUBLANES, columns), jnp.float32), products_out, products_out,
         ],
         [smem, hbm, hbm, hbm] + [vmem] * (devices + 3) + [anywhere],
-        [hbm] * 4,
+        [hbm] * 5,
         [
             room(devices * capacity + block_count, tile, columns), tiles_room, tiles_room, room(people, 1), full_room,
             full_room, room(SUBLANES, columns), room(*products.shape), room(*products.shape),
             pltpu.SemaphoreType.DMA((2 * devices + 7,)),
         ],
         limit=large,
-    )(table, *at_home(high, low, diagonal), direction, norm, *grouped, *received, direction_share)
-    scaled_products = lax.all_to_all(
-        scaled_products, "samples", split_axis=0, concat_axis=0, tiled=True,
-        axis_index_groups=[[i, i + 1] for i in range(0, devices, 2)],
-    )
+    )(table, high, low, diagonal, direction, norm, *grouped, *received, direction_share)
     later = lax.all_to_all(outgoing, "samples", split_axis=0, concat_axis=0, tiled=True)
-    direction_kept, direction_given = add_step(direction_even, direction_share)
-    scaled_kept, scaled_given = call(
-        pair_kernel, [float_of(half // 2, 2 * share_rows, columns)] * 2, [vmem], [vmem] * 2
-    )(scaled_products)
-    for step in steps[:-1]:
-        direction_taken = swap(after(direction_given, scaled), "samples", devices, step)
-        direction_kept, direction_given = add_step(direction_kept, direction_taken)
-    direction_taken = swap(direction_given, "samples", devices, steps[-1])
+    scaled_share = swap(scaled_odd, "samples", devices, 1)
+    direction_kept, direction_given = add_step(add_kernel, direction_even, direction_share)
+    direction_taken = swap(after(direction_given, scaled), "samples", devices, steps[0])
+    scaled_kept, scaled_given = add_step(add_kernel, scaled_even, scaled_share)
     scaled_taken = swap(scaled_given, "samples", devices, steps[0])
     sums = call(
         functools.partial(curvature_kernel, devices),
         pltpu.HBM((2 * devices, SUBLANES, columns), jnp.float32),
-        [smem] + [hbm] * 6 + [anywhere] * 3,
+        [smem] + [hbm] * 6 + [anywhere] * 2,
         hbm,
         [
             room(2 * devices, SUBLANES, columns), tiles_room, tiles_room, full_room, room(people, 1), full_room,
             full_room, room(devices, tile + SUBLANES, columns), pltpu.SemaphoreType.DMA((8,)),
         ],
-    )(
-        table, *at_home(high, low, direction_kept_hbm, diagonal, scaled, handled), later, scaled_given, direction_given
-    )
+    )(table, *at_home(high, low, direction_kept_hbm, diagonal, scaled, handled), later, scaled_given)
     all_sums = lax.all_to_all(sums, ("samples", "cols"), split_axis=0, concat_axis=0, tiled=True)
-    for step in steps[1:]:
-        scaled_kept, scaled_given = add_step(scaled_kept, scaled_taken, sums)
-        scaled_taken = swap(scaled_given, "samples", devices, step)
+    halves = float_of(scaled_kept.shape[0], 2 * share_rows, columns)
+    kept, given = call(
+        merge_kernel, [halves] * 2, [vmem] * 4 + [hbm], [vmem] * 2
+    )(direction_kept, direction_taken, scaled_kept, scaled_taken, *at_home(sums))
+    for step in steps[1:-1]:
+        kept, given = add_step(add_both_kernel, kept, swap(given, "samples", devices, step))
+    taken = swap(given, "samples", devices, steps[-1])
     rows = float_of(2, share_rows, columns)
-    own_scores, other_scores = call(
-        last_add_kernel, [rows] * 2, [vmem] * 4, [vmem] * 2
-    )(direction_kept, direction_taken, scaled_kept, scaled_taken)
+    own_scores, other_scores = call(last_add_kernel, [rows] * 2, [vmem] * 2, [vmem] * 2)(kept, taken)
     solved, factors = call(
         functools.partial(solved_kernel, devices),
         [full, float_of(SUBLANES, columns)],

time: 130 us -> 114 us (0.88)
  blocking collectives: 17.6 us -> 0 us
  starting transfers between devices: 28.4 us -> 31.4 us
    all_to_all x1 -> x0, blocking collectives: 17.6 us -> none  [per_device(): lax.all_to_all(scaled_products, 'samples', split_axis=0, concat_axis=0, t...]
    all_to_all x1, waiting for transfers between devices: 5.95 us -> 1.49 us  [per_device(): lax.all_to_all(sums, ('samples', 'cols'), split_axis=0, concat_axis=0, ti...]
    ppermute x14, starting transfers between devices: 18.1 us -> 21.8 us  [swap(): return lax.ppermute(values, axis, [(i, i ^ step) for i in range(devices)])]
    ppermute x14, waiting for transfers between devices: 51.6 us -> 55.1 us  [swap(): return lax.ppermute(values, axis, [(i, i ^ step) for i in range(devices)])]
  transfers between devices with their start and end apart: 16 -> 16, of which waited for: 9 -> 10; matrix products, arithmetic and copies ran while one was open for 2% -> 3% of each run, Pallas kernels for 9% -> 11%
where the time goes in v18:
time: 114 us; the launch traced here: 113 us
  waiting for transfers between devices  56.7 us (50%)
  starting transfers between devices  31.4 us (28%)
  Pallas kernels  20.1 us (18%)
  local copies, waits for them, and re-layouts  4.12 us (4%)
    ppermute x14, waiting for transfers between devices, swap(): return lax.ppermute(values, axis, [(i, i ^ step) for i in range(devices)])  55.1 us
    ppermute x14, starting transfers between devices, swap(): return lax.ppermute(values, axis, [(i, i ^ step) for i in range(devices)])  21.8 us
    all_to_all x1, starting transfers between devices, per_device(): lax.all_to_all(outgoing, 'samples', split_axis=0, concat_axis=0, tiled=True)  6.09 us
    pallas_call x1, Pallas kernels, per_device(): call(functools.partial(apply_kernel, devices, capacity), [full_out, full_...  4.75 us
    pallas_call x1, Pallas kernels, per_device(): call(functools.partial(curvature_kernel, devices), pltpu.HBM((2 * devices...  3.99 us
    all_to_all x1, starting transfers between devices, per_device(): lax.all_to_all(sums, ('samples', 'cols'), split_axis=0, concat_axis=0, ti...  3.51 us
    pallas_call x1, Pallas kernels, per_device(): call(direction_kernel, [full, full_out, pltpu.HBM((people, 1), jnp.float3...  2.46 us
    pallas_call x1, Pallas kernels, per_device(): call(tiles_kernel, [tiles_out] * 2, [hbm], [hbm] * 2, [room(*kinship.shap...  2.32 us
  transfers between devices with their start and end apart: 16, of which 10 were waited for; matrix products, arithmetic and copies ran while one was open for 3% of the time, Pallas kernels for 11%

profile of v18, /device:TPU:0, one launch (start us, length us, event | category | flops | bytes accessed | tf_op | source)
XLA Modules:
  0.0 113.1 jit_solution(6375142095750428154)
XLA Ops:
  0.7 2.5 %shard_map.68 = (f32[512,256]{1,0:T(8,128)S(1)}, f32[512,256]{1,0:T(8,128)}, f32[512,1]{1,0:T(8,128)}, f32[8,256]{1,0:T(8,128)S(1)}) custom-call(f32[4,4,128,128]{3,2,1,0:T(8,128)} %kinship_hbm.3, f32[4,128]{1,0:T(4,128)} %bitcast.9, f32[512,256]{1,0:T(8,128)} %phenotypes_hbm.1), custom_call_target="tpu_custom_call" | custom-call | tf_op jit(solution)/shard_map/pallas_call | solution.py:421
  3.7 3.7 %collective-permute-start.4 = (f32[512,256]{1,0:T(8,128)S(1)}, f32[512,256]{1,0:T(8,128)S(1)}, u32[]{:S(2)}, u32[]{:S(2)}) collective-permute-start(f32[512,256]{1,0:T(8,128)S(1)} %get-tuple-element.39.direction_ref.values_ref), channel_id=1, source_target_pairs={{0,8},{2,10},{4,12},{6,14},{8,0},{10,2},{12,4},{14,6},{1,9},{3,11}... | collective-permute-start | bytes 1572872 | tf_op jit(solution)/shard_map/ppermute | solution.py:390
  7.3 1.8 %shard_map.69 = (s32[4,12]{1,0:T(4,128)S(1)}, s32[2,4]{1,0:T(2,128)S(1)}, f32[2,128,256]{2,1,0:T(8,128)}, f32[2,128,256]{2,1,0:T(8,128)}, f32[2,128,256]{2,1,0:T(8,128)}) custom-call(s32[3,32]{1,0:T(4,128)S(1)} %bitcast.8, f32[512,256]{1,0:T(8,128)S(1)} %get-tuple-element.39.direction_ref.values_ref, f32[512,512]{1,0:T(8,128)S(1)} %collective-permute-done.gate_ref), custom_call_target="tpu_custom_call" | custom-call | tf_op jit(solution)/shard_map/pallas_call | solution.py:440
  9.2 2.6 %collective-permute-start.1 = (f32[2,128,256]{2,1,0:T(8,128)}, f32[2,128,256]{2,1,0:T(8,128)S(1)}, u32[]{:S(2)}, u32[]{:S(2)}) collective-permute-start(f32[2,128,256]{2,1,0:T(8,128)} %get-tuple-element.49), channel_id=1, source_target_pairs={{0,6},{2,4},{4,2},{6,0},{8,14},{10,12},{12,10},{14,8},{1,7},{3,5},... | collective-permute-start | bytes 786440 | tf_op jit(solution)/shard_map/ppermute | solution.py:390
  12.7 1.6 %copy.7 = f32[512,512]{0,1:T(8,128)S(1)} copy(f32[512,512]{1,0:T(8,128)} %param.9) | data formatting | bytes 2097152 | tf_op jit(solution)/shard_map/optimization_barrier | solution.py:394
  18.0 1.6 %collective-permute-start.8 = (f32[4,128,256]{2,1,0:T(8,128)S(1)}, f32[4,128,256]{2,1,0:T(8,128)S(1)}, u32[]{:S(2)}, u32[]{:S(2)}) collective-permute-start(f32[4,128,256]{2,1,0:T(8,128)S(1)} %get-tuple-element.54.refs_4_), channel_id=1, source_target_pairs={{0,2},{2,0},{4,6},{6,4},{8,10},{10,8},{12,14},{14,12},{1,3},{3,1},... | collective-permute-start | bytes 1572872 | tf_op jit(solution)/shard_map/ppermute | solution.py:390
  19.6 2.3 %shard_map.70 = (bf16[4,128,512]{2,1,0:T(8,128)(2,1)}, bf16[4,128,512]{2,1,0:T(8,128)(2,1)}) custom-call(f32[4,4,128,128]{3,2,1,0:T(8,128)} %kinship_hbm.3), custom_call_target="tpu_custom_call" | custom-call | tf_op jit(solution)/shard_map/pallas_call | solution.py:450
  22.0 9.2 %collective-permute-done.4.partner_ref = f32[512,256]{1,0:T(8,128)S(1)} collective-permute-done((f32[512,256]{1,0:T(8,128)S(1)}, f32[512,256]{1,0:T(8,128)S(1)}, u32[]{:S(2)}, u32[]{:S(2)}) %collective-permute-start.4) | collective-permute-done | bytes 524320 | tf_op jit(solution)/shard_map/ppermute | solution.py:390
  31.2 3.4 %collective-permute-done.2.refs_1_ = f32[2,128,256]{2,1,0:T(8,128)} collective-permute-done((f32[2,128,256]{2,1,0:T(8,128)}, f32[2,128,256]{2,1,0:T(8,128)}, u32[]{:S(2)}, u32[]{:S(2)}) %collective-permute-start.2) | collective-permute-done | bytes 262176 | tf_op jit(solution)/shard_map/ppermute | solution.py:390
  35.3 2.0 %collective-permute-start.6 = (f32[2,128,256]{2,1,0:T(8,128)S(1)}, f32[2,128,256]{2,1,0:T(8,128)S(1)}, u32[]{:S(2)}, u32[]{:S(2)}) collective-permute-start(f32[2,128,256]{2,1,0:T(8,128)S(1)} %get-tuple-element.56), channel_id=1, source_target_pairs={{0,4},{2,6},{4,0},{6,2},{8,12},{10,14},{12,8},{14,10},{1,5},{3,7},... | collective-permute-start | bytes 786440 | tf_op jit(solution)/shard_map/ppermute | solution.py:390
  38.8 6.7 %collective-permute-done.5.refs_3_ = f32[2,128,256]{2,1,0:T(8,128)S(1)} collective-permute-done((f32[2,128,256]{2,1,0:T(8,128)S(1)}, f32[2,128,256]{2,1,0:T(8,128)S(1)}, u32[]{:S(2)}, u32[]{:S(2)}) %collective-permute-start.5) | collective-permute-done | bytes 262176 | tf_op jit(solution)/shard_map/ppermute | solution.py:390
  45.5 3.0 %collective-permute-done.6.refs_4_ = f32[2,128,256]{2,1,0:T(8,128)S(1)} collective-permute-done((f32[2,128,256]{2,1,0:T(8,128)S(1)}, f32[2,128,256]{2,1,0:T(8,128)S(1)}, u32[]{:S(2)}, u32[]{:S(2)}) %collective-permute-start.6) | collective-permute-done | bytes 262176 | tf_op jit(solution)/shard_map/ppermute | solution.py:390
  49.4 4.8 %shard_map.74 = (f32[512,256]{1,0:T(8,128)}, f32[512,256]{1,0:T(8,128)}, f32[8,136,256]{2,1,0:T(8,128)}, f32[4,128,256]{2,1,0:T(8,128)}, f32[4,128,256]{2,1,0:T(8,128)}) custom-call(s32[4,12]{1,0:T(4,128)S(1)} %get-tuple-element.41.table_ref, bf16[4,128,512]{2,1,0:T(8,128)(2,1)S(1)} %copy-done, bf16[4,128,512]{2,1,0:T(8,128)(2,1)S(1)} %copy-done.1, ...), custom_call_target="tpu_custom_call" | custom-call | tf_op jit(solution)/shard_map/pallas_call | solution.py:481
  54.1 6.1 %all-to-all-start = ((f32[8,136,256]{2,1,0:T(8,128)}), f32[8,136,256]{2,1,0:T(8,128)S(1)}, u32[]{:S(2)}, u32[]{:S(2)}) async-start(f32[8,136,256]{2,1,0:T(8,128)} %get-tuple-element.60), calls=%async_computation | async-start | bytes 2228224 | tf_op jit(solution)/shard_map/all_to_all | solution.py:495
  60.2 2.0 %collective-permute-start.9 = (f32[4,128,256]{2,1,0:T(8,128)}, f32[4,128,256]{2,1,0:T(8,128)S(1)}, u32[]{:S(2)}, u32[]{:S(2)}) collective-permute-start(f32[4,128,256]{2,1,0:T(8,128)} %get-tuple-element.62), channel_id=1, source_target_pairs={{0,2},{2,0},{4,6},{6,4},{8,10},{10,8},{12,14},{14,12},{1,3},{3,1},... | collective-permute-start | bytes 1572872 | tf_op jit(solution)/shard_map/ppermute | solution.py:390
  62.3 1.5 %collective-permute-start.10 = (f32[2,128,256]{2,1,0:T(8,128)S(1)}, f32[2,128,256]{2,1,0:T(8,128)S(1)}, u32[]{:S(2)}, u32[]{:S(2)}) collective-permute-start(f32[2,128,256]{2,1,0:T(8,128)S(1)} %get-tuple-element.68), channel_id=1, source_target_pairs={{0,4},{2,6},{4,0},{6,2},{8,12},{10,14},{12,8},{14,10},{1,5},{3,7},... | collective-permute-start | bytes 786440 | tf_op jit(solution)/shard_map/ppermute | solution.py:390
  63.8 22.0 %collective-permute-done.9.taken_ref = f32[4,128,256]{2,1,0:T(8,128)S(1)} collective-permute-done((f32[4,128,256]{2,1,0:T(8,128)}, f32[4,128,256]{2,1,0:T(8,128)S(1)}, u32[]{:S(2)}, u32[]{:S(2)}) %collective-permute-start.9) | collective-permute-done | bytes 524320 | tf_op jit(solution)/shard_map/ppermute | solution.py:390
  85.9 1.5 %collective-permute-start.11 = (f32[2,128,256]{2,1,0:T(8,128)S(1)}, f32[2,128,256]{2,1,0:T(8,128)S(1)}, u32[]{:S(2)}, u32[]{:S(2)}) collective-permute-start(f32[2,128,256]{2,1,0:T(8,128)S(1)} %get-tuple-element.63.refs_0_), channel_id=1, source_target_pairs={{0,4},{2,6},{4,0},{6,2},{8,12},{10,14},{12,8},{14,10},{1,5},{3,7},... | collective-permute-start | bytes 786440 | tf_op jit(solution)/shard_map/ppermute | solution.py:390
  87.5 4.0 %shard_map.76.gate_ref = f32[16,8,256]{2,1,0:T(8,128)} custom-call(s32[4,12]{1,0:T(4,128)S(1)} %get-tuple-element.41.table_ref, bf16[4,128,512]{2,1,0:T(8,128)(2,1)} %get-tuple-element.42.refs_5_.high_hbm, bf16[4,128,512]{2,1,0:T(8,128)(2,1)} %get-tuple-element.43.refs_6_.low_hbm, f32[512,256]{1,0:T(8,128)} %get-tuple-element.38.direction_hbm, ...), custom_call_target="tpu_custom_call" | custom-call | tf_op jit(solution)/shard_map/pallas_call | solution.py:501
  91.5 1.6 %collective-permute-done.11.second_taken_ref = f32[2,128,256]{2,1,0:T(8,128)S(1)} collective-permute-done((f32[2,128,256]{2,1,0:T(8,128)S(1)}, f32[2,128,256]{2,1,0:T(8,128)S(1)}, u32[]{:S(2)}, u32[]{:S(2)}) %collective-permute-start.11) | collective-permute-done | bytes 262176 | tf_op jit(solution)/shard_map/ppermute | solution.py:390
  93.2 3.8 %collective-permute-start.12 = (f32[2,128,256]{2,1,0:T(8,128)S(1)}, f32[2,128,256]{2,1,0:T(8,128)S(1)}, u32[]{:S(2)}, u32[]{:S(2)}) collective-permute-start(f32[2,128,256]{2,1,0:T(8,128)S(1)} %get-tuple-element.71), channel_id=1, source_target_pairs={{0,8},{2,10},{4,12},{6,14},{8,0},{10,2},{12,4},{14,6},{1,9},{3,11}... | collective-permute-start | bytes 786440 | tf_op jit(solution)/shard_map/ppermute | solution.py:390
  97.0 3.5 %all-to-all-start.1 = ((f32[16,8,256]{2,1,0:T(8,128)}), f32[16,8,256]{2,1,0:T(8,128)S(1)}, u32[]{:S(2)}, u32[]{:S(2)}) async-start(f32[16,8,256]{2,1,0:T(8,128)} %shard_map.76.gate_ref), calls=%async_computation.1 | async-start | bytes 262144 | tf_op jit(solution)/shard_map/all_to_all | solution.py:511
  100.5 8.3 %collective-permute-done.12.taken_ref = f32[2,128,256]{2,1,0:T(8,128)S(1)} collective-permute-done((f32[2,128,256]{2,1,0:T(8,128)S(1)}, f32[2,128,256]{2,1,0:T(8,128)S(1)}, u32[]{:S(2)}, u32[]{:S(2)}) %collective-permute-start.12) | collective-permute-done | bytes 262176 | tf_op jit(solution)/shard_map/ppermute | solution.py:390
  110.4 2.0 %shard_map.77 = (f32[512,256]{1,0:T(8,128)}, f32[8,256]{1,0:T(8,128)S(1)}) custom-call(f32[512,256]{1,0:T(8,128)} %get-tuple-element.38.direction_hbm, f32[512,256]{1,0:T(8,128)} %get-tuple-element.58.scaled_hbm, f32[16,8,256]{2,1,0:T(8,128)S(1)} %all-to-all-done.1.sums_ref), custom_call_target="tpu_custom_call" | custom-call | tf_op jit(solution)/shard_map/pallas_call | solution.py:521
  (38 shorter events, 10.8 us)
Async XLA Ops:
  0.6 2.5 %copy-start.6 = (f32[512,512]{1,0:T(8,128)S(1)}, f32[512,512]{1,0:T(8,128)}, u32[]{:S(2)}) copy-start(f32[512,512]{1,0:T(8,128)} %param.9) | copy-start | bytes 3145732
  0.6 6.7 %copy-start.5 = (s32[32,3]{0,1:T(4,128)S(1)}, s32[32,3]{0,1:T(4,128)}, u32[]{:S(2)}) copy-start(s32[32,3]{0,1:T(4,128)} %param.6) | copy-start | bytes 1156
  3.1 4.2 %collective-permute-start = (f32[512,512]{1,0:T(8,128)S(1)}, f32[512,512]{1,0:T(8,128)S(1)}, u32[]{:S(2)}, u32[]{:S(2)}) collective-permute-start(f32[512,512]{1,0:T(8,128)S(1)} %copy-done.6), channel_id=1, source_target_pairs={{0,1},{1,0},{2,3},{3,2},{4,5},{5,4},{6,7},{7,6},{8,9},{9,8},{10,11... | collective-permute-start | bytes 3145736 | tf_op jit(solution)/shard_map/ppermute | solution.py:390
  3.7 27.5 %collective-permute-start.4 = (f32[512,256]{1,0:T(8,128)S(1)}, f32[512,256]{1,0:T(8,128)S(1)}, u32[]{:S(2)}, u32[]{:S(2)}) collective-permute-start(f32[512,256]{1,0:T(8,128)S(1)} %get-tuple-element.39.direction_ref.values_ref), channel_id=1, source_target_pairs={{0,8},{2,10},{4,12},{6,14},{8,0},{10,2},{12,4},{14,6},{1,9},{3,11}... | collective-permute-start | bytes 1572872 | tf_op jit(solution)/shard_map/ppermute | solution.py:390
  9.2 22.0 %collective-permute-start.1 = (f32[2,128,256]{2,1,0:T(8,128)}, f32[2,128,256]{2,1,0:T(8,128)S(1)}, u32[]{:S(2)}, u32[]{:S(2)}) collective-permute-start(f32[2,128,256]{2,1,0:T(8,128)} %get-tuple-element.49), channel_id=1, source_target_pairs={{0,6},{2,4},{4,2},{6,0},{8,14},{10,12},{12,10},{14,8},{1,7},{3,5},... | collective-permute-start | bytes 786440 | tf_op jit(solution)/shard_map/ppermute | solution.py:390
  11.8 22.8 %collective-permute-start.2 = (f32[2,128,256]{2,1,0:T(8,128)}, f32[2,128,256]{2,1,0:T(8,128)}, u32[]{:S(2)}, u32[]{:S(2)}) collective-permute-start(f32[2,128,256]{2,1,0:T(8,128)} %get-tuple-element.50), channel_id=1, source_target_pairs={{0,4},{2,6},{4,0},{6,2},{8,12},{10,14},{12,8},{14,10},{1,5},{3,7},... | collective-permute-start | bytes 786440 | tf_op jit(solution)/shard_map/ppermute | solution.py:390
  12.2 22.4 %collective-permute-start.3 = (f32[2,128,256]{2,1,0:T(8,128)}, f32[2,128,256]{2,1,0:T(8,128)}, u32[]{:S(2)}, u32[]{:S(2)}) collective-permute-start(f32[2,128,256]{2,1,0:T(8,128)} %get-tuple-element.51), channel_id=1, source_target_pairs={{0,2},{2,0},{4,6},{6,4},{8,10},{10,8},{12,14},{14,12},{1,3},{3,1},... | collective-permute-start | bytes 786440 | tf_op jit(solution)/shard_map/ppermute | solution.py:390
  15.6 1.2 %copy-start.2 = (f32[512,512]{0,1:T(8,128)S(1)}, f32[512,512]{0,1:T(8,128)}, u32[]{:S(2)}) copy-start(f32[512,512]{0,1:T(8,128)} %copy.8) | copy-start | bytes 3145732
  18.0 20.7 %collective-permute-start.8 = (f32[4,128,256]{2,1,0:T(8,128)S(1)}, f32[4,128,256]{2,1,0:T(8,128)S(1)}, u32[]{:S(2)}, u32[]{:S(2)}) collective-permute-start(f32[4,128,256]{2,1,0:T(8,128)S(1)} %get-tuple-element.54.refs_4_), channel_id=1, source_target_pairs={{0,2},{2,0},{4,6},{6,4},{8,10},{10,8},{12,14},{14,12},{1,3},{3,1},... | collective-permute-start | bytes 1572872 | tf_op jit(solution)/shard_map/ppermute | solution.py:390
  34.6 14.8 %copy-start = (bf16[4,128,512]{2,1,0:T(8,128)(2,1)S(1)}, bf16[4,128,512]{2,1,0:T(8,128)(2,1)}, u32[]{:S(2)}) copy-start(bf16[4,128,512]{2,1,0:T(8,128)(2,1)} %get-tuple-element.42.refs_5_.high_hbm) | copy-start | bytes 1572868
  34.6 14.8 %copy-start.1 = (bf16[4,128,512]{2,1,0:T(8,128)(2,1)S(1)}, bf16[4,128,512]{2,1,0:T(8,128)(2,1)}, u32[]{:S(2)}) copy-start(bf16[4,128,512]{2,1,0:T(8,128)(2,1)} %get-tuple-element.43.refs_6_.low_hbm) | copy-start | bytes 1572868
  34.6 14.8 %copy-start.3 = (f32[512,1]{1,0:T(8,128)S(1)}, f32[512,1]{1,0:T(8,128)}, u32[]{:S(2)}) copy-start(f32[512,1]{1,0:T(8,128)} %get-tuple-element.44.diagonal_hbm) | copy-start | bytes 6148
  35.2 10.3 %collective-permute-start.5 = (f32[2,128,256]{2,1,0:T(8,128)S(1)}, f32[2,128,256]{2,1,0:T(8,128)S(1)}, u32[]{:S(2)}, u32[]{:S(2)}) collective-permute-start(f32[2,128,256]{2,1,0:T(8,128)S(1)} %get-tuple-element.55), channel_id=1, source_target_pairs={{0,6},{2,4},{4,2},{6,0},{8,14},{10,12},{12,10},{14,8},{1,7},{3,5},... | collective-permute-start | bytes 786440 | tf_op jit(solution)/shard_map/ppermute | solution.py:390
  35.3 13.2 %collective-permute-start.6 = (f32[2,128,256]{2,1,0:T(8,128)S(1)}, f32[2,128,256]{2,1,0:T(8,128)S(1)}, u32[]{:S(2)}, u32[]{:S(2)}) collective-permute-start(f32[2,128,256]{2,1,0:T(8,128)S(1)} %get-tuple-element.56), channel_id=1, source_target_pairs={{0,4},{2,6},{4,0},{6,2},{8,12},{10,14},{12,8},{14,10},{1,5},{3,7},... | collective-permute-start | bytes 786440 | tf_op jit(solution)/shard_map/ppermute | solution.py:390
  37.3 12.0 %collective-permute-start.7 = (f32[2,128,256]{2,1,0:T(8,128)S(1)}, f32[2,128,256]{2,1,0:T(8,128)S(1)}, u32[]{:S(2)}, u32[]{:S(2)}) collective-permute-start(f32[2,128,256]{2,1,0:T(8,128)S(1)} %get-tuple-element.57), channel_id=1, source_target_pairs={{0,2},{2,0},{4,6},{6,4},{8,10},{10,8},{12,14},{14,12},{1,3},{3,1},... | collective-permute-start | bytes 786440 | tf_op jit(solution)/shard_map/ppermute | solution.py:390
  54.1 31.8 %copy-start.4 = (f32[4,128,256]{2,1,0:T(8,128)S(1)}, f32[4,128,256]{2,1,0:T(8,128)}, u32[]{:S(2)}) copy-start(f32[4,128,256]{2,1,0:T(8,128)} %get-tuple-element.61.kept_ref) | copy-start | bytes 1572868
  54.1 33.4 %all-to-all-start = ((f32[8,136,256]{2,1,0:T(8,128)}), f32[8,136,256]{2,1,0:T(8,128)S(1)}, u32[]{:S(2)}, u32[]{:S(2)}) async-start(f32[8,136,256]{2,1,0:T(8,128)} %get-tuple-element.60), calls=%async_computation | async-start | bytes 2228224 | tf_op jit(solution)/shard_map/all_to_all | solution.py:495
  60.2 25.6 %collective-permute-start.9 = (f32[4,128,256]{2,1,0:T(8,128)}, f32[4,128,256]{2,1,0:T(8,128)S(1)}, u32[]{:S(2)}, u32[]{:S(2)}) collective-permute-start(f32[4,128,256]{2,1,0:T(8,128)} %get-tuple-element.62), channel_id=1, source_target_pairs={{0,2},{2,0},{4,6},{6,4},{8,10},{10,8},{12,14},{14,12},{1,3},{3,1},... | collective-permute-start | bytes 1572872 | tf_op jit(solution)/shard_map/ppermute | solution.py:390
  62.3 29.2 %collective-permute-start.10 = (f32[2,128,256]{2,1,0:T(8,128)S(1)}, f32[2,128,256]{2,1,0:T(8,128)S(1)}, u32[]{:S(2)}, u32[]{:S(2)}) collective-permute-start(f32[2,128,256]{2,1,0:T(8,128)S(1)} %get-tuple-element.68), channel_id=1, source_target_pairs={{0,4},{2,6},{4,0},{6,2},{8,12},{10,14},{12,8},{14,10},{1,5},{3,7},... | collective-permute-start | bytes 786440 | tf_op jit(solution)/shard_map/ppermute | solution.py:390
  85.9 7.2 %collective-permute-start.11 = (f32[2,128,256]{2,1,0:T(8,128)S(1)}, f32[2,128,256]{2,1,0:T(8,128)S(1)}, u32[]{:S(2)}, u32[]{:S(2)}) collective-permute-start(f32[2,128,256]{2,1,0:T(8,128)S(1)} %get-tuple-element.63.refs_0_), channel_id=1, source_target_pairs={{0,4},{2,6},{4,0},{6,2},{8,12},{10,14},{12,8},{14,10},{1,5},{3,7},... | collective-permute-start | bytes 786440 | tf_op jit(solution)/shard_map/ppermute | solution.py:390
  93.2 15.6 %collective-permute-start.12 = (f32[2,128,256]{2,1,0:T(8,128)S(1)}, f32[2,128,256]{2,1,0:T(8,128)S(1)}, u32[]{:S(2)}, u32[]{:S(2)}) collective-permute-start(f32[2,128,256]{2,1,0:T(8,128)S(1)} %get-tuple-element.71), channel_id=1, source_target_pairs={{0,8},{2,10},{4,12},{6,14},{8,0},{10,2},{12,4},{14,6},{1,9},{3,11}... | collective-permute-start | bytes 786440 | tf_op jit(solution)/shard_map/ppermute | solution.py:390
  97.0 13.4 %all-to-all-start.1 = ((f32[16,8,256]{2,1,0:T(8,128)}), f32[16,8,256]{2,1,0:T(8,128)S(1)}, u32[]{:S(2)}, u32[]{:S(2)}) async-start(f32[16,8,256]{2,1,0:T(8,128)} %shard_map.76.gate_ref), calls=%async_computation.1 | async-start | bytes 262144 | tf_op jit(solution)/shard_map/all_to_all | solution.py:511
  108.8 3.6 %collective-permute-start.13 = (f32[2,64,256]{2,1,0:T(8,128)S(1)}, f32[2,64,256]{2,1,0:T(8,128)S(1)}, u32[]{:S(2)}, u32[]{:S(2)}) collective-permute-start(f32[2,64,256]{2,1,0:T(8,128)S(1)} %get-tuple-element.73), channel_id=1, source_target_pairs={{0,1},{1,0},{2,3},{3,2},{4,5},{5,4},{6,7},{7,6},{8,9},{9,8},{10,11... | collective-permute-start | bytes 393224 | tf_op jit(solution)/shard_map/ppermute | solution.py:390

commit v19 on v18

--- a/solution.py
+++ b/solution.py
@@ -287,33 +287,26 @@
     copies.start(sums_ref, sums_hbm).wait()
 
 
-def add_kernel(kept_ref, taken_ref, near_ref, far_ref):
+def add_kernel(kept_ref, taken_ref, *refs):
+    near_ref, far_ref = refs[-2:]
     count = near_ref.shape[0]
     near_ref[...] = kept_ref[pl.ds(0, count)] + taken_ref[pl.ds(0, count)]
     far_ref[...] = kept_ref[pl.ds(count, count)] + taken_ref[pl.ds(count, count)]
 
 
-def merge_kernel(first_kept_ref, first_taken_ref, second_kept_ref, second_taken_ref, gate_ref, near_ref, far_ref):
-    count = first_kept_ref.shape[0] // 2
-    for start, out_ref in ((0, near_ref), (count, far_ref)):
-        here = pl.ds(start, count)
-        out_ref[pl.ds(0, count)] = first_kept_ref[here] + first_taken_ref[here]
-        out_ref[pl.ds(count, count)] = second_kept_ref[here] + second_taken_ref[here]
-
-
-def add_both_kernel(kept_ref, taken_ref, near_ref, far_ref):
-    count = kept_ref.shape[0] // 4
-    for start, out_ref in ((0, near_ref), (count, far_ref)):
-        for i in range(2):
-            here = pl.ds(2 * i * count + start, count)
-            out_ref[pl.ds(i * count, count)] = kept_ref[here] + taken_ref[here]
-
-
-def last_add_kernel(kept_ref, taken_ref, own_ref, other_ref):
+def odd_kernel(kept_ref, taken_ref, near_ref, far_ref):
+    for i in range(near_ref.shape[0]):
+        near_ref[i] = kept_ref[2 * i] + taken_ref[2 * i]
+        far_ref[i] = kept_ref[2 * i + 1] + taken_ref[2 * i + 1]
+
+
+def last_add_kernel(first_kept_ref, first_taken_ref, second_kept_ref, second_taken_ref, own_ref, other_ref):
     rows = own_ref.shape[1]
-    for start, out_ref in ((0, own_ref), (rows, other_ref)):
-        here = pl.ds(start, rows)
-        out_ref[...] = kept_ref[:, here, :] + taken_ref[:, here, :]
+    for i, (kept_ref, taken_ref) in enumerate(
+        ((first_kept_ref, first_taken_ref), (second_kept_ref, second_taken_ref))
+    ):
+        own_ref[i] = kept_ref[0, pl.ds(0, rows), :] + taken_ref[0, pl.ds(0, rows), :]
+        other_ref[i] = kept_ref[0, pl.ds(rows, rows), :] + taken_ref[0, pl.ds(rows, rows), :]
 
 
 def group_kernel(order, own_ref, other_ref, high_ref, low_ref):
@@ -460,9 +453,9 @@
 
     products = float_of(half, 2 * share_rows, columns)
 
-    def add_step(kernel, kept, *taken):
+    def add_step(kernel, kept, taken, *gates):
         rows = float_of(kept.shape[0] // 2, 2 * share_rows, columns)
-        return call(kernel, [rows] * 2, [vmem] * (1 + len(taken)), [vmem] * 2)(kept, *taken)
+        return call(kernel, [rows] * 2, [vmem] * 2 + [hbm] * len(gates), [vmem] * 2)(kept, taken, *gates)
 
     partner = swap(direction, "samples", devices, half)
     near = to_mates(outgoing)
@@ -476,6 +469,9 @@
         [smem, vmem] + [anywhere] * (half + 1) + [hbm] * 2,
         [vmem] * (half - 1),
     )(forward, partner, *near, direction_even, direction_odd, *at_home(high, low)))
+    direction_kept, direction_given = add_step(odd_kernel, direction_even, direction_share)
+    direction_given, *far = lax.optimization_barrier((direction_given, *far))
+    direction_taken = swap(direction_given, "samples", devices, half)
     received = near + far + [partner.reshape(block_count, tile, columns)]
     products_out = pltpu.HBM(products.shape, jnp.float32)
     scaled, handled, outgoing, scaled_even, scaled_odd = call(
@@ -493,10 +489,12 @@
         limit=large,
     )(table, high, low, diagonal, direction, norm, *grouped, *received, direction_share)
     later = lax.all_to_all(outgoing, "samples", split_axis=0, concat_axis=0, tiled=True)
+    scaled_odd, direction_taken = lax.optimization_barrier((scaled_odd, direction_taken))
     scaled_share = swap(scaled_odd, "samples", devices, 1)
-    direction_kept, direction_given = add_step(add_kernel, direction_even, direction_share)
-    direction_taken = swap(after(direction_given, scaled), "samples", devices, steps[0])
-    scaled_kept, scaled_given = add_step(add_kernel, scaled_even, scaled_share)
+    for step in steps[:-1]:
+        direction_kept, direction_given = add_step(add_kernel, direction_kept, direction_taken)
+        direction_taken = swap(direction_given, "samples", devices, step)
+    scaled_kept, scaled_given = add_step(add_kernel, scaled_even, scaled_share, direction_taken)
     scaled_taken = swap(scaled_given, "samples", devices, steps[0])
     sums = call(
         functools.partial(curvature_kernel, devices),
@@ -509,15 +507,13 @@
         ],
     )(table, *at_home(high, low, direction_kept_hbm, diagonal, scaled, handled), later, scaled_given)
     all_sums = lax.all_to_all(sums, ("samples", "cols"), split_axis=0, concat_axis=0, tiled=True)
-    halves = float_of(scaled_kept.shape[0], 2 * share_rows, columns)
-    kept, given = call(
-        merge_kernel, [halves] * 2, [vmem] * 4 + [hbm], [vmem] * 2
-    )(direction_kept, direction_taken, scaled_kept, scaled_taken, *at_home(sums))
-    for step in steps[1:-1]:
-        kept, given = add_step(add_both_kernel, kept, swap(given, "samples", devices, step))
-    taken = swap(given, "samples", devices, steps[-1])
+    for step in steps[1:]:
+        scaled_kept, scaled_given = add_step(add_kernel, scaled_kept, scaled_taken, *at_home(sums))
+        scaled_taken = swap(scaled_given, "samples", devices, step)
     rows = float_of(2, share_rows, columns)
-    own_scores, other_scores = call(last_add_kernel, [rows] * 2, [vmem] * 2, [vmem] * 2)(kept, taken)
+    own_scores, other_scores = call(
+        last_add_kernel, [rows] * 2, [vmem] * 4, [vmem] * 2
+    )(direction_kept, direction_taken, scaled_kept, scaled_taken)
     solved, factors = call(
         functools.partial(solved_kernel, devices),
         [full, float_of(SUBLANES, columns)],

time: 114 us -> 136 us (1.19)
  waiting for transfers between devices: 56.7 us -> 80 us
    ppermute x14 -> x15, waiting for transfers between devices: 55.1 us -> 73.3 us  [swap(): return lax.ppermute(values, axis, [(i, i ^ step) for i in range(devices)])]
    all_to_all x1, waiting for transfers between devices: 1.49 us -> 6.76 us  [per_device(): lax.all_to_all(sums, ('samples', 'cols'), split_axis=0, concat_axis=0, ti...]
    ppermute x14 -> x15, starting transfers between devices: 21.8 us -> 20.1 us  [swap(): return lax.ppermute(values, axis, [(i, i ^ step) for i in range(devices)])]
  transfers between devices with their start and end apart: 16 -> 17, of which waited for: 10 -> 11; matrix products, arithmetic and copies ran while one was open for 3% -> 2% of each run, Pallas kernels for 11% -> 9%
where the time goes in v19:
time: 136 us; the launch traced here: 135 us
  waiting for transfers between devices  80 us (59%)
  starting transfers between devices  30.1 us (22%)
  Pallas kernels  20.1 us (15%)
  local copies, waits for them, and re-layouts  4.16 us (3%)
    ppermute x15, waiting for transfers between devices, swap(): return lax.ppermute(values, axis, [(i, i ^ step) for i in range(devices)])  73.3 us
    ppermute x15, starting transfers between devices, swap(): return lax.ppermute(values, axis, [(i, i ^ step) for i in range(devices)])  20.1 us
    all_to_all x1, waiting for transfers between devices, per_device(): lax.all_to_all(sums, ('samples', 'cols'), split_axis=0, concat_axis=0, ti...  6.76 us
    all_to_all x1, starting transfers between devices, per_device(): lax.all_to_all(outgoing, 'samples', split_axis=0, concat_axis=0, tiled=True)  6.09 us
    pallas_call x1, Pallas kernels, per_device(): call(functools.partial(apply_kernel, devices, capacity), [full_out, full_...  4.77 us
    pallas_call x1, Pallas kernels, per_device(): call(functools.partial(curvature_kernel, devices), pltpu.HBM((2 * devices...  4 us
    all_to_all x1, starting transfers between devices, per_device(): lax.all_to_all(sums, ('samples', 'cols'), split_axis=0, concat_axis=0, ti...  3.93 us
  transfers between devices with their start and end apart: 17, of which 11 were waited for; matrix products, arithmetic and copies ran while one was open for 2% of the time, Pallas kernels for 9%

profile of v19, /device:TPU:0, one launch (start us, length us, event | category | flops | bytes accessed | tf_op | source)
XLA Modules:
  0.0 135.3 jit_solution(7351853542855192722)
XLA Ops:
  0.7 2.5 %shard_map.68 = (f32[512,256]{1,0:T(8,128)S(1)}, f32[512,256]{1,0:T(8,128)}, f32[512,1]{1,0:T(8,128)}, f32[8,256]{1,0:T(8,128)S(1)}) custom-call(f32[4,4,128,128]{3,2,1,0:T(8,128)} %kinship_hbm.3, f32[4,128]{1,0:T(4,128)} %bitcast.9, f32[512,256]{1,0:T(8,128)} %phenotypes_hbm.1), custom_call_target="tpu_custom_call" | custom-call | tf_op jit(solution)/shard_map/pallas_call | solution.py:414
  3.7 3.7 %collective-permute-start.5 = (f32[512,256]{1,0:T(8,128)S(1)}, f32[512,256]{1,0:T(8,128)S(1)}, u32[]{:S(2)}, u32[]{:S(2)}) collective-permute-start(f32[512,256]{1,0:T(8,128)S(1)} %get-tuple-element.46.direction_ref.values_ref), channel_id=1, source_target_pairs={{0,8},{2,10},{4,12},{6,14},{8,0},{10,2},{12,4},{14,6},{1,9},{3,11}... | collective-permute-start | bytes 1572872 | tf_op jit(solution)/shard_map/ppermute | solution.py:383
  7.3 1.8 %shard_map.69 = (s32[4,12]{1,0:T(4,128)S(1)}, s32[2,4]{1,0:T(2,128)S(1)}, f32[2,128,256]{2,1,0:T(8,128)}, f32[2,128,256]{2,1,0:T(8,128)}, f32[2,128,256]{2,1,0:T(8,128)}) custom-call(s32[3,32]{1,0:T(4,128)S(1)} %bitcast.8, f32[512,256]{1,0:T(8,128)S(1)} %get-tuple-element.46.direction_ref.values_ref, f32[512,512]{1,0:T(8,128)S(1)} %collective-permute-done.gate_ref), custom_call_target="tpu_custom_call" | custom-call | tf_op jit(solution)/shard_map/pallas_call | solution.py:433
  9.1 2.6 %collective-permute-start.1 = (f32[2,128,256]{2,1,0:T(8,128)}, f32[2,128,256]{2,1,0:T(8,128)S(1)}, u32[]{:S(2)}, u32[]{:S(2)}) collective-permute-start(f32[2,128,256]{2,1,0:T(8,128)} %get-tuple-element.56), channel_id=1, source_target_pairs={{0,6},{2,4},{4,2},{6,0},{8,14},{10,12},{12,10},{14,8},{1,7},{3,5},... | collective-permute-start | bytes 786440 | tf_op jit(solution)/shard_map/ppermute | solution.py:383
  12.7 1.6 %copy.7 = f32[512,512]{0,1:T(8,128)S(1)} copy(f32[512,512]{1,0:T(8,128)} %param.9) | data formatting | bytes 2097152 | tf_op jit(solution)/shard_map/optimization_barrier | solution.py:387
  18.0 1.6 %collective-permute-start.4 = (f32[4,128,256]{2,1,0:T(8,128)S(1)}, f32[4,128,256]{2,1,0:T(8,128)S(1)}, u32[]{:S(2)}, u32[]{:S(2)}) collective-permute-start(f32[4,128,256]{2,1,0:T(8,128)S(1)} %get-tuple-element.60.refs_4_), channel_id=1, source_target_pairs={{0,2},{2,0},{4,6},{6,4},{8,10},{10,8},{12,14},{14,12},{1,3},{3,1},... | collective-permute-start | bytes 1572872 | tf_op jit(solution)/shard_map/ppermute | solution.py:383
  19.6 2.3 %shard_map.70 = (bf16[4,128,512]{2,1,0:T(8,128)(2,1)}, bf16[4,128,512]{2,1,0:T(8,128)(2,1)}) custom-call(f32[4,4,128,128]{3,2,1,0:T(8,128)} %kinship_hbm.3), custom_call_target="tpu_custom_call" | custom-call | tf_op jit(solution)/shard_map/pallas_call | solution.py:443
  21.9 9.2 %collective-permute-done.5.partner_ref = f32[512,256]{1,0:T(8,128)S(1)} collective-permute-done((f32[512,256]{1,0:T(8,128)S(1)}, f32[512,256]{1,0:T(8,128)S(1)}, u32[]{:S(2)}, u32[]{:S(2)}) %collective-permute-start.5) | collective-permute-done | bytes 524320 | tf_op jit(solution)/shard_map/ppermute | solution.py:383
  31.2 3.4 %collective-permute-done.2.refs_1_ = f32[2,128,256]{2,1,0:T(8,128)} collective-permute-done((f32[2,128,256]{2,1,0:T(8,128)}, f32[2,128,256]{2,1,0:T(8,128)}, u32[]{:S(2)}, u32[]{:S(2)}) %collective-permute-start.2) | collective-permute-done | bytes 262176 | tf_op jit(solution)/shard_map/ppermute | solution.py:383
  35.3 2.0 %collective-permute-start.7 = (f32[2,128,256]{2,1,0:T(8,128)S(1)}, f32[2,128,256]{2,1,0:T(8,128)S(1)}, u32[]{:S(2)}, u32[]{:S(2)}) collective-permute-start(f32[2,128,256]{2,1,0:T(8,128)S(1)} %get-tuple-element.64), channel_id=1, source_target_pairs={{0,4},{2,6},{4,0},{6,2},{8,12},{10,14},{12,8},{14,10},{1,5},{3,7},... | collective-permute-start | bytes 786440 | tf_op jit(solution)/shard_map/ppermute | solution.py:383
  38.8 6.6 %collective-permute-done.6.refs_3_ = f32[2,128,256]{2,1,0:T(8,128)S(1)} collective-permute-done((f32[2,128,256]{2,1,0:T(8,128)S(1)}, f32[2,128,256]{2,1,0:T(8,128)S(1)}, u32[]{:S(2)}, u32[]{:S(2)}) %collective-permute-start.6) | collective-permute-done | bytes 262176 | tf_op jit(solution)/shard_map/ppermute | solution.py:383
  45.5 3.0 %collective-permute-done.7.refs_4_ = f32[2,128,256]{2,1,0:T(8,128)S(1)} collective-permute-done((f32[2,128,256]{2,1,0:T(8,128)S(1)}, f32[2,128,256]{2,1,0:T(8,128)S(1)}, u32[]{:S(2)}, u32[]{:S(2)}) %collective-permute-start.7) | collective-permute-done | bytes 262176 | tf_op jit(solution)/shard_map/ppermute | solution.py:383
  49.3 4.8 %shard_map.75 = (f32[512,256]{1,0:T(8,128)}, f32[512,256]{1,0:T(8,128)}, f32[8,136,256]{2,1,0:T(8,128)}, f32[4,128,256]{2,1,0:T(8,128)}, f32[4,128,256]{2,1,0:T(8,128)}) custom-call(s32[4,12]{1,0:T(4,128)S(1)} %get-tuple-element.48.table_ref, bf16[4,128,512]{2,1,0:T(8,128)(2,1)S(1)} %copy-done, bf16[4,128,512]{2,1,0:T(8,128)(2,1)S(1)} %copy-done.1, ...), custom_call_target="tpu_custom_call" | custom-call | tf_op jit(solution)/shard_map/pallas_call | solution.py:477
  54.2 6.1 %all-to-all-start = ((f32[8,136,256]{2,1,0:T(8,128)}), f32[8,136,256]{2,1,0:T(8,128)S(1)}, u32[]{:S(2)}, u32[]{:S(2)}) async-start(f32[8,136,256]{2,1,0:T(8,128)} %get-tuple-element.71), calls=%async_computation | async-start | bytes 2228224 | tf_op jit(solution)/shard_map/all_to_all | solution.py:491
  60.3 2.9 %collective-permute-start.9 = (f32[2,128,256]{2,1,0:T(8,128)S(1)}, f32[2,128,256]{2,1,0:T(8,128)S(1)}, u32[]{:S(2)}, u32[]{:S(2)}) collective-permute-start(f32[2,128,256]{2,1,0:T(8,128)S(1)} %copy-done.9), channel_id=1, source_target_pairs={{0,8},{2,10},{4,12},{6,14},{8,0},{10,2},{12,4},{14,6},{1,9},{3,11}... | collective-permute-start | bytes 786440 | tf_op jit(solution)/shard_map/ppermute | solution.py:383
  63.2 35.6 %collective-permute-done.9.taken_ref = f32[2,128,256]{2,1,0:T(8,128)S(1)} collective-permute-done((f32[2,128,256]{2,1,0:T(8,128)S(1)}, f32[2,128,256]{2,1,0:T(8,128)S(1)}, u32[]{:S(2)}, u32[]{:S(2)}) %collective-permute-start.9) | collective-permute-done | bytes 262176 | tf_op jit(solution)/shard_map/ppermute | solution.py:383
  100.4 5.0 %collective-permute-done.11.refs_0_.first_taken_ref = f32[1,128,256]{2,1,0:T(8,128)S(1)} collective-permute-done((f32[1,128,256]{2,1,0:T(8,128)S(1)}, f32[1,128,256]{2,1,0:T(8,128)S(1)}, u32[]{:S(2)}, u32[]{:S(2)}) %collective-permute-start.11) | collective-permute-done | bytes 131104 | tf_op jit(solution)/shard_map/ppermute | solution.py:383
  105.3 6.2 %collective-permute-done.10.taken_ref = f32[4,128,256]{2,1,0:T(8,128)S(1)} collective-permute-done((f32[4,128,256]{2,1,0:T(8,128)S(1)}, f32[4,128,256]{2,1,0:T(8,128)S(1)}, u32[]{:S(2)}, u32[]{:S(2)}) %collective-permute-start.10) | collective-permute-done | bytes 524320 | tf_op jit(solution)/shard_map/ppermute | solution.py:383
  111.6 4.0 %shard_map.78.refs_0_ = f32[16,8,256]{2,1,0:T(8,128)} custom-call(s32[4,12]{1,0:T(4,128)S(1)} %get-tuple-element.48.table_ref, bf16[4,128,512]{2,1,0:T(8,128)(2,1)} %get-tuple-element.49.refs_5_.high_hbm, bf16[4,128,512]{2,1,0:T(8,128)(2,1)} %get-tuple-element.50.refs_6_.low_hbm, f32[512,256]{1,0:T(8,128)} %get-tuple-element.45.direction_hbm, ...), custom_call_target="tpu_custom_call" | custom-call | tf_op jit(solution)/shard_map/pallas_call | solution.py:499
  115.6 2.3 %collective-permute-done.12.taken_ref = f32[2,128,256]{2,1,0:T(8,128)S(1)} collective-permute-done((f32[2,128,256]{2,1,0:T(8,128)S(1)}, f32[2,128,256]{2,1,0:T(8,128)S(1)}, u32[]{:S(2)}, u32[]{:S(2)}) %collective-permute-start.12) | collective-permute-done | bytes 262176 | tf_op jit(solution)/shard_map/ppermute | solution.py:383
  118.0 2.6 %collective-permute-start.13 = (f32[1,128,256]{2,1,0:T(8,128)S(1)}, f32[1,128,256]{2,1,0:T(8,128)S(1)}, u32[]{:S(2)}, u32[]{:S(2)}) collective-permute-start(f32[1,128,256]{2,1,0:T(8,128)S(1)} %get-tuple-element.85), channel_id=1, source_target_pairs={{0,8},{2,10},{4,12},{6,14},{8,0},{10,2},{12,4},{14,6},{1,9},{3,11}... | collective-permute-start | bytes 393224 | tf_op jit(solution)/shard_map/ppermute | solution.py:383
  120.7 3.9 %all-to-all-start.1 = ((f32[16,8,256]{2,1,0:T(8,128)}), f32[16,8,256]{2,1,0:T(8,128)S(1)}, u32[]{:S(2)}, u32[]{:S(2)}) async-start(f32[16,8,256]{2,1,0:T(8,128)} %shard_map.78.refs_0_), calls=%async_computation.1 | async-start | bytes 262144 | tf_op jit(solution)/shard_map/all_to_all | solution.py:509
  125.8 6.8 %all-to-all-done.1.sums_ref = f32[16,8,256]{2,1,0:T(8,128)S(1)} async-done(((f32[16,8,256]{2,1,0:T(8,128)}), f32[16,8,256]{2,1,0:T(8,128)S(1)}, u32[]{:S(2)}, u32[]{:S(2)}) %all-to-all-start.1) | async-done | bytes 131104 | tf_op jit(solution)/shard_map/all_to_all | solution.py:509
  132.5 2.0 %shard_map.79 = (f32[512,256]{1,0:T(8,128)}, f32[8,256]{1,0:T(8,128)S(1)}) custom-call(f32[512,256]{1,0:T(8,128)} %get-tuple-element.45.direction_hbm, f32[512,256]{1,0:T(8,128)} %get-tuple-element.69.scaled_hbm, f32[16,8,256]{2,1,0:T(8,128)S(1)} %all-to-all-done.1.sums_ref), custom_call_target="tpu_custom_call" | custom-call | tf_op jit(solution)/shard_map/pallas_call | solution.py:517
  (51 shorter events, 11.9 us)
Async XLA Ops:
  3.1 4.2 %collective-permute-start = (f32[512,512]{1,0:T(8,128)S(1)}, f32[512,512]{1,0:T(8,128)S(1)}, u32[]{:S(2)}, u32[]{:S(2)}) collective-permute-start(f32[512,512]{1,0:T(8,128)S(1)} %copy-done.10), channel_id=1, source_target_pairs={{0,1},{1,0},{2,3},{3,2},{4,5},{5,4},{6,7},{7,6},{8,9},{9,8},{10,11... | collective-permute-start | bytes 3145736 | tf_op jit(solution)/shard_map/ppermute | solution.py:383
  3.7 27.5 %collective-permute-start.5 = (f32[512,256]{1,0:T(8,128)S(1)}, f32[512,256]{1,0:T(8,128)S(1)}, u32[]{:S(2)}, u32[]{:S(2)}) collective-permute-start(f32[512,256]{1,0:T(8,128)S(1)} %get-tuple-element.46.direction_ref.values_ref), channel_id=1, source_target_pairs={{0,8},{2,10},{4,12},{6,14},{8,0},{10,2},{12,4},{14,6},{1,9},{3,11}... | collective-permute-start | bytes 1572872 | tf_op jit(solution)/shard_map/ppermute | solution.py:383
  9.1 22.0 %collective-permute-start.1 = (f32[2,128,256]{2,1,0:T(8,128)}, f32[2,128,256]{2,1,0:T(8,128)S(1)}, u32[]{:S(2)}, u32[]{:S(2)}) collective-permute-start(f32[2,128,256]{2,1,0:T(8,128)} %get-tuple-element.56), channel_id=1, source_target_pairs={{0,6},{2,4},{4,2},{6,0},{8,14},{10,12},{12,10},{14,8},{1,7},{3,5},... | collective-permute-start | bytes 786440 | tf_op jit(solution)/shard_map/ppermute | solution.py:383
  11.7 22.8 %collective-permute-start.2 = (f32[2,128,256]{2,1,0:T(8,128)}, f32[2,128,256]{2,1,0:T(8,128)}, u32[]{:S(2)}, u32[]{:S(2)}) collective-permute-start(f32[2,128,256]{2,1,0:T(8,128)} %get-tuple-element.57), channel_id=1, source_target_pairs={{0,4},{2,6},{4,0},{6,2},{8,12},{10,14},{12,8},{14,10},{1,5},{3,7},... | collective-permute-start | bytes 786440 | tf_op jit(solution)/shard_map/ppermute | solution.py:383
  12.2 22.4 %collective-permute-start.3 = (f32[2,128,256]{2,1,0:T(8,128)}, f32[2,128,256]{2,1,0:T(8,128)}, u32[]{:S(2)}, u32[]{:S(2)}) collective-permute-start(f32[2,128,256]{2,1,0:T(8,128)} %get-tuple-element.58), channel_id=1, source_target_pairs={{0,2},{2,0},{4,6},{6,4},{8,10},{10,8},{12,14},{14,12},{1,3},{3,1},... | collective-permute-start | bytes 786440 | tf_op jit(solution)/shard_map/ppermute | solution.py:383
  18.0 20.7 %collective-permute-start.4 = (f32[4,128,256]{2,1,0:T(8,128)S(1)}, f32[4,128,256]{2,1,0:T(8,128)S(1)}, u32[]{:S(2)}, u32[]{:S(2)}) collective-permute-start(f32[4,128,256]{2,1,0:T(8,128)S(1)} %get-tuple-element.60.refs_4_), channel_id=1, source_target_pairs={{0,2},{2,0},{4,6},{6,4},{8,10},{10,8},{12,14},{14,12},{1,3},{3,1},... | collective-permute-start | bytes 1572872 | tf_op jit(solution)/shard_map/ppermute | solution.py:383
  34.6 14.8 %copy-start.3 = (f32[512,1]{1,0:T(8,128)S(1)}, f32[512,1]{1,0:T(8,128)}, u32[]{:S(2)}) copy-start(f32[512,1]{1,0:T(8,128)} %get-tuple-element.51.diagonal_hbm) | copy-start | bytes 6148
  35.2 14.2 %copy-start = (bf16[4,128,512]{2,1,0:T(8,128)(2,1)S(1)}, bf16[4,128,512]{2,1,0:T(8,128)(2,1)}, u32[]{:S(2)}) copy-start(bf16[4,128,512]{2,1,0:T(8,128)(2,1)} %get-tuple-element.49.refs_5_.high_hbm) | copy-start | bytes 1572868
  35.2 10.3 %collective-permute-start.6 = (f32[2,128,256]{2,1,0:T(8,128)S(1)}, f32[2,128,256]{2,1,0:T(8,128)S(1)}, u32[]{:S(2)}, u32[]{:S(2)}) collective-permute-start(f32[2,128,256]{2,1,0:T(8,128)S(1)} %get-tuple-element.63), channel_id=1, source_target_pairs={{0,6},{2,4},{4,2},{6,0},{8,14},{10,12},{12,10},{14,8},{1,7},{3,5},... | collective-permute-start | bytes 786440 | tf_op jit(solution)/shard_map/ppermute | solution.py:383
  35.3 13.2 %collective-permute-start.7 = (f32[2,128,256]{2,1,0:T(8,128)S(1)}, f32[2,128,256]{2,1,0:T(8,128)S(1)}, u32[]{:S(2)}, u32[]{:S(2)}) collective-permute-start(f32[2,128,256]{2,1,0:T(8,128)S(1)} %get-tuple-element.64), channel_id=1, source_target_pairs={{0,4},{2,6},{4,0},{6,2},{8,12},{10,14},{12,8},{14,10},{1,5},{3,7},... | collective-permute-start | bytes 786440 | tf_op jit(solution)/shard_map/ppermute | solution.py:383
  37.3 12.0 %collective-permute-start.8 = (f32[2,128,256]{2,1,0:T(8,128)S(1)}, f32[2,128,256]{2,1,0:T(8,128)S(1)}, u32[]{:S(2)}, u32[]{:S(2)}) collective-permute-start(f32[2,128,256]{2,1,0:T(8,128)S(1)} %get-tuple-element.65), channel_id=1, source_target_pairs={{0,2},{2,0},{4,6},{6,4},{8,10},{10,8},{12,14},{14,12},{1,3},{3,1},... | collective-permute-start | bytes 786440 | tf_op jit(solution)/shard_map/ppermute | solution.py:383
  38.8 15.3 %copy-start.5 = (f32[2,128,256]{2,1,0:T(8,128)}, f32[2,128,256]{2,1,0:T(8,128)S(1)}, u32[]{:S(2)}) copy-start(f32[2,128,256]{2,1,0:T(8,128)S(1)} %get-tuple-element.76.kept_ref) | copy-start | bytes 786436
  38.8 15.3 %copy-start.8 = (f32[2,128,256]{2,1,0:T(8,128)}, f32[2,128,256]{2,1,0:T(8,128)S(1)}, u32[]{:S(2)}) copy-start(f32[2,128,256]{2,1,0:T(8,128)S(1)} %get-tuple-element.74) | copy-start | bytes 786436
  54.2 44.7 %copy-start.11 = (f32[4,128,256]{2,1,0:T(8,128)S(1)}, f32[4,128,256]{2,1,0:T(8,128)}, u32[]{:S(2)}) copy-start(f32[4,128,256]{2,1,0:T(8,128)} %get-tuple-element.75) | copy-start | bytes 1572868
  54.2 46.1 %copy-start.6 = (f32[2,128,256]{2,1,0:T(8,128)S(1)}, f32[2,128,256]{2,1,0:T(8,128)}, u32[]{:S(2)}) copy-start(f32[2,128,256]{2,1,0:T(8,128)} %copy-done.5) | copy-start | bytes 786436
  54.2 57.3 %copy-start.4 = (f32[4,128,256]{2,1,0:T(8,128)S(1)}, f32[4,128,256]{2,1,0:T(8,128)}, u32[]{:S(2)}) copy-start(f32[4,128,256]{2,1,0:T(8,128)} %get-tuple-element.72.kept_ref) | copy-start | bytes 1572868
  54.2 57.4 %all-to-all-start = ((f32[8,136,256]{2,1,0:T(8,128)}), f32[8,136,256]{2,1,0:T(8,128)S(1)}, u32[]{:S(2)}, u32[]{:S(2)}) async-start(f32[8,136,256]{2,1,0:T(8,128)} %get-tuple-element.71), calls=%async_computation | async-start | bytes 2228224 | tf_op jit(solution)/shard_map/all_to_all | solution.py:491
  60.3 38.5 %collective-permute-start.9 = (f32[2,128,256]{2,1,0:T(8,128)S(1)}, f32[2,128,256]{2,1,0:T(8,128)S(1)}, u32[]{:S(2)}, u32[]{:S(2)}) collective-permute-start(f32[2,128,256]{2,1,0:T(8,128)S(1)} %copy-done.9), channel_id=1, source_target_pairs={{0,8},{2,10},{4,12},{6,14},{8,0},{10,2},{12,4},{14,6},{1,9},{3,11}... | collective-permute-start | bytes 786440 | tf_op jit(solution)/shard_map/ppermute | solution.py:383
  98.8 12.7 %collective-permute-start.10 = (f32[4,128,256]{2,1,0:T(8,128)S(1)}, f32[4,128,256]{2,1,0:T(8,128)S(1)}, u32[]{:S(2)}, u32[]{:S(2)}) collective-permute-start(f32[4,128,256]{2,1,0:T(8,128)S(1)} %copy-done.11), channel_id=1, source_target_pairs={{0,2},{2,0},{4,6},{6,4},{8,10},{10,8},{12,14},{14,12},{1,3},{3,1},... | collective-permute-start | bytes 1572872 | tf_op jit(solution)/shard_map/ppermute | solution.py:383
  100.3 5.0 %collective-permute-start.11 = (f32[1,128,256]{2,1,0:T(8,128)S(1)}, f32[1,128,256]{2,1,0:T(8,128)S(1)}, u32[]{:S(2)}, u32[]{:S(2)}) collective-permute-start(f32[1,128,256]{2,1,0:T(8,128)S(1)} %get-tuple-element.78), channel_id=1, source_target_pairs={{0,4},{2,6},{4,0},{6,2},{8,12},{10,14},{12,8},{14,10},{1,5},{3,7},... | collective-permute-start | bytes 393224 | tf_op jit(solution)/shard_map/ppermute | solution.py:383
  111.5 6.4 %collective-permute-start.12 = (f32[2,128,256]{2,1,0:T(8,128)S(1)}, f32[2,128,256]{2,1,0:T(8,128)S(1)}, u32[]{:S(2)}, u32[]{:S(2)}) collective-permute-start(f32[2,128,256]{2,1,0:T(8,128)S(1)} %get-tuple-element.79.refs_0_), channel_id=1, source_target_pairs={{0,4},{2,6},{4,0},{6,2},{8,12},{10,14},{12,8},{14,10},{1,5},{3,7},... | collective-permute-start | bytes 786440 | tf_op jit(solution)/shard_map/ppermute | solution.py:383
  118.0 7.6 %collective-permute-start.13 = (f32[1,128,256]{2,1,0:T(8,128)S(1)}, f32[1,128,256]{2,1,0:T(8,128)S(1)}, u32[]{:S(2)}, u32[]{:S(2)}) collective-permute-start(f32[1,128,256]{2,1,0:T(8,128)S(1)} %get-tuple-element.85), channel_id=1, source_target_pairs={{0,8},{2,10},{4,12},{6,14},{8,0},{10,2},{12,4},{14,6},{1,9},{3,11}... | collective-permute-start | bytes 393224 | tf_op jit(solution)/shard_map/ppermute | solution.py:383
  120.7 11.9 %all-to-all-start.1 = ((f32[16,8,256]{2,1,0:T(8,128)}), f32[16,8,256]{2,1,0:T(8,128)S(1)}, u32[]{:S(2)}, u32[]{:S(2)}) async-start(f32[16,8,256]{2,1,0:T(8,128)} %shard_map.78.refs_0_), calls=%async_computation.1 | async-start | bytes 262144 | tf_op jit(solution)/shard_map/all_to_all | solution.py:509
  125.7 8.9 %collective-permute-start.14 = (f32[2,64,256]{2,1,0:T(8,128)S(1)}, f32[2,64,256]{2,1,0:T(8,128)S(1)}, u32[]{:S(2)}, u32[]{:S(2)}) collective-permute-start(f32[2,64,256]{2,1,0:T(8,128)S(1)} %get-tuple-element.87), channel_id=1, source_target_pairs={{0,1},{1,0},{2,3},{3,2},{4,5},{5,4},{6,7},{7,6},{8,9},{9,8},{10,11... | collective-permute-start | bytes 393224 | tf_op jit(solution)/shard_map/ppermute | solution.py:383
  (5 other events, 30.7 us)

commit v20 on v19

--- a/solution.py
+++ b/solution.py
@@ -294,12 +294,6 @@
     far_ref[...] = kept_ref[pl.ds(count, count)] + taken_ref[pl.ds(count, count)]
 
 
-def odd_kernel(kept_ref, taken_ref, near_ref, far_ref):
-    for i in range(near_ref.shape[0]):
-        near_ref[i] = kept_ref[2 * i] + taken_ref[2 * i]
-        far_ref[i] = kept_ref[2 * i + 1] + taken_ref[2 * i + 1]
-
-
 def last_add_kernel(first_kept_ref, first_taken_ref, second_kept_ref, second_taken_ref, own_ref, other_ref):
     rows = own_ref.shape[1]
     for i, (kept_ref, taken_ref) in enumerate(
@@ -332,12 +326,10 @@
     return start * (1.0 + step * (ratio + cross / norm)), -start * step
 
 
-def solved_kernel(devices, direction_hbm, scaled_hbm, sums_ref, solved_hbm, factors_ref, direction_ref, scaled_ref,
-                  semaphores):
+def solved_kernel(devices, direction_ref, scaled_ref, sums_ref, solved_hbm, factors_ref, solved_ref, semaphores):
     people, columns = direction_ref.shape
     column = lax.axis_index("cols")
     copies = Copies(semaphores)
-    loads = [copies.start(direction_hbm, direction_ref), copies.start(scaled_hbm, scaled_ref)]
 
     def total(which):
         sums = sums_ref[which]
@@ -349,13 +341,12 @@
     along, across = coefficients(*total(column))
     factors = jnp.concatenate([along, across, *coefficients(*total(1 - column))], axis=0)
     factors_ref[...] = jnp.concatenate([factors, factors], axis=0)
-    wait_all(loads)
     stores = []
     part_rows = people // 4
     for part in range(4):
         block = pl.ds(part * part_rows, part_rows)
-        direction_ref[block, :] = along * direction_ref[block, :] + across * scaled_ref[block, :]
-        stores.append(copies.start(direction_ref.at[block], solved_hbm.at[block]))
+        solved_ref[block, :] = along * direction_ref[block, :] + across * scaled_ref[block, :]
+        stores.append(copies.start(solved_ref.at[block], solved_hbm.at[block]))
     wait_all(stores)
 
 
@@ -453,9 +444,11 @@
 
     products = float_of(half, 2 * share_rows, columns)
 
-    def add_step(kernel, kept, taken, *gates):
+    def add_step(kept, taken, *gates):
         rows = float_of(kept.shape[0] // 2, 2 * share_rows, columns)
-        return call(kernel, [rows] * 2, [vmem] * 2 + [hbm] * len(gates), [vmem] * 2)(kept, taken, *gates)
+        return call(
+            add_kernel, [rows] * 2, [vmem] * 2 + [hbm] * len(gates), [vmem] * 2
+        )(kept, taken, *at_home(*gates))
 
     partner = swap(direction, "samples", devices, half)
     near = to_mates(outgoing)
@@ -469,9 +462,6 @@
         [smem, vmem] + [anywhere] * (half + 1) + [hbm] * 2,
         [vmem] * (half - 1),
     )(forward, partner, *near, direction_even, direction_odd, *at_home(high, low)))
-    direction_kept, direction_given = add_step(odd_kernel, direction_even, direction_share)
-    direction_given, *far = lax.optimization_barrier((direction_given, *far))
-    direction_taken = swap(direction_given, "samples", devices, half)
     received = near + far + [partner.reshape(block_count, tile, columns)]
     products_out = pltpu.HBM(products.shape, jnp.float32)
     scaled, handled, outgoing, scaled_even, scaled_odd = call(
@@ -489,27 +479,27 @@
         limit=large,
     )(table, high, low, diagonal, direction, norm, *grouped, *received, direction_share)
     later = lax.all_to_all(outgoing, "samples", split_axis=0, concat_axis=0, tiled=True)
-    scaled_odd, direction_taken = lax.optimization_barrier((scaled_odd, direction_taken))
     scaled_share = swap(scaled_odd, "samples", devices, 1)
-    for step in steps[:-1]:
-        direction_kept, direction_given = add_step(add_kernel, direction_kept, direction_taken)
-        direction_taken = swap(direction_given, "samples", devices, step)
-    scaled_kept, scaled_given = add_step(add_kernel, scaled_even, scaled_share, direction_taken)
-    scaled_taken = swap(scaled_given, "samples", devices, steps[0])
+    direction_kept, direction_given = add_step(direction_even, direction_share)
+    direction_taken = swap(after(direction_given, scaled), "samples", devices, steps[0])
     sums = call(
         functools.partial(curvature_kernel, devices),
         pltpu.HBM((2 * devices, SUBLANES, columns), jnp.float32),
-        [smem] + [hbm] * 6 + [anywhere] * 2,
+        [smem] + [hbm] * 6 + [anywhere],
         hbm,
         [
             room(2 * devices, SUBLANES, columns), tiles_room, tiles_room, full_room, room(people, 1), full_room,
             full_room, room(devices, tile + SUBLANES, columns), pltpu.SemaphoreType.DMA((8,)),
         ],
-    )(table, *at_home(high, low, direction_kept_hbm, diagonal, scaled, handled), later, scaled_given)
+    )(table, *at_home(high, low, direction_kept_hbm, diagonal, scaled, handled), later)
     all_sums = lax.all_to_all(sums, ("samples", "cols"), split_axis=0, concat_axis=0, tiled=True)
+    scaled_kept, scaled_taken = scaled_even, scaled_share
+    for step in steps:
+        scaled_kept, scaled_given = add_step(scaled_kept, scaled_taken, sums)
+        scaled_taken = swap(scaled_given, "samples", devices, step)
     for step in steps[1:]:
-        scaled_kept, scaled_given = add_step(add_kernel, scaled_kept, scaled_taken, *at_home(sums))
-        scaled_taken = swap(scaled_given, "samples", devices, step)
+        direction_kept, direction_given = add_step(direction_kept, direction_taken, sums)
+        direction_taken = swap(direction_given, "samples", devices, step)
     rows = float_of(2, share_rows, columns)
     own_scores, other_scores = call(
         last_add_kernel, [rows] * 2, [vmem] * 4, [vmem] * 2
@@ -517,10 +507,10 @@
     solved, factors = call(
         functools.partial(solved_kernel, devices),
         [full, float_of(SUBLANES, columns)],
-        [hbm, hbm, vmem],
+        [vmem] * 3,
         [hbm, vmem],
-        [full_room, full_room, pltpu.SemaphoreType.DMA((6,))],
-    )(*at_home(direction_kept_hbm, scaled), all_sums)
+        [full_room, pltpu.SemaphoreType.DMA((4,))],
+    )(direction_kept_hbm, scaled, all_sums)
     scores = call(
         functools.partial(scores_kernel, 1.0 / math.sqrt(people * devices)),
         float_of(share_rows, 2 * columns), [vmem] * 3, vmem,

time: 136 us -> 118 us (0.87)
  waiting for transfers between devices: 80 us -> 61.6 us
  local copies, waits for them, and re-layouts: 4.16 us -> 5.79 us
    ppermute x15, waiting for transfers between devices: 73.3 us -> 32.2 us  [swap(): return lax.ppermute(values, axis, [(i, i ^ step) for i in range(devices)])]
    all_to_all x1, waiting for transfers between devices: 0.01 us -> 23.7 us  [per_device(): lax.all_to_all(outgoing, 'samples', split_axis=0, concat_axis=0, tiled=True)]
    unnamed x24 -> x22, local copies, waits for them, and re-layouts: 1.27 us -> 2.9 us
  transfers between devices with their start and end apart: 17 -> 17, of which waited for: 11 -> 9; matrix products, arithmetic and copies ran while one was open for 2% -> 2% of each run, Pallas kernels for 9% -> 9%
where the time goes in v20:
time: 118 us; the launch traced here: 117 us
  waiting for transfers between devices  61.6 us (52%)
  starting transfers between devices  30.3 us (26%)
  Pallas kernels  18.8 us (16%)
  local copies, waits for them, and re-layouts  5.79 us (5%)
    ppermute x15, waiting for transfers between devices, swap(): return lax.ppermute(values, axis, [(i, i ^ step) for i in range(devices)])  32.2 us
    all_to_all x1, waiting for transfers between devices, per_device(): lax.all_to_all(outgoing, 'samples', split_axis=0, concat_axis=0, tiled=True)  23.7 us
    ppermute x15, starting transfers between devices, swap(): return lax.ppermute(values, axis, [(i, i ^ step) for i in range(devices)])  19.6 us
    all_to_all x1, starting transfers between devices, per_device(): lax.all_to_all(outgoing, 'samples', split_axis=0, concat_axis=0, tiled=True)  5.95 us
    all_to_all x1, waiting for transfers between devices, per_device(): lax.all_to_all(sums, ('samples', 'cols'), split_axis=0, concat_axis=0, ti...  5.71 us
    all_to_all x1, starting transfers between devices, per_device(): lax.all_to_all(sums, ('samples', 'cols'), split_axis=0, concat_axis=0, ti...  4.74 us
    pallas_call x1, Pallas kernels, per_device(): call(functools.partial(apply_kernel, devices, capacity), [full_out, full_...  4.71 us
    pallas_call x1, Pallas kernels, per_device(): call(functools.partial(curvature_kernel, devices), pltpu.HBM((2 * devices...  3.98 us
  transfers between devices with their start and end apart: 17, of which 9 were waited for; matrix products, arithmetic and copies ran while one was open for 2% of the time, Pallas kernels for 9%

profile of v20, /device:TPU:0, one launch (start us, length us, event | category | flops | bytes accessed | tf_op | source)
XLA Modules:
  0.0 117.4 jit_solution(1851241711625239218)
XLA Ops:
  0.7 2.4 %shard_map.68 = (f32[512,256]{1,0:T(8,128)S(1)}, f32[512,256]{1,0:T(8,128)}, f32[512,1]{1,0:T(8,128)}, f32[8,256]{1,0:T(8,128)S(1)}) custom-call(f32[4,4,128,128]{3,2,1,0:T(8,128)} %kinship_hbm.3, f32[4,128]{1,0:T(4,128)} %bitcast.9, f32[512,256]{1,0:T(8,128)} %phenotypes_hbm.1), custom_call_target="tpu_custom_call" | custom-call | tf_op jit(solution)/shard_map/pallas_call | solution.py:405
  3.6 3.7 %collective-permute-start.4 = (f32[512,256]{1,0:T(8,128)S(1)}, f32[512,256]{1,0:T(8,128)S(1)}, u32[]{:S(2)}, u32[]{:S(2)}) collective-permute-start(f32[512,256]{1,0:T(8,128)S(1)} %get-tuple-element.41.direction_ref.values_ref), channel_id=1, source_target_pairs={{0,8},{2,10},{4,12},{6,14},{8,0},{10,2},{12,4},{14,6},{1,9},{3,11}... | collective-permute-start | bytes 1572872 | tf_op jit(solution)/shard_map/ppermute | solution.py:374
  7.3 1.8 %shard_map.69 = (s32[4,12]{1,0:T(4,128)S(1)}, s32[2,4]{1,0:T(2,128)S(1)}, f32[2,128,256]{2,1,0:T(8,128)}, f32[2,128,256]{2,1,0:T(8,128)}, f32[2,128,256]{2,1,0:T(8,128)}) custom-call(s32[3,32]{1,0:T(4,128)S(1)} %bitcast.8, f32[512,256]{1,0:T(8,128)S(1)} %get-tuple-element.41.direction_ref.values_ref, f32[512,512]{1,0:T(8,128)S(1)} %collective-permute-done.gate_ref), custom_call_target="tpu_custom_call" | custom-call | tf_op jit(solution)/shard_map/pallas_call | solution.py:424
  9.1 2.6 %collective-permute-start.1 = (f32[2,128,256]{2,1,0:T(8,128)}, f32[2,128,256]{2,1,0:T(8,128)S(1)}, u32[]{:S(2)}, u32[]{:S(2)}) collective-permute-start(f32[2,128,256]{2,1,0:T(8,128)} %get-tuple-element.51), channel_id=1, source_target_pairs={{0,6},{2,4},{4,2},{6,0},{8,14},{10,12},{12,10},{14,8},{1,7},{3,5},... | collective-permute-start | bytes 786440 | tf_op jit(solution)/shard_map/ppermute | solution.py:374
  12.7 1.6 %copy.7 = f32[512,512]{0,1:T(8,128)S(1)} copy(f32[512,512]{1,0:T(8,128)} %param.9) | data formatting | bytes 2097152 | tf_op jit(solution)/shard_map/optimization_barrier | solution.py:378
  18.0 1.6 %collective-permute-start.8 = (f32[4,128,256]{2,1,0:T(8,128)S(1)}, f32[4,128,256]{2,1,0:T(8,128)S(1)}, u32[]{:S(2)}, u32[]{:S(2)}) collective-permute-start(f32[4,128,256]{2,1,0:T(8,128)S(1)} %get-tuple-element.56.refs_4_), channel_id=1, source_target_pairs={{0,2},{2,0},{4,6},{6,4},{8,10},{10,8},{12,14},{14,12},{1,3},{3,1},... | collective-permute-start | bytes 1572872 | tf_op jit(solution)/shard_map/ppermute | solution.py:374
  19.6 2.3 %shard_map.70 = (bf16[4,128,512]{2,1,0:T(8,128)(2,1)}, bf16[4,128,512]{2,1,0:T(8,128)(2,1)}) custom-call(f32[4,4,128,128]{3,2,1,0:T(8,128)} %kinship_hbm.3), custom_call_target="tpu_custom_call" | custom-call | tf_op jit(solution)/shard_map/pallas_call | solution.py:434
  21.9 9.2 %collective-permute-done.4.partner_ref = f32[512,256]{1,0:T(8,128)S(1)} collective-permute-done((f32[512,256]{1,0:T(8,128)S(1)}, f32[512,256]{1,0:T(8,128)S(1)}, u32[]{:S(2)}, u32[]{:S(2)}) %collective-permute-start.4) | collective-permute-done | bytes 524320 | tf_op jit(solution)/shard_map/ppermute | solution.py:374
  31.9 2.7 %collective-permute-done.2.refs_1_ = f32[2,128,256]{2,1,0:T(8,128)} collective-permute-done((f32[2,128,256]{2,1,0:T(8,128)}, f32[2,128,256]{2,1,0:T(8,128)}, u32[]{:S(2)}, u32[]{:S(2)}) %collective-permute-start.2) | collective-permute-done | bytes 262176 | tf_op jit(solution)/shard_map/ppermute | solution.py:374
  36.2 2.0 %collective-permute-start.6 = (f32[2,128,256]{2,1,0:T(8,128)S(1)}, f32[2,128,256]{2,1,0:T(8,128)S(1)}, u32[]{:S(2)}, u32[]{:S(2)}) collective-permute-start(f32[2,128,256]{2,1,0:T(8,128)S(1)} %get-tuple-element.58), channel_id=1, source_target_pairs={{0,4},{2,6},{4,0},{6,2},{8,12},{10,14},{12,8},{14,10},{1,5},{3,7},... | collective-permute-start | bytes 786440 | tf_op jit(solution)/shard_map/ppermute | solution.py:374
  38.2 1.5 %collective-permute-start.7 = (f32[2,128,256]{2,1,0:T(8,128)S(1)}, f32[2,128,256]{2,1,0:T(8,128)S(1)}, u32[]{:S(2)}, u32[]{:S(2)}) collective-permute-start(f32[2,128,256]{2,1,0:T(8,128)S(1)} %get-tuple-element.59), channel_id=1, source_target_pairs={{0,2},{2,0},{4,6},{6,4},{8,10},{10,8},{12,14},{14,12},{1,3},{3,1},... | collective-permute-start | bytes 786440 | tf_op jit(solution)/shard_map/ppermute | solution.py:374
  39.7 6.7 %collective-permute-done.5.refs_3_ = f32[2,128,256]{2,1,0:T(8,128)S(1)} collective-permute-done((f32[2,128,256]{2,1,0:T(8,128)S(1)}, f32[2,128,256]{2,1,0:T(8,128)S(1)}, u32[]{:S(2)}, u32[]{:S(2)}) %collective-permute-start.5) | collective-permute-done | bytes 262176 | tf_op jit(solution)/shard_map/ppermute | solution.py:374
  46.4 3.0 %collective-permute-done.6.refs_4_ = f32[2,128,256]{2,1,0:T(8,128)S(1)} collective-permute-done((f32[2,128,256]{2,1,0:T(8,128)S(1)}, f32[2,128,256]{2,1,0:T(8,128)S(1)}, u32[]{:S(2)}, u32[]{:S(2)}) %collective-permute-start.6) | collective-permute-done | bytes 262176 | tf_op jit(solution)/shard_map/ppermute | solution.py:374
  50.3 4.7 %shard_map.74 = (f32[512,256]{1,0:T(8,128)}, f32[512,256]{1,0:T(8,128)}, f32[8,136,256]{2,1,0:T(8,128)}, f32[4,128,256]{2,1,0:T(8,128)}, f32[4,128,256]{2,1,0:T(8,128)}) custom-call(s32[4,12]{1,0:T(4,128)S(1)} %get-tuple-element.43.table_ref, bf16[4,128,512]{2,1,0:T(8,128)(2,1)S(1)} %copy-done, bf16[4,128,512]{2,1,0:T(8,128)(2,1)S(1)} %copy-done.1, ...), custom_call_target="tpu_custom_call" | custom-call | tf_op jit(solution)/shard_map/pallas_call | solution.py:467
  55.0 5.9 %all-to-all-start = ((f32[8,136,256]{2,1,0:T(8,128)}), f32[8,136,256]{2,1,0:T(8,128)S(1)}, u32[]{:S(2)}, u32[]{:S(2)}) async-start(f32[8,136,256]{2,1,0:T(8,128)} %get-tuple-element.62), calls=%async_computation | async-start | bytes 2228224 | tf_op jit(solution)/shard_map/all_to_all | solution.py:481
  60.9 2.0 %collective-permute-start.11 = (f32[4,128,256]{2,1,0:T(8,128)}, f32[4,128,256]{2,1,0:T(8,128)S(1)}, u32[]{:S(2)}, u32[]{:S(2)}) collective-permute-start(f32[4,128,256]{2,1,0:T(8,128)} %get-tuple-element.71), channel_id=1, source_target_pairs={{0,2},{2,0},{4,6},{6,4},{8,10},{10,8},{12,14},{14,12},{1,3},{3,1},... | collective-permute-start | bytes 1572872 | tf_op jit(solution)/shard_map/ppermute | solution.py:374
  63.0 1.5 %collective-permute-start.9 = (f32[2,128,256]{2,1,0:T(8,128)S(1)}, f32[2,128,256]{2,1,0:T(8,128)S(1)}, u32[]{:S(2)}, u32[]{:S(2)}) collective-permute-start(f32[2,128,256]{2,1,0:T(8,128)S(1)} %get-tuple-element.67), channel_id=1, source_target_pairs={{0,4},{2,6},{4,0},{6,2},{8,12},{10,14},{12,8},{14,10},{1,5},{3,7},... | collective-permute-start | bytes 786440 | tf_op jit(solution)/shard_map/ppermute | solution.py:374
  64.5 23.7 %all-to-all-done.later_hbm = f32[8,136,256]{2,1,0:T(8,128)S(1)} async-done(((f32[8,136,256]{2,1,0:T(8,128)}), f32[8,136,256]{2,1,0:T(8,128)S(1)}, u32[]{:S(2)}, u32[]{:S(2)}) %all-to-all-start) | async-done | bytes 1114144 | tf_op jit(solution)/shard_map/all_to_all | solution.py:481
  88.2 4.0 %shard_map.75.refs_0_ = f32[16,8,256]{2,1,0:T(8,128)} custom-call(s32[4,12]{1,0:T(4,128)S(1)} %get-tuple-element.43.table_ref, bf16[4,128,512]{2,1,0:T(8,128)(2,1)} %get-tuple-element.44.refs_5_.high_hbm, bf16[4,128,512]{2,1,0:T(8,128)(2,1)} %get-tuple-element.45.refs_6_.low_hbm, f32[512,256]{1,0:T(8,128)} %get-tuple-element.40.direction_hbm.direction_ref, ...), custom_call_target="tpu_custom_call" | custom-call | tf_op jit(solution)/shard_map/pallas_call | solution.py:485
  92.5 2.2 %collective-permute-start.10 = (f32[1,128,256]{2,1,0:T(8,128)S(1)}, f32[1,128,256]{2,1,0:T(8,128)S(1)}, u32[]{:S(2)}, u32[]{:S(2)}) collective-permute-start(f32[1,128,256]{2,1,0:T(8,128)S(1)} %get-tuple-element.69), channel_id=1, source_target_pairs={{0,8},{2,10},{4,12},{6,14},{8,0},{10,2},{12,4},{14,6},{1,9},{3,11}... | collective-permute-start | bytes 393224 | tf_op jit(solution)/shard_map/ppermute | solution.py:374
  94.7 7.6 %collective-permute-done.12.taken_ref = f32[2,128,256]{2,1,0:T(8,128)S(1)} collective-permute-done((f32[2,128,256]{2,1,0:T(8,128)S(1)}, f32[2,128,256]{2,1,0:T(8,128)S(1)}, u32[]{:S(2)}, u32[]{:S(2)}) %collective-permute-start.12) | collective-permute-done | bytes 262176 | tf_op jit(solution)/shard_map/ppermute | solution.py:374
  103.2 4.7 %all-to-all-start.1 = ((f32[16,8,256]{2,1,0:T(8,128)}), f32[16,8,256]{2,1,0:T(8,128)S(1)}, u32[]{:S(2)}, u32[]{:S(2)}) async-start(f32[16,8,256]{2,1,0:T(8,128)} %shard_map.75.refs_0_), calls=%async_computation.1 | async-start | bytes 262144 | tf_op jit(solution)/shard_map/all_to_all | solution.py:495
  107.9 2.1 %collective-permute-done.13.second_taken_ref = f32[1,128,256]{2,1,0:T(8,128)S(1)} collective-permute-done((f32[1,128,256]{2,1,0:T(8,128)S(1)}, f32[1,128,256]{2,1,0:T(8,128)S(1)}, u32[]{:S(2)}, u32[]{:S(2)}) %collective-permute-start.13) | collective-permute-done | bytes 131104 | tf_op jit(solution)/shard_map/ppermute | solution.py:374
  110.2 5.7 %all-to-all-done.1.sums_ref = f32[16,8,256]{2,1,0:T(8,128)S(1)} async-done(((f32[16,8,256]{2,1,0:T(8,128)}), f32[16,8,256]{2,1,0:T(8,128)S(1)}, u32[]{:S(2)}, u32[]{:S(2)}) %all-to-all-start.1) | async-done | bytes 131104 | tf_op jit(solution)/shard_map/all_to_all | solution.py:495
  (49 shorter events, 11.2 us)
Async XLA Ops:
  0.6 6.7 %copy-start.9 = (s32[32,3]{0,1:T(4,128)S(1)}, s32[32,3]{0,1:T(4,128)}, u32[]{:S(2)}) copy-start(s32[32,3]{0,1:T(4,128)} %param.6) | copy-start | bytes 1156
  3.1 4.2 %collective-permute-start = (f32[512,512]{1,0:T(8,128)S(1)}, f32[512,512]{1,0:T(8,128)S(1)}, u32[]{:S(2)}, u32[]{:S(2)}) collective-permute-start(f32[512,512]{1,0:T(8,128)S(1)} %copy-done.10), channel_id=1, source_target_pairs={{0,1},{1,0},{2,3},{3,2},{4,5},{5,4},{6,7},{7,6},{8,9},{9,8},{10,11... | collective-permute-start | bytes 3145736 | tf_op jit(solution)/shard_map/ppermute | solution.py:374
  3.6 27.5 %collective-permute-start.4 = (f32[512,256]{1,0:T(8,128)S(1)}, f32[512,256]{1,0:T(8,128)S(1)}, u32[]{:S(2)}, u32[]{:S(2)}) collective-permute-start(f32[512,256]{1,0:T(8,128)S(1)} %get-tuple-element.41.direction_ref.values_ref), channel_id=1, source_target_pairs={{0,8},{2,10},{4,12},{6,14},{8,0},{10,2},{12,4},{14,6},{1,9},{3,11}... | collective-permute-start | bytes 1572872 | tf_op jit(solution)/shard_map/ppermute | solution.py:374
  9.1 22.0 %collective-permute-start.1 = (f32[2,128,256]{2,1,0:T(8,128)}, f32[2,128,256]{2,1,0:T(8,128)S(1)}, u32[]{:S(2)}, u32[]{:S(2)}) collective-permute-start(f32[2,128,256]{2,1,0:T(8,128)} %get-tuple-element.51), channel_id=1, source_target_pairs={{0,6},{2,4},{4,2},{6,0},{8,14},{10,12},{12,10},{14,8},{1,7},{3,5},... | collective-permute-start | bytes 786440 | tf_op jit(solution)/shard_map/ppermute | solution.py:374
  11.7 22.8 %collective-permute-start.2 = (f32[2,128,256]{2,1,0:T(8,128)}, f32[2,128,256]{2,1,0:T(8,128)}, u32[]{:S(2)}, u32[]{:S(2)}) collective-permute-start(f32[2,128,256]{2,1,0:T(8,128)} %get-tuple-element.52), channel_id=1, source_target_pairs={{0,4},{2,6},{4,0},{6,2},{8,12},{10,14},{12,8},{14,10},{1,5},{3,7},... | collective-permute-start | bytes 786440 | tf_op jit(solution)/shard_map/ppermute | solution.py:374
  12.2 22.4 %collective-permute-start.3 = (f32[2,128,256]{2,1,0:T(8,128)}, f32[2,128,256]{2,1,0:T(8,128)}, u32[]{:S(2)}, u32[]{:S(2)}) collective-permute-start(f32[2,128,256]{2,1,0:T(8,128)} %get-tuple-element.53), channel_id=1, source_target_pairs={{0,2},{2,0},{4,6},{6,4},{8,10},{10,8},{12,14},{14,12},{1,3},{3,1},... | collective-permute-start | bytes 786440 | tf_op jit(solution)/shard_map/ppermute | solution.py:374
  18.0 21.7 %collective-permute-start.8 = (f32[4,128,256]{2,1,0:T(8,128)S(1)}, f32[4,128,256]{2,1,0:T(8,128)S(1)}, u32[]{:S(2)}, u32[]{:S(2)}) collective-permute-start(f32[4,128,256]{2,1,0:T(8,128)S(1)} %get-tuple-element.56.refs_4_), channel_id=1, source_target_pairs={{0,2},{2,0},{4,6},{6,4},{8,10},{10,8},{12,14},{14,12},{1,3},{3,1},... | collective-permute-start | bytes 1572872 | tf_op jit(solution)/shard_map/ppermute | solution.py:374
  35.5 14.8 %copy-start = (bf16[4,128,512]{2,1,0:T(8,128)(2,1)S(1)}, bf16[4,128,512]{2,1,0:T(8,128)(2,1)}, u32[]{:S(2)}) copy-start(bf16[4,128,512]{2,1,0:T(8,128)(2,1)} %get-tuple-element.44.refs_5_.high_hbm) | copy-start | bytes 1572868
  35.5 14.8 %copy-start.1 = (bf16[4,128,512]{2,1,0:T(8,128)(2,1)S(1)}, bf16[4,128,512]{2,1,0:T(8,128)(2,1)}, u32[]{:S(2)}) copy-start(bf16[4,128,512]{2,1,0:T(8,128)(2,1)} %get-tuple-element.45.refs_6_.low_hbm) | copy-start | bytes 1572868
  35.5 14.8 %copy-start.5 = (f32[512,1]{1,0:T(8,128)S(1)}, f32[512,1]{1,0:T(8,128)}, u32[]{:S(2)}) copy-start(f32[512,1]{1,0:T(8,128)} %get-tuple-element.46.diagonal_hbm) | copy-start | bytes 6148
  36.1 10.3 %collective-permute-start.5 = (f32[2,128,256]{2,1,0:T(8,128)S(1)}, f32[2,128,256]{2,1,0:T(8,128)S(1)}, u32[]{:S(2)}, u32[]{:S(2)}) collective-permute-start(f32[2,128,256]{2,1,0:T(8,128)S(1)} %get-tuple-element.57), channel_id=1, source_target_pairs={{0,6},{2,4},{4,2},{6,0},{8,14},{10,12},{12,10},{14,8},{1,7},{3,5},... | collective-permute-start | bytes 786440 | tf_op jit(solution)/shard_map/ppermute | solution.py:374
  36.2 13.2 %collective-permute-start.6 = (f32[2,128,256]{2,1,0:T(8,128)S(1)}, f32[2,128,256]{2,1,0:T(8,128)S(1)}, u32[]{:S(2)}, u32[]{:S(2)}) collective-permute-start(f32[2,128,256]{2,1,0:T(8,128)S(1)} %get-tuple-element.58), channel_id=1, source_target_pairs={{0,4},{2,6},{4,0},{6,2},{8,12},{10,14},{12,8},{14,10},{1,5},{3,7},... | collective-permute-start | bytes 786440 | tf_op jit(solution)/shard_map/ppermute | solution.py:374
  38.2 12.0 %collective-permute-start.7 = (f32[2,128,256]{2,1,0:T(8,128)S(1)}, f32[2,128,256]{2,1,0:T(8,128)S(1)}, u32[]{:S(2)}, u32[]{:S(2)}) collective-permute-start(f32[2,128,256]{2,1,0:T(8,128)S(1)} %get-tuple-element.59), channel_id=1, source_target_pairs={{0,2},{2,0},{4,6},{6,4},{8,10},{10,8},{12,14},{14,12},{1,3},{3,1},... | collective-permute-start | bytes 786440 | tf_op jit(solution)/shard_map/ppermute | solution.py:374
  55.0 33.3 %all-to-all-start = ((f32[8,136,256]{2,1,0:T(8,128)}), f32[8,136,256]{2,1,0:T(8,128)S(1)}, u32[]{:S(2)}, u32[]{:S(2)}) async-start(f32[8,136,256]{2,1,0:T(8,128)} %get-tuple-element.62), calls=%async_computation | async-start | bytes 2228224 | tf_op jit(solution)/shard_map/all_to_all | solution.py:481
  60.9 31.3 %collective-permute-start.11 = (f32[4,128,256]{2,1,0:T(8,128)}, f32[4,128,256]{2,1,0:T(8,128)S(1)}, u32[]{:S(2)}, u32[]{:S(2)}) collective-permute-start(f32[4,128,256]{2,1,0:T(8,128)} %get-tuple-element.71), channel_id=1, source_target_pairs={{0,2},{2,0},{4,6},{6,4},{8,10},{10,8},{12,14},{14,12},{1,3},{3,1},... | collective-permute-start | bytes 1572872 | tf_op jit(solution)/shard_map/ppermute | solution.py:374
  63.0 29.4 %collective-permute-start.9 = (f32[2,128,256]{2,1,0:T(8,128)S(1)}, f32[2,128,256]{2,1,0:T(8,128)S(1)}, u32[]{:S(2)}, u32[]{:S(2)}) collective-permute-start(f32[2,128,256]{2,1,0:T(8,128)S(1)} %get-tuple-element.67), channel_id=1, source_target_pairs={{0,4},{2,6},{4,0},{6,2},{8,12},{10,14},{12,8},{14,10},{1,5},{3,7},... | collective-permute-start | bytes 786440 | tf_op jit(solution)/shard_map/ppermute | solution.py:374
  88.2 4.0 %copy-start.8 = (f32[4,128,256]{2,1,0:T(8,128)S(1)}, f32[4,128,256]{2,1,0:T(8,128)}, u32[]{:S(2)}) copy-start(f32[4,128,256]{2,1,0:T(8,128)} %get-tuple-element.70.kept_ref) | copy-start | bytes 1572868
  92.3 23.6 %copy-start.3 = (f32[512,256]{1,0:T(8,128)S(1)}, f32[512,256]{1,0:T(8,128)}, u32[]{:S(2)}) copy-start(f32[512,256]{1,0:T(8,128)} %get-tuple-element.40.direction_hbm.direction_ref) | copy-start | bytes 1572868
  92.3 23.5 %copy-start.4 = (f32[512,256]{1,0:T(8,128)S(1)}, f32[512,256]{1,0:T(8,128)}, u32[]{:S(2)}) copy-start(f32[512,256]{1,0:T(8,128)} %get-tuple-element.60.scaled_hbm.scaled_ref) | copy-start | bytes 1572868
  92.3 9.9 %collective-permute-start.12 = (f32[2,128,256]{2,1,0:T(8,128)S(1)}, f32[2,128,256]{2,1,0:T(8,128)S(1)}, u32[]{:S(2)}, u32[]{:S(2)}) collective-permute-start(f32[2,128,256]{2,1,0:T(8,128)S(1)} %get-tuple-element.73), channel_id=1, source_target_pairs={{0,4},{2,6},{4,0},{6,2},{8,12},{10,14},{12,8},{14,10},{1,5},{3,7},... | collective-permute-start | bytes 786440 | tf_op jit(solution)/shard_map/ppermute | solution.py:374
  92.5 15.5 %collective-permute-start.10 = (f32[1,128,256]{2,1,0:T(8,128)S(1)}, f32[1,128,256]{2,1,0:T(8,128)S(1)}, u32[]{:S(2)}, u32[]{:S(2)}) collective-permute-start(f32[1,128,256]{2,1,0:T(8,128)S(1)} %get-tuple-element.69), channel_id=1, source_target_pairs={{0,8},{2,10},{4,12},{6,14},{8,0},{10,2},{12,4},{14,6},{1,9},{3,11}... | collective-permute-start | bytes 393224 | tf_op jit(solution)/shard_map/ppermute | solution.py:374
  102.3 7.7 %collective-permute-start.13 = (f32[1,128,256]{2,1,0:T(8,128)S(1)}, f32[1,128,256]{2,1,0:T(8,128)S(1)}, u32[]{:S(2)}, u32[]{:S(2)}) collective-permute-start(f32[1,128,256]{2,1,0:T(8,128)S(1)} %get-tuple-element.75), channel_id=1, source_target_pairs={{0,8},{2,10},{4,12},{6,14},{8,0},{10,2},{12,4},{14,6},{1,9},{3,11}... | collective-permute-start | bytes 393224 | tf_op jit(solution)/shard_map/ppermute | solution.py:374
  103.2 12.7 %all-to-all-start.1 = ((f32[16,8,256]{2,1,0:T(8,128)}), f32[16,8,256]{2,1,0:T(8,128)S(1)}, u32[]{:S(2)}, u32[]{:S(2)}) async-start(f32[16,8,256]{2,1,0:T(8,128)} %shard_map.75.refs_0_), calls=%async_computation.1 | async-start | bytes 262144 | tf_op jit(solution)/shard_map/all_to_all | solution.py:495
  110.1 6.7 %collective-permute-start.14 = (f32[2,64,256]{2,1,0:T(8,128)S(1)}, f32[2,64,256]{2,1,0:T(8,128)S(1)}, u32[]{:S(2)}, u32[]{:S(2)}) collective-permute-start(f32[2,64,256]{2,1,0:T(8,128)S(1)} %get-tuple-element.77), channel_id=1, source_target_pairs={{0,1},{1,0},{2,3},{3,2},{4,5},{5,4},{6,7},{7,6},{8,9},{9,8},{10,11... | collective-permute-start | bytes 393224 | tf_op jit(solution)/shard_map/ppermute | solution.py:374
  (4 other events, 5.4 us)

commit v21 on v20

--- a/solution.py
+++ b/solution.py
@@ -482,19 +482,20 @@
     scaled_share = swap(scaled_odd, "samples", devices, 1)
     direction_kept, direction_given = add_step(direction_even, direction_share)
     direction_taken = swap(after(direction_given, scaled), "samples", devices, steps[0])
+    scaled_kept, scaled_given = add_step(scaled_even, scaled_share)
+    scaled_taken = swap(scaled_given, "samples", devices, steps[0])
     sums = call(
         functools.partial(curvature_kernel, devices),
         pltpu.HBM((2 * devices, SUBLANES, columns), jnp.float32),
-        [smem] + [hbm] * 6 + [anywhere],
+        [smem] + [hbm] * 6 + [anywhere] * 2,
         hbm,
         [
             room(2 * devices, SUBLANES, columns), tiles_room, tiles_room, full_room, room(people, 1), full_room,
             full_room, room(devices, tile + SUBLANES, columns), pltpu.SemaphoreType.DMA((8,)),
         ],
-    )(table, *at_home(high, low, direction_kept_hbm, diagonal, scaled, handled), later)
+    )(table, *at_home(high, low, direction_kept_hbm, diagonal, scaled, handled), later, scaled_given)
     all_sums = lax.all_to_all(sums, ("samples", "cols"), split_axis=0, concat_axis=0, tiled=True)
-    scaled_kept, scaled_taken = scaled_even, scaled_share
-    for step in steps:
+    for step in steps[1:]:
         scaled_kept, scaled_given = add_step(scaled_kept, scaled_taken, sums)
         scaled_taken = swap(scaled_given, "samples", devices, step)
     for step in steps[1:]:

time: 118 us -> 111 us (0.941)
  waiting for transfers between devices: 61.6 us -> 52.5 us
  starting transfers between devices: 30.3 us -> 33.6 us
  local copies, waits for them, and re-layouts: 5.79 us -> 4.13 us
    all_to_all x1, waiting for transfers between devices: 23.7 us -> 0.05 us  [per_device(): lax.all_to_all(outgoing, 'samples', split_axis=0, concat_axis=0, tiled=True)]
    ppermute x15, waiting for transfers between devices: 32.2 us -> 49.2 us  [swap(): return lax.ppermute(values, axis, [(i, i ^ step) for i in range(devices)])]
    ppermute x15, starting transfers between devices: 19.6 us -> 24 us  [swap(): return lax.ppermute(values, axis, [(i, i ^ step) for i in range(devices)])]
    all_to_all x1, waiting for transfers between devices: 5.71 us -> 3.27 us  [per_device(): lax.all_to_all(sums, ('samples', 'cols'), split_axis=0, concat_axis=0, ti...]
    unnamed x22 -> x18, local copies, waits for them, and re-layouts: 2.9 us -> 1.26 us
    all_to_all x1, starting transfers between devices: 4.74 us -> 3.51 us  [per_device(): lax.all_to_all(sums, ('samples', 'cols'), split_axis=0, concat_axis=0, ti...]
  transfers between devices with their start and end apart: 17 -> 17, of which waited for: 9 -> 9; matrix products, arithmetic and copies ran while one was open for 2% -> 3% of each run, Pallas kernels for 9% -> 11%
where the time goes in v21:
time: 111 us
  waiting for transfers between devices  52.5 us (47%)
  starting transfers between devices  33.6 us (30%)
  Pallas kernels  19.6 us (18%)
  local copies, waits for them, and re-layouts  4.13 us (4%)
    ppermute x15, waiting for transfers between devices, swap(): return lax.ppermute(values, axis, [(i, i ^ step) for i in range(devices)])  49.2 us
    ppermute x15, starting transfers between devices, swap(): return lax.ppermute(values, axis, [(i, i ^ step) for i in range(devices)])  24 us
    all_to_all x1, starting transfers between devices, per_device(): lax.all_to_all(outgoing, 'samples', split_axis=0, concat_axis=0, tiled=True)  6.09 us
    pallas_call x1, Pallas kernels, per_device(): call(functools.partial(apply_kernel, devices, capacity), [full_out, full_...  4.72 us
    pallas_call x1, Pallas kernels, per_device(): call(functools.partial(curvature_kernel, devices), pltpu.HBM((2 * devices...  3.98 us
    all_to_all x1, starting transfers between devices, per_device(): lax.all_to_all(sums, ('samples', 'cols'), split_axis=0, concat_axis=0, ti...  3.51 us
    all_to_all x1, waiting for transfers between devices, per_device(): lax.all_to_all(sums, ('samples', 'cols'), split_axis=0, concat_axis=0, ti...  3.27 us
    pallas_call x1, Pallas kernels, per_device(): call(direction_kernel, [full, full_out, pltpu.HBM((people, 1), jnp.float3...  2.45 us
  transfers between devices with their start and end apart: 17, of which 9 were waited for; matrix products, arithmetic and copies ran while one was open for 3% of the time, Pallas kernels for 11%

profile of v21, /device:TPU:0, one launch (start us, length us, event | category | flops | bytes accessed | tf_op | source)
XLA Modules:
  0.0 110.6 jit_solution(4621078642367558081)
XLA Ops:
  0.7 2.5 %shard_map.68 = (f32[512,256]{1,0:T(8,128)S(1)}, f32[512,256]{1,0:T(8,128)}, f32[512,1]{1,0:T(8,128)}, f32[8,256]{1,0:T(8,128)S(1)}) custom-call(f32[4,4,128,128]{3,2,1,0:T(8,128)} %kinship_hbm.3, f32[4,128]{1,0:T(4,128)} %bitcast.9, f32[512,256]{1,0:T(8,128)} %phenotypes_hbm.1), custom_call_target="tpu_custom_call" | custom-call | tf_op jit(solution)/shard_map/pallas_call | solution.py:405
  3.6 3.7 %collective-permute-start.4 = (f32[512,256]{1,0:T(8,128)S(1)}, f32[512,256]{1,0:T(8,128)S(1)}, u32[]{:S(2)}, u32[]{:S(2)}) collective-permute-start(f32[512,256]{1,0:T(8,128)S(1)} %get-tuple-element.41.direction_ref.values_ref), channel_id=1, source_target_pairs={{0,8},{2,10},{4,12},{6,14},{8,0},{10,2},{12,4},{14,6},{1,9},{3,11}... | collective-permute-start | bytes 1572872 | tf_op jit(solution)/shard_map/ppermute | solution.py:374
  7.3 1.8 %shard_map.69 = (s32[4,12]{1,0:T(4,128)S(1)}, s32[2,4]{1,0:T(2,128)S(1)}, f32[2,128,256]{2,1,0:T(8,128)}, f32[2,128,256]{2,1,0:T(8,128)}, f32[2,128,256]{2,1,0:T(8,128)}) custom-call(s32[3,32]{1,0:T(4,128)S(1)} %bitcast.8, f32[512,256]{1,0:T(8,128)S(1)} %get-tuple-element.41.direction_ref.values_ref, f32[512,512]{1,0:T(8,128)S(1)} %collective-permute-done.gate_ref), custom_call_target="tpu_custom_call" | custom-call | tf_op jit(solution)/shard_map/pallas_call | solution.py:424
  9.1 2.6 %collective-permute-start.1 = (f32[2,128,256]{2,1,0:T(8,128)}, f32[2,128,256]{2,1,0:T(8,128)S(1)}, u32[]{:S(2)}, u32[]{:S(2)}) collective-permute-start(f32[2,128,256]{2,1,0:T(8,128)} %get-tuple-element.51), channel_id=1, source_target_pairs={{0,6},{2,4},{4,2},{6,0},{8,14},{10,12},{12,10},{14,8},{1,7},{3,5},... | collective-permute-start | bytes 786440 | tf_op jit(solution)/shard_map/ppermute | solution.py:374
  12.7 1.6 %copy.7 = f32[512,512]{0,1:T(8,128)S(1)} copy(f32[512,512]{1,0:T(8,128)} %param.9) | data formatting | bytes 2097152 | tf_op jit(solution)/shard_map/optimization_barrier | solution.py:378
  18.0 1.6 %collective-permute-start.8 = (f32[4,128,256]{2,1,0:T(8,128)S(1)}, f32[4,128,256]{2,1,0:T(8,128)S(1)}, u32[]{:S(2)}, u32[]{:S(2)}) collective-permute-start(f32[4,128,256]{2,1,0:T(8,128)S(1)} %get-tuple-element.56.refs_4_), channel_id=1, source_target_pairs={{0,2},{2,0},{4,6},{6,4},{8,10},{10,8},{12,14},{14,12},{1,3},{3,1},... | collective-permute-start | bytes 1572872 | tf_op jit(solution)/shard_map/ppermute | solution.py:374
  19.6 2.3 %shard_map.70 = (bf16[4,128,512]{2,1,0:T(8,128)(2,1)}, bf16[4,128,512]{2,1,0:T(8,128)(2,1)}) custom-call(f32[4,4,128,128]{3,2,1,0:T(8,128)} %kinship_hbm.3), custom_call_target="tpu_custom_call" | custom-call | tf_op jit(solution)/shard_map/pallas_call | solution.py:434
  21.9 9.2 %collective-permute-done.4.partner_ref = f32[512,256]{1,0:T(8,128)S(1)} collective-permute-done((f32[512,256]{1,0:T(8,128)S(1)}, f32[512,256]{1,0:T(8,128)S(1)}, u32[]{:S(2)}, u32[]{:S(2)}) %collective-permute-start.4) | collective-permute-done | bytes 524320 | tf_op jit(solution)/shard_map/ppermute | solution.py:374
  31.2 3.4 %collective-permute-done.2.refs_1_ = f32[2,128,256]{2,1,0:T(8,128)} collective-permute-done((f32[2,128,256]{2,1,0:T(8,128)}, f32[2,128,256]{2,1,0:T(8,128)}, u32[]{:S(2)}, u32[]{:S(2)}) %collective-permute-start.2) | collective-permute-done | bytes 262176 | tf_op jit(solution)/shard_map/ppermute | solution.py:374
  35.3 2.0 %collective-permute-start.6 = (f32[2,128,256]{2,1,0:T(8,128)S(1)}, f32[2,128,256]{2,1,0:T(8,128)S(1)}, u32[]{:S(2)}, u32[]{:S(2)}) collective-permute-start(f32[2,128,256]{2,1,0:T(8,128)S(1)} %get-tuple-element.58), channel_id=1, source_target_pairs={{0,4},{2,6},{4,0},{6,2},{8,12},{10,14},{12,8},{14,10},{1,5},{3,7},... | collective-permute-start | bytes 786440 | tf_op jit(solution)/shard_map/ppermute | solution.py:374
  38.8 6.7 %collective-permute-done.5.refs_3_ = f32[2,128,256]{2,1,0:T(8,128)S(1)} collective-permute-done((f32[2,128,256]{2,1,0:T(8,128)S(1)}, f32[2,128,256]{2,1,0:T(8,128)S(1)}, u32[]{:S(2)}, u32[]{:S(2)}) %collective-permute-start.5) | collective-permute-done | bytes 262176 | tf_op jit(solution)/shard_map/ppermute | solution.py:374
  45.5 3.0 %collective-permute-done.6.refs_4_ = f32[2,128,256]{2,1,0:T(8,128)S(1)} collective-permute-done((f32[2,128,256]{2,1,0:T(8,128)S(1)}, f32[2,128,256]{2,1,0:T(8,128)S(1)}, u32[]{:S(2)}, u32[]{:S(2)}) %collective-permute-start.6) | collective-permute-done | bytes 262176 | tf_op jit(solution)/shard_map/ppermute | solution.py:374
  49.3 4.7 %shard_map.74 = (f32[512,256]{1,0:T(8,128)}, f32[512,256]{1,0:T(8,128)}, f32[8,136,256]{2,1,0:T(8,128)}, f32[4,128,256]{2,1,0:T(8,128)}, f32[4,128,256]{2,1,0:T(8,128)}) custom-call(s32[4,12]{1,0:T(4,128)S(1)} %get-tuple-element.43.table_ref, bf16[4,128,512]{2,1,0:T(8,128)(2,1)S(1)} %copy-done, bf16[4,128,512]{2,1,0:T(8,128)(2,1)S(1)} %copy-done.1, ...), custom_call_target="tpu_custom_call" | custom-call | tf_op jit(solution)/shard_map/pallas_call | solution.py:467
  54.1 6.1 %all-to-all-start = ((f32[8,136,256]{2,1,0:T(8,128)}), f32[8,136,256]{2,1,0:T(8,128)S(1)}, u32[]{:S(2)}, u32[]{:S(2)}) async-start(f32[8,136,256]{2,1,0:T(8,128)} %get-tuple-element.62), calls=%async_computation | async-start | bytes 2228224 | tf_op jit(solution)/shard_map/all_to_all | solution.py:481
  60.2 2.0 %collective-permute-start.9 = (f32[4,128,256]{2,1,0:T(8,128)}, f32[4,128,256]{2,1,0:T(8,128)S(1)}, u32[]{:S(2)}, u32[]{:S(2)}) collective-permute-start(f32[4,128,256]{2,1,0:T(8,128)} %get-tuple-element.64), channel_id=1, source_target_pairs={{0,2},{2,0},{4,6},{6,4},{8,10},{10,8},{12,14},{14,12},{1,3},{3,1},... | collective-permute-start | bytes 1572872 | tf_op jit(solution)/shard_map/ppermute | solution.py:374
  64.4 21.4 %collective-permute-done.9.taken_ref = f32[4,128,256]{2,1,0:T(8,128)S(1)} collective-permute-done((f32[4,128,256]{2,1,0:T(8,128)}, f32[4,128,256]{2,1,0:T(8,128)S(1)}, u32[]{:S(2)}, u32[]{:S(2)}) %collective-permute-start.9) | collective-permute-done | bytes 524320 | tf_op jit(solution)/shard_map/ppermute | solution.py:374
  85.9 1.5 %collective-permute-start.12 = (f32[2,128,256]{2,1,0:T(8,128)S(1)}, f32[2,128,256]{2,1,0:T(8,128)S(1)}, u32[]{:S(2)}, u32[]{:S(2)}) collective-permute-start(f32[2,128,256]{2,1,0:T(8,128)S(1)} %get-tuple-element.65.refs_0_), channel_id=1, source_target_pairs={{0,4},{2,6},{4,0},{6,2},{8,12},{10,14},{12,8},{14,10},{1,5},{3,7},... | collective-permute-start | bytes 786440 | tf_op jit(solution)/shard_map/ppermute | solution.py:374
  87.5 4.0 %shard_map.76.refs_0_ = f32[16,8,256]{2,1,0:T(8,128)} custom-call(s32[4,12]{1,0:T(4,128)S(1)} %get-tuple-element.43.table_ref, bf16[4,128,512]{2,1,0:T(8,128)(2,1)} %get-tuple-element.44.refs_5_.high_hbm, bf16[4,128,512]{2,1,0:T(8,128)(2,1)} %get-tuple-element.45.refs_6_.low_hbm, f32[512,256]{1,0:T(8,128)} %get-tuple-element.40.direction_hbm.direction_ref, ...), custom_call_target="tpu_custom_call" | custom-call | tf_op jit(solution)/shard_map/pallas_call | solution.py:487
  91.5 2.4 %collective-permute-start.11 = (f32[1,128,256]{2,1,0:T(8,128)S(1)}, f32[1,128,256]{2,1,0:T(8,128)S(1)}, u32[]{:S(2)}, u32[]{:S(2)}) collective-permute-start(f32[1,128,256]{2,1,0:T(8,128)S(1)} %get-tuple-element.72), channel_id=1, source_target_pairs={{0,8},{2,10},{4,12},{6,14},{8,0},{10,2},{12,4},{14,6},{1,9},{3,11}... | collective-permute-start | bytes 393224 | tf_op jit(solution)/shard_map/ppermute | solution.py:374
  94.0 3.6 %collective-permute-start.13 = (f32[1,128,256]{2,1,0:T(8,128)S(1)}, f32[1,128,256]{2,1,0:T(8,128)S(1)}, u32[]{:S(2)}, u32[]{:S(2)}) collective-permute-start(f32[1,128,256]{2,1,0:T(8,128)S(1)} %get-tuple-element.75), channel_id=1, source_target_pairs={{0,8},{2,10},{4,12},{6,14},{8,0},{10,2},{12,4},{14,6},{1,9},{3,11}... | collective-permute-start | bytes 393224 | tf_op jit(solution)/shard_map/ppermute | solution.py:374
  97.6 3.5 %all-to-all-start.1 = ((f32[16,8,256]{2,1,0:T(8,128)}), f32[16,8,256]{2,1,0:T(8,128)S(1)}, u32[]{:S(2)}, u32[]{:S(2)}) async-start(f32[16,8,256]{2,1,0:T(8,128)} %shard_map.76.refs_0_), calls=%async_computation.1 | async-start | bytes 262144 | tf_op jit(solution)/shard_map/all_to_all | solution.py:497
  101.1 2.6 %collective-permute-done.11.first_taken_ref = f32[1,128,256]{2,1,0:T(8,128)S(1)} collective-permute-done((f32[1,128,256]{2,1,0:T(8,128)S(1)}, f32[1,128,256]{2,1,0:T(8,128)S(1)}, u32[]{:S(2)}, u32[]{:S(2)}) %collective-permute-start.11) | collective-permute-done | bytes 131104 | tf_op jit(solution)/shard_map/ppermute | solution.py:374
  103.7 2.0 %collective-permute-done.13.second_taken_ref = f32[1,128,256]{2,1,0:T(8,128)S(1)} collective-permute-done((f32[1,128,256]{2,1,0:T(8,128)S(1)}, f32[1,128,256]{2,1,0:T(8,128)S(1)}, u32[]{:S(2)}, u32[]{:S(2)}) %collective-permute-start.13) | collective-permute-done | bytes 131104 | tf_op jit(solution)/shard_map/ppermute | solution.py:374
  105.8 3.3 %all-to-all-done.1.sums_ref = f32[16,8,256]{2,1,0:T(8,128)S(1)} async-done(((f32[16,8,256]{2,1,0:T(8,128)}), f32[16,8,256]{2,1,0:T(8,128)S(1)}, u32[]{:S(2)}, u32[]{:S(2)}) %all-to-all-start.1) | async-done | bytes 131104 | tf_op jit(solution)/shard_map/all_to_all | solution.py:497
  (45 shorter events, 12.3 us)
Async XLA Ops:
  0.6 6.7 %copy-start.7 = (s32[32,3]{0,1:T(4,128)S(1)}, s32[32,3]{0,1:T(4,128)}, u32[]{:S(2)}) copy-start(s32[32,3]{0,1:T(4,128)} %param.6) | copy-start | bytes 1156
  3.1 4.2 %collective-permute-start = (f32[512,512]{1,0:T(8,128)S(1)}, f32[512,512]{1,0:T(8,128)S(1)}, u32[]{:S(2)}, u32[]{:S(2)}) collective-permute-start(f32[512,512]{1,0:T(8,128)S(1)} %copy-done.8), channel_id=1, source_target_pairs={{0,1},{1,0},{2,3},{3,2},{4,5},{5,4},{6,7},{7,6},{8,9},{9,8},{10,11... | collective-permute-start | bytes 3145736 | tf_op jit(solution)/shard_map/ppermute | solution.py:374
  3.6 27.5 %collective-permute-start.4 = (f32[512,256]{1,0:T(8,128)S(1)}, f32[512,256]{1,0:T(8,128)S(1)}, u32[]{:S(2)}, u32[]{:S(2)}) collective-permute-start(f32[512,256]{1,0:T(8,128)S(1)} %get-tuple-element.41.direction_ref.values_ref), channel_id=1, source_target_pairs={{0,8},{2,10},{4,12},{6,14},{8,0},{10,2},{12,4},{14,6},{1,9},{3,11}... | collective-permute-start | bytes 1572872 | tf_op jit(solution)/shard_map/ppermute | solution.py:374
  9.1 22.0 %collective-permute-start.1 = (f32[2,128,256]{2,1,0:T(8,128)}, f32[2,128,256]{2,1,0:T(8,128)S(1)}, u32[]{:S(2)}, u32[]{:S(2)}) collective-permute-start(f32[2,128,256]{2,1,0:T(8,128)} %get-tuple-element.51), channel_id=1, source_target_pairs={{0,6},{2,4},{4,2},{6,0},{8,14},{10,12},{12,10},{14,8},{1,7},{3,5},... | collective-permute-start | bytes 786440 | tf_op jit(solution)/shard_map/ppermute | solution.py:374
  11.7 22.8 %collective-permute-start.2 = (f32[2,128,256]{2,1,0:T(8,128)}, f32[2,128,256]{2,1,0:T(8,128)}, u32[]{:S(2)}, u32[]{:S(2)}) collective-permute-start(f32[2,128,256]{2,1,0:T(8,128)} %get-tuple-element.52), channel_id=1, source_target_pairs={{0,4},{2,6},{4,0},{6,2},{8,12},{10,14},{12,8},{14,10},{1,5},{3,7},... | collective-permute-start | bytes 786440 | tf_op jit(solution)/shard_map/ppermute | solution.py:374
  12.2 22.4 %collective-permute-start.3 = (f32[2,128,256]{2,1,0:T(8,128)}, f32[2,128,256]{2,1,0:T(8,128)}, u32[]{:S(2)}, u32[]{:S(2)}) collective-permute-start(f32[2,128,256]{2,1,0:T(8,128)} %get-tuple-element.53), channel_id=1, source_target_pairs={{0,2},{2,0},{4,6},{6,4},{8,10},{10,8},{12,14},{14,12},{1,3},{3,1},... | collective-permute-start | bytes 786440 | tf_op jit(solution)/shard_map/ppermute | solution.py:374
  18.0 20.7 %collective-permute-start.8 = (f32[4,128,256]{2,1,0:T(8,128)S(1)}, f32[4,128,256]{2,1,0:T(8,128)S(1)}, u32[]{:S(2)}, u32[]{:S(2)}) collective-permute-start(f32[4,128,256]{2,1,0:T(8,128)S(1)} %get-tuple-element.56.refs_4_), channel_id=1, source_target_pairs={{0,2},{2,0},{4,6},{6,4},{8,10},{10,8},{12,14},{14,12},{1,3},{3,1},... | collective-permute-start | bytes 1572872 | tf_op jit(solution)/shard_map/ppermute | solution.py:374
  34.6 14.8 %copy-start = (bf16[4,128,512]{2,1,0:T(8,128)(2,1)S(1)}, bf16[4,128,512]{2,1,0:T(8,128)(2,1)}, u32[]{:S(2)}) copy-start(bf16[4,128,512]{2,1,0:T(8,128)(2,1)} %get-tuple-element.44.refs_5_.high_hbm) | copy-start | bytes 1572868
  34.6 14.8 %copy-start.1 = (bf16[4,128,512]{2,1,0:T(8,128)(2,1)S(1)}, bf16[4,128,512]{2,1,0:T(8,128)(2,1)}, u32[]{:S(2)}) copy-start(bf16[4,128,512]{2,1,0:T(8,128)(2,1)} %get-tuple-element.45.refs_6_.low_hbm) | copy-start | bytes 1572868
  34.6 14.8 %copy-start.5 = (f32[512,1]{1,0:T(8,128)S(1)}, f32[512,1]{1,0:T(8,128)}, u32[]{:S(2)}) copy-start(f32[512,1]{1,0:T(8,128)} %get-tuple-element.46.diagonal_hbm) | copy-start | bytes 6148
  35.2 10.3 %collective-permute-start.5 = (f32[2,128,256]{2,1,0:T(8,128)S(1)}, f32[2,128,256]{2,1,0:T(8,128)S(1)}, u32[]{:S(2)}, u32[]{:S(2)}) collective-permute-start(f32[2,128,256]{2,1,0:T(8,128)S(1)} %get-tuple-element.57), channel_id=1, source_target_pairs={{0,6},{2,4},{4,2},{6,0},{8,14},{10,12},{12,10},{14,8},{1,7},{3,5},... | collective-permute-start | bytes 786440 | tf_op jit(solution)/shard_map/ppermute | solution.py:374
  35.3 13.2 %collective-permute-start.6 = (f32[2,128,256]{2,1,0:T(8,128)S(1)}, f32[2,128,256]{2,1,0:T(8,128)S(1)}, u32[]{:S(2)}, u32[]{:S(2)}) collective-permute-start(f32[2,128,256]{2,1,0:T(8,128)S(1)} %get-tuple-element.58), channel_id=1, source_target_pairs={{0,4},{2,6},{4,0},{6,2},{8,12},{10,14},{12,8},{14,10},{1,5},{3,7},... | collective-permute-start | bytes 786440 | tf_op jit(solution)/shard_map/ppermute | solution.py:374
  37.3 12.0 %collective-permute-start.7 = (f32[2,128,256]{2,1,0:T(8,128)S(1)}, f32[2,128,256]{2,1,0:T(8,128)S(1)}, u32[]{:S(2)}, u32[]{:S(2)}) collective-permute-start(f32[2,128,256]{2,1,0:T(8,128)S(1)} %get-tuple-element.59), channel_id=1, source_target_pairs={{0,2},{2,0},{4,6},{6,4},{8,10},{10,8},{12,14},{14,12},{1,3},{3,1},... | collective-permute-start | bytes 786440 | tf_op jit(solution)/shard_map/ppermute | solution.py:374
  54.1 31.8 %copy-start.6 = (f32[4,128,256]{2,1,0:T(8,128)S(1)}, f32[4,128,256]{2,1,0:T(8,128)}, u32[]{:S(2)}) copy-start(f32[4,128,256]{2,1,0:T(8,128)} %get-tuple-element.63.kept_ref) | copy-start | bytes 1572868
  54.1 33.4 %all-to-all-start = ((f32[8,136,256]{2,1,0:T(8,128)}), f32[8,136,256]{2,1,0:T(8,128)S(1)}, u32[]{:S(2)}, u32[]{:S(2)}) async-start(f32[8,136,256]{2,1,0:T(8,128)} %get-tuple-element.62), calls=%async_computation | async-start | bytes 2228224 | tf_op jit(solution)/shard_map/all_to_all | solution.py:481
  60.2 25.7 %collective-permute-start.9 = (f32[4,128,256]{2,1,0:T(8,128)}, f32[4,128,256]{2,1,0:T(8,128)S(1)}, u32[]{:S(2)}, u32[]{:S(2)}) collective-permute-start(f32[4,128,256]{2,1,0:T(8,128)} %get-tuple-element.64), channel_id=1, source_target_pairs={{0,2},{2,0},{4,6},{6,4},{8,10},{10,8},{12,14},{14,12},{1,3},{3,1},... | collective-permute-start | bytes 1572872 | tf_op jit(solution)/shard_map/ppermute | solution.py:374
  62.9 28.6 %collective-permute-start.10 = (f32[2,128,256]{2,1,0:T(8,128)}, f32[2,128,256]{2,1,0:T(8,128)S(1)}, u32[]{:S(2)}, u32[]{:S(2)}) collective-permute-start(f32[2,128,256]{2,1,0:T(8,128)} %get-tuple-element.70), channel_id=1, source_target_pairs={{0,4},{2,6},{4,0},{6,2},{8,12},{10,14},{12,8},{14,10},{1,5},{3,7},... | collective-permute-start | bytes 786440 | tf_op jit(solution)/shard_map/ppermute | solution.py:374
  85.9 8.0 %collective-permute-start.12 = (f32[2,128,256]{2,1,0:T(8,128)S(1)}, f32[2,128,256]{2,1,0:T(8,128)S(1)}, u32[]{:S(2)}, u32[]{:S(2)}) collective-permute-start(f32[2,128,256]{2,1,0:T(8,128)S(1)} %get-tuple-element.65.refs_0_), channel_id=1, source_target_pairs={{0,4},{2,6},{4,0},{6,2},{8,12},{10,14},{12,8},{14,10},{1,5},{3,7},... | collective-permute-start | bytes 786440 | tf_op jit(solution)/shard_map/ppermute | solution.py:374
  91.5 17.6 %copy-start.3 = (f32[512,256]{1,0:T(8,128)S(1)}, f32[512,256]{1,0:T(8,128)}, u32[]{:S(2)}) copy-start(f32[512,256]{1,0:T(8,128)} %get-tuple-element.40.direction_hbm.direction_ref) | copy-start | bytes 1572868
  91.5 17.6 %copy-start.4 = (f32[512,256]{1,0:T(8,128)S(1)}, f32[512,256]{1,0:T(8,128)}, u32[]{:S(2)}) copy-start(f32[512,256]{1,0:T(8,128)} %get-tuple-element.60.scaled_hbm.scaled_ref) | copy-start | bytes 1572868
  91.5 12.1 %collective-permute-start.11 = (f32[1,128,256]{2,1,0:T(8,128)S(1)}, f32[1,128,256]{2,1,0:T(8,128)S(1)}, u32[]{:S(2)}, u32[]{:S(2)}) collective-permute-start(f32[1,128,256]{2,1,0:T(8,128)S(1)} %get-tuple-element.72), channel_id=1, source_target_pairs={{0,8},{2,10},{4,12},{6,14},{8,0},{10,2},{12,4},{14,6},{1,9},{3,11}... | collective-permute-start | bytes 393224 | tf_op jit(solution)/shard_map/ppermute | solution.py:374
  94.0 11.7 %collective-permute-start.13 = (f32[1,128,256]{2,1,0:T(8,128)S(1)}, f32[1,128,256]{2,1,0:T(8,128)S(1)}, u32[]{:S(2)}, u32[]{:S(2)}) collective-permute-start(f32[1,128,256]{2,1,0:T(8,128)S(1)} %get-tuple-element.75), channel_id=1, source_target_pairs={{0,8},{2,10},{4,12},{6,14},{8,0},{10,2},{12,4},{14,6},{1,9},{3,11}... | collective-permute-start | bytes 393224 | tf_op jit(solution)/shard_map/ppermute | solution.py:374
  97.6 11.4 %all-to-all-start.1 = ((f32[16,8,256]{2,1,0:T(8,128)}), f32[16,8,256]{2,1,0:T(8,128)S(1)}, u32[]{:S(2)}, u32[]{:S(2)}) async-start(f32[16,8,256]{2,1,0:T(8,128)} %shard_map.76.refs_0_), calls=%async_computation.1 | async-start | bytes 262144 | tf_op jit(solution)/shard_map/all_to_all | solution.py:497
  105.7 4.2 %collective-permute-start.14 = (f32[2,64,256]{2,1,0:T(8,128)S(1)}, f32[2,64,256]{2,1,0:T(8,128)S(1)}, u32[]{:S(2)}, u32[]{:S(2)}) collective-permute-start(f32[2,64,256]{2,1,0:T(8,128)S(1)} %get-tuple-element.77), channel_id=1, source_target_pairs={{0,1},{1,0},{2,3},{3,2},{4,5},{5,4},{6,7},{7,6},{8,9},{9,8},{10,11... | collective-permute-start | bytes 393224 | tf_op jit(solution)/shard_map/ppermute | solution.py:374
  (2 other events, 3.7 us)

commit v22 on v21

--- a/solution.py
+++ b/solution.py
@@ -210,17 +210,13 @@
     score_products(high_ref, low_ref, values_ref[...], even_ref, odd_ref)
 
 
-def apply_kernel(devices, capacity, table_ref, high_hbm, low_hbm, diagonal_hbm, direction_ref, norm_ref, dosage_high_ref,
+def apply_kernel(devices, capacity, table_ref, high_ref, low_ref, diagonal_ref, direction_ref, norm_ref, dosage_high_ref,
                  dosage_low_ref, *refs):
     received_refs = refs[:devices - 1]
-    (scaled_hbm, handled_hbm, outgoing_hbm, even_hbm, odd_hbm, gathered_ref, high_ref, low_ref, diagonal_ref, scaled_ref,
-     handled_ref, sums_ref, even_ref, odd_ref, semaphores) = refs[-15:]
+    (scaled_hbm, handled_hbm, outgoing_hbm, even_hbm, odd_hbm, gathered_ref, scaled_ref, handled_ref, sums_ref, even_ref,
+     odd_ref, semaphores) = refs[-12:]
     copies = Copies(semaphores)
-    loads = [
-        copies.start(high_hbm, high_ref), copies.start(low_hbm, low_ref), copies.start(diagonal_hbm, diagonal_ref)
-    ]
     gather_received(devices, capacity, received_refs, gathered_ref)
-    wait_all(loads)
     block_count, tile, depth = high_ref.shape
     others = depth // tile - 1
     cross = jnp.zeros(norm_ref.shape, jnp.float32)
@@ -251,16 +247,12 @@
     wait_all(stores)
 
 
-def curvature_kernel(devices, table_ref, high_hbm, low_hbm, direction_hbm, diagonal_hbm, scaled_hbm, handled_hbm,
-                     later_hbm, *refs):
-    (sums_hbm, sums_ref, high_ref, low_ref, direction_ref, diagonal_ref, scaled_ref, handled_ref, later_ref,
-     semaphores) = refs[-10:]
+def curvature_kernel(devices, table_ref, high_ref, low_ref, direction_ref, diagonal_ref, scaled_ref, handled_hbm,
+                     later_ref, *refs):
+    sums_hbm, sums_ref, handled_ref, semaphores = refs[-4:]
     block_count, tile, depth = high_ref.shape
     copies = Copies(semaphores)
-    wait_all([copies.start(source, target) for source, target in (
-        (later_hbm, later_ref), (scaled_hbm, scaled_ref), (direction_hbm, direction_ref), (high_hbm, high_ref),
-        (low_hbm, low_ref), (handled_hbm, handled_ref), (diagonal_hbm, diagonal_ref),
-    )])
+    load = copies.start(handled_hbm, handled_ref)
     others = depth // tile - 1
     first_sums = later_ref[0, pl.ds(tile, SUBLANES), :]
     for other in range(1, devices):
@@ -276,7 +268,10 @@
             entry = row * others + i
             weight = table_ref[2, entry].astype(jnp.float32)
             blocks.append(weight * later_ref[table_ref[1, entry], pl.ds(0, tile), :])
-        mapped = product(high_ref[row], low_ref[row], blocks) - rho * handled_ref[block, :]
+        mapped = product(high_ref[row], low_ref[row], blocks)
+        if row == 0:
+            load.wait()
+        mapped = mapped - rho * handled_ref[block, :]
         norm = norm + column_sums(here * here * diagonal_ref[block, :])
         bend = bend + column_sums(here * mapped)
     row_ids = lax.broadcasted_iota(jnp.int32, first_sums.shape, 0)
@@ -469,12 +464,11 @@
         [
             full_out, full_out, pltpu.HBM((devices, tile + SUBLANES, columns), jnp.float32), products_out, products_out,
         ],
-        [smem, hbm, hbm, hbm] + [vmem] * (devices + 3) + [anywhere],
+        [smem] + [vmem] * (devices + 6) + [anywhere],
         [hbm] * 5,
         [
-            room(devices * capacity + block_count, tile, columns), tiles_room, tiles_room, room(people, 1), full_room,
-            full_room, room(SUBLANES, columns), room(*products.shape), room(*products.shape),
-            pltpu.SemaphoreType.DMA((2 * devices + 7,)),
+            room(devices * capacity + block_count, tile, columns), full_room, full_room, room(SUBLANES, columns), room(*products.shape), room(*products.shape),
+            pltpu.SemaphoreType.DMA((2 * devices + 4,)),
         ],
         limit=large,
     )(table, high, low, diagonal, direction, norm, *grouped, *received, direction_share)
@@ -487,13 +481,10 @@
     sums = call(
         functools.partial(curvature_kernel, devices),
         pltpu.HBM((2 * devices, SUBLANES, columns), jnp.float32),
-        [smem] + [hbm] * 6 + [anywhere] * 2,
+        [smem] + [vmem] * 5 + [hbm, vmem, anywhere],
         hbm,
-        [
-            room(2 * devices, SUBLANES, columns), tiles_room, tiles_room, full_room, room(people, 1), full_room,
-            full_room, room(devices, tile + SUBLANES, columns), pltpu.SemaphoreType.DMA((8,)),
-        ],
-    )(table, *at_home(high, low, direction_kept_hbm, diagonal, scaled, handled), later, scaled_given)
+        [room(2 * devices, SUBLANES, columns), full_room, pltpu.SemaphoreType.DMA((2,))],
+    )(table, high, low, direction_kept_hbm, diagonal, scaled, *at_home(handled), later, scaled_given)
     all_sums = lax.all_to_all(sums, ("samples", "cols"), split_axis=0, concat_axis=0, tiled=True)
     for step in steps[1:]:
         scaled_kept, scaled_given = add_step(scaled_kept, scaled_taken, sums)

time: 111 us -> 114 us (1.027)
  Pallas kernels: 19.6 us -> 21.3 us
  local copies, waits for them, and re-layouts: 4.13 us -> 5.56 us
    pallas_call x4, Pallas kernels: 0.9 us -> 3.49 us  [add_step(): call(add_kernel, [rows] * 2, [vmem] * 2 + [hbm] * len(gates), [vmem] * 2)]
    ppermute x15, waiting for transfers between devices: 49.2 us -> 47.1 us  [swap(): return lax.ppermute(values, axis, [(i, i ^ step) for i in range(devices)])]
    unnamed x18 -> x36, local copies, waits for them, and re-layouts: 1.26 us -> 2.67 us
    all_to_all x1, waiting for transfers between devices: 3.27 us -> 4.57 us  [per_device(): lax.all_to_all(sums, ('samples', 'cols'), split_axis=0, concat_axis=0, ti...]
  transfers between devices with their start and end apart: 17 -> 17, of which waited for: 9 -> 9; matrix products, arithmetic and copies ran while one was open for 3% -> 3% of each run, Pallas kernels for 11% -> 12%
where the time goes in v22:
time: 114 us; the launch traced here: 113 us
  waiting for transfers between devices  51.7 us (45%)
  starting transfers between devices  33.8 us (30%)
  Pallas kernels  21.3 us (19%)
  local copies, waits for them, and re-layouts  5.56 us (5%)
    ppermute x15, waiting for transfers between devices, swap(): return lax.ppermute(values, axis, [(i, i ^ step) for i in range(devices)])  47.1 us
    ppermute x15, starting transfers between devices, swap(): return lax.ppermute(values, axis, [(i, i ^ step) for i in range(devices)])  24.2 us
    all_to_all x1, starting transfers between devices, per_device(): lax.all_to_all(outgoing, 'samples', split_axis=0, concat_axis=0, tiled=True)  6.09 us
    pallas_call x1, Pallas kernels, per_device(): call(functools.partial(apply_kernel, devices, capacity), [full_out, full_...  4.72 us
    all_to_all x1, waiting for transfers between devices, per_device(): lax.all_to_all(sums, ('samples', 'cols'), split_axis=0, concat_axis=0, ti...  4.57 us
    all_to_all x1, starting transfers between devices, per_device(): lax.all_to_all(sums, ('samples', 'cols'), split_axis=0, concat_axis=0, ti...  3.51 us
    pallas_call x4, Pallas kernels, add_step(): call(add_kernel, [rows] * 2, [vmem] * 2 + [hbm] * len(gates), [vmem] * 2)  3.49 us
    pallas_call x1, Pallas kernels, per_device(): call(functools.partial(curvature_kernel, devices), pltpu.HBM((2 * devices...  3.04 us
  transfers between devices with their start and end apart: 17, of which 9 were waited for; matrix products, arithmetic and copies ran while one was open for 3% of the time, Pallas kernels for 12%

profile of v22, /device:TPU:0, one launch (start us, length us, event | category | flops | bytes accessed | tf_op | source)
XLA Modules:
  0.0 113.2 jit_solution(15712683570508328416)
XLA Ops:
  0.7 2.4 %shard_map.68 = (f32[512,256]{1,0:T(8,128)S(1)}, f32[512,256]{1,0:T(8,128)}, f32[512,1]{1,0:T(8,128)}, f32[8,256]{1,0:T(8,128)S(1)}) custom-call(f32[4,4,128,128]{3,2,1,0:T(8,128)} %kinship_hbm.3, f32[4,128]{1,0:T(4,128)} %bitcast.9, f32[512,256]{1,0:T(8,128)} %phenotypes_hbm.1), custom_call_target="tpu_custom_call" | custom-call | tf_op jit(solution)/shard_map/pallas_call | solution.py:400
  3.6 3.7 %collective-permute-start.4 = (f32[512,256]{1,0:T(8,128)S(1)}, f32[512,256]{1,0:T(8,128)S(1)}, u32[]{:S(2)}, u32[]{:S(2)}) collective-permute-start(f32[512,256]{1,0:T(8,128)S(1)} %get-tuple-element.41.direction_ref.values_ref), channel_id=1, source_target_pairs={{0,8},{2,10},{4,12},{6,14},{8,0},{10,2},{12,4},{14,6},{1,9},{3,11}... | collective-permute-start | bytes 1572872 | tf_op jit(solution)/shard_map/ppermute | solution.py:369
  7.3 1.9 %shard_map.69 = (s32[4,12]{1,0:T(4,128)S(1)}, s32[2,4]{1,0:T(2,128)S(1)}, f32[2,128,256]{2,1,0:T(8,128)}, f32[2,128,256]{2,1,0:T(8,128)}, f32[2,128,256]{2,1,0:T(8,128)}) custom-call(s32[3,32]{1,0:T(4,128)S(1)} %bitcast.8, f32[512,256]{1,0:T(8,128)S(1)} %get-tuple-element.41.direction_ref.values_ref, f32[512,512]{1,0:T(8,128)S(1)} %collective-permute-done.gate_ref), custom_call_target="tpu_custom_call" | custom-call | tf_op jit(solution)/shard_map/pallas_call | solution.py:419
  9.2 2.6 %collective-permute-start.1 = (f32[2,128,256]{2,1,0:T(8,128)}, f32[2,128,256]{2,1,0:T(8,128)S(1)}, u32[]{:S(2)}, u32[]{:S(2)}) collective-permute-start(f32[2,128,256]{2,1,0:T(8,128)} %get-tuple-element.51), channel_id=1, source_target_pairs={{0,6},{2,4},{4,2},{6,0},{8,14},{10,12},{12,10},{14,8},{1,7},{3,5},... | collective-permute-start | bytes 786440 | tf_op jit(solution)/shard_map/ppermute | solution.py:369
  12.7 1.6 %copy.7 = f32[512,512]{0,1:T(8,128)S(1)} copy(f32[512,512]{1,0:T(8,128)} %param.9) | data formatting | bytes 2097152 | tf_op jit(solution)/shard_map/optimization_barrier | solution.py:373
  18.1 1.6 %collective-permute-start.8 = (f32[4,128,256]{2,1,0:T(8,128)S(1)}, f32[4,128,256]{2,1,0:T(8,128)S(1)}, u32[]{:S(2)}, u32[]{:S(2)}) collective-permute-start(f32[4,128,256]{2,1,0:T(8,128)S(1)} %get-tuple-element.56.refs_4_), channel_id=1, source_target_pairs={{0,2},{2,0},{4,6},{6,4},{8,10},{10,8},{12,14},{14,12},{1,3},{3,1},... | collective-permute-start | bytes 1572872 | tf_op jit(solution)/shard_map/ppermute | solution.py:369
  19.7 2.3 %shard_map.70 = (bf16[4,128,512]{2,1,0:T(8,128)(2,1)}, bf16[4,128,512]{2,1,0:T(8,128)(2,1)}) custom-call(f32[4,4,128,128]{3,2,1,0:T(8,128)} %kinship_hbm.3), custom_call_target="tpu_custom_call" | custom-call | tf_op jit(solution)/shard_map/pallas_call | solution.py:429
  22.0 9.2 %collective-permute-done.4.partner_ref = f32[512,256]{1,0:T(8,128)S(1)} collective-permute-done((f32[512,256]{1,0:T(8,128)S(1)}, f32[512,256]{1,0:T(8,128)S(1)}, u32[]{:S(2)}, u32[]{:S(2)}) %collective-permute-start.4) | collective-permute-done | bytes 524320 | tf_op jit(solution)/shard_map/ppermute | solution.py:369
  31.2 3.4 %collective-permute-done.2.refs_1_ = f32[2,128,256]{2,1,0:T(8,128)} collective-permute-done((f32[2,128,256]{2,1,0:T(8,128)}, f32[2,128,256]{2,1,0:T(8,128)}, u32[]{:S(2)}, u32[]{:S(2)}) %collective-permute-start.2) | collective-permute-done | bytes 262176 | tf_op jit(solution)/shard_map/ppermute | solution.py:369
  35.3 2.0 %collective-permute-start.6 = (f32[2,128,256]{2,1,0:T(8,128)S(1)}, f32[2,128,256]{2,1,0:T(8,128)S(1)}, u32[]{:S(2)}, u32[]{:S(2)}) collective-permute-start(f32[2,128,256]{2,1,0:T(8,128)S(1)} %get-tuple-element.58), channel_id=1, source_target_pairs={{0,4},{2,6},{4,0},{6,2},{8,12},{10,14},{12,8},{14,10},{1,5},{3,7},... | collective-permute-start | bytes 786440 | tf_op jit(solution)/shard_map/ppermute | solution.py:369
  38.8 6.7 %collective-permute-done.5.refs_3_ = f32[2,128,256]{2,1,0:T(8,128)S(1)} collective-permute-done((f32[2,128,256]{2,1,0:T(8,128)S(1)}, f32[2,128,256]{2,1,0:T(8,128)S(1)}, u32[]{:S(2)}, u32[]{:S(2)}) %collective-permute-start.5) | collective-permute-done | bytes 262176 | tf_op jit(solution)/shard_map/ppermute | solution.py:369
  45.5 3.0 %collective-permute-done.6.refs_4_ = f32[2,128,256]{2,1,0:T(8,128)S(1)} collective-permute-done((f32[2,128,256]{2,1,0:T(8,128)S(1)}, f32[2,128,256]{2,1,0:T(8,128)S(1)}, u32[]{:S(2)}, u32[]{:S(2)}) %collective-permute-start.6) | collective-permute-done | bytes 262176 | tf_op jit(solution)/shard_map/ppermute | solution.py:369
  49.4 4.7 %shard_map.74 = (f32[512,256]{1,0:T(8,128)}, f32[512,256]{1,0:T(8,128)}, f32[8,136,256]{2,1,0:T(8,128)}, f32[4,128,256]{2,1,0:T(8,128)}, f32[4,128,256]{2,1,0:T(8,128)}) custom-call(s32[4,12]{1,0:T(4,128)S(1)} %get-tuple-element.43.table_ref, bf16[4,128,512]{2,1,0:T(8,128)(2,1)S(1)} %copy-done, bf16[4,128,512]{2,1,0:T(8,128)(2,1)S(1)} %copy-done.1, ...), custom_call_target="tpu_custom_call" | custom-call | tf_op jit(solution)/shard_map/pallas_call | solution.py:462
  54.1 6.1 %all-to-all-start = ((f32[8,136,256]{2,1,0:T(8,128)}), f32[8,136,256]{2,1,0:T(8,128)S(1)}, u32[]{:S(2)}, u32[]{:S(2)}) async-start(f32[8,136,256]{2,1,0:T(8,128)} %get-tuple-element.62), calls=%async_computation | async-start | bytes 2228224 | tf_op jit(solution)/shard_map/all_to_all | solution.py:475
  60.2 2.0 %collective-permute-start.9 = (f32[4,128,256]{2,1,0:T(8,128)}, f32[4,128,256]{2,1,0:T(8,128)S(1)}, u32[]{:S(2)}, u32[]{:S(2)}) collective-permute-start(f32[4,128,256]{2,1,0:T(8,128)} %get-tuple-element.64), channel_id=1, source_target_pairs={{0,2},{2,0},{4,6},{6,4},{8,10},{10,8},{12,14},{14,12},{1,3},{3,1},... | collective-permute-start | bytes 1572872 | tf_op jit(solution)/shard_map/ppermute | solution.py:369
  63.7 1.5 %collective-permute-start.10 = (f32[2,128,256]{2,1,0:T(8,128)}, f32[2,128,256]{2,1,0:T(8,128)}, u32[]{:S(2)}, u32[]{:S(2)}) collective-permute-start(f32[2,128,256]{2,1,0:T(8,128)} %get-tuple-element.70), channel_id=1, source_target_pairs={{0,4},{2,6},{4,0},{6,2},{8,12},{10,14},{12,8},{14,10},{1,5},{3,7},... | collective-permute-start | bytes 786440 | tf_op jit(solution)/shard_map/ppermute | solution.py:369
  65.2 20.7 %collective-permute-done.9.taken_ref = f32[4,128,256]{2,1,0:T(8,128)S(1)} collective-permute-done((f32[4,128,256]{2,1,0:T(8,128)}, f32[4,128,256]{2,1,0:T(8,128)S(1)}, u32[]{:S(2)}, u32[]{:S(2)}) %collective-permute-start.9) | collective-permute-done | bytes 524320 | tf_op jit(solution)/shard_map/ppermute | solution.py:369
  87.3 1.5 %collective-permute-start.12 = (f32[2,128,256]{2,1,0:T(8,128)}, f32[2,128,256]{2,1,0:T(8,128)}, u32[]{:S(2)}, u32[]{:S(2)}) collective-permute-start(f32[2,128,256]{2,1,0:T(8,128)} %get-tuple-element.65.refs_0_), channel_id=1, source_target_pairs={{0,4},{2,6},{4,0},{6,2},{8,12},{10,14},{12,8},{14,10},{1,5},{3,7},... | collective-permute-start | bytes 786440 | tf_op jit(solution)/shard_map/ppermute | solution.py:369
  88.8 3.0 %shard_map.76.refs_0_ = f32[16,8,256]{2,1,0:T(8,128)} custom-call(s32[4,12]{1,0:T(4,128)S(1)} %get-tuple-element.43.table_ref, bf16[4,128,512]{2,1,0:T(8,128)(2,1)S(1)} %copy-done, bf16[4,128,512]{2,1,0:T(8,128)(2,1)S(1)} %copy-done.1, f32[512,256]{1,0:T(8,128)S(1)} %copy-done.7, f32[512,1]{1,0:T(8,128)S(1)} %copy-done.10, f32[512,256]{1,0:T(8,128)S(1)} %copy-done.8, ...), custom_call_target="tpu_custom_call" | custom-call | tf_op jit(solution)/shard_map/pallas_call | solution.py:481
  92.9 2.4 %collective-permute-start.11 = (f32[1,128,256]{2,1,0:T(8,128)S(1)}, f32[1,128,256]{2,1,0:T(8,128)S(1)}, u32[]{:S(2)}, u32[]{:S(2)}) collective-permute-start(f32[1,128,256]{2,1,0:T(8,128)S(1)} %get-tuple-element.72), channel_id=1, source_target_pairs={{0,8},{2,10},{4,12},{6,14},{8,0},{10,2},{12,4},{14,6},{1,9},{3,11}... | collective-permute-start | bytes 393224 | tf_op jit(solution)/shard_map/ppermute | solution.py:369
  96.3 3.9 %collective-permute-start.13 = (f32[1,128,256]{2,1,0:T(8,128)S(1)}, f32[1,128,256]{2,1,0:T(8,128)S(1)}, u32[]{:S(2)}, u32[]{:S(2)}) collective-permute-start(f32[1,128,256]{2,1,0:T(8,128)S(1)} %get-tuple-element.75), channel_id=1, source_target_pairs={{0,8},{2,10},{4,12},{6,14},{8,0},{10,2},{12,4},{14,6},{1,9},{3,11}... | collective-permute-start | bytes 393224 | tf_op jit(solution)/shard_map/ppermute | solution.py:369
  100.2 3.5 %all-to-all-start.1 = ((f32[16,8,256]{2,1,0:T(8,128)}), f32[16,8,256]{2,1,0:T(8,128)S(1)}, u32[]{:S(2)}, u32[]{:S(2)}) async-start(f32[16,8,256]{2,1,0:T(8,128)} %shard_map.76.refs_0_), calls=%async_computation.1 | async-start | bytes 262144 | tf_op jit(solution)/shard_map/all_to_all | solution.py:488
  104.8 2.1 %collective-permute-done.13.second_taken_ref = f32[1,128,256]{2,1,0:T(8,128)S(1)} collective-permute-done((f32[1,128,256]{2,1,0:T(8,128)S(1)}, f32[1,128,256]{2,1,0:T(8,128)S(1)}, u32[]{:S(2)}, u32[]{:S(2)}) %collective-permute-start.13) | collective-permute-done | bytes 131104 | tf_op jit(solution)/shard_map/ppermute | solution.py:369
  107.1 4.6 %all-to-all-done.1.sums_ref = f32[16,8,256]{2,1,0:T(8,128)S(1)} async-done(((f32[16,8,256]{2,1,0:T(8,128)}), f32[16,8,256]{2,1,0:T(8,128)S(1)}, u32[]{:S(2)}, u32[]{:S(2)}) %all-to-all-start.1) | async-done | bytes 131104 | tf_op jit(solution)/shard_map/all_to_all | solution.py:488
  (63 shorter events, 15.9 us)
Async XLA Ops:
  3.1 4.2 %collective-permute-start = (f32[512,512]{1,0:T(8,128)S(1)}, f32[512,512]{1,0:T(8,128)S(1)}, u32[]{:S(2)}, u32[]{:S(2)}) collective-permute-start(f32[512,512]{1,0:T(8,128)S(1)} %copy-done.17), channel_id=1, source_target_pairs={{0,1},{1,0},{2,3},{3,2},{4,5},{5,4},{6,7},{7,6},{8,9},{9,8},{10,11... | collective-permute-start | bytes 3145736 | tf_op jit(solution)/shard_map/ppermute | solution.py:369
  3.6 27.5 %collective-permute-start.4 = (f32[512,256]{1,0:T(8,128)S(1)}, f32[512,256]{1,0:T(8,128)S(1)}, u32[]{:S(2)}, u32[]{:S(2)}) collective-permute-start(f32[512,256]{1,0:T(8,128)S(1)} %get-tuple-element.41.direction_ref.values_ref), channel_id=1, source_target_pairs={{0,8},{2,10},{4,12},{6,14},{8,0},{10,2},{12,4},{14,6},{1,9},{3,11}... | collective-permute-start | bytes 1572872 | tf_op jit(solution)/shard_map/ppermute | solution.py:369
  9.2 22.0 %collective-permute-start.1 = (f32[2,128,256]{2,1,0:T(8,128)}, f32[2,128,256]{2,1,0:T(8,128)S(1)}, u32[]{:S(2)}, u32[]{:S(2)}) collective-permute-start(f32[2,128,256]{2,1,0:T(8,128)} %get-tuple-element.51), channel_id=1, source_target_pairs={{0,6},{2,4},{4,2},{6,0},{8,14},{10,12},{12,10},{14,8},{1,7},{3,5},... | collective-permute-start | bytes 786440 | tf_op jit(solution)/shard_map/ppermute | solution.py:369
  11.8 22.8 %collective-permute-start.2 = (f32[2,128,256]{2,1,0:T(8,128)}, f32[2,128,256]{2,1,0:T(8,128)}, u32[]{:S(2)}, u32[]{:S(2)}) collective-permute-start(f32[2,128,256]{2,1,0:T(8,128)} %get-tuple-element.52), channel_id=1, source_target_pairs={{0,4},{2,6},{4,0},{6,2},{8,12},{10,14},{12,8},{14,10},{1,5},{3,7},... | collective-permute-start | bytes 786440 | tf_op jit(solution)/shard_map/ppermute | solution.py:369
  12.2 22.4 %collective-permute-start.3 = (f32[2,128,256]{2,1,0:T(8,128)}, f32[2,128,256]{2,1,0:T(8,128)}, u32[]{:S(2)}, u32[]{:S(2)}) collective-permute-start(f32[2,128,256]{2,1,0:T(8,128)} %get-tuple-element.53), channel_id=1, source_target_pairs={{0,2},{2,0},{4,6},{6,4},{8,10},{10,8},{12,14},{14,12},{1,3},{3,1},... | collective-permute-start | bytes 786440 | tf_op jit(solution)/shard_map/ppermute | solution.py:369
  18.1 17.2 %copy-start.3 = (f32[4,128,256]{2,1,0:T(8,128)}, f32[4,128,256]{2,1,0:T(8,128)S(1)}, u32[]{:S(2)}) copy-start(f32[4,128,256]{2,1,0:T(8,128)S(1)} %get-tuple-element.55.refs_3_.kept_ref) | copy-start | bytes 1572868
  18.1 20.7 %collective-permute-start.8 = (f32[4,128,256]{2,1,0:T(8,128)S(1)}, f32[4,128,256]{2,1,0:T(8,128)S(1)}, u32[]{:S(2)}, u32[]{:S(2)}) collective-permute-start(f32[4,128,256]{2,1,0:T(8,128)S(1)} %get-tuple-element.56.refs_4_), channel_id=1, source_target_pairs={{0,2},{2,0},{4,6},{6,4},{8,10},{10,8},{12,14},{14,12},{1,3},{3,1},... | collective-permute-start | bytes 1572872 | tf_op jit(solution)/shard_map/ppermute | solution.py:369
  34.6 14.8 %copy-start.9 = (f32[512,1]{1,0:T(8,128)S(1)}, f32[512,1]{1,0:T(8,128)}, u32[]{:S(2)}) copy-start(f32[512,1]{1,0:T(8,128)} %get-tuple-element.46.diagonal_ref) | copy-start | bytes 6148
  35.2 10.3 %collective-permute-start.5 = (f32[2,128,256]{2,1,0:T(8,128)S(1)}, f32[2,128,256]{2,1,0:T(8,128)S(1)}, u32[]{:S(2)}, u32[]{:S(2)}) collective-permute-start(f32[2,128,256]{2,1,0:T(8,128)S(1)} %get-tuple-element.57), channel_id=1, source_target_pairs={{0,6},{2,4},{4,2},{6,0},{8,14},{10,12},{12,10},{14,8},{1,7},{3,5},... | collective-permute-start | bytes 786440 | tf_op jit(solution)/shard_map/ppermute | solution.py:369
  35.3 13.2 %collective-permute-start.6 = (f32[2,128,256]{2,1,0:T(8,128)S(1)}, f32[2,128,256]{2,1,0:T(8,128)S(1)}, u32[]{:S(2)}, u32[]{:S(2)}) collective-permute-start(f32[2,128,256]{2,1,0:T(8,128)S(1)} %get-tuple-element.58), channel_id=1, source_target_pairs={{0,4},{2,6},{4,0},{6,2},{8,12},{10,14},{12,8},{14,10},{1,5},{3,7},... | collective-permute-start | bytes 786440 | tf_op jit(solution)/shard_map/ppermute | solution.py:369
  37.3 12.0 %collective-permute-start.7 = (f32[2,128,256]{2,1,0:T(8,128)S(1)}, f32[2,128,256]{2,1,0:T(8,128)S(1)}, u32[]{:S(2)}, u32[]{:S(2)}) collective-permute-start(f32[2,128,256]{2,1,0:T(8,128)S(1)} %get-tuple-element.59), channel_id=1, source_target_pairs={{0,2},{2,0},{4,6},{6,4},{8,10},{10,8},{12,14},{14,12},{1,3},{3,1},... | collective-permute-start | bytes 786440 | tf_op jit(solution)/shard_map/ppermute | solution.py:369
  38.8 15.3 %copy-start.5 = (f32[4,128,256]{2,1,0:T(8,128)}, f32[4,128,256]{2,1,0:T(8,128)S(1)}, u32[]{:S(2)}) copy-start(f32[4,128,256]{2,1,0:T(8,128)S(1)} %collective-permute-done.8.refs_7_.taken_ref) | copy-start | bytes 1572868
  54.1 34.7 %all-to-all-start = ((f32[8,136,256]{2,1,0:T(8,128)}), f32[8,136,256]{2,1,0:T(8,128)S(1)}, u32[]{:S(2)}, u32[]{:S(2)}) async-start(f32[8,136,256]{2,1,0:T(8,128)} %get-tuple-element.62), calls=%async_computation | async-start | bytes 2228224 | tf_op jit(solution)/shard_map/all_to_all | solution.py:475
  60.2 25.7 %copy-start.11 = (f32[4,128,256]{2,1,0:T(8,128)S(1)}, f32[4,128,256]{2,1,0:T(8,128)}, u32[]{:S(2)}) copy-start(f32[4,128,256]{2,1,0:T(8,128)} %get-tuple-element.63.kept_ref) | copy-start | bytes 1572868
  60.2 28.6 %copy-start.10 = (f32[512,1]{1,0:T(8,128)S(1)}, f32[512,1]{1,0:T(8,128)}, u32[]{:S(2)}) copy-start(f32[512,1]{1,0:T(8,128)} %get-tuple-element.46.diagonal_ref) | copy-start | bytes 6148
  60.2 25.6 %collective-permute-start.9 = (f32[4,128,256]{2,1,0:T(8,128)}, f32[4,128,256]{2,1,0:T(8,128)S(1)}, u32[]{:S(2)}, u32[]{:S(2)}) collective-permute-start(f32[4,128,256]{2,1,0:T(8,128)} %get-tuple-element.64), channel_id=1, source_target_pairs={{0,2},{2,0},{4,6},{6,4},{8,10},{10,8},{12,14},{14,12},{1,3},{3,1},... | collective-permute-start | bytes 1572872 | tf_op jit(solution)/shard_map/ppermute | solution.py:369
  63.7 25.1 %copy-start.7 = (f32[512,256]{1,0:T(8,128)S(1)}, f32[512,256]{1,0:T(8,128)}, u32[]{:S(2)}) copy-start(f32[512,256]{1,0:T(8,128)} %get-tuple-element.40.direction_ref) | copy-start | bytes 1572868
  63.7 25.1 %copy-start.8 = (f32[512,256]{1,0:T(8,128)S(1)}, f32[512,256]{1,0:T(8,128)}, u32[]{:S(2)}) copy-start(f32[512,256]{1,0:T(8,128)} %get-tuple-element.60.scaled_ref) | copy-start | bytes 1572868
  63.7 28.2 %collective-permute-start.10 = (f32[2,128,256]{2,1,0:T(8,128)}, f32[2,128,256]{2,1,0:T(8,128)}, u32[]{:S(2)}, u32[]{:S(2)}) collective-permute-start(f32[2,128,256]{2,1,0:T(8,128)} %get-tuple-element.70), channel_id=1, source_target_pairs={{0,4},{2,6},{4,0},{6,2},{8,12},{10,14},{12,8},{14,10},{1,5},{3,7},... | collective-permute-start | bytes 786440 | tf_op jit(solution)/shard_map/ppermute | solution.py:369
  87.3 8.0 %collective-permute-start.12 = (f32[2,128,256]{2,1,0:T(8,128)}, f32[2,128,256]{2,1,0:T(8,128)}, u32[]{:S(2)}, u32[]{:S(2)}) collective-permute-start(f32[2,128,256]{2,1,0:T(8,128)} %get-tuple-element.65.refs_0_), channel_id=1, source_target_pairs={{0,4},{2,6},{4,0},{6,2},{8,12},{10,14},{12,8},{14,10},{1,5},{3,7},... | collective-permute-start | bytes 786440 | tf_op jit(solution)/shard_map/ppermute | solution.py:369
  92.9 11.9 %collective-permute-start.11 = (f32[1,128,256]{2,1,0:T(8,128)S(1)}, f32[1,128,256]{2,1,0:T(8,128)S(1)}, u32[]{:S(2)}, u32[]{:S(2)}) collective-permute-start(f32[1,128,256]{2,1,0:T(8,128)S(1)} %get-tuple-element.72), channel_id=1, source_target_pairs={{0,8},{2,10},{4,12},{6,14},{8,0},{10,2},{12,4},{14,6},{1,9},{3,11}... | collective-permute-start | bytes 393224 | tf_op jit(solution)/shard_map/ppermute | solution.py:369
  96.3 10.7 %collective-permute-start.13 = (f32[1,128,256]{2,1,0:T(8,128)S(1)}, f32[1,128,256]{2,1,0:T(8,128)S(1)}, u32[]{:S(2)}, u32[]{:S(2)}) collective-permute-start(f32[1,128,256]{2,1,0:T(8,128)S(1)} %get-tuple-element.75), channel_id=1, source_target_pairs={{0,8},{2,10},{4,12},{6,14},{8,0},{10,2},{12,4},{14,6},{1,9},{3,11}... | collective-permute-start | bytes 393224 | tf_op jit(solution)/shard_map/ppermute | solution.py:369
  100.2 11.4 %all-to-all-start.1 = ((f32[16,8,256]{2,1,0:T(8,128)}), f32[16,8,256]{2,1,0:T(8,128)S(1)}, u32[]{:S(2)}, u32[]{:S(2)}) async-start(f32[16,8,256]{2,1,0:T(8,128)} %shard_map.76.refs_0_), calls=%async_computation.1 | async-start | bytes 262144 | tf_op jit(solution)/shard_map/all_to_all | solution.py:488
  107.0 5.5 %collective-permute-start.14 = (f32[2,64,256]{2,1,0:T(8,128)S(1)}, f32[2,64,256]{2,1,0:T(8,128)S(1)}, u32[]{:S(2)}, u32[]{:S(2)}) collective-permute-start(f32[2,64,256]{2,1,0:T(8,128)S(1)} %get-tuple-element.77), channel_id=1, source_target_pairs={{0,1},{1,0},{2,3},{3,2},{4,5},{5,4},{6,7},{7,6},{8,9},{9,8},{10,11... | collective-permute-start | bytes 393224 | tf_op jit(solution)/shard_map/ppermute | solution.py:369
  (11 other events, 67.1 us)

commit v23 on v21

--- a/solution.py
+++ b/solution.py
@@ -252,14 +252,13 @@
 
 
 def curvature_kernel(devices, table_ref, high_hbm, low_hbm, direction_hbm, diagonal_hbm, scaled_hbm, handled_hbm,
-                     later_hbm, *refs):
-    (sums_hbm, sums_ref, high_ref, low_ref, direction_ref, diagonal_ref, scaled_ref, handled_ref, later_ref,
-     semaphores) = refs[-10:]
+                     later_ref, *refs):
+    sums_ref, high_ref, low_ref, direction_ref, diagonal_ref, scaled_ref, handled_ref, semaphores = refs[-8:]
     block_count, tile, depth = high_ref.shape
     copies = Copies(semaphores)
     wait_all([copies.start(source, target) for source, target in (
-        (later_hbm, later_ref), (scaled_hbm, scaled_ref), (direction_hbm, direction_ref), (high_hbm, high_ref),
-        (low_hbm, low_ref), (handled_hbm, handled_ref), (diagonal_hbm, diagonal_ref),
+        (scaled_hbm, scaled_ref), (direction_hbm, direction_ref), (high_hbm, high_ref), (low_hbm, low_ref),
+        (handled_hbm, handled_ref), (diagonal_hbm, diagonal_ref),
     )])
     others = depth // tile - 1
     first_sums = later_ref[0, pl.ds(tile, SUBLANES), :]
@@ -284,7 +283,6 @@
     sums = jnp.where(row_ids == 3, jnp.sum(bend, axis=0, keepdims=True), sums)
     for i in range(2 * devices):
         sums_ref[i] = sums
-    copies.start(sums_ref, sums_hbm).wait()
 
 
 def add_kernel(kept_ref, taken_ref, *refs):
@@ -447,8 +445,8 @@
     def add_step(kept, taken, *gates):
         rows = float_of(kept.shape[0] // 2, 2 * share_rows, columns)
         return call(
-            add_kernel, [rows] * 2, [vmem] * 2 + [hbm] * len(gates), [vmem] * 2
-        )(kept, taken, *at_home(*gates))
+            add_kernel, [rows] * 2, [vmem] * (2 + len(gates)), [vmem] * 2
+        )(kept, taken, *gates)
 
     partner = swap(direction, "samples", devices, half)
     near = to_mates(outgoing)
@@ -486,13 +484,10 @@
     scaled_taken = swap(scaled_given, "samples", devices, steps[0])
     sums = call(
         functools.partial(curvature_kernel, devices),
-        pltpu.HBM((2 * devices, SUBLANES, columns), jnp.float32),
-        [smem] + [hbm] * 6 + [anywhere] * 2,
-        hbm,
-        [
-            room(2 * devices, SUBLANES, columns), tiles_room, tiles_room, full_room, room(people, 1), full_room,
-            full_room, room(devices, tile + SUBLANES, columns), pltpu.SemaphoreType.DMA((8,)),
-        ],
+        float_of(2 * devices, SUBLANES, columns),
+        [smem] + [hbm] * 6 + [vmem, anywhere],
+        vmem,
+        [tiles_room, tiles_room, full_room, room(people, 1), full_room, full_room, pltpu.SemaphoreType.DMA((6,))],
     )(table, *at_home(high, low, direction_kept_hbm, diagonal, scaled, handled), later, scaled_given)
     all_sums = lax.all_to_all(sums, ("samples", "cols"), split_axis=0, concat_axis=0, tiled=True)
     for step in steps[1:]:

time: 111 us -> 112 us (level)
  Pallas kernels: 19.6 us -> 21.3 us
  starting transfers between devices: 33.6 us -> 32.3 us
    pallas_call x5, Pallas kernels: 4.87 us -> 6.62 us  [the longest x1 3.83 us: per_device(): call(functools.partial(curvature_kernel, devices), float_of(2 * devices,...]
    ppermute x15, starting transfers between devices: 24 us -> 22.7 us  [swap(): return lax.ppermute(values, axis, [(i, i ^ step) for i in range(devices)])]
  transfers between devices with their start and end apart: 17 -> 17, of which waited for: 9 -> 9; matrix products, arithmetic and copies ran while one was open for 3% -> 3% of each run, Pallas kernels for 11% -> 12%
where the time goes in v23:
time: 112 us; the launch traced here: 111 us
  waiting for transfers between devices  52.5 us (47%)
  starting transfers between devices  32.3 us (29%)
  Pallas kernels  21.3 us (19%)
  local copies, waits for them, and re-layouts  4.13 us (4%)
    ppermute x15, waiting for transfers between devices, swap(): return lax.ppermute(values, axis, [(i, i ^ step) for i in range(devices)])  49.4 us
    ppermute x15, starting transfers between devices, swap(): return lax.ppermute(values, axis, [(i, i ^ step) for i in range(devices)])  22.7 us
    all_to_all x1, starting transfers between devices, per_device(): lax.all_to_all(outgoing, 'samples', split_axis=0, concat_axis=0, tiled=True)  6.09 us
    pallas_call x1, Pallas kernels, per_device(): call(functools.partial(apply_kernel, devices, capacity), [full_out, full_...  4.72 us
    pallas_call x1, Pallas kernels, per_device(): call(functools.partial(curvature_kernel, devices), float_of(2 * devices,...  3.83 us
    all_to_all x1, starting transfers between devices, per_device(): lax.all_to_all(sums, ('samples', 'cols'), split_axis=0, concat_axis=0, ti...  3.51 us
    all_to_all x1, waiting for transfers between devices, per_device(): lax.all_to_all(sums, ('samples', 'cols'), split_axis=0, concat_axis=0, ti...  3.06 us
    pallas_call x4, Pallas kernels, add_step(): call(add_kernel, [rows] * 2, [vmem] * (2 + len(gates)), [vmem] * 2)  2.79 us
  transfers between devices with their start and end apart: 17, of which 9 were waited for; matrix products, arithmetic and copies ran while one was open for 3% of the time, Pallas kernels for 12%

profile of v23, /device:TPU:0, one launch (start us, length us, event | category | flops | bytes accessed | tf_op | source)
XLA Modules:
  0.0 111.1 jit_solution(15698266682888061515)
XLA Ops:
  0.7 2.5 %shard_map.68 = (f32[512,256]{1,0:T(8,128)S(1)}, f32[512,256]{1,0:T(8,128)}, f32[512,1]{1,0:T(8,128)}, f32[8,256]{1,0:T(8,128)S(1)}) custom-call(f32[4,4,128,128]{3,2,1,0:T(8,128)} %kinship_hbm.3, f32[4,128]{1,0:T(4,128)} %bitcast.9, f32[512,256]{1,0:T(8,128)} %phenotypes_hbm.1), custom_call_target="tpu_custom_call" | custom-call | tf_op jit(solution)/shard_map/pallas_call | solution.py:403
  3.6 3.7 %collective-permute-start.4 = (f32[512,256]{1,0:T(8,128)S(1)}, f32[512,256]{1,0:T(8,128)S(1)}, u32[]{:S(2)}, u32[]{:S(2)}) collective-permute-start(f32[512,256]{1,0:T(8,128)S(1)} %get-tuple-element.41.direction_ref.values_ref), channel_id=1, source_target_pairs={{0,8},{2,10},{4,12},{6,14},{8,0},{10,2},{12,4},{14,6},{1,9},{3,11}... | collective-permute-start | bytes 1572872 | tf_op jit(solution)/shard_map/ppermute | solution.py:372
  7.3 1.8 %shard_map.69 = (s32[4,12]{1,0:T(4,128)S(1)}, s32[2,4]{1,0:T(2,128)S(1)}, f32[2,128,256]{2,1,0:T(8,128)}, f32[2,128,256]{2,1,0:T(8,128)}, f32[2,128,256]{2,1,0:T(8,128)}) custom-call(s32[3,32]{1,0:T(4,128)S(1)} %bitcast.8, f32[512,256]{1,0:T(8,128)S(1)} %get-tuple-element.41.direction_ref.values_ref, f32[512,512]{1,0:T(8,128)S(1)} %collective-permute-done.gate_ref), custom_call_target="tpu_custom_call" | custom-call | tf_op jit(solution)/shard_map/pallas_call | solution.py:422
  9.1 2.6 %collective-permute-start.1 = (f32[2,128,256]{2,1,0:T(8,128)}, f32[2,128,256]{2,1,0:T(8,128)S(1)}, u32[]{:S(2)}, u32[]{:S(2)}) collective-permute-start(f32[2,128,256]{2,1,0:T(8,128)} %get-tuple-element.51), channel_id=1, source_target_pairs={{0,6},{2,4},{4,2},{6,0},{8,14},{10,12},{12,10},{14,8},{1,7},{3,5},... | collective-permute-start | bytes 786440 | tf_op jit(solution)/shard_map/ppermute | solution.py:372
  12.7 1.6 %copy.7 = f32[512,512]{0,1:T(8,128)S(1)} copy(f32[512,512]{1,0:T(8,128)} %param.9) | data formatting | bytes 2097152 | tf_op jit(solution)/shard_map/optimization_barrier | solution.py:376
  18.0 1.6 %collective-permute-start.8 = (f32[4,128,256]{2,1,0:T(8,128)S(1)}, f32[4,128,256]{2,1,0:T(8,128)S(1)}, u32[]{:S(2)}, u32[]{:S(2)}) collective-permute-start(f32[4,128,256]{2,1,0:T(8,128)S(1)} %get-tuple-element.56.refs_4_), channel_id=1, source_target_pairs={{0,2},{2,0},{4,6},{6,4},{8,10},{10,8},{12,14},{14,12},{1,3},{3,1},... | collective-permute-start | bytes 1572872 | tf_op jit(solution)/shard_map/ppermute | solution.py:372
  19.6 2.3 %shard_map.70 = (bf16[4,128,512]{2,1,0:T(8,128)(2,1)}, bf16[4,128,512]{2,1,0:T(8,128)(2,1)}) custom-call(f32[4,4,128,128]{3,2,1,0:T(8,128)} %kinship_hbm.3), custom_call_target="tpu_custom_call" | custom-call | tf_op jit(solution)/shard_map/pallas_call | solution.py:432
  21.9 9.2 %collective-permute-done.4.partner_ref = f32[512,256]{1,0:T(8,128)S(1)} collective-permute-done((f32[512,256]{1,0:T(8,128)S(1)}, f32[512,256]{1,0:T(8,128)S(1)}, u32[]{:S(2)}, u32[]{:S(2)}) %collective-permute-start.4) | collective-permute-done | bytes 524320 | tf_op jit(solution)/shard_map/ppermute | solution.py:372
  31.2 3.4 %collective-permute-done.2.refs_1_ = f32[2,128,256]{2,1,0:T(8,128)} collective-permute-done((f32[2,128,256]{2,1,0:T(8,128)}, f32[2,128,256]{2,1,0:T(8,128)}, u32[]{:S(2)}, u32[]{:S(2)}) %collective-permute-start.2) | collective-permute-done | bytes 262176 | tf_op jit(solution)/shard_map/ppermute | solution.py:372
  35.3 2.0 %collective-permute-start.6 = (f32[2,128,256]{2,1,0:T(8,128)S(1)}, f32[2,128,256]{2,1,0:T(8,128)S(1)}, u32[]{:S(2)}, u32[]{:S(2)}) collective-permute-start(f32[2,128,256]{2,1,0:T(8,128)S(1)} %get-tuple-element.58), channel_id=1, source_target_pairs={{0,4},{2,6},{4,0},{6,2},{8,12},{10,14},{12,8},{14,10},{1,5},{3,7},... | collective-permute-start | bytes 786440 | tf_op jit(solution)/shard_map/ppermute | solution.py:372
  38.8 6.7 %collective-permute-done.5.refs_3_ = f32[2,128,256]{2,1,0:T(8,128)S(1)} collective-permute-done((f32[2,128,256]{2,1,0:T(8,128)S(1)}, f32[2,128,256]{2,1,0:T(8,128)S(1)}, u32[]{:S(2)}, u32[]{:S(2)}) %collective-permute-start.5) | collective-permute-done | bytes 262176 | tf_op jit(solution)/shard_map/ppermute | solution.py:372
  45.5 3.0 %collective-permute-done.6.refs_4_ = f32[2,128,256]{2,1,0:T(8,128)S(1)} collective-permute-done((f32[2,128,256]{2,1,0:T(8,128)S(1)}, f32[2,128,256]{2,1,0:T(8,128)S(1)}, u32[]{:S(2)}, u32[]{:S(2)}) %collective-permute-start.6) | collective-permute-done | bytes 262176 | tf_op jit(solution)/shard_map/ppermute | solution.py:372
  49.3 4.7 %shard_map.74 = (f32[512,256]{1,0:T(8,128)}, f32[512,256]{1,0:T(8,128)}, f32[8,136,256]{2,1,0:T(8,128)}, f32[4,128,256]{2,1,0:T(8,128)}, f32[4,128,256]{2,1,0:T(8,128)}) custom-call(s32[4,12]{1,0:T(4,128)S(1)} %get-tuple-element.43.table_ref, bf16[4,128,512]{2,1,0:T(8,128)(2,1)S(1)} %copy-done, bf16[4,128,512]{2,1,0:T(8,128)(2,1)S(1)} %copy-done.1, ...), custom_call_target="tpu_custom_call" | custom-call | tf_op jit(solution)/shard_map/pallas_call | solution.py:465
  54.1 6.1 %all-to-all-start = ((f32[8,136,256]{2,1,0:T(8,128)}), f32[8,136,256]{2,1,0:T(8,128)S(1)}, u32[]{:S(2)}, u32[]{:S(2)}) async-start(f32[8,136,256]{2,1,0:T(8,128)} %get-tuple-element.62), calls=%async_computation | async-start | bytes 2228224 | tf_op jit(solution)/shard_map/all_to_all | solution.py:479
  60.2 2.0 %collective-permute-start.9 = (f32[4,128,256]{2,1,0:T(8,128)}, f32[4,128,256]{2,1,0:T(8,128)S(1)}, u32[]{:S(2)}, u32[]{:S(2)}) collective-permute-start(f32[4,128,256]{2,1,0:T(8,128)} %get-tuple-element.64), channel_id=1, source_target_pairs={{0,2},{2,0},{4,6},{6,4},{8,10},{10,8},{12,14},{14,12},{1,3},{3,1},... | collective-permute-start | bytes 1572872 | tf_op jit(solution)/shard_map/ppermute | solution.py:372
  64.4 21.4 %collective-permute-done.9.taken_ref = f32[4,128,256]{2,1,0:T(8,128)S(1)} collective-permute-done((f32[4,128,256]{2,1,0:T(8,128)}, f32[4,128,256]{2,1,0:T(8,128)S(1)}, u32[]{:S(2)}, u32[]{:S(2)}) %collective-permute-start.9) | collective-permute-done | bytes 524320 | tf_op jit(solution)/shard_map/ppermute | solution.py:372
  85.9 1.5 %collective-permute-start.12 = (f32[2,128,256]{2,1,0:T(8,128)S(1)}, f32[2,128,256]{2,1,0:T(8,128)S(1)}, u32[]{:S(2)}, u32[]{:S(2)}) collective-permute-start(f32[2,128,256]{2,1,0:T(8,128)S(1)} %get-tuple-element.65.refs_0_), channel_id=1, source_target_pairs={{0,4},{2,6},{4,0},{6,2},{8,12},{10,14},{12,8},{14,10},{1,5},{3,7},... | collective-permute-start | bytes 786440 | tf_op jit(solution)/shard_map/ppermute | solution.py:372
  87.5 3.8 %shard_map.76.refs_0_ = f32[16,8,256]{2,1,0:T(8,128)} custom-call(s32[4,12]{1,0:T(4,128)S(1)} %get-tuple-element.43.table_ref, bf16[4,128,512]{2,1,0:T(8,128)(2,1)} %get-tuple-element.44.refs_5_.high_hbm, bf16[4,128,512]{2,1,0:T(8,128)(2,1)} %get-tuple-element.45.refs_6_.low_hbm, f32[512,256]{1,0:T(8,128)} %get-tuple-element.40.direction_hbm.direction_ref, ...), custom_call_target="tpu_custom_call" | custom-call | tf_op jit(solution)/shard_map/pallas_call | solution.py:485
  92.4 2.4 %collective-permute-start.11 = (f32[1,128,256]{2,1,0:T(8,128)S(1)}, f32[1,128,256]{2,1,0:T(8,128)S(1)}, u32[]{:S(2)}, u32[]{:S(2)}) collective-permute-start(f32[1,128,256]{2,1,0:T(8,128)S(1)} %get-tuple-element.72), channel_id=1, source_target_pairs={{0,8},{2,10},{4,12},{6,14},{8,0},{10,2},{12,4},{14,6},{1,9},{3,11}... | collective-permute-start | bytes 393224 | tf_op jit(solution)/shard_map/ppermute | solution.py:372
  95.7 2.4 %collective-permute-start.13 = (f32[1,128,256]{2,1,0:T(8,128)S(1)}, f32[1,128,256]{2,1,0:T(8,128)S(1)}, u32[]{:S(2)}, u32[]{:S(2)}) collective-permute-start(f32[1,128,256]{2,1,0:T(8,128)S(1)} %get-tuple-element.75), channel_id=1, source_target_pairs={{0,8},{2,10},{4,12},{6,14},{8,0},{10,2},{12,4},{14,6},{1,9},{3,11}... | collective-permute-start | bytes 393224 | tf_op jit(solution)/shard_map/ppermute | solution.py:372
  98.1 3.5 %all-to-all-start.1 = ((f32[16,8,256]{2,1,0:T(8,128)}), f32[16,8,256]{2,1,0:T(8,128)S(1)}, u32[]{:S(2)}, u32[]{:S(2)}) async-start(f32[16,8,256]{2,1,0:T(8,128)} %shard_map.76.refs_0_), calls=%async_computation.1 | async-start | bytes 262144 | tf_op jit(solution)/shard_map/all_to_all | solution.py:492
  101.6 2.9 %collective-permute-done.11.first_taken_ref = f32[1,128,256]{2,1,0:T(8,128)S(1)} collective-permute-done((f32[1,128,256]{2,1,0:T(8,128)S(1)}, f32[1,128,256]{2,1,0:T(8,128)S(1)}, u32[]{:S(2)}, u32[]{:S(2)}) %collective-permute-start.11) | collective-permute-done | bytes 131104 | tf_op jit(solution)/shard_map/ppermute | solution.py:372
  104.6 1.8 %collective-permute-done.13.second_taken_ref = f32[1,128,256]{2,1,0:T(8,128)S(1)} collective-permute-done((f32[1,128,256]{2,1,0:T(8,128)S(1)}, f32[1,128,256]{2,1,0:T(8,128)S(1)}, u32[]{:S(2)}, u32[]{:S(2)}) %collective-permute-start.13) | collective-permute-done | bytes 131104 | tf_op jit(solution)/shard_map/ppermute | solution.py:372
  106.5 3.1 %all-to-all-done.1.sums_ref = f32[16,8,256]{2,1,0:T(8,128)S(1)} async-done(((f32[16,8,256]{2,1,0:T(8,128)}), f32[16,8,256]{2,1,0:T(8,128)S(1)}, u32[]{:S(2)}, u32[]{:S(2)}) %all-to-all-start.1) | async-done | bytes 131104 | tf_op jit(solution)/shard_map/all_to_all | solution.py:492
  (45 shorter events, 14.2 us)
Async XLA Ops:
  0.6 6.7 %copy-start.7 = (s32[32,3]{0,1:T(4,128)S(1)}, s32[32,3]{0,1:T(4,128)}, u32[]{:S(2)}) copy-start(s32[32,3]{0,1:T(4,128)} %param.6) | copy-start | bytes 1156
  3.1 4.2 %collective-permute-start = (f32[512,512]{1,0:T(8,128)S(1)}, f32[512,512]{1,0:T(8,128)S(1)}, u32[]{:S(2)}, u32[]{:S(2)}) collective-permute-start(f32[512,512]{1,0:T(8,128)S(1)} %copy-done.8), channel_id=1, source_target_pairs={{0,1},{1,0},{2,3},{3,2},{4,5},{5,4},{6,7},{7,6},{8,9},{9,8},{10,11... | collective-permute-start | bytes 3145736 | tf_op jit(solution)/shard_map/ppermute | solution.py:372
  3.6 27.5 %collective-permute-start.4 = (f32[512,256]{1,0:T(8,128)S(1)}, f32[512,256]{1,0:T(8,128)S(1)}, u32[]{:S(2)}, u32[]{:S(2)}) collective-permute-start(f32[512,256]{1,0:T(8,128)S(1)} %get-tuple-element.41.direction_ref.values_ref), channel_id=1, source_target_pairs={{0,8},{2,10},{4,12},{6,14},{8,0},{10,2},{12,4},{14,6},{1,9},{3,11}... | collective-permute-start | bytes 1572872 | tf_op jit(solution)/shard_map/ppermute | solution.py:372
  9.1 22.0 %collective-permute-start.1 = (f32[2,128,256]{2,1,0:T(8,128)}, f32[2,128,256]{2,1,0:T(8,128)S(1)}, u32[]{:S(2)}, u32[]{:S(2)}) collective-permute-start(f32[2,128,256]{2,1,0:T(8,128)} %get-tuple-element.51), channel_id=1, source_target_pairs={{0,6},{2,4},{4,2},{6,0},{8,14},{10,12},{12,10},{14,8},{1,7},{3,5},... | collective-permute-start | bytes 786440 | tf_op jit(solution)/shard_map/ppermute | solution.py:372
  11.7 22.8 %collective-permute-start.2 = (f32[2,128,256]{2,1,0:T(8,128)}, f32[2,128,256]{2,1,0:T(8,128)}, u32[]{:S(2)}, u32[]{:S(2)}) collective-permute-start(f32[2,128,256]{2,1,0:T(8,128)} %get-tuple-element.52), channel_id=1, source_target_pairs={{0,4},{2,6},{4,0},{6,2},{8,12},{10,14},{12,8},{14,10},{1,5},{3,7},... | collective-permute-start | bytes 786440 | tf_op jit(solution)/shard_map/ppermute | solution.py:372
  12.2 22.4 %collective-permute-start.3 = (f32[2,128,256]{2,1,0:T(8,128)}, f32[2,128,256]{2,1,0:T(8,128)}, u32[]{:S(2)}, u32[]{:S(2)}) collective-permute-start(f32[2,128,256]{2,1,0:T(8,128)} %get-tuple-element.53), channel_id=1, source_target_pairs={{0,2},{2,0},{4,6},{6,4},{8,10},{10,8},{12,14},{14,12},{1,3},{3,1},... | collective-permute-start | bytes 786440 | tf_op jit(solution)/shard_map/ppermute | solution.py:372
  18.0 20.7 %collective-permute-start.8 = (f32[4,128,256]{2,1,0:T(8,128)S(1)}, f32[4,128,256]{2,1,0:T(8,128)S(1)}, u32[]{:S(2)}, u32[]{:S(2)}) collective-permute-start(f32[4,128,256]{2,1,0:T(8,128)S(1)} %get-tuple-element.56.refs_4_), channel_id=1, source_target_pairs={{0,2},{2,0},{4,6},{6,4},{8,10},{10,8},{12,14},{14,12},{1,3},{3,1},... | collective-permute-start | bytes 1572872 | tf_op jit(solution)/shard_map/ppermute | solution.py:372
  34.6 14.8 %copy-start = (bf16[4,128,512]{2,1,0:T(8,128)(2,1)S(1)}, bf16[4,128,512]{2,1,0:T(8,128)(2,1)}, u32[]{:S(2)}) copy-start(bf16[4,128,512]{2,1,0:T(8,128)(2,1)} %get-tuple-element.44.refs_5_.high_hbm) | copy-start | bytes 1572868
  34.6 14.8 %copy-start.1 = (bf16[4,128,512]{2,1,0:T(8,128)(2,1)S(1)}, bf16[4,128,512]{2,1,0:T(8,128)(2,1)}, u32[]{:S(2)}) copy-start(bf16[4,128,512]{2,1,0:T(8,128)(2,1)} %get-tuple-element.45.refs_6_.low_hbm) | copy-start | bytes 1572868
  34.6 14.8 %copy-start.5 = (f32[512,1]{1,0:T(8,128)S(1)}, f32[512,1]{1,0:T(8,128)}, u32[]{:S(2)}) copy-start(f32[512,1]{1,0:T(8,128)} %get-tuple-element.46.diagonal_hbm) | copy-start | bytes 6148
  35.2 10.3 %collective-permute-start.5 = (f32[2,128,256]{2,1,0:T(8,128)S(1)}, f32[2,128,256]{2,1,0:T(8,128)S(1)}, u32[]{:S(2)}, u32[]{:S(2)}) collective-permute-start(f32[2,128,256]{2,1,0:T(8,128)S(1)} %get-tuple-element.57), channel_id=1, source_target_pairs={{0,6},{2,4},{4,2},{6,0},{8,14},{10,12},{12,10},{14,8},{1,7},{3,5},... | collective-permute-start | bytes 786440 | tf_op jit(solution)/shard_map/ppermute | solution.py:372
  35.3 13.2 %collective-permute-start.6 = (f32[2,128,256]{2,1,0:T(8,128)S(1)}, f32[2,128,256]{2,1,0:T(8,128)S(1)}, u32[]{:S(2)}, u32[]{:S(2)}) collective-permute-start(f32[2,128,256]{2,1,0:T(8,128)S(1)} %get-tuple-element.58), channel_id=1, source_target_pairs={{0,4},{2,6},{4,0},{6,2},{8,12},{10,14},{12,8},{14,10},{1,5},{3,7},... | collective-permute-start | bytes 786440 | tf_op jit(solution)/shard_map/ppermute | solution.py:372
  37.3 12.0 %collective-permute-start.7 = (f32[2,128,256]{2,1,0:T(8,128)S(1)}, f32[2,128,256]{2,1,0:T(8,128)S(1)}, u32[]{:S(2)}, u32[]{:S(2)}) collective-permute-start(f32[2,128,256]{2,1,0:T(8,128)S(1)} %get-tuple-element.59), channel_id=1, source_target_pairs={{0,2},{2,0},{4,6},{6,4},{8,10},{10,8},{12,14},{14,12},{1,3},{3,1},... | collective-permute-start | bytes 786440 | tf_op jit(solution)/shard_map/ppermute | solution.py:372
  54.1 31.8 %copy-start.6 = (f32[4,128,256]{2,1,0:T(8,128)S(1)}, f32[4,128,256]{2,1,0:T(8,128)}, u32[]{:S(2)}) copy-start(f32[4,128,256]{2,1,0:T(8,128)} %get-tuple-element.63.kept_ref) | copy-start | bytes 1572868
  54.1 33.4 %all-to-all-start = ((f32[8,136,256]{2,1,0:T(8,128)}), f32[8,136,256]{2,1,0:T(8,128)S(1)}, u32[]{:S(2)}, u32[]{:S(2)}) async-start(f32[8,136,256]{2,1,0:T(8,128)} %get-tuple-element.62), calls=%async_computation | async-start | bytes 2228224 | tf_op jit(solution)/shard_map/all_to_all | solution.py:479
  60.2 25.7 %collective-permute-start.9 = (f32[4,128,256]{2,1,0:T(8,128)}, f32[4,128,256]{2,1,0:T(8,128)S(1)}, u32[]{:S(2)}, u32[]{:S(2)}) collective-permute-start(f32[4,128,256]{2,1,0:T(8,128)} %get-tuple-element.64), channel_id=1, source_target_pairs={{0,2},{2,0},{4,6},{6,4},{8,10},{10,8},{12,14},{14,12},{1,3},{3,1},... | collective-permute-start | bytes 1572872 | tf_op jit(solution)/shard_map/ppermute | solution.py:372
  62.9 28.4 %collective-permute-start.10 = (f32[2,128,256]{2,1,0:T(8,128)}, f32[2,128,256]{2,1,0:T(8,128)S(1)}, u32[]{:S(2)}, u32[]{:S(2)}) collective-permute-start(f32[2,128,256]{2,1,0:T(8,128)} %get-tuple-element.70), channel_id=1, source_target_pairs={{0,4},{2,6},{4,0},{6,2},{8,12},{10,14},{12,8},{14,10},{1,5},{3,7},... | collective-permute-start | bytes 786440 | tf_op jit(solution)/shard_map/ppermute | solution.py:372
  85.9 8.9 %collective-permute-start.12 = (f32[2,128,256]{2,1,0:T(8,128)S(1)}, f32[2,128,256]{2,1,0:T(8,128)S(1)}, u32[]{:S(2)}, u32[]{:S(2)}) collective-permute-start(f32[2,128,256]{2,1,0:T(8,128)S(1)} %get-tuple-element.65.refs_0_), channel_id=1, source_target_pairs={{0,4},{2,6},{4,0},{6,2},{8,12},{10,14},{12,8},{14,10},{1,5},{3,7},... | collective-permute-start | bytes 786440 | tf_op jit(solution)/shard_map/ppermute | solution.py:372
  91.3 18.2 %copy-start.3 = (f32[512,256]{1,0:T(8,128)S(1)}, f32[512,256]{1,0:T(8,128)}, u32[]{:S(2)}) copy-start(f32[512,256]{1,0:T(8,128)} %get-tuple-element.40.direction_hbm.direction_ref) | copy-start | bytes 1572868
  91.3 18.2 %copy-start.4 = (f32[512,256]{1,0:T(8,128)S(1)}, f32[512,256]{1,0:T(8,128)}, u32[]{:S(2)}) copy-start(f32[512,256]{1,0:T(8,128)} %get-tuple-element.60.scaled_hbm.scaled_ref) | copy-start | bytes 1572868
  92.4 12.2 %collective-permute-start.11 = (f32[1,128,256]{2,1,0:T(8,128)S(1)}, f32[1,128,256]{2,1,0:T(8,128)S(1)}, u32[]{:S(2)}, u32[]{:S(2)}) collective-permute-start(f32[1,128,256]{2,1,0:T(8,128)S(1)} %get-tuple-element.72), channel_id=1, source_target_pairs={{0,8},{2,10},{4,12},{6,14},{8,0},{10,2},{12,4},{14,6},{1,9},{3,11}... | collective-permute-start | bytes 393224 | tf_op jit(solution)/shard_map/ppermute | solution.py:372
  95.7 10.6 %collective-permute-start.13 = (f32[1,128,256]{2,1,0:T(8,128)S(1)}, f32[1,128,256]{2,1,0:T(8,128)S(1)}, u32[]{:S(2)}, u32[]{:S(2)}) collective-permute-start(f32[1,128,256]{2,1,0:T(8,128)S(1)} %get-tuple-element.75), channel_id=1, source_target_pairs={{0,8},{2,10},{4,12},{6,14},{8,0},{10,2},{12,4},{14,6},{1,9},{3,11}... | collective-permute-start | bytes 393224 | tf_op jit(solution)/shard_map/ppermute | solution.py:372
  98.1 11.4 %all-to-all-start.1 = ((f32[16,8,256]{2,1,0:T(8,128)}), f32[16,8,256]{2,1,0:T(8,128)S(1)}, u32[]{:S(2)}, u32[]{:S(2)}) async-start(f32[16,8,256]{2,1,0:T(8,128)} %shard_map.76.refs_0_), calls=%async_computation.1 | async-start | bytes 262144 | tf_op jit(solution)/shard_map/all_to_all | solution.py:492
  106.4 4.0 %collective-permute-start.14 = (f32[2,64,256]{2,1,0:T(8,128)S(1)}, f32[2,64,256]{2,1,0:T(8,128)S(1)}, u32[]{:S(2)}, u32[]{:S(2)}) collective-permute-start(f32[2,64,256]{2,1,0:T(8,128)S(1)} %get-tuple-element.77), channel_id=1, source_target_pairs={{0,1},{1,0},{2,3},{3,2},{4,5},{5,4},{6,7},{7,6},{8,9},{9,8},{10,11... | collective-permute-start | bytes 393224 | tf_op jit(solution)/shard_map/ppermute | solution.py:372
  (2 other events, 3.7 us)

commit v24 on v23

--- a/solution.py
+++ b/solution.py
@@ -12,6 +12,7 @@
 VMEM_LIMIT = 24 * 1024 * 1024
 LARGE_VMEM = 56 * 1024 * 1024
 SUBLANES = 8
+LANES = 128
 
 
 def split(values):
@@ -27,6 +28,10 @@
 def on_diagonal(size):
     rows = lax.broadcasted_iota(jnp.int32, (size, size), 0)
     return rows == lax.broadcasted_iota(jnp.int32, (size, size), 1)
+
+
+def wide(values, columns):
+    return jnp.concatenate([values] * (columns // LANES), axis=1)
 
 
 def split_tiles(kinship_ref, high_ref, low_ref):
@@ -97,7 +102,7 @@
         for position in range(1, positions):
             total = total + kinship_ref[row, position]
         diagonal = jnp.sum(total, axis=1, keepdims=True)
-        diagonal_ref[block, :] = diagonal
+        diagonal_ref[block, :] = jnp.broadcast_to(diagonal, (tile, LANES))
         here = phenotypes_ref[block, :] * (1.0 / diagonal)
         direction_ref[block, :] = here
         norm = norm + column_sums(here * phenotypes_ref[block, :])
@@ -229,7 +234,7 @@
         here = direction_ref[block, :]
         blocks = [here] + [gathered_ref[table_ref[0, row * others + i]] for i in range(others)]
         mapped = product(high_ref[row], low_ref[row], blocks)
-        scaled_ref[block, :] = mapped * (1.0 / diagonal_ref[block, :])
+        scaled_ref[block, :] = mapped * wide(1.0 / diagonal_ref[block, :], mapped.shape[1])
         cross = cross + column_sums(here * mapped)
     row_ids = lax.broadcasted_iota(jnp.int32, cross.shape, 0)
     sums_ref[...] = jnp.where(row_ids == 1, jnp.sum(cross, axis=0, keepdims=True), norm_ref[...])
@@ -276,7 +281,7 @@
             weight = table_ref[2, entry].astype(jnp.float32)
             blocks.append(weight * later_ref[table_ref[1, entry], pl.ds(0, tile), :])
         mapped = product(high_ref[row], low_ref[row], blocks) - rho * handled_ref[block, :]
-        norm = norm + column_sums(here * here * diagonal_ref[block, :])
+        norm = norm + column_sums(here * here * wide(diagonal_ref[block, :], here.shape[1]))
         bend = bend + column_sums(here * mapped)
     row_ids = lax.broadcasted_iota(jnp.int32, first_sums.shape, 0)
     sums = jnp.where(row_ids == 2, jnp.sum(norm, axis=0, keepdims=True), first_sums)
@@ -402,11 +407,11 @@
     full_out = pltpu.HBM((people, columns), jnp.float32)
     direction, direction_kept_hbm, diagonal, norm = call(
         direction_kernel,
-        [full, full_out, pltpu.HBM((people, 1), jnp.float32), float_of(SUBLANES, columns)],
+        [full, full_out, pltpu.HBM((people, LANES), jnp.float32), float_of(SUBLANES, columns)],
         [hbm] * 3,
         [vmem, hbm, hbm, vmem],
         [
-            room(*kinship.shape), room(block_count, tile), full_room, room(people, 1),
+            room(*kinship.shape), room(block_count, tile), full_room, room(people, LANES),
             pltpu.SemaphoreType.DMA((3 * block_count + 2,)),
         ],
     )(
@@ -470,7 +475,7 @@
         [smem, hbm, hbm, hbm] + [vmem] * (devices + 3) + [anywhere],
         [hbm] * 5,
         [
-            room(devices * capacity + block_count, tile, columns), tiles_room, tiles_room, room(people, 1), full_room,
+            room(devices * capacity + block_count, tile, columns), tiles_room, tiles_room, room(people, LANES), full_room,
             full_room, room(SUBLANES, columns), room(*products.shape), room(*products.shape),
             pltpu.SemaphoreType.DMA((2 * devices + 7,)),
         ],
@@ -487,7 +492,7 @@
         float_of(2 * devices, SUBLANES, columns),
         [smem] + [hbm] * 6 + [vmem, anywhere],
         vmem,
-        [tiles_room, tiles_room, full_room, room(people, 1), full_room, full_room, pltpu.SemaphoreType.DMA((6,))],
+        [tiles_room, tiles_room, full_room, room(people, LANES), full_room, full_room, pltpu.SemaphoreType.DMA((6,))],
     )(table, *at_home(high, low, direction_kept_hbm, diagonal, scaled, handled), later, scaled_given)
     all_sums = lax.all_to_all(sums, ("samples", "cols"), split_axis=0, concat_axis=0, tiled=True)
     for step in steps[1:]:

time: 112 us -> 112 us (level)
  no operation moved by 1% of the time
where the time goes in v24:
time: 112 us; the launch traced here: 111 us
  waiting for transfers between devices  52.5 us (47%)
  starting transfers between devices  32.3 us (29%)
  Pallas kernels  21.3 us (19%)
  local copies, waits for them, and re-layouts  4.13 us (4%)
    ppermute x15, waiting for transfers between devices, swap(): return lax.ppermute(values, axis, [(i, i ^ step) for i in range(devices)])  49.4 us
    ppermute x15, starting transfers between devices, swap(): return lax.ppermute(values, axis, [(i, i ^ step) for i in range(devices)])  22.7 us
    all_to_all x1, starting transfers between devices, per_device(): lax.all_to_all(outgoing, 'samples', split_axis=0, concat_axis=0, tiled=True)  6.09 us
    pallas_call x1, Pallas kernels, per_device(): call(functools.partial(apply_kernel, devices, capacity), [full_out, full_...  4.71 us
    pallas_call x1, Pallas kernels, per_device(): call(functools.partial(curvature_kernel, devices), float_of(2 * devices,...  3.83 us
    all_to_all x1, starting transfers between devices, per_device(): lax.all_to_all(sums, ('samples', 'cols'), split_axis=0, concat_axis=0, ti...  3.51 us
    all_to_all x1, waiting for transfers between devices, per_device(): lax.all_to_all(sums, ('samples', 'cols'), split_axis=0, concat_axis=0, ti...  3.05 us
    pallas_call x4, Pallas kernels, add_step(): call(add_kernel, [rows] * 2, [vmem] * (2 + len(gates)), [vmem] * 2)  2.79 us
  transfers between devices with their start and end apart: 17, of which 9 were waited for; matrix products, arithmetic and copies ran while one was open for 3% of the time, Pallas kernels for 12%

profile of v24, /device:TPU:0, one launch (start us, length us, event | category | flops | bytes accessed | tf_op | source)
XLA Modules:
  0.0 111.1 jit_solution(10393457142187512036)
XLA Ops:
  0.7 2.5 %shard_map.68 = (f32[512,256]{1,0:T(8,128)S(1)}, f32[512,256]{1,0:T(8,128)}, f32[512,128]{1,0:T(8,128)}, f32[8,256]{1,0:T(8,128)S(1)}) custom-call(f32[4,4,128,128]{3,2,1,0:T(8,128)} %kinship_hbm.3, f32[4,128]{1,0:T(4,128)} %bitcast.9, f32[512,256]{1,0:T(8,128)} %phenotypes_hbm.1), custom_call_target="tpu_custom_call" | custom-call | tf_op jit(solution)/shard_map/pallas_call | solution.py:408
  3.6 3.7 %collective-permute-start.4 = (f32[512,256]{1,0:T(8,128)S(1)}, f32[512,256]{1,0:T(8,128)S(1)}, u32[]{:S(2)}, u32[]{:S(2)}) collective-permute-start(f32[512,256]{1,0:T(8,128)S(1)} %get-tuple-element.41.direction_ref.values_ref), channel_id=1, source_target_pairs={{0,8},{2,10},{4,12},{6,14},{8,0},{10,2},{12,4},{14,6},{1,9},{3,11}... | collective-permute-start | bytes 1572872 | tf_op jit(solution)/shard_map/ppermute | solution.py:377
  7.3 1.8 %shard_map.69 = (s32[4,12]{1,0:T(4,128)S(1)}, s32[2,4]{1,0:T(2,128)S(1)}, f32[2,128,256]{2,1,0:T(8,128)}, f32[2,128,256]{2,1,0:T(8,128)}, f32[2,128,256]{2,1,0:T(8,128)}) custom-call(s32[3,32]{1,0:T(4,128)S(1)} %bitcast.8, f32[512,256]{1,0:T(8,128)S(1)} %get-tuple-element.41.direction_ref.values_ref, f32[512,512]{1,0:T(8,128)S(1)} %collective-permute-done.gate_ref), custom_call_target="tpu_custom_call" | custom-call | tf_op jit(solution)/shard_map/pallas_call | solution.py:427
  9.1 2.6 %collective-permute-start.1 = (f32[2,128,256]{2,1,0:T(8,128)}, f32[2,128,256]{2,1,0:T(8,128)S(1)}, u32[]{:S(2)}, u32[]{:S(2)}) collective-permute-start(f32[2,128,256]{2,1,0:T(8,128)} %get-tuple-element.51), channel_id=1, source_target_pairs={{0,6},{2,4},{4,2},{6,0},{8,14},{10,12},{12,10},{14,8},{1,7},{3,5},... | collective-permute-start | bytes 786440 | tf_op jit(solution)/shard_map/ppermute | solution.py:377
  12.7 1.6 %copy.7 = f32[512,512]{0,1:T(8,128)S(1)} copy(f32[512,512]{1,0:T(8,128)} %param.9) | data formatting | bytes 2097152 | tf_op jit(solution)/shard_map/optimization_barrier | solution.py:381
  18.0 1.6 %collective-permute-start.8 = (f32[4,128,256]{2,1,0:T(8,128)S(1)}, f32[4,128,256]{2,1,0:T(8,128)S(1)}, u32[]{:S(2)}, u32[]{:S(2)}) collective-permute-start(f32[4,128,256]{2,1,0:T(8,128)S(1)} %get-tuple-element.56.refs_4_), channel_id=1, source_target_pairs={{0,2},{2,0},{4,6},{6,4},{8,10},{10,8},{12,14},{14,12},{1,3},{3,1},... | collective-permute-start | bytes 1572872 | tf_op jit(solution)/shard_map/ppermute | solution.py:377
  19.6 2.3 %shard_map.70 = (bf16[4,128,512]{2,1,0:T(8,128)(2,1)}, bf16[4,128,512]{2,1,0:T(8,128)(2,1)}) custom-call(f32[4,4,128,128]{3,2,1,0:T(8,128)} %kinship_hbm.3), custom_call_target="tpu_custom_call" | custom-call | tf_op jit(solution)/shard_map/pallas_call | solution.py:437
  21.9 9.2 %collective-permute-done.4.partner_ref = f32[512,256]{1,0:T(8,128)S(1)} collective-permute-done((f32[512,256]{1,0:T(8,128)S(1)}, f32[512,256]{1,0:T(8,128)S(1)}, u32[]{:S(2)}, u32[]{:S(2)}) %collective-permute-start.4) | collective-permute-done | bytes 524320 | tf_op jit(solution)/shard_map/ppermute | solution.py:377
  31.2 3.4 %collective-permute-done.2.refs_1_ = f32[2,128,256]{2,1,0:T(8,128)} collective-permute-done((f32[2,128,256]{2,1,0:T(8,128)}, f32[2,128,256]{2,1,0:T(8,128)}, u32[]{:S(2)}, u32[]{:S(2)}) %collective-permute-start.2) | collective-permute-done | bytes 262176 | tf_op jit(solution)/shard_map/ppermute | solution.py:377
  35.3 2.0 %collective-permute-start.6 = (f32[2,128,256]{2,1,0:T(8,128)S(1)}, f32[2,128,256]{2,1,0:T(8,128)S(1)}, u32[]{:S(2)}, u32[]{:S(2)}) collective-permute-start(f32[2,128,256]{2,1,0:T(8,128)S(1)} %get-tuple-element.58), channel_id=1, source_target_pairs={{0,4},{2,6},{4,0},{6,2},{8,12},{10,14},{12,8},{14,10},{1,5},{3,7},... | collective-permute-start | bytes 786440 | tf_op jit(solution)/shard_map/ppermute | solution.py:377
  38.8 6.7 %collective-permute-done.5.refs_3_ = f32[2,128,256]{2,1,0:T(8,128)S(1)} collective-permute-done((f32[2,128,256]{2,1,0:T(8,128)S(1)}, f32[2,128,256]{2,1,0:T(8,128)S(1)}, u32[]{:S(2)}, u32[]{:S(2)}) %collective-permute-start.5) | collective-permute-done | bytes 262176 | tf_op jit(solution)/shard_map/ppermute | solution.py:377
  45.5 3.0 %collective-permute-done.6.refs_4_ = f32[2,128,256]{2,1,0:T(8,128)S(1)} collective-permute-done((f32[2,128,256]{2,1,0:T(8,128)S(1)}, f32[2,128,256]{2,1,0:T(8,128)S(1)}, u32[]{:S(2)}, u32[]{:S(2)}) %collective-permute-start.6) | collective-permute-done | bytes 262176 | tf_op jit(solution)/shard_map/ppermute | solution.py:377
  49.3 4.7 %shard_map.74 = (f32[512,256]{1,0:T(8,128)}, f32[512,256]{1,0:T(8,128)}, f32[8,136,256]{2,1,0:T(8,128)}, f32[4,128,256]{2,1,0:T(8,128)}, f32[4,128,256]{2,1,0:T(8,128)}) custom-call(s32[4,12]{1,0:T(4,128)S(1)} %get-tuple-element.43.table_ref, bf16[4,128,512]{2,1,0:T(8,128)(2,1)S(1)} %copy-done, bf16[4,128,512]{2,1,0:T(8,128)(2,1)S(1)} %copy-done.1, ...), custom_call_target="tpu_custom_call" | custom-call | tf_op jit(solution)/shard_map/pallas_call | solution.py:470
  54.1 6.1 %all-to-all-start = ((f32[8,136,256]{2,1,0:T(8,128)}), f32[8,136,256]{2,1,0:T(8,128)S(1)}, u32[]{:S(2)}, u32[]{:S(2)}) async-start(f32[8,136,256]{2,1,0:T(8,128)} %get-tuple-element.62), calls=%async_computation | async-start | bytes 2228224 | tf_op jit(solution)/shard_map/all_to_all | solution.py:484
  60.2 2.0 %collective-permute-start.9 = (f32[4,128,256]{2,1,0:T(8,128)}, f32[4,128,256]{2,1,0:T(8,128)S(1)}, u32[]{:S(2)}, u32[]{:S(2)}) collective-permute-start(f32[4,128,256]{2,1,0:T(8,128)} %get-tuple-element.64), channel_id=1, source_target_pairs={{0,2},{2,0},{4,6},{6,4},{8,10},{10,8},{12,14},{14,12},{1,3},{3,1},... | collective-permute-start | bytes 1572872 | tf_op jit(solution)/shard_map/ppermute | solution.py:377
  64.4 21.4 %collective-permute-done.9.taken_ref = f32[4,128,256]{2,1,0:T(8,128)S(1)} collective-permute-done((f32[4,128,256]{2,1,0:T(8,128)}, f32[4,128,256]{2,1,0:T(8,128)S(1)}, u32[]{:S(2)}, u32[]{:S(2)}) %collective-permute-start.9) | collective-permute-done | bytes 524320 | tf_op jit(solution)/shard_map/ppermute | solution.py:377
  85.9 1.5 %collective-permute-start.12 = (f32[2,128,256]{2,1,0:T(8,128)S(1)}, f32[2,128,256]{2,1,0:T(8,128)S(1)}, u32[]{:S(2)}, u32[]{:S(2)}) collective-permute-start(f32[2,128,256]{2,1,0:T(8,128)S(1)} %get-tuple-element.65.refs_0_), channel_id=1, source_target_pairs={{0,4},{2,6},{4,0},{6,2},{8,12},{10,14},{12,8},{14,10},{1,5},{3,7},... | collective-permute-start | bytes 786440 | tf_op jit(solution)/shard_map/ppermute | solution.py:377
  87.5 3.8 %shard_map.76.refs_0_ = f32[16,8,256]{2,1,0:T(8,128)} custom-call(s32[4,12]{1,0:T(4,128)S(1)} %get-tuple-element.43.table_ref, bf16[4,128,512]{2,1,0:T(8,128)(2,1)} %get-tuple-element.44.refs_5_.high_hbm, bf16[4,128,512]{2,1,0:T(8,128)(2,1)} %get-tuple-element.45.refs_6_.low_hbm, f32[512,256]{1,0:T(8,128)} %get-tuple-element.40.direction_hbm.direction_ref, ...), custom_call_target="tpu_custom_call" | custom-call | tf_op jit(solution)/shard_map/pallas_call | solution.py:490
  92.4 2.4 %collective-permute-start.11 = (f32[1,128,256]{2,1,0:T(8,128)S(1)}, f32[1,128,256]{2,1,0:T(8,128)S(1)}, u32[]{:S(2)}, u32[]{:S(2)}) collective-permute-start(f32[1,128,256]{2,1,0:T(8,128)S(1)} %get-tuple-element.72), channel_id=1, source_target_pairs={{0,8},{2,10},{4,12},{6,14},{8,0},{10,2},{12,4},{14,6},{1,9},{3,11}... | collective-permute-start | bytes 393224 | tf_op jit(solution)/shard_map/ppermute | solution.py:377
  95.7 2.4 %collective-permute-start.13 = (f32[1,128,256]{2,1,0:T(8,128)S(1)}, f32[1,128,256]{2,1,0:T(8,128)S(1)}, u32[]{:S(2)}, u32[]{:S(2)}) collective-permute-start(f32[1,128,256]{2,1,0:T(8,128)S(1)} %get-tuple-element.75), channel_id=1, source_target_pairs={{0,8},{2,10},{4,12},{6,14},{8,0},{10,2},{12,4},{14,6},{1,9},{3,11}... | collective-permute-start | bytes 393224 | tf_op jit(solution)/shard_map/ppermute | solution.py:377
  98.1 3.5 %all-to-all-start.1 = ((f32[16,8,256]{2,1,0:T(8,128)}), f32[16,8,256]{2,1,0:T(8,128)S(1)}, u32[]{:S(2)}, u32[]{:S(2)}) async-start(f32[16,8,256]{2,1,0:T(8,128)} %shard_map.76.refs_0_), calls=%async_computation.1 | async-start | bytes 262144 | tf_op jit(solution)/shard_map/all_to_all | solution.py:497
  101.6 2.9 %collective-permute-done.11.first_taken_ref = f32[1,128,256]{2,1,0:T(8,128)S(1)} collective-permute-done((f32[1,128,256]{2,1,0:T(8,128)S(1)}, f32[1,128,256]{2,1,0:T(8,128)S(1)}, u32[]{:S(2)}, u32[]{:S(2)}) %collective-permute-start.11) | collective-permute-done | bytes 131104 | tf_op jit(solution)/shard_map/ppermute | solution.py:377
  104.6 1.8 %collective-permute-done.13.second_taken_ref = f32[1,128,256]{2,1,0:T(8,128)S(1)} collective-permute-done((f32[1,128,256]{2,1,0:T(8,128)S(1)}, f32[1,128,256]{2,1,0:T(8,128)S(1)}, u32[]{:S(2)}, u32[]{:S(2)}) %collective-permute-start.13) | collective-permute-done | bytes 131104 | tf_op jit(solution)/shard_map/ppermute | solution.py:377
  106.5 3.1 %all-to-all-done.1.sums_ref = f32[16,8,256]{2,1,0:T(8,128)S(1)} async-done(((f32[16,8,256]{2,1,0:T(8,128)}), f32[16,8,256]{2,1,0:T(8,128)S(1)}, u32[]{:S(2)}, u32[]{:S(2)}) %all-to-all-start.1) | async-done | bytes 131104 | tf_op jit(solution)/shard_map/all_to_all | solution.py:497
  (45 shorter events, 14.2 us)
Async XLA Ops:
  0.6 6.7 %copy-start.7 = (s32[32,3]{0,1:T(4,128)S(1)}, s32[32,3]{0,1:T(4,128)}, u32[]{:S(2)}) copy-start(s32[32,3]{0,1:T(4,128)} %param.6) | copy-start | bytes 1156
  3.1 4.2 %collective-permute-start = (f32[512,512]{1,0:T(8,128)S(1)}, f32[512,512]{1,0:T(8,128)S(1)}, u32[]{:S(2)}, u32[]{:S(2)}) collective-permute-start(f32[512,512]{1,0:T(8,128)S(1)} %copy-done.8), channel_id=1, source_target_pairs={{0,1},{1,0},{2,3},{3,2},{4,5},{5,4},{6,7},{7,6},{8,9},{9,8},{10,11... | collective-permute-start | bytes 3145736 | tf_op jit(solution)/shard_map/ppermute | solution.py:377
  3.6 27.5 %collective-permute-start.4 = (f32[512,256]{1,0:T(8,128)S(1)}, f32[512,256]{1,0:T(8,128)S(1)}, u32[]{:S(2)}, u32[]{:S(2)}) collective-permute-start(f32[512,256]{1,0:T(8,128)S(1)} %get-tuple-element.41.direction_ref.values_ref), channel_id=1, source_target_pairs={{0,8},{2,10},{4,12},{6,14},{8,0},{10,2},{12,4},{14,6},{1,9},{3,11}... | collective-permute-start | bytes 1572872 | tf_op jit(solution)/shard_map/ppermute | solution.py:377
  9.1 22.0 %collective-permute-start.1 = (f32[2,128,256]{2,1,0:T(8,128)}, f32[2,128,256]{2,1,0:T(8,128)S(1)}, u32[]{:S(2)}, u32[]{:S(2)}) collective-permute-start(f32[2,128,256]{2,1,0:T(8,128)} %get-tuple-element.51), channel_id=1, source_target_pairs={{0,6},{2,4},{4,2},{6,0},{8,14},{10,12},{12,10},{14,8},{1,7},{3,5},... | collective-permute-start | bytes 786440 | tf_op jit(solution)/shard_map/ppermute | solution.py:377
  11.7 22.8 %collective-permute-start.2 = (f32[2,128,256]{2,1,0:T(8,128)}, f32[2,128,256]{2,1,0:T(8,128)}, u32[]{:S(2)}, u32[]{:S(2)}) collective-permute-start(f32[2,128,256]{2,1,0:T(8,128)} %get-tuple-element.52), channel_id=1, source_target_pairs={{0,4},{2,6},{4,0},{6,2},{8,12},{10,14},{12,8},{14,10},{1,5},{3,7},... | collective-permute-start | bytes 786440 | tf_op jit(solution)/shard_map/ppermute | solution.py:377
  12.2 22.4 %collective-permute-start.3 = (f32[2,128,256]{2,1,0:T(8,128)}, f32[2,128,256]{2,1,0:T(8,128)}, u32[]{:S(2)}, u32[]{:S(2)}) collective-permute-start(f32[2,128,256]{2,1,0:T(8,128)} %get-tuple-element.53), channel_id=1, source_target_pairs={{0,2},{2,0},{4,6},{6,4},{8,10},{10,8},{12,14},{14,12},{1,3},{3,1},... | collective-permute-start | bytes 786440 | tf_op jit(solution)/shard_map/ppermute | solution.py:377
  18.0 20.7 %collective-permute-start.8 = (f32[4,128,256]{2,1,0:T(8,128)S(1)}, f32[4,128,256]{2,1,0:T(8,128)S(1)}, u32[]{:S(2)}, u32[]{:S(2)}) collective-permute-start(f32[4,128,256]{2,1,0:T(8,128)S(1)} %get-tuple-element.56.refs_4_), channel_id=1, source_target_pairs={{0,2},{2,0},{4,6},{6,4},{8,10},{10,8},{12,14},{14,12},{1,3},{3,1},... | collective-permute-start | bytes 1572872 | tf_op jit(solution)/shard_map/ppermute | solution.py:377
  34.6 14.8 %copy-start = (bf16[4,128,512]{2,1,0:T(8,128)(2,1)S(1)}, bf16[4,128,512]{2,1,0:T(8,128)(2,1)}, u32[]{:S(2)}) copy-start(bf16[4,128,512]{2,1,0:T(8,128)(2,1)} %get-tuple-element.44.refs_5_.high_hbm) | copy-start | bytes 1572868
  34.6 14.8 %copy-start.1 = (bf16[4,128,512]{2,1,0:T(8,128)(2,1)S(1)}, bf16[4,128,512]{2,1,0:T(8,128)(2,1)}, u32[]{:S(2)}) copy-start(bf16[4,128,512]{2,1,0:T(8,128)(2,1)} %get-tuple-element.45.refs_6_.low_hbm) | copy-start | bytes 1572868
  34.6 14.8 %copy-start.5 = (f32[512,128]{1,0:T(8,128)S(1)}, f32[512,128]{1,0:T(8,128)}, u32[]{:S(2)}) copy-start(f32[512,128]{1,0:T(8,128)} %get-tuple-element.46.diagonal_hbm) | copy-start | bytes 786436
  35.2 10.3 %collective-permute-start.5 = (f32[2,128,256]{2,1,0:T(8,128)S(1)}, f32[2,128,256]{2,1,0:T(8,128)S(1)}, u32[]{:S(2)}, u32[]{:S(2)}) collective-permute-start(f32[2,128,256]{2,1,0:T(8,128)S(1)} %get-tuple-element.57), channel_id=1, source_target_pairs={{0,6},{2,4},{4,2},{6,0},{8,14},{10,12},{12,10},{14,8},{1,7},{3,5},... | collective-permute-start | bytes 786440 | tf_op jit(solution)/shard_map/ppermute | solution.py:377
  35.3 13.2 %collective-permute-start.6 = (f32[2,128,256]{2,1,0:T(8,128)S(1)}, f32[2,128,256]{2,1,0:T(8,128)S(1)}, u32[]{:S(2)}, u32[]{:S(2)}) collective-permute-start(f32[2,128,256]{2,1,0:T(8,128)S(1)} %get-tuple-element.58), channel_id=1, source_target_pairs={{0,4},{2,6},{4,0},{6,2},{8,12},{10,14},{12,8},{14,10},{1,5},{3,7},... | collective-permute-start | bytes 786440 | tf_op jit(solution)/shard_map/ppermute | solution.py:377
  37.3 12.0 %collective-permute-start.7 = (f32[2,128,256]{2,1,0:T(8,128)S(1)}, f32[2,128,256]{2,1,0:T(8,128)S(1)}, u32[]{:S(2)}, u32[]{:S(2)}) collective-permute-start(f32[2,128,256]{2,1,0:T(8,128)S(1)} %get-tuple-element.59), channel_id=1, source_target_pairs={{0,2},{2,0},{4,6},{6,4},{8,10},{10,8},{12,14},{14,12},{1,3},{3,1},... | collective-permute-start | bytes 786440 | tf_op jit(solution)/shard_map/ppermute | solution.py:377
  54.1 31.8 %copy-start.6 = (f32[4,128,256]{2,1,0:T(8,128)S(1)}, f32[4,128,256]{2,1,0:T(8,128)}, u32[]{:S(2)}) copy-start(f32[4,128,256]{2,1,0:T(8,128)} %get-tuple-element.63.kept_ref) | copy-start | bytes 1572868
  54.1 33.4 %all-to-all-start = ((f32[8,136,256]{2,1,0:T(8,128)}), f32[8,136,256]{2,1,0:T(8,128)S(1)}, u32[]{:S(2)}, u32[]{:S(2)}) async-start(f32[8,136,256]{2,1,0:T(8,128)} %get-tuple-element.62), calls=%async_computation | async-start | bytes 2228224 | tf_op jit(solution)/shard_map/all_to_all | solution.py:484
  60.2 25.7 %collective-permute-start.9 = (f32[4,128,256]{2,1,0:T(8,128)}, f32[4,128,256]{2,1,0:T(8,128)S(1)}, u32[]{:S(2)}, u32[]{:S(2)}) collective-permute-start(f32[4,128,256]{2,1,0:T(8,128)} %get-tuple-element.64), channel_id=1, source_target_pairs={{0,2},{2,0},{4,6},{6,4},{8,10},{10,8},{12,14},{14,12},{1,3},{3,1},... | collective-permute-start | bytes 1572872 | tf_op jit(solution)/shard_map/ppermute | solution.py:377
  62.9 28.4 %collective-permute-start.10 = (f32[2,128,256]{2,1,0:T(8,128)}, f32[2,128,256]{2,1,0:T(8,128)S(1)}, u32[]{:S(2)}, u32[]{:S(2)}) collective-permute-start(f32[2,128,256]{2,1,0:T(8,128)} %get-tuple-element.70), channel_id=1, source_target_pairs={{0,4},{2,6},{4,0},{6,2},{8,12},{10,14},{12,8},{14,10},{1,5},{3,7},... | collective-permute-start | bytes 786440 | tf_op jit(solution)/shard_map/ppermute | solution.py:377
  85.9 8.9 %collective-permute-start.12 = (f32[2,128,256]{2,1,0:T(8,128)S(1)}, f32[2,128,256]{2,1,0:T(8,128)S(1)}, u32[]{:S(2)}, u32[]{:S(2)}) collective-permute-start(f32[2,128,256]{2,1,0:T(8,128)S(1)} %get-tuple-element.65.refs_0_), channel_id=1, source_target_pairs={{0,4},{2,6},{4,0},{6,2},{8,12},{10,14},{12,8},{14,10},{1,5},{3,7},... | collective-permute-start | bytes 786440 | tf_op jit(solution)/shard_map/ppermute | solution.py:377
  91.3 18.2 %copy-start.3 = (f32[512,256]{1,0:T(8,128)S(1)}, f32[512,256]{1,0:T(8,128)}, u32[]{:S(2)}) copy-start(f32[512,256]{1,0:T(8,128)} %get-tuple-element.40.direction_hbm.direction_ref) | copy-start | bytes 1572868
  91.3 18.2 %copy-start.4 = (f32[512,256]{1,0:T(8,128)S(1)}, f32[512,256]{1,0:T(8,128)}, u32[]{:S(2)}) copy-start(f32[512,256]{1,0:T(8,128)} %get-tuple-element.60.scaled_hbm.scaled_ref) | copy-start | bytes 1572868
  92.4 12.2 %collective-permute-start.11 = (f32[1,128,256]{2,1,0:T(8,128)S(1)}, f32[1,128,256]{2,1,0:T(8,128)S(1)}, u32[]{:S(2)}, u32[]{:S(2)}) collective-permute-start(f32[1,128,256]{2,1,0:T(8,128)S(1)} %get-tuple-element.72), channel_id=1, source_target_pairs={{0,8},{2,10},{4,12},{6,14},{8,0},{10,2},{12,4},{14,6},{1,9},{3,11}... | collective-permute-start | bytes 393224 | tf_op jit(solution)/shard_map/ppermute | solution.py:377
  95.7 10.6 %collective-permute-start.13 = (f32[1,128,256]{2,1,0:T(8,128)S(1)}, f32[1,128,256]{2,1,0:T(8,128)S(1)}, u32[]{:S(2)}, u32[]{:S(2)}) collective-permute-start(f32[1,128,256]{2,1,0:T(8,128)S(1)} %get-tuple-element.75), channel_id=1, source_target_pairs={{0,8},{2,10},{4,12},{6,14},{8,0},{10,2},{12,4},{14,6},{1,9},{3,11}... | collective-permute-start | bytes 393224 | tf_op jit(solution)/shard_map/ppermute | solution.py:377
  98.1 11.4 %all-to-all-start.1 = ((f32[16,8,256]{2,1,0:T(8,128)}), f32[16,8,256]{2,1,0:T(8,128)S(1)}, u32[]{:S(2)}, u32[]{:S(2)}) async-start(f32[16,8,256]{2,1,0:T(8,128)} %shard_map.76.refs_0_), calls=%async_computation.1 | async-start | bytes 262144 | tf_op jit(solution)/shard_map/all_to_all | solution.py:497
  106.4 4.0 %collective-permute-start.14 = (f32[2,64,256]{2,1,0:T(8,128)S(1)}, f32[2,64,256]{2,1,0:T(8,128)S(1)}, u32[]{:S(2)}, u32[]{:S(2)}) collective-permute-start(f32[2,64,256]{2,1,0:T(8,128)S(1)} %get-tuple-element.77), channel_id=1, source_target_pairs={{0,1},{1,0},{2,3},{3,2},{4,5},{5,4},{6,7},{7,6},{8,9},{9,8},{10,11... | collective-permute-start | bytes 393224 | tf_op jit(solution)/shard_map/ppermute | solution.py:377
  (2 other events, 3.7 us)

commit v25 on v24

--- a/solution.py
+++ b/solution.py
@@ -462,9 +462,9 @@
     far = to_mates(call(
         forward_kernel,
         [float_of(capacity, tile, columns)] * (half - 1),
-        [smem, vmem] + [anywhere] * (half + 1) + [hbm] * 2,
+        [smem, vmem] + [anywhere] * 3 + [hbm] * 2,
         [vmem] * (half - 1),
-    )(forward, partner, *near, direction_even, direction_odd, *at_home(high, low)))
+    )(forward, partner, near[0], direction_even, direction_odd, *at_home(high, low)))
     received = near + far + [partner.reshape(block_count, tile, columns)]
     products_out = pltpu.HBM(products.shape, jnp.float32)
     scaled, handled, outgoing, scaled_even, scaled_odd = call(

time: 112 us -> 113 us (level)
  starting transfers between devices: 32.3 us -> 36 us
  waiting for transfers between devices: 52.5 us -> 49.6 us
  local copies, waits for them, and re-layouts: 4.13 us -> 5.57 us
    ppermute x15, waiting for transfers between devices: 49.4 us -> 46.6 us  [swap(): return lax.ppermute(values, axis, [(i, i ^ step) for i in range(devices)])]
    all_to_all x1, starting transfers between devices: 6.09 us -> 8.58 us  [per_device(): lax.all_to_all(outgoing, 'samples', split_axis=0, concat_axis=0, tiled=True)]
    unnamed x18 -> x26, local copies, waits for them, and re-layouts: 1.26 us -> 2.69 us
    ppermute x15, starting transfers between devices: 22.7 us -> 23.9 us  [swap(): return lax.ppermute(values, axis, [(i, i ^ step) for i in range(devices)])]
  transfers between devices with their start and end apart: 17 -> 17, of which waited for: 9 -> 10; matrix products, arithmetic and copies ran while one was open for 3% -> 3% of each run, Pallas kernels for 12% -> 12%
where the time goes in v25:
time: 113 us
  waiting for transfers between devices  49.6 us (44%)
  starting transfers between devices  36 us (32%)
  Pallas kernels  20.8 us (18%)
  local copies, waits for them, and re-layouts  5.57 us (5%)
    ppermute x15, waiting for transfers between devices, swap(): return lax.ppermute(values, axis, [(i, i ^ step) for i in range(devices)])  46.6 us
    ppermute x15, starting transfers between devices, swap(): return lax.ppermute(values, axis, [(i, i ^ step) for i in range(devices)])  23.9 us
    all_to_all x1, starting transfers between devices, per_device(): lax.all_to_all(outgoing, 'samples', split_axis=0, concat_axis=0, tiled=True)  8.58 us
    pallas_call x1, Pallas kernels, per_device(): call(functools.partial(apply_kernel, devices, capacity), [full_out, full_...  4.26 us
    pallas_call x1, Pallas kernels, per_device(): call(functools.partial(curvature_kernel, devices), float_of(2 * devices,...  3.82 us
    all_to_all x1, starting transfers between devices, per_device(): lax.all_to_all(sums, ('samples', 'cols'), split_axis=0, concat_axis=0, ti...  3.51 us
    all_to_all x1, waiting for transfers between devices, per_device(): lax.all_to_all(sums, ('samples', 'cols'), split_axis=0, concat_axis=0, ti...  2.95 us
    pallas_call x4, Pallas kernels, add_step(): call(add_kernel, [rows] * 2, [vmem] * (2 + len(gates)), [vmem] * 2)  2.82 us
  transfers between devices with their start and end apart: 17, of which 10 were waited for; matrix products, arithmetic and copies ran while one was open for 3% of the time, Pallas kernels for 12%

profile of v25, /device:TPU:0, one launch (start us, length us, event | category | flops | bytes accessed | tf_op | source)
XLA Modules:
  0.0 112.8 jit_solution(7802373437507208767)
XLA Ops:
  0.7 2.4 %shard_map.68 = (f32[512,256]{1,0:T(8,128)S(1)}, f32[512,256]{1,0:T(8,128)}, f32[512,128]{1,0:T(8,128)}, f32[8,256]{1,0:T(8,128)S(1)}) custom-call(f32[4,4,128,128]{3,2,1,0:T(8,128)} %kinship_hbm.3, f32[4,128]{1,0:T(4,128)} %bitcast.9, f32[512,256]{1,0:T(8,128)} %phenotypes_hbm.1), custom_call_target="tpu_custom_call" | custom-call | tf_op jit(solution)/shard_map/pallas_call | solution.py:408
  3.6 3.7 %collective-permute-start.4 = (f32[512,256]{1,0:T(8,128)S(1)}, f32[512,256]{1,0:T(8,128)S(1)}, u32[]{:S(2)}, u32[]{:S(2)}) collective-permute-start(f32[512,256]{1,0:T(8,128)S(1)} %get-tuple-element.41.direction_ref.values_ref), channel_id=1, source_target_pairs={{0,8},{2,10},{4,12},{6,14},{8,0},{10,2},{12,4},{14,6},{1,9},{3,11}... | collective-permute-start | bytes 1572872 | tf_op jit(solution)/shard_map/ppermute | solution.py:377
  7.3 1.7 %shard_map.69 = (s32[4,12]{1,0:T(4,128)S(1)}, s32[2,4]{1,0:T(2,128)S(1)}, f32[2,128,256]{2,1,0:T(8,128)S(1)}, f32[2,128,256]{2,1,0:T(8,128)S(1)}, f32[2,128,256]{2,1,0:T(8,128)}) custom-call(s32[3,32]{1,0:T(4,128)S(1)} %bitcast.8, f32[512,256]{1,0:T(8,128)S(1)} %get-tuple-element.41.direction_ref.values_ref, f32[512,512]{1,0:T(8,128)S(1)} %collective-permute-done.gate_ref), custom_call_target="tpu_custom_call" | custom-call | tf_op jit(solution)/shard_map/pallas_call | solution.py:427
  10.5 2.5 %collective-permute-start.1 = (f32[2,128,256]{2,1,0:T(8,128)}, f32[2,128,256]{2,1,0:T(8,128)S(1)}, u32[]{:S(2)}, u32[]{:S(2)}) collective-permute-start(f32[2,128,256]{2,1,0:T(8,128)} %get-tuple-element.51), channel_id=1, source_target_pairs={{0,6},{2,4},{4,2},{6,0},{8,14},{10,12},{12,10},{14,8},{1,7},{3,5},... | collective-permute-start | bytes 786440 | tf_op jit(solution)/shard_map/ppermute | solution.py:377
  13.0 1.6 %copy.7 = f32[512,512]{0,1:T(8,128)S(1)} copy(f32[512,512]{1,0:T(8,128)} %param.9) | data formatting | bytes 2097152 | tf_op jit(solution)/shard_map/optimization_barrier | solution.py:381
  19.4 2.3 %shard_map.70 = (bf16[4,128,512]{2,1,0:T(8,128)(2,1)}, bf16[4,128,512]{2,1,0:T(8,128)(2,1)}) custom-call(f32[4,4,128,128]{3,2,1,0:T(8,128)} %kinship_hbm.3), custom_call_target="tpu_custom_call" | custom-call | tf_op jit(solution)/shard_map/pallas_call | solution.py:437
  21.7 1.6 %collective-permute-start.3 = (f32[2,128,256]{2,1,0:T(8,128)S(1)}, f32[2,128,256]{2,1,0:T(8,128)S(1)}, u32[]{:S(2)}, u32[]{:S(2)}) collective-permute-start(f32[2,128,256]{2,1,0:T(8,128)S(1)} %copy-done.9), channel_id=1, source_target_pairs={{0,2},{2,0},{4,6},{6,4},{8,10},{10,8},{12,14},{14,12},{1,3},{3,1},... | collective-permute-start | bytes 786440 | tf_op jit(solution)/shard_map/ppermute | solution.py:377
  23.3 7.8 %collective-permute-done.4.partner_ref = f32[512,256]{1,0:T(8,128)S(1)} collective-permute-done((f32[512,256]{1,0:T(8,128)S(1)}, f32[512,256]{1,0:T(8,128)S(1)}, u32[]{:S(2)}, u32[]{:S(2)}) %collective-permute-start.4) | collective-permute-done | bytes 524320 | tf_op jit(solution)/shard_map/ppermute | solution.py:377
  31.8 1.7 %collective-permute-start.5 = (f32[2,128,256]{2,1,0:T(8,128)S(1)}, f32[2,128,256]{2,1,0:T(8,128)S(1)}, u32[]{:S(2)}, u32[]{:S(2)}) collective-permute-start(f32[2,128,256]{2,1,0:T(8,128)S(1)} %get-tuple-element.57), channel_id=1, source_target_pairs={{0,6},{2,4},{4,2},{6,0},{8,14},{10,12},{12,10},{14,8},{1,7},{3,5},... | collective-permute-start | bytes 786440 | tf_op jit(solution)/shard_map/ppermute | solution.py:377
  34.9 1.9 %collective-permute-done.2.refs_1_ = f32[2,128,256]{2,1,0:T(8,128)S(1)} collective-permute-done((f32[2,128,256]{2,1,0:T(8,128)S(1)}, f32[2,128,256]{2,1,0:T(8,128)S(1)}, u32[]{:S(2)}, u32[]{:S(2)}) %collective-permute-start.2) | collective-permute-done | bytes 262176 | tf_op jit(solution)/shard_map/ppermute | solution.py:377
  36.8 1.6 %collective-permute-start.7 = (f32[2,128,256]{2,1,0:T(8,128)S(1)}, f32[2,128,256]{2,1,0:T(8,128)S(1)}, u32[]{:S(2)}, u32[]{:S(2)}) collective-permute-start(f32[2,128,256]{2,1,0:T(8,128)S(1)} %get-tuple-element.59), channel_id=1, source_target_pairs={{0,2},{2,0},{4,6},{6,4},{8,10},{10,8},{12,14},{14,12},{1,3},{3,1},... | collective-permute-start | bytes 786440 | tf_op jit(solution)/shard_map/ppermute | solution.py:377
  38.3 5.0 %collective-permute-done.3.refs_2_ = f32[2,128,256]{2,1,0:T(8,128)S(1)} collective-permute-done((f32[2,128,256]{2,1,0:T(8,128)S(1)}, f32[2,128,256]{2,1,0:T(8,128)S(1)}, u32[]{:S(2)}, u32[]{:S(2)}) %collective-permute-start.3) | collective-permute-done | bytes 262176 | tf_op jit(solution)/shard_map/ppermute | solution.py:377
  43.4 4.4 %collective-permute-done.6.refs_4_ = f32[2,128,256]{2,1,0:T(8,128)S(1)} collective-permute-done((f32[2,128,256]{2,1,0:T(8,128)S(1)}, f32[2,128,256]{2,1,0:T(8,128)S(1)}, u32[]{:S(2)}, u32[]{:S(2)}) %collective-permute-start.6) | collective-permute-done | bytes 262176 | tf_op jit(solution)/shard_map/ppermute | solution.py:377
  49.0 4.3 %shard_map.74 = (f32[512,256]{1,0:T(8,128)}, f32[512,256]{1,0:T(8,128)}, f32[8,136,256]{2,1,0:T(8,128)}, f32[4,128,256]{2,1,0:T(8,128)}, f32[4,128,256]{2,1,0:T(8,128)}) custom-call(s32[4,12]{1,0:T(4,128)S(1)} %get-tuple-element.43.table_ref, bf16[4,128,512]{2,1,0:T(8,128)(2,1)S(1)} %copy-done, bf16[4,128,512]{2,1,0:T(8,128)(2,1)S(1)} %copy-done.1, ...), custom_call_target="tpu_custom_call" | custom-call | tf_op jit(solution)/shard_map/pallas_call | solution.py:470
  53.3 8.6 %all-to-all-start = ((f32[8,136,256]{2,1,0:T(8,128)}), f32[8,136,256]{2,1,0:T(8,128)S(1)}, u32[]{:S(2)}, u32[]{:S(2)}) async-start(f32[8,136,256]{2,1,0:T(8,128)} %get-tuple-element.62), calls=%async_computation | async-start | bytes 2228224 | tf_op jit(solution)/shard_map/all_to_all | solution.py:484
  61.9 2.0 %collective-permute-start.9 = (f32[4,128,256]{2,1,0:T(8,128)}, f32[4,128,256]{2,1,0:T(8,128)S(1)}, u32[]{:S(2)}, u32[]{:S(2)}) collective-permute-start(f32[4,128,256]{2,1,0:T(8,128)} %get-tuple-element.64), channel_id=1, source_target_pairs={{0,2},{2,0},{4,6},{6,4},{8,10},{10,8},{12,14},{14,12},{1,3},{3,1},... | collective-permute-start | bytes 1572872 | tf_op jit(solution)/shard_map/ppermute | solution.py:377
  66.1 21.4 %collective-permute-done.9.taken_ref = f32[4,128,256]{2,1,0:T(8,128)S(1)} collective-permute-done((f32[4,128,256]{2,1,0:T(8,128)}, f32[4,128,256]{2,1,0:T(8,128)S(1)}, u32[]{:S(2)}, u32[]{:S(2)}) %collective-permute-start.9) | collective-permute-done | bytes 524320 | tf_op jit(solution)/shard_map/ppermute | solution.py:377
  89.2 3.8 %shard_map.76.refs_0_ = f32[16,8,256]{2,1,0:T(8,128)} custom-call(s32[4,12]{1,0:T(4,128)S(1)} %get-tuple-element.43.table_ref, bf16[4,128,512]{2,1,0:T(8,128)(2,1)} %get-tuple-element.44.refs_3_.high_hbm, bf16[4,128,512]{2,1,0:T(8,128)(2,1)} %get-tuple-element.45.refs_4_.low_hbm, f32[512,256]{1,0:T(8,128)} %get-tuple-element.40.direction_hbm.direction_ref, ...), custom_call_target="tpu_custom_call" | custom-call | tf_op jit(solution)/shard_map/pallas_call | solution.py:490
  94.1 2.4 %collective-permute-start.11 = (f32[1,128,256]{2,1,0:T(8,128)S(1)}, f32[1,128,256]{2,1,0:T(8,128)S(1)}, u32[]{:S(2)}, u32[]{:S(2)}) collective-permute-start(f32[1,128,256]{2,1,0:T(8,128)S(1)} %get-tuple-element.72), channel_id=1, source_target_pairs={{0,8},{2,10},{4,12},{6,14},{8,0},{10,2},{12,4},{14,6},{1,9},{3,11}... | collective-permute-start | bytes 393224 | tf_op jit(solution)/shard_map/ppermute | solution.py:377
  97.5 2.4 %collective-permute-start.13 = (f32[1,128,256]{2,1,0:T(8,128)S(1)}, f32[1,128,256]{2,1,0:T(8,128)S(1)}, u32[]{:S(2)}, u32[]{:S(2)}) collective-permute-start(f32[1,128,256]{2,1,0:T(8,128)S(1)} %get-tuple-element.75), channel_id=1, source_target_pairs={{0,8},{2,10},{4,12},{6,14},{8,0},{10,2},{12,4},{14,6},{1,9},{3,11}... | collective-permute-start | bytes 393224 | tf_op jit(solution)/shard_map/ppermute | solution.py:377
  99.9 3.5 %all-to-all-start.1 = ((f32[16,8,256]{2,1,0:T(8,128)}), f32[16,8,256]{2,1,0:T(8,128)S(1)}, u32[]{:S(2)}, u32[]{:S(2)}) async-start(f32[16,8,256]{2,1,0:T(8,128)} %shard_map.76.refs_0_), calls=%async_computation.1 | async-start | bytes 262144 | tf_op jit(solution)/shard_map/all_to_all | solution.py:497
  103.4 2.9 %collective-permute-done.11.first_taken_ref = f32[1,128,256]{2,1,0:T(8,128)S(1)} collective-permute-done((f32[1,128,256]{2,1,0:T(8,128)S(1)}, f32[1,128,256]{2,1,0:T(8,128)S(1)}, u32[]{:S(2)}, u32[]{:S(2)}) %collective-permute-start.11) | collective-permute-done | bytes 131104 | tf_op jit(solution)/shard_map/ppermute | solution.py:377
  106.3 1.9 %collective-permute-done.13.second_taken_ref = f32[1,128,256]{2,1,0:T(8,128)S(1)} collective-permute-done((f32[1,128,256]{2,1,0:T(8,128)S(1)}, f32[1,128,256]{2,1,0:T(8,128)S(1)}, u32[]{:S(2)}, u32[]{:S(2)}) %collective-permute-start.13) | collective-permute-done | bytes 131104 | tf_op jit(solution)/shard_map/ppermute | solution.py:377
  108.3 2.9 %all-to-all-done.1.sums_ref = f32[16,8,256]{2,1,0:T(8,128)S(1)} async-done(((f32[16,8,256]{2,1,0:T(8,128)}), f32[16,8,256]{2,1,0:T(8,128)S(1)}, u32[]{:S(2)}, u32[]{:S(2)}) %all-to-all-start.1) | async-done | bytes 131104 | tf_op jit(solution)/shard_map/all_to_all | solution.py:497
  (53 shorter events, 17.5 us)
Async XLA Ops:
  0.6 6.7 %copy-start.7 = (s32[32,3]{0,1:T(4,128)S(1)}, s32[32,3]{0,1:T(4,128)}, u32[]{:S(2)}) copy-start(s32[32,3]{0,1:T(4,128)} %param.6) | copy-start | bytes 1156
  3.1 4.2 %collective-permute-start = (f32[512,512]{1,0:T(8,128)S(1)}, f32[512,512]{1,0:T(8,128)S(1)}, u32[]{:S(2)}, u32[]{:S(2)}) collective-permute-start(f32[512,512]{1,0:T(8,128)S(1)} %copy-done.12), channel_id=1, source_target_pairs={{0,1},{1,0},{2,3},{3,2},{4,5},{5,4},{6,7},{7,6},{8,9},{9,8},{10,11... | collective-permute-start | bytes 3145736 | tf_op jit(solution)/shard_map/ppermute | solution.py:377
  3.6 27.5 %collective-permute-start.4 = (f32[512,256]{1,0:T(8,128)S(1)}, f32[512,256]{1,0:T(8,128)S(1)}, u32[]{:S(2)}, u32[]{:S(2)}) collective-permute-start(f32[512,256]{1,0:T(8,128)S(1)} %get-tuple-element.41.direction_ref.values_ref), channel_id=1, source_target_pairs={{0,8},{2,10},{4,12},{6,14},{8,0},{10,2},{12,4},{14,6},{1,9},{3,11}... | collective-permute-start | bytes 1572872 | tf_op jit(solution)/shard_map/ppermute | solution.py:377
  10.5 20.7 %collective-permute-start.1 = (f32[2,128,256]{2,1,0:T(8,128)}, f32[2,128,256]{2,1,0:T(8,128)S(1)}, u32[]{:S(2)}, u32[]{:S(2)}) collective-permute-start(f32[2,128,256]{2,1,0:T(8,128)} %get-tuple-element.51), channel_id=1, source_target_pairs={{0,6},{2,4},{4,2},{6,0},{8,14},{10,12},{12,10},{14,8},{1,7},{3,5},... | collective-permute-start | bytes 786440 | tf_op jit(solution)/shard_map/ppermute | solution.py:377
  18.4 25.0 %collective-permute-start.8 = (f32[4,128,256]{2,1,0:T(8,128)S(1)}, f32[4,128,256]{2,1,0:T(8,128)S(1)}, u32[]{:S(2)}, u32[]{:S(2)}) collective-permute-start(f32[4,128,256]{2,1,0:T(8,128)S(1)} %get-tuple-element.56.refs_2_), channel_id=1, source_target_pairs={{0,2},{2,0},{4,6},{6,4},{8,10},{10,8},{12,14},{14,12},{1,3},{3,1},... | collective-permute-start | bytes 1572872 | tf_op jit(solution)/shard_map/ppermute | solution.py:377
  18.9 17.8 %collective-permute-start.2 = (f32[2,128,256]{2,1,0:T(8,128)S(1)}, f32[2,128,256]{2,1,0:T(8,128)S(1)}, u32[]{:S(2)}, u32[]{:S(2)}) collective-permute-start(f32[2,128,256]{2,1,0:T(8,128)S(1)} %copy-done.11), channel_id=1, source_target_pairs={{0,4},{2,6},{4,0},{6,2},{8,12},{10,14},{12,8},{14,10},{1,5},{3,7},... | collective-permute-start | bytes 786440 | tf_op jit(solution)/shard_map/ppermute | solution.py:377
  21.7 21.6 %collective-permute-start.3 = (f32[2,128,256]{2,1,0:T(8,128)S(1)}, f32[2,128,256]{2,1,0:T(8,128)S(1)}, u32[]{:S(2)}, u32[]{:S(2)}) collective-permute-start(f32[2,128,256]{2,1,0:T(8,128)S(1)} %copy-done.9), channel_id=1, source_target_pairs={{0,2},{2,0},{4,6},{6,4},{8,10},{10,8},{12,14},{14,12},{1,3},{3,1},... | collective-permute-start | bytes 786440 | tf_op jit(solution)/shard_map/ppermute | solution.py:377
  31.2 17.8 %copy-start = (bf16[4,128,512]{2,1,0:T(8,128)(2,1)S(1)}, bf16[4,128,512]{2,1,0:T(8,128)(2,1)}, u32[]{:S(2)}) copy-start(bf16[4,128,512]{2,1,0:T(8,128)(2,1)} %get-tuple-element.44.refs_3_.high_hbm) | copy-start | bytes 1572868
  31.2 17.8 %copy-start.1 = (bf16[4,128,512]{2,1,0:T(8,128)(2,1)S(1)}, bf16[4,128,512]{2,1,0:T(8,128)(2,1)}, u32[]{:S(2)}) copy-start(bf16[4,128,512]{2,1,0:T(8,128)(2,1)} %get-tuple-element.45.refs_4_.low_hbm) | copy-start | bytes 1572868
  31.2 17.8 %copy-start.5 = (f32[512,128]{1,0:T(8,128)S(1)}, f32[512,128]{1,0:T(8,128)}, u32[]{:S(2)}) copy-start(f32[512,128]{1,0:T(8,128)} %get-tuple-element.46.diagonal_hbm) | copy-start | bytes 786436
  31.8 11.7 %collective-permute-start.5 = (f32[2,128,256]{2,1,0:T(8,128)S(1)}, f32[2,128,256]{2,1,0:T(8,128)S(1)}, u32[]{:S(2)}, u32[]{:S(2)}) collective-permute-start(f32[2,128,256]{2,1,0:T(8,128)S(1)} %get-tuple-element.57), channel_id=1, source_target_pairs={{0,6},{2,4},{4,2},{6,0},{8,14},{10,12},{12,10},{14,8},{1,7},{3,5},... | collective-permute-start | bytes 786440 | tf_op jit(solution)/shard_map/ppermute | solution.py:377
  33.5 14.3 %collective-permute-start.6 = (f32[2,128,256]{2,1,0:T(8,128)S(1)}, f32[2,128,256]{2,1,0:T(8,128)S(1)}, u32[]{:S(2)}, u32[]{:S(2)}) collective-permute-start(f32[2,128,256]{2,1,0:T(8,128)S(1)} %get-tuple-element.58), channel_id=1, source_target_pairs={{0,4},{2,6},{4,0},{6,2},{8,12},{10,14},{12,8},{14,10},{1,5},{3,7},... | collective-permute-start | bytes 786440 | tf_op jit(solution)/shard_map/ppermute | solution.py:377
  36.8 12.2 %collective-permute-start.7 = (f32[2,128,256]{2,1,0:T(8,128)S(1)}, f32[2,128,256]{2,1,0:T(8,128)S(1)}, u32[]{:S(2)}, u32[]{:S(2)}) collective-permute-start(f32[2,128,256]{2,1,0:T(8,128)S(1)} %get-tuple-element.59), channel_id=1, source_target_pairs={{0,2},{2,0},{4,6},{6,4},{8,10},{10,8},{12,14},{14,12},{1,3},{3,1},... | collective-permute-start | bytes 786440 | tf_op jit(solution)/shard_map/ppermute | solution.py:377
  53.3 34.3 %copy-start.6 = (f32[4,128,256]{2,1,0:T(8,128)S(1)}, f32[4,128,256]{2,1,0:T(8,128)}, u32[]{:S(2)}) copy-start(f32[4,128,256]{2,1,0:T(8,128)} %get-tuple-element.63.kept_ref) | copy-start | bytes 1572868
  53.3 35.9 %all-to-all-start = ((f32[8,136,256]{2,1,0:T(8,128)}), f32[8,136,256]{2,1,0:T(8,128)S(1)}, u32[]{:S(2)}, u32[]{:S(2)}) async-start(f32[8,136,256]{2,1,0:T(8,128)} %get-tuple-element.62), calls=%async_computation | async-start | bytes 2228224 | tf_op jit(solution)/shard_map/all_to_all | solution.py:484
  61.9 25.7 %collective-permute-start.9 = (f32[4,128,256]{2,1,0:T(8,128)}, f32[4,128,256]{2,1,0:T(8,128)S(1)}, u32[]{:S(2)}, u32[]{:S(2)}) collective-permute-start(f32[4,128,256]{2,1,0:T(8,128)} %get-tuple-element.64), channel_id=1, source_target_pairs={{0,2},{2,0},{4,6},{6,4},{8,10},{10,8},{12,14},{14,12},{1,3},{3,1},... | collective-permute-start | bytes 1572872 | tf_op jit(solution)/shard_map/ppermute | solution.py:377
  64.7 28.4 %collective-permute-start.10 = (f32[2,128,256]{2,1,0:T(8,128)}, f32[2,128,256]{2,1,0:T(8,128)S(1)}, u32[]{:S(2)}, u32[]{:S(2)}) collective-permute-start(f32[2,128,256]{2,1,0:T(8,128)} %get-tuple-element.70), channel_id=1, source_target_pairs={{0,4},{2,6},{4,0},{6,2},{8,12},{10,14},{12,8},{14,10},{1,5},{3,7},... | collective-permute-start | bytes 786440 | tf_op jit(solution)/shard_map/ppermute | solution.py:377
  87.7 8.9 %collective-permute-start.12 = (f32[2,128,256]{2,1,0:T(8,128)S(1)}, f32[2,128,256]{2,1,0:T(8,128)S(1)}, u32[]{:S(2)}, u32[]{:S(2)}) collective-permute-start(f32[2,128,256]{2,1,0:T(8,128)S(1)} %get-tuple-element.65.refs_0_), channel_id=1, source_target_pairs={{0,4},{2,6},{4,0},{6,2},{8,12},{10,14},{12,8},{14,10},{1,5},{3,7},... | collective-permute-start | bytes 786440 | tf_op jit(solution)/shard_map/ppermute | solution.py:377
  93.1 18.2 %copy-start.3 = (f32[512,256]{1,0:T(8,128)S(1)}, f32[512,256]{1,0:T(8,128)}, u32[]{:S(2)}) copy-start(f32[512,256]{1,0:T(8,128)} %get-tuple-element.40.direction_hbm.direction_ref) | copy-start | bytes 1572868
  93.1 18.2 %copy-start.4 = (f32[512,256]{1,0:T(8,128)S(1)}, f32[512,256]{1,0:T(8,128)}, u32[]{:S(2)}) copy-start(f32[512,256]{1,0:T(8,128)} %get-tuple-element.60.scaled_hbm.scaled_ref) | copy-start | bytes 1572868
  94.1 12.2 %collective-permute-start.11 = (f32[1,128,256]{2,1,0:T(8,128)S(1)}, f32[1,128,256]{2,1,0:T(8,128)S(1)}, u32[]{:S(2)}, u32[]{:S(2)}) collective-permute-start(f32[1,128,256]{2,1,0:T(8,128)S(1)} %get-tuple-element.72), channel_id=1, source_target_pairs={{0,8},{2,10},{4,12},{6,14},{8,0},{10,2},{12,4},{14,6},{1,9},{3,11}... | collective-permute-start | bytes 393224 | tf_op jit(solution)/shard_map/ppermute | solution.py:377
  97.5 10.8 %collective-permute-start.13 = (f32[1,128,256]{2,1,0:T(8,128)S(1)}, f32[1,128,256]{2,1,0:T(8,128)S(1)}, u32[]{:S(2)}, u32[]{:S(2)}) collective-permute-start(f32[1,128,256]{2,1,0:T(8,128)S(1)} %get-tuple-element.75), channel_id=1, source_target_pairs={{0,8},{2,10},{4,12},{6,14},{8,0},{10,2},{12,4},{14,6},{1,9},{3,11}... | collective-permute-start | bytes 393224 | tf_op jit(solution)/shard_map/ppermute | solution.py:377
  99.9 11.4 %all-to-all-start.1 = ((f32[16,8,256]{2,1,0:T(8,128)}), f32[16,8,256]{2,1,0:T(8,128)S(1)}, u32[]{:S(2)}, u32[]{:S(2)}) async-start(f32[16,8,256]{2,1,0:T(8,128)} %shard_map.76.refs_0_), calls=%async_computation.1 | async-start | bytes 262144 | tf_op jit(solution)/shard_map/all_to_all | solution.py:497
  108.3 3.9 %collective-permute-start.14 = (f32[2,64,256]{2,1,0:T(8,128)S(1)}, f32[2,64,256]{2,1,0:T(8,128)S(1)}, u32[]{:S(2)}, u32[]{:S(2)}) collective-permute-start(f32[2,64,256]{2,1,0:T(8,128)S(1)} %get-tuple-element.77), channel_id=1, source_target_pairs={{0,1},{1,0},{2,3},{3,2},{4,5},{5,4},{6,7},{7,6},{8,9},{9,8},{10,11... | collective-permute-start | bytes 393224 | tf_op jit(solution)/shard_map/ppermute | solution.py:377
  (6 other events, 11.1 us)

commit v26 on v24

--- a/solution.py
+++ b/solution.py
@@ -256,13 +256,13 @@
     wait_all(stores)
 
 
-def curvature_kernel(devices, table_ref, high_hbm, low_hbm, direction_hbm, diagonal_hbm, scaled_hbm, handled_hbm,
+def curvature_kernel(devices, table_ref, high_ref, low_ref, direction_hbm, diagonal_hbm, scaled_hbm, handled_hbm,
                      later_ref, *refs):
-    sums_ref, high_ref, low_ref, direction_ref, diagonal_ref, scaled_ref, handled_ref, semaphores = refs[-8:]
+    sums_ref, direction_ref, diagonal_ref, scaled_ref, handled_ref, semaphores = refs[-6:]
     block_count, tile, depth = high_ref.shape
     copies = Copies(semaphores)
     wait_all([copies.start(source, target) for source, target in (
-        (scaled_hbm, scaled_ref), (direction_hbm, direction_ref), (high_hbm, high_ref), (low_hbm, low_ref),
+        (scaled_hbm, scaled_ref), (direction_hbm, direction_ref),
         (handled_hbm, handled_ref), (diagonal_hbm, diagonal_ref),
     )])
     others = depth // tile - 1
@@ -490,10 +490,10 @@
     sums = call(
         functools.partial(curvature_kernel, devices),
         float_of(2 * devices, SUBLANES, columns),
-        [smem] + [hbm] * 6 + [vmem, anywhere],
+        [smem, vmem, vmem] + [hbm] * 4 + [vmem, anywhere],
         vmem,
-        [tiles_room, tiles_room, full_room, room(people, LANES), full_room, full_room, pltpu.SemaphoreType.DMA((6,))],
-    )(table, *at_home(high, low, direction_kept_hbm, diagonal, scaled, handled), later, scaled_given)
+        [full_room, room(people, LANES), full_room, full_room, pltpu.SemaphoreType.DMA((4,))],
+    )(table, high, low, *at_home(direction_kept_hbm, diagonal, scaled, handled), later, scaled_given)
     all_sums = lax.all_to_all(sums, ("samples", "cols"), split_axis=0, concat_axis=0, tiled=True)
     for step in steps[1:]:
         scaled_kept, scaled_given = add_step(scaled_kept, scaled_taken, sums)

time: 112 us -> 113 us (level)
  no operation moved by 1% of the time
where the time goes in v26:
time: 113 us; the launch traced here: 112 us
  waiting for transfers between devices  52.4 us (46%)
  starting transfers between devices  33.2 us (29%)
  Pallas kernels  21.7 us (19%)
  local copies, waits for them, and re-layouts  4.15 us (4%)
    ppermute x15, waiting for transfers between devices, swap(): return lax.ppermute(values, axis, [(i, i ^ step) for i in range(devices)])  48.3 us
    ppermute x15, starting transfers between devices, swap(): return lax.ppermute(values, axis, [(i, i ^ step) for i in range(devices)])  23.6 us
    all_to_all x1, starting transfers between devices, per_device(): lax.all_to_all(outgoing, 'samples', split_axis=0, concat_axis=0, tiled=True)  6.09 us
    pallas_call x1, Pallas kernels, per_device(): call(functools.partial(apply_kernel, devices, capacity), [full_out, full_...  4.68 us
    all_to_all x1, waiting for transfers between devices, per_device(): lax.all_to_all(sums, ('samples', 'cols'), split_axis=0, concat_axis=0, ti...  4.11 us
    pallas_call x4, Pallas kernels, add_step(): call(add_kernel, [rows] * 2, [vmem] * (2 + len(gates)), [vmem] * 2)  3.56 us
    all_to_all x1, starting transfers between devices, per_device(): lax.all_to_all(sums, ('samples', 'cols'), split_axis=0, concat_axis=0, ti...  3.51 us
    pallas_call x1, Pallas kernels, per_device(): call(functools.partial(curvature_kernel, devices), float_of(2 * devices,...  3.48 us
  transfers between devices with their start and end apart: 17, of which 9 were waited for; matrix products, arithmetic and copies ran while one was open for 3% of the time, Pallas kernels for 12%

profile of v26, /device:TPU:0, one launch (start us, length us, event | category | flops | bytes accessed | tf_op | source)
XLA Modules:
  0.0 112.3 jit_solution(12357966539080836976)
XLA Ops:
  0.7 2.4 %shard_map.68 = (f32[512,256]{1,0:T(8,128)S(1)}, f32[512,256]{1,0:T(8,128)}, f32[512,128]{1,0:T(8,128)}, f32[8,256]{1,0:T(8,128)S(1)}) custom-call(f32[4,4,128,128]{3,2,1,0:T(8,128)} %kinship_hbm.3, f32[4,128]{1,0:T(4,128)} %bitcast.9, f32[512,256]{1,0:T(8,128)} %phenotypes_hbm.1), custom_call_target="tpu_custom_call" | custom-call | tf_op jit(solution)/shard_map/pallas_call | solution.py:408
  3.6 3.7 %collective-permute-start.4 = (f32[512,256]{1,0:T(8,128)S(1)}, f32[512,256]{1,0:T(8,128)S(1)}, u32[]{:S(2)}, u32[]{:S(2)}) collective-permute-start(f32[512,256]{1,0:T(8,128)S(1)} %get-tuple-element.41.direction_ref.values_ref), channel_id=1, source_target_pairs={{0,8},{2,10},{4,12},{6,14},{8,0},{10,2},{12,4},{14,6},{1,9},{3,11}... | collective-permute-start | bytes 1572872 | tf_op jit(solution)/shard_map/ppermute | solution.py:377
  7.3 1.8 %shard_map.69 = (s32[4,12]{1,0:T(4,128)S(1)}, s32[2,4]{1,0:T(2,128)S(1)}, f32[2,128,256]{2,1,0:T(8,128)}, f32[2,128,256]{2,1,0:T(8,128)}, f32[2,128,256]{2,1,0:T(8,128)}) custom-call(s32[3,32]{1,0:T(4,128)S(1)} %bitcast.8, f32[512,256]{1,0:T(8,128)S(1)} %get-tuple-element.41.direction_ref.values_ref, f32[512,512]{1,0:T(8,128)S(1)} %collective-permute-done.gate_ref), custom_call_target="tpu_custom_call" | custom-call | tf_op jit(solution)/shard_map/pallas_call | solution.py:427
  9.1 2.6 %collective-permute-start.1 = (f32[2,128,256]{2,1,0:T(8,128)}, f32[2,128,256]{2,1,0:T(8,128)S(1)}, u32[]{:S(2)}, u32[]{:S(2)}) collective-permute-start(f32[2,128,256]{2,1,0:T(8,128)} %get-tuple-element.51), channel_id=1, source_target_pairs={{0,6},{2,4},{4,2},{6,0},{8,14},{10,12},{12,10},{14,8},{1,7},{3,5},... | collective-permute-start | bytes 786440 | tf_op jit(solution)/shard_map/ppermute | solution.py:377
  12.7 1.6 %copy.7 = f32[512,512]{0,1:T(8,128)S(1)} copy(f32[512,512]{1,0:T(8,128)} %param.9) | data formatting | bytes 2097152 | tf_op jit(solution)/shard_map/optimization_barrier | solution.py:381
  18.0 1.6 %collective-permute-start.8 = (f32[4,128,256]{2,1,0:T(8,128)S(1)}, f32[4,128,256]{2,1,0:T(8,128)S(1)}, u32[]{:S(2)}, u32[]{:S(2)}) collective-permute-start(f32[4,128,256]{2,1,0:T(8,128)S(1)} %get-tuple-element.56.refs_4_), channel_id=1, source_target_pairs={{0,2},{2,0},{4,6},{6,4},{8,10},{10,8},{12,14},{14,12},{1,3},{3,1},... | collective-permute-start | bytes 1572872 | tf_op jit(solution)/shard_map/ppermute | solution.py:377
  19.6 2.3 %shard_map.70 = (bf16[4,128,512]{2,1,0:T(8,128)(2,1)}, bf16[4,128,512]{2,1,0:T(8,128)(2,1)}) custom-call(f32[4,4,128,128]{3,2,1,0:T(8,128)} %kinship_hbm.3), custom_call_target="tpu_custom_call" | custom-call | tf_op jit(solution)/shard_map/pallas_call | solution.py:437
  21.9 9.2 %collective-permute-done.4.partner_ref = f32[512,256]{1,0:T(8,128)S(1)} collective-permute-done((f32[512,256]{1,0:T(8,128)S(1)}, f32[512,256]{1,0:T(8,128)S(1)}, u32[]{:S(2)}, u32[]{:S(2)}) %collective-permute-start.4) | collective-permute-done | bytes 524320 | tf_op jit(solution)/shard_map/ppermute | solution.py:377
  31.2 3.4 %collective-permute-done.2.refs_1_ = f32[2,128,256]{2,1,0:T(8,128)} collective-permute-done((f32[2,128,256]{2,1,0:T(8,128)}, f32[2,128,256]{2,1,0:T(8,128)}, u32[]{:S(2)}, u32[]{:S(2)}) %collective-permute-start.2) | collective-permute-done | bytes 262176 | tf_op jit(solution)/shard_map/ppermute | solution.py:377
  35.3 2.0 %collective-permute-start.6 = (f32[2,128,256]{2,1,0:T(8,128)S(1)}, f32[2,128,256]{2,1,0:T(8,128)S(1)}, u32[]{:S(2)}, u32[]{:S(2)}) collective-permute-start(f32[2,128,256]{2,1,0:T(8,128)S(1)} %get-tuple-element.58), channel_id=1, source_target_pairs={{0,4},{2,6},{4,0},{6,2},{8,12},{10,14},{12,8},{14,10},{1,5},{3,7},... | collective-permute-start | bytes 786440 | tf_op jit(solution)/shard_map/ppermute | solution.py:377
  38.8 6.7 %collective-permute-done.5.refs_3_ = f32[2,128,256]{2,1,0:T(8,128)S(1)} collective-permute-done((f32[2,128,256]{2,1,0:T(8,128)S(1)}, f32[2,128,256]{2,1,0:T(8,128)S(1)}, u32[]{:S(2)}, u32[]{:S(2)}) %collective-permute-start.5) | collective-permute-done | bytes 262176 | tf_op jit(solution)/shard_map/ppermute | solution.py:377
  45.4 3.0 %collective-permute-done.6.refs_4_ = f32[2,128,256]{2,1,0:T(8,128)S(1)} collective-permute-done((f32[2,128,256]{2,1,0:T(8,128)S(1)}, f32[2,128,256]{2,1,0:T(8,128)S(1)}, u32[]{:S(2)}, u32[]{:S(2)}) %collective-permute-start.6) | collective-permute-done | bytes 262176 | tf_op jit(solution)/shard_map/ppermute | solution.py:377
  49.3 4.7 %shard_map.74 = (f32[512,256]{1,0:T(8,128)}, f32[512,256]{1,0:T(8,128)}, f32[8,136,256]{2,1,0:T(8,128)}, f32[4,128,256]{2,1,0:T(8,128)}, f32[4,128,256]{2,1,0:T(8,128)}) custom-call(s32[4,12]{1,0:T(4,128)S(1)} %get-tuple-element.43.table_ref, bf16[4,128,512]{2,1,0:T(8,128)(2,1)S(1)} %copy-done, bf16[4,128,512]{2,1,0:T(8,128)(2,1)S(1)} %copy-done.1, ...), custom_call_target="tpu_custom_call" | custom-call | tf_op jit(solution)/shard_map/pallas_call | solution.py:470
  54.1 6.1 %all-to-all-start = ((f32[8,136,256]{2,1,0:T(8,128)}), f32[8,136,256]{2,1,0:T(8,128)S(1)}, u32[]{:S(2)}, u32[]{:S(2)}) async-start(f32[8,136,256]{2,1,0:T(8,128)} %get-tuple-element.62), calls=%async_computation | async-start | bytes 2228224 | tf_op jit(solution)/shard_map/all_to_all | solution.py:484
  60.1 2.0 %collective-permute-start.9 = (f32[4,128,256]{2,1,0:T(8,128)}, f32[4,128,256]{2,1,0:T(8,128)S(1)}, u32[]{:S(2)}, u32[]{:S(2)}) collective-permute-start(f32[4,128,256]{2,1,0:T(8,128)} %get-tuple-element.64), channel_id=1, source_target_pairs={{0,2},{2,0},{4,6},{6,4},{8,10},{10,8},{12,14},{14,12},{1,3},{3,1},... | collective-permute-start | bytes 1572872 | tf_op jit(solution)/shard_map/ppermute | solution.py:377
  62.9 1.5 %collective-permute-start.10 = (f32[2,128,256]{2,1,0:T(8,128)}, f32[2,128,256]{2,1,0:T(8,128)}, u32[]{:S(2)}, u32[]{:S(2)}) collective-permute-start(f32[2,128,256]{2,1,0:T(8,128)} %get-tuple-element.70), channel_id=1, source_target_pairs={{0,4},{2,6},{4,0},{6,2},{8,12},{10,14},{12,8},{14,10},{1,5},{3,7},... | collective-permute-start | bytes 786440 | tf_op jit(solution)/shard_map/ppermute | solution.py:377
  64.4 21.4 %collective-permute-done.9.taken_ref = f32[4,128,256]{2,1,0:T(8,128)S(1)} collective-permute-done((f32[4,128,256]{2,1,0:T(8,128)}, f32[4,128,256]{2,1,0:T(8,128)S(1)}, u32[]{:S(2)}, u32[]{:S(2)}) %collective-permute-start.9) | collective-permute-done | bytes 524320 | tf_op jit(solution)/shard_map/ppermute | solution.py:377
  88.0 3.5 %shard_map.76.refs_0_ = f32[16,8,256]{2,1,0:T(8,128)} custom-call(s32[4,12]{1,0:T(4,128)S(1)} %get-tuple-element.43.table_ref, bf16[4,128,512]{2,1,0:T(8,128)(2,1)S(1)} %copy-done, bf16[4,128,512]{2,1,0:T(8,128)(2,1)S(1)} %copy-done.1, f32[512,256]{1,0:T(8,128)} %get-tuple-element.40.direction_hbm.direction_ref, f32[512,128]{1,0:T(8,128)} %get-tuple-element.46.diagonal_hbm, ...), custom_call_target="tpu_custom_call" | custom-call | tf_op jit(solution)/shard_map/pallas_call | solution.py:490
  92.6 2.4 %collective-permute-start.11 = (f32[1,128,256]{2,1,0:T(8,128)S(1)}, f32[1,128,256]{2,1,0:T(8,128)S(1)}, u32[]{:S(2)}, u32[]{:S(2)}) collective-permute-start(f32[1,128,256]{2,1,0:T(8,128)S(1)} %get-tuple-element.72), channel_id=1, source_target_pairs={{0,8},{2,10},{4,12},{6,14},{8,0},{10,2},{12,4},{14,6},{1,9},{3,11}... | collective-permute-start | bytes 393224 | tf_op jit(solution)/shard_map/ppermute | solution.py:377
  96.0 3.3 %collective-permute-start.13 = (f32[1,128,256]{2,1,0:T(8,128)S(1)}, f32[1,128,256]{2,1,0:T(8,128)S(1)}, u32[]{:S(2)}, u32[]{:S(2)}) collective-permute-start(f32[1,128,256]{2,1,0:T(8,128)S(1)} %get-tuple-element.75), channel_id=1, source_target_pairs={{0,8},{2,10},{4,12},{6,14},{8,0},{10,2},{12,4},{14,6},{1,9},{3,11}... | collective-permute-start | bytes 393224 | tf_op jit(solution)/shard_map/ppermute | solution.py:377
  99.3 3.5 %all-to-all-start.1 = ((f32[16,8,256]{2,1,0:T(8,128)}), f32[16,8,256]{2,1,0:T(8,128)S(1)}, u32[]{:S(2)}, u32[]{:S(2)}) async-start(f32[16,8,256]{2,1,0:T(8,128)} %shard_map.76.refs_0_), calls=%async_computation.1 | async-start | bytes 262144 | tf_op jit(solution)/shard_map/all_to_all | solution.py:497
  102.8 1.8 %collective-permute-done.11.first_taken_ref = f32[1,128,256]{2,1,0:T(8,128)S(1)} collective-permute-done((f32[1,128,256]{2,1,0:T(8,128)S(1)}, f32[1,128,256]{2,1,0:T(8,128)S(1)}, u32[]{:S(2)}, u32[]{:S(2)}) %collective-permute-start.11) | collective-permute-done | bytes 131104 | tf_op jit(solution)/shard_map/ppermute | solution.py:377
  104.6 1.9 %collective-permute-done.13.second_taken_ref = f32[1,128,256]{2,1,0:T(8,128)S(1)} collective-permute-done((f32[1,128,256]{2,1,0:T(8,128)S(1)}, f32[1,128,256]{2,1,0:T(8,128)S(1)}, u32[]{:S(2)}, u32[]{:S(2)}) %collective-permute-start.13) | collective-permute-done | bytes 131104 | tf_op jit(solution)/shard_map/ppermute | solution.py:377
  106.6 4.1 %all-to-all-done.1.sums_ref = f32[16,8,256]{2,1,0:T(8,128)S(1)} async-done(((f32[16,8,256]{2,1,0:T(8,128)}), f32[16,8,256]{2,1,0:T(8,128)S(1)}, u32[]{:S(2)}, u32[]{:S(2)}) %all-to-all-start.1) | async-done | bytes 131104 | tf_op jit(solution)/shard_map/all_to_all | solution.py:497
  (53 shorter events, 15.0 us)
Async XLA Ops:
  3.1 4.2 %collective-permute-start = (f32[512,512]{1,0:T(8,128)S(1)}, f32[512,512]{1,0:T(8,128)S(1)}, u32[]{:S(2)}, u32[]{:S(2)}) collective-permute-start(f32[512,512]{1,0:T(8,128)S(1)} %copy-done.12), channel_id=1, source_target_pairs={{0,1},{1,0},{2,3},{3,2},{4,5},{5,4},{6,7},{7,6},{8,9},{9,8},{10,11... | collective-permute-start | bytes 3145736 | tf_op jit(solution)/shard_map/ppermute | solution.py:377
  3.6 27.5 %collective-permute-start.4 = (f32[512,256]{1,0:T(8,128)S(1)}, f32[512,256]{1,0:T(8,128)S(1)}, u32[]{:S(2)}, u32[]{:S(2)}) collective-permute-start(f32[512,256]{1,0:T(8,128)S(1)} %get-tuple-element.41.direction_ref.values_ref), channel_id=1, source_target_pairs={{0,8},{2,10},{4,12},{6,14},{8,0},{10,2},{12,4},{14,6},{1,9},{3,11}... | collective-permute-start | bytes 1572872 | tf_op jit(solution)/shard_map/ppermute | solution.py:377
  9.1 22.0 %collective-permute-start.1 = (f32[2,128,256]{2,1,0:T(8,128)}, f32[2,128,256]{2,1,0:T(8,128)S(1)}, u32[]{:S(2)}, u32[]{:S(2)}) collective-permute-start(f32[2,128,256]{2,1,0:T(8,128)} %get-tuple-element.51), channel_id=1, source_target_pairs={{0,6},{2,4},{4,2},{6,0},{8,14},{10,12},{12,10},{14,8},{1,7},{3,5},... | collective-permute-start | bytes 786440 | tf_op jit(solution)/shard_map/ppermute | solution.py:377
  11.7 22.8 %collective-permute-start.2 = (f32[2,128,256]{2,1,0:T(8,128)}, f32[2,128,256]{2,1,0:T(8,128)}, u32[]{:S(2)}, u32[]{:S(2)}) collective-permute-start(f32[2,128,256]{2,1,0:T(8,128)} %get-tuple-element.52), channel_id=1, source_target_pairs={{0,4},{2,6},{4,0},{6,2},{8,12},{10,14},{12,8},{14,10},{1,5},{3,7},... | collective-permute-start | bytes 786440 | tf_op jit(solution)/shard_map/ppermute | solution.py:377
  12.2 22.4 %collective-permute-start.3 = (f32[2,128,256]{2,1,0:T(8,128)}, f32[2,128,256]{2,1,0:T(8,128)}, u32[]{:S(2)}, u32[]{:S(2)}) collective-permute-start(f32[2,128,256]{2,1,0:T(8,128)} %get-tuple-element.53), channel_id=1, source_target_pairs={{0,2},{2,0},{4,6},{6,4},{8,10},{10,8},{12,14},{14,12},{1,3},{3,1},... | collective-permute-start | bytes 786440 | tf_op jit(solution)/shard_map/ppermute | solution.py:377
  18.0 17.2 %copy-start.3 = (f32[4,128,256]{2,1,0:T(8,128)}, f32[4,128,256]{2,1,0:T(8,128)S(1)}, u32[]{:S(2)}) copy-start(f32[4,128,256]{2,1,0:T(8,128)S(1)} %get-tuple-element.55.refs_3_.kept_ref) | copy-start | bytes 1572868
  18.0 20.7 %collective-permute-start.8 = (f32[4,128,256]{2,1,0:T(8,128)S(1)}, f32[4,128,256]{2,1,0:T(8,128)S(1)}, u32[]{:S(2)}, u32[]{:S(2)}) collective-permute-start(f32[4,128,256]{2,1,0:T(8,128)S(1)} %get-tuple-element.56.refs_4_), channel_id=1, source_target_pairs={{0,2},{2,0},{4,6},{6,4},{8,10},{10,8},{12,14},{14,12},{1,3},{3,1},... | collective-permute-start | bytes 1572872 | tf_op jit(solution)/shard_map/ppermute | solution.py:377
  34.6 14.8 %copy-start.1 = (bf16[4,128,512]{2,1,0:T(8,128)(2,1)S(1)}, bf16[4,128,512]{2,1,0:T(8,128)(2,1)}, u32[]{:S(2)}) copy-start(bf16[4,128,512]{2,1,0:T(8,128)(2,1)} %get-tuple-element.45.refs_6_.low_hbm.low_ref) | copy-start | bytes 1572868
  34.6 14.8 %copy-start.9 = (f32[512,128]{1,0:T(8,128)S(1)}, f32[512,128]{1,0:T(8,128)}, u32[]{:S(2)}) copy-start(f32[512,128]{1,0:T(8,128)} %get-tuple-element.46.diagonal_hbm) | copy-start | bytes 786436
  35.2 10.3 %collective-permute-start.5 = (f32[2,128,256]{2,1,0:T(8,128)S(1)}, f32[2,128,256]{2,1,0:T(8,128)S(1)}, u32[]{:S(2)}, u32[]{:S(2)}) collective-permute-start(f32[2,128,256]{2,1,0:T(8,128)S(1)} %get-tuple-element.57), channel_id=1, source_target_pairs={{0,6},{2,4},{4,2},{6,0},{8,14},{10,12},{12,10},{14,8},{1,7},{3,5},... | collective-permute-start | bytes 786440 | tf_op jit(solution)/shard_map/ppermute | solution.py:377
  35.3 13.2 %collective-permute-start.6 = (f32[2,128,256]{2,1,0:T(8,128)S(1)}, f32[2,128,256]{2,1,0:T(8,128)S(1)}, u32[]{:S(2)}, u32[]{:S(2)}) collective-permute-start(f32[2,128,256]{2,1,0:T(8,128)S(1)} %get-tuple-element.58), channel_id=1, source_target_pairs={{0,4},{2,6},{4,0},{6,2},{8,12},{10,14},{12,8},{14,10},{1,5},{3,7},... | collective-permute-start | bytes 786440 | tf_op jit(solution)/shard_map/ppermute | solution.py:377
  37.3 12.0 %collective-permute-start.7 = (f32[2,128,256]{2,1,0:T(8,128)S(1)}, f32[2,128,256]{2,1,0:T(8,128)S(1)}, u32[]{:S(2)}, u32[]{:S(2)}) collective-permute-start(f32[2,128,256]{2,1,0:T(8,128)S(1)} %get-tuple-element.59), channel_id=1, source_target_pairs={{0,2},{2,0},{4,6},{6,4},{8,10},{10,8},{12,14},{14,12},{1,3},{3,1},... | collective-permute-start | bytes 786440 | tf_op jit(solution)/shard_map/ppermute | solution.py:377
  38.8 15.3 %copy-start.5 = (f32[4,128,256]{2,1,0:T(8,128)}, f32[4,128,256]{2,1,0:T(8,128)S(1)}, u32[]{:S(2)}) copy-start(f32[4,128,256]{2,1,0:T(8,128)S(1)} %collective-permute-done.8.refs_7_.taken_ref) | copy-start | bytes 1572868
  54.1 34.0 %all-to-all-start = ((f32[8,136,256]{2,1,0:T(8,128)}), f32[8,136,256]{2,1,0:T(8,128)S(1)}, u32[]{:S(2)}, u32[]{:S(2)}) async-start(f32[8,136,256]{2,1,0:T(8,128)} %get-tuple-element.62), calls=%async_computation | async-start | bytes 2228224 | tf_op jit(solution)/shard_map/all_to_all | solution.py:484
  60.1 25.7 %copy-start.10 = (f32[4,128,256]{2,1,0:T(8,128)S(1)}, f32[4,128,256]{2,1,0:T(8,128)}, u32[]{:S(2)}) copy-start(f32[4,128,256]{2,1,0:T(8,128)} %get-tuple-element.63.kept_ref) | copy-start | bytes 1572868
  60.1 25.6 %collective-permute-start.9 = (f32[4,128,256]{2,1,0:T(8,128)}, f32[4,128,256]{2,1,0:T(8,128)S(1)}, u32[]{:S(2)}, u32[]{:S(2)}) collective-permute-start(f32[4,128,256]{2,1,0:T(8,128)} %get-tuple-element.64), channel_id=1, source_target_pairs={{0,2},{2,0},{4,6},{6,4},{8,10},{10,8},{12,14},{14,12},{1,3},{3,1},... | collective-permute-start | bytes 1572872 | tf_op jit(solution)/shard_map/ppermute | solution.py:377
  62.9 28.6 %collective-permute-start.10 = (f32[2,128,256]{2,1,0:T(8,128)}, f32[2,128,256]{2,1,0:T(8,128)}, u32[]{:S(2)}, u32[]{:S(2)}) collective-permute-start(f32[2,128,256]{2,1,0:T(8,128)} %get-tuple-element.70), channel_id=1, source_target_pairs={{0,4},{2,6},{4,0},{6,2},{8,12},{10,14},{12,8},{14,10},{1,5},{3,7},... | collective-permute-start | bytes 786440 | tf_op jit(solution)/shard_map/ppermute | solution.py:377
  86.6 8.5 %collective-permute-start.12 = (f32[2,128,256]{2,1,0:T(8,128)}, f32[2,128,256]{2,1,0:T(8,128)S(1)}, u32[]{:S(2)}, u32[]{:S(2)}) collective-permute-start(f32[2,128,256]{2,1,0:T(8,128)} %get-tuple-element.65.refs_0_), channel_id=1, source_target_pairs={{0,4},{2,6},{4,0},{6,2},{8,12},{10,14},{12,8},{14,10},{1,5},{3,7},... | collective-permute-start | bytes 786440 | tf_op jit(solution)/shard_map/ppermute | solution.py:377
  91.5 19.2 %copy-start.7 = (f32[512,256]{1,0:T(8,128)S(1)}, f32[512,256]{1,0:T(8,128)}, u32[]{:S(2)}) copy-start(f32[512,256]{1,0:T(8,128)} %get-tuple-element.40.direction_hbm.direction_ref) | copy-start | bytes 1572868
  91.5 19.2 %copy-start.8 = (f32[512,256]{1,0:T(8,128)S(1)}, f32[512,256]{1,0:T(8,128)}, u32[]{:S(2)}) copy-start(f32[512,256]{1,0:T(8,128)} %get-tuple-element.60.scaled_hbm.scaled_ref) | copy-start | bytes 1572868
  92.6 12.0 %collective-permute-start.11 = (f32[1,128,256]{2,1,0:T(8,128)S(1)}, f32[1,128,256]{2,1,0:T(8,128)S(1)}, u32[]{:S(2)}, u32[]{:S(2)}) collective-permute-start(f32[1,128,256]{2,1,0:T(8,128)S(1)} %get-tuple-element.72), channel_id=1, source_target_pairs={{0,8},{2,10},{4,12},{6,14},{8,0},{10,2},{12,4},{14,6},{1,9},{3,11}... | collective-permute-start | bytes 393224 | tf_op jit(solution)/shard_map/ppermute | solution.py:377
  96.0 10.5 %collective-permute-start.13 = (f32[1,128,256]{2,1,0:T(8,128)S(1)}, f32[1,128,256]{2,1,0:T(8,128)S(1)}, u32[]{:S(2)}, u32[]{:S(2)}) collective-permute-start(f32[1,128,256]{2,1,0:T(8,128)S(1)} %get-tuple-element.75), channel_id=1, source_target_pairs={{0,8},{2,10},{4,12},{6,14},{8,0},{10,2},{12,4},{14,6},{1,9},{3,11}... | collective-permute-start | bytes 393224 | tf_op jit(solution)/shard_map/ppermute | solution.py:377
  99.3 11.4 %all-to-all-start.1 = ((f32[16,8,256]{2,1,0:T(8,128)}), f32[16,8,256]{2,1,0:T(8,128)S(1)}, u32[]{:S(2)}, u32[]{:S(2)}) async-start(f32[16,8,256]{2,1,0:T(8,128)} %shard_map.76.refs_0_), calls=%async_computation.1 | async-start | bytes 262144 | tf_op jit(solution)/shard_map/all_to_all | solution.py:497
  106.5 5.1 %collective-permute-start.14 = (f32[2,64,256]{2,1,0:T(8,128)S(1)}, f32[2,64,256]{2,1,0:T(8,128)S(1)}, u32[]{:S(2)}, u32[]{:S(2)}) collective-permute-start(f32[2,64,256]{2,1,0:T(8,128)S(1)} %get-tuple-element.77), channel_id=1, source_target_pairs={{0,1},{1,0},{2,3},{3,2},{4,5},{5,4},{6,7},{7,6},{8,9},{9,8},{10,11... | collective-permute-start | bytes 393224 | tf_op jit(solution)/shard_map/ppermute | solution.py:377
  (6 other events, 41.4 us)

commit v27 on v24

--- a/solution.py
+++ b/solution.py
@@ -499,7 +499,7 @@
         scaled_kept, scaled_given = add_step(scaled_kept, scaled_taken, sums)
         scaled_taken = swap(scaled_given, "samples", devices, step)
     for step in steps[1:]:
-        direction_kept, direction_given = add_step(direction_kept, direction_taken, sums)
+        direction_kept, direction_given = add_step(direction_kept, direction_taken)
         direction_taken = swap(direction_given, "samples", devices, step)
     rows = float_of(2, share_rows, columns)
     own_scores, other_scores = call(

time: 112 us -> 113 us (level)
  waiting for transfers between devices: 52.5 us -> 55.2 us
  Pallas kernels: 21.3 us -> 19.6 us
    all_to_all x1, waiting for transfers between devices: 3.05 us -> 6.37 us  [per_device(): lax.all_to_all(sums, ('samples', 'cols'), split_axis=0, concat_axis=0, ti...]
    pallas_call x4, Pallas kernels: 2.79 us -> 1.09 us  [add_step(): call(add_kernel, [rows] * 2, [vmem] * (2 + len(gates)), [vmem] * 2)]
  transfers between devices with their start and end apart: 17 -> 17, of which waited for: 9 -> 9; matrix products, arithmetic and copies ran while one was open for 3% -> 3% of each run, Pallas kernels for 12% -> 10%
where the time goes in v27:
time: 113 us; the launch traced here: 112 us
  waiting for transfers between devices  55.2 us (49%)
  starting transfers between devices  32.6 us (29%)
  Pallas kernels  19.6 us (17%)
  local copies, waits for them, and re-layouts  4.14 us (4%)
    ppermute x15, waiting for transfers between devices, swap(): return lax.ppermute(values, axis, [(i, i ^ step) for i in range(devices)])  48.8 us
    ppermute x15, starting transfers between devices, swap(): return lax.ppermute(values, axis, [(i, i ^ step) for i in range(devices)])  22.1 us
    all_to_all x1, waiting for transfers between devices, per_device(): lax.all_to_all(sums, ('samples', 'cols'), split_axis=0, concat_axis=0, ti...  6.37 us
    all_to_all x1, starting transfers between devices, per_device(): lax.all_to_all(outgoing, 'samples', split_axis=0, concat_axis=0, tiled=True)  6.09 us
    pallas_call x1, Pallas kernels, per_device(): call(functools.partial(apply_kernel, devices, capacity), [full_out, full_...  4.71 us
    all_to_all x1, starting transfers between devices, per_device(): lax.all_to_all(sums, ('samples', 'cols'), split_axis=0, concat_axis=0, ti...  4.4 us
    pallas_call x1, Pallas kernels, per_device(): call(functools.partial(curvature_kernel, devices), float_of(2 * devices,...  3.83 us
    pallas_call x1, Pallas kernels, per_device(): call(direction_kernel, [full, full_out, pltpu.HBM((people, LANES), jnp.fl...  2.44 us
  transfers between devices with their start and end apart: 17, of which 9 were waited for; matrix products, arithmetic and copies ran while one was open for 3% of the time, Pallas kernels for 10%

profile of v27, /device:TPU:0, one launch (start us, length us, event | category | flops | bytes accessed | tf_op | source)
XLA Modules:
  0.0 112.4 jit_solution(14958500616908770101)
XLA Ops:
  0.7 2.4 %shard_map.68 = (f32[512,256]{1,0:T(8,128)S(1)}, f32[512,256]{1,0:T(8,128)}, f32[512,128]{1,0:T(8,128)}, f32[8,256]{1,0:T(8,128)S(1)}) custom-call(f32[4,4,128,128]{3,2,1,0:T(8,128)} %kinship_hbm.3, f32[4,128]{1,0:T(4,128)} %bitcast.9, f32[512,256]{1,0:T(8,128)} %phenotypes_hbm.1), custom_call_target="tpu_custom_call" | custom-call | tf_op jit(solution)/shard_map/pallas_call | solution.py:408
  3.6 3.7 %collective-permute-start.4 = (f32[512,256]{1,0:T(8,128)S(1)}, f32[512,256]{1,0:T(8,128)S(1)}, u32[]{:S(2)}, u32[]{:S(2)}) collective-permute-start(f32[512,256]{1,0:T(8,128)S(1)} %get-tuple-element.41.direction_ref.values_ref), channel_id=1, source_target_pairs={{0,8},{2,10},{4,12},{6,14},{8,0},{10,2},{12,4},{14,6},{1,9},{3,11}... | collective-permute-start | bytes 1572872 | tf_op jit(solution)/shard_map/ppermute | solution.py:377
  7.3 1.8 %shard_map.69 = (s32[4,12]{1,0:T(4,128)S(1)}, s32[2,4]{1,0:T(2,128)S(1)}, f32[2,128,256]{2,1,0:T(8,128)}, f32[2,128,256]{2,1,0:T(8,128)}, f32[2,128,256]{2,1,0:T(8,128)}) custom-call(s32[3,32]{1,0:T(4,128)S(1)} %bitcast.8, f32[512,256]{1,0:T(8,128)S(1)} %get-tuple-element.41.direction_ref.values_ref, f32[512,512]{1,0:T(8,128)S(1)} %collective-permute-done.gate_ref), custom_call_target="tpu_custom_call" | custom-call | tf_op jit(solution)/shard_map/pallas_call | solution.py:427
  9.1 2.6 %collective-permute-start.1 = (f32[2,128,256]{2,1,0:T(8,128)}, f32[2,128,256]{2,1,0:T(8,128)S(1)}, u32[]{:S(2)}, u32[]{:S(2)}) collective-permute-start(f32[2,128,256]{2,1,0:T(8,128)} %get-tuple-element.51), channel_id=1, source_target_pairs={{0,6},{2,4},{4,2},{6,0},{8,14},{10,12},{12,10},{14,8},{1,7},{3,5},... | collective-permute-start | bytes 786440 | tf_op jit(solution)/shard_map/ppermute | solution.py:377
  12.7 1.6 %copy.7 = f32[512,512]{0,1:T(8,128)S(1)} copy(f32[512,512]{1,0:T(8,128)} %param.9) | data formatting | bytes 2097152 | tf_op jit(solution)/shard_map/optimization_barrier | solution.py:381
  18.0 1.6 %collective-permute-start.8 = (f32[4,128,256]{2,1,0:T(8,128)S(1)}, f32[4,128,256]{2,1,0:T(8,128)S(1)}, u32[]{:S(2)}, u32[]{:S(2)}) collective-permute-start(f32[4,128,256]{2,1,0:T(8,128)S(1)} %get-tuple-element.56.refs_4_), channel_id=1, source_target_pairs={{0,2},{2,0},{4,6},{6,4},{8,10},{10,8},{12,14},{14,12},{1,3},{3,1},... | collective-permute-start | bytes 1572872 | tf_op jit(solution)/shard_map/ppermute | solution.py:377
  19.6 2.3 %shard_map.70 = (bf16[4,128,512]{2,1,0:T(8,128)(2,1)}, bf16[4,128,512]{2,1,0:T(8,128)(2,1)}) custom-call(f32[4,4,128,128]{3,2,1,0:T(8,128)} %kinship_hbm.3), custom_call_target="tpu_custom_call" | custom-call | tf_op jit(solution)/shard_map/pallas_call | solution.py:437
  21.9 9.2 %collective-permute-done.4.partner_ref = f32[512,256]{1,0:T(8,128)S(1)} collective-permute-done((f32[512,256]{1,0:T(8,128)S(1)}, f32[512,256]{1,0:T(8,128)S(1)}, u32[]{:S(2)}, u32[]{:S(2)}) %collective-permute-start.4) | collective-permute-done | bytes 524320 | tf_op jit(solution)/shard_map/ppermute | solution.py:377
  31.2 3.4 %collective-permute-done.2.refs_1_ = f32[2,128,256]{2,1,0:T(8,128)} collective-permute-done((f32[2,128,256]{2,1,0:T(8,128)}, f32[2,128,256]{2,1,0:T(8,128)}, u32[]{:S(2)}, u32[]{:S(2)}) %collective-permute-start.2) | collective-permute-done | bytes 262176 | tf_op jit(solution)/shard_map/ppermute | solution.py:377
  35.3 2.0 %collective-permute-start.6 = (f32[2,128,256]{2,1,0:T(8,128)S(1)}, f32[2,128,256]{2,1,0:T(8,128)S(1)}, u32[]{:S(2)}, u32[]{:S(2)}) collective-permute-start(f32[2,128,256]{2,1,0:T(8,128)S(1)} %get-tuple-element.58), channel_id=1, source_target_pairs={{0,4},{2,6},{4,0},{6,2},{8,12},{10,14},{12,8},{14,10},{1,5},{3,7},... | collective-permute-start | bytes 786440 | tf_op jit(solution)/shard_map/ppermute | solution.py:377
  38.7 6.7 %collective-permute-done.5.refs_3_ = f32[2,128,256]{2,1,0:T(8,128)S(1)} collective-permute-done((f32[2,128,256]{2,1,0:T(8,128)S(1)}, f32[2,128,256]{2,1,0:T(8,128)S(1)}, u32[]{:S(2)}, u32[]{:S(2)}) %collective-permute-start.5) | collective-permute-done | bytes 262176 | tf_op jit(solution)/shard_map/ppermute | solution.py:377
  45.4 3.0 %collective-permute-done.6.refs_4_ = f32[2,128,256]{2,1,0:T(8,128)S(1)} collective-permute-done((f32[2,128,256]{2,1,0:T(8,128)S(1)}, f32[2,128,256]{2,1,0:T(8,128)S(1)}, u32[]{:S(2)}, u32[]{:S(2)}) %collective-permute-start.6) | collective-permute-done | bytes 262176 | tf_op jit(solution)/shard_map/ppermute | solution.py:377
  49.3 4.7 %shard_map.74 = (f32[512,256]{1,0:T(8,128)}, f32[512,256]{1,0:T(8,128)}, f32[8,136,256]{2,1,0:T(8,128)}, f32[4,128,256]{2,1,0:T(8,128)}, f32[4,128,256]{2,1,0:T(8,128)}) custom-call(s32[4,12]{1,0:T(4,128)S(1)} %get-tuple-element.43.table_ref, bf16[4,128,512]{2,1,0:T(8,128)(2,1)S(1)} %copy-done, bf16[4,128,512]{2,1,0:T(8,128)(2,1)S(1)} %copy-done.1, ...), custom_call_target="tpu_custom_call" | custom-call | tf_op jit(solution)/shard_map/pallas_call | solution.py:470
  54.1 6.1 %all-to-all-start = ((f32[8,136,256]{2,1,0:T(8,128)}), f32[8,136,256]{2,1,0:T(8,128)S(1)}, u32[]{:S(2)}, u32[]{:S(2)}) async-start(f32[8,136,256]{2,1,0:T(8,128)} %get-tuple-element.62), calls=%async_computation | async-start | bytes 2228224 | tf_op jit(solution)/shard_map/all_to_all | solution.py:484
  60.2 2.0 %collective-permute-start.9 = (f32[4,128,256]{2,1,0:T(8,128)S(1)}, f32[4,128,256]{2,1,0:T(8,128)S(1)}, u32[]{:S(2)}, u32[]{:S(2)}) collective-permute-start(f32[4,128,256]{2,1,0:T(8,128)S(1)} %copy-done.9), channel_id=1, source_target_pairs={{0,2},{2,0},{4,6},{6,4},{8,10},{10,8},{12,14},{14,12},{1,3},{3,1},... | collective-permute-start | bytes 1572872 | tf_op jit(solution)/shard_map/ppermute | solution.py:377
  62.2 1.5 %collective-permute-start.10 = (f32[2,128,256]{2,1,0:T(8,128)S(1)}, f32[2,128,256]{2,1,0:T(8,128)S(1)}, u32[]{:S(2)}, u32[]{:S(2)}) collective-permute-start(f32[2,128,256]{2,1,0:T(8,128)S(1)} %get-tuple-element.70), channel_id=1, source_target_pairs={{0,4},{2,6},{4,0},{6,2},{8,12},{10,14},{12,8},{14,10},{1,5},{3,7},... | collective-permute-start | bytes 786440 | tf_op jit(solution)/shard_map/ppermute | solution.py:377
  63.8 22.0 %collective-permute-done.9.taken_ref = f32[4,128,256]{2,1,0:T(8,128)S(1)} collective-permute-done((f32[4,128,256]{2,1,0:T(8,128)S(1)}, f32[4,128,256]{2,1,0:T(8,128)S(1)}, u32[]{:S(2)}, u32[]{:S(2)}) %collective-permute-start.9) | collective-permute-done | bytes 524320 | tf_op jit(solution)/shard_map/ppermute | solution.py:377
  85.9 1.5 %collective-permute-start.12 = (f32[2,128,256]{2,1,0:T(8,128)S(1)}, f32[2,128,256]{2,1,0:T(8,128)S(1)}, u32[]{:S(2)}, u32[]{:S(2)}) collective-permute-start(f32[2,128,256]{2,1,0:T(8,128)S(1)} %get-tuple-element.65.refs_0_), channel_id=1, source_target_pairs={{0,4},{2,6},{4,0},{6,2},{8,12},{10,14},{12,8},{14,10},{1,5},{3,7},... | collective-permute-start | bytes 786440 | tf_op jit(solution)/shard_map/ppermute | solution.py:377
  87.4 2.4 %collective-permute-start.11 = (f32[1,128,256]{2,1,0:T(8,128)S(1)}, f32[1,128,256]{2,1,0:T(8,128)S(1)}, u32[]{:S(2)}, u32[]{:S(2)}) collective-permute-start(f32[1,128,256]{2,1,0:T(8,128)S(1)} %get-tuple-element.72), channel_id=1, source_target_pairs={{0,8},{2,10},{4,12},{6,14},{8,0},{10,2},{12,4},{14,6},{1,9},{3,11}... | collective-permute-start | bytes 393224 | tf_op jit(solution)/shard_map/ppermute | solution.py:377
  89.9 3.8 %shard_map.76.refs_0_ = f32[16,8,256]{2,1,0:T(8,128)} custom-call(s32[4,12]{1,0:T(4,128)S(1)} %get-tuple-element.43.table_ref, bf16[4,128,512]{2,1,0:T(8,128)(2,1)} %get-tuple-element.44.refs_5_.high_hbm, bf16[4,128,512]{2,1,0:T(8,128)(2,1)} %get-tuple-element.45.refs_6_.low_hbm, f32[512,256]{1,0:T(8,128)} %get-tuple-element.40.direction_hbm.direction_ref, ...), custom_call_target="tpu_custom_call" | custom-call | tf_op jit(solution)/shard_map/pallas_call | solution.py:490
  93.7 2.1 %collective-permute-done.12.taken_ref = f32[2,128,256]{2,1,0:T(8,128)S(1)} collective-permute-done((f32[2,128,256]{2,1,0:T(8,128)S(1)}, f32[2,128,256]{2,1,0:T(8,128)S(1)}, u32[]{:S(2)}, u32[]{:S(2)}) %collective-permute-start.12) | collective-permute-done | bytes 262176 | tf_op jit(solution)/shard_map/ppermute | solution.py:377
  96.8 1.7 %collective-permute-start.13 = (f32[1,128,256]{2,1,0:T(8,128)S(1)}, f32[1,128,256]{2,1,0:T(8,128)S(1)}, u32[]{:S(2)}, u32[]{:S(2)}) collective-permute-start(f32[1,128,256]{2,1,0:T(8,128)S(1)} %get-tuple-element.75), channel_id=1, source_target_pairs={{0,8},{2,10},{4,12},{6,14},{8,0},{10,2},{12,4},{14,6},{1,9},{3,11}... | collective-permute-start | bytes 393224 | tf_op jit(solution)/shard_map/ppermute | solution.py:377
  98.5 4.4 %all-to-all-start.1 = ((f32[16,8,256]{2,1,0:T(8,128)}), f32[16,8,256]{2,1,0:T(8,128)S(1)}, u32[]{:S(2)}, u32[]{:S(2)}) async-start(f32[16,8,256]{2,1,0:T(8,128)} %shard_map.76.refs_0_), calls=%async_computation.1 | async-start | bytes 262144 | tf_op jit(solution)/shard_map/all_to_all | solution.py:497
  104.5 6.4 %all-to-all-done.1.sums_ref = f32[16,8,256]{2,1,0:T(8,128)S(1)} async-done(((f32[16,8,256]{2,1,0:T(8,128)}), f32[16,8,256]{2,1,0:T(8,128)S(1)}, u32[]{:S(2)}, u32[]{:S(2)}) %all-to-all-start.1) | async-done | bytes 131104 | tf_op jit(solution)/shard_map/all_to_all | solution.py:497
  (47 shorter events, 12.5 us)
Async XLA Ops:
  0.6 6.7 %copy-start.7 = (s32[32,3]{0,1:T(4,128)S(1)}, s32[32,3]{0,1:T(4,128)}, u32[]{:S(2)}) copy-start(s32[32,3]{0,1:T(4,128)} %param.6) | copy-start | bytes 1156
  3.1 4.2 %collective-permute-start = (f32[512,512]{1,0:T(8,128)S(1)}, f32[512,512]{1,0:T(8,128)S(1)}, u32[]{:S(2)}, u32[]{:S(2)}) collective-permute-start(f32[512,512]{1,0:T(8,128)S(1)} %copy-done.8), channel_id=1, source_target_pairs={{0,1},{1,0},{2,3},{3,2},{4,5},{5,4},{6,7},{7,6},{8,9},{9,8},{10,11... | collective-permute-start | bytes 3145736 | tf_op jit(solution)/shard_map/ppermute | solution.py:377
  3.6 27.5 %collective-permute-start.4 = (f32[512,256]{1,0:T(8,128)S(1)}, f32[512,256]{1,0:T(8,128)S(1)}, u32[]{:S(2)}, u32[]{:S(2)}) collective-permute-start(f32[512,256]{1,0:T(8,128)S(1)} %get-tuple-element.41.direction_ref.values_ref), channel_id=1, source_target_pairs={{0,8},{2,10},{4,12},{6,14},{8,0},{10,2},{12,4},{14,6},{1,9},{3,11}... | collective-permute-start | bytes 1572872 | tf_op jit(solution)/shard_map/ppermute | solution.py:377
  9.1 22.0 %collective-permute-start.1 = (f32[2,128,256]{2,1,0:T(8,128)}, f32[2,128,256]{2,1,0:T(8,128)S(1)}, u32[]{:S(2)}, u32[]{:S(2)}) collective-permute-start(f32[2,128,256]{2,1,0:T(8,128)} %get-tuple-element.51), channel_id=1, source_target_pairs={{0,6},{2,4},{4,2},{6,0},{8,14},{10,12},{12,10},{14,8},{1,7},{3,5},... | collective-permute-start | bytes 786440 | tf_op jit(solution)/shard_map/ppermute | solution.py:377
  11.7 22.8 %collective-permute-start.2 = (f32[2,128,256]{2,1,0:T(8,128)}, f32[2,128,256]{2,1,0:T(8,128)}, u32[]{:S(2)}, u32[]{:S(2)}) collective-permute-start(f32[2,128,256]{2,1,0:T(8,128)} %get-tuple-element.52), channel_id=1, source_target_pairs={{0,4},{2,6},{4,0},{6,2},{8,12},{10,14},{12,8},{14,10},{1,5},{3,7},... | collective-permute-start | bytes 786440 | tf_op jit(solution)/shard_map/ppermute | solution.py:377
  12.2 22.4 %collective-permute-start.3 = (f32[2,128,256]{2,1,0:T(8,128)}, f32[2,128,256]{2,1,0:T(8,128)}, u32[]{:S(2)}, u32[]{:S(2)}) collective-permute-start(f32[2,128,256]{2,1,0:T(8,128)} %get-tuple-element.53), channel_id=1, source_target_pairs={{0,2},{2,0},{4,6},{6,4},{8,10},{10,8},{12,14},{14,12},{1,3},{3,1},... | collective-permute-start | bytes 786440 | tf_op jit(solution)/shard_map/ppermute | solution.py:377
  18.0 20.7 %collective-permute-start.8 = (f32[4,128,256]{2,1,0:T(8,128)S(1)}, f32[4,128,256]{2,1,0:T(8,128)S(1)}, u32[]{:S(2)}, u32[]{:S(2)}) collective-permute-start(f32[4,128,256]{2,1,0:T(8,128)S(1)} %get-tuple-element.56.refs_4_), channel_id=1, source_target_pairs={{0,2},{2,0},{4,6},{6,4},{8,10},{10,8},{12,14},{14,12},{1,3},{3,1},... | collective-permute-start | bytes 1572872 | tf_op jit(solution)/shard_map/ppermute | solution.py:377
  34.6 14.8 %copy-start = (bf16[4,128,512]{2,1,0:T(8,128)(2,1)S(1)}, bf16[4,128,512]{2,1,0:T(8,128)(2,1)}, u32[]{:S(2)}) copy-start(bf16[4,128,512]{2,1,0:T(8,128)(2,1)} %get-tuple-element.44.refs_5_.high_hbm) | copy-start | bytes 1572868
  34.6 14.8 %copy-start.1 = (bf16[4,128,512]{2,1,0:T(8,128)(2,1)S(1)}, bf16[4,128,512]{2,1,0:T(8,128)(2,1)}, u32[]{:S(2)}) copy-start(bf16[4,128,512]{2,1,0:T(8,128)(2,1)} %get-tuple-element.45.refs_6_.low_hbm) | copy-start | bytes 1572868
  34.6 14.8 %copy-start.5 = (f32[512,128]{1,0:T(8,128)S(1)}, f32[512,128]{1,0:T(8,128)}, u32[]{:S(2)}) copy-start(f32[512,128]{1,0:T(8,128)} %get-tuple-element.46.diagonal_hbm) | copy-start | bytes 786436
  35.2 10.3 %collective-permute-start.5 = (f32[2,128,256]{2,1,0:T(8,128)S(1)}, f32[2,128,256]{2,1,0:T(8,128)S(1)}, u32[]{:S(2)}, u32[]{:S(2)}) collective-permute-start(f32[2,128,256]{2,1,0:T(8,128)S(1)} %get-tuple-element.57), channel_id=1, source_target_pairs={{0,6},{2,4},{4,2},{6,0},{8,14},{10,12},{12,10},{14,8},{1,7},{3,5},... | collective-permute-start | bytes 786440 | tf_op jit(solution)/shard_map/ppermute | solution.py:377
  35.3 13.2 %collective-permute-start.6 = (f32[2,128,256]{2,1,0:T(8,128)S(1)}, f32[2,128,256]{2,1,0:T(8,128)S(1)}, u32[]{:S(2)}, u32[]{:S(2)}) collective-permute-start(f32[2,128,256]{2,1,0:T(8,128)S(1)} %get-tuple-element.58), channel_id=1, source_target_pairs={{0,4},{2,6},{4,0},{6,2},{8,12},{10,14},{12,8},{14,10},{1,5},{3,7},... | collective-permute-start | bytes 786440 | tf_op jit(solution)/shard_map/ppermute | solution.py:377
  37.3 12.0 %collective-permute-start.7 = (f32[2,128,256]{2,1,0:T(8,128)S(1)}, f32[2,128,256]{2,1,0:T(8,128)S(1)}, u32[]{:S(2)}, u32[]{:S(2)}) collective-permute-start(f32[2,128,256]{2,1,0:T(8,128)S(1)} %get-tuple-element.59), channel_id=1, source_target_pairs={{0,2},{2,0},{4,6},{6,4},{8,10},{10,8},{12,14},{14,12},{1,3},{3,1},... | collective-permute-start | bytes 786440 | tf_op jit(solution)/shard_map/ppermute | solution.py:377
  54.0 31.8 %copy-start.6 = (f32[4,128,256]{2,1,0:T(8,128)S(1)}, f32[4,128,256]{2,1,0:T(8,128)}, u32[]{:S(2)}) copy-start(f32[4,128,256]{2,1,0:T(8,128)} %get-tuple-element.63.kept_ref) | copy-start | bytes 1572868
  54.1 35.8 %all-to-all-start = ((f32[8,136,256]{2,1,0:T(8,128)}), f32[8,136,256]{2,1,0:T(8,128)S(1)}, u32[]{:S(2)}, u32[]{:S(2)}) async-start(f32[8,136,256]{2,1,0:T(8,128)} %get-tuple-element.62), calls=%async_computation | async-start | bytes 2228224 | tf_op jit(solution)/shard_map/all_to_all | solution.py:484
  60.2 25.6 %collective-permute-start.9 = (f32[4,128,256]{2,1,0:T(8,128)S(1)}, f32[4,128,256]{2,1,0:T(8,128)S(1)}, u32[]{:S(2)}, u32[]{:S(2)}) collective-permute-start(f32[4,128,256]{2,1,0:T(8,128)S(1)} %copy-done.9), channel_id=1, source_target_pairs={{0,2},{2,0},{4,6},{6,4},{8,10},{10,8},{12,14},{14,12},{1,3},{3,1},... | collective-permute-start | bytes 1572872 | tf_op jit(solution)/shard_map/ppermute | solution.py:377
  62.2 25.2 %collective-permute-start.10 = (f32[2,128,256]{2,1,0:T(8,128)S(1)}, f32[2,128,256]{2,1,0:T(8,128)S(1)}, u32[]{:S(2)}, u32[]{:S(2)}) collective-permute-start(f32[2,128,256]{2,1,0:T(8,128)S(1)} %get-tuple-element.70), channel_id=1, source_target_pairs={{0,4},{2,6},{4,0},{6,2},{8,12},{10,14},{12,8},{14,10},{1,5},{3,7},... | collective-permute-start | bytes 786440 | tf_op jit(solution)/shard_map/ppermute | solution.py:377
  85.9 10.0 %collective-permute-start.12 = (f32[2,128,256]{2,1,0:T(8,128)S(1)}, f32[2,128,256]{2,1,0:T(8,128)S(1)}, u32[]{:S(2)}, u32[]{:S(2)}) collective-permute-start(f32[2,128,256]{2,1,0:T(8,128)S(1)} %get-tuple-element.65.refs_0_), channel_id=1, source_target_pairs={{0,4},{2,6},{4,0},{6,2},{8,12},{10,14},{12,8},{14,10},{1,5},{3,7},... | collective-permute-start | bytes 786440 | tf_op jit(solution)/shard_map/ppermute | solution.py:377
  87.4 15.5 %collective-permute-start.11 = (f32[1,128,256]{2,1,0:T(8,128)S(1)}, f32[1,128,256]{2,1,0:T(8,128)S(1)}, u32[]{:S(2)}, u32[]{:S(2)}) collective-permute-start(f32[1,128,256]{2,1,0:T(8,128)S(1)} %get-tuple-element.72), channel_id=1, source_target_pairs={{0,8},{2,10},{4,12},{6,14},{8,0},{10,2},{12,4},{14,6},{1,9},{3,11}... | collective-permute-start | bytes 393224 | tf_op jit(solution)/shard_map/ppermute | solution.py:377
  93.7 17.1 %copy-start.3 = (f32[512,256]{1,0:T(8,128)S(1)}, f32[512,256]{1,0:T(8,128)}, u32[]{:S(2)}) copy-start(f32[512,256]{1,0:T(8,128)} %get-tuple-element.40.direction_hbm.direction_ref) | copy-start | bytes 1572868
  93.7 17.1 %copy-start.4 = (f32[512,256]{1,0:T(8,128)S(1)}, f32[512,256]{1,0:T(8,128)}, u32[]{:S(2)}) copy-start(f32[512,256]{1,0:T(8,128)} %get-tuple-element.60.scaled_hbm.scaled_ref) | copy-start | bytes 1572868
  96.8 7.6 %collective-permute-start.13 = (f32[1,128,256]{2,1,0:T(8,128)S(1)}, f32[1,128,256]{2,1,0:T(8,128)S(1)}, u32[]{:S(2)}, u32[]{:S(2)}) collective-permute-start(f32[1,128,256]{2,1,0:T(8,128)S(1)} %get-tuple-element.75), channel_id=1, source_target_pairs={{0,8},{2,10},{4,12},{6,14},{8,0},{10,2},{12,4},{14,6},{1,9},{3,11}... | collective-permute-start | bytes 393224 | tf_op jit(solution)/shard_map/ppermute | solution.py:377
  98.5 12.3 %all-to-all-start.1 = ((f32[16,8,256]{2,1,0:T(8,128)}), f32[16,8,256]{2,1,0:T(8,128)S(1)}, u32[]{:S(2)}, u32[]{:S(2)}) async-start(f32[16,8,256]{2,1,0:T(8,128)} %shard_map.76.refs_0_), calls=%async_computation.1 | async-start | bytes 262144 | tf_op jit(solution)/shard_map/all_to_all | solution.py:497
  104.4 7.3 %collective-permute-start.14 = (f32[2,64,256]{2,1,0:T(8,128)S(1)}, f32[2,64,256]{2,1,0:T(8,128)S(1)}, u32[]{:S(2)}, u32[]{:S(2)}) collective-permute-start(f32[2,64,256]{2,1,0:T(8,128)S(1)} %get-tuple-element.77), channel_id=1, source_target_pairs={{0,1},{1,0},{2,3},{3,2},{4,5},{5,4},{6,7},{7,6},{8,9},{9,8},{10,11... | collective-permute-start | bytes 393224 | tf_op jit(solution)/shard_map/ppermute | solution.py:377
  (3 other events, 9.8 us)
